TPU v7x, 32 devices: a whole 2x2x4 slice. The times are simulated.
32 devices in a mesh: pair: 4 (over y, x), task: 8 (over z, core).
Axes of the slice: x: 2, y: 2, z: 4, core: 2. Of those that a mesh axis runs over, the one named last changes fastest.
Arguments:
- factor_blocks: bfloat16 [16, 1536, 625], P('task', 'pair'), may hold values from -1.25 to 1.25
- amplitudes: bfloat16 [16, 512, 625], P('task', 'pair'), may hold values from -0.15625 to 0.15625
- residual_in: float32 [16, 512, 625], P('task', 'pair'), may hold values from -6 to 6
- task_owners: int32 [32, 3], replicated, may hold values from 0 to 7, all different within a row; in each aligned block of 4 rows (0 to 3, 4 to 7, ...) at most 2 rows name the same one
- task_local: int32 [32, 4], replicated, may hold values from 0 to 1
Outputs:
- residual_out: float32 [16, 512, 625], P('task', 'pair')
Inputs may be any that keep to these rules, and one draw needn't show every extreme that they name: `task_owners`: the three numbers of a row differ; in each aligned block of 4 rows no number appears more than 2 times.
All inputs are finite; a program needn't handle non-finite values.
Results may differ from a plain program's by a relative error of at most 0.012.
Values may be sent and summed in bfloat16 or wider, within the bound.
No kernel may reach another device: no remote copies, remote signals or barrier semaphores. Data moves between devices by JAX's collectives and lax.ppermute only.
A program may use at most 64 MiB of HBM per device.

v0:
```python
import jax
import jax.numpy as jnp
from jax import lax
from jax.sharding import PartitionSpec as P

TV = 25


def per_device(factor_blocks, amplitudes, residual_in, task_owners, task_local):
    pair_count = lax.axis_size("pair")
    task_count = lax.axis_size("task")
    column = lax.axis_index("task")
    blocks_here = factor_blocks.shape[0]
    slice_rows = amplitudes.shape[1]
    tile_width = factor_blocks.shape[2]
    owners_all = task_owners.reshape(task_count, pair_count, 3)
    local_all = task_local.reshape(task_count, pair_count, 4)
    my_owners = lax.dynamic_index_in_dim(owners_all, column, 0, keepdims=False)
    my_local = lax.dynamic_index_in_dim(local_all, column, 0, keepdims=False)
    factor_all, amps_all = (
        lax.all_gather(factor_blocks, "task", axis=0, tiled=True),
        lax.all_gather(amplitudes, "task", axis=0, tiled=True),
    )
    global_ids = my_owners * blocks_here + my_local[:, :3]
    factor_send = jnp.stack([factor_all[global_ids[:, 0]], factor_all[global_ids[:, 1]]], axis=0)
    amp_send = amps_all[global_ids[:, 2]][None]
    factor_recv, amp_recv = (
        lax.all_to_all(factor_send, "pair", split_axis=1, concat_axis=1, tiled=True),
        lax.all_to_all(amp_send, "pair", split_axis=1, concat_axis=1, tiled=True),
    )
    row_factor = factor_recv[0].reshape(-1, tile_width)
    col_factor = factor_recv[1].reshape(-1, tile_width)
    amp_block = amp_recv[0].reshape(-1, tile_width)
    integral_tile = lax.dot_general(
        row_factor, col_factor, (((0,), (0,)), ((), ())), preferred_element_type=jnp.float32
    ).astype(jnp.bfloat16)
    ladder = jnp.einsum(
        "icd,acbd->iab",
        amp_block.reshape(-1, TV, TV),
        integral_tile.reshape(TV, TV, TV, TV),
        preferred_element_type=jnp.float32,
    )
    ladder = ladder.astype(jnp.bfloat16).reshape(-1, tile_width)
    onehot = my_local[:, 3][None, :] == jnp.arange(blocks_here, dtype=jnp.int32)[:, None]
    returned = lax.all_to_all(
        ladder.reshape(pair_count, slice_rows, tile_width),
        "pair",
        split_axis=0,
        concat_axis=0,
        tiled=True,
    )
    block_sums = jnp.dot(
        onehot.astype(jnp.bfloat16),
        returned.reshape(pair_count, -1),
        preferred_element_type=jnp.float32,
    )
    block_sums = block_sums.reshape(blocks_here, slice_rows, tile_width)
    return residual_in + block_sums


def solution(mesh):
    placed = (P("task", "pair", None), P("task", "pair", None), P("task", "pair", None), P(), P())
    return jax.shard_map(
        per_device, mesh=mesh, in_specs=placed, out_specs=P("task", "pair", None), check_vma=False
    )
```

profile of v0, /device:TPU:0, one launch (start us, length us, event | category | flops | bytes accessed | tf_op | source)
XLA Modules:
  0.0 241.3 jit_solution(12032044076605689347)
XLA Ops:
  6.5 0.0 copy-start
  6.5 0.0 copy-start.1
  6.5 0.0 all-gather.3.cloned.1.call-start
  6.5 1.8 copy.16
  8.3 0.0 all-gather.3.cloned.1.call-update
  8.3 0.0 all-gather.5.cloned.1.call-start
  8.4 2.3 copy.20
  10.7 0.0 all-gather.5.cloned.1.call-update
  10.7 0.0 copy-done
  10.7 0.1 reshape.23
  10.8 0.1 copy.15
  10.9 0.0 copy-done.1
  10.9 0.1 reshape.24
  11.0 0.1 copy.17
  11.1 0.2 fusion.2
  11.3 34.1 %all-gather.3.cloned.1.call-done = bf16[16,128,625]{1,2,0:T(8,128)(2,1)} async-done(((bf16[2,128,625]{1,2,0:T(8,128)(2,1)}), bf16[16,128,625]{1,2,0:T(8,128)(2,1)}) %all-gather.3.cloned.1.call-update) | async-done | bytes 2560016 | tf_op jit(solution)/shard_map/all_gather | solution.py:22
  45.3 3.2 %gather_fusion = bf16[4,128,625]{1,2,0:T(8,128)(2,1)} fusion(bf16[16,128,625]{1,2,0:T(8,128)(2,1)} %all-gather.3.cloned.1.call-done, s32[1024]{0:T(1024)S(1)} %pad_clamp_fusion.2), kind=kCustom, calls=%fused_computation | custom fusion | bytes 1280016 | tf_op jit(solution)/shard_map/gather | solution.py:26
  48.5 3.7 %all-to-all-start = ((bf16[1,4,128,625]{2,3,0,1:T(8,128)(2,1)}), bf16[1,4,128,625]{2,3,0,1:T(8,128)(2,1)S(1)}, u32[]{:S(2)}, u32[]{:S(2)}) async-start(bf16[1,4,128,625]{2,3,0,1:T(8,128)(2,1)} %bitcast.4), calls=%async_computation | async-start | bytes 1294336 | tf_op jit(solution)/shard_map/all_to_all | solution.py:29
  52.2 70.7 %all-gather.5.cloned.1.call-done = bf16[16,384,625]{1,2,0:T(8,128)(2,1)} async-done(((bf16[2,384,625]{1,2,0:T(8,128)(2,1)}), bf16[16,384,625]{1,2,0:T(8,128)(2,1)}) %all-gather.5.cloned.1.call-update) | async-done | bytes 7680016 | tf_op jit(solution)/shard_map/all_gather | solution.py:21
  122.9 4.2 %gather_fusion.1 = bf16[4,384,625]{1,2,0:T(8,128)(2,1)S(1)} fusion(bf16[16,384,625]{1,2,0:T(8,128)(2,1)} %all-gather.5.cloned.1.call-done, s32[1024]{0:T(1024)S(1)} %get-tuple-element.11), kind=kCustom, calls=%fused_computation.1 | custom fusion | bytes 3840016 | tf_op jit(solution)/shard_map/gather | solution.py:25
  127.1 5.4 %gather_fusion.2 = bf16[4,384,625]{1,2,0:T(8,128)(2,1)} fusion(bf16[16,384,625]{1,2,0:T(8,128)(2,1)} %all-gather.5.cloned.1.call-done, s32[1024]{0:T(1024)S(1)} %get-tuple-element.10), kind=kCustom, calls=%fused_computation.2 | custom fusion | bytes 3840016 | tf_op jit(solution)/shard_map/gather | solution.py:25
  132.5 2.0 pad_maximum_fusion
  134.5 4.8 %copy.21 = bf16[2,4,384,625]{2,0,3,1:T(2,128)(2,1)} copy(bf16[2,4,384,625]{2,3,1,0:T(8,128)(2,1)S(1)} %pad_maximum_fusion) | data formatting | bytes 7680000 | tf_op jit(solution)/shard_map/stack | solution.py:25
  139.3 0.0 all-to-all-done
  139.3 5.0 %all-to-all-start.1 = ((bf16[2,4,384,625]{2,0,3,1:T(2,128)(2,1)}), bf16[2,4,384,625]{2,0,3,1:T(2,128)(2,1)}, u32[]{:S(2)}, u32[]{:S(2)}) async-start(bf16[2,4,384,625]{2,0,3,1:T(2,128)(2,1)} %copy.21), calls=%async_computation.1 | async-start | bytes 7680000 | tf_op jit(solution)/shard_map/all_to_all | solution.py:28
  144.3 0.2 copy.19
  144.5 0.5 reshape.54
  145.0 43.4 %all-to-all-done.1 = bf16[2,4,384,625]{2,0,3,1:T(2,128)(2,1)} async-done(((bf16[2,4,384,625]{2,0,3,1:T(2,128)(2,1)}), bf16[2,4,384,625]{2,0,3,1:T(2,128)(2,1)}, u32[]{:S(2)}, u32[]{:S(2)}) %all-to-all-start.1) | async-done | bytes 3840032 | tf_op jit(solution)/shard_map/all_to_all | solution.py:28
  188.4 8.2 %fusion.8 = (bf16[1,4,384,625]{2,0,3,1:T(2,128)(2,1)S(1)}, bf16[1,4,384,625]{2,0,3,1:T(2,128)(2,1)S(1)}) fusion(bf16[2,4,384,625]{2,0,3,1:T(2,128)(2,1)} %all-to-all-done.1), kind=kLoop, calls=%fused_computation.27 | loop fusion | bytes 7680000 | tf_op jit(solution)/shard_map/slice | solution.py:31
  196.6 1.8 bitcast_convert_fusion.1
  198.4 12.5 %reshape.27 = bf16[25,25,25,25]{3,2,1,0:T(8,128)(2,1)} reshape(bf16[625,625]{1,0:T(8,128)(2,1)S(1)} %bitcast_convert_fusion.1) | data formatting | bytes 1562500 | tf_op jit(solution)/shard_map/reshape | solution.py:40
  210.9 3.6 %bitcast_convert_fusion = bf16[512,25,25]{0,2,1:T(8,128)(2,1)S(1)} fusion(bf16[512,25,25,1]{0,2,1,3:T(8,128)(2,1)S(1)} %reshape.54, bf16[25,25,25,25]{3,2,1,0:T(8,128)(2,1)} %reshape.27), kind=kOutput, calls=%fused_computation.7 | convolution fusion | flops 400320000 | bytes 2061250 | tf_op jit(solution)/shard_map/icd,acbd->iab/dot_general | solution.py:37
  214.5 0.6 reshape_reshape.3
  215.1 0.0 copy-start.2
  215.1 0.9 copy.24
  216.0 3.7 %all-to-all-start.2 = ((bf16[4,128,625]{1,2,0:T(8,128)(2,1)}), bf16[4,128,625]{1,2,0:T(8,128)(2,1)S(1)}, u32[]{:S(2)}, u32[]{:S(2)}) async-start(bf16[4,128,625]{1,2,0:T(8,128)(2,1)} %copy.24), calls=%async_computation.2 | async-start | bytes 1294336 | tf_op jit(solution)/shard_map/all_to_all | solution.py:45
  219.8 0.2 slice_reduce_fusion
  219.9 8.8 %all-to-all-done.2 = bf16[4,128,625]{1,2,0:T(8,128)(2,1)S(1)} async-done(((bf16[4,128,625]{1,2,0:T(8,128)(2,1)}), bf16[4,128,625]{1,2,0:T(8,128)(2,1)S(1)}, u32[]{:S(2)}, u32[]{:S(2)}) %all-to-all-start.2) | async-done | bytes 640032 | tf_op jit(solution)/shard_map/all_to_all | solution.py:45
  228.7 0.3 copy.25
  229.0 1.5 reshape.28
  230.5 1.5 dot_general.16
  232.0 1.1 copy.26
  233.1 0.0 copy-done.2
  233.1 1.3 convolution_add_fusion
  (5 shorter events, 0.0 us)
Async XLA Ops:
  6.5 4.1 %copy-start = (s32[32,4]{0,1:T(4,128)S(1)}, s32[32,4]{0,1:T(4,128)}, u32[]{:S(2)}) copy-start(s32[32,4]{0,1:T(4,128)} %param.9) | copy-start | bytes 1540
  6.5 4.3 %copy-start.1 = (s32[32,3]{0,1:T(4,128)S(1)}, s32[32,3]{0,1:T(4,128)}, u32[]{:S(2)}) copy-start(s32[32,3]{0,1:T(4,128)} %param.8) | copy-start | bytes 1156
  6.5 38.8 %all-gather.3.cloned.1.call-start = ((), (), s32[]{:S(2)}) async-start(), calls=%async_computation.3 | async-start | bytes 2912256 | tf_op jit(solution)/shard_map/all_gather | solution.py:22
  8.3 114.6 %all-gather.5.cloned.1.call-start = ((), (), s32[]{:S(2)}) async-start(), calls=%async_computation.4 | async-start | bytes 8736768 | tf_op jit(solution)/shard_map/all_gather | solution.py:21
  48.5 90.8 %all-to-all-start = ((bf16[1,4,128,625]{2,3,0,1:T(8,128)(2,1)}), bf16[1,4,128,625]{2,3,0,1:T(8,128)(2,1)S(1)}, u32[]{:S(2)}, u32[]{:S(2)}) async-start(bf16[1,4,128,625]{2,3,0,1:T(8,128)(2,1)} %bitcast.4), calls=%async_computation | async-start | bytes 1294336 | tf_op jit(solution)/shard_map/all_to_all | solution.py:29
  139.3 49.1 %all-to-all-start.1 = ((bf16[2,4,384,625]{2,0,3,1:T(2,128)(2,1)}), bf16[2,4,384,625]{2,0,3,1:T(2,128)(2,1)}, u32[]{:S(2)}, u32[]{:S(2)}) async-start(bf16[2,4,384,625]{2,0,3,1:T(2,128)(2,1)} %copy.21), calls=%async_computation.1 | async-start | bytes 7680000 | tf_op jit(solution)/shard_map/all_to_all | solution.py:28
  215.1 18.0 %copy-start.2 = (f32[2,128,625]{1,0,2:T(2,128)S(1)}, f32[2,128,625]{1,0,2:T(2,128)}, u32[]{:S(2)}) copy-start(f32[2,128,625]{1,0,2:T(2,128)} %param.7) | copy-start | bytes 1920004
  216.0 12.7 %all-to-all-start.2 = ((bf16[4,128,625]{1,2,0:T(8,128)(2,1)}), bf16[4,128,625]{1,2,0:T(8,128)(2,1)S(1)}, u32[]{:S(2)}, u32[]{:S(2)}) async-start(bf16[4,128,625]{1,2,0:T(8,128)(2,1)} %copy.24), calls=%async_computation.2 | async-start | bytes 1294336 | tf_op jit(solution)/shard_map/all_to_all | solution.py:45
Sparse Core Ops, SparseCore 0:
  9.0 36.2 all-gather.2
  47.0 75.9 all-gather.4
where the time goes:
time: 242 us; the launch traced here: 241 us
  waiting for transfers between devices  157 us (65%)
  local copies, waits for them, and re-layouts  49.5 us (20%)
  between operations  13.6 us (6%)
  starting transfers between devices  12.4 us (5%)
  matrix products  6.76 us (3%)
    all_gather x1, waiting for transfers between devices, per_device(): lax.all_gather(factor_blocks, 'task', axis=0, tiled=True)  70.7 us
    all_to_all x1, waiting for transfers between devices, per_device(): lax.all_to_all(factor_send, 'pair', split_axis=1, concat_axis=1, tiled=True)  43.4 us
    all_gather x1, waiting for transfers between devices, per_device(): lax.all_gather(amplitudes, 'task', axis=0, tiled=True)  34.1 us
    reshape x1, local copies, waits for them, and re-layouts, per_device(): integral_tile.reshape(TV, TV, TV, TV)  12.5 us
    all_to_all x1, waiting for transfers between devices, per_device(): lax.all_to_all(ladder.reshape(pair_count, slice_rows, tile_width), 'pair'...  8.76 us
    slice x1, local copies, waits for them, and re-layouts, per_device(): row_factor = factor_recv[0].reshape(-1, tile_width)  8.22 us
    gather x1, local copies, waits for them, and re-layouts, per_device(): factor_all[global_ids[:, 1]]  5.38 us
    all_to_all x1, starting transfers between devices, per_device(): lax.all_to_all(factor_send, 'pair', split_axis=1, concat_axis=1, tiled=True)  4.95 us
  transfers between devices with their start and end apart: 5, of which 4 were waited for; matrix products, arithmetic and copies ran while one was open for 10% of the time, Pallas kernels for 0%

commit v1 on v0

v1 whole, which is shorter than its diff:
```python
import functools

import jax
import jax.numpy as jnp
import numpy as np
from jax import lax
from jax.experimental import pallas as pl
from jax.experimental.pallas import tpu as pltpu
from jax.sharding import PartitionSpec as P

TV = 25
PAD = 32
GROUP = 4
LANES = PAD * GROUP
GROUPS = -(-TV // GROUP)
ROWS = TV * PAD
WIDE = GROUPS * LANES
STEP = 2 * LANES
BF = jnp.bfloat16
F32 = jnp.float32
VMEM_BYTES = 48 * 1024 * 1024


def placement(major_first, width):
    x, y = np.divmod(np.arange(TV * TV), TV)
    spots = x * PAD + y if major_first else y * PAD + x
    return (spots[:, None] == np.arange(width)[None, :]).astype(jnp.bfloat16)


def prepare_kernel(tile_ref, rows_of_ref, lanes_of_ref, *refs):
    rows_ref, lanes_ref = refs[-2:]
    tile = tile_ref[0]
    rows_ref[0] = lax.dot_general(
        rows_of_ref[...], tile, (((1,), (1,)), ((), ())), preferred_element_type=F32
    ).astype(BF)
    lanes_ref[0] = jnp.dot(tile, lanes_of_ref[...], preferred_element_type=F32).astype(BF)


def prepare(tiles, first, total, rows_of, lanes_of, held):
    count, depth, width = tiles.shape
    whole = lambda shape: pl.BlockSpec(shape, lambda i: (0,) * len(shape))
    out_shape = (
        jax.ShapeDtypeStruct((total, ROWS, depth), BF),
        jax.ShapeDtypeStruct((total, depth, WIDE), BF),
    )
    out_specs = (
        pl.BlockSpec((1, ROWS, depth), lambda i: (first + i, 0, 0)),
        pl.BlockSpec((1, depth, WIDE), lambda i: (first + i, 0, 0)),
    )
    in_specs = [
        pl.BlockSpec((1, depth, width), lambda i: (i, 0, 0)),
        whole(rows_of.shape),
        whole(lanes_of.shape),
    ]
    operands = [tiles, rows_of, lanes_of]
    aliases = {}
    if held is not None:
        in_specs += [pl.BlockSpec(memory_space=pl.ANY)] * 2
        operands += list(held)
        aliases = {3: 0, 4: 1}
    return pl.pallas_call(
        prepare_kernel,
        out_shape=out_shape,
        grid=(count,),
        in_specs=in_specs,
        out_specs=out_specs,
        input_output_aliases=aliases,
        compiler_params=pltpu.CompilerParams(vmem_limit_bytes=VMEM_BYTES),
        cost_estimate=pl.CostEstimate(
            flops=4 * count * depth * width * ROWS,
            bytes_accessed=2 * count * depth * (width + ROWS + WIDE),
            transcendentals=0,
        ),
    )(*operands)


def swap_blocks(blocks, low, even):
    r0, r1, r2, r3 = blocks
    turn = lambda block, by: pltpu.roll(block, by, 1)
    s0 = jnp.where(low, r0, turn(r2, LANES // 2))
    s2 = jnp.where(low, turn(r0, LANES // 2), r2)
    s1 = jnp.where(low, r1, turn(r3, LANES // 2))
    s3 = jnp.where(low, turn(r1, LANES // 2), r3)
    return (
        jnp.where(even, s0, turn(s1, PAD)),
        jnp.where(even, turn(s0, LANES - PAD), s1),
        jnp.where(even, s2, turn(s3, PAD)),
        jnp.where(even, turn(s2, LANES - PAD), s3),
    )


def ladder_kernel(r_at, c_at, t_at, o_at, rows_ref, lanes_ref, amp_ref, back_ref, out_ref, v_ref, w_ref, acc_ref):
    step, steps = pl.program_id(1), pl.num_programs(1)
    at = pl.program_id(0) * steps + step

    @pl.when(step == 0)
    def _():
        acc_ref[...] = jnp.zeros_like(acc_ref)

    lane = lax.broadcasted_iota(jnp.int32, (PAD, LANES), 1)
    low = lane < LANES // 2
    even = (lane // PAD) % 2 == 0
    nothing = jnp.zeros((PAD, LANES), F32)
    ladder = None
    for part, start in enumerate(range(0, WIDE, STEP)):
        size = min(STEP, WIDE - start)
        slot = part % 2
        v_ref[slot, :, :size] = jnp.dot(
            rows_ref[0], lanes_ref[0, :, start : start + size], preferred_element_type=F32
        )
        for inner in range(0, size, LANES):
            first = (start + inner) // PAD
            for group in range(GROUPS):
                blocks = [
                    v_ref[slot, b * PAD : (b + 1) * PAD, inner : inner + LANES] if b < TV else nothing
                    for b in range(group * GROUP, (group + 1) * GROUP)
                ]
                for c, block in enumerate(swap_blocks(blocks, low, even), first):
                    if c < TV:
                        w_ref[c * PAD : (c + 1) * PAD, group * LANES : (group + 1) * LANES] = block.astype(BF)
        stop = min(start + size, ROWS)
        term = jnp.dot(amp_ref[0, :, start:stop], w_ref[start:stop, :], preferred_element_type=F32)
        ladder = term if ladder is None else ladder + term
    acc_ref[o_at[at]] += ladder

    @pl.when(step == steps - 1)
    def _():
        for m in range(acc_ref.shape[0]):
            out_ref[0, m] = jnp.dot(acc_ref[m].astype(BF), back_ref[...], preferred_element_type=F32).astype(BF)


def ladders(places, rows, lanes, amps, back, blocks_here):
    columns, tasks, _ = places.shape
    depth, pairs = lanes.shape[1], amps.shape[1]
    tables = [places[:, :, i].reshape(-1) for i in range(4)]
    return pl.pallas_call(
        ladder_kernel,
        out_shape=jax.ShapeDtypeStruct((columns, blocks_here, pairs, TV * TV), BF),
        grid_spec=pltpu.PrefetchScalarGridSpec(
            num_scalar_prefetch=4,
            grid=(columns, tasks),
            in_specs=[
                pl.BlockSpec((1, ROWS, depth), lambda i, j, r, c, t, o: (c[i * tasks + j], 0, 0)),
                pl.BlockSpec((1, depth, WIDE), lambda i, j, r, c, t, o: (r[i * tasks + j], 0, 0)),
                pl.BlockSpec((1, pairs, WIDE), lambda i, j, r, c, t, o: (t[i * tasks + j], 0, 0)),
                pl.BlockSpec(back.shape, lambda i, j, r, c, t, o: (0, 0)),
            ],
            out_specs=pl.BlockSpec((1, blocks_here, pairs, TV * TV), lambda i, j, r, c, t, o: (i, 0, 0, 0)),
            scratch_shapes=[
                pltpu.VMEM((2, ROWS, STEP), F32),
                pltpu.VMEM((ROWS, WIDE), BF),
                pltpu.VMEM((blocks_here, pairs, WIDE), F32),
            ],
        ),
        compiler_params=pltpu.CompilerParams(vmem_limit_bytes=VMEM_BYTES),
        cost_estimate=pl.CostEstimate(
            flops=2 * columns * tasks * ROWS * WIDE * (depth + pairs),
            bytes_accessed=2 * columns * tasks * ((ROWS + WIDE) * depth + pairs * WIDE),
            transcendentals=0,
        ),
    )(*tables, rows, lanes, amps, back)


def gather_pairs(part, pair_count):
    if pair_count != 4 or part.shape[0] != 2:
        return lax.all_gather(part, "pair", axis=1, tiled=True)
    beside = lambda x, bit: lax.ppermute(x, "pair", [(p, p ^ bit) for p in range(pair_count)])
    across, along = beside(part, 1), beside(part, 2)
    corner = jnp.concatenate([beside(along[:1], 1), beside(across[1:], 2)], axis=0)
    return jnp.concatenate([part, across, along, corner], axis=1)


def per_device(factor_blocks, amplitudes, residual_in, task_owners, task_local):
    pair_count = lax.axis_size("pair")
    task_count = lax.axis_size("task")
    column = lax.axis_index("task")
    blocks_here, depth_here, _ = factor_blocks.shape
    levels = task_count // 2
    level, core = column // 2, column % 2
    depth = depth_here // levels
    other_core = lambda x: lax.ppermute(x, "task", [(c, c ^ 1) for c in range(task_count)])

    def up(x, by):
        return lax.ppermute(x, "task", [(c, (c + 2 * by) % task_count) for c in range(task_count)])

    rows_of = jnp.asarray(placement(True, ROWS).T)
    lanes_of = jnp.asarray(placement(False, WIDE))
    amp_lanes = jnp.asarray(placement(True, WIDE))
    back = jnp.asarray(placement(False, WIDE).T)

    slices = factor_blocks.reshape(blocks_here, levels, depth, -1)
    mine = [
        lax.dynamic_index_in_dim(slices, (level + by) % levels, 1, keepdims=False) for by in range(levels)
    ]
    parts = [mine[0]] + [up(mine[by], by) for by in range(1, levels)]
    amp_parts = [amplitudes] + [up(amplitudes, by) for by in range(1, levels)]

    total = 2 * levels * blocks_here
    held = None
    for by, part in enumerate(parts):
        tiles = gather_pairs(part, pair_count)
        held = prepare(tiles, 2 * by * blocks_here, total, rows_of, lanes_of, held)
        held = prepare(other_core(tiles), (2 * by + 1) * blocks_here, total, rows_of, lanes_of, held)
    amps_mine = jnp.stack(amp_parts, axis=0)
    amps = jnp.stack([amps_mine, other_core(amps_mine)], axis=1)
    amps = amps.reshape(total, *amplitudes.shape[1:])
    amps = jnp.einsum("tiw,wv->tiv", amps, amp_lanes, preferred_element_type=F32).astype(BF)

    owners = task_owners.reshape(levels, 2, -1, 3)
    local = task_local.reshape(levels, 2, -1, 4)
    owners = lax.dynamic_index_in_dim(owners, core, 1, keepdims=False)
    local = lax.dynamic_index_in_dim(local, core, 1, keepdims=False)
    spot = (((level - owners // 2) % levels) * 2 + (owners % 2 != core)) * blocks_here + local[:, :, :3]
    places = jnp.concatenate([spot, local[:, :, 3:]], axis=2).astype(jnp.int32)
    order = (level + jnp.arange(levels)) % levels
    places = places[order]

    total_sum = residual_in
    calls = min(levels, 4)
    width = levels // calls
    for call in reversed(range(calls)):
        sums = ladders(places[call * width : (call + 1) * width], *held, amps, back, blocks_here)
        for i in range(width):
            by = call * width + i
            total_sum = total_sum + (up(sums[i], by) if by else sums[i]).astype(F32)
    return total_sum


def solution(mesh):
    placed = (P("task", "pair", None), P("task", "pair", None), P("task", "pair", None), P(), P())
    return jax.shard_map(
        per_device, mesh=mesh, in_specs=placed, out_specs=P("task", "pair", None), check_vma=False
    )
```

time: 242 us -> 204 us (0.84)
  waiting for transfers between devices: 157 us -> 12.2 us
  Pallas kernels: 0 us -> 81.9 us
  starting transfers between devices: 12.4 us -> 39.8 us
  other arithmetic: 2.19 us -> 21 us
  between operations: 13.6 us -> 0.43 us
  local copies, waits for them, and re-layouts: 49.5 us -> 44.1 us
  matrix products: 6.76 us -> 3.74 us
    all_gather x2 -> x0, waiting for transfers between devices: 105 us -> none  [the longest x1 70.7 us: per_device(): lax.all_gather(factor_blocks, 'task', axis=0, tiled=True)]
    pallas_call x0 -> x12, Pallas kernels: none -> 81.9 us  [the longest x4 52.5 us: ladders(): pl.pallas_call(ladder_kernel, out_shape=jax.ShapeDtypeStruct((columns, bl...]
    all_to_all x3 -> x0, waiting for transfers between devices: 52.2 us -> none  [the longest x1 43.4 us: per_device(): lax.all_to_all(factor_send, 'pair', split_axis=1, concat_axis=1, tiled=True)]
    ppermute x0 -> x30, starting transfers between devices: none -> 39.8 us  [the longest x9 20.8 us: up(): lax.ppermute(x, 'task', [(c, (c + 2 * by) % task_count) for c in range(ta...]
    ppermute x0 -> x4, local copies, waits for them, and re-layouts: none -> 16.4 us  [per_device(): lax.ppermute(x, 'task', [(c, c ^ 1) for c in range(task_count)])]
    reshape x4 -> x2, local copies, waits for them, and re-layouts: 14.1 us -> 0.18 us  [the longest x1 0.09 us: per_device(): local = task_local.reshape(levels, 2, -1, 4)]
    all_to_all x3 -> x0, starting transfers between devices: 12.3 us -> none  [the longest x1 4.95 us: per_device(): lax.all_to_all(factor_send, 'pair', split_axis=1, concat_axis=1, tiled=True)]
    another operation x1 -> x3, other arithmetic: 1.97 us -> 14.3 us  [the longest x2 9.63 us: per_device(): amps = jnp.stack([amps_mine, other_core(amps_mine)], axis=1)]
  transfers between devices with their start and end apart: 5 -> 30, of which waited for: 4 -> 5; matrix products, arithmetic and copies ran while one was open for 10% -> 23% of each run, Pallas kernels for 0% -> 34%
where the time goes in v1:
time: 204 us; the launch traced here: 203 us
  Pallas kernels  81.9 us (40%)
  local copies, waits for them, and re-layouts  44.1 us (22%)
  starting transfers between devices  39.8 us (20%)
  other arithmetic  21 us (10%)
  waiting for transfers between devices  12.2 us (6%)
  matrix products  3.74 us (2%)
    pallas_call x4, Pallas kernels, ladders(): pl.pallas_call(ladder_kernel, out_shape=jax.ShapeDtypeStruct((columns, bl...  52.5 us
    pallas_call x8, Pallas kernels, prepare(): pl.pallas_call(prepare_kernel, out_shape=out_shape, grid=(count,), in_spe...  29.4 us
    ppermute x9, starting transfers between devices, up(): lax.ppermute(x, 'task', [(c, (c + 2 * by) % task_count) for c in range(ta...  20.8 us
    ppermute x16, starting transfers between devices, gather_pairs(): lax.ppermute(x, 'pair', [(p, p ^ bit) for p in range(pair_count)])  18 us
    ppermute x4, local copies, waits for them, and re-layouts, per_device(): lax.ppermute(x, 'task', [(c, c ^ 1) for c in range(task_count)])  16.4 us
    ppermute x9, waiting for transfers between devices, up(): lax.ppermute(x, 'task', [(c, (c + 2 * by) % task_count) for c in range(ta...  11 us
    concatenate x4, local copies, waits for them, and re-layouts, gather_pairs(): return jnp.concatenate([part, across, along, corner], axis=1)  10.8 us
    unnamed x70, local copies, waits for them, and re-layouts  10.5 us
  transfers between devices with their start and end apart: 30, of which 5 were waited for; matrix products, arithmetic and copies ran while one was open for 23% of the time, Pallas kernels for 34%

profile of v1, /device:TPU:0, one launch (start us, length us, event | category | flops | bytes accessed | tf_op | source)
XLA Modules:
  0.0 203.2 jit_solution(896643304454554808)
XLA Ops:
  0.0 3.4 %copy.57 = bf16[2,384,625]{2,1,0:T(8,128)(2,1)S(1)} copy(bf16[2,384,625]{1,0,2:T(2,128)(2,1)} %param.9) | data formatting | bytes 1920000 | tf_op args[0]
  3.5 3.0 %collective-permute-start.19 = (bf16[2,96,625]{2,1,0:T(8,128)(2,1)S(1)}, bf16[2,96,625]{2,1,0:T(8,128)(2,1)S(1)}, u32[]{:S(2)}, u32[]{:S(2)}) collective-permute-start(bf16[2,96,625]{2,1,0:T(8,128)(2,1)S(1)} %get-tuple-element.53), channel_id=1, source_target_pairs={{0,16},{8,24},{16,0},{24,8},{1,17},{9,25},{17,1},{25,9},{2,18},{10... | collective-permute-start | bytes 720008 | tf_op jit(solution)/shard_map/ppermute | solution.py:167
  6.6 1.5 collective-permute-start.18
  8.1 1.6 collective-permute-start.12
  9.6 2.6 %collective-permute-start.6 = (bf16[2,96,625]{2,1,0:T(8,128)(2,1)S(1)}, bf16[2,96,625]{2,1,0:T(8,128)(2,1)}, u32[]{:S(2)}, u32[]{:S(2)}) collective-permute-start(bf16[2,96,625]{2,1,0:T(8,128)(2,1)S(1)} %get-tuple-element.55), channel_id=1, source_target_pairs={{0,4},{1,5},{2,6},{3,7},{4,0},{5,1},{6,2},{7,3},{8,12},{9,13},{10,... | collective-permute-start | bytes 720008 | tf_op jit(solution)/shard_map/ppermute | solution.py:184
  12.2 1.3 collective-permute-start
  14.2 4.7 %collective-permute-done.12 = bf16[2,96,625]{2,1,0:T(8,128)(2,1)S(1)} collective-permute-done((bf16[2,96,625]{2,1,0:T(8,128)(2,1)S(1)}, bf16[2,96,625]{2,1,0:T(8,128)(2,1)S(1)}, u32[]{:S(2)}, u32[]{:S(2)}) %collective-permute-start.12) | collective-permute-done | bytes 240032 | tf_op jit(solution)/shard_map/ppermute | solution.py:184
  19.8 1.8 collective-permute-start.20
  21.6 6.2 %collective-permute-done.6 = bf16[2,96,625]{2,1,0:T(8,128)(2,1)} collective-permute-done((bf16[2,96,625]{2,1,0:T(8,128)(2,1)S(1)}, bf16[2,96,625]{2,1,0:T(8,128)(2,1)}, u32[]{:S(2)}, u32[]{:S(2)}) %collective-permute-start.6) | collective-permute-done | bytes 240032 | tf_op jit(solution)/shard_map/ppermute | solution.py:184
  27.8 0.5 collective-permute-start.7
  28.4 0.6 collective-permute-start.21
  29.0 0.6 gather_fusion
  29.6 1.6 collective-permute-start.8
  31.7 1.6 collective-permute-start.1
  33.7 0.7 slice.136
  34.7 1.5 collective-permute-start.15
  36.2 0.7 collective-permute-done.7
  37.4 1.1 maximum_maximum_fusion.3.tile_ref
  38.5 2.7 %copy.61 = bf16[2,384,625]{1,0,2:T(2,128)(2,1)} copy(bf16[2,384,625]{2,1,0:T(8,128)(2,1)S(1)} %maximum_maximum_fusion.3.tile_ref) | data formatting | bytes 1920000 | tf_op jit(solution)/shard_map/concatenate | solution.py:170
  41.2 0.7 slice.135
  41.9 8.4 %collective-permute-start.24 = (bf16[2,128,625]{1,0,2:T(2,128)(2,1)S(1)}, bf16[2,128,625]{1,0,2:T(2,128)(2,1)S(1)}, u32[]{:S(2)}, u32[]{:S(2)}) collective-permute-start(bf16[2,128,625]{1,0,2:T(2,128)(2,1)S(1)} %copy-done.16), channel_id=1, source_target_pairs={{0,4},{1,5},{2,6},{3,7},{4,0},{5,1},{6,2},{7,3},{8,12},{9,13},{10,... | collective-permute-start | bytes 960008 | tf_op jit(solution)/shard_map/ppermute | solution.py:184
  50.3 0.7 slice.134
  50.9 2.1 %collective-permute-start.25 = (bf16[2,128,625]{1,0,2:T(2,128)(2,1)S(1)}, bf16[2,128,625]{1,0,2:T(2,128)(2,1)S(1)}, u32[]{:S(2)}, u32[]{:S(2)}) collective-permute-start(bf16[2,128,625]{1,0,2:T(2,128)(2,1)S(1)} %copy-done.16), channel_id=1, source_target_pairs={{0,6},{1,7},{2,0},{3,1},{4,2},{5,3},{6,4},{7,5},{8,14},{9,15},{10,... | collective-permute-start | bytes 960008 | tf_op jit(solution)/shard_map/ppermute | solution.py:184
  53.0 0.7 slice.132
  53.9 0.6 slice.133
  54.6 1.2 collective-permute-start.10
  55.8 0.6 collective-permute-start.9
  56.4 1.4 maximum_maximum_fusion.2.tile_ref
  57.8 2.7 %copy.60 = bf16[2,384,625]{1,0,2:T(2,128)(2,1)} copy(bf16[2,384,625]{2,1,0:T(8,128)(2,1)S(1)} %maximum_maximum_fusion.2.tile_ref) | data formatting | bytes 1920000 | tf_op jit(solution)/shard_map/concatenate | solution.py:170
  60.5 1.5 collective-permute-start.3
  62.0 0.8 collective-permute-start.4
  62.8 1.4 maximum_maximum_fusion.1.tile_ref
  64.2 2.6 %copy.59 = bf16[2,384,625]{1,0,2:T(2,128)(2,1)} copy(bf16[2,384,625]{2,1,0:T(8,128)(2,1)S(1)} %maximum_maximum_fusion.1.tile_ref) | data formatting | bytes 1920000 | tf_op jit(solution)/shard_map/concatenate | solution.py:170
  67.4 1.4 maximum_maximum_fusion.tile_ref
  68.8 2.8 %copy.58 = bf16[2,384,625]{1,0,2:T(2,128)(2,1)} copy(bf16[2,384,625]{2,1,0:T(8,128)(2,1)S(1)} %maximum_maximum_fusion.tile_ref) | data formatting | bytes 1920000 | tf_op jit(solution)/shard_map/concatenate | solution.py:170
  72.8 4.6 %pad_maximum_fusion.1 = bf16[4,2,128,625]{2,1,3,0:T(2,128)(2,1)} fusion(bf16[1,2,128,625]{2,1,3,0:T(2,128)(2,1)} %bitcast.43, bf16[1,2,128,625]{2,1,3,0:T(2,128)(2,1)} %bitcast.41, bf16[1,2,128,625]{2,1,3,0:T(2,128)(2,1)} %bitcast.45, bf16[1,2,128,625]{2,1,3,0:T(2,128)(2,1)S(1)} %bitcast.39), kind=kLoop, calls=%fused_computation.3 | loop fusion | flops 1920000 | bytes 2560000 | tf_op jit(solution)/shard_map/stack | solution.py:204
  77.6 4.5 %fusion.12 = bf16[4,1,2,128,625]{3,2,4,0,1:T(2,128)(2,1)} fusion(bf16[1,2,128,625]{2,1,3,0:T(2,128)(2,1)} %bitcast.44, bf16[1,2,128,625]{2,1,3,0:T(2,128)(2,1)} %bitcast.42, bf16[1,2,128,625]{2,1,3,0:T(2,128)(2,1)} %bitcast.46, bf16[1,2,128,625]{2,1,3,0:T(2,128)(2,1)S(1)} %bitcast.40), kind=kLoop, calls=%fused_computation.56 | loop fusion | flops 1920000 | bytes 2560000 | tf_op jit(solution)/shard_map/stack | solution.py:205
  82.1 3.7 %shard_map.91 = (bf16[16,800,384]{2,1,0:T(8,128)(2,1)}, bf16[16,384,896]{2,1,0:T(8,128)(2,1)}) custom-call(bf16[2,384,625]{2,1,0:T(8,128)(2,1)S(1)} %copy-done.10, bf16[800,625]{1,0:T(8,128)(2,1)S(1)} %copy-done.3, bf16[625,896]{1,0:T(8,128)(2,1)S(1)} %copy-done.2), custom_call_target="tpu_custom_call" | custom-call | flops 1536000000 | bytes 3565056 | tf_op jit(solution)/shard_map/pallas_call | solution.py:61
  85.8 4.1 %copy.62.tile_ref = bf16[2,384,625]{2,1,0:T(8,128)(2,1)} copy(bf16[2,384,625]{1,0,2:T(2,128)(2,1)} %collective-permute-done.22) | data formatting | bytes 1920000 | tf_op jit(solution)/shard_map/ppermute | solution.py:181
  89.9 1.2 copy-done.14
  91.1 3.6 %shard_map.92 = (bf16[16,800,384]{2,1,0:T(8,128)(2,1)}, bf16[16,384,896]{2,1,0:T(8,128)(2,1)}) custom-call(bf16[2,384,625]{2,1,0:T(8,128)(2,1)S(1)} %copy-done.14, bf16[800,625]{1,0:T(8,128)(2,1)S(1)} %copy-done.3, bf16[625,896]{1,0:T(8,128)(2,1)S(1)} %copy-done.2, ...), custom_call_target="tpu_custom_call", output_to_operand_aliasing={{0}: (3, {}), {1}: (4, {})} | custom-call | flops 1536000000 | bytes 3565056 | tf_op jit(solution)/shard_map/pallas_call | solution.py:61
  94.7 3.6 %shard_map.93 = (bf16[16,800,384]{2,1,0:T(8,128)(2,1)}, bf16[16,384,896]{2,1,0:T(8,128)(2,1)}) custom-call(bf16[2,384,625]{2,1,0:T(8,128)(2,1)S(1)} %copy-done.6, bf16[800,625]{1,0:T(8,128)(2,1)S(1)} %copy-done.3, bf16[625,896]{1,0:T(8,128)(2,1)S(1)} %copy-done.2, ...), custom_call_target="tpu_custom_call", output_to_operand_aliasing={{0}: (3, {}), {1}: (4, {})} | custom-call | flops 1536000000 | bytes 3565056 | tf_op jit(solution)/shard_map/pallas_call | solution.py:61
  98.3 4.1 %copy.63.tile_ref = bf16[2,384,625]{2,1,0:T(8,128)(2,1)} copy(bf16[2,384,625]{1,0,2:T(2,128)(2,1)} %collective-permute-done.17) | data formatting | bytes 1920000 | tf_op jit(solution)/shard_map/ppermute | solution.py:181
  102.4 4.1 %copy.64.tile_ref = bf16[2,384,625]{2,1,0:T(8,128)(2,1)} copy(bf16[2,384,625]{1,0,2:T(2,128)(2,1)} %collective-permute-done.11) | data formatting | bytes 1920000 | tf_op jit(solution)/shard_map/ppermute | solution.py:181
  106.5 4.1 %copy.65.tile_ref = bf16[2,384,625]{2,1,0:T(8,128)(2,1)} copy(bf16[2,384,625]{1,0,2:T(2,128)(2,1)} %collective-permute-done.5) | data formatting | bytes 1920000 | tf_op jit(solution)/shard_map/ppermute | solution.py:181
  110.6 1.2 copy-done.13
  111.8 3.6 %shard_map.94 = (bf16[16,800,384]{2,1,0:T(8,128)(2,1)}, bf16[16,384,896]{2,1,0:T(8,128)(2,1)}) custom-call(bf16[2,384,625]{2,1,0:T(8,128)(2,1)S(1)} %copy-done.13, bf16[800,625]{1,0:T(8,128)(2,1)S(1)} %copy-done.3, bf16[625,896]{1,0:T(8,128)(2,1)S(1)} %copy-done.2, ...), custom_call_target="tpu_custom_call", output_to_operand_aliasing={{0}: (3, {}), {1}: (4, {})} | custom-call | flops 1536000000 | bytes 3565056 | tf_op jit(solution)/shard_map/pallas_call | solution.py:61
  115.4 3.7 %shard_map.95 = (bf16[16,800,384]{2,1,0:T(8,128)(2,1)}, bf16[16,384,896]{2,1,0:T(8,128)(2,1)}) custom-call(bf16[2,384,625]{2,1,0:T(8,128)(2,1)S(1)} %maximum_maximum_fusion.1.tile_ref, bf16[800,625]{1,0:T(8,128)(2,1)S(1)} %copy-done.3, bf16[625,896]{1,0:T(8,128)(2,1)S(1)} %copy-done.2, ...), custom_call_target="tpu_custom_call", output_to_operand_aliasing={{0}: (3, {}), {1}: (4, {})} | custom-call | flops 1536000000 | bytes 3565056 | tf_op jit(solution)/shard_map/pallas_call | solution.py:61
  119.1 3.7 %shard_map.96 = (bf16[16,800,384]{2,1,0:T(8,128)(2,1)}, bf16[16,384,896]{2,1,0:T(8,128)(2,1)}) custom-call(bf16[2,384,625]{2,1,0:T(8,128)(2,1)S(1)} %copy-done.12, bf16[800,625]{1,0:T(8,128)(2,1)S(1)} %copy-done.3, bf16[625,896]{1,0:T(8,128)(2,1)S(1)} %copy-done.2, ...), custom_call_target="tpu_custom_call", output_to_operand_aliasing={{0}: (3, {}), {1}: (4, {})} | custom-call | flops 1536000000 | bytes 3565056 | tf_op jit(solution)/shard_map/pallas_call | solution.py:61
  122.8 3.6 %shard_map.97 = (bf16[16,800,384]{2,1,0:T(8,128)(2,1)}, bf16[16,384,896]{2,1,0:T(8,128)(2,1)}) custom-call(bf16[2,384,625]{2,1,0:T(8,128)(2,1)S(1)} %copy-done.8, bf16[800,625]{1,0:T(8,128)(2,1)S(1)} %copy-done.3, bf16[625,896]{1,0:T(8,128)(2,1)S(1)} %copy-done.2, ...), custom_call_target="tpu_custom_call", output_to_operand_aliasing={{0}: (3, {}), {1}: (4, {})} | custom-call | flops 1536000000 | bytes 3565056 | tf_op jit(solution)/shard_map/pallas_call | solution.py:61
  126.5 3.9 %shard_map.98 = (bf16[16,800,384]{2,1,0:T(8,128)(2,1)}, bf16[16,384,896]{2,1,0:T(8,128)(2,1)}) custom-call(bf16[2,384,625]{2,1,0:T(8,128)(2,1)S(1)} %copy-done.11, bf16[800,625]{1,0:T(8,128)(2,1)S(1)} %copy-done.3, bf16[625,896]{1,0:T(8,128)(2,1)S(1)} %copy-done.2, ...), custom_call_target="tpu_custom_call", output_to_operand_aliasing={{0}: (3, {}), {1}: (4, {})} | custom-call | flops 1536000000 | bytes 3565056 | tf_op jit(solution)/shard_map/pallas_call | solution.py:61
  130.3 5.1 %pad_maximum_fusion = bf16[4,2,2,128,625]{3,2,4,0,1:T(2,128)(2,1)S(1)} fusion(bf16[4,1,2,128,625]{3,2,4,0,1:T(2,128)(2,1)} %bitcast.13, bf16[4,1,2,128,625]{3,2,4,0,1:T(2,128)(2,1)S(1)} %copy-done.15), kind=kLoop, calls=%fused_computation.1 | loop fusion | flops 1280000 | bytes 5120000 | tf_op jit(solution)/shard_map/stack | solution.py:205
  135.8 0.9 copy-done.33
  136.7 3.7 %convolution_convert_fusion.amp_ref = bf16[16,128,896]{2,1,0:T(8,128)(2,1)S(1)} fusion(bf16[16,128,625]{1,2,0:T(8,128)(2,1)S(1)} %bitcast.38, bf16[625,896,1]{1,0,2:T(8,128)(2,1)S(1)} %copy-done.33), kind=kOutput, calls=%fused_computation.2 | convolution fusion | flops 2295595008 | bytes 7350016 | tf_op jit(solution)/shard_map/tiw,wv->tiv/dot_general | solution.py:207
  140.5 13.6 %shard_map.99 = bf16[1,2,128,625]{3,2,1,0:T(8,128)(2,1)S(1)} custom-call(s32[4]{0:T(128)S(1)} %get-tuple-element.52.r_at, s32[4]{0:T(128)S(1)} %get-tuple-element.51.c_at, s32[4]{0:T(128)S(1)} %get-tuple-element.50.t_at, s32[4]{0:T(128)S(1)} %get-tuple-element.49.o_at, bf16[16,800,384]{2,1,0:T(8,128)(2,1)} %get-tuple-element.35.rows_ref, ...), custom_call_target="tpu_custom_call" | custom-call | flops 2936012800 | bytes 6127616 | tf_op jit(solution)/shard_map/pallas_call | solution.py:136
  154.1 3.9 %collective-permute-start.27 = (bf16[2,128,625]{2,1,0:T(8,128)(2,1)S(1)}, bf16[2,128,625]{2,1,0:T(8,128)(2,1)}, u32[]{:S(2)}, u32[]{:S(2)}) collective-permute-start(bf16[2,128,625]{2,1,0:T(8,128)(2,1)S(1)} %bitcast.34), channel_id=1, source_target_pairs={{0,6},{1,7},{2,0},{3,1},{4,2},{5,3},{6,4},{7,5},{8,14},{9,15},{10,... | collective-permute-start | bytes 960008 | tf_op jit(solution)/shard_map/ppermute | solution.py:184
  158.0 13.1 %shard_map.100 = bf16[1,2,128,625]{3,2,1,0:T(8,128)(2,1)S(1)} custom-call(s32[4]{0:T(128)S(1)} %get-tuple-element.48.r_at, s32[4]{0:T(128)S(1)} %get-tuple-element.47.c_at, s32[4]{0:T(128)S(1)} %get-tuple-element.46.t_at, s32[4]{0:T(128)S(1)} %get-tuple-element.45.o_at, bf16[16,800,384]{2,1,0:T(8,128)(2,1)} %get-tuple-element.35.rows_ref, ...), custom_call_target="tpu_custom_call" | custom-call | flops 2936012800 | bytes 6127616 | tf_op jit(solution)/shard_map/pallas_call | solution.py:136
  171.2 12.9 %shard_map.101 = bf16[1,2,128,625]{3,2,1,0:T(8,128)(2,1)S(1)} custom-call(s32[4]{0:T(128)S(1)} %get-tuple-element.44.r_at, s32[4]{0:T(128)S(1)} %get-tuple-element.43.c_at, s32[4]{0:T(128)S(1)} %get-tuple-element.42.t_at, s32[4]{0:T(128)S(1)} %get-tuple-element.41.o_at, bf16[16,800,384]{2,1,0:T(8,128)(2,1)} %get-tuple-element.35.rows_ref, ...), custom_call_target="tpu_custom_call" | custom-call | flops 2936012800 | bytes 6127616 | tf_op jit(solution)/shard_map/pallas_call | solution.py:136
  184.1 0.6 collective-permute-start.29
  184.8 1.0 copy.67
  185.7 2.0 copy-done.1
  187.8 12.9 %shard_map.102 = bf16[1,2,128,625]{3,2,1,0:T(8,128)(2,1)S(1)} custom-call(s32[4]{0:T(128)S(1)} %get-tuple-element.40.r_at, s32[4]{0:T(128)S(1)} %get-tuple-element.39.c_at, s32[4]{0:T(128)S(1)} %get-tuple-element.38.t_at, s32[4]{0:T(128)S(1)} %get-tuple-element.37.o_at, bf16[16,800,384]{2,1,0:T(8,128)(2,1)} %get-tuple-element.35.rows_ref, ...), custom_call_target="tpu_custom_call" | custom-call | flops 2936012800 | bytes 6127616 | tf_op jit(solution)/shard_map/pallas_call | solution.py:136
  200.7 1.3 convert_add_fusion
  202.1 1.2 copy.68
  (119 shorter events, 6.1 us)
Async XLA Ops:
  0.0 13.6 %copy-start.31 = (s32[32,3]{0,1:T(4,128)S(1)}, s32[32,3]{0,1:T(4,128)}, u32[]{:S(2)}) copy-start(s32[32,3]{0,1:T(4,128)} %param.12) | copy-start | bytes 1156
  0.0 13.7 %copy-start.32 = (s32[32,4]{0,1:T(4,128)S(1)}, s32[32,4]{0,1:T(4,128)}, u32[]{:S(2)}) copy-start(s32[32,4]{0,1:T(4,128)} %param.13) | copy-start | bytes 1540
  3.5 15.9 %collective-permute-start.19 = (bf16[2,96,625]{2,1,0:T(8,128)(2,1)S(1)}, bf16[2,96,625]{2,1,0:T(8,128)(2,1)S(1)}, u32[]{:S(2)}, u32[]{:S(2)}) collective-permute-start(bf16[2,96,625]{2,1,0:T(8,128)(2,1)S(1)} %get-tuple-element.53), channel_id=1, source_target_pairs={{0,16},{8,24},{16,0},{24,8},{1,17},{9,25},{17,1},{25,9},{2,18},{10... | collective-permute-start | bytes 720008 | tf_op jit(solution)/shard_map/ppermute | solution.py:167
  6.6 13.2 %collective-permute-start.18 = (bf16[2,96,625]{2,1,0:T(8,128)(2,1)S(1)}, bf16[2,96,625]{2,1,0:T(8,128)(2,1)S(1)}, u32[]{:S(2)}, u32[]{:S(2)}) collective-permute-start(bf16[2,96,625]{2,1,0:T(8,128)(2,1)S(1)} %get-tuple-element.53), channel_id=1, source_target_pairs={{0,8},{8,0},{16,24},{24,16},{1,9},{9,1},{17,25},{25,17},{2,10},{10... | collective-permute-start | bytes 720008 | tf_op jit(solution)/shard_map/ppermute | solution.py:167
  8.1 10.8 %collective-permute-start.12 = (bf16[2,96,625]{2,1,0:T(8,128)(2,1)S(1)}, bf16[2,96,625]{2,1,0:T(8,128)(2,1)S(1)}, u32[]{:S(2)}, u32[]{:S(2)}) collective-permute-start(bf16[2,96,625]{2,1,0:T(8,128)(2,1)S(1)} %get-tuple-element.54), channel_id=1, source_target_pairs={{0,2},{1,3},{2,4},{3,5},{4,6},{5,7},{6,0},{7,1},{8,10},{9,11},{10,... | collective-permute-start | bytes 720008 | tf_op jit(solution)/shard_map/ppermute | solution.py:184
  9.6 18.2 %collective-permute-start.6 = (bf16[2,96,625]{2,1,0:T(8,128)(2,1)S(1)}, bf16[2,96,625]{2,1,0:T(8,128)(2,1)}, u32[]{:S(2)}, u32[]{:S(2)}) collective-permute-start(bf16[2,96,625]{2,1,0:T(8,128)(2,1)S(1)} %get-tuple-element.55), channel_id=1, source_target_pairs={{0,4},{1,5},{2,6},{3,7},{4,0},{5,1},{6,2},{7,3},{8,12},{9,13},{10,... | collective-permute-start | bytes 720008 | tf_op jit(solution)/shard_map/ppermute | solution.py:184
  12.2 16.2 %collective-permute-start = (bf16[2,96,625]{2,1,0:T(8,128)(2,1)S(1)}, bf16[2,96,625]{2,1,0:T(8,128)(2,1)S(1)}, u32[]{:S(2)}, u32[]{:S(2)}) collective-permute-start(bf16[2,96,625]{2,1,0:T(8,128)(2,1)S(1)} %get-tuple-element.56), channel_id=1, source_target_pairs={{0,6},{1,7},{2,0},{3,1},{4,2},{5,3},{6,4},{7,5},{8,14},{9,15},{10,... | collective-permute-start | bytes 720008 | tf_op jit(solution)/shard_map/ppermute | solution.py:184
  18.9 12.8 %copy-start.28 = (bf16[2,96,625]{2,1,0:T(8,128)(2,1)}, bf16[2,96,625]{2,1,0:T(8,128)(2,1)S(1)}, u32[]{:S(2)}) copy-start(bf16[2,96,625]{2,1,0:T(8,128)(2,1)S(1)} %collective-permute-done.12) | copy-start | bytes 720004
  18.9 12.3 %collective-permute-start.14 = (bf16[2,96,625]{2,1,0:T(8,128)(2,1)S(1)}, bf16[2,96,625]{2,1,0:T(8,128)(2,1)S(1)}, u32[]{:S(2)}, u32[]{:S(2)}) collective-permute-start(bf16[2,96,625]{2,1,0:T(8,128)(2,1)S(1)} %collective-permute-done.12), channel_id=1, source_target_pairs={{0,16},{8,24},{16,0},{24,8},{1,17},{9,25},{17,1},{25,9},{2,18},{10... | collective-permute-start | bytes 720008 | tf_op jit(solution)/shard_map/ppermute | solution.py:167
  19.4 12.3 %collective-permute-start.13 = (bf16[2,96,625]{2,1,0:T(8,128)(2,1)S(1)}, bf16[2,96,625]{2,1,0:T(8,128)(2,1)S(1)}, u32[]{:S(2)}, u32[]{:S(2)}) collective-permute-start(bf16[2,96,625]{2,1,0:T(8,128)(2,1)S(1)} %collective-permute-done.12), channel_id=1, source_target_pairs={{0,8},{8,0},{16,24},{24,16},{1,9},{9,1},{17,25},{25,17},{2,10},{10... | collective-permute-start | bytes 720008 | tf_op jit(solution)/shard_map/ppermute | solution.py:167
  19.8 9.8 %collective-permute-start.20 = (bf16[1,96,625]{2,1,0:T(8,128)(2,1)S(1)}, bf16[1,96,625]{2,1,0:T(8,128)(2,1)}, u32[]{:S(2)}, u32[]{:S(2)}) collective-permute-start(bf16[1,96,625]{2,1,0:T(8,128)(2,1)S(1)} %slice.138), channel_id=1, source_target_pairs={{0,8},{8,0},{16,24},{24,16},{1,9},{9,1},{17,25},{25,17},{2,10},{10... | collective-permute-start | bytes 360008 | tf_op jit(solution)/shard_map/ppermute | solution.py:167
  27.8 9.0 %collective-permute-start.7 = (bf16[2,96,625]{2,1,0:T(8,128)(2,1)}, bf16[2,96,625]{2,1,0:T(8,128)(2,1)S(1)}, u32[]{:S(2)}, u32[]{:S(2)}) collective-permute-start(bf16[2,96,625]{2,1,0:T(8,128)(2,1)} %collective-permute-done.6), channel_id=1, source_target_pairs={{0,8},{8,0},{16,24},{24,16},{1,9},{9,1},{17,25},{25,17},{2,10},{10... | collective-permute-start | bytes 720008 | tf_op jit(solution)/shard_map/ppermute | solution.py:167
  28.4 25.3 %copy-start.27 = (bf16[2,96,625]{2,1,0:T(8,128)(2,1)}, bf16[2,96,625]{2,1,0:T(8,128)(2,1)S(1)}, u32[]{:S(2)}) copy-start(bf16[2,96,625]{2,1,0:T(8,128)(2,1)S(1)} %collective-permute-done) | copy-start | bytes 720004
  28.4 6.3 %collective-permute-start.21 = (bf16[1,96,625]{2,1,0:T(8,128)(2,1)S(1)}, bf16[1,96,625]{2,1,0:T(8,128)(2,1)S(1)}, u32[]{:S(2)}, u32[]{:S(2)}) collective-permute-start(bf16[1,96,625]{2,1,0:T(8,128)(2,1)S(1)} %slice.139), channel_id=1, source_target_pairs={{0,16},{8,24},{16,0},{24,8},{1,17},{9,25},{17,1},{25,9},{2,18},{10... | collective-permute-start | bytes 360008 | tf_op jit(solution)/shard_map/ppermute | solution.py:167
  29.6 12.3 %collective-permute-start.8 = (bf16[2,96,625]{2,1,0:T(8,128)(2,1)}, bf16[2,96,625]{2,1,0:T(8,128)(2,1)S(1)}, u32[]{:S(2)}, u32[]{:S(2)}) collective-permute-start(bf16[2,96,625]{2,1,0:T(8,128)(2,1)} %collective-permute-done.6), channel_id=1, source_target_pairs={{0,16},{8,24},{16,0},{24,8},{1,17},{9,25},{17,1},{25,9},{2,18},{10... | collective-permute-start | bytes 720008 | tf_op jit(solution)/shard_map/ppermute | solution.py:167
  31.2 3.2 %copy-start.21 = (bf16[2,96,625]{2,1,0:T(8,128)(2,1)}, bf16[2,96,625]{2,1,0:T(8,128)(2,1)S(1)}, u32[]{:S(2)}) copy-start(bf16[2,96,625]{2,1,0:T(8,128)(2,1)S(1)} %collective-permute-done.14) | copy-start | bytes 720004
  31.2 19.8 %collective-permute-start.2 = (bf16[2,96,625]{2,1,0:T(8,128)(2,1)S(1)}, bf16[2,96,625]{2,1,0:T(8,128)(2,1)S(1)}, u32[]{:S(2)}, u32[]{:S(2)}) collective-permute-start(bf16[2,96,625]{2,1,0:T(8,128)(2,1)S(1)} %collective-permute-done), channel_id=1, source_target_pairs={{0,16},{8,24},{16,0},{24,8},{1,17},{9,25},{17,1},{25,9},{2,18},{10... | collective-permute-start | bytes 720008 | tf_op jit(solution)/shard_map/ppermute | solution.py:167
  31.7 2.7 %copy-start.23 = (bf16[2,96,625]{2,1,0:T(8,128)(2,1)}, bf16[2,96,625]{2,1,0:T(8,128)(2,1)S(1)}, u32[]{:S(2)}) copy-start(bf16[2,96,625]{2,1,0:T(8,128)(2,1)S(1)} %collective-permute-done.13) | copy-start | bytes 720004
  31.7 22.0 %collective-permute-start.1 = (bf16[2,96,625]{2,1,0:T(8,128)(2,1)S(1)}, bf16[2,96,625]{2,1,0:T(8,128)(2,1)S(1)}, u32[]{:S(2)}, u32[]{:S(2)}) collective-permute-start(bf16[2,96,625]{2,1,0:T(8,128)(2,1)S(1)} %collective-permute-done), channel_id=1, source_target_pairs={{0,8},{8,0},{16,24},{24,16},{1,9},{9,1},{17,25},{25,17},{2,10},{10... | collective-permute-start | bytes 720008 | tf_op jit(solution)/shard_map/ppermute | solution.py:167
  34.4 7.5 %copy-start.16 = (bf16[2,128,625]{1,0,2:T(2,128)(2,1)S(1)}, bf16[2,128,625]{1,0,2:T(2,128)(2,1)}, u32[]{:S(2)}) copy-start(bf16[2,128,625]{1,0,2:T(2,128)(2,1)} %param.10) | copy-start | bytes 960004
  34.7 2.2 %copy-start.30 = (bf16[1,96,625]{2,1,0:T(8,128)(2,1)}, bf16[1,96,625]{2,1,0:T(8,128)(2,1)S(1)}, u32[]{:S(2)}) copy-start(bf16[1,96,625]{2,1,0:T(8,128)(2,1)S(1)} %collective-permute-done.21) | copy-start | bytes 360004
  34.7 19.9 %collective-permute-start.15 = (bf16[1,96,625]{2,1,0:T(8,128)(2,1)}, bf16[1,96,625]{2,1,0:T(8,128)(2,1)}, u32[]{:S(2)}, u32[]{:S(2)}) collective-permute-start(bf16[1,96,625]{2,1,0:T(8,128)(2,1)} %slice.136), channel_id=1, source_target_pairs={{0,8},{8,0},{16,24},{24,16},{1,9},{9,1},{17,25},{25,17},{2,10},{10... | collective-permute-start | bytes 360008 | tf_op jit(solution)/shard_map/ppermute | solution.py:167
  36.9 5.0 %copy-start.22 = (bf16[2,96,625]{2,1,0:T(8,128)(2,1)}, bf16[2,96,625]{2,1,0:T(8,128)(2,1)S(1)}, u32[]{:S(2)}) copy-start(bf16[2,96,625]{2,1,0:T(8,128)(2,1)S(1)} %collective-permute-done.7) | copy-start | bytes 720004
  36.9 18.9 %collective-permute-start.16 = (bf16[1,96,625]{2,1,0:T(8,128)(2,1)S(1)}, bf16[1,96,625]{2,1,0:T(8,128)(2,1)}, u32[]{:S(2)}, u32[]{:S(2)}) collective-permute-start(bf16[1,96,625]{2,1,0:T(8,128)(2,1)S(1)} %slice.137), channel_id=1, source_target_pairs={{0,16},{8,24},{16,0},{24,8},{1,17},{9,25},{17,1},{25,9},{2,18},{10... | collective-permute-start | bytes 360008 | tf_op jit(solution)/shard_map/ppermute | solution.py:167
  38.4 17.4 %copy-start.9 = (bf16[2,384,625]{2,1,0:T(8,128)(2,1)}, bf16[2,384,625]{2,1,0:T(8,128)(2,1)S(1)}, u32[]{:S(2)}) copy-start(bf16[2,384,625]{2,1,0:T(8,128)(2,1)S(1)} %maximum_maximum_fusion.3.tile_ref) | copy-start | bytes 2880004
  41.9 11.8 %copy-start.26 = (bf16[2,96,625]{2,1,0:T(8,128)(2,1)}, bf16[2,96,625]{2,1,0:T(8,128)(2,1)S(1)}, u32[]{:S(2)}) copy-start(bf16[2,96,625]{2,1,0:T(8,128)(2,1)S(1)} %collective-permute-done.8) | copy-start | bytes 720004
  41.9 29.7 %collective-permute-start.24 = (bf16[2,128,625]{1,0,2:T(2,128)(2,1)S(1)}, bf16[2,128,625]{1,0,2:T(2,128)(2,1)S(1)}, u32[]{:S(2)}, u32[]{:S(2)}) collective-permute-start(bf16[2,128,625]{1,0,2:T(2,128)(2,1)S(1)} %copy-done.16), channel_id=1, source_target_pairs={{0,4},{1,5},{2,6},{3,7},{4,0},{5,1},{6,2},{7,3},{8,12},{9,13},{10,... | collective-permute-start | bytes 960008 | tf_op jit(solution)/shard_map/ppermute | solution.py:184
  50.9 4.9 %copy-start.24 = (bf16[2,96,625]{2,1,0:T(8,128)(2,1)}, bf16[2,96,625]{2,1,0:T(8,128)(2,1)S(1)}, u32[]{:S(2)}) copy-start(bf16[2,96,625]{2,1,0:T(8,128)(2,1)S(1)} %collective-permute-done.2) | copy-start | bytes 720004
  50.9 20.8 %collective-permute-start.25 = (bf16[2,128,625]{1,0,2:T(2,128)(2,1)S(1)}, bf16[2,128,625]{1,0,2:T(2,128)(2,1)S(1)}, u32[]{:S(2)}, u32[]{:S(2)}) collective-permute-start(bf16[2,128,625]{1,0,2:T(2,128)(2,1)S(1)} %copy-done.16), channel_id=1, source_target_pairs={{0,6},{1,7},{2,0},{3,1},{4,2},{5,3},{6,4},{7,5},{8,14},{9,15},{10,... | collective-permute-start | bytes 960008 | tf_op jit(solution)/shard_map/ppermute | solution.py:184
  53.7 2.1 %copy-start.25 = (bf16[2,96,625]{2,1,0:T(8,128)(2,1)}, bf16[2,96,625]{2,1,0:T(8,128)(2,1)S(1)}, u32[]{:S(2)}) copy-start(bf16[2,96,625]{2,1,0:T(8,128)(2,1)S(1)} %collective-permute-done.1) | copy-start | bytes 720004
  53.7 18.4 %collective-permute-start.23 = (bf16[2,128,625]{1,0,2:T(2,128)(2,1)S(1)}, bf16[2,128,625]{1,0,2:T(2,128)(2,1)S(1)}, u32[]{:S(2)}, u32[]{:S(2)}) collective-permute-start(bf16[2,128,625]{1,0,2:T(2,128)(2,1)S(1)} %copy-done.16), channel_id=1, source_target_pairs={{0,2},{1,3},{2,4},{3,5},{4,6},{5,7},{6,0},{7,1},{8,10},{9,11},{10,... | collective-permute-start | bytes 960008 | tf_op jit(solution)/shard_map/ppermute | solution.py:184
  54.6 5.9 %collective-permute-start.10 = (bf16[1,96,625]{2,1,0:T(8,128)(2,1)}, bf16[1,96,625]{2,1,0:T(8,128)(2,1)}, u32[]{:S(2)}, u32[]{:S(2)}) collective-permute-start(bf16[1,96,625]{2,1,0:T(8,128)(2,1)} %slice.135), channel_id=1, source_target_pairs={{0,16},{8,24},{16,0},{24,8},{1,17},{9,25},{17,1},{25,9},{2,18},{10... | collective-permute-start | bytes 360008 | tf_op jit(solution)/shard_map/ppermute | solution.py:167
  55.8 6.2 %copy-start.29 = (bf16[1,96,625]{2,1,0:T(8,128)(2,1)S(1)}, bf16[1,96,625]{2,1,0:T(8,128)(2,1)}, u32[]{:S(2)}) copy-start(bf16[1,96,625]{2,1,0:T(8,128)(2,1)} %slice.133) | copy-start | bytes 360004
  55.8 6.2 %collective-permute-start.9 = (bf16[1,96,625]{2,1,0:T(8,128)(2,1)}, bf16[1,96,625]{2,1,0:T(8,128)(2,1)}, u32[]{:S(2)}, u32[]{:S(2)}) collective-permute-start(bf16[1,96,625]{2,1,0:T(8,128)(2,1)} %slice.134), channel_id=1, source_target_pairs={{0,8},{8,0},{16,24},{24,16},{1,9},{9,1},{17,25},{25,17},{2,10},{10... | collective-permute-start | bytes 360008 | tf_op jit(solution)/shard_map/ppermute | solution.py:167
  57.8 9.0 %copy-start.5 = (bf16[2,384,625]{2,1,0:T(8,128)(2,1)}, bf16[2,384,625]{2,1,0:T(8,128)(2,1)S(1)}, u32[]{:S(2)}) copy-start(bf16[2,384,625]{2,1,0:T(8,128)(2,1)S(1)} %maximum_maximum_fusion.2.tile_ref) | copy-start | bytes 2880004
  60.5 6.4 %collective-permute-start.3 = (bf16[1,96,625]{2,1,0:T(8,128)(2,1)}, bf16[1,96,625]{2,1,0:T(8,128)(2,1)}, u32[]{:S(2)}, u32[]{:S(2)}) collective-permute-start(bf16[1,96,625]{2,1,0:T(8,128)(2,1)} %slice.132), channel_id=1, source_target_pairs={{0,8},{8,0},{16,24},{24,16},{1,9},{9,1},{17,25},{25,17},{2,10},{10... | collective-permute-start | bytes 360008 | tf_op jit(solution)/shard_map/ppermute | solution.py:167
  62.0 5.0 %collective-permute-start.4 = (bf16[1,96,625]{2,1,0:T(8,128)(2,1)S(1)}, bf16[1,96,625]{2,1,0:T(8,128)(2,1)}, u32[]{:S(2)}, u32[]{:S(2)}) collective-permute-start(bf16[1,96,625]{2,1,0:T(8,128)(2,1)S(1)} %copy-done.29), channel_id=1, source_target_pairs={{0,16},{8,24},{16,0},{24,8},{1,17},{9,25},{17,1},{25,9},{2,18},{10... | collective-permute-start | bytes 360008 | tf_op jit(solution)/shard_map/ppermute | solution.py:167
  66.9 18.9 %collective-permute-start.22 = (bf16[2,384,625]{1,0,2:T(2,128)(2,1)}, bf16[2,384,625]{1,0,2:T(2,128)(2,1)}, u32[]{:S(2)}, u32[]{:S(2)}) collective-permute-start(bf16[2,384,625]{1,0,2:T(2,128)(2,1)} %copy.61), channel_id=1, source_target_pairs={{0,1},{1,0},{2,3},{3,2},{4,5},{5,4},{6,7},{7,6},{8,9},{9,8},{10,11... | collective-permute-start | bytes 2880008 | tf_op jit(solution)/shard_map/ppermute | solution.py:181
  67.0 31.3 %collective-permute-start.17 = (bf16[2,384,625]{1,0,2:T(2,128)(2,1)}, bf16[2,384,625]{1,0,2:T(2,128)(2,1)}, u32[]{:S(2)}, u32[]{:S(2)}) collective-permute-start(bf16[2,384,625]{1,0,2:T(2,128)(2,1)} %copy.60), channel_id=1, source_target_pairs={{0,1},{1,0},{2,3},{3,2},{4,5},{5,4},{6,7},{7,6},{8,9},{9,8},{10,11... | collective-permute-start | bytes 2880008 | tf_op jit(solution)/shard_map/ppermute | solution.py:181
  68.8 3.3 %copy-start.7 = (bf16[2,384,625]{2,1,0:T(8,128)(2,1)}, bf16[2,384,625]{2,1,0:T(8,128)(2,1)S(1)}, u32[]{:S(2)}) copy-start(bf16[2,384,625]{2,1,0:T(8,128)(2,1)S(1)} %maximum_maximum_fusion.tile_ref) | copy-start | bytes 2880004
  71.6 0.7 copy-start.17
  71.6 30.9 %collective-permute-start.11 = (bf16[2,384,625]{1,0,2:T(2,128)(2,1)}, bf16[2,384,625]{1,0,2:T(2,128)(2,1)}, u32[]{:S(2)}, u32[]{:S(2)}) collective-permute-start(bf16[2,384,625]{1,0,2:T(2,128)(2,1)} %copy.59), channel_id=1, source_target_pairs={{0,1},{1,0},{2,3},{3,2},{4,5},{5,4},{6,7},{7,6},{8,9},{9,8},{10,11... | collective-permute-start | bytes 2880008 | tf_op jit(solution)/shard_map/ppermute | solution.py:181
  71.7 0.7 copy-start.18
  71.7 34.8 %collective-permute-start.5 = (bf16[2,384,625]{1,0,2:T(2,128)(2,1)}, bf16[2,384,625]{1,0,2:T(2,128)(2,1)}, u32[]{:S(2)}, u32[]{:S(2)}) collective-permute-start(bf16[2,384,625]{1,0,2:T(2,128)(2,1)} %copy.58), channel_id=1, source_target_pairs={{0,1},{1,0},{2,3},{3,2},{4,5},{5,4},{6,7},{7,6},{8,9},{9,8},{10,11... | collective-permute-start | bytes 2880008 | tf_op jit(solution)/shard_map/ppermute | solution.py:181
  72.1 0.7 copy-start.19
  72.8 9.3 %copy-start.2 = (bf16[625,896]{1,0:T(8,128)(2,1)S(1)}, bf16[625,896]{1,0:T(8,128)(2,1)}, u32[]{:S(2)}) copy-start(bf16[625,896]{1,0:T(8,128)(2,1)} %constant.112.clone.lanes_of_ref) | copy-start | bytes 3360004
  72.8 9.3 %copy-start.3 = (bf16[800,625]{1,0:T(8,128)(2,1)S(1)}, bf16[800,625]{1,0:T(8,128)(2,1)}, u32[]{:S(2)}) copy-start(bf16[800,625]{1,0:T(8,128)(2,1)} %constant.111.clone.rows_of_ref) | copy-start | bytes 3000004
  72.8 9.3 %copy-start.10 = (bf16[2,384,625]{2,1,0:T(8,128)(2,1)S(1)}, bf16[2,384,625]{2,1,0:T(8,128)(2,1)}, u32[]{:S(2)}) copy-start(bf16[2,384,625]{2,1,0:T(8,128)(2,1)} %copy-done.9) | copy-start | bytes 2880004
  77.5 52.9 %collective-permute-start.26 = (bf16[4,2,128,625]{2,1,3,0:T(2,128)(2,1)}, bf16[4,2,128,625]{2,1,3,0:T(2,128)(2,1)}, u32[]{:S(2)}, u32[]{:S(2)}) collective-permute-start(bf16[4,2,128,625]{2,1,3,0:T(2,128)(2,1)} %pad_maximum_fusion.1), channel_id=1, source_target_pairs={{0,1},{1,0},{2,3},{3,2},{4,5},{5,4},{6,7},{7,6},{8,9},{9,8},{10,11... | collective-permute-start | bytes 3840008 | tf_op jit(solution)/shard_map/ppermute | solution.py:181
  89.9 1.2 copy-start.14
  91.1 3.6 %copy-start.6 = (bf16[2,384,625]{2,1,0:T(8,128)(2,1)S(1)}, bf16[2,384,625]{2,1,0:T(8,128)(2,1)}, u32[]{:S(2)}) copy-start(bf16[2,384,625]{2,1,0:T(8,128)(2,1)} %copy-done.5) | copy-start | bytes 2880004
  110.6 1.2 copy-start.13
  115.4 3.7 %copy-start.12 = (bf16[2,384,625]{2,1,0:T(8,128)(2,1)S(1)}, bf16[2,384,625]{2,1,0:T(8,128)(2,1)}, u32[]{:S(2)}) copy-start(bf16[2,384,625]{2,1,0:T(8,128)(2,1)} %copy.64.tile_ref) | copy-start | bytes 2880004
  119.1 3.7 %copy-start.8 = (bf16[2,384,625]{2,1,0:T(8,128)(2,1)S(1)}, bf16[2,384,625]{2,1,0:T(8,128)(2,1)}, u32[]{:S(2)}) copy-start(bf16[2,384,625]{2,1,0:T(8,128)(2,1)} %copy-done.7) | copy-start | bytes 2880004
  122.8 3.6 %copy-start.11 = (bf16[2,384,625]{2,1,0:T(8,128)(2,1)S(1)}, bf16[2,384,625]{2,1,0:T(8,128)(2,1)}, u32[]{:S(2)}) copy-start(bf16[2,384,625]{2,1,0:T(8,128)(2,1)} %copy.65.tile_ref) | copy-start | bytes 2880004
  126.5 3.9 %copy-start.15 = (bf16[4,1,2,128,625]{3,2,4,0,1:T(2,128)(2,1)S(1)}, bf16[4,1,2,128,625]{3,2,4,0,1:T(2,128)(2,1)}, u32[]{:S(2)}) copy-start(bf16[4,1,2,128,625]{3,2,4,0,1:T(2,128)(2,1)} %fusion.12) | copy-start | bytes 3840004
  135.5 1.3 copy-start.33
  136.7 3.8 %copy-start.4 = (bf16[896,625]{1,0:T(8,128)(2,1)S(1)}, bf16[896,625]{1,0:T(8,128)(2,1)}, u32[]{:S(2)}) copy-start(bf16[896,625]{1,0:T(8,128)(2,1)} %constant.114.clone.back_ref) | copy-start | bytes 3360004
  140.5 30.7 %copy-start = (bf16[16,128,896]{2,1,0:T(8,128)(2,1)}, bf16[16,128,896]{2,1,0:T(8,128)(2,1)S(1)}, u32[]{:S(2)}) copy-start(bf16[16,128,896]{2,1,0:T(8,128)(2,1)S(1)} %convolution_convert_fusion.amp_ref) | copy-start | bytes 11010052
  154.1 46.6 %collective-permute-start.27 = (bf16[2,128,625]{2,1,0:T(8,128)(2,1)S(1)}, bf16[2,128,625]{2,1,0:T(8,128)(2,1)}, u32[]{:S(2)}, u32[]{:S(2)}) collective-permute-start(bf16[2,128,625]{2,1,0:T(8,128)(2,1)S(1)} %bitcast.34), channel_id=1, source_target_pairs={{0,6},{1,7},{2,0},{3,1},{4,2},{5,3},{6,4},{7,5},{8,14},{9,15},{10,... | collective-permute-start | bytes 960008 | tf_op jit(solution)/shard_map/ppermute | solution.py:184
  171.1 29.5 %collective-permute-start.28 = (bf16[2,128,625]{2,1,0:T(8,128)(2,1)S(1)}, bf16[2,128,625]{2,1,0:T(8,128)(2,1)}, u32[]{:S(2)}, u32[]{:S(2)}) collective-permute-start(bf16[2,128,625]{2,1,0:T(8,128)(2,1)S(1)} %bitcast.35), channel_id=1, source_target_pairs={{0,4},{1,5},{2,6},{3,7},{4,0},{5,1},{6,2},{7,3},{8,12},{9,13},{10,... | collective-permute-start | bytes 960008 | tf_op jit(solution)/shard_map/ppermute | solution.py:184
  171.2 13.5 %copy-start.20 = (f32[2,128,625]{1,0,2:T(2,128)S(1)}, f32[2,128,625]{1,0,2:T(2,128)}, u32[]{:S(2)}) copy-start(f32[2,128,625]{1,0,2:T(2,128)} %param.11) | copy-start | bytes 1920004
  184.1 16.6 %collective-permute-start.29 = (bf16[2,128,625]{2,1,0:T(8,128)(2,1)S(1)}, bf16[2,128,625]{2,1,0:T(8,128)(2,1)}, u32[]{:S(2)}, u32[]{:S(2)}) collective-permute-start(bf16[2,128,625]{2,1,0:T(8,128)(2,1)S(1)} %bitcast.36), channel_id=1, source_target_pairs={{0,2},{1,3},{2,4},{3,5},{4,6},{5,7},{6,0},{7,1},{8,10},{9,11},{10,... | collective-permute-start | bytes 960008 | tf_op jit(solution)/shard_map/ppermute | solution.py:184
  185.7 2.0 %copy-start.1 = (bf16[16,128,896]{2,1,0:T(8,128)(2,1)S(1)}, bf16[16,128,896]{2,1,0:T(8,128)(2,1)}, u32[]{:S(2)}) copy-start(bf16[16,128,896]{2,1,0:T(8,128)(2,1)} %copy-done) | copy-start | bytes 11010052

commit v2 on v0

v2 whole, which is shorter than its diff:
```python
import functools

import jax
import jax.numpy as jnp
import numpy as np
from jax import lax
from jax.experimental import pallas as pl
from jax.experimental.pallas import tpu as pltpu
from jax.sharding import PartitionSpec as P

TV = 25
PAD = 32
GROUP = 4
LANES = PAD * GROUP
GROUPS = -(-TV // GROUP)
ROWS = TV * PAD
WIDE = GROUPS * LANES
ORDER = [x for g in range(GROUP) for x in range(g, TV, GROUP)]
START = [ORDER.index(g) * PAD for g in range(GROUP)] + [ROWS]
PLACE = np.argsort(ORDER)
PREPARE_STEPS = 5
BF = jnp.bfloat16
F32 = jnp.float32
VMEM_BYTES = 48 * 1024 * 1024


def spread(spots, rows):
    return (np.arange(rows)[:, None] == spots[None, :]).astype(jnp.bfloat16)


def forms_matrix():
    x, y = np.divmod(np.arange(TV * TV), TV)
    return np.concatenate([spread(PLACE[y] * PAD + x, ROWS), spread(x * PAD + y, ROWS)], axis=0)


def back_matrix():
    a, b = np.divmod(np.arange(TV * TV), TV)
    return spread(PLACE[a] * PAD + b, ROWS).T


def prepare_kernel(pieces, *refs):
    tile_refs, matrix_ref = refs[:pieces], refs[pieces]
    forms_ref, all_ref = refs[-2:]
    count, size, _ = tile_refs[0].shape
    depth = forms_ref.shape[2]

    @pl.when(pl.program_id(0) == 0)
    def _():
        for m in range(count):
            for i, ref in enumerate(tile_refs):
                start = m * depth + i * size
                all_ref[start : start + size, :] = ref[m]

    wide = count if depth % LANES == 0 else 1
    for first in range(0, count, wide):
        made = lax.dot_general(
            matrix_ref[...],
            all_ref[first * depth : (first + wide) * depth, :],
            (((1,), (1,)), ((), ())),
            preferred_element_type=F32,
        ).astype(BF)
        for m in range(wide):
            forms_ref[first + m] = made[:, m * depth : (m + 1) * depth]


def prepare(parts, first, total, matrix, held):
    count, size, width = parts[0].shape
    depth = size * len(parts)
    rows = matrix.shape[0] // PREPARE_STEPS
    in_specs = [pl.BlockSpec(part.shape, lambda i: (0, 0, 0)) for part in parts]
    in_specs.append(pl.BlockSpec((rows, width), lambda i: (i, 0)))
    operands = [*parts, matrix]
    aliases = {}
    if held is not None:
        aliases = {len(operands): 0}
        in_specs.append(pl.BlockSpec(memory_space=pl.ANY))
        operands.append(held)
    return pl.pallas_call(
        functools.partial(prepare_kernel, len(parts)),
        out_shape=jax.ShapeDtypeStruct((total, matrix.shape[0], depth), BF),
        grid=(PREPARE_STEPS,),
        in_specs=in_specs,
        out_specs=pl.BlockSpec((count, rows, depth), lambda i: (first, i, 0)),
        scratch_shapes=[pltpu.VMEM((count * depth, width), BF)],
        input_output_aliases=aliases,
        compiler_params=pltpu.CompilerParams(vmem_limit_bytes=VMEM_BYTES),
        cost_estimate=pl.CostEstimate(
            flops=2 * count * depth * width * matrix.shape[0],
            bytes_accessed=2 * count * depth * (width + matrix.shape[0]),
            transcendentals=0,
        ),
    )(*operands)


def turned(ref, groups, by):
    numbers = [min(A * GROUP + (p - by) % GROUP, TV - 1) for A in groups for p in range(GROUP)]
    return jnp.concatenate([ref[x * PAD : (x + 1) * PAD, :] for x in numbers], axis=0)


def ladder_kernel(
    c_at, r_at, t_at, core_at, o_at, c_ref, r_ref, mine_ref, other_ref, back_ref, matrix_ref, out_ref, *scratch
):
    v_ref, u_ref, amp_ref, acc_ref = scratch[:4]
    step, steps = pl.program_id(1), pl.num_programs(1)
    at = pl.program_id(0) * steps + step

    @pl.when(step == 0)
    def _():
        acc_ref[...] = jnp.zeros_like(acc_ref)

    @pl.when(core_at[at] == 0)
    def _():
        amp_ref[...] = mine_ref[0]

    @pl.when(core_at[at] != 0)
    def _():
        amp_ref[...] = other_ref[0]

    if len(scratch) > 4:
        forms = scratch[4]
        for i, tile_ref in enumerate((c_ref, r_ref)):
            forms[i] = lax.dot_general(
                matrix_ref[i * ROWS : (i + 1) * ROWS, :],
                tile_ref[0],
                (((1,), (1,)), ((), ())),
                preferred_element_type=F32,
            ).astype(BF)
        c_form, r_form = forms.at[0], forms.at[1]
    else:
        c_form, r_form = c_ref.at[0], r_ref.at[0]

    spot = lax.broadcasted_iota(jnp.int32, (PAD, LANES), 1) // PAD
    at_spot = [spot == p for p in range(GROUP)]
    nothing = jnp.zeros((PAD, LANES), F32)
    for first in range(0, GROUPS, 2):
        groups = range(first, min(first + 2, GROUPS))
        lanes = slice(groups[0] * LANES, (groups[-1] + 1) * LANES)
        for g in range(GROUP):
            v_ref[START[g] : START[g + 1], lanes] = lax.dot_general(
                c_form[START[g] : START[g + 1], :],
                turned(r_form, groups, g),
                (((1,), (1,)), ((), ())),
                preferred_element_type=F32,
            )
        for A in groups:
            for D in range(GROUPS):
                blocks = [
                    v_ref[START[g] + D * PAD : START[g] + (D + 1) * PAD, A * LANES : (A + 1) * LANES]
                    if D * GROUP + g < TV
                    else nothing
                    for g in range(GROUP)
                ]
                for i in range(min(GROUP, TV - A * GROUP)):
                    block = blocks[-i % GROUP]
                    for p in range(1, GROUP):
                        block = jnp.where(at_spot[p], blocks[(p - i) % GROUP], block)
                    u_ref[START[i] + A * PAD : START[i] + (A + 1) * PAD, D * LANES : (D + 1) * LANES] = block.astype(BF)
    for i in range(GROUP):
        acc_ref[o_at[at], START[i] : START[i + 1], :] += jnp.dot(
            u_ref[START[i] : START[i + 1], :], turned(amp_ref, range(GROUPS), i), preferred_element_type=F32
        )

    @pl.when(step == steps - 1)
    def _():
        for m in range(acc_ref.shape[0]):
            out_ref[0, m] = jnp.dot(back_ref[...], acc_ref[m].astype(BF), preferred_element_type=F32).astype(BF)


def ladders(places, tiles, amps, back, matrix, blocks_here):
    columns, tasks, kinds = places.shape
    pairs = amps[0].shape[2]
    made = tiles.shape[1] == 2 * ROWS
    depth = tiles.shape[2] if made else tiles.shape[1]
    held = (1, ROWS, depth) if made else (1, *tiles.shape[1:])
    more = [] if made else [pltpu.VMEM((2, ROWS, depth), BF)]
    matrix = matrix[:PAD] if made else matrix
    tables = [places[:, :, i].reshape(-1) for i in range(kinds)]
    amp_spec = pl.BlockSpec((1, ROWS, pairs), lambda i, j, c, r, t, k, o: (t[i * tasks + j], 0, 0))
    return pl.pallas_call(
        ladder_kernel,
        out_shape=jax.ShapeDtypeStruct((columns, blocks_here, TV * TV, pairs), BF),
        grid_spec=pltpu.PrefetchScalarGridSpec(
            num_scalar_prefetch=kinds,
            grid=(columns, tasks),
            in_specs=[
                pl.BlockSpec(held, lambda i, j, c, r, t, k, o: (c[i * tasks + j], 0, 0)),
                pl.BlockSpec(held, lambda i, j, c, r, t, k, o: (r[i * tasks + j], int(made), 0)),
                amp_spec,
                amp_spec,
                pl.BlockSpec(back.shape, lambda i, j, c, r, t, k, o: (0, 0)),
                pl.BlockSpec(matrix.shape, lambda i, j, c, r, t, k, o: (0, 0)),
            ],
            out_specs=pl.BlockSpec((1, blocks_here, TV * TV, pairs), lambda i, j, c, r, t, k, o: (i, 0, 0, 0)),
            scratch_shapes=[
                pltpu.VMEM((ROWS, WIDE), F32),
                pltpu.VMEM((ROWS, WIDE), BF),
                pltpu.VMEM((ROWS, pairs), BF),
                pltpu.VMEM((blocks_here, ROWS, pairs), F32),
                *more,
            ],
        ),
        compiler_params=pltpu.CompilerParams(vmem_limit_bytes=VMEM_BYTES),
        cost_estimate=pl.CostEstimate(
            flops=2 * columns * tasks * ROWS * WIDE * (depth + pairs),
            bytes_accessed=2 * columns * tasks * ROWS * 2 * (depth + pairs),
            transcendentals=0,
        ),
    )(*tables, tiles, tiles, *amps, back, matrix)


def gather_pairs(part, by, pair_count):
    beside = lambda x, bit: lax.ppermute(x, "pair", [(p, p ^ bit) for p in range(pair_count)])
    across, along = beside(part, 1), beside(part, 2)
    return [part, across, along, beside(along, 1) if by % 2 == 0 else beside(across, 2)]


def per_device(factor_blocks, amplitudes, residual_in, task_owners, task_local):
    pair_count = lax.axis_size("pair")
    task_count = lax.axis_size("task")
    column = lax.axis_index("task")
    blocks_here, depth_here, _ = factor_blocks.shape
    pairs = amplitudes.shape[1]
    levels = task_count // 2
    level, core = column // 2, column % 2
    depth = depth_here // levels
    other_core = lambda x: lax.ppermute(x, "task", [(c, c ^ 1) for c in range(task_count)])

    def up(x, by):
        return lax.ppermute(x, "task", [(c, (c + 2 * by) % task_count) for c in range(task_count)])

    same_core = [[2 * z + k for z in range(levels)] for k in range(2)]
    tiles = amplitudes.reshape(blocks_here, pairs, TV, TV).transpose(0, 3, 2, 1)
    tiles = jnp.pad(tiles, ((0, 0), (0, 0), (0, PAD - TV), (0, 0))).reshape(blocks_here, ROWS, pairs)
    amps = lax.all_gather(tiles, "task", axis=0, tiled=True, axis_index_groups=same_core)
    amps = (amps, other_core(amps))

    matrix = jnp.asarray(forms_matrix())
    back = jnp.asarray(back_matrix())
    slices = factor_blocks.reshape(blocks_here, levels, depth, -1)
    mine = [lax.dynamic_index_in_dim(slices, (level + by) % levels, 1, keepdims=False) for by in range(levels)]
    parts = [mine[0]] + [up(mine[by], by) for by in range(1, levels)]

    total = 2 * levels * blocks_here
    if pair_count == 4:
        held = None
        for by, part in enumerate(parts):
            pieces = gather_pairs(part, by, pair_count)
            held = prepare(pieces, 2 * by, total, matrix, held)
            held = prepare([other_core(piece) for piece in pieces], 2 * by + 1, total, matrix, held)
    else:
        held = lax.all_gather(jnp.stack(parts), "pair", axis=2, tiled=True)
        held = jnp.stack([held, other_core(held)], axis=1).reshape(total, depth * pair_count, -1)

    owners = lax.dynamic_index_in_dim(task_owners.reshape(levels, 2, -1, 3), core, 1, keepdims=False)
    local = lax.dynamic_index_in_dim(task_local.reshape(levels, 2, -1, 4), core, 1, keepdims=False)
    owner_level, far_core = owners // 2, (owners % 2 != core).astype(jnp.int32)
    factor_at = (((level - owner_level) % levels) * 2 + far_core) * blocks_here + local[:, :, :3]
    amp_at = owner_level[:, :, 2:] * blocks_here + local[:, :, 2:3]
    places = jnp.concatenate(
        [factor_at[:, :, 1:2], factor_at[:, :, :1], amp_at, far_core[:, :, 2:], local[:, :, 3:]], axis=2
    ).astype(jnp.int32)
    places = places[(level + jnp.arange(levels)) % levels]

    ladder = None
    calls = min(levels, 4)
    width = levels // calls
    for call in reversed(range(calls)):
        sums = ladders(places[call * width : (call + 1) * width], held, amps, back, matrix, blocks_here)
        for i in range(width):
            by = call * width + i
            term = (up(sums[i], by) if by else sums[i]).astype(F32)
            ladder = term if ladder is None else ladder + term
    return residual_in + ladder.transpose(0, 2, 1)


def solution(mesh):
    placed = (P("task", "pair", None), P("task", "pair", None), P("task", "pair", None), P(), P())
    return jax.shard_map(
        per_device, mesh=mesh, in_specs=placed, out_specs=P("task", "pair", None), check_vma=False
    )
```

time: 242 us -> 184 us (0.76)
  waiting for transfers between devices: 157 us -> 47.6 us
  Pallas kernels: 0 us -> 78 us
  local copies, waits for them, and re-layouts: 49.5 us -> 14.8 us
  starting transfers between devices: 12.4 us -> 26 us
  matrix products: 6.76 us -> 0 us
    all_gather x2 -> x1, waiting for transfers between devices: 105 us -> 18.2 us  [per_device(): lax.all_gather(tiles, 'task', axis=0, tiled=True, axis_index_groups=same_...]
    pallas_call x0 -> x12, Pallas kernels: none -> 78 us  [the longest x8 40 us: prepare(): pl.pallas_call(functools.partial(prepare_kernel, len(parts)), out_shape=j...]
    all_to_all x3 -> x0, waiting for transfers between devices: 52.2 us -> none  [the longest x1 43.4 us: per_device(): lax.all_to_all(factor_send, 'pair', split_axis=1, concat_axis=1, tiled=True)]
    ppermute x0 -> x35, waiting for transfers between devices: none -> 29.4 us  [the longest x6 25.2 us: up(): lax.ppermute(x, 'task', [(c, (c + 2 * by) % task_count) for c in range(ta...]
    ppermute x0 -> x35, starting transfers between devices: none -> 26 us  [the longest x12 12.6 us: gather_pairs(): lax.ppermute(x, 'pair', [(p, p ^ bit) for p in range(pair_count)])]
    all_to_all x3 -> x0, starting transfers between devices: 12.3 us -> none  [the longest x1 4.95 us: per_device(): lax.all_to_all(factor_send, 'pair', split_axis=1, concat_axis=1, tiled=True)]
    gather x3 -> x1, local copies, waits for them, and re-layouts: 12.8 us -> 0.57 us  [per_device(): places = places[(level + jnp.arange(levels)) % levels]]
    reshape x4 -> x3, local copies, waits for them, and re-layouts: 14.1 us -> 3.32 us  [the longest x1 1.37 us: per_device(): task_owners.reshape(levels, 2, -1, 3)]
  transfers between devices with their start and end apart: 5 -> 36, of which waited for: 4 -> 8; matrix products, arithmetic and copies ran while one was open for 10% -> 7% of each run, Pallas kernels for 0% -> 37%
where the time goes in v2:
time: 184 us
  Pallas kernels  78 us (42%)
  waiting for transfers between devices  47.6 us (26%)
  starting transfers between devices  26 us (14%)
  local copies, waits for them, and re-layouts  14.8 us (8%)
  between operations  13.7 us (7%)
  other arithmetic  3.4 us (2%)
    pallas_call x8, Pallas kernels, prepare(): pl.pallas_call(functools.partial(prepare_kernel, len(parts)), out_shape=j...  40 us
    pallas_call x4, Pallas kernels, ladders(): pl.pallas_call(ladder_kernel, out_shape=jax.ShapeDtypeStruct((columns, bl...  38.1 us
    ppermute x6, waiting for transfers between devices, up(): lax.ppermute(x, 'task', [(c, (c + 2 * by) % task_count) for c in range(ta...  25.2 us
    all_gather x1, waiting for transfers between devices, per_device(): lax.all_gather(tiles, 'task', axis=0, tiled=True, axis_index_groups=same_...  18.2 us
    ppermute x12, starting transfers between devices, gather_pairs(): lax.ppermute(x, 'pair', [(p, p ^ bit) for p in range(pair_count)])  12.6 us
    ppermute x6, starting transfers between devices, up(): lax.ppermute(x, 'task', [(c, (c + 2 * by) % task_count) for c in range(ta...  10.5 us
    unnamed x13, local copies, waits for them, and re-layouts  4.94 us
    ppermute x12, waiting for transfers between devices, gather_pairs(): lax.ppermute(x, 'pair', [(p, p ^ bit) for p in range(pair_count)])  4.19 us
  transfers between devices with their start and end apart: 36, of which 8 were waited for; matrix products, arithmetic and copies ran while one was open for 7% of the time, Pallas kernels for 37%

profile of v2, /device:TPU:0, one launch (start us, length us, event | category | flops | bytes accessed | tf_op | source)
XLA Modules:
  0.0 183.6 jit_solution(13233242676845758052)
XLA Ops:
  6.5 1.2 copy.55
  7.7 0.8 pad.4
  8.6 3.3 %copy.49 = bf16[2,384,625]{2,1,0:T(8,128)(2,1)S(1)} copy(bf16[2,384,625]{1,0,2:T(2,128)(2,1)} %param.7) | data formatting | bytes 1920000 | tf_op args[0]
  12.0 0.9 dynamic-slice_bitcast_fusion
  12.9 3.0 %collective-permute-start.27 = (bf16[2,96,625]{2,1,0:T(8,128)(2,1)S(1)}, bf16[2,96,625]{2,1,0:T(8,128)(2,1)S(1)}, u32[]{:S(2)}, u32[]{:S(2)}) collective-permute-start(bf16[2,96,625]{2,1,0:T(8,128)(2,1)S(1)} %get-tuple-element.27.refs_0_), channel_id=1, source_target_pairs={{0,16},{8,24},{16,0},{24,8},{1,17},{9,25},{17,1},{25,9},{2,18},{10... | collective-permute-start | bytes 720008 | tf_op jit(solution)/shard_map/ppermute | solution.py:212
  15.9 1.5 collective-permute-start.25
  17.4 1.6 collective-permute-start.16
  19.0 2.6 %collective-permute-start.8 = (bf16[2,96,625]{2,1,0:T(8,128)(2,1)}, bf16[2,96,625]{2,1,0:T(8,128)(2,1)S(1)}, u32[]{:S(2)}, u32[]{:S(2)}) collective-permute-start(bf16[2,96,625]{2,1,0:T(8,128)(2,1)} %get-tuple-element.29), channel_id=1, source_target_pairs={{0,4},{1,5},{2,6},{3,7},{4,0},{5,1},{6,2},{7,3},{8,12},{9,13},{10,... | collective-permute-start | bytes 720008 | tf_op jit(solution)/shard_map/ppermute | solution.py:229
  21.6 0.3 collective-permute-done.27.refs_2_
  21.8 3.8 %collective-permute-start = (bf16[2,96,625]{2,1,0:T(8,128)(2,1)}, bf16[2,96,625]{2,1,0:T(8,128)(2,1)S(1)}, u32[]{:S(2)}, u32[]{:S(2)}) collective-permute-start(bf16[2,96,625]{2,1,0:T(8,128)(2,1)} %get-tuple-element.30), channel_id=1, source_target_pairs={{0,6},{1,7},{2,0},{3,1},{4,2},{5,3},{6,4},{7,5},{8,14},{9,15},{10,... | collective-permute-start | bytes 720008 | tf_op jit(solution)/shard_map/ppermute | solution.py:229
  25.7 1.4 reshape.66
  27.0 0.8 reshape.67
  27.8 1.6 collective-permute-start.29
  29.4 0.7 constant_dynamic-slice_fusion.1
  30.4 2.2 %collective-permute-done.16.refs_0_ = bf16[2,96,625]{2,1,0:T(8,128)(2,1)S(1)} collective-permute-done((bf16[2,96,625]{2,1,0:T(8,128)(2,1)}, bf16[2,96,625]{2,1,0:T(8,128)(2,1)S(1)}, u32[]{:S(2)}, u32[]{:S(2)}) %collective-permute-start.16) | collective-permute-done | bytes 240032 | tf_op jit(solution)/shard_map/ppermute | solution.py:229
  32.6 17.7 %collective-permute-done.8.refs_0_ = bf16[2,96,625]{2,1,0:T(8,128)(2,1)S(1)} collective-permute-done((bf16[2,96,625]{2,1,0:T(8,128)(2,1)}, bf16[2,96,625]{2,1,0:T(8,128)(2,1)S(1)}, u32[]{:S(2)}, u32[]{:S(2)}) %collective-permute-start.8) | collective-permute-done | bytes 240032 | tf_op jit(solution)/shard_map/ppermute | solution.py:229
  50.3 0.5 collective-permute-start.20
  50.8 0.7 collective-permute-done.refs_0_
  51.6 0.6 fusion.6
  52.2 18.2 %all-gather.2.cloned.1.call-done.mine_ref = bf16[8,800,128]{2,1,0:T(8,128)(2,1)} async-done(((bf16[2,800,128]{2,1,0:T(8,128)(2,1)}), bf16[8,800,128]{2,1,0:T(8,128)(2,1)}) %all-gather.2.cloned.1.call-update) | async-done | bytes 1638416 | tf_op jit(solution)/shard_map/all_gather | solution.py:234
  70.4 1.4 fusion.13
  71.8 0.5 collective-permute-start.17
  72.3 0.5 collective-permute-start.12
  72.8 0.5 collective-permute-start.10
  73.3 0.6 fusion.11
  73.9 0.8 slice.146
  74.6 0.8 concatenate.3
  75.5 0.6 pad_clamp_fusion
  76.1 0.6 gather_fusion
  76.7 0.5 slice_reduce_fusion
  77.2 1.6 collective-permute-start.2
  78.7 1.6 collective-permute-done.12.refs_2_
  80.3 0.5 collective-permute-start.4
  80.8 1.6 collective-permute-start.22
  82.4 0.1 slice_reduce_fusion.19.c_at
  82.5 1.6 copy-done
  84.1 5.2 %shard_map.73.refs_5_ = bf16[16,1600,384]{2,1,0:T(8,128)(2,1)} custom-call(bf16[2,96,625]{2,1,0:T(8,128)(2,1)S(1)} %get-tuple-element.27.refs_0_, bf16[2,96,625]{2,1,0:T(8,128)(2,1)} %collective-permute-done.25.refs_1_, bf16[2,96,625]{2,1,0:T(8,128)(2,1)S(1)} %collective-permute-done.27.refs_2_, bf16[2,96,625]{2,1,0:T(8,128)(2,1)} %collective-permute-done.29.refs_3_, ...), custom_call_target="tpu_custom_call" | custom-call | flops 1536000000 | bytes 3417600 | tf_op jit(solution)/shard_map/pallas_call | solution.py:78
  89.4 0.1 collective-permute-start.19
  89.5 0.4 collective-permute-start.21
  89.9 0.5 collective-permute-start.14
  90.4 2.3 %collective-permute-done.22.refs_3_ = bf16[2,96,625]{2,1,0:T(8,128)(2,1)S(1)} collective-permute-done((bf16[2,96,625]{2,1,0:T(8,128)(2,1)}, bf16[2,96,625]{2,1,0:T(8,128)(2,1)S(1)}, u32[]{:S(2)}, u32[]{:S(2)}) %collective-permute-start.22) | collective-permute-done | bytes 240032 | tf_op jit(solution)/shard_map/ppermute | solution.py:212
  92.7 5.3 %shard_map.74.refs_5_ = bf16[16,1600,384]{2,1,0:T(8,128)(2,1)} custom-call(bf16[2,96,625]{2,1,0:T(8,128)(2,1)S(1)} %collective-permute-done.24.refs_0_, bf16[2,96,625]{2,1,0:T(8,128)(2,1)} %collective-permute-done.26.refs_1_, bf16[2,96,625]{2,1,0:T(8,128)(2,1)} %collective-permute-done.28.refs_2_, ...), custom_call_target="tpu_custom_call", output_to_operand_aliasing={{}: (5, {})} | custom-call | flops 1536000000 | bytes 3417600 | tf_op jit(solution)/shard_map/pallas_call | solution.py:78
  98.0 5.3 %shard_map.75.refs_5_ = bf16[16,1600,384]{2,1,0:T(8,128)(2,1)} custom-call(bf16[2,96,625]{2,1,0:T(8,128)(2,1)S(1)} %collective-permute-done.16.refs_0_, bf16[2,96,625]{2,1,0:T(8,128)(2,1)} %collective-permute-done.18.refs_1_, bf16[2,96,625]{2,1,0:T(8,128)(2,1)} %collective-permute-done.20.refs_2_, ...), custom_call_target="tpu_custom_call", output_to_operand_aliasing={{}: (5, {})} | custom-call | flops 1536000000 | bytes 3417600 | tf_op jit(solution)/shard_map/pallas_call | solution.py:78
  103.3 0.5 collective-permute-start.13
  103.9 0.9 collective-permute-start.6
  104.8 0.2 collective-permute-start.15
  105.0 5.2 %shard_map.76.refs_5_ = bf16[16,1600,384]{2,1,0:T(8,128)(2,1)} custom-call(bf16[2,96,625]{2,1,0:T(8,128)(2,1)} %collective-permute-done.17.refs_0_, bf16[2,96,625]{2,1,0:T(8,128)(2,1)S(1)} %collective-permute-done.19.refs_1_, bf16[2,96,625]{2,1,0:T(8,128)(2,1)S(1)} %collective-permute-done.21.refs_2_, ...), custom_call_target="tpu_custom_call", output_to_operand_aliasing={{}: (5, {})} | custom-call | flops 1536000000 | bytes 3417600 | tf_op jit(solution)/shard_map/pallas_call | solution.py:78
  110.1 5.3 %shard_map.77.refs_5_ = bf16[16,1600,384]{2,1,0:T(8,128)(2,1)} custom-call(bf16[2,96,625]{2,1,0:T(8,128)(2,1)S(1)} %collective-permute-done.8.refs_0_, bf16[2,96,625]{2,1,0:T(8,128)(2,1)} %collective-permute-done.10.refs_1_, bf16[2,96,625]{2,1,0:T(8,128)(2,1)} %collective-permute-done.12.refs_2_, ...), custom_call_target="tpu_custom_call", output_to_operand_aliasing={{}: (5, {})} | custom-call | flops 1536000000 | bytes 3417600 | tf_op jit(solution)/shard_map/pallas_call | solution.py:78
  115.4 0.3 collective-permute-start.1
  115.8 0.2 collective-permute-start.3
  115.9 0.3 collective-permute-start.5
  116.3 0.2 collective-permute-start.7
  116.5 5.2 %shard_map.78.refs_5_ = bf16[16,1600,384]{2,1,0:T(8,128)(2,1)} custom-call(bf16[2,96,625]{2,1,0:T(8,128)(2,1)} %collective-permute-done.9.refs_0_, bf16[2,96,625]{2,1,0:T(8,128)(2,1)S(1)} %collective-permute-done.11.refs_1_, bf16[2,96,625]{2,1,0:T(8,128)(2,1)S(1)} %collective-permute-done.13.refs_2_, ...), custom_call_target="tpu_custom_call", output_to_operand_aliasing={{}: (5, {})} | custom-call | flops 1536000000 | bytes 3417600 | tf_op jit(solution)/shard_map/pallas_call | solution.py:78
  121.7 4.2 %shard_map.79.refs_5_ = bf16[16,1600,384]{2,1,0:T(8,128)(2,1)} custom-call(bf16[2,96,625]{2,1,0:T(8,128)(2,1)S(1)} %collective-permute-done.refs_0_, bf16[2,96,625]{2,1,0:T(8,128)(2,1)S(1)} %collective-permute-done.2.refs_1_, bf16[2,96,625]{2,1,0:T(8,128)(2,1)S(1)} %collective-permute-done.4.refs_2_, ...), custom_call_target="tpu_custom_call", output_to_operand_aliasing={{}: (5, {})} | custom-call | flops 1536000000 | bytes 3417600 | tf_op jit(solution)/shard_map/pallas_call | solution.py:78
  125.9 4.3 %shard_map.80.c_ref.r_ref = bf16[16,1600,384]{2,1,0:T(8,128)(2,1)} custom-call(bf16[2,96,625]{2,1,0:T(8,128)(2,1)S(1)} %collective-permute-done.1.refs_0_, bf16[2,96,625]{2,1,0:T(8,128)(2,1)S(1)} %collective-permute-done.3.refs_1_, bf16[2,96,625]{2,1,0:T(8,128)(2,1)S(1)} %collective-permute-done.5.refs_2_, ...), custom_call_target="tpu_custom_call", output_to_operand_aliasing={{}: (5, {})} | custom-call | flops 1536000000 | bytes 3417600 | tf_op jit(solution)/shard_map/pallas_call | solution.py:78
  130.2 9.5 %shard_map.81 = bf16[1,2,625,128]{3,2,1,0:T(8,128)(2,1)S(1)} custom-call(s32[4]{0:T(128)S(1)} %slice_reduce_fusion.19.c_at, s32[4]{0:T(128)S(1)} %get-tuple-element.23.r_at, s32[4]{0:T(128)S(1)} %get-tuple-element.22.t_at, s32[4]{0:T(128)S(1)} %get-tuple-element.21.core_at, s32[4]{0:T(128)S(1)} %get-tuple-element.20.o_at, ...), custom_call_target="tpu_custom_call" | custom-call | flops 2936012800 | bytes 6553600 | tf_op jit(solution)/shard_map/pallas_call | solution.py:179
  139.7 1.8 collective-permute-start.32
  141.5 9.5 %shard_map.82 = bf16[1,2,625,128]{3,2,1,0:T(8,128)(2,1)S(1)} custom-call(s32[4]{0:T(128)S(1)} %get-tuple-element.19.c_at, s32[4]{0:T(128)S(1)} %get-tuple-element.18.r_at, s32[4]{0:T(128)S(1)} %get-tuple-element.17.t_at, s32[4]{0:T(128)S(1)} %get-tuple-element.16.core_at, s32[4]{0:T(128)S(1)} %get-tuple-element.15.o_at, ...), custom_call_target="tpu_custom_call" | custom-call | flops 2936012800 | bytes 6553600 | tf_op jit(solution)/shard_map/pallas_call | solution.py:179
  151.1 9.5 %shard_map.83 = bf16[1,2,625,128]{3,2,1,0:T(8,128)(2,1)S(1)} custom-call(s32[4]{0:T(128)S(1)} %get-tuple-element.14.c_at, s32[4]{0:T(128)S(1)} %get-tuple-element.13.r_at, s32[4]{0:T(128)S(1)} %get-tuple-element.12.t_at, s32[4]{0:T(128)S(1)} %get-tuple-element.11.core_at, s32[4]{0:T(128)S(1)} %get-tuple-element.10.o_at, ...), custom_call_target="tpu_custom_call" | custom-call | flops 2936012800 | bytes 6553600 | tf_op jit(solution)/shard_map/pallas_call | solution.py:179
  160.6 0.6 collective-permute-start.34
  161.3 9.5 %shard_map.84 = bf16[1,2,625,128]{3,2,1,0:T(8,128)(2,1)S(1)} custom-call(s32[4]{0:T(128)S(1)} %get-tuple-element.9.c_at, s32[4]{0:T(128)S(1)} %get-tuple-element.8.r_at, s32[4]{0:T(128)S(1)} %get-tuple-element.7.t_at, s32[4]{0:T(128)S(1)} %get-tuple-element.6.core_at, s32[4]{0:T(128)S(1)} %get-tuple-element.5.o_at, ...), custom_call_target="tpu_custom_call" | custom-call | flops 2936012800 | bytes 6553600 | tf_op jit(solution)/shard_map/pallas_call | solution.py:179
  170.8 4.6 %collective-permute-done.33 = bf16[2,625,128]{2,1,0:T(8,128)(2,1)S(1)} collective-permute-done((bf16[2,625,128]{2,1,0:T(8,128)(2,1)S(1)}, bf16[2,625,128]{2,1,0:T(8,128)(2,1)S(1)}, u32[]{:S(2)}, u32[]{:S(2)}) %collective-permute-start.33) | collective-permute-done | bytes 320032 | tf_op jit(solution)/shard_map/ppermute | solution.py:229
  175.3 0.2 fusion.1
  175.5 1.2 copy.52
  (54 shorter events, 0.7 us)
Async XLA Ops:
  6.5 86.2 %copy-start.1 = (bf16[1600,625]{1,0:T(8,128)(2,1)S(1)}, bf16[1600,625]{1,0:T(8,128)(2,1)}, u32[]{:S(2)}) copy-start(bf16[1600,625]{1,0:T(8,128)(2,1)} %constant.111.clone.refs_4_) | copy-start | bytes 6000004
  6.5 63.8 %all-gather.2.cloned.1.call-start = ((), (), s32[]{:S(2)}) async-start(), calls=%async_computation | async-start | bytes 2048000 | tf_op jit(solution)/shard_map/all_gather | solution.py:234
  12.9 8.9 %collective-permute-start.27 = (bf16[2,96,625]{2,1,0:T(8,128)(2,1)S(1)}, bf16[2,96,625]{2,1,0:T(8,128)(2,1)S(1)}, u32[]{:S(2)}, u32[]{:S(2)}) collective-permute-start(bf16[2,96,625]{2,1,0:T(8,128)(2,1)S(1)} %get-tuple-element.27.refs_0_), channel_id=1, source_target_pairs={{0,16},{8,24},{16,0},{24,8},{1,17},{9,25},{17,1},{25,9},{2,18},{10... | collective-permute-start | bytes 720008 | tf_op jit(solution)/shard_map/ppermute | solution.py:212
  15.9 11.9 %collective-permute-start.25 = (bf16[2,96,625]{2,1,0:T(8,128)(2,1)S(1)}, bf16[2,96,625]{2,1,0:T(8,128)(2,1)}, u32[]{:S(2)}, u32[]{:S(2)}) collective-permute-start(bf16[2,96,625]{2,1,0:T(8,128)(2,1)S(1)} %get-tuple-element.27.refs_0_), channel_id=1, source_target_pairs={{0,8},{8,0},{16,24},{24,16},{1,9},{9,1},{17,25},{25,17},{2,10},{10... | collective-permute-start | bytes 720008 | tf_op jit(solution)/shard_map/ppermute | solution.py:212
  17.4 13.0 %collective-permute-start.24 = (bf16[2,96,625]{2,1,0:T(8,128)(2,1)S(1)}, bf16[2,96,625]{2,1,0:T(8,128)(2,1)S(1)}, u32[]{:S(2)}, u32[]{:S(2)}) collective-permute-start(bf16[2,96,625]{2,1,0:T(8,128)(2,1)S(1)} %get-tuple-element.27.refs_0_), channel_id=1, source_target_pairs={{0,1},{1,0},{2,3},{3,2},{4,5},{5,4},{6,7},{7,6},{8,9},{9,8},{10,11... | collective-permute-start | bytes 720008 | tf_op jit(solution)/shard_map/ppermute | solution.py:226
  17.4 15.2 %collective-permute-start.16 = (bf16[2,96,625]{2,1,0:T(8,128)(2,1)}, bf16[2,96,625]{2,1,0:T(8,128)(2,1)S(1)}, u32[]{:S(2)}, u32[]{:S(2)}) collective-permute-start(bf16[2,96,625]{2,1,0:T(8,128)(2,1)} %get-tuple-element.28), channel_id=1, source_target_pairs={{0,2},{1,3},{2,4},{3,5},{4,6},{5,7},{6,0},{7,1},{8,10},{9,11},{10,... | collective-permute-start | bytes 720008 | tf_op jit(solution)/shard_map/ppermute | solution.py:229
  19.0 31.3 %collective-permute-start.8 = (bf16[2,96,625]{2,1,0:T(8,128)(2,1)}, bf16[2,96,625]{2,1,0:T(8,128)(2,1)S(1)}, u32[]{:S(2)}, u32[]{:S(2)}) collective-permute-start(bf16[2,96,625]{2,1,0:T(8,128)(2,1)} %get-tuple-element.29), channel_id=1, source_target_pairs={{0,4},{1,5},{2,6},{3,7},{4,0},{5,1},{6,2},{7,3},{8,12},{9,13},{10,... | collective-permute-start | bytes 720008 | tf_op jit(solution)/shard_map/ppermute | solution.py:229
  21.8 29.7 %collective-permute-start = (bf16[2,96,625]{2,1,0:T(8,128)(2,1)}, bf16[2,96,625]{2,1,0:T(8,128)(2,1)S(1)}, u32[]{:S(2)}, u32[]{:S(2)}) collective-permute-start(bf16[2,96,625]{2,1,0:T(8,128)(2,1)} %get-tuple-element.30), channel_id=1, source_target_pairs={{0,6},{1,7},{2,0},{3,1},{4,2},{5,3},{6,4},{7,5},{8,14},{9,15},{10,... | collective-permute-start | bytes 720008 | tf_op jit(solution)/shard_map/ppermute | solution.py:229
  27.8 24.4 %collective-permute-start.29 = (bf16[2,96,625]{2,1,0:T(8,128)(2,1)S(1)}, bf16[2,96,625]{2,1,0:T(8,128)(2,1)}, u32[]{:S(2)}, u32[]{:S(2)}) collective-permute-start(bf16[2,96,625]{2,1,0:T(8,128)(2,1)S(1)} %collective-permute-done.27.refs_2_), channel_id=1, source_target_pairs={{0,8},{8,0},{16,24},{24,16},{1,9},{9,1},{17,25},{25,17},{2,10},{10... | collective-permute-start | bytes 720008 | tf_op jit(solution)/shard_map/ppermute | solution.py:212
  30.3 41.9 %collective-permute-start.28 = (bf16[2,96,625]{2,1,0:T(8,128)(2,1)S(1)}, bf16[2,96,625]{2,1,0:T(8,128)(2,1)}, u32[]{:S(2)}, u32[]{:S(2)}) collective-permute-start(bf16[2,96,625]{2,1,0:T(8,128)(2,1)S(1)} %collective-permute-done.27.refs_2_), channel_id=1, source_target_pairs={{0,1},{1,0},{2,3},{3,2},{4,5},{5,4},{6,7},{7,6},{8,9},{9,8},{10,11... | collective-permute-start | bytes 720008 | tf_op jit(solution)/shard_map/ppermute | solution.py:226
  32.6 40.2 %collective-permute-start.18 = (bf16[2,96,625]{2,1,0:T(8,128)(2,1)S(1)}, bf16[2,96,625]{2,1,0:T(8,128)(2,1)}, u32[]{:S(2)}, u32[]{:S(2)}) collective-permute-start(bf16[2,96,625]{2,1,0:T(8,128)(2,1)S(1)} %collective-permute-done.16.refs_0_), channel_id=1, source_target_pairs={{0,8},{8,0},{16,24},{24,16},{1,9},{9,1},{17,25},{25,17},{2,10},{10... | collective-permute-start | bytes 720008 | tf_op jit(solution)/shard_map/ppermute | solution.py:212
  50.3 23.0 %collective-permute-start.20 = (bf16[2,96,625]{2,1,0:T(8,128)(2,1)S(1)}, bf16[2,96,625]{2,1,0:T(8,128)(2,1)}, u32[]{:S(2)}, u32[]{:S(2)}) collective-permute-start(bf16[2,96,625]{2,1,0:T(8,128)(2,1)S(1)} %collective-permute-done.16.refs_0_), channel_id=1, source_target_pairs={{0,16},{8,24},{16,0},{24,8},{1,17},{9,25},{17,1},{25,9},{2,18},{10... | collective-permute-start | bytes 720008 | tf_op jit(solution)/shard_map/ppermute | solution.py:212
  51.5 20.3 %collective-permute-start.26 = (bf16[2,96,625]{2,1,0:T(8,128)(2,1)}, bf16[2,96,625]{2,1,0:T(8,128)(2,1)}, u32[]{:S(2)}, u32[]{:S(2)}) collective-permute-start(bf16[2,96,625]{2,1,0:T(8,128)(2,1)} %collective-permute-done.25.refs_1_), channel_id=1, source_target_pairs={{0,1},{1,0},{2,3},{3,2},{4,5},{5,4},{6,7},{7,6},{8,9},{9,8},{10,11... | collective-permute-start | bytes 720008 | tf_op jit(solution)/shard_map/ppermute | solution.py:226
  70.4 59.8 %collective-permute-start.31 = (bf16[8,800,128]{2,1,0:T(8,128)(2,1)}, bf16[8,800,128]{2,1,0:T(8,128)(2,1)}, u32[]{:S(2)}, u32[]{:S(2)}) collective-permute-start(bf16[8,800,128]{2,1,0:T(8,128)(2,1)} %all-gather.2.cloned.1.call-done.mine_ref), channel_id=1, source_target_pairs={{0,1},{1,0},{2,3},{3,2},{4,5},{5,4},{6,7},{7,6},{8,9},{9,8},{10,11... | collective-permute-start | bytes 4915208 | tf_op jit(solution)/shard_map/ppermute | solution.py:226
  71.8 5.4 %collective-permute-start.17 = (bf16[2,96,625]{2,1,0:T(8,128)(2,1)S(1)}, bf16[2,96,625]{2,1,0:T(8,128)(2,1)}, u32[]{:S(2)}, u32[]{:S(2)}) collective-permute-start(bf16[2,96,625]{2,1,0:T(8,128)(2,1)S(1)} %collective-permute-done.16.refs_0_), channel_id=1, source_target_pairs={{0,1},{1,0},{2,3},{3,2},{4,5},{5,4},{6,7},{7,6},{8,9},{9,8},{10,11... | collective-permute-start | bytes 720008 | tf_op jit(solution)/shard_map/ppermute | solution.py:226
  72.3 8.0 %collective-permute-start.12 = (bf16[2,96,625]{2,1,0:T(8,128)(2,1)S(1)}, bf16[2,96,625]{2,1,0:T(8,128)(2,1)}, u32[]{:S(2)}, u32[]{:S(2)}) collective-permute-start(bf16[2,96,625]{2,1,0:T(8,128)(2,1)S(1)} %collective-permute-done.8.refs_0_), channel_id=1, source_target_pairs={{0,16},{8,24},{16,0},{24,8},{1,17},{9,25},{17,1},{25,9},{2,18},{10... | collective-permute-start | bytes 720008 | tf_op jit(solution)/shard_map/ppermute | solution.py:212
  72.8 8.0 %collective-permute-start.10 = (bf16[2,96,625]{2,1,0:T(8,128)(2,1)S(1)}, bf16[2,96,625]{2,1,0:T(8,128)(2,1)}, u32[]{:S(2)}, u32[]{:S(2)}) collective-permute-start(bf16[2,96,625]{2,1,0:T(8,128)(2,1)S(1)} %collective-permute-done.8.refs_0_), channel_id=1, source_target_pairs={{0,8},{8,0},{16,24},{24,16},{1,9},{9,1},{17,25},{25,17},{2,10},{10... | collective-permute-start | bytes 720008 | tf_op jit(solution)/shard_map/ppermute | solution.py:212
  73.3 7.5 %collective-permute-start.9 = (bf16[2,96,625]{2,1,0:T(8,128)(2,1)S(1)}, bf16[2,96,625]{2,1,0:T(8,128)(2,1)}, u32[]{:S(2)}, u32[]{:S(2)}) collective-permute-start(bf16[2,96,625]{2,1,0:T(8,128)(2,1)S(1)} %collective-permute-done.8.refs_0_), channel_id=1, source_target_pairs={{0,1},{1,0},{2,3},{3,2},{4,5},{5,4},{6,7},{7,6},{8,9},{9,8},{10,11... | collective-permute-start | bytes 720008 | tf_op jit(solution)/shard_map/ppermute | solution.py:226
  77.2 12.2 %collective-permute-start.2 = (bf16[2,96,625]{2,1,0:T(8,128)(2,1)S(1)}, bf16[2,96,625]{2,1,0:T(8,128)(2,1)S(1)}, u32[]{:S(2)}, u32[]{:S(2)}) collective-permute-start(bf16[2,96,625]{2,1,0:T(8,128)(2,1)S(1)} %collective-permute-done.refs_0_), channel_id=1, source_target_pairs={{0,8},{8,0},{16,24},{24,16},{1,9},{9,1},{17,25},{25,17},{2,10},{10... | collective-permute-start | bytes 720008 | tf_op jit(solution)/shard_map/ppermute | solution.py:212
  80.3 9.2 %collective-permute-start.4 = (bf16[2,96,625]{2,1,0:T(8,128)(2,1)S(1)}, bf16[2,96,625]{2,1,0:T(8,128)(2,1)S(1)}, u32[]{:S(2)}, u32[]{:S(2)}) collective-permute-start(bf16[2,96,625]{2,1,0:T(8,128)(2,1)S(1)} %collective-permute-done.refs_0_), channel_id=1, source_target_pairs={{0,16},{8,24},{16,0},{24,8},{1,17},{9,25},{17,1},{25,9},{2,18},{10... | collective-permute-start | bytes 720008 | tf_op jit(solution)/shard_map/ppermute | solution.py:212
  80.8 9.1 %collective-permute-start.30 = (bf16[2,96,625]{2,1,0:T(8,128)(2,1)}, bf16[2,96,625]{2,1,0:T(8,128)(2,1)S(1)}, u32[]{:S(2)}, u32[]{:S(2)}) collective-permute-start(bf16[2,96,625]{2,1,0:T(8,128)(2,1)} %collective-permute-done.29.refs_3_), channel_id=1, source_target_pairs={{0,1},{1,0},{2,3},{3,2},{4,5},{5,4},{6,7},{7,6},{8,9},{9,8},{10,11... | collective-permute-start | bytes 720008 | tf_op jit(solution)/shard_map/ppermute | solution.py:226
  80.8 11.9 %collective-permute-start.22 = (bf16[2,96,625]{2,1,0:T(8,128)(2,1)}, bf16[2,96,625]{2,1,0:T(8,128)(2,1)S(1)}, u32[]{:S(2)}, u32[]{:S(2)}) collective-permute-start(bf16[2,96,625]{2,1,0:T(8,128)(2,1)} %collective-permute-done.18.refs_1_), channel_id=1, source_target_pairs={{0,16},{8,24},{16,0},{24,8},{1,17},{9,25},{17,1},{25,9},{2,18},{10... | collective-permute-start | bytes 720008 | tf_op jit(solution)/shard_map/ppermute | solution.py:212
  82.5 1.6 copy-start
  89.4 13.9 %collective-permute-start.19 = (bf16[2,96,625]{2,1,0:T(8,128)(2,1)}, bf16[2,96,625]{2,1,0:T(8,128)(2,1)S(1)}, u32[]{:S(2)}, u32[]{:S(2)}) collective-permute-start(bf16[2,96,625]{2,1,0:T(8,128)(2,1)} %collective-permute-done.18.refs_1_), channel_id=1, source_target_pairs={{0,1},{1,0},{2,3},{3,2},{4,5},{5,4},{6,7},{7,6},{8,9},{9,8},{10,11... | collective-permute-start | bytes 720008 | tf_op jit(solution)/shard_map/ppermute | solution.py:226
  89.5 14.3 %collective-permute-start.21 = (bf16[2,96,625]{2,1,0:T(8,128)(2,1)}, bf16[2,96,625]{2,1,0:T(8,128)(2,1)S(1)}, u32[]{:S(2)}, u32[]{:S(2)}) collective-permute-start(bf16[2,96,625]{2,1,0:T(8,128)(2,1)} %collective-permute-done.20.refs_2_), channel_id=1, source_target_pairs={{0,1},{1,0},{2,3},{3,2},{4,5},{5,4},{6,7},{7,6},{8,9},{9,8},{10,11... | collective-permute-start | bytes 720008 | tf_op jit(solution)/shard_map/ppermute | solution.py:226
  89.9 14.0 %collective-permute-start.14 = (bf16[2,96,625]{2,1,0:T(8,128)(2,1)}, bf16[2,96,625]{2,1,0:T(8,128)(2,1)S(1)}, u32[]{:S(2)}, u32[]{:S(2)}) collective-permute-start(bf16[2,96,625]{2,1,0:T(8,128)(2,1)} %collective-permute-done.12.refs_2_), channel_id=1, source_target_pairs={{0,8},{8,0},{16,24},{24,16},{1,9},{9,1},{17,25},{25,17},{2,10},{10... | collective-permute-start | bytes 720008 | tf_op jit(solution)/shard_map/ppermute | solution.py:212
  92.7 12.1 %collective-permute-start.23 = (bf16[2,96,625]{2,1,0:T(8,128)(2,1)S(1)}, bf16[2,96,625]{2,1,0:T(8,128)(2,1)S(1)}, u32[]{:S(2)}, u32[]{:S(2)}) collective-permute-start(bf16[2,96,625]{2,1,0:T(8,128)(2,1)S(1)} %collective-permute-done.22.refs_3_), channel_id=1, source_target_pairs={{0,1},{1,0},{2,3},{3,2},{4,5},{5,4},{6,7},{7,6},{8,9},{9,8},{10,11... | collective-permute-start | bytes 720008 | tf_op jit(solution)/shard_map/ppermute | solution.py:226
  103.3 12.5 %collective-permute-start.13 = (bf16[2,96,625]{2,1,0:T(8,128)(2,1)}, bf16[2,96,625]{2,1,0:T(8,128)(2,1)S(1)}, u32[]{:S(2)}, u32[]{:S(2)}) collective-permute-start(bf16[2,96,625]{2,1,0:T(8,128)(2,1)} %collective-permute-done.12.refs_2_), channel_id=1, source_target_pairs={{0,1},{1,0},{2,3},{3,2},{4,5},{5,4},{6,7},{7,6},{8,9},{9,8},{10,11... | collective-permute-start | bytes 720008 | tf_op jit(solution)/shard_map/ppermute | solution.py:226
  103.8 11.6 %collective-permute-start.11 = (bf16[2,96,625]{2,1,0:T(8,128)(2,1)}, bf16[2,96,625]{2,1,0:T(8,128)(2,1)S(1)}, u32[]{:S(2)}, u32[]{:S(2)}) collective-permute-start(bf16[2,96,625]{2,1,0:T(8,128)(2,1)} %collective-permute-done.10.refs_1_), channel_id=1, source_target_pairs={{0,1},{1,0},{2,3},{3,2},{4,5},{5,4},{6,7},{7,6},{8,9},{9,8},{10,11... | collective-permute-start | bytes 720008 | tf_op jit(solution)/shard_map/ppermute | solution.py:226
  103.9 12.1 %collective-permute-start.6 = (bf16[2,96,625]{2,1,0:T(8,128)(2,1)S(1)}, bf16[2,96,625]{2,1,0:T(8,128)(2,1)S(1)}, u32[]{:S(2)}, u32[]{:S(2)}) collective-permute-start(bf16[2,96,625]{2,1,0:T(8,128)(2,1)S(1)} %collective-permute-done.2.refs_1_), channel_id=1, source_target_pairs={{0,16},{8,24},{16,0},{24,8},{1,17},{9,25},{17,1},{25,9},{2,18},{10... | collective-permute-start | bytes 720008 | tf_op jit(solution)/shard_map/ppermute | solution.py:212
  104.8 11.5 %collective-permute-start.15 = (bf16[2,96,625]{2,1,0:T(8,128)(2,1)S(1)}, bf16[2,96,625]{2,1,0:T(8,128)(2,1)S(1)}, u32[]{:S(2)}, u32[]{:S(2)}) collective-permute-start(bf16[2,96,625]{2,1,0:T(8,128)(2,1)S(1)} %collective-permute-done.14.refs_3_), channel_id=1, source_target_pairs={{0,1},{1,0},{2,3},{3,2},{4,5},{5,4},{6,7},{7,6},{8,9},{9,8},{10,11... | collective-permute-start | bytes 720008 | tf_op jit(solution)/shard_map/ppermute | solution.py:226
  115.4 10.4 %collective-permute-start.1 = (bf16[2,96,625]{2,1,0:T(8,128)(2,1)S(1)}, bf16[2,96,625]{2,1,0:T(8,128)(2,1)S(1)}, u32[]{:S(2)}, u32[]{:S(2)}) collective-permute-start(bf16[2,96,625]{2,1,0:T(8,128)(2,1)S(1)} %collective-permute-done.refs_0_), channel_id=1, source_target_pairs={{0,1},{1,0},{2,3},{3,2},{4,5},{5,4},{6,7},{7,6},{8,9},{9,8},{10,11... | collective-permute-start | bytes 720008 | tf_op jit(solution)/shard_map/ppermute | solution.py:226
  115.8 10.1 %collective-permute-start.3 = (bf16[2,96,625]{2,1,0:T(8,128)(2,1)S(1)}, bf16[2,96,625]{2,1,0:T(8,128)(2,1)S(1)}, u32[]{:S(2)}, u32[]{:S(2)}) collective-permute-start(bf16[2,96,625]{2,1,0:T(8,128)(2,1)S(1)} %collective-permute-done.2.refs_1_), channel_id=1, source_target_pairs={{0,1},{1,0},{2,3},{3,2},{4,5},{5,4},{6,7},{7,6},{8,9},{9,8},{10,11... | collective-permute-start | bytes 720008 | tf_op jit(solution)/shard_map/ppermute | solution.py:226
  115.9 9.9 %collective-permute-start.5 = (bf16[2,96,625]{2,1,0:T(8,128)(2,1)S(1)}, bf16[2,96,625]{2,1,0:T(8,128)(2,1)S(1)}, u32[]{:S(2)}, u32[]{:S(2)}) collective-permute-start(bf16[2,96,625]{2,1,0:T(8,128)(2,1)S(1)} %collective-permute-done.4.refs_2_), channel_id=1, source_target_pairs={{0,1},{1,0},{2,3},{3,2},{4,5},{5,4},{6,7},{7,6},{8,9},{9,8},{10,11... | collective-permute-start | bytes 720008 | tf_op jit(solution)/shard_map/ppermute | solution.py:226
  116.3 9.6 %collective-permute-start.7 = (bf16[2,96,625]{2,1,0:T(8,128)(2,1)S(1)}, bf16[2,96,625]{2,1,0:T(8,128)(2,1)S(1)}, u32[]{:S(2)}, u32[]{:S(2)}) collective-permute-start(bf16[2,96,625]{2,1,0:T(8,128)(2,1)S(1)} %collective-permute-done.6.refs_3_), channel_id=1, source_target_pairs={{0,1},{1,0},{2,3},{3,2},{4,5},{5,4},{6,7},{7,6},{8,9},{9,8},{10,11... | collective-permute-start | bytes 720008 | tf_op jit(solution)/shard_map/ppermute | solution.py:226
  125.9 4.3 %copy-start.2 = (bf16[8,800,128]{2,1,0:T(8,128)(2,1)S(1)}, bf16[8,800,128]{2,1,0:T(8,128)(2,1)}, u32[]{:S(2)}) copy-start(bf16[8,800,128]{2,1,0:T(8,128)(2,1)} %all-gather.2.cloned.1.call-done.mine_ref) | copy-start | bytes 4915204
  125.9 4.3 %copy-start.3 = (bf16[625,800]{1,0:T(8,128)(2,1)S(1)}, bf16[625,800]{1,0:T(8,128)(2,1)}, u32[]{:S(2)}) copy-start(bf16[625,800]{1,0:T(8,128)(2,1)} %constant.112.clone.back_ref) | copy-start | bytes 3000004
  125.9 4.3 %copy-start.4 = (bf16[32,625]{1,0:T(8,128)(2,1)S(1)}, bf16[32,625]{1,0:T(8,128)(2,1)}, u32[]{:S(2)}) copy-start(bf16[32,625]{1,0:T(8,128)(2,1)} %constant.118.matrix_ref) | copy-start | bytes 120004
  139.7 31.1 %collective-permute-start.32 = (bf16[2,625,128]{2,1,0:T(8,128)(2,1)S(1)}, bf16[2,625,128]{2,1,0:T(8,128)(2,1)S(1)}, u32[]{:S(2)}, u32[]{:S(2)}) collective-permute-start(bf16[2,625,128]{2,1,0:T(8,128)(2,1)S(1)} %bitcast.32), channel_id=1, source_target_pairs={{0,6},{1,7},{2,0},{3,1},{4,2},{5,3},{6,4},{7,5},{8,14},{9,15},{10,... | collective-permute-start | bytes 960008 | tf_op jit(solution)/shard_map/ppermute | solution.py:229
  151.0 24.3 %collective-permute-start.33 = (bf16[2,625,128]{2,1,0:T(8,128)(2,1)S(1)}, bf16[2,625,128]{2,1,0:T(8,128)(2,1)S(1)}, u32[]{:S(2)}, u32[]{:S(2)}) collective-permute-start(bf16[2,625,128]{2,1,0:T(8,128)(2,1)S(1)} %bitcast.33), channel_id=1, source_target_pairs={{0,4},{1,5},{2,6},{3,7},{4,0},{5,1},{6,2},{7,3},{8,12},{9,13},{10,... | collective-permute-start | bytes 960008 | tf_op jit(solution)/shard_map/ppermute | solution.py:229
  160.6 14.7 %collective-permute-start.34 = (bf16[2,625,128]{2,1,0:T(8,128)(2,1)S(1)}, bf16[2,625,128]{2,1,0:T(8,128)(2,1)S(1)}, u32[]{:S(2)}, u32[]{:S(2)}) collective-permute-start(bf16[2,625,128]{2,1,0:T(8,128)(2,1)S(1)} %bitcast.34), channel_id=1, source_target_pairs={{0,2},{1,3},{2,4},{3,5},{4,6},{5,7},{6,0},{7,1},{8,10},{9,11},{10,... | collective-permute-start | bytes 960008 | tf_op jit(solution)/shard_map/ppermute | solution.py:229
  161.3 14.1 %copy-start.5 = (f32[2,128,625]{1,0,2:T(2,128)S(1)}, f32[2,128,625]{1,0,2:T(2,128)}, u32[]{:S(2)}) copy-start(f32[2,128,625]{1,0,2:T(2,128)} %param.9) | copy-start | bytes 1920004
Sparse Core Ops, SparseCore 0:
  8.9 61.4 all-gather.1

commit v3 on v2

--- a/solution.py
+++ b/solution.py
@@ -18,7 +18,7 @@
 ORDER = [x for g in range(GROUP) for x in range(g, TV, GROUP)]
 START = [ORDER.index(g) * PAD for g in range(GROUP)] + [ROWS]
 PLACE = np.argsort(ORDER)
-PREPARE_STEPS = 5
+PREPARE_STEPS = 2
 BF = jnp.bfloat16
 F32 = jnp.float32
 VMEM_BYTES = 48 * 1024 * 1024
@@ -31,6 +31,11 @@
 def forms_matrix():
     x, y = np.divmod(np.arange(TV * TV), TV)
     return np.concatenate([spread(PLACE[y] * PAD + x, ROWS), spread(x * PAD + y, ROWS)], axis=0)
+
+
+def amp_matrix():
+    c, d = np.divmod(np.arange(TV * TV), TV)
+    return spread(d * PAD + c, ROWS)
 
 
 def back_matrix():
@@ -92,32 +97,61 @@
     )(*operands)
 
 
+def amp_kernel(levels, matrix_ref, *refs):
+    tile_refs, out_ref = refs[:-1], refs[-1]
+    blocks_here = out_ref.shape[0] // levels
+    pairs = out_ref.shape[2]
+    for by in range(levels):
+        tiles = tile_refs[0][...] if by == 0 else tile_refs[by][...] + tile_refs[2 * levels - 1 - by][...]
+        made = jnp.dot(matrix_ref[...], tiles, preferred_element_type=F32).astype(BF)
+        for m in range(blocks_here):
+            out_ref[by * blocks_here + m] = made[:, m * pairs : (m + 1) * pairs]
+
+
+def prepare_amps(own, ups, downs, blocks_here, matrix):
+    levels = len(ups) + 1
+    pairs = own.shape[1] // blocks_here
+    return pl.pallas_call(
+        functools.partial(amp_kernel, levels),
+        out_shape=jax.ShapeDtypeStruct((levels * blocks_here, ROWS, pairs), BF),
+        compiler_params=pltpu.CompilerParams(vmem_limit_bytes=VMEM_BYTES),
+        cost_estimate=pl.CostEstimate(
+            flops=2 * levels * own.size * ROWS,
+            bytes_accessed=4 * levels * own.size,
+            transcendentals=0,
+        ),
+    )(matrix, own, *ups, *downs)
+
+
 def turned(ref, groups, by):
     numbers = [min(A * GROUP + (p - by) % GROUP, TV - 1) for A in groups for p in range(GROUP)]
     return jnp.concatenate([ref[x * PAD : (x + 1) * PAD, :] for x in numbers], axis=0)
 
 
 def ladder_kernel(
-    c_at, r_at, t_at, core_at, o_at, c_ref, r_ref, mine_ref, other_ref, back_ref, matrix_ref, out_ref, *scratch
+    find, made, column_ref, owners_ref, local_ref, c_ref, r_ref, mine_ref, other_ref, back_ref, *refs
 ):
-    v_ref, u_ref, amp_ref, acc_ref = scratch[:4]
+    matrix_ref = None if made else refs[0]
+    out_ref, v_ref, u_ref, amp_ref, acc_ref = refs[:5] if made else refs[1:6]
     step, steps = pl.program_id(1), pl.num_programs(1)
-    at = pl.program_id(0) * steps + step
+    places = find(pl.program_id(0), step, column_ref, owners_ref, local_ref)
 
     @pl.when(step == 0)
     def _():
         acc_ref[...] = jnp.zeros_like(acc_ref)
 
-    @pl.when(core_at[at] == 0)
+    @pl.when(places["amp_core"] == 0)
     def _():
         amp_ref[...] = mine_ref[0]
 
-    @pl.when(core_at[at] != 0)
+    @pl.when(places["amp_core"] != 0)
     def _():
         amp_ref[...] = other_ref[0]
 
-    if len(scratch) > 4:
-        forms = scratch[4]
+    if made:
+        c_form, r_form = c_ref.at[0], r_ref.at[0]
+    else:
+        forms = refs[6]
         for i, tile_ref in enumerate((c_ref, r_ref)):
             forms[i] = lax.dot_general(
                 matrix_ref[i * ROWS : (i + 1) * ROWS, :],
@@ -126,8 +160,6 @@
                 preferred_element_type=F32,
             ).astype(BF)
         c_form, r_form = forms.at[0], forms.at[1]
-    else:
-        c_form, r_form = c_ref.at[0], r_ref.at[0]
 
     spot = lax.broadcasted_iota(jnp.int32, (PAD, LANES), 1) // PAD
     at_spot = [spot == p for p in range(GROUP)]
@@ -156,7 +188,7 @@
                         block = jnp.where(at_spot[p], blocks[(p - i) % GROUP], block)
                     u_ref[START[i] + A * PAD : START[i] + (A + 1) * PAD, D * LANES : (D + 1) * LANES] = block.astype(BF)
     for i in range(GROUP):
-        acc_ref[o_at[at], START[i] : START[i + 1], :] += jnp.dot(
+        acc_ref[places["out"], START[i] : START[i + 1], :] += jnp.dot(
             u_ref[START[i] : START[i + 1], :], turned(amp_ref, range(GROUPS), i), preferred_element_type=F32
         )
 
@@ -166,38 +198,61 @@
             out_ref[0, m] = jnp.dot(back_ref[...], acc_ref[m].astype(BF), preferred_element_type=F32).astype(BF)
 
 
-def ladders(places, tiles, amps, back, matrix, blocks_here):
-    columns, tasks, kinds = places.shape
+def ladders(first, columns, levels, blocks_here, column, task_owners, task_local, tiles, amps, back, matrix):
+    tasks = task_owners.shape[0] // (2 * levels)
     pairs = amps[0].shape[2]
     made = tiles.shape[1] == 2 * ROWS
     depth = tiles.shape[2] if made else tiles.shape[1]
     held = (1, ROWS, depth) if made else (1, *tiles.shape[1:])
-    more = [] if made else [pltpu.VMEM((2, ROWS, depth), BF)]
-    matrix = matrix[:PAD] if made else matrix
-    tables = [places[:, :, i].reshape(-1) for i in range(kinds)]
-    amp_spec = pl.BlockSpec((1, ROWS, pairs), lambda i, j, c, r, t, k, o: (t[i * tasks + j], 0, 0))
+
+    def find(i, j, column_ref, owners_ref, local_ref):
+        level, core = column_ref[0] // 2, lax.rem(column_ref[0], 2)
+        task = (2 * lax.rem(level + first + i, levels) + core) * tasks + j
+
+        def place(kind):
+            owner = owners_ref[task, kind]
+            below = lax.rem(level - owner // 2 + levels, levels)
+            far = jnp.where(lax.rem(owner, 2) != core, 1, 0)
+            return below, far, local_ref[task, kind]
+
+        (row_below, row_far, row_m), (col_below, col_far, col_m), (amp_below, amp_far, amp_m) = map(place, range(3))
+        return {
+            "row": (row_below * 2 + row_far) * blocks_here + row_m,
+            "col": (col_below * 2 + col_far) * blocks_here + col_m,
+            "amp": amp_below * blocks_here + amp_m,
+            "amp_core": amp_far,
+            "out": local_ref[task, 3],
+        }
+
+    fixed = lambda shape: pl.BlockSpec(shape, lambda i, j, *tables: (0,) * len(shape))
+    amp_spec = pl.BlockSpec((1, ROWS, pairs), lambda i, j, *tables: (find(i, j, *tables)["amp"], 0, 0))
+    in_specs = [
+        pl.BlockSpec(held, lambda i, j, *tables: (find(i, j, *tables)["col"], 0, 0)),
+        pl.BlockSpec(held, lambda i, j, *tables: (find(i, j, *tables)["row"], int(made), 0)),
+        amp_spec,
+        amp_spec,
+        fixed(back.shape),
+    ]
+    scratch = [
+        pltpu.VMEM((ROWS, WIDE), F32),
+        pltpu.VMEM((ROWS, WIDE), BF),
+        pltpu.VMEM((ROWS, pairs), BF),
+        pltpu.VMEM((blocks_here, ROWS, pairs), F32),
+    ]
+    operands = [tiles, tiles, *amps, back]
+    if not made:
+        in_specs.append(fixed(matrix.shape))
+        scratch.append(pltpu.VMEM((2, ROWS, depth), BF))
+        operands.append(matrix)
     return pl.pallas_call(
-        ladder_kernel,
+        functools.partial(ladder_kernel, find, made),
         out_shape=jax.ShapeDtypeStruct((columns, blocks_here, TV * TV, pairs), BF),
         grid_spec=pltpu.PrefetchScalarGridSpec(
-            num_scalar_prefetch=kinds,
+            num_scalar_prefetch=3,
             grid=(columns, tasks),
-            in_specs=[
-                pl.BlockSpec(held, lambda i, j, c, r, t, k, o: (c[i * tasks + j], 0, 0)),
-                pl.BlockSpec(held, lambda i, j, c, r, t, k, o: (r[i * tasks + j], int(made), 0)),
-                amp_spec,
-                amp_spec,
-                pl.BlockSpec(back.shape, lambda i, j, c, r, t, k, o: (0, 0)),
-                pl.BlockSpec(matrix.shape, lambda i, j, c, r, t, k, o: (0, 0)),
-            ],
-            out_specs=pl.BlockSpec((1, blocks_here, TV * TV, pairs), lambda i, j, c, r, t, k, o: (i, 0, 0, 0)),
-            scratch_shapes=[
-                pltpu.VMEM((ROWS, WIDE), F32),
-                pltpu.VMEM((ROWS, WIDE), BF),
-                pltpu.VMEM((ROWS, pairs), BF),
-                pltpu.VMEM((blocks_here, ROWS, pairs), F32),
-                *more,
-            ],
+            in_specs=in_specs,
+            out_specs=pl.BlockSpec((1, blocks_here, TV * TV, pairs), lambda i, j, *tables: (i, 0, 0, 0)),
+            scratch_shapes=scratch,
         ),
         compiler_params=pltpu.CompilerParams(vmem_limit_bytes=VMEM_BYTES),
         cost_estimate=pl.CostEstimate(
@@ -205,7 +260,7 @@
             bytes_accessed=2 * columns * tasks * ROWS * 2 * (depth + pairs),
             transcendentals=0,
         ),
-    )(*tables, tiles, tiles, *amps, back, matrix)
+    )(column, task_owners, task_local, *operands)
 
 
 def gather_pairs(part, by, pair_count):
@@ -221,54 +276,56 @@
     blocks_here, depth_here, _ = factor_blocks.shape
     pairs = amplitudes.shape[1]
     levels = task_count // 2
-    level, core = column // 2, column % 2
+    level = column // 2
     depth = depth_here // levels
-    other_core = lambda x: lax.ppermute(x, "task", [(c, c ^ 1) for c in range(task_count)])
-
-    def up(x, by):
-        return lax.ppermute(x, "task", [(c, (c + 2 * by) % task_count) for c in range(task_count)])
-
-    same_core = [[2 * z + k for z in range(levels)] for k in range(2)]
-    tiles = amplitudes.reshape(blocks_here, pairs, TV, TV).transpose(0, 3, 2, 1)
-    tiles = jnp.pad(tiles, ((0, 0), (0, 0), (0, PAD - TV), (0, 0))).reshape(blocks_here, ROWS, pairs)
-    amps = lax.all_gather(tiles, "task", axis=0, tiled=True, axis_index_groups=same_core)
-    amps = (amps, other_core(amps))
-
+    total = 2 * levels * blocks_here
     matrix = jnp.asarray(forms_matrix())
     back = jnp.asarray(back_matrix())
+    other_core = lambda x: lax.ppermute(x, "task", [(c, c ^ 1) for c in range(task_count)])
+
+    def around(x, by):
+        return lax.ppermute(x, "task", [(c, (c + 2 * by) % task_count) for c in range(task_count)])
+
+    def hop(x, by):
+        return lax.ppermute(x, "task", [(c, c + by) for c in range(task_count) if 0 <= c + by < task_count])
+
     slices = factor_blocks.reshape(blocks_here, levels, depth, -1)
     mine = [lax.dynamic_index_in_dim(slices, (level + by) % levels, 1, keepdims=False) for by in range(levels)]
-    parts = [mine[0]] + [up(mine[by], by) for by in range(1, levels)]
-
-    total = 2 * levels * blocks_here
+    parts = [mine[0]] + [around(mine[by], by) for by in range(1, levels)]
     if pair_count == 4:
+        own = amplitudes.transpose(2, 0, 1).reshape(TV * TV, blocks_here * pairs)
+        ups, downs = [hop(own, 2)], [hop(own, -2)]
+        for by in range(2, levels):
+            (up, down), _ = lax.optimization_barrier(((ups[-1], downs[-1]), parts[1:]))
+            ups.append(hop(up, 2))
+            downs.append(hop(down, -2))
+        amps = prepare_amps(own, ups, downs, blocks_here, jnp.asarray(amp_matrix()))
         held = None
         for by, part in enumerate(parts):
             pieces = gather_pairs(part, by, pair_count)
             held = prepare(pieces, 2 * by, total, matrix, held)
             held = prepare([other_core(piece) for piece in pieces], 2 * by + 1, total, matrix, held)
     else:
+        tiles = amplitudes.reshape(blocks_here, pairs, TV, TV).transpose(0, 3, 2, 1)
+        tiles = jnp.pad(tiles, ((0, 0), (0, 0), (0, PAD - TV), (0, 0))).reshape(blocks_here, ROWS, pairs)
+        same_core = [[2 * z + k for z in range(levels)] for k in range(2)]
+        amps = lax.all_gather(tiles, "task", axis=0, axis_index_groups=same_core)
+        amps = amps[(level - jnp.arange(levels)) % levels].reshape(levels * blocks_here, ROWS, pairs)
         held = lax.all_gather(jnp.stack(parts), "pair", axis=2, tiled=True)
         held = jnp.stack([held, other_core(held)], axis=1).reshape(total, depth * pair_count, -1)
-
-    owners = lax.dynamic_index_in_dim(task_owners.reshape(levels, 2, -1, 3), core, 1, keepdims=False)
-    local = lax.dynamic_index_in_dim(task_local.reshape(levels, 2, -1, 4), core, 1, keepdims=False)
-    owner_level, far_core = owners // 2, (owners % 2 != core).astype(jnp.int32)
-    factor_at = (((level - owner_level) % levels) * 2 + far_core) * blocks_here + local[:, :, :3]
-    amp_at = owner_level[:, :, 2:] * blocks_here + local[:, :, 2:3]
-    places = jnp.concatenate(
-        [factor_at[:, :, 1:2], factor_at[:, :, :1], amp_at, far_core[:, :, 2:], local[:, :, 3:]], axis=2
-    ).astype(jnp.int32)
-    places = places[(level + jnp.arange(levels)) % levels]
+    amps = (amps, other_core(amps))
 
     ladder = None
     calls = min(levels, 4)
     width = levels // calls
-    for call in reversed(range(calls)):
-        sums = ladders(places[call * width : (call + 1) * width], held, amps, back, matrix, blocks_here)
+    order = [2, 3, 1, 0] if calls == 4 else list(reversed(range(calls)))
+    for call in order:
+        first = call * width
+        sums = ladders(
+            first, width, levels, blocks_here, column[None], task_owners, task_local, held, amps, back, matrix
+        )
         for i in range(width):
-            by = call * width + i
-            term = (up(sums[i], by) if by else sums[i]).astype(F32)
+            term = (around(sums[i], first + i) if first + i else sums[i]).astype(F32)
             ladder = term if ladder is None else ladder + term
     return residual_in + ladder.transpose(0, 2, 1)
 

time: 184 us -> 177 us (0.962)
  starting transfers between devices: 26 us -> 44.8 us
  between operations: 13.7 us -> 0.43 us
  waiting for transfers between devices: 47.6 us -> 35.3 us
  other arithmetic: 3.4 us -> 0.2 us
  local copies, waits for them, and re-layouts: 14.8 us -> 17.8 us
    ppermute x6 -> x12, starting transfers between devices: 10.5 us -> 29.5 us  [the longest x6 17.7 us: hop(): lax.ppermute(x, 'task', [(c, c + by) for c in range(task_count) if 0 <= c...]
    all_gather x1 -> x0, waiting for transfers between devices: 18.2 us -> none  [per_device(): lax.all_gather(tiles, 'task', axis=0, tiled=True, axis_index_groups=same_...]
    unnamed x13 -> x59, local copies, waits for them, and re-layouts: 4.94 us -> 15.3 us
    pallas_call x8, Pallas kernels: 40 us -> 32.3 us  [prepare(): pl.pallas_call(functools.partial(prepare_kernel, len(parts)), out_shape=j...]
    pallas_call x4 -> x5, Pallas kernels: 38.1 us -> 45.7 us  [the longest x4 43 us: ladders(): pl.pallas_call(functools.partial(ladder_kernel, find, made), out_shape=ja...]
    ppermute x12, waiting for transfers between devices: 4.19 us -> 11.2 us  [gather_pairs(): lax.ppermute(x, 'pair', [(p, p ^ bit) for p in range(pair_count)])]
    reshape x3 -> x0, local copies, waits for them, and re-layouts: 3.32 us -> none  [the longest x1 1.37 us: per_device(): task_owners.reshape(levels, 2, -1, 3)]
    ppermute x6 -> x12, waiting for transfers between devices: 25.2 us -> 23 us  [the longest x6 15.7 us: around(): lax.ppermute(x, 'task', [(c, (c + 2 * by) % task_count) for c in range(ta...]
  transfers between devices with their start and end apart: 36 -> 41, of which waited for: 8 -> 9; matrix products, arithmetic and copies ran while one was open for 7% -> 4% of each run, Pallas kernels for 37% -> 38%
where the time goes in v3:
time: 177 us; the launch traced here: 176 us
  Pallas kernels  78 us (44%)
  starting transfers between devices  44.8 us (25%)
  waiting for transfers between devices  35.3 us (20%)
  local copies, waits for them, and re-layouts  17.8 us (10%)
    pallas_call x4, Pallas kernels, ladders(): pl.pallas_call(functools.partial(ladder_kernel, find, made), out_shape=ja...  43 us
    pallas_call x8, Pallas kernels, prepare(): pl.pallas_call(functools.partial(prepare_kernel, len(parts)), out_shape=j...  32.3 us
    ppermute x6, starting transfers between devices, hop(): lax.ppermute(x, 'task', [(c, c + by) for c in range(task_count) if 0 <= c...  17.7 us
    ppermute x6, waiting for transfers between devices, around(): lax.ppermute(x, 'task', [(c, (c + 2 * by) % task_count) for c in range(ta...  15.7 us
    unnamed x59, local copies, waits for them, and re-layouts  15.3 us
    ppermute x12, starting transfers between devices, gather_pairs(): lax.ppermute(x, 'pair', [(p, p ^ bit) for p in range(pair_count)])  12.5 us
    ppermute x6, starting transfers between devices, around(): lax.ppermute(x, 'task', [(c, (c + 2 * by) % task_count) for c in range(ta...  11.8 us
    ppermute x12, waiting for transfers between devices, gather_pairs(): lax.ppermute(x, 'pair', [(p, p ^ bit) for p in range(pair_count)])  11.2 us
  transfers between devices with their start and end apart: 41, of which 9 were waited for; matrix products, arithmetic and copies ran while one was open for 4% of the time, Pallas kernels for 38%

profile of v3, /device:TPU:0, one launch (start us, length us, event | category | flops | bytes accessed | tf_op | source)
XLA Modules:
  0.0 176.4 jit_solution(17073833370114763226)
XLA Ops:
  0.0 1.4 pad
  1.4 4.9 %collective-permute-start.31 = (bf16[625,256]{1,0:T(8,128)(2,1)S(1)}, bf16[625,256]{1,0:T(8,128)(2,1)S(1)}, u32[]{:S(2)}, u32[]{:S(2)}) collective-permute-start(bf16[625,256]{1,0:T(8,128)(2,1)S(1)} %bitcast.24), channel_id=1, source_target_pairs={{0,2},{1,3},{2,4},{3,5},{4,6},{5,7},{8,10},{9,11},{10,12},{11,13},... | collective-permute-start | bytes 960008 | tf_op jit(solution)/shard_map/ppermute | solution.py:290
  6.4 1.3 collective-permute-start.32
  7.8 4.1 %copy.30 = bf16[2,384,625]{2,1,0:T(8,128)(2,1)} copy(bf16[2,384,625]{1,0,2:T(2,128)(2,1)} %param.8) | data formatting | bytes 1920000 | tf_op args[0]
  11.9 1.4 dynamic-slice_bitcast_fusion
  13.3 2.7 %collective-permute-start.16 = (bf16[2,96,625]{2,1,0:T(8,128)(2,1)S(1)}, bf16[2,96,625]{2,1,0:T(8,128)(2,1)S(1)}, u32[]{:S(2)}, u32[]{:S(2)}) collective-permute-start(bf16[2,96,625]{2,1,0:T(8,128)(2,1)S(1)} %get-tuple-element.14), channel_id=1, source_target_pairs={{0,2},{1,3},{2,4},{3,5},{4,6},{5,7},{6,0},{7,1},{8,10},{9,11},{10,... | collective-permute-start | bytes 720008 | tf_op jit(solution)/shard_map/ppermute | solution.py:287
  16.0 2.6 %collective-permute-start.8 = (bf16[2,96,625]{2,1,0:T(8,128)(2,1)S(1)}, bf16[2,96,625]{2,1,0:T(8,128)(2,1)S(1)}, u32[]{:S(2)}, u32[]{:S(2)}) collective-permute-start(bf16[2,96,625]{2,1,0:T(8,128)(2,1)S(1)} %get-tuple-element.15), channel_id=1, source_target_pairs={{0,4},{1,5},{2,6},{3,7},{4,0},{5,1},{6,2},{7,3},{8,12},{9,13},{10,... | collective-permute-start | bytes 720008 | tf_op jit(solution)/shard_map/ppermute | solution.py:287
  18.6 1.3 collective-permute-start
  19.9 6.0 %collective-permute-done.16.refs_0_ = bf16[2,96,625]{2,1,0:T(8,128)(2,1)S(1)} collective-permute-done((bf16[2,96,625]{2,1,0:T(8,128)(2,1)S(1)}, bf16[2,96,625]{2,1,0:T(8,128)(2,1)S(1)}, u32[]{:S(2)}, u32[]{:S(2)}) %collective-permute-start.16) | collective-permute-done | bytes 240032 | tf_op jit(solution)/shard_map/ppermute | solution.py:287
  25.9 9.3 %collective-permute-done.8.refs_0_ = bf16[2,96,625]{2,1,0:T(8,128)(2,1)S(1)} collective-permute-done((bf16[2,96,625]{2,1,0:T(8,128)(2,1)S(1)}, bf16[2,96,625]{2,1,0:T(8,128)(2,1)S(1)}, u32[]{:S(2)}, u32[]{:S(2)}) %collective-permute-start.8) | collective-permute-done | bytes 240032 | tf_op jit(solution)/shard_map/ppermute | solution.py:287
  35.3 6.7 %collective-permute-start.33 = (bf16[625,256]{1,0:T(8,128)(2,1)S(1)}, bf16[625,256]{1,0:T(8,128)(2,1)S(1)}, u32[]{:S(2)}, u32[]{:S(2)}) collective-permute-start(bf16[625,256]{1,0:T(8,128)(2,1)S(1)} %collective-permute-done.31.refs_1_), channel_id=1, source_target_pairs={{0,2},{1,3},{2,4},{3,5},{4,6},{5,7},{8,10},{9,11},{10,12},{11,13},... | collective-permute-start | bytes 960008 | tf_op jit(solution)/shard_map/ppermute | solution.py:290
  42.0 1.3 collective-permute-start.34
  43.3 1.6 collective-permute-start.27
  44.8 3.2 %collective-permute-done.33.refs_2_ = bf16[625,256]{1,0:T(8,128)(2,1)S(1)} collective-permute-done((bf16[625,256]{1,0:T(8,128)(2,1)S(1)}, bf16[625,256]{1,0:T(8,128)(2,1)S(1)}, u32[]{:S(2)}, u32[]{:S(2)}) %collective-permute-start.33) | collective-permute-done | bytes 320032 | tf_op jit(solution)/shard_map/ppermute | solution.py:290
  48.0 4.1 %collective-permute-done.34.refs_5_ = bf16[625,256]{1,0:T(8,128)(2,1)S(1)} collective-permute-done((bf16[625,256]{1,0:T(8,128)(2,1)S(1)}, bf16[625,256]{1,0:T(8,128)(2,1)S(1)}, u32[]{:S(2)}, u32[]{:S(2)}) %collective-permute-start.34) | collective-permute-done | bytes 320032 | tf_op jit(solution)/shard_map/ppermute | solution.py:290
  52.2 2.2 %collective-permute-start.35 = (bf16[625,256]{1,0:T(8,128)(2,1)S(1)}, bf16[625,256]{1,0:T(8,128)(2,1)S(1)}, u32[]{:S(2)}, u32[]{:S(2)}) collective-permute-start(bf16[625,256]{1,0:T(8,128)(2,1)S(1)} %collective-permute-done.33.refs_2_), channel_id=1, source_target_pairs={{0,2},{1,3},{2,4},{3,5},{4,6},{5,7},{8,10},{9,11},{10,12},{11,13},... | collective-permute-start | bytes 960008 | tf_op jit(solution)/shard_map/ppermute | solution.py:290
  54.4 1.3 collective-permute-start.36
  55.7 1.6 collective-permute-start.25
  57.2 0.6 collective-permute-start.29
  57.8 5.7 %collective-permute-done.25.refs_1_ = bf16[2,96,625]{2,1,0:T(8,128)(2,1)S(1)} collective-permute-done((bf16[2,96,625]{2,1,0:T(8,128)(2,1)S(1)}, bf16[2,96,625]{2,1,0:T(8,128)(2,1)S(1)}, u32[]{:S(2)}, u32[]{:S(2)}) %collective-permute-start.25) | collective-permute-done | bytes 240032 | tf_op jit(solution)/shard_map/ppermute | solution.py:267
  63.5 2.5 %collective-permute-start.18 = (bf16[2,96,625]{2,1,0:T(8,128)(2,1)S(1)}, bf16[2,96,625]{2,1,0:T(8,128)(2,1)}, u32[]{:S(2)}, u32[]{:S(2)}) collective-permute-start(bf16[2,96,625]{2,1,0:T(8,128)(2,1)S(1)} %collective-permute-done.16.refs_0_), channel_id=1, source_target_pairs={{0,8},{8,0},{16,24},{24,16},{1,9},{9,1},{17,25},{25,17},{2,10},{10... | collective-permute-start | bytes 720008 | tf_op jit(solution)/shard_map/ppermute | solution.py:267
  66.1 1.5 collective-permute-start.20
  67.6 1.2 copy-done.3
  68.8 2.7 %shard_map.90.mine_ref = bf16[8,800,128]{2,1,0:T(8,128)(2,1)} custom-call(bf16[800,625]{1,0:T(8,128)(2,1)S(1)} %copy-done.3, bf16[625,256]{1,0:T(8,128)(2,1)S(1)} %bitcast.26, bf16[625,256]{1,0:T(8,128)(2,1)S(1)} %collective-permute-done.31.refs_1_, bf16[625,256]{1,0:T(8,128)(2,1)S(1)} %collective-permute-done.33.refs_2_, ...), custom_call_target="tpu_custom_call" | custom-call | flops 1024000000 | bytes 2560000 | tf_op jit(solution)/shard_map/pallas_call | solution.py:114
  71.5 0.5 collective-permute-start.37
  72.0 0.7 copy-done.24
  72.7 0.7 copy-done.16
  73.4 0.5 collective-permute-start.12
  73.9 0.5 collective-permute-start.10
  74.5 1.0 collective-permute-done.17.refs_0_
  75.5 0.7 copy-done.18
  76.2 0.5 collective-permute-start.2
  76.8 5.1 %collective-permute-done.12.refs_2_ = bf16[2,96,625]{2,1,0:T(8,128)(2,1)} collective-permute-done((bf16[2,96,625]{2,1,0:T(8,128)(2,1)S(1)}, bf16[2,96,625]{2,1,0:T(8,128)(2,1)}, u32[]{:S(2)}, u32[]{:S(2)}) %collective-permute-start.12) | collective-permute-done | bytes 240032 | tf_op jit(solution)/shard_map/ppermute | solution.py:267
  81.9 0.5 collective-permute-start.4
  82.8 0.6 copy-done.20
  83.4 0.7 copy-done.8
  84.1 1.5 collective-permute-start.22
  85.7 0.8 copy.31.owners_ref
  86.4 0.8 copy.32.local_ref
  87.2 1.6 copy-done
  88.8 0.9 copy-done.13
  89.7 0.9 copy-done.23
  90.7 4.9 %shard_map.82.refs_5_ = bf16[16,1600,384]{2,1,0:T(8,128)(2,1)} custom-call(bf16[2,96,625]{2,1,0:T(8,128)(2,1)S(1)} %get-tuple-element.13.refs_0_, bf16[2,96,625]{2,1,0:T(8,128)(2,1)S(1)} %copy-done.23, bf16[2,96,625]{2,1,0:T(8,128)(2,1)S(1)} %copy-done.13, bf16[2,96,625]{2,1,0:T(8,128)(2,1)} %collective-permute-done.29.refs_3_, bf16[1600,625]{1,0:T(8,128)(2,1)S(1)} %copy-done), custom_call_target="tpu_custom_call" | custom-call | flops 1536000000 | bytes 3417600 | tf_op jit(solution)/shard_map/pallas_call | solution.py:83
  95.6 0.5 collective-permute-start.21
  96.0 0.6 collective-permute-start.14
  96.7 4.5 %shard_map.83.refs_5_ = bf16[16,1600,384]{2,1,0:T(8,128)(2,1)} custom-call(bf16[2,96,625]{2,1,0:T(8,128)(2,1)S(1)} %copy-done.11, bf16[2,96,625]{2,1,0:T(8,128)(2,1)S(1)} %copy-done.25, bf16[2,96,625]{2,1,0:T(8,128)(2,1)S(1)} %copy-done.17, bf16[2,96,625]{2,1,0:T(8,128)(2,1)} %collective-permute-done.30.refs_3_, ...), custom_call_target="tpu_custom_call", output_to_operand_aliasing={{}: (5, {})} | custom-call | flops 1536000000 | bytes 3417600 | tf_op jit(solution)/shard_map/pallas_call | solution.py:83
  101.1 4.6 %shard_map.84.refs_5_ = bf16[16,1600,384]{2,1,0:T(8,128)(2,1)} custom-call(bf16[2,96,625]{2,1,0:T(8,128)(2,1)S(1)} %copy-done.7, bf16[2,96,625]{2,1,0:T(8,128)(2,1)} %collective-permute-done.18.refs_1_, bf16[2,96,625]{2,1,0:T(8,128)(2,1)S(1)} %copy-done.15, bf16[2,96,625]{2,1,0:T(8,128)(2,1)} %collective-permute-done.22.refs_3_, ...), custom_call_target="tpu_custom_call", output_to_operand_aliasing={{}: (5, {})} | custom-call | flops 1536000000 | bytes 3417600 | tf_op jit(solution)/shard_map/pallas_call | solution.py:83
  105.8 0.5 collective-permute-start.13
  106.3 0.5 collective-permute-start.6
  107.0 3.5 %shard_map.85.refs_5_ = bf16[16,1600,384]{2,1,0:T(8,128)(2,1)} custom-call(bf16[2,96,625]{2,1,0:T(8,128)(2,1)S(1)} %copy-done.19, bf16[2,96,625]{2,1,0:T(8,128)(2,1)S(1)} %collective-permute-done.19.refs_1_, bf16[2,96,625]{2,1,0:T(8,128)(2,1)S(1)} %collective-permute-done.21.refs_2_, ...), custom_call_target="tpu_custom_call", output_to_operand_aliasing={{}: (5, {})} | custom-call | flops 1536000000 | bytes 3417600 | tf_op jit(solution)/shard_map/pallas_call | solution.py:83
  110.5 4.5 %shard_map.86.refs_5_ = bf16[16,1600,384]{2,1,0:T(8,128)(2,1)} custom-call(bf16[2,96,625]{2,1,0:T(8,128)(2,1)S(1)} %copy-done.5, bf16[2,96,625]{2,1,0:T(8,128)(2,1)S(1)} %copy-done.21, bf16[2,96,625]{2,1,0:T(8,128)(2,1)} %collective-permute-done.12.refs_2_, bf16[2,96,625]{2,1,0:T(8,128)(2,1)S(1)} %collective-permute-done.14.refs_3_, ...), custom_call_target="tpu_custom_call", output_to_operand_aliasing={{}: (5, {})} | custom-call | flops 1536000000 | bytes 3417600 | tf_op jit(solution)/shard_map/pallas_call | solution.py:83
  115.0 0.4 collective-permute-start.1
  115.5 0.4 collective-permute-start.5
  116.0 3.4 %shard_map.87.refs_5_ = bf16[16,1600,384]{2,1,0:T(8,128)(2,1)} custom-call(bf16[2,96,625]{2,1,0:T(8,128)(2,1)S(1)} %copy-done.9, bf16[2,96,625]{2,1,0:T(8,128)(2,1)S(1)} %collective-permute-done.11.refs_1_, bf16[2,96,625]{2,1,0:T(8,128)(2,1)S(1)} %collective-permute-done.13.refs_2_, ...), custom_call_target="tpu_custom_call", output_to_operand_aliasing={{}: (5, {})} | custom-call | flops 1536000000 | bytes 3417600 | tf_op jit(solution)/shard_map/pallas_call | solution.py:83
  119.5 3.5 %shard_map.88.refs_5_ = bf16[16,1600,384]{2,1,0:T(8,128)(2,1)} custom-call(bf16[2,96,625]{2,1,0:T(8,128)(2,1)S(1)} %collective-permute-done.refs_0_, bf16[2,96,625]{2,1,0:T(8,128)(2,1)S(1)} %collective-permute-done.2.refs_1_, bf16[2,96,625]{2,1,0:T(8,128)(2,1)S(1)} %collective-permute-done.4.refs_2_, ...), custom_call_target="tpu_custom_call", output_to_operand_aliasing={{}: (5, {})} | custom-call | flops 1536000000 | bytes 3417600 | tf_op jit(solution)/shard_map/pallas_call | solution.py:83
  123.0 3.5 %shard_map.89.c_ref.r_ref = bf16[16,1600,384]{2,1,0:T(8,128)(2,1)} custom-call(bf16[2,96,625]{2,1,0:T(8,128)(2,1)S(1)} %collective-permute-done.1.refs_0_, bf16[2,96,625]{2,1,0:T(8,128)(2,1)S(1)} %collective-permute-done.3.refs_1_, bf16[2,96,625]{2,1,0:T(8,128)(2,1)S(1)} %collective-permute-done.5.refs_2_, ...), custom_call_target="tpu_custom_call", output_to_operand_aliasing={{}: (5, {})} | custom-call | flops 1536000000 | bytes 3417600 | tf_op jit(solution)/shard_map/pallas_call | solution.py:83
  126.4 10.7 %shard_map.91 = bf16[1,2,625,128]{3,2,1,0:T(8,128)(2,1)S(1)} custom-call(s32[1]{0:T(128)} %bitcast.column_ref, s32[32,3]{1,0:T(8,128)S(1)} %copy.31.owners_ref, s32[32,4]{1,0:T(8,128)S(1)} %copy.32.local_ref, bf16[16,1600,384]{2,1,0:T(8,128)(2,1)} %shard_map.89.c_ref.r_ref, bf16[16,1600,384]{2,1,0:T(8,128)(2,1)} %shard_map.89.c_ref.r_ref, ...), custom_call_target="tpu_custom_call" | custom-call | flops 2936012800 | bytes 6553600 | tf_op jit(solution)/shard_map/pallas_call | solution.py:247
  137.2 3.1 %collective-permute-start.38 = (bf16[2,625,128]{2,1,0:T(8,128)(2,1)S(1)}, bf16[2,625,128]{2,1,0:T(8,128)(2,1)S(1)}, u32[]{:S(2)}, u32[]{:S(2)}) collective-permute-start(bf16[2,625,128]{2,1,0:T(8,128)(2,1)S(1)} %bitcast.27), channel_id=1, source_target_pairs={{0,4},{1,5},{2,6},{3,7},{4,0},{5,1},{6,2},{7,3},{8,12},{9,13},{10,... | collective-permute-start | bytes 960008 | tf_op jit(solution)/shard_map/ppermute | solution.py:287
  140.2 10.9 %shard_map.92 = bf16[1,2,625,128]{3,2,1,0:T(8,128)(2,1)S(1)} custom-call(s32[1]{0:T(128)} %bitcast.column_ref, s32[32,3]{1,0:T(8,128)S(1)} %copy.31.owners_ref, s32[32,4]{1,0:T(8,128)S(1)} %copy.32.local_ref, bf16[16,1600,384]{2,1,0:T(8,128)(2,1)} %shard_map.89.c_ref.r_ref, bf16[16,1600,384]{2,1,0:T(8,128)(2,1)} %shard_map.89.c_ref.r_ref, ...), custom_call_target="tpu_custom_call" | custom-call | flops 2936012800 | bytes 6553600 | tf_op jit(solution)/shard_map/pallas_call | solution.py:247
  151.1 2.1 %collective-permute-start.39 = (bf16[2,625,128]{2,1,0:T(8,128)(2,1)S(1)}, bf16[2,625,128]{2,1,0:T(8,128)(2,1)S(1)}, u32[]{:S(2)}, u32[]{:S(2)}) collective-permute-start(bf16[2,625,128]{2,1,0:T(8,128)(2,1)S(1)} %bitcast.28), channel_id=1, source_target_pairs={{0,6},{1,7},{2,0},{3,1},{4,2},{5,3},{6,4},{7,5},{8,14},{9,15},{10,... | collective-permute-start | bytes 960008 | tf_op jit(solution)/shard_map/ppermute | solution.py:287
  153.2 10.7 %shard_map.93 = bf16[1,2,625,128]{3,2,1,0:T(8,128)(2,1)S(1)} custom-call(s32[1]{0:T(128)} %bitcast.column_ref, s32[32,3]{1,0:T(8,128)S(1)} %copy.31.owners_ref, s32[32,4]{1,0:T(8,128)S(1)} %copy.32.local_ref, bf16[16,1600,384]{2,1,0:T(8,128)(2,1)} %shard_map.89.c_ref.r_ref, bf16[16,1600,384]{2,1,0:T(8,128)(2,1)} %shard_map.89.c_ref.r_ref, ...), custom_call_target="tpu_custom_call" | custom-call | flops 2936012800 | bytes 6553600 | tf_op jit(solution)/shard_map/pallas_call | solution.py:247
  164.0 10.7 %shard_map.94 = bf16[1,2,625,128]{3,2,1,0:T(8,128)(2,1)S(1)} custom-call(s32[1]{0:T(128)} %bitcast.column_ref, s32[32,3]{1,0:T(8,128)S(1)} %copy.31.owners_ref, s32[32,4]{1,0:T(8,128)S(1)} %copy.32.local_ref, bf16[16,1600,384]{2,1,0:T(8,128)(2,1)} %shard_map.89.c_ref.r_ref, bf16[16,1600,384]{2,1,0:T(8,128)(2,1)} %shard_map.89.c_ref.r_ref, ...), custom_call_target="tpu_custom_call" | custom-call | flops 2936012800 | bytes 6553600 | tf_op jit(solution)/shard_map/pallas_call | solution.py:247
  174.7 0.4 collective-permute-done.40
  175.3 1.2 copy.40
  (93 shorter events, 1.4 us)
Async XLA Ops:
  0.0 96.6 %copy-start.1 = (bf16[1600,625]{1,0:T(8,128)(2,1)S(1)}, bf16[1600,625]{1,0:T(8,128)(2,1)}, u32[]{:S(2)}) copy-start(bf16[1600,625]{1,0:T(8,128)(2,1)} %constant.61.clone.refs_4_) | copy-start | bytes 6000004
  1.4 33.8 %collective-permute-start.31 = (bf16[625,256]{1,0:T(8,128)(2,1)S(1)}, bf16[625,256]{1,0:T(8,128)(2,1)S(1)}, u32[]{:S(2)}, u32[]{:S(2)}) collective-permute-start(bf16[625,256]{1,0:T(8,128)(2,1)S(1)} %bitcast.24), channel_id=1, source_target_pairs={{0,2},{1,3},{2,4},{3,5},{4,6},{5,7},{8,10},{9,11},{10,12},{11,13},... | collective-permute-start | bytes 960008 | tf_op jit(solution)/shard_map/ppermute | solution.py:290
  6.4 28.9 %collective-permute-start.32 = (bf16[625,256]{1,0:T(8,128)(2,1)S(1)}, bf16[625,256]{1,0:T(8,128)(2,1)S(1)}, u32[]{:S(2)}, u32[]{:S(2)}) collective-permute-start(bf16[625,256]{1,0:T(8,128)(2,1)S(1)} %bitcast.25), channel_id=1, source_target_pairs={{2,0},{3,1},{4,2},{5,3},{6,4},{7,5},{10,8},{11,9},{12,10},{13,11},... | collective-permute-start | bytes 960008 | tf_op jit(solution)/shard_map/ppermute | solution.py:290
  13.3 12.7 %collective-permute-start.16 = (bf16[2,96,625]{2,1,0:T(8,128)(2,1)S(1)}, bf16[2,96,625]{2,1,0:T(8,128)(2,1)S(1)}, u32[]{:S(2)}, u32[]{:S(2)}) collective-permute-start(bf16[2,96,625]{2,1,0:T(8,128)(2,1)S(1)} %get-tuple-element.14), channel_id=1, source_target_pairs={{0,2},{1,3},{2,4},{3,5},{4,6},{5,7},{6,0},{7,1},{8,10},{9,11},{10,... | collective-permute-start | bytes 720008 | tf_op jit(solution)/shard_map/ppermute | solution.py:287
  16.0 19.2 %collective-permute-start.8 = (bf16[2,96,625]{2,1,0:T(8,128)(2,1)S(1)}, bf16[2,96,625]{2,1,0:T(8,128)(2,1)S(1)}, u32[]{:S(2)}, u32[]{:S(2)}) collective-permute-start(bf16[2,96,625]{2,1,0:T(8,128)(2,1)S(1)} %get-tuple-element.15), channel_id=1, source_target_pairs={{0,4},{1,5},{2,6},{3,7},{4,0},{5,1},{6,2},{7,3},{8,12},{9,13},{10,... | collective-permute-start | bytes 720008 | tf_op jit(solution)/shard_map/ppermute | solution.py:287
  18.6 16.7 %collective-permute-start = (bf16[2,96,625]{2,1,0:T(8,128)(2,1)S(1)}, bf16[2,96,625]{2,1,0:T(8,128)(2,1)S(1)}, u32[]{:S(2)}, u32[]{:S(2)}) collective-permute-start(bf16[2,96,625]{2,1,0:T(8,128)(2,1)S(1)} %get-tuple-element.16), channel_id=1, source_target_pairs={{0,6},{1,7},{2,0},{3,1},{4,2},{5,3},{6,4},{7,5},{8,14},{9,15},{10,... | collective-permute-start | bytes 720008 | tf_op jit(solution)/shard_map/ppermute | solution.py:287
  25.9 56.8 %copy-start.6 = (bf16[2,96,625]{2,1,0:T(8,128)(2,1)}, bf16[2,96,625]{2,1,0:T(8,128)(2,1)S(1)}, u32[]{:S(2)}) copy-start(bf16[2,96,625]{2,1,0:T(8,128)(2,1)S(1)} %collective-permute-done.16.refs_0_) | copy-start | bytes 720004
  35.2 47.5 %copy-start.4 = (bf16[2,96,625]{2,1,0:T(8,128)(2,1)}, bf16[2,96,625]{2,1,0:T(8,128)(2,1)S(1)}, u32[]{:S(2)}) copy-start(bf16[2,96,625]{2,1,0:T(8,128)(2,1)S(1)} %collective-permute-done.8.refs_0_) | copy-start | bytes 720004
  35.3 12.8 %collective-permute-start.33 = (bf16[625,256]{1,0:T(8,128)(2,1)S(1)}, bf16[625,256]{1,0:T(8,128)(2,1)S(1)}, u32[]{:S(2)}, u32[]{:S(2)}) collective-permute-start(bf16[625,256]{1,0:T(8,128)(2,1)S(1)} %collective-permute-done.31.refs_1_), channel_id=1, source_target_pairs={{0,2},{1,3},{2,4},{3,5},{4,6},{5,7},{8,10},{9,11},{10,12},{11,13},... | collective-permute-start | bytes 960008 | tf_op jit(solution)/shard_map/ppermute | solution.py:290
  42.0 10.2 %collective-permute-start.34 = (bf16[625,256]{1,0:T(8,128)(2,1)S(1)}, bf16[625,256]{1,0:T(8,128)(2,1)S(1)}, u32[]{:S(2)}, u32[]{:S(2)}) collective-permute-start(bf16[625,256]{1,0:T(8,128)(2,1)S(1)} %collective-permute-done.32.refs_4_), channel_id=1, source_target_pairs={{2,0},{3,1},{4,2},{5,3},{6,4},{7,5},{10,8},{11,9},{12,10},{13,11},... | collective-permute-start | bytes 960008 | tf_op jit(solution)/shard_map/ppermute | solution.py:290
  43.3 14.0 %collective-permute-start.27 = (bf16[2,96,625]{2,1,0:T(8,128)(2,1)S(1)}, bf16[2,96,625]{2,1,0:T(8,128)(2,1)S(1)}, u32[]{:S(2)}, u32[]{:S(2)}) collective-permute-start(bf16[2,96,625]{2,1,0:T(8,128)(2,1)S(1)} %get-tuple-element.13.refs_0_), channel_id=1, source_target_pairs={{0,16},{8,24},{16,0},{24,8},{1,17},{9,25},{17,1},{25,9},{2,18},{10... | collective-permute-start | bytes 720008 | tf_op jit(solution)/shard_map/ppermute | solution.py:267
  52.2 13.9 %collective-permute-start.35 = (bf16[625,256]{1,0:T(8,128)(2,1)S(1)}, bf16[625,256]{1,0:T(8,128)(2,1)S(1)}, u32[]{:S(2)}, u32[]{:S(2)}) collective-permute-start(bf16[625,256]{1,0:T(8,128)(2,1)S(1)} %collective-permute-done.33.refs_2_), channel_id=1, source_target_pairs={{0,2},{1,3},{2,4},{3,5},{4,6},{5,7},{8,10},{9,11},{10,12},{11,13},... | collective-permute-start | bytes 960008 | tf_op jit(solution)/shard_map/ppermute | solution.py:290
  54.4 13.2 %collective-permute-start.36 = (bf16[625,256]{1,0:T(8,128)(2,1)S(1)}, bf16[625,256]{1,0:T(8,128)(2,1)S(1)}, u32[]{:S(2)}, u32[]{:S(2)}) collective-permute-start(bf16[625,256]{1,0:T(8,128)(2,1)S(1)} %collective-permute-done.34.refs_5_), channel_id=1, source_target_pairs={{2,0},{3,1},{4,2},{5,3},{6,4},{7,5},{10,8},{11,9},{12,10},{13,11},... | collective-permute-start | bytes 960008 | tf_op jit(solution)/shard_map/ppermute | solution.py:290
  55.7 7.8 %collective-permute-start.25 = (bf16[2,96,625]{2,1,0:T(8,128)(2,1)S(1)}, bf16[2,96,625]{2,1,0:T(8,128)(2,1)S(1)}, u32[]{:S(2)}, u32[]{:S(2)}) collective-permute-start(bf16[2,96,625]{2,1,0:T(8,128)(2,1)S(1)} %get-tuple-element.13.refs_0_), channel_id=1, source_target_pairs={{0,8},{8,0},{16,24},{24,16},{1,9},{9,1},{17,25},{25,17},{2,10},{10... | collective-permute-start | bytes 720008 | tf_op jit(solution)/shard_map/ppermute | solution.py:267
  57.2 6.3 %collective-permute-start.24 = (bf16[2,96,625]{2,1,0:T(8,128)(2,1)S(1)}, bf16[2,96,625]{2,1,0:T(8,128)(2,1)S(1)}, u32[]{:S(2)}, u32[]{:S(2)}) collective-permute-start(bf16[2,96,625]{2,1,0:T(8,128)(2,1)S(1)} %get-tuple-element.13.refs_0_), channel_id=1, source_target_pairs={{0,1},{1,0},{2,3},{3,2},{4,5},{5,4},{6,7},{7,6},{8,9},{9,8},{10,11... | collective-permute-start | bytes 720008 | tf_op jit(solution)/shard_map/ppermute | solution.py:284
  57.2 25.5 %copy-start.12 = (bf16[2,96,625]{2,1,0:T(8,128)(2,1)}, bf16[2,96,625]{2,1,0:T(8,128)(2,1)S(1)}, u32[]{:S(2)}) copy-start(bf16[2,96,625]{2,1,0:T(8,128)(2,1)S(1)} %collective-permute-done.27.refs_2_) | copy-start | bytes 720004
  57.2 14.3 %collective-permute-start.29 = (bf16[2,96,625]{2,1,0:T(8,128)(2,1)S(1)}, bf16[2,96,625]{2,1,0:T(8,128)(2,1)}, u32[]{:S(2)}, u32[]{:S(2)}) collective-permute-start(bf16[2,96,625]{2,1,0:T(8,128)(2,1)S(1)} %collective-permute-done.27.refs_2_), channel_id=1, source_target_pairs={{0,8},{8,0},{16,24},{24,16},{1,9},{9,1},{17,25},{25,17},{2,10},{10... | collective-permute-start | bytes 720008 | tf_op jit(solution)/shard_map/ppermute | solution.py:267
  63.5 19.2 %copy-start.22 = (bf16[2,96,625]{2,1,0:T(8,128)(2,1)}, bf16[2,96,625]{2,1,0:T(8,128)(2,1)S(1)}, u32[]{:S(2)}) copy-start(bf16[2,96,625]{2,1,0:T(8,128)(2,1)S(1)} %collective-permute-done.25.refs_1_) | copy-start | bytes 720004
  63.5 9.2 %collective-permute-start.28 = (bf16[2,96,625]{2,1,0:T(8,128)(2,1)S(1)}, bf16[2,96,625]{2,1,0:T(8,128)(2,1)S(1)}, u32[]{:S(2)}, u32[]{:S(2)}) collective-permute-start(bf16[2,96,625]{2,1,0:T(8,128)(2,1)S(1)} %collective-permute-done.27.refs_2_), channel_id=1, source_target_pairs={{0,1},{1,0},{2,3},{3,2},{4,5},{5,4},{6,7},{7,6},{8,9},{9,8},{10,11... | collective-permute-start | bytes 720008 | tf_op jit(solution)/shard_map/ppermute | solution.py:284
  63.5 19.2 %copy-start.10 = (bf16[2,96,625]{2,1,0:T(8,128)(2,1)}, bf16[2,96,625]{2,1,0:T(8,128)(2,1)S(1)}, u32[]{:S(2)}) copy-start(bf16[2,96,625]{2,1,0:T(8,128)(2,1)S(1)} %collective-permute-done.24.refs_0_) | copy-start | bytes 720004
  63.5 10.4 %collective-permute-start.18 = (bf16[2,96,625]{2,1,0:T(8,128)(2,1)S(1)}, bf16[2,96,625]{2,1,0:T(8,128)(2,1)}, u32[]{:S(2)}, u32[]{:S(2)}) collective-permute-start(bf16[2,96,625]{2,1,0:T(8,128)(2,1)S(1)} %collective-permute-done.16.refs_0_), channel_id=1, source_target_pairs={{0,8},{8,0},{16,24},{24,16},{1,9},{9,1},{17,25},{25,17},{2,10},{10... | collective-permute-start | bytes 720008 | tf_op jit(solution)/shard_map/ppermute | solution.py:267
  66.1 8.4 %collective-permute-start.20 = (bf16[2,96,625]{2,1,0:T(8,128)(2,1)S(1)}, bf16[2,96,625]{2,1,0:T(8,128)(2,1)S(1)}, u32[]{:S(2)}, u32[]{:S(2)}) collective-permute-start(bf16[2,96,625]{2,1,0:T(8,128)(2,1)S(1)} %collective-permute-done.16.refs_0_), channel_id=1, source_target_pairs={{0,16},{8,24},{16,0},{24,8},{1,17},{9,25},{17,1},{25,9},{2,18},{10... | collective-permute-start | bytes 720008 | tf_op jit(solution)/shard_map/ppermute | solution.py:267
  67.6 4.4 %collective-permute-start.26 = (bf16[2,96,625]{2,1,0:T(8,128)(2,1)S(1)}, bf16[2,96,625]{2,1,0:T(8,128)(2,1)S(1)}, u32[]{:S(2)}, u32[]{:S(2)}) collective-permute-start(bf16[2,96,625]{2,1,0:T(8,128)(2,1)S(1)} %collective-permute-done.25.refs_1_), channel_id=1, source_target_pairs={{0,1},{1,0},{2,3},{3,2},{4,5},{5,4},{6,7},{7,6},{8,9},{9,8},{10,11... | collective-permute-start | bytes 720008 | tf_op jit(solution)/shard_map/ppermute | solution.py:284
  67.6 1.2 copy-start.3
  71.5 54.9 %collective-permute-start.37 = (bf16[8,800,128]{2,1,0:T(8,128)(2,1)}, bf16[8,800,128]{2,1,0:T(8,128)(2,1)}, u32[]{:S(2)}, u32[]{:S(2)}) collective-permute-start(bf16[8,800,128]{2,1,0:T(8,128)(2,1)} %shard_map.90.mine_ref), channel_id=1, source_target_pairs={{0,1},{1,0},{2,3},{3,2},{4,5},{5,4},{6,7},{7,6},{8,9},{9,8},{10,11... | collective-permute-start | bytes 4915208 | tf_op jit(solution)/shard_map/ppermute | solution.py:284
  72.7 2.8 %collective-permute-start.17 = (bf16[2,96,625]{2,1,0:T(8,128)(2,1)S(1)}, bf16[2,96,625]{2,1,0:T(8,128)(2,1)S(1)}, u32[]{:S(2)}, u32[]{:S(2)}) collective-permute-start(bf16[2,96,625]{2,1,0:T(8,128)(2,1)S(1)} %collective-permute-done.16.refs_0_), channel_id=1, source_target_pairs={{0,1},{1,0},{2,3},{3,2},{4,5},{5,4},{6,7},{7,6},{8,9},{9,8},{10,11... | collective-permute-start | bytes 720008 | tf_op jit(solution)/shard_map/ppermute | solution.py:284
  73.4 8.5 %collective-permute-start.12 = (bf16[2,96,625]{2,1,0:T(8,128)(2,1)S(1)}, bf16[2,96,625]{2,1,0:T(8,128)(2,1)}, u32[]{:S(2)}, u32[]{:S(2)}) collective-permute-start(bf16[2,96,625]{2,1,0:T(8,128)(2,1)S(1)} %collective-permute-done.8.refs_0_), channel_id=1, source_target_pairs={{0,16},{8,24},{16,0},{24,8},{1,17},{9,25},{17,1},{25,9},{2,18},{10... | collective-permute-start | bytes 720008 | tf_op jit(solution)/shard_map/ppermute | solution.py:267
  73.9 8.8 %collective-permute-start.10 = (bf16[2,96,625]{2,1,0:T(8,128)(2,1)S(1)}, bf16[2,96,625]{2,1,0:T(8,128)(2,1)S(1)}, u32[]{:S(2)}, u32[]{:S(2)}) collective-permute-start(bf16[2,96,625]{2,1,0:T(8,128)(2,1)S(1)} %collective-permute-done.8.refs_0_), channel_id=1, source_target_pairs={{0,8},{8,0},{16,24},{24,16},{1,9},{9,1},{17,25},{25,17},{2,10},{10... | collective-permute-start | bytes 720008 | tf_op jit(solution)/shard_map/ppermute | solution.py:267
  74.5 8.3 %copy-start.14 = (bf16[2,96,625]{2,1,0:T(8,128)(2,1)}, bf16[2,96,625]{2,1,0:T(8,128)(2,1)S(1)}, u32[]{:S(2)}) copy-start(bf16[2,96,625]{2,1,0:T(8,128)(2,1)S(1)} %collective-permute-done.20.refs_2_) | copy-start | bytes 720004
  74.5 8.2 %collective-permute-start.9 = (bf16[2,96,625]{2,1,0:T(8,128)(2,1)S(1)}, bf16[2,96,625]{2,1,0:T(8,128)(2,1)S(1)}, u32[]{:S(2)}, u32[]{:S(2)}) collective-permute-start(bf16[2,96,625]{2,1,0:T(8,128)(2,1)S(1)} %collective-permute-done.8.refs_0_), channel_id=1, source_target_pairs={{0,1},{1,0},{2,3},{3,2},{4,5},{5,4},{6,7},{7,6},{8,9},{9,8},{10,11... | collective-permute-start | bytes 720008 | tf_op jit(solution)/shard_map/ppermute | solution.py:284
  75.5 0.7 copy-start.18
  76.2 19.3 %collective-permute-start.2 = (bf16[2,96,625]{2,1,0:T(8,128)(2,1)S(1)}, bf16[2,96,625]{2,1,0:T(8,128)(2,1)S(1)}, u32[]{:S(2)}, u32[]{:S(2)}) collective-permute-start(bf16[2,96,625]{2,1,0:T(8,128)(2,1)S(1)} %collective-permute-done.refs_0_), channel_id=1, source_target_pairs={{0,8},{8,0},{16,24},{24,16},{1,9},{9,1},{17,25},{25,17},{2,10},{10... | collective-permute-start | bytes 720008 | tf_op jit(solution)/shard_map/ppermute | solution.py:267
  81.9 13.6 %collective-permute-start.4 = (bf16[2,96,625]{2,1,0:T(8,128)(2,1)S(1)}, bf16[2,96,625]{2,1,0:T(8,128)(2,1)S(1)}, u32[]{:S(2)}, u32[]{:S(2)}) collective-permute-start(bf16[2,96,625]{2,1,0:T(8,128)(2,1)S(1)} %collective-permute-done.refs_0_), channel_id=1, source_target_pairs={{0,16},{8,24},{16,0},{24,8},{1,17},{9,25},{17,1},{25,9},{2,18},{10... | collective-permute-start | bytes 720008 | tf_op jit(solution)/shard_map/ppermute | solution.py:267
  82.7 13.3 %collective-permute-start.30 = (bf16[2,96,625]{2,1,0:T(8,128)(2,1)}, bf16[2,96,625]{2,1,0:T(8,128)(2,1)}, u32[]{:S(2)}, u32[]{:S(2)}) collective-permute-start(bf16[2,96,625]{2,1,0:T(8,128)(2,1)} %collective-permute-done.29.refs_3_), channel_id=1, source_target_pairs={{0,1},{1,0},{2,3},{3,2},{4,5},{5,4},{6,7},{7,6},{8,9},{9,8},{10,11... | collective-permute-start | bytes 720008 | tf_op jit(solution)/shard_map/ppermute | solution.py:284
  84.1 12.5 %collective-permute-start.22 = (bf16[2,96,625]{2,1,0:T(8,128)(2,1)}, bf16[2,96,625]{2,1,0:T(8,128)(2,1)}, u32[]{:S(2)}, u32[]{:S(2)}) collective-permute-start(bf16[2,96,625]{2,1,0:T(8,128)(2,1)} %collective-permute-done.18.refs_1_), channel_id=1, source_target_pairs={{0,16},{8,24},{16,0},{24,8},{1,17},{9,25},{17,1},{25,9},{2,18},{10... | collective-permute-start | bytes 720008 | tf_op jit(solution)/shard_map/ppermute | solution.py:267
  87.2 1.6 copy-start
  88.8 0.9 copy-start.13
  89.7 0.9 copy-start.23
  90.6 4.9 %copy-start.15 = (bf16[2,96,625]{2,1,0:T(8,128)(2,1)S(1)}, bf16[2,96,625]{2,1,0:T(8,128)(2,1)}, u32[]{:S(2)}) copy-start(bf16[2,96,625]{2,1,0:T(8,128)(2,1)} %copy-done.14) | copy-start | bytes 720004
  90.6 6.0 %copy-start.11 = (bf16[2,96,625]{2,1,0:T(8,128)(2,1)S(1)}, bf16[2,96,625]{2,1,0:T(8,128)(2,1)}, u32[]{:S(2)}) copy-start(bf16[2,96,625]{2,1,0:T(8,128)(2,1)} %copy-done.10) | copy-start | bytes 720004
  90.6 6.0 %copy-start.17 = (bf16[2,96,625]{2,1,0:T(8,128)(2,1)S(1)}, bf16[2,96,625]{2,1,0:T(8,128)(2,1)}, u32[]{:S(2)}) copy-start(bf16[2,96,625]{2,1,0:T(8,128)(2,1)} %copy-done.16) | copy-start | bytes 720004
  90.6 6.0 %copy-start.25 = (bf16[2,96,625]{2,1,0:T(8,128)(2,1)S(1)}, bf16[2,96,625]{2,1,0:T(8,128)(2,1)}, u32[]{:S(2)}) copy-start(bf16[2,96,625]{2,1,0:T(8,128)(2,1)} %copy-done.24) | copy-start | bytes 720004
  95.5 5.6 %copy-start.7 = (bf16[2,96,625]{2,1,0:T(8,128)(2,1)S(1)}, bf16[2,96,625]{2,1,0:T(8,128)(2,1)}, u32[]{:S(2)}) copy-start(bf16[2,96,625]{2,1,0:T(8,128)(2,1)} %copy-done.6) | copy-start | bytes 720004
  95.5 10.2 %collective-permute-start.19 = (bf16[2,96,625]{2,1,0:T(8,128)(2,1)}, bf16[2,96,625]{2,1,0:T(8,128)(2,1)S(1)}, u32[]{:S(2)}, u32[]{:S(2)}) collective-permute-start(bf16[2,96,625]{2,1,0:T(8,128)(2,1)} %collective-permute-done.18.refs_1_), channel_id=1, source_target_pairs={{0,1},{1,0},{2,3},{3,2},{4,5},{5,4},{6,7},{7,6},{8,9},{9,8},{10,11... | collective-permute-start | bytes 720008 | tf_op jit(solution)/shard_map/ppermute | solution.py:284
  95.6 10.7 %collective-permute-start.21 = (bf16[2,96,625]{2,1,0:T(8,128)(2,1)S(1)}, bf16[2,96,625]{2,1,0:T(8,128)(2,1)S(1)}, u32[]{:S(2)}, u32[]{:S(2)}) collective-permute-start(bf16[2,96,625]{2,1,0:T(8,128)(2,1)S(1)} %copy-done.15), channel_id=1, source_target_pairs={{0,1},{1,0},{2,3},{3,2},{4,5},{5,4},{6,7},{7,6},{8,9},{9,8},{10,11... | collective-permute-start | bytes 720008 | tf_op jit(solution)/shard_map/ppermute | solution.py:284
  96.0 10.3 %collective-permute-start.14 = (bf16[2,96,625]{2,1,0:T(8,128)(2,1)}, bf16[2,96,625]{2,1,0:T(8,128)(2,1)S(1)}, u32[]{:S(2)}, u32[]{:S(2)}) collective-permute-start(bf16[2,96,625]{2,1,0:T(8,128)(2,1)} %collective-permute-done.12.refs_2_), channel_id=1, source_target_pairs={{0,8},{8,0},{16,24},{24,16},{1,9},{9,1},{17,25},{25,17},{2,10},{10... | collective-permute-start | bytes 720008 | tf_op jit(solution)/shard_map/ppermute | solution.py:267
  96.6 10.2 %collective-permute-start.23 = (bf16[2,96,625]{2,1,0:T(8,128)(2,1)}, bf16[2,96,625]{2,1,0:T(8,128)(2,1)S(1)}, u32[]{:S(2)}, u32[]{:S(2)}) collective-permute-start(bf16[2,96,625]{2,1,0:T(8,128)(2,1)} %collective-permute-done.22.refs_3_), channel_id=1, source_target_pairs={{0,1},{1,0},{2,3},{3,2},{4,5},{5,4},{6,7},{7,6},{8,9},{9,8},{10,11... | collective-permute-start | bytes 720008 | tf_op jit(solution)/shard_map/ppermute | solution.py:284
  101.1 5.1 %copy-start.21 = (bf16[2,96,625]{2,1,0:T(8,128)(2,1)S(1)}, bf16[2,96,625]{2,1,0:T(8,128)(2,1)}, u32[]{:S(2)}) copy-start(bf16[2,96,625]{2,1,0:T(8,128)(2,1)} %copy-done.20) | copy-start | bytes 720004
  101.1 5.9 %copy-start.19 = (bf16[2,96,625]{2,1,0:T(8,128)(2,1)S(1)}, bf16[2,96,625]{2,1,0:T(8,128)(2,1)}, u32[]{:S(2)}) copy-start(bf16[2,96,625]{2,1,0:T(8,128)(2,1)} %copy-done.18) | copy-start | bytes 720004
  105.8 4.7 %copy-start.5 = (bf16[2,96,625]{2,1,0:T(8,128)(2,1)S(1)}, bf16[2,96,625]{2,1,0:T(8,128)(2,1)}, u32[]{:S(2)}) copy-start(bf16[2,96,625]{2,1,0:T(8,128)(2,1)} %copy-done.4) | copy-start | bytes 720004
  105.8 9.6 %collective-permute-start.13 = (bf16[2,96,625]{2,1,0:T(8,128)(2,1)}, bf16[2,96,625]{2,1,0:T(8,128)(2,1)S(1)}, u32[]{:S(2)}, u32[]{:S(2)}) collective-permute-start(bf16[2,96,625]{2,1,0:T(8,128)(2,1)} %collective-permute-done.12.refs_2_), channel_id=1, source_target_pairs={{0,1},{1,0},{2,3},{3,2},{4,5},{5,4},{6,7},{7,6},{8,9},{9,8},{10,11... | collective-permute-start | bytes 720008 | tf_op jit(solution)/shard_map/ppermute | solution.py:284
  106.3 8.7 %collective-permute-start.11 = (bf16[2,96,625]{2,1,0:T(8,128)(2,1)S(1)}, bf16[2,96,625]{2,1,0:T(8,128)(2,1)S(1)}, u32[]{:S(2)}, u32[]{:S(2)}) collective-permute-start(bf16[2,96,625]{2,1,0:T(8,128)(2,1)S(1)} %copy-done.21), channel_id=1, source_target_pairs={{0,1},{1,0},{2,3},{3,2},{4,5},{5,4},{6,7},{7,6},{8,9},{9,8},{10,11... | collective-permute-start | bytes 720008 | tf_op jit(solution)/shard_map/ppermute | solution.py:284
  106.3 9.2 %collective-permute-start.6 = (bf16[2,96,625]{2,1,0:T(8,128)(2,1)S(1)}, bf16[2,96,625]{2,1,0:T(8,128)(2,1)S(1)}, u32[]{:S(2)}, u32[]{:S(2)}) collective-permute-start(bf16[2,96,625]{2,1,0:T(8,128)(2,1)S(1)} %collective-permute-done.2.refs_1_), channel_id=1, source_target_pairs={{0,16},{8,24},{16,0},{24,8},{1,17},{9,25},{17,1},{25,9},{2,18},{10... | collective-permute-start | bytes 720008 | tf_op jit(solution)/shard_map/ppermute | solution.py:267
  106.9 9.0 %collective-permute-start.15 = (bf16[2,96,625]{2,1,0:T(8,128)(2,1)S(1)}, bf16[2,96,625]{2,1,0:T(8,128)(2,1)S(1)}, u32[]{:S(2)}, u32[]{:S(2)}) collective-permute-start(bf16[2,96,625]{2,1,0:T(8,128)(2,1)S(1)} %collective-permute-done.14.refs_3_), channel_id=1, source_target_pairs={{0,1},{1,0},{2,3},{3,2},{4,5},{5,4},{6,7},{7,6},{8,9},{9,8},{10,11... | collective-permute-start | bytes 720008 | tf_op jit(solution)/shard_map/ppermute | solution.py:284
  110.5 5.5 %copy-start.9 = (bf16[2,96,625]{2,1,0:T(8,128)(2,1)S(1)}, bf16[2,96,625]{2,1,0:T(8,128)(2,1)}, u32[]{:S(2)}) copy-start(bf16[2,96,625]{2,1,0:T(8,128)(2,1)} %copy-done.8) | copy-start | bytes 720004
  115.0 8.0 %collective-permute-start.1 = (bf16[2,96,625]{2,1,0:T(8,128)(2,1)S(1)}, bf16[2,96,625]{2,1,0:T(8,128)(2,1)S(1)}, u32[]{:S(2)}, u32[]{:S(2)}) collective-permute-start(bf16[2,96,625]{2,1,0:T(8,128)(2,1)S(1)} %collective-permute-done.refs_0_), channel_id=1, source_target_pairs={{0,1},{1,0},{2,3},{3,2},{4,5},{5,4},{6,7},{7,6},{8,9},{9,8},{10,11... | collective-permute-start | bytes 720008 | tf_op jit(solution)/shard_map/ppermute | solution.py:284
  115.3 7.6 %collective-permute-start.3 = (bf16[2,96,625]{2,1,0:T(8,128)(2,1)S(1)}, bf16[2,96,625]{2,1,0:T(8,128)(2,1)S(1)}, u32[]{:S(2)}, u32[]{:S(2)}) collective-permute-start(bf16[2,96,625]{2,1,0:T(8,128)(2,1)S(1)} %collective-permute-done.2.refs_1_), channel_id=1, source_target_pairs={{0,1},{1,0},{2,3},{3,2},{4,5},{5,4},{6,7},{7,6},{8,9},{9,8},{10,11... | collective-permute-start | bytes 720008 | tf_op jit(solution)/shard_map/ppermute | solution.py:284
  115.5 7.5 %collective-permute-start.5 = (bf16[2,96,625]{2,1,0:T(8,128)(2,1)S(1)}, bf16[2,96,625]{2,1,0:T(8,128)(2,1)S(1)}, u32[]{:S(2)}, u32[]{:S(2)}) collective-permute-start(bf16[2,96,625]{2,1,0:T(8,128)(2,1)S(1)} %collective-permute-done.4.refs_2_), channel_id=1, source_target_pairs={{0,1},{1,0},{2,3},{3,2},{4,5},{5,4},{6,7},{7,6},{8,9},{9,8},{10,11... | collective-permute-start | bytes 720008 | tf_op jit(solution)/shard_map/ppermute | solution.py:284
  115.9 7.1 %collective-permute-start.7 = (bf16[2,96,625]{2,1,0:T(8,128)(2,1)S(1)}, bf16[2,96,625]{2,1,0:T(8,128)(2,1)S(1)}, u32[]{:S(2)}, u32[]{:S(2)}) collective-permute-start(bf16[2,96,625]{2,1,0:T(8,128)(2,1)S(1)} %collective-permute-done.6.refs_3_), channel_id=1, source_target_pairs={{0,1},{1,0},{2,3},{3,2},{4,5},{5,4},{6,7},{7,6},{8,9},{9,8},{10,11... | collective-permute-start | bytes 720008 | tf_op jit(solution)/shard_map/ppermute | solution.py:284
  122.9 3.5 %copy-start.2 = (bf16[625,800]{1,0:T(8,128)(2,1)S(1)}, bf16[625,800]{1,0:T(8,128)(2,1)}, u32[]{:S(2)}) copy-start(bf16[625,800]{1,0:T(8,128)(2,1)} %constant.62.clone.back_ref) | copy-start | bytes 3000004
  137.2 37.5 %collective-permute-start.38 = (bf16[2,625,128]{2,1,0:T(8,128)(2,1)S(1)}, bf16[2,625,128]{2,1,0:T(8,128)(2,1)S(1)}, u32[]{:S(2)}, u32[]{:S(2)}) collective-permute-start(bf16[2,625,128]{2,1,0:T(8,128)(2,1)S(1)} %bitcast.27), channel_id=1, source_target_pairs={{0,4},{1,5},{2,6},{3,7},{4,0},{5,1},{6,2},{7,3},{8,12},{9,13},{10,... | collective-permute-start | bytes 960008 | tf_op jit(solution)/shard_map/ppermute | solution.py:287
  151.1 23.6 %collective-permute-start.39 = (bf16[2,625,128]{2,1,0:T(8,128)(2,1)S(1)}, bf16[2,625,128]{2,1,0:T(8,128)(2,1)S(1)}, u32[]{:S(2)}, u32[]{:S(2)}) collective-permute-start(bf16[2,625,128]{2,1,0:T(8,128)(2,1)S(1)} %bitcast.28), channel_id=1, source_target_pairs={{0,6},{1,7},{2,0},{3,1},{4,2},{5,3},{6,4},{7,5},{8,14},{9,15},{10,... | collective-permute-start | bytes 960008 | tf_op jit(solution)/shard_map/ppermute | solution.py:287
  163.9 11.2 %copy-start.26 = (f32[2,128,625]{1,0,2:T(2,128)S(1)}, f32[2,128,625]{1,0,2:T(2,128)}, u32[]{:S(2)}) copy-start(f32[2,128,625]{1,0,2:T(2,128)} %param.10) | copy-start | bytes 1920004
  163.9 11.2 %collective-permute-start.40 = (bf16[2,625,128]{2,1,0:T(8,128)(2,1)S(1)}, bf16[2,625,128]{2,1,0:T(8,128)(2,1)S(1)}, u32[]{:S(2)}, u32[]{:S(2)}) collective-permute-start(bf16[2,625,128]{2,1,0:T(8,128)(2,1)S(1)} %bitcast.29), channel_id=1, source_target_pairs={{0,2},{1,3},{2,4},{3,5},{4,6},{5,7},{6,0},{7,1},{8,10},{9,11},{10,... | collective-permute-start | bytes 960008 | tf_op jit(solution)/shard_map/ppermute | solution.py:287
  (4 other events, 2.8 us)

commit v4 on v3

--- a/solution.py
+++ b/solution.py
@@ -68,33 +68,26 @@
             forms_ref[first + m] = made[:, m * depth : (m + 1) * depth]
 
 
-def prepare(parts, first, total, matrix, held):
+def prepare(parts, matrix):
     count, size, width = parts[0].shape
     depth = size * len(parts)
     rows = matrix.shape[0] // PREPARE_STEPS
     in_specs = [pl.BlockSpec(part.shape, lambda i: (0, 0, 0)) for part in parts]
     in_specs.append(pl.BlockSpec((rows, width), lambda i: (i, 0)))
-    operands = [*parts, matrix]
-    aliases = {}
-    if held is not None:
-        aliases = {len(operands): 0}
-        in_specs.append(pl.BlockSpec(memory_space=pl.ANY))
-        operands.append(held)
     return pl.pallas_call(
         functools.partial(prepare_kernel, len(parts)),
-        out_shape=jax.ShapeDtypeStruct((total, matrix.shape[0], depth), BF),
+        out_shape=jax.ShapeDtypeStruct((count, matrix.shape[0], depth), BF),
         grid=(PREPARE_STEPS,),
         in_specs=in_specs,
-        out_specs=pl.BlockSpec((count, rows, depth), lambda i: (first, i, 0)),
+        out_specs=pl.BlockSpec((count, rows, depth), lambda i: (0, i, 0)),
         scratch_shapes=[pltpu.VMEM((count * depth, width), BF)],
-        input_output_aliases=aliases,
         compiler_params=pltpu.CompilerParams(vmem_limit_bytes=VMEM_BYTES),
         cost_estimate=pl.CostEstimate(
             flops=2 * count * depth * width * matrix.shape[0],
             bytes_accessed=2 * count * depth * (width + matrix.shape[0]),
             transcendentals=0,
         ),
-    )(*operands)
+    )(*parts, matrix)
 
 
 def amp_kernel(levels, matrix_ref, *refs):
@@ -128,34 +121,51 @@
     return jnp.concatenate([ref[x * PAD : (x + 1) * PAD, :] for x in numbers], axis=0)
 
 
-def ladder_kernel(
-    find, made, column_ref, owners_ref, local_ref, c_ref, r_ref, mine_ref, other_ref, back_ref, *refs
-):
-    matrix_ref = None if made else refs[0]
-    out_ref, v_ref, u_ref, amp_ref, acc_ref = refs[:5] if made else refs[1:6]
+def ladder_kernel(find, made, sources, column_ref, owners_ref, local_ref, *refs):
+    factor_refs, amp_refs, refs = refs[:sources], refs[sources : sources + 2], refs[sources + 2 :]
+    back_ref, matrix_ref, refs = refs[0], None if made else refs[1], refs[1 if made else 2 :]
+    out_ref, v_ref, u_ref, acc_ref, c_buf, r_buf, amp_buf, sems = refs[:8]
+    column, columns = pl.program_id(0), pl.num_programs(0)
     step, steps = pl.program_id(1), pl.num_programs(1)
-    places = find(pl.program_id(0), step, column_ref, owners_ref, local_ref)
+    at = column * steps + step
+    slot = lax.rem(at, 2)
+
+    def fetch(choices, source, index, part, buffer, to, sem):
+        for n, ref in enumerate(choices):
+
+            @pl.when(source == n)
+            def _():
+                tile = ref.at[index, pl.ds(part * ROWS, ROWS)] if part is not None else ref.at[index]
+                pltpu.make_async_copy(tile, buffer.at[to], sem).start()
+
+    def fetch_task(i, j, to):
+        places = find(i, j, column_ref, owners_ref, local_ref)
+        fetch(factor_refs, *places["col"], 0 if made else None, c_buf, to, sems.at[to, 0])
+        fetch(factor_refs, *places["row"], 1 if made else None, r_buf, to, sems.at[to, 1])
+        fetch(amp_refs, *places["amp"], None, amp_buf, to, sems.at[to, 2])
+
+    @pl.when(at == 0)
+    def _():
+        fetch_task(0, 0, 0)
+
+    @pl.when(at + 1 < columns * steps)
+    def _():
+        last = step == steps - 1
+        fetch_task(jnp.where(last, column + 1, column), jnp.where(last, 0, step + 1), 1 - slot)
 
     @pl.when(step == 0)
     def _():
         acc_ref[...] = jnp.zeros_like(acc_ref)
 
-    @pl.when(places["amp_core"] == 0)
-    def _():
-        amp_ref[...] = mine_ref[0]
-
-    @pl.when(places["amp_core"] != 0)
-    def _():
-        amp_ref[...] = other_ref[0]
-
-    if made:
-        c_form, r_form = c_ref.at[0], r_ref.at[0]
-    else:
-        forms = refs[6]
-        for i, tile_ref in enumerate((c_ref, r_ref)):
+    for n, buffer in enumerate((c_buf, r_buf, amp_buf)):
+        pltpu.make_async_copy(buffer.at[slot], buffer.at[slot], sems.at[slot, n]).wait()
+    c_form, r_form, amp_form = c_buf.at[slot], r_buf.at[slot], amp_buf.at[slot]
+    if not made:
+        forms = refs[8]
+        for i, tile in enumerate((c_form, r_form)):
             forms[i] = lax.dot_general(
                 matrix_ref[i * ROWS : (i + 1) * ROWS, :],
-                tile_ref[0],
+                tile[...],
                 (((1,), (1,)), ((), ())),
                 preferred_element_type=F32,
             ).astype(BF)
@@ -187,9 +197,10 @@
                     for p in range(1, GROUP):
                         block = jnp.where(at_spot[p], blocks[(p - i) % GROUP], block)
                     u_ref[START[i] + A * PAD : START[i] + (A + 1) * PAD, D * LANES : (D + 1) * LANES] = block.astype(BF)
+    out = local_ref[find(column, step, column_ref, owners_ref, local_ref)["task"], 3]
     for i in range(GROUP):
-        acc_ref[places["out"], START[i] : START[i + 1], :] += jnp.dot(
-            u_ref[START[i] : START[i + 1], :], turned(amp_ref, range(GROUPS), i), preferred_element_type=F32
+        acc_ref[out, START[i] : START[i + 1], :] += jnp.dot(
+            u_ref[START[i] : START[i + 1], :], turned(amp_form, range(GROUPS), i), preferred_element_type=F32
         )
 
     @pl.when(step == steps - 1)
@@ -201,9 +212,9 @@
 def ladders(first, columns, levels, blocks_here, column, task_owners, task_local, tiles, amps, back, matrix):
     tasks = task_owners.shape[0] // (2 * levels)
     pairs = amps[0].shape[2]
-    made = tiles.shape[1] == 2 * ROWS
-    depth = tiles.shape[2] if made else tiles.shape[1]
-    held = (1, ROWS, depth) if made else (1, *tiles.shape[1:])
+    made = tiles[0].shape[1] == 2 * ROWS
+    depth = tiles[0].shape[2] if made else tiles[0].shape[1]
+    held = (ROWS, depth) if made else tiles[0].shape[1:]
 
     def find(i, j, column_ref, owners_ref, local_ref):
         level, core = column_ref[0] // 2, lax.rem(column_ref[0], 2)
@@ -215,37 +226,32 @@
             far = jnp.where(lax.rem(owner, 2) != core, 1, 0)
             return below, far, local_ref[task, kind]
 
-        (row_below, row_far, row_m), (col_below, col_far, col_m), (amp_below, amp_far, amp_m) = map(place, range(3))
-        return {
-            "row": (row_below * 2 + row_far) * blocks_here + row_m,
-            "col": (col_below * 2 + col_far) * blocks_here + col_m,
-            "amp": amp_below * blocks_here + amp_m,
-            "amp_core": amp_far,
-            "out": local_ref[task, 3],
-        }
-
+        def factor(kind):
+            below, far, m = place(kind)
+            return (below * 2 + far, m) if made else (0, (below * 2 + far) * blocks_here + m)
+
+        below, far, m = place(2)
+        return {"task": task, "row": factor(0), "col": factor(1), "amp": (far, below * blocks_here + m)}
+
+    anywhere = pl.BlockSpec(memory_space=pl.ANY)
     fixed = lambda shape: pl.BlockSpec(shape, lambda i, j, *tables: (0,) * len(shape))
-    amp_spec = pl.BlockSpec((1, ROWS, pairs), lambda i, j, *tables: (find(i, j, *tables)["amp"], 0, 0))
-    in_specs = [
-        pl.BlockSpec(held, lambda i, j, *tables: (find(i, j, *tables)["col"], 0, 0)),
-        pl.BlockSpec(held, lambda i, j, *tables: (find(i, j, *tables)["row"], int(made), 0)),
-        amp_spec,
-        amp_spec,
-        fixed(back.shape),
-    ]
+    operands = [*tiles, *amps, back]
+    in_specs = [anywhere] * (len(tiles) + 2) + [fixed(back.shape)]
     scratch = [
         pltpu.VMEM((ROWS, WIDE), F32),
         pltpu.VMEM((ROWS, WIDE), BF),
-        pltpu.VMEM((ROWS, pairs), BF),
         pltpu.VMEM((blocks_here, ROWS, pairs), F32),
+        pltpu.VMEM((2, *held), BF),
+        pltpu.VMEM((2, *held), BF),
+        pltpu.VMEM((2, ROWS, pairs), BF),
+        pltpu.SemaphoreType.DMA((2, 3)),
     ]
-    operands = [tiles, tiles, *amps, back]
     if not made:
         in_specs.append(fixed(matrix.shape))
         scratch.append(pltpu.VMEM((2, ROWS, depth), BF))
         operands.append(matrix)
     return pl.pallas_call(
-        functools.partial(ladder_kernel, find, made),
+        functools.partial(ladder_kernel, find, made, len(tiles)),
         out_shape=jax.ShapeDtypeStruct((columns, blocks_here, TV * TV, pairs), BF),
         grid_spec=pltpu.PrefetchScalarGridSpec(
             num_scalar_prefetch=3,
@@ -263,10 +269,8 @@
     )(column, task_owners, task_local, *operands)
 
 
-def gather_pairs(part, by, pair_count):
-    beside = lambda x, bit: lax.ppermute(x, "pair", [(p, p ^ bit) for p in range(pair_count)])
-    across, along = beside(part, 1), beside(part, 2)
-    return [part, across, along, beside(along, 1) if by % 2 == 0 else beside(across, 2)]
+def beside(x, bit, pair_count):
+    return lax.ppermute(x, "pair", [(p, p ^ bit) for p in range(pair_count)])
 
 
 def per_device(factor_blocks, amplitudes, residual_in, task_owners, task_local):
@@ -294,17 +298,20 @@
     parts = [mine[0]] + [around(mine[by], by) for by in range(1, levels)]
     if pair_count == 4:
         own = amplitudes.transpose(2, 0, 1).reshape(TV * TV, blocks_here * pairs)
+        (own,), _ = lax.optimization_barrier(((own,), parts[1:]))
         ups, downs = [hop(own, 2)], [hop(own, -2)]
         for by in range(2, levels):
-            (up, down), _ = lax.optimization_barrier(((ups[-1], downs[-1]), parts[1:]))
-            ups.append(hop(up, 2))
-            downs.append(hop(down, -2))
+            ups.append(hop(ups[-1], 2))
+            downs.append(hop(downs[-1], -2))
         amps = prepare_amps(own, ups, downs, blocks_here, jnp.asarray(amp_matrix()))
-        held = None
+        held, flying = [], ()
         for by, part in enumerate(parts):
-            pieces = gather_pairs(part, by, pair_count)
-            held = prepare(pieces, 2 * by, total, matrix, held)
-            held = prepare([other_core(piece) for piece in pieces], 2 * by + 1, total, matrix, held)
+            part, flying = lax.optimization_barrier((part, flying))
+            across, along = beside(part, 1, pair_count), beside(part, 2, pair_count)
+            corner = beside(along, 1, pair_count) if by % 2 == 0 else beside(across, 2, pair_count)
+            flying = (across, along)
+            forms = prepare([part, across, along, corner], matrix)
+            held += [forms, other_core(forms)]
     else:
         tiles = amplitudes.reshape(blocks_here, pairs, TV, TV).transpose(0, 3, 2, 1)
         tiles = jnp.pad(tiles, ((0, 0), (0, 0), (0, PAD - TV), (0, 0))).reshape(blocks_here, ROWS, pairs)
@@ -312,7 +319,7 @@
         amps = lax.all_gather(tiles, "task", axis=0, axis_index_groups=same_core)
         amps = amps[(level - jnp.arange(levels)) % levels].reshape(levels * blocks_here, ROWS, pairs)
         held = lax.all_gather(jnp.stack(parts), "pair", axis=2, tiled=True)
-        held = jnp.stack([held, other_core(held)], axis=1).reshape(total, depth * pair_count, -1)
+        held = [jnp.stack([held, other_core(held)], axis=1).reshape(total, depth * pair_count, -1)]
     amps = (amps, other_core(amps))
 
     ladder = None

time: 177 us -> 148 us (0.84)
  Pallas kernels: 78 us -> 57.7 us
  local copies, waits for them, and re-layouts: 17.8 us -> 6.54 us
  starting transfers between devices: 44.8 us -> 49.6 us
    pallas_call x8 -> x4, Pallas kernels: 32.3 us -> 13.9 us  [prepare(): pl.pallas_call(functools.partial(prepare_kernel, len(parts)), out_shape=j...]
    unnamed x59 -> x19, local copies, waits for them, and re-layouts: 15.3 us -> 5.23 us
    ppermute x12, waiting for transfers between devices: 11.2 us -> 1.56 us  [beside(): return lax.ppermute(x, 'pair', [(p, p ^ bit) for p in range(pair_count)])]
    ppermute x6, waiting for transfers between devices: 7.34 us -> 16.9 us  [hop(): lax.ppermute(x, 'task', [(c, c + by) for c in range(task_count) if 0 <= c...]
    ppermute x6, starting transfers between devices: 17.7 us -> 22.5 us  [hop(): lax.ppermute(x, 'task', [(c, c + by) for c in range(task_count) if 0 <= c...]
    ppermute x6, waiting for transfers between devices: 15.7 us -> 12 us  [around(): lax.ppermute(x, 'task', [(c, (c + 2 * by) % task_count) for c in range(ta...]
    ppermute x17 -> x5, waiting for transfers between devices: 1.05 us -> 3.31 us  [per_device(): lax.ppermute(x, 'task', [(c, c ^ 1) for c in range(task_count)])]
    ppermute x17 -> x5, starting transfers between devices: 2.77 us -> 0.86 us  [per_device(): lax.ppermute(x, 'task', [(c, c ^ 1) for c in range(task_count)])]
  transfers between devices with their start and end apart: 41 -> 29, of which waited for: 9 -> 7; matrix products, arithmetic and copies ran while one was open for 4% -> 0% of each run, Pallas kernels for 38% -> 32%
where the time goes in v4:
time: 148 us
  Pallas kernels  57.7 us (39%)
  starting transfers between devices  49.6 us (34%)
  waiting for transfers between devices  33.7 us (23%)
  local copies, waits for them, and re-layouts  6.54 us (4%)
    pallas_call x4, Pallas kernels, ladders(): pl.pallas_call(functools.partial(ladder_kernel, find, made, len(tiles)),...  42.3 us
    ppermute x6, starting transfers between devices, hop(): lax.ppermute(x, 'task', [(c, c + by) for c in range(task_count) if 0 <= c...  22.5 us
    ppermute x6, waiting for transfers between devices, hop(): lax.ppermute(x, 'task', [(c, c + by) for c in range(task_count) if 0 <= c...  16.9 us
    ppermute x12, starting transfers between devices, beside(): return lax.ppermute(x, 'pair', [(p, p ^ bit) for p in range(pair_count)])  14 us
    pallas_call x4, Pallas kernels, prepare(): pl.pallas_call(functools.partial(prepare_kernel, len(parts)), out_shape=j...  13.9 us
    ppermute x6, starting transfers between devices, around(): lax.ppermute(x, 'task', [(c, (c + 2 * by) % task_count) for c in range(ta...  12.2 us
    ppermute x6, waiting for transfers between devices, around(): lax.ppermute(x, 'task', [(c, (c + 2 * by) % task_count) for c in range(ta...  12 us
    unnamed x19, local copies, waits for them, and re-layouts  5.23 us
  transfers between devices with their start and end apart: 29, of which 7 were waited for; matrix products, arithmetic and copies ran while one was open for 0% of the time, Pallas kernels for 32%

profile of v4, /device:TPU:0, one launch (start us, length us, event | category | flops | bytes accessed | tf_op | source)
XLA Modules:
  0.0 148.0 jit_solution(2662715557773414800)
XLA Ops:
  0.0 3.5 %copy.23 = bf16[2,384,625]{2,1,0:T(8,128)(2,1)S(1)} copy(bf16[2,384,625]{1,0,2:T(2,128)(2,1)} %param.8) | data formatting | bytes 1920000 | tf_op args[0]
  3.5 0.1 dynamic-slice_bitcast_fusion
  3.7 3.1 %collective-permute-start.4 = (bf16[2,96,625]{2,1,0:T(8,128)(2,1)S(1)}, bf16[2,96,625]{2,1,0:T(8,128)(2,1)S(1)}, u32[]{:S(2)}, u32[]{:S(2)}) collective-permute-start(bf16[2,96,625]{2,1,0:T(8,128)(2,1)S(1)} %get-tuple-element.15), channel_id=1, source_target_pairs={{0,2},{1,3},{2,4},{3,5},{4,6},{5,7},{6,0},{7,1},{8,10},{9,11},{10,... | collective-permute-start | bytes 720008 | tf_op jit(solution)/shard_map/ppermute | solution.py:291
  6.7 1.5 %collective-permute-start.1 = (bf16[2,96,625]{2,1,0:T(8,128)(2,1)S(1)}, bf16[2,96,625]{2,1,0:T(8,128)(2,1)S(1)}, u32[]{:S(2)}, u32[]{:S(2)}) collective-permute-start(bf16[2,96,625]{2,1,0:T(8,128)(2,1)S(1)} %get-tuple-element.16.refs_0_), channel_id=1, source_target_pairs={{0,16},{8,24},{16,0},{24,8},{1,17},{9,25},{17,1},{25,9},{2,18},{10... | collective-permute-start | bytes 720008 | tf_op jit(solution)/shard_map/ppermute | solution.py:273
  8.3 1.5 %collective-permute-start = (bf16[2,96,625]{2,1,0:T(8,128)(2,1)S(1)}, bf16[2,96,625]{2,1,0:T(8,128)(2,1)S(1)}, u32[]{:S(2)}, u32[]{:S(2)}) collective-permute-start(bf16[2,96,625]{2,1,0:T(8,128)(2,1)S(1)} %get-tuple-element.16.refs_0_), channel_id=1, source_target_pairs={{0,8},{8,0},{16,24},{24,16},{1,9},{9,1},{17,25},{25,17},{2,10},{10... | collective-permute-start | bytes 720008 | tf_op jit(solution)/shard_map/ppermute | solution.py:273
  9.8 2.6 %collective-permute-start.9 = (bf16[2,96,625]{2,1,0:T(8,128)(2,1)S(1)}, bf16[2,96,625]{2,1,0:T(8,128)(2,1)S(1)}, u32[]{:S(2)}, u32[]{:S(2)}) collective-permute-start(bf16[2,96,625]{2,1,0:T(8,128)(2,1)S(1)} %get-tuple-element.14), channel_id=1, source_target_pairs={{0,4},{1,5},{2,6},{3,7},{4,0},{5,1},{6,2},{7,3},{8,12},{9,13},{10,... | collective-permute-start | bytes 720008 | tf_op jit(solution)/shard_map/ppermute | solution.py:291
  12.3 3.3 %collective-permute-done.4.refs_0_ = bf16[2,96,625]{2,1,0:T(8,128)(2,1)S(1)} collective-permute-done((bf16[2,96,625]{2,1,0:T(8,128)(2,1)S(1)}, bf16[2,96,625]{2,1,0:T(8,128)(2,1)S(1)}, u32[]{:S(2)}, u32[]{:S(2)}) %collective-permute-start.4) | collective-permute-done | bytes 240032 | tf_op jit(solution)/shard_map/ppermute | solution.py:291
  15.7 0.0 collective-permute-done.1.refs_2_
  15.7 0.0 collective-permute-done.refs_1_
  15.7 1.8 %collective-permute-start.6 = (bf16[2,96,625]{2,1,0:T(8,128)(2,1)S(1)}, bf16[2,96,625]{2,1,0:T(8,128)(2,1)S(1)}, u32[]{:S(2)}, u32[]{:S(2)}) collective-permute-start(bf16[2,96,625]{2,1,0:T(8,128)(2,1)S(1)} %collective-permute-done.4.refs_0_), channel_id=1, source_target_pairs={{0,16},{8,24},{16,0},{24,8},{1,17},{9,25},{17,1},{25,9},{2,18},{10... | collective-permute-start | bytes 720008 | tf_op jit(solution)/shard_map/ppermute | solution.py:273
  17.4 1.5 %collective-permute-start.5 = (bf16[2,96,625]{2,1,0:T(8,128)(2,1)S(1)}, bf16[2,96,625]{2,1,0:T(8,128)(2,1)S(1)}, u32[]{:S(2)}, u32[]{:S(2)}) collective-permute-start(bf16[2,96,625]{2,1,0:T(8,128)(2,1)S(1)} %collective-permute-done.4.refs_0_), channel_id=1, source_target_pairs={{0,8},{8,0},{16,24},{24,16},{1,9},{9,1},{17,25},{25,17},{2,10},{10... | collective-permute-start | bytes 720008 | tf_op jit(solution)/shard_map/ppermute | solution.py:273
  18.9 0.9 collective-permute-start.14
  19.9 5.5 %collective-permute-done.9.refs_0_ = bf16[2,96,625]{2,1,0:T(8,128)(2,1)S(1)} collective-permute-done((bf16[2,96,625]{2,1,0:T(8,128)(2,1)S(1)}, bf16[2,96,625]{2,1,0:T(8,128)(2,1)S(1)}, u32[]{:S(2)}, u32[]{:S(2)}) %collective-permute-start.9) | collective-permute-done | bytes 240032 | tf_op jit(solution)/shard_map/ppermute | solution.py:291
  25.4 1.5 %collective-permute-start.11 = (bf16[2,96,625]{2,1,0:T(8,128)(2,1)S(1)}, bf16[2,96,625]{2,1,0:T(8,128)(2,1)S(1)}, u32[]{:S(2)}, u32[]{:S(2)}) collective-permute-start(bf16[2,96,625]{2,1,0:T(8,128)(2,1)S(1)} %collective-permute-done.9.refs_0_), channel_id=1, source_target_pairs={{0,16},{8,24},{16,0},{24,8},{1,17},{9,25},{17,1},{25,9},{2,18},{10... | collective-permute-start | bytes 720008 | tf_op jit(solution)/shard_map/ppermute | solution.py:273
  26.9 1.4 collective-permute-start.10
  28.4 0.6 collective-permute-start.2
  29.0 0.3 pad
  29.3 3.1 %collective-permute-done.14.refs_0_ = bf16[2,96,625]{2,1,0:T(8,128)(2,1)S(1)} collective-permute-done((bf16[2,96,625]{2,1,0:T(8,128)(2,1)S(1)}, bf16[2,96,625]{2,1,0:T(8,128)(2,1)S(1)}, u32[]{:S(2)}, u32[]{:S(2)}) %collective-permute-start.14) | collective-permute-done | bytes 240032 | tf_op jit(solution)/shard_map/ppermute | solution.py:291
  32.4 1.3 collective-permute-start.22
  33.7 0.6 collective-permute-start.7
  34.3 1.5 %collective-permute-done.10.refs_1_ = bf16[2,96,625]{2,1,0:T(8,128)(2,1)S(1)} collective-permute-done((bf16[2,96,625]{2,1,0:T(8,128)(2,1)S(1)}, bf16[2,96,625]{2,1,0:T(8,128)(2,1)S(1)}, u32[]{:S(2)}, u32[]{:S(2)}) %collective-permute-start.10) | collective-permute-done | bytes 240032 | tf_op jit(solution)/shard_map/ppermute | solution.py:273
  35.8 1.4 collective-permute-start.15
  37.2 9.2 %collective-permute-start.19 = (bf16[625,256]{1,0:T(8,128)(2,1)S(1)}, bf16[625,256]{1,0:T(8,128)(2,1)S(1)}, u32[]{:S(2)}, u32[]{:S(2)}) collective-permute-start(bf16[625,256]{1,0:T(8,128)(2,1)S(1)} %bitcast.25), channel_id=1, source_target_pairs={{0,2},{1,3},{2,4},{3,5},{4,6},{5,7},{8,10},{9,11},{10,12},{11,13},... | collective-permute-start | bytes 960008 | tf_op jit(solution)/shard_map/ppermute | solution.py:294
  46.5 0.1 collective-permute-start.12
  46.6 3.5 %shard_map.82.refs_0_ = bf16[2,1600,384]{2,1,0:T(8,128)(2,1)} custom-call(bf16[2,96,625]{2,1,0:T(8,128)(2,1)S(1)} %get-tuple-element.16.refs_0_, bf16[2,96,625]{2,1,0:T(8,128)(2,1)S(1)} %collective-permute-done.refs_1_, bf16[2,96,625]{2,1,0:T(8,128)(2,1)S(1)} %collective-permute-done.1.refs_2_, bf16[2,96,625]{2,1,0:T(8,128)(2,1)S(1)} %collective-permute-done.2.refs_3_, ...), custom_call_target="tpu_custom_call" | custom-call | flops 1536000000 | bytes 3417600 | tf_op jit(solution)/shard_map/pallas_call | solution.py:77
  50.1 0.0 collective-permute-done.22.refs_4_
  50.1 1.3 collective-permute-start.23
  51.4 0.0 collective-permute-done.7.refs_3_
  51.4 1.6 %collective-permute-start.16 = (bf16[2,96,625]{2,1,0:T(8,128)(2,1)S(1)}, bf16[2,96,625]{2,1,0:T(8,128)(2,1)S(1)}, u32[]{:S(2)}, u32[]{:S(2)}) collective-permute-start(bf16[2,96,625]{2,1,0:T(8,128)(2,1)S(1)} %collective-permute-done.14.refs_0_), channel_id=1, source_target_pairs={{0,16},{8,24},{16,0},{24,8},{1,17},{9,25},{17,1},{25,9},{2,18},{10... | collective-permute-start | bytes 720008 | tf_op jit(solution)/shard_map/ppermute | solution.py:273
  53.0 0.0 collective-permute-done.15.refs_1_
  53.0 0.5 collective-permute-start.17
  53.5 3.5 %shard_map.83.refs_2_ = bf16[2,1600,384]{2,1,0:T(8,128)(2,1)} custom-call(bf16[2,96,625]{2,1,0:T(8,128)(2,1)S(1)} %collective-permute-done.4.refs_0_, bf16[2,96,625]{2,1,0:T(8,128)(2,1)S(1)} %collective-permute-done.5.refs_1_, bf16[2,96,625]{2,1,0:T(8,128)(2,1)S(1)} %collective-permute-done.6.refs_2_, ...), custom_call_target="tpu_custom_call" | custom-call | flops 1536000000 | bytes 3417600 | tf_op jit(solution)/shard_map/pallas_call | solution.py:77
  56.9 0.0 collective-permute-done.19.refs_1_
  56.9 0.0 collective-permute-start.3
  56.9 0.0 collective-permute-done.12.refs_3_
  57.0 5.8 %collective-permute-start.20 = (bf16[625,256]{1,0:T(8,128)(2,1)S(1)}, bf16[625,256]{1,0:T(8,128)(2,1)S(1)}, u32[]{:S(2)}, u32[]{:S(2)}) collective-permute-start(bf16[625,256]{1,0:T(8,128)(2,1)S(1)} %collective-permute-done.19.refs_1_), channel_id=1, source_target_pairs={{0,2},{1,3},{2,4},{3,5},{4,6},{5,7},{8,10},{9,11},{10,12},{11,13},... | collective-permute-start | bytes 960008 | tf_op jit(solution)/shard_map/ppermute | solution.py:294
  62.7 3.5 %shard_map.84.refs_4_ = bf16[2,1600,384]{2,1,0:T(8,128)(2,1)} custom-call(bf16[2,96,625]{2,1,0:T(8,128)(2,1)S(1)} %collective-permute-done.9.refs_0_, bf16[2,96,625]{2,1,0:T(8,128)(2,1)S(1)} %collective-permute-done.10.refs_1_, bf16[2,96,625]{2,1,0:T(8,128)(2,1)S(1)} %collective-permute-done.11.refs_2_, ...), custom_call_target="tpu_custom_call" | custom-call | flops 1536000000 | bytes 3417600 | tf_op jit(solution)/shard_map/pallas_call | solution.py:77
  66.2 0.0 collective-permute-done.16.refs_2_
  66.2 0.2 collective-permute-start.8
  66.4 0.3 collective-permute-start.13
  66.7 3.5 %shard_map.85.refs_6_ = bf16[2,1600,384]{2,1,0:T(8,128)(2,1)} custom-call(bf16[2,96,625]{2,1,0:T(8,128)(2,1)S(1)} %collective-permute-done.14.refs_0_, bf16[2,96,625]{2,1,0:T(8,128)(2,1)S(1)} %collective-permute-done.15.refs_1_, bf16[2,96,625]{2,1,0:T(8,128)(2,1)S(1)} %collective-permute-done.16.refs_2_, ...), custom_call_target="tpu_custom_call" | custom-call | flops 1536000000 | bytes 3417600 | tf_op jit(solution)/shard_map/pallas_call | solution.py:77
  70.2 0.3 collective-permute-start.18
  70.5 0.0 collective-permute-done.20.refs_2_
  70.5 1.3 collective-permute-start.24
  71.7 10.7 %collective-permute-done.24.refs_6_ = bf16[625,256]{1,0:T(8,128)(2,1)S(1)} collective-permute-done((bf16[625,256]{1,0:T(8,128)(2,1)S(1)}, bf16[625,256]{1,0:T(8,128)(2,1)S(1)}, u32[]{:S(2)}, u32[]{:S(2)}) %collective-permute-start.24) | collective-permute-done | bytes 320032 | tf_op jit(solution)/shard_map/ppermute | solution.py:294
  82.4 3.6 %collective-permute-start.21 = (bf16[625,256]{1,0:T(8,128)(2,1)S(1)}, bf16[625,256]{1,0:T(8,128)(2,1)S(1)}, u32[]{:S(2)}, u32[]{:S(2)}) collective-permute-start(bf16[625,256]{1,0:T(8,128)(2,1)S(1)} %collective-permute-done.20.refs_2_), channel_id=1, source_target_pairs={{0,2},{1,3},{2,4},{3,5},{4,6},{5,7},{8,10},{9,11},{10,12},{11,13},... | collective-permute-start | bytes 960008 | tf_op jit(solution)/shard_map/ppermute | solution.py:294
  86.1 6.2 %collective-permute-done.21.refs_3_ = bf16[625,256]{1,0:T(8,128)(2,1)S(1)} collective-permute-done((bf16[625,256]{1,0:T(8,128)(2,1)S(1)}, bf16[625,256]{1,0:T(8,128)(2,1)S(1)}, u32[]{:S(2)}, u32[]{:S(2)}) %collective-permute-start.21) | collective-permute-done | bytes 320032 | tf_op jit(solution)/shard_map/ppermute | solution.py:294
  92.3 1.5 shard_map.86.refs_8_
  93.8 0.1 collective-permute-start.25
  93.9 0.1 copy.24.owners_ref
  93.9 0.1 copy.25.local_ref
  94.0 3.3 %collective-permute-done.25.refs_9_ = bf16[8,800,128]{2,1,0:T(8,128)(2,1)S(1)} collective-permute-done((bf16[8,800,128]{2,1,0:T(8,128)(2,1)S(1)}, bf16[8,800,128]{2,1,0:T(8,128)(2,1)S(1)}, u32[]{:S(2)}, u32[]{:S(2)}) %collective-permute-start.25) | collective-permute-done | bytes 1638432 | tf_op jit(solution)/shard_map/ppermute | solution.py:288
  97.4 0.0 copy-start
  97.4 1.2 copy-done
  98.6 10.6 %shard_map.88 = bf16[1,2,625,128]{3,2,1,0:T(8,128)(2,1)S(1)} custom-call(s32[1]{0:T(128)} %bitcast.column_ref, s32[32,3]{1,0:T(8,128)S(1)} %copy.24.owners_ref, s32[32,4]{1,0:T(8,128)S(1)} %copy.25.local_ref, bf16[2,1600,384]{2,1,0:T(8,128)(2,1)} %shard_map.82.refs_0_, bf16[2,1600,384]{2,1,0:T(8,128)(2,1)} %collective-permute-done.3.refs_1_, ...), custom_call_target="tpu_custom_call" | custom-call | flops 2936012800 | bytes 6553600 | tf_op jit(solution)/shard_map/pallas_call | solution.py:253
  109.2 3.2 %collective-permute-start.27 = (bf16[2,625,128]{2,1,0:T(8,128)(2,1)S(1)}, bf16[2,625,128]{2,1,0:T(8,128)(2,1)S(1)}, u32[]{:S(2)}, u32[]{:S(2)}) collective-permute-start(bf16[2,625,128]{2,1,0:T(8,128)(2,1)S(1)} %bitcast.27), channel_id=1, source_target_pairs={{0,6},{1,7},{2,0},{3,1},{4,2},{5,3},{6,4},{7,5},{8,14},{9,15},{10,... | collective-permute-start | bytes 960008 | tf_op jit(solution)/shard_map/ppermute | solution.py:291
  112.4 10.6 %shard_map.87 = bf16[1,2,625,128]{3,2,1,0:T(8,128)(2,1)S(1)} custom-call(s32[1]{0:T(128)} %bitcast.column_ref, s32[32,3]{1,0:T(8,128)S(1)} %copy.24.owners_ref, s32[32,4]{1,0:T(8,128)S(1)} %copy.25.local_ref, bf16[2,1600,384]{2,1,0:T(8,128)(2,1)} %shard_map.82.refs_0_, bf16[2,1600,384]{2,1,0:T(8,128)(2,1)} %collective-permute-done.3.refs_1_, ...), custom_call_target="tpu_custom_call" | custom-call | flops 2936012800 | bytes 6553600 | tf_op jit(solution)/shard_map/pallas_call | solution.py:253
  123.0 1.0 collective-permute-start.26
  124.0 10.6 %shard_map.89 = bf16[1,2,625,128]{3,2,1,0:T(8,128)(2,1)S(1)} custom-call(s32[1]{0:T(128)} %bitcast.column_ref, s32[32,3]{1,0:T(8,128)S(1)} %copy.24.owners_ref, s32[32,4]{1,0:T(8,128)S(1)} %copy.25.local_ref, bf16[2,1600,384]{2,1,0:T(8,128)(2,1)} %shard_map.82.refs_0_, bf16[2,1600,384]{2,1,0:T(8,128)(2,1)} %collective-permute-done.3.refs_1_, ...), custom_call_target="tpu_custom_call" | custom-call | flops 2936012800 | bytes 6553600 | tf_op jit(solution)/shard_map/pallas_call | solution.py:253
  134.6 0.0 copy-start.3
  134.7 1.4 collective-permute-start.28
  136.0 10.6 %shard_map.90 = bf16[1,2,625,128]{3,2,1,0:T(8,128)(2,1)S(1)} custom-call(s32[1]{0:T(128)} %bitcast.column_ref, s32[32,3]{1,0:T(8,128)S(1)} %copy.24.owners_ref, s32[32,4]{1,0:T(8,128)S(1)} %copy.25.local_ref, bf16[2,1600,384]{2,1,0:T(8,128)(2,1)} %shard_map.82.refs_0_, bf16[2,1600,384]{2,1,0:T(8,128)(2,1)} %collective-permute-done.3.refs_1_, ...), custom_call_target="tpu_custom_call" | custom-call | flops 2936012800 | bytes 6553600 | tf_op jit(solution)/shard_map/pallas_call | solution.py:253
  146.7 0.2 fusion.1
  146.9 1.2 copy.33
  (25 shorter events, 0.1 us)
Async XLA Ops:
  0.0 29.0 %copy-start.4 = (bf16[2,128,625]{1,0,2:T(2,128)(2,1)S(1)}, bf16[2,128,625]{1,0,2:T(2,128)(2,1)}, u32[]{:S(2)}) copy-start(bf16[2,128,625]{1,0,2:T(2,128)(2,1)} %param.9) | copy-start | bytes 960004
  0.0 46.6 %copy-start.2 = (bf16[1600,625]{1,0:T(8,128)(2,1)S(1)}, bf16[1600,625]{1,0:T(8,128)(2,1)}, u32[]{:S(2)}) copy-start(bf16[1600,625]{1,0:T(8,128)(2,1)} %constant.61.clone.refs_4_) | copy-start | bytes 6000004
  3.7 12.0 %collective-permute-start.4 = (bf16[2,96,625]{2,1,0:T(8,128)(2,1)S(1)}, bf16[2,96,625]{2,1,0:T(8,128)(2,1)S(1)}, u32[]{:S(2)}, u32[]{:S(2)}) collective-permute-start(bf16[2,96,625]{2,1,0:T(8,128)(2,1)S(1)} %get-tuple-element.15), channel_id=1, source_target_pairs={{0,2},{1,3},{2,4},{3,5},{4,6},{5,7},{6,0},{7,1},{8,10},{9,11},{10,... | collective-permute-start | bytes 720008 | tf_op jit(solution)/shard_map/ppermute | solution.py:291
  6.7 8.9 %collective-permute-start.1 = (bf16[2,96,625]{2,1,0:T(8,128)(2,1)S(1)}, bf16[2,96,625]{2,1,0:T(8,128)(2,1)S(1)}, u32[]{:S(2)}, u32[]{:S(2)}) collective-permute-start(bf16[2,96,625]{2,1,0:T(8,128)(2,1)S(1)} %get-tuple-element.16.refs_0_), channel_id=1, source_target_pairs={{0,16},{8,24},{16,0},{24,8},{1,17},{9,25},{17,1},{25,9},{2,18},{10... | collective-permute-start | bytes 720008 | tf_op jit(solution)/shard_map/ppermute | solution.py:273
  8.3 7.4 %collective-permute-start = (bf16[2,96,625]{2,1,0:T(8,128)(2,1)S(1)}, bf16[2,96,625]{2,1,0:T(8,128)(2,1)S(1)}, u32[]{:S(2)}, u32[]{:S(2)}) collective-permute-start(bf16[2,96,625]{2,1,0:T(8,128)(2,1)S(1)} %get-tuple-element.16.refs_0_), channel_id=1, source_target_pairs={{0,8},{8,0},{16,24},{24,16},{1,9},{9,1},{17,25},{25,17},{2,10},{10... | collective-permute-start | bytes 720008 | tf_op jit(solution)/shard_map/ppermute | solution.py:273
  9.8 15.6 %collective-permute-start.9 = (bf16[2,96,625]{2,1,0:T(8,128)(2,1)S(1)}, bf16[2,96,625]{2,1,0:T(8,128)(2,1)S(1)}, u32[]{:S(2)}, u32[]{:S(2)}) collective-permute-start(bf16[2,96,625]{2,1,0:T(8,128)(2,1)S(1)} %get-tuple-element.14), channel_id=1, source_target_pairs={{0,4},{1,5},{2,6},{3,7},{4,0},{5,1},{6,2},{7,3},{8,12},{9,13},{10,... | collective-permute-start | bytes 720008 | tf_op jit(solution)/shard_map/ppermute | solution.py:291
  15.7 9.7 %collective-permute-start.6 = (bf16[2,96,625]{2,1,0:T(8,128)(2,1)S(1)}, bf16[2,96,625]{2,1,0:T(8,128)(2,1)S(1)}, u32[]{:S(2)}, u32[]{:S(2)}) collective-permute-start(bf16[2,96,625]{2,1,0:T(8,128)(2,1)S(1)} %collective-permute-done.4.refs_0_), channel_id=1, source_target_pairs={{0,16},{8,24},{16,0},{24,8},{1,17},{9,25},{17,1},{25,9},{2,18},{10... | collective-permute-start | bytes 720008 | tf_op jit(solution)/shard_map/ppermute | solution.py:273
  17.4 8.0 %collective-permute-start.5 = (bf16[2,96,625]{2,1,0:T(8,128)(2,1)S(1)}, bf16[2,96,625]{2,1,0:T(8,128)(2,1)S(1)}, u32[]{:S(2)}, u32[]{:S(2)}) collective-permute-start(bf16[2,96,625]{2,1,0:T(8,128)(2,1)S(1)} %collective-permute-done.4.refs_0_), channel_id=1, source_target_pairs={{0,8},{8,0},{16,24},{24,16},{1,9},{9,1},{17,25},{25,17},{2,10},{10... | collective-permute-start | bytes 720008 | tf_op jit(solution)/shard_map/ppermute | solution.py:273
  18.9 13.5 %collective-permute-start.14 = (bf16[2,96,625]{2,1,0:T(8,128)(2,1)S(1)}, bf16[2,96,625]{2,1,0:T(8,128)(2,1)S(1)}, u32[]{:S(2)}, u32[]{:S(2)}) collective-permute-start(bf16[2,96,625]{2,1,0:T(8,128)(2,1)S(1)} %get-tuple-element.13), channel_id=1, source_target_pairs={{0,6},{1,7},{2,0},{3,1},{4,2},{5,3},{6,4},{7,5},{8,14},{9,15},{10,... | collective-permute-start | bytes 720008 | tf_op jit(solution)/shard_map/ppermute | solution.py:291
  25.4 8.9 %collective-permute-start.11 = (bf16[2,96,625]{2,1,0:T(8,128)(2,1)S(1)}, bf16[2,96,625]{2,1,0:T(8,128)(2,1)S(1)}, u32[]{:S(2)}, u32[]{:S(2)}) collective-permute-start(bf16[2,96,625]{2,1,0:T(8,128)(2,1)S(1)} %collective-permute-done.9.refs_0_), channel_id=1, source_target_pairs={{0,16},{8,24},{16,0},{24,8},{1,17},{9,25},{17,1},{25,9},{2,18},{10... | collective-permute-start | bytes 720008 | tf_op jit(solution)/shard_map/ppermute | solution.py:273
  26.9 8.9 %collective-permute-start.10 = (bf16[2,96,625]{2,1,0:T(8,128)(2,1)S(1)}, bf16[2,96,625]{2,1,0:T(8,128)(2,1)S(1)}, u32[]{:S(2)}, u32[]{:S(2)}) collective-permute-start(bf16[2,96,625]{2,1,0:T(8,128)(2,1)S(1)} %collective-permute-done.9.refs_0_), channel_id=1, source_target_pairs={{0,8},{8,0},{16,24},{24,16},{1,9},{9,1},{17,25},{25,17},{2,10},{10... | collective-permute-start | bytes 720008 | tf_op jit(solution)/shard_map/ppermute | solution.py:273
  28.4 18.1 %collective-permute-start.2 = (bf16[2,96,625]{2,1,0:T(8,128)(2,1)S(1)}, bf16[2,96,625]{2,1,0:T(8,128)(2,1)S(1)}, u32[]{:S(2)}, u32[]{:S(2)}) collective-permute-start(bf16[2,96,625]{2,1,0:T(8,128)(2,1)S(1)} %collective-permute-done.1.refs_2_), channel_id=1, source_target_pairs={{0,8},{8,0},{16,24},{24,16},{1,9},{9,1},{17,25},{25,17},{2,10},{10... | collective-permute-start | bytes 720008 | tf_op jit(solution)/shard_map/ppermute | solution.py:273
  32.4 17.7 %collective-permute-start.22 = (bf16[625,256]{1,0:T(8,128)(2,1)S(1)}, bf16[625,256]{1,0:T(8,128)(2,1)S(1)}, u32[]{:S(2)}, u32[]{:S(2)}) collective-permute-start(bf16[625,256]{1,0:T(8,128)(2,1)S(1)} %bitcast.24), channel_id=1, source_target_pairs={{2,0},{3,1},{4,2},{5,3},{6,4},{7,5},{10,8},{11,9},{12,10},{13,11},... | collective-permute-start | bytes 960008 | tf_op jit(solution)/shard_map/ppermute | solution.py:294
  33.7 17.7 %collective-permute-start.7 = (bf16[2,96,625]{2,1,0:T(8,128)(2,1)S(1)}, bf16[2,96,625]{2,1,0:T(8,128)(2,1)S(1)}, u32[]{:S(2)}, u32[]{:S(2)}) collective-permute-start(bf16[2,96,625]{2,1,0:T(8,128)(2,1)S(1)} %collective-permute-done.5.refs_1_), channel_id=1, source_target_pairs={{0,16},{8,24},{16,0},{24,8},{1,17},{9,25},{17,1},{25,9},{2,18},{10... | collective-permute-start | bytes 720008 | tf_op jit(solution)/shard_map/ppermute | solution.py:273
  35.8 17.2 %collective-permute-start.15 = (bf16[2,96,625]{2,1,0:T(8,128)(2,1)S(1)}, bf16[2,96,625]{2,1,0:T(8,128)(2,1)S(1)}, u32[]{:S(2)}, u32[]{:S(2)}) collective-permute-start(bf16[2,96,625]{2,1,0:T(8,128)(2,1)S(1)} %collective-permute-done.14.refs_0_), channel_id=1, source_target_pairs={{0,8},{8,0},{16,24},{24,16},{1,9},{9,1},{17,25},{25,17},{2,10},{10... | collective-permute-start | bytes 720008 | tf_op jit(solution)/shard_map/ppermute | solution.py:273
  37.2 19.7 %collective-permute-start.19 = (bf16[625,256]{1,0:T(8,128)(2,1)S(1)}, bf16[625,256]{1,0:T(8,128)(2,1)S(1)}, u32[]{:S(2)}, u32[]{:S(2)}) collective-permute-start(bf16[625,256]{1,0:T(8,128)(2,1)S(1)} %bitcast.25), channel_id=1, source_target_pairs={{0,2},{1,3},{2,4},{3,5},{4,6},{5,7},{8,10},{9,11},{10,12},{11,13},... | collective-permute-start | bytes 960008 | tf_op jit(solution)/shard_map/ppermute | solution.py:294
  46.5 10.5 %collective-permute-start.12 = (bf16[2,96,625]{2,1,0:T(8,128)(2,1)S(1)}, bf16[2,96,625]{2,1,0:T(8,128)(2,1)S(1)}, u32[]{:S(2)}, u32[]{:S(2)}) collective-permute-start(bf16[2,96,625]{2,1,0:T(8,128)(2,1)S(1)} %collective-permute-done.11.refs_2_), channel_id=1, source_target_pairs={{0,8},{8,0},{16,24},{24,16},{1,9},{9,1},{17,25},{25,17},{2,10},{10... | collective-permute-start | bytes 720008 | tf_op jit(solution)/shard_map/ppermute | solution.py:273
  50.1 20.1 %collective-permute-start.23 = (bf16[625,256]{1,0:T(8,128)(2,1)S(1)}, bf16[625,256]{1,0:T(8,128)(2,1)S(1)}, u32[]{:S(2)}, u32[]{:S(2)}) collective-permute-start(bf16[625,256]{1,0:T(8,128)(2,1)S(1)} %collective-permute-done.22.refs_4_), channel_id=1, source_target_pairs={{2,0},{3,1},{4,2},{5,3},{6,4},{7,5},{10,8},{11,9},{12,10},{13,11},... | collective-permute-start | bytes 960008 | tf_op jit(solution)/shard_map/ppermute | solution.py:294
  51.4 14.8 %collective-permute-start.16 = (bf16[2,96,625]{2,1,0:T(8,128)(2,1)S(1)}, bf16[2,96,625]{2,1,0:T(8,128)(2,1)S(1)}, u32[]{:S(2)}, u32[]{:S(2)}) collective-permute-start(bf16[2,96,625]{2,1,0:T(8,128)(2,1)S(1)} %collective-permute-done.14.refs_0_), channel_id=1, source_target_pairs={{0,16},{8,24},{16,0},{24,8},{1,17},{9,25},{17,1},{25,9},{2,18},{10... | collective-permute-start | bytes 720008 | tf_op jit(solution)/shard_map/ppermute | solution.py:273
  53.0 13.4 %collective-permute-start.17 = (bf16[2,96,625]{2,1,0:T(8,128)(2,1)S(1)}, bf16[2,96,625]{2,1,0:T(8,128)(2,1)S(1)}, u32[]{:S(2)}, u32[]{:S(2)}) collective-permute-start(bf16[2,96,625]{2,1,0:T(8,128)(2,1)S(1)} %collective-permute-done.15.refs_1_), channel_id=1, source_target_pairs={{0,16},{8,24},{16,0},{24,8},{1,17},{9,25},{17,1},{25,9},{2,18},{10... | collective-permute-start | bytes 720008 | tf_op jit(solution)/shard_map/ppermute | solution.py:273
  56.9 40.4 %collective-permute-start.3 = (bf16[2,1600,384]{2,1,0:T(8,128)(2,1)}, bf16[2,1600,384]{2,1,0:T(8,128)(2,1)}, u32[]{:S(2)}, u32[]{:S(2)}) collective-permute-start(bf16[2,1600,384]{2,1,0:T(8,128)(2,1)} %shard_map.82.refs_0_), channel_id=1, source_target_pairs={{0,1},{1,0},{2,3},{3,2},{4,5},{5,4},{6,7},{7,6},{8,9},{9,8},{10,11... | collective-permute-start | bytes 7372808 | tf_op jit(solution)/shard_map/ppermute | solution.py:288
  57.0 13.5 %collective-permute-start.20 = (bf16[625,256]{1,0:T(8,128)(2,1)S(1)}, bf16[625,256]{1,0:T(8,128)(2,1)S(1)}, u32[]{:S(2)}, u32[]{:S(2)}) collective-permute-start(bf16[625,256]{1,0:T(8,128)(2,1)S(1)} %collective-permute-done.19.refs_1_), channel_id=1, source_target_pairs={{0,2},{1,3},{2,4},{3,5},{4,6},{5,7},{8,10},{9,11},{10,12},{11,13},... | collective-permute-start | bytes 960008 | tf_op jit(solution)/shard_map/ppermute | solution.py:294
  66.2 26.1 %copy-start.1 = (bf16[800,625]{1,0:T(8,128)(2,1)S(1)}, bf16[800,625]{1,0:T(8,128)(2,1)}, u32[]{:S(2)}) copy-start(bf16[800,625]{1,0:T(8,128)(2,1)} %constant.63.clone.matrix_ref) | copy-start | bytes 3000004
  66.2 31.1 %collective-permute-start.8 = (bf16[2,1600,384]{2,1,0:T(8,128)(2,1)}, bf16[2,1600,384]{2,1,0:T(8,128)(2,1)}, u32[]{:S(2)}, u32[]{:S(2)}) collective-permute-start(bf16[2,1600,384]{2,1,0:T(8,128)(2,1)} %shard_map.83.refs_2_), channel_id=1, source_target_pairs={{0,1},{1,0},{2,3},{3,2},{4,5},{5,4},{6,7},{7,6},{8,9},{9,8},{10,11... | collective-permute-start | bytes 7372808 | tf_op jit(solution)/shard_map/ppermute | solution.py:288
  66.4 30.9 %collective-permute-start.13 = (bf16[2,1600,384]{2,1,0:T(8,128)(2,1)}, bf16[2,1600,384]{2,1,0:T(8,128)(2,1)}, u32[]{:S(2)}, u32[]{:S(2)}) collective-permute-start(bf16[2,1600,384]{2,1,0:T(8,128)(2,1)} %shard_map.84.refs_4_), channel_id=1, source_target_pairs={{0,1},{1,0},{2,3},{3,2},{4,5},{5,4},{6,7},{7,6},{8,9},{9,8},{10,11... | collective-permute-start | bytes 7372808 | tf_op jit(solution)/shard_map/ppermute | solution.py:288
  70.2 23.7 %copy-start.5 = (s32[32,3]{0,1:T(4,128)S(1)}, s32[32,3]{0,1:T(4,128)}, u32[]{:S(2)}) copy-start(s32[32,3]{0,1:T(4,128)} %param.11) | copy-start | bytes 1156
  70.2 23.8 %copy-start.6 = (s32[32,4]{0,1:T(4,128)S(1)}, s32[32,4]{0,1:T(4,128)}, u32[]{:S(2)}) copy-start(s32[32,4]{0,1:T(4,128)} %param.12) | copy-start | bytes 1540
  70.2 27.2 %collective-permute-start.18 = (bf16[2,1600,384]{2,1,0:T(8,128)(2,1)}, bf16[2,1600,384]{2,1,0:T(8,128)(2,1)}, u32[]{:S(2)}, u32[]{:S(2)}) collective-permute-start(bf16[2,1600,384]{2,1,0:T(8,128)(2,1)} %shard_map.85.refs_6_), channel_id=1, source_target_pairs={{0,1},{1,0},{2,3},{3,2},{4,5},{5,4},{6,7},{7,6},{8,9},{9,8},{10,11... | collective-permute-start | bytes 7372808 | tf_op jit(solution)/shard_map/ppermute | solution.py:288
  70.5 12.0 %collective-permute-start.24 = (bf16[625,256]{1,0:T(8,128)(2,1)S(1)}, bf16[625,256]{1,0:T(8,128)(2,1)S(1)}, u32[]{:S(2)}, u32[]{:S(2)}) collective-permute-start(bf16[625,256]{1,0:T(8,128)(2,1)S(1)} %collective-permute-done.23.refs_5_), channel_id=1, source_target_pairs={{2,0},{3,1},{4,2},{5,3},{6,4},{7,5},{10,8},{11,9},{12,10},{13,11},... | collective-permute-start | bytes 960008 | tf_op jit(solution)/shard_map/ppermute | solution.py:294
  82.4 9.9 %collective-permute-start.21 = (bf16[625,256]{1,0:T(8,128)(2,1)S(1)}, bf16[625,256]{1,0:T(8,128)(2,1)S(1)}, u32[]{:S(2)}, u32[]{:S(2)}) collective-permute-start(bf16[625,256]{1,0:T(8,128)(2,1)S(1)} %collective-permute-done.20.refs_2_), channel_id=1, source_target_pairs={{0,2},{1,3},{2,4},{3,5},{4,6},{5,7},{8,10},{9,11},{10,12},{11,13},... | collective-permute-start | bytes 960008 | tf_op jit(solution)/shard_map/ppermute | solution.py:294
  93.8 3.6 %collective-permute-start.25 = (bf16[8,800,128]{2,1,0:T(8,128)(2,1)S(1)}, bf16[8,800,128]{2,1,0:T(8,128)(2,1)S(1)}, u32[]{:S(2)}, u32[]{:S(2)}) collective-permute-start(bf16[8,800,128]{2,1,0:T(8,128)(2,1)S(1)} %shard_map.86.refs_8_), channel_id=1, source_target_pairs={{0,1},{1,0},{2,3},{3,2},{4,5},{5,4},{6,7},{7,6},{8,9},{9,8},{10,11... | collective-permute-start | bytes 4915208 | tf_op jit(solution)/shard_map/ppermute | solution.py:288
  97.4 1.3 copy-start
  109.2 37.4 %collective-permute-start.27 = (bf16[2,625,128]{2,1,0:T(8,128)(2,1)S(1)}, bf16[2,625,128]{2,1,0:T(8,128)(2,1)S(1)}, u32[]{:S(2)}, u32[]{:S(2)}) collective-permute-start(bf16[2,625,128]{2,1,0:T(8,128)(2,1)S(1)} %bitcast.27), channel_id=1, source_target_pairs={{0,6},{1,7},{2,0},{3,1},{4,2},{5,3},{6,4},{7,5},{8,14},{9,15},{10,... | collective-permute-start | bytes 960008 | tf_op jit(solution)/shard_map/ppermute | solution.py:291
  123.0 23.6 %collective-permute-start.26 = (bf16[2,625,128]{2,1,0:T(8,128)(2,1)S(1)}, bf16[2,625,128]{2,1,0:T(8,128)(2,1)S(1)}, u32[]{:S(2)}, u32[]{:S(2)}) collective-permute-start(bf16[2,625,128]{2,1,0:T(8,128)(2,1)S(1)} %bitcast.28), channel_id=1, source_target_pairs={{0,4},{1,5},{2,6},{3,7},{4,0},{5,1},{6,2},{7,3},{8,12},{9,13},{10,... | collective-permute-start | bytes 960008 | tf_op jit(solution)/shard_map/ppermute | solution.py:291
  134.6 12.0 %copy-start.3 = (f32[2,128,625]{1,0,2:T(2,128)S(1)}, f32[2,128,625]{1,0,2:T(2,128)}, u32[]{:S(2)}) copy-start(f32[2,128,625]{1,0,2:T(2,128)} %param.10) | copy-start | bytes 1920004
  134.7 12.0 %collective-permute-start.28 = (bf16[2,625,128]{2,1,0:T(8,128)(2,1)S(1)}, bf16[2,625,128]{2,1,0:T(8,128)(2,1)S(1)}, u32[]{:S(2)}, u32[]{:S(2)}) collective-permute-start(bf16[2,625,128]{2,1,0:T(8,128)(2,1)S(1)} %bitcast.29), channel_id=1, source_target_pairs={{0,2},{1,3},{2,4},{3,5},{4,6},{5,7},{6,0},{7,1},{8,10},{9,11},{10,... | collective-permute-start | bytes 960008 | tf_op jit(solution)/shard_map/ppermute | solution.py:291

commit v5 on v4

--- a/solution.py
+++ b/solution.py
@@ -90,30 +90,26 @@
     )(*parts, matrix)
 
 
-def amp_kernel(levels, matrix_ref, *refs):
+def amp_kernel(matrix_ref, *refs):
     tile_refs, out_ref = refs[:-1], refs[-1]
-    blocks_here = out_ref.shape[0] // levels
-    pairs = out_ref.shape[2]
-    for by in range(levels):
-        tiles = tile_refs[0][...] if by == 0 else tile_refs[by][...] + tile_refs[2 * levels - 1 - by][...]
-        made = jnp.dot(matrix_ref[...], tiles, preferred_element_type=F32).astype(BF)
+    blocks_here, pairs = out_ref.shape[0] // len(tile_refs), out_ref.shape[2]
+    for by, ref in enumerate(tile_refs):
+        made = jnp.dot(matrix_ref[...], ref[...], preferred_element_type=F32).astype(BF)
         for m in range(blocks_here):
             out_ref[by * blocks_here + m] = made[:, m * pairs : (m + 1) * pairs]
 
 
-def prepare_amps(own, ups, downs, blocks_here, matrix):
-    levels = len(ups) + 1
-    pairs = own.shape[1] // blocks_here
+def prepare_amps(parts, blocks_here, matrix):
+    levels, size = len(parts), parts[0].size
+    pairs = parts[0].shape[1] // blocks_here
     return pl.pallas_call(
-        functools.partial(amp_kernel, levels),
+        amp_kernel,
         out_shape=jax.ShapeDtypeStruct((levels * blocks_here, ROWS, pairs), BF),
         compiler_params=pltpu.CompilerParams(vmem_limit_bytes=VMEM_BYTES),
         cost_estimate=pl.CostEstimate(
-            flops=2 * levels * own.size * ROWS,
-            bytes_accessed=4 * levels * own.size,
-            transcendentals=0,
+            flops=2 * levels * size * ROWS, bytes_accessed=4 * levels * size, transcendentals=0
         ),
-    )(matrix, own, *ups, *downs)
+    )(matrix, *parts)
 
 
 def turned(ref, groups, by):
@@ -205,8 +201,11 @@
 
     @pl.when(step == steps - 1)
     def _():
-        for m in range(acc_ref.shape[0]):
-            out_ref[0, m] = jnp.dot(back_ref[...], acc_ref[m].astype(BF), preferred_element_type=F32).astype(BF)
+        blocks_here, pairs = out_ref.shape[1], out_ref.shape[3]
+        sums = jnp.concatenate([acc_ref[m].astype(BF) for m in range(blocks_here)], axis=1)
+        sums = jnp.dot(back_ref[...], sums, preferred_element_type=F32).astype(BF)
+        for m in range(blocks_here):
+            out_ref[0, m] = sums[:, m * pairs : (m + 1) * pairs]
 
 
 def ladders(first, columns, levels, blocks_here, column, task_owners, task_local, tiles, amps, back, matrix):
@@ -290,20 +289,14 @@
     def around(x, by):
         return lax.ppermute(x, "task", [(c, (c + 2 * by) % task_count) for c in range(task_count)])
 
-    def hop(x, by):
-        return lax.ppermute(x, "task", [(c, c + by) for c in range(task_count) if 0 <= c + by < task_count])
-
     slices = factor_blocks.reshape(blocks_here, levels, depth, -1)
     mine = [lax.dynamic_index_in_dim(slices, (level + by) % levels, 1, keepdims=False) for by in range(levels)]
     parts = [mine[0]] + [around(mine[by], by) for by in range(1, levels)]
     if pair_count == 4:
         own = amplitudes.transpose(2, 0, 1).reshape(TV * TV, blocks_here * pairs)
         (own,), _ = lax.optimization_barrier(((own,), parts[1:]))
-        ups, downs = [hop(own, 2)], [hop(own, -2)]
-        for by in range(2, levels):
-            ups.append(hop(ups[-1], 2))
-            downs.append(hop(downs[-1], -2))
-        amps = prepare_amps(own, ups, downs, blocks_here, jnp.asarray(amp_matrix()))
+        amps = [own] + [around(own, by) for by in range(1, levels)]
+        amps = prepare_amps(amps, blocks_here, jnp.asarray(amp_matrix()))
         held, flying = [], ()
         for by, part in enumerate(parts):
             part, flying = lax.optimization_barrier((part, flying))

time: 148 us -> 150 us (1.014)
  waiting for transfers between devices: 33.7 us -> 51 us
  starting transfers between devices: 49.6 us -> 35.5 us
    ppermute x6 -> x9, waiting for transfers between devices: 12 us -> 40.1 us  [around(): lax.ppermute(x, 'task', [(c, (c + 2 * by) % task_count) for c in range(ta...]
    ppermute x6 -> x0, starting transfers between devices: 22.5 us -> none  [hop(): lax.ppermute(x, 'task', [(c, c + by) for c in range(task_count) if 0 <= c...]
    ppermute x6 -> x0, waiting for transfers between devices: 16.9 us -> none  [hop(): lax.ppermute(x, 'task', [(c, c + by) for c in range(task_count) if 0 <= c...]
    ppermute x6 -> x9, starting transfers between devices: 12.2 us -> 20.6 us  [around(): lax.ppermute(x, 'task', [(c, (c + 2 * by) % task_count) for c in range(ta...]
    ppermute x12, waiting for transfers between devices: 1.56 us -> 7.6 us  [beside(): return lax.ppermute(x, 'pair', [(p, p ^ bit) for p in range(pair_count)])]
  transfers between devices with their start and end apart: 29 -> 26, of which waited for: 7 -> 10; matrix products, arithmetic and copies ran while one was open for 0% -> 0% of each run, Pallas kernels for 32% -> 31%
where the time goes in v5:
time: 150 us
  Pallas kernels  56.6 us (38%)
  waiting for transfers between devices  51 us (34%)
  starting transfers between devices  35.5 us (24%)
  local copies, waits for them, and re-layouts  6.54 us (4%)
    pallas_call x4, Pallas kernels, ladders(): pl.pallas_call(functools.partial(ladder_kernel, find, made, len(tiles)),...  41.4 us
    ppermute x9, waiting for transfers between devices, around(): lax.ppermute(x, 'task', [(c, (c + 2 * by) % task_count) for c in range(ta...  40.1 us
    ppermute x9, starting transfers between devices, around(): lax.ppermute(x, 'task', [(c, (c + 2 * by) % task_count) for c in range(ta...  20.6 us
    ppermute x12, starting transfers between devices, beside(): return lax.ppermute(x, 'pair', [(p, p ^ bit) for p in range(pair_count)])  14.3 us
    pallas_call x4, Pallas kernels, prepare(): pl.pallas_call(functools.partial(prepare_kernel, len(parts)), out_shape=j...  13.8 us
    ppermute x12, waiting for transfers between devices, beside(): return lax.ppermute(x, 'pair', [(p, p ^ bit) for p in range(pair_count)])  7.6 us
    unnamed x19, local copies, waits for them, and re-layouts  5.23 us
    ppermute x5, waiting for transfers between devices, per_device(): lax.ppermute(x, 'task', [(c, c ^ 1) for c in range(task_count)])  3.31 us
  transfers between devices with their start and end apart: 26, of which 10 were waited for; matrix products, arithmetic and copies ran while one was open for 0% of the time, Pallas kernels for 31%

profile of v5, /device:TPU:0, one launch (start us, length us, event | category | flops | bytes accessed | tf_op | source)
XLA Modules:
  0.0 150.1 jit_solution(16649954143709103284)
XLA Ops:
  0.0 3.5 %copy.23 = bf16[2,384,625]{2,1,0:T(8,128)(2,1)S(1)} copy(bf16[2,384,625]{1,0,2:T(2,128)(2,1)} %param.8) | data formatting | bytes 1920000 | tf_op args[0]
  3.5 0.1 dynamic-slice_bitcast_fusion
  3.7 3.1 %collective-permute-start.4 = (bf16[2,96,625]{2,1,0:T(8,128)(2,1)S(1)}, bf16[2,96,625]{2,1,0:T(8,128)(2,1)S(1)}, u32[]{:S(2)}, u32[]{:S(2)}) collective-permute-start(bf16[2,96,625]{2,1,0:T(8,128)(2,1)S(1)} %get-tuple-element.15), channel_id=1, source_target_pairs={{0,2},{1,3},{2,4},{3,5},{4,6},{5,7},{6,0},{7,1},{8,10},{9,11},{10,... | collective-permute-start | bytes 720008 | tf_op jit(solution)/shard_map/ppermute | solution.py:290
  6.7 1.5 %collective-permute-start.1 = (bf16[2,96,625]{2,1,0:T(8,128)(2,1)S(1)}, bf16[2,96,625]{2,1,0:T(8,128)(2,1)S(1)}, u32[]{:S(2)}, u32[]{:S(2)}) collective-permute-start(bf16[2,96,625]{2,1,0:T(8,128)(2,1)S(1)} %get-tuple-element.16.refs_0_), channel_id=1, source_target_pairs={{0,16},{8,24},{16,0},{24,8},{1,17},{9,25},{17,1},{25,9},{2,18},{10... | collective-permute-start | bytes 720008 | tf_op jit(solution)/shard_map/ppermute | solution.py:272
  8.3 1.5 collective-permute-start
  9.8 2.6 %collective-permute-start.9 = (bf16[2,96,625]{2,1,0:T(8,128)(2,1)S(1)}, bf16[2,96,625]{2,1,0:T(8,128)(2,1)S(1)}, u32[]{:S(2)}, u32[]{:S(2)}) collective-permute-start(bf16[2,96,625]{2,1,0:T(8,128)(2,1)S(1)} %get-tuple-element.14), channel_id=1, source_target_pairs={{0,4},{1,5},{2,6},{3,7},{4,0},{5,1},{6,2},{7,3},{8,12},{9,13},{10,... | collective-permute-start | bytes 720008 | tf_op jit(solution)/shard_map/ppermute | solution.py:290
  12.3 3.3 %collective-permute-done.4.refs_0_ = bf16[2,96,625]{2,1,0:T(8,128)(2,1)S(1)} collective-permute-done((bf16[2,96,625]{2,1,0:T(8,128)(2,1)S(1)}, bf16[2,96,625]{2,1,0:T(8,128)(2,1)S(1)}, u32[]{:S(2)}, u32[]{:S(2)}) %collective-permute-start.4) | collective-permute-done | bytes 240032 | tf_op jit(solution)/shard_map/ppermute | solution.py:290
  15.7 0.0 collective-permute-done.1.refs_2_
  15.7 0.0 collective-permute-done.refs_1_
  15.7 1.8 %collective-permute-start.6 = (bf16[2,96,625]{2,1,0:T(8,128)(2,1)S(1)}, bf16[2,96,625]{2,1,0:T(8,128)(2,1)S(1)}, u32[]{:S(2)}, u32[]{:S(2)}) collective-permute-start(bf16[2,96,625]{2,1,0:T(8,128)(2,1)S(1)} %collective-permute-done.4.refs_0_), channel_id=1, source_target_pairs={{0,16},{8,24},{16,0},{24,8},{1,17},{9,25},{17,1},{25,9},{2,18},{10... | collective-permute-start | bytes 720008 | tf_op jit(solution)/shard_map/ppermute | solution.py:272
  17.4 1.5 collective-permute-start.5
  18.9 0.9 collective-permute-start.14
  19.9 5.5 %collective-permute-done.9.refs_0_ = bf16[2,96,625]{2,1,0:T(8,128)(2,1)S(1)} collective-permute-done((bf16[2,96,625]{2,1,0:T(8,128)(2,1)S(1)}, bf16[2,96,625]{2,1,0:T(8,128)(2,1)S(1)}, u32[]{:S(2)}, u32[]{:S(2)}) %collective-permute-start.9) | collective-permute-done | bytes 240032 | tf_op jit(solution)/shard_map/ppermute | solution.py:290
  25.4 0.0 collective-permute-done.6.refs_2_
  25.4 0.0 collective-permute-done.5.refs_1_
  25.4 1.5 %collective-permute-start.11 = (bf16[2,96,625]{2,1,0:T(8,128)(2,1)S(1)}, bf16[2,96,625]{2,1,0:T(8,128)(2,1)S(1)}, u32[]{:S(2)}, u32[]{:S(2)}) collective-permute-start(bf16[2,96,625]{2,1,0:T(8,128)(2,1)S(1)} %collective-permute-done.9.refs_0_), channel_id=1, source_target_pairs={{0,16},{8,24},{16,0},{24,8},{1,17},{9,25},{17,1},{25,9},{2,18},{10... | collective-permute-start | bytes 720008 | tf_op jit(solution)/shard_map/ppermute | solution.py:272
  26.9 1.4 collective-permute-start.10
  28.4 0.6 collective-permute-start.2
  29.0 0.5 collective-permute-start.7
  29.5 3.0 %collective-permute-done.14.refs_0_ = bf16[2,96,625]{2,1,0:T(8,128)(2,1)S(1)} collective-permute-done((bf16[2,96,625]{2,1,0:T(8,128)(2,1)S(1)}, bf16[2,96,625]{2,1,0:T(8,128)(2,1)S(1)}, u32[]{:S(2)}, u32[]{:S(2)}) %collective-permute-start.14) | collective-permute-done | bytes 240032 | tf_op jit(solution)/shard_map/ppermute | solution.py:290
  32.4 1.8 %collective-permute-done.11.refs_2_ = bf16[2,96,625]{2,1,0:T(8,128)(2,1)S(1)} collective-permute-done((bf16[2,96,625]{2,1,0:T(8,128)(2,1)S(1)}, bf16[2,96,625]{2,1,0:T(8,128)(2,1)S(1)}, u32[]{:S(2)}, u32[]{:S(2)}) %collective-permute-start.11) | collective-permute-done | bytes 240032 | tf_op jit(solution)/shard_map/ppermute | solution.py:272
  34.2 1.6 %collective-permute-done.10.refs_1_ = bf16[2,96,625]{2,1,0:T(8,128)(2,1)S(1)} collective-permute-done((bf16[2,96,625]{2,1,0:T(8,128)(2,1)S(1)}, bf16[2,96,625]{2,1,0:T(8,128)(2,1)S(1)}, u32[]{:S(2)}, u32[]{:S(2)}) %collective-permute-start.10) | collective-permute-done | bytes 240032 | tf_op jit(solution)/shard_map/ppermute | solution.py:272
  35.8 1.4 collective-permute-start.15
  37.2 0.3 pad
  37.6 6.9 %collective-permute-start.21 = (bf16[625,256]{1,0:T(8,128)(2,1)S(1)}, bf16[625,256]{1,0:T(8,128)(2,1)S(1)}, u32[]{:S(2)}, u32[]{:S(2)}) collective-permute-start(bf16[625,256]{1,0:T(8,128)(2,1)S(1)} %bitcast.24), channel_id=1, source_target_pairs={{0,6},{1,7},{2,0},{3,1},{4,2},{5,3},{6,4},{7,5},{8,14},{9,15},{10,... | collective-permute-start | bytes 960008 | tf_op jit(solution)/shard_map/ppermute | solution.py:290
  44.4 0.5 collective-permute-start.12
  45.0 0.0 collective-permute-done.2.refs_3_
  45.0 3.4 %shard_map.82.refs_0_ = bf16[2,1600,384]{2,1,0:T(8,128)(2,1)} custom-call(bf16[2,96,625]{2,1,0:T(8,128)(2,1)S(1)} %get-tuple-element.16.refs_0_, bf16[2,96,625]{2,1,0:T(8,128)(2,1)S(1)} %collective-permute-done.refs_1_, bf16[2,96,625]{2,1,0:T(8,128)(2,1)S(1)} %collective-permute-done.1.refs_2_, bf16[2,96,625]{2,1,0:T(8,128)(2,1)S(1)} %collective-permute-done.2.refs_3_, ...), custom_call_target="tpu_custom_call" | custom-call | flops 1536000000 | bytes 3417600 | tf_op jit(solution)/shard_map/pallas_call | solution.py:77
  48.4 0.5 collective-permute-start.16
  48.9 1.5 %collective-permute-start.17 = (bf16[2,96,625]{2,1,0:T(8,128)(2,1)S(1)}, bf16[2,96,625]{2,1,0:T(8,128)(2,1)S(1)}, u32[]{:S(2)}, u32[]{:S(2)}) collective-permute-start(bf16[2,96,625]{2,1,0:T(8,128)(2,1)S(1)} %collective-permute-done.15.refs_1_), channel_id=1, source_target_pairs={{0,16},{8,24},{16,0},{24,8},{1,17},{9,25},{17,1},{25,9},{2,18},{10... | collective-permute-start | bytes 720008 | tf_op jit(solution)/shard_map/ppermute | solution.py:272
  50.4 3.5 %shard_map.83.refs_2_ = bf16[2,1600,384]{2,1,0:T(8,128)(2,1)} custom-call(bf16[2,96,625]{2,1,0:T(8,128)(2,1)S(1)} %collective-permute-done.4.refs_0_, bf16[2,96,625]{2,1,0:T(8,128)(2,1)S(1)} %collective-permute-done.5.refs_1_, bf16[2,96,625]{2,1,0:T(8,128)(2,1)S(1)} %collective-permute-done.6.refs_2_, ...), custom_call_target="tpu_custom_call" | custom-call | flops 1536000000 | bytes 3417600 | tf_op jit(solution)/shard_map/pallas_call | solution.py:77
  53.9 0.0 collective-permute-done.12.refs_3_
  53.9 0.0 collective-permute-start.8
  53.9 3.5 %shard_map.84.refs_4_ = bf16[2,1600,384]{2,1,0:T(8,128)(2,1)} custom-call(bf16[2,96,625]{2,1,0:T(8,128)(2,1)S(1)} %collective-permute-done.9.refs_0_, bf16[2,96,625]{2,1,0:T(8,128)(2,1)S(1)} %collective-permute-done.10.refs_1_, bf16[2,96,625]{2,1,0:T(8,128)(2,1)S(1)} %collective-permute-done.11.refs_2_, ...), custom_call_target="tpu_custom_call" | custom-call | flops 1536000000 | bytes 3417600 | tf_op jit(solution)/shard_map/pallas_call | solution.py:77
  57.4 0.5 collective-permute-start.13
  57.9 4.2 %collective-permute-done.17.refs_3_ = bf16[2,96,625]{2,1,0:T(8,128)(2,1)S(1)} collective-permute-done((bf16[2,96,625]{2,1,0:T(8,128)(2,1)S(1)}, bf16[2,96,625]{2,1,0:T(8,128)(2,1)S(1)}, u32[]{:S(2)}, u32[]{:S(2)}) %collective-permute-start.17) | collective-permute-done | bytes 240032 | tf_op jit(solution)/shard_map/ppermute | solution.py:272
  62.0 3.4 %shard_map.85.refs_6_ = bf16[2,1600,384]{2,1,0:T(8,128)(2,1)} custom-call(bf16[2,96,625]{2,1,0:T(8,128)(2,1)S(1)} %collective-permute-done.14.refs_0_, bf16[2,96,625]{2,1,0:T(8,128)(2,1)S(1)} %collective-permute-done.15.refs_1_, bf16[2,96,625]{2,1,0:T(8,128)(2,1)S(1)} %collective-permute-done.16.refs_2_, ...), custom_call_target="tpu_custom_call" | custom-call | flops 1536000000 | bytes 3417600 | tf_op jit(solution)/shard_map/pallas_call | solution.py:77
  65.5 0.0 collective-permute-start.18
  65.5 0.0 collective-permute-done.21.refs_3_
  65.5 3.7 %collective-permute-start.20 = (bf16[625,256]{1,0:T(8,128)(2,1)S(1)}, bf16[625,256]{1,0:T(8,128)(2,1)S(1)}, u32[]{:S(2)}, u32[]{:S(2)}) collective-permute-start(bf16[625,256]{1,0:T(8,128)(2,1)S(1)} %bitcast.25), channel_id=1, source_target_pairs={{0,4},{1,5},{2,6},{3,7},{4,0},{5,1},{6,2},{7,3},{8,12},{9,13},{10,... | collective-permute-start | bytes 960008 | tf_op jit(solution)/shard_map/ppermute | solution.py:290
  69.2 15.2 %collective-permute-done.20.refs_2_ = bf16[625,256]{1,0:T(8,128)(2,1)S(1)} collective-permute-done((bf16[625,256]{1,0:T(8,128)(2,1)S(1)}, bf16[625,256]{1,0:T(8,128)(2,1)S(1)}, u32[]{:S(2)}, u32[]{:S(2)}) %collective-permute-start.20) | collective-permute-done | bytes 320032 | tf_op jit(solution)/shard_map/ppermute | solution.py:290
  84.4 0.7 collective-permute-start.19
  85.1 10.7 %collective-permute-done.19.refs_1_ = bf16[625,256]{1,0:T(8,128)(2,1)S(1)} collective-permute-done((bf16[625,256]{1,0:T(8,128)(2,1)S(1)}, bf16[625,256]{1,0:T(8,128)(2,1)S(1)}, u32[]{:S(2)}, u32[]{:S(2)}) %collective-permute-start.19) | collective-permute-done | bytes 320032 | tf_op jit(solution)/shard_map/ppermute | solution.py:290
  95.8 1.4 shard_map.86.refs_8_
  97.2 0.1 collective-permute-start.22
  97.3 0.1 copy.24.owners_ref
  97.4 0.1 copy.25.local_ref
  97.5 3.3 %collective-permute-done.22.refs_9_ = bf16[8,800,128]{2,1,0:T(8,128)(2,1)S(1)} collective-permute-done((bf16[8,800,128]{2,1,0:T(8,128)(2,1)S(1)}, bf16[8,800,128]{2,1,0:T(8,128)(2,1)S(1)}, u32[]{:S(2)}, u32[]{:S(2)}) %collective-permute-start.22) | collective-permute-done | bytes 1638432 | tf_op jit(solution)/shard_map/ppermute | solution.py:287
  100.8 0.0 collective-permute-done.3.refs_1_
  100.8 0.0 collective-permute-done.8.refs_3_
  100.8 0.0 collective-permute-done.13.refs_5_
  100.8 0.0 copy-start
  100.8 1.2 copy-done
  102.1 10.4 %shard_map.88 = bf16[1,2,625,128]{3,2,1,0:T(8,128)(2,1)S(1)} custom-call(s32[1]{0:T(128)} %bitcast.column_ref, s32[32,3]{1,0:T(8,128)S(1)} %copy.24.owners_ref, s32[32,4]{1,0:T(8,128)S(1)} %copy.25.local_ref, bf16[2,1600,384]{2,1,0:T(8,128)(2,1)} %shard_map.82.refs_0_, bf16[2,1600,384]{2,1,0:T(8,128)(2,1)} %collective-permute-done.3.refs_1_, ...), custom_call_target="tpu_custom_call" | custom-call | flops 2936012800 | bytes 6553600 | tf_op jit(solution)/shard_map/pallas_call | solution.py:252
  112.4 2.0 %collective-permute-start.24 = (bf16[2,625,128]{2,1,0:T(8,128)(2,1)S(1)}, bf16[2,625,128]{2,1,0:T(8,128)(2,1)S(1)}, u32[]{:S(2)}, u32[]{:S(2)}) collective-permute-start(bf16[2,625,128]{2,1,0:T(8,128)(2,1)S(1)} %bitcast.28), channel_id=1, source_target_pairs={{0,6},{1,7},{2,0},{3,1},{4,2},{5,3},{6,4},{7,5},{8,14},{9,15},{10,... | collective-permute-start | bytes 960008 | tf_op jit(solution)/shard_map/ppermute | solution.py:290
  114.4 10.4 %shard_map.87 = bf16[1,2,625,128]{3,2,1,0:T(8,128)(2,1)S(1)} custom-call(s32[1]{0:T(128)} %bitcast.column_ref, s32[32,3]{1,0:T(8,128)S(1)} %copy.24.owners_ref, s32[32,4]{1,0:T(8,128)S(1)} %copy.25.local_ref, bf16[2,1600,384]{2,1,0:T(8,128)(2,1)} %shard_map.82.refs_0_, bf16[2,1600,384]{2,1,0:T(8,128)(2,1)} %collective-permute-done.3.refs_1_, ...), custom_call_target="tpu_custom_call" | custom-call | flops 2936012800 | bytes 6553600 | tf_op jit(solution)/shard_map/pallas_call | solution.py:252
  124.8 0.1 collective-permute-start.23
  124.9 10.4 %shard_map.89 = bf16[1,2,625,128]{3,2,1,0:T(8,128)(2,1)S(1)} custom-call(s32[1]{0:T(128)} %bitcast.column_ref, s32[32,3]{1,0:T(8,128)S(1)} %copy.24.owners_ref, s32[32,4]{1,0:T(8,128)S(1)} %copy.25.local_ref, bf16[2,1600,384]{2,1,0:T(8,128)(2,1)} %shard_map.82.refs_0_, bf16[2,1600,384]{2,1,0:T(8,128)(2,1)} %collective-permute-done.3.refs_1_, ...), custom_call_target="tpu_custom_call" | custom-call | flops 2936012800 | bytes 6553600 | tf_op jit(solution)/shard_map/pallas_call | solution.py:252
  135.2 0.0 copy-start.3
  135.2 0.6 collective-permute-start.25
  135.9 10.3 %shard_map.90 = bf16[1,2,625,128]{3,2,1,0:T(8,128)(2,1)S(1)} custom-call(s32[1]{0:T(128)} %bitcast.column_ref, s32[32,3]{1,0:T(8,128)S(1)} %copy.24.owners_ref, s32[32,4]{1,0:T(8,128)S(1)} %copy.25.local_ref, bf16[2,1600,384]{2,1,0:T(8,128)(2,1)} %shard_map.82.refs_0_, bf16[2,1600,384]{2,1,0:T(8,128)(2,1)} %collective-permute-done.3.refs_1_, ...), custom_call_target="tpu_custom_call" | custom-call | flops 2936012800 | bytes 6553600 | tf_op jit(solution)/shard_map/pallas_call | solution.py:252
  146.2 2.5 %collective-permute-done.23 = bf16[2,625,128]{2,1,0:T(8,128)(2,1)S(1)} collective-permute-done((bf16[2,625,128]{2,1,0:T(8,128)(2,1)S(1)}, bf16[2,625,128]{2,1,0:T(8,128)(2,1)S(1)}, u32[]{:S(2)}, u32[]{:S(2)}) %collective-permute-start.23) | collective-permute-done | bytes 320032 | tf_op jit(solution)/shard_map/ppermute | solution.py:290
  148.7 0.2 fusion.1
  148.9 1.2 copy.33
  (19 shorter events, 0.1 us)
Async XLA Ops:
  0.0 37.2 %copy-start.4 = (bf16[2,128,625]{1,0,2:T(2,128)(2,1)S(1)}, bf16[2,128,625]{1,0,2:T(2,128)(2,1)}, u32[]{:S(2)}) copy-start(bf16[2,128,625]{1,0,2:T(2,128)(2,1)} %param.9) | copy-start | bytes 960004
  0.0 45.0 %copy-start.2 = (bf16[1600,625]{1,0:T(8,128)(2,1)S(1)}, bf16[1600,625]{1,0:T(8,128)(2,1)}, u32[]{:S(2)}) copy-start(bf16[1600,625]{1,0:T(8,128)(2,1)} %constant.61.clone.refs_4_) | copy-start | bytes 6000004
  3.7 12.0 %collective-permute-start.4 = (bf16[2,96,625]{2,1,0:T(8,128)(2,1)S(1)}, bf16[2,96,625]{2,1,0:T(8,128)(2,1)S(1)}, u32[]{:S(2)}, u32[]{:S(2)}) collective-permute-start(bf16[2,96,625]{2,1,0:T(8,128)(2,1)S(1)} %get-tuple-element.15), channel_id=1, source_target_pairs={{0,2},{1,3},{2,4},{3,5},{4,6},{5,7},{6,0},{7,1},{8,10},{9,11},{10,... | collective-permute-start | bytes 720008 | tf_op jit(solution)/shard_map/ppermute | solution.py:290
  6.7 8.9 %collective-permute-start.1 = (bf16[2,96,625]{2,1,0:T(8,128)(2,1)S(1)}, bf16[2,96,625]{2,1,0:T(8,128)(2,1)S(1)}, u32[]{:S(2)}, u32[]{:S(2)}) collective-permute-start(bf16[2,96,625]{2,1,0:T(8,128)(2,1)S(1)} %get-tuple-element.16.refs_0_), channel_id=1, source_target_pairs={{0,16},{8,24},{16,0},{24,8},{1,17},{9,25},{17,1},{25,9},{2,18},{10... | collective-permute-start | bytes 720008 | tf_op jit(solution)/shard_map/ppermute | solution.py:272
  8.3 7.4 %collective-permute-start = (bf16[2,96,625]{2,1,0:T(8,128)(2,1)S(1)}, bf16[2,96,625]{2,1,0:T(8,128)(2,1)S(1)}, u32[]{:S(2)}, u32[]{:S(2)}) collective-permute-start(bf16[2,96,625]{2,1,0:T(8,128)(2,1)S(1)} %get-tuple-element.16.refs_0_), channel_id=1, source_target_pairs={{0,8},{8,0},{16,24},{24,16},{1,9},{9,1},{17,25},{25,17},{2,10},{10... | collective-permute-start | bytes 720008 | tf_op jit(solution)/shard_map/ppermute | solution.py:272
  9.8 15.6 %collective-permute-start.9 = (bf16[2,96,625]{2,1,0:T(8,128)(2,1)S(1)}, bf16[2,96,625]{2,1,0:T(8,128)(2,1)S(1)}, u32[]{:S(2)}, u32[]{:S(2)}) collective-permute-start(bf16[2,96,625]{2,1,0:T(8,128)(2,1)S(1)} %get-tuple-element.14), channel_id=1, source_target_pairs={{0,4},{1,5},{2,6},{3,7},{4,0},{5,1},{6,2},{7,3},{8,12},{9,13},{10,... | collective-permute-start | bytes 720008 | tf_op jit(solution)/shard_map/ppermute | solution.py:290
  15.7 9.7 %collective-permute-start.6 = (bf16[2,96,625]{2,1,0:T(8,128)(2,1)S(1)}, bf16[2,96,625]{2,1,0:T(8,128)(2,1)S(1)}, u32[]{:S(2)}, u32[]{:S(2)}) collective-permute-start(bf16[2,96,625]{2,1,0:T(8,128)(2,1)S(1)} %collective-permute-done.4.refs_0_), channel_id=1, source_target_pairs={{0,16},{8,24},{16,0},{24,8},{1,17},{9,25},{17,1},{25,9},{2,18},{10... | collective-permute-start | bytes 720008 | tf_op jit(solution)/shard_map/ppermute | solution.py:272
  17.4 8.0 %collective-permute-start.5 = (bf16[2,96,625]{2,1,0:T(8,128)(2,1)S(1)}, bf16[2,96,625]{2,1,0:T(8,128)(2,1)S(1)}, u32[]{:S(2)}, u32[]{:S(2)}) collective-permute-start(bf16[2,96,625]{2,1,0:T(8,128)(2,1)S(1)} %collective-permute-done.4.refs_0_), channel_id=1, source_target_pairs={{0,8},{8,0},{16,24},{24,16},{1,9},{9,1},{17,25},{25,17},{2,10},{10... | collective-permute-start | bytes 720008 | tf_op jit(solution)/shard_map/ppermute | solution.py:272
  18.9 13.5 %collective-permute-start.14 = (bf16[2,96,625]{2,1,0:T(8,128)(2,1)S(1)}, bf16[2,96,625]{2,1,0:T(8,128)(2,1)S(1)}, u32[]{:S(2)}, u32[]{:S(2)}) collective-permute-start(bf16[2,96,625]{2,1,0:T(8,128)(2,1)S(1)} %get-tuple-element.13), channel_id=1, source_target_pairs={{0,6},{1,7},{2,0},{3,1},{4,2},{5,3},{6,4},{7,5},{8,14},{9,15},{10,... | collective-permute-start | bytes 720008 | tf_op jit(solution)/shard_map/ppermute | solution.py:290
  25.4 8.8 %collective-permute-start.11 = (bf16[2,96,625]{2,1,0:T(8,128)(2,1)S(1)}, bf16[2,96,625]{2,1,0:T(8,128)(2,1)S(1)}, u32[]{:S(2)}, u32[]{:S(2)}) collective-permute-start(bf16[2,96,625]{2,1,0:T(8,128)(2,1)S(1)} %collective-permute-done.9.refs_0_), channel_id=1, source_target_pairs={{0,16},{8,24},{16,0},{24,8},{1,17},{9,25},{17,1},{25,9},{2,18},{10... | collective-permute-start | bytes 720008 | tf_op jit(solution)/shard_map/ppermute | solution.py:272
  26.9 8.9 %collective-permute-start.10 = (bf16[2,96,625]{2,1,0:T(8,128)(2,1)S(1)}, bf16[2,96,625]{2,1,0:T(8,128)(2,1)S(1)}, u32[]{:S(2)}, u32[]{:S(2)}) collective-permute-start(bf16[2,96,625]{2,1,0:T(8,128)(2,1)S(1)} %collective-permute-done.9.refs_0_), channel_id=1, source_target_pairs={{0,8},{8,0},{16,24},{24,16},{1,9},{9,1},{17,25},{25,17},{2,10},{10... | collective-permute-start | bytes 720008 | tf_op jit(solution)/shard_map/ppermute | solution.py:272
  28.4 16.6 %collective-permute-start.2 = (bf16[2,96,625]{2,1,0:T(8,128)(2,1)S(1)}, bf16[2,96,625]{2,1,0:T(8,128)(2,1)S(1)}, u32[]{:S(2)}, u32[]{:S(2)}) collective-permute-start(bf16[2,96,625]{2,1,0:T(8,128)(2,1)S(1)} %collective-permute-done.1.refs_2_), channel_id=1, source_target_pairs={{0,8},{8,0},{16,24},{24,16},{1,9},{9,1},{17,25},{25,17},{2,10},{10... | collective-permute-start | bytes 720008 | tf_op jit(solution)/shard_map/ppermute | solution.py:272
  29.0 19.5 %collective-permute-start.7 = (bf16[2,96,625]{2,1,0:T(8,128)(2,1)S(1)}, bf16[2,96,625]{2,1,0:T(8,128)(2,1)S(1)}, u32[]{:S(2)}, u32[]{:S(2)}) collective-permute-start(bf16[2,96,625]{2,1,0:T(8,128)(2,1)S(1)} %collective-permute-done.5.refs_1_), channel_id=1, source_target_pairs={{0,16},{8,24},{16,0},{24,8},{1,17},{9,25},{17,1},{25,9},{2,18},{10... | collective-permute-start | bytes 720008 | tf_op jit(solution)/shard_map/ppermute | solution.py:272
  35.8 13.1 %collective-permute-start.15 = (bf16[2,96,625]{2,1,0:T(8,128)(2,1)S(1)}, bf16[2,96,625]{2,1,0:T(8,128)(2,1)S(1)}, u32[]{:S(2)}, u32[]{:S(2)}) collective-permute-start(bf16[2,96,625]{2,1,0:T(8,128)(2,1)S(1)} %collective-permute-done.14.refs_0_), channel_id=1, source_target_pairs={{0,8},{8,0},{16,24},{24,16},{1,9},{9,1},{17,25},{25,17},{2,10},{10... | collective-permute-start | bytes 720008 | tf_op jit(solution)/shard_map/ppermute | solution.py:272
  37.6 27.9 %collective-permute-start.21 = (bf16[625,256]{1,0:T(8,128)(2,1)S(1)}, bf16[625,256]{1,0:T(8,128)(2,1)S(1)}, u32[]{:S(2)}, u32[]{:S(2)}) collective-permute-start(bf16[625,256]{1,0:T(8,128)(2,1)S(1)} %bitcast.24), channel_id=1, source_target_pairs={{0,6},{1,7},{2,0},{3,1},{4,2},{5,3},{6,4},{7,5},{8,14},{9,15},{10,... | collective-permute-start | bytes 960008 | tf_op jit(solution)/shard_map/ppermute | solution.py:290
  44.4 9.5 %collective-permute-start.12 = (bf16[2,96,625]{2,1,0:T(8,128)(2,1)S(1)}, bf16[2,96,625]{2,1,0:T(8,128)(2,1)S(1)}, u32[]{:S(2)}, u32[]{:S(2)}) collective-permute-start(bf16[2,96,625]{2,1,0:T(8,128)(2,1)S(1)} %collective-permute-done.11.refs_2_), channel_id=1, source_target_pairs={{0,8},{8,0},{16,24},{24,16},{1,9},{9,1},{17,25},{25,17},{2,10},{10... | collective-permute-start | bytes 720008 | tf_op jit(solution)/shard_map/ppermute | solution.py:272
  48.4 52.4 %collective-permute-start.3 = (bf16[2,1600,384]{2,1,0:T(8,128)(2,1)}, bf16[2,1600,384]{2,1,0:T(8,128)(2,1)}, u32[]{:S(2)}, u32[]{:S(2)}) collective-permute-start(bf16[2,1600,384]{2,1,0:T(8,128)(2,1)} %shard_map.82.refs_0_), channel_id=1, source_target_pairs={{0,1},{1,0},{2,3},{3,2},{4,5},{5,4},{6,7},{7,6},{8,9},{9,8},{10,11... | collective-permute-start | bytes 7372808 | tf_op jit(solution)/shard_map/ppermute | solution.py:287
  48.4 9.0 %collective-permute-start.16 = (bf16[2,96,625]{2,1,0:T(8,128)(2,1)S(1)}, bf16[2,96,625]{2,1,0:T(8,128)(2,1)S(1)}, u32[]{:S(2)}, u32[]{:S(2)}) collective-permute-start(bf16[2,96,625]{2,1,0:T(8,128)(2,1)S(1)} %collective-permute-done.14.refs_0_), channel_id=1, source_target_pairs={{0,16},{8,24},{16,0},{24,8},{1,17},{9,25},{17,1},{25,9},{2,18},{10... | collective-permute-start | bytes 720008 | tf_op jit(solution)/shard_map/ppermute | solution.py:272
  48.9 13.1 %collective-permute-start.17 = (bf16[2,96,625]{2,1,0:T(8,128)(2,1)S(1)}, bf16[2,96,625]{2,1,0:T(8,128)(2,1)S(1)}, u32[]{:S(2)}, u32[]{:S(2)}) collective-permute-start(bf16[2,96,625]{2,1,0:T(8,128)(2,1)S(1)} %collective-permute-done.15.refs_1_), channel_id=1, source_target_pairs={{0,16},{8,24},{16,0},{24,8},{1,17},{9,25},{17,1},{25,9},{2,18},{10... | collective-permute-start | bytes 720008 | tf_op jit(solution)/shard_map/ppermute | solution.py:272
  53.9 46.9 %collective-permute-start.8 = (bf16[2,1600,384]{2,1,0:T(8,128)(2,1)}, bf16[2,1600,384]{2,1,0:T(8,128)(2,1)}, u32[]{:S(2)}, u32[]{:S(2)}) collective-permute-start(bf16[2,1600,384]{2,1,0:T(8,128)(2,1)} %shard_map.83.refs_2_), channel_id=1, source_target_pairs={{0,1},{1,0},{2,3},{3,2},{4,5},{5,4},{6,7},{7,6},{8,9},{9,8},{10,11... | collective-permute-start | bytes 7372808 | tf_op jit(solution)/shard_map/ppermute | solution.py:287
  57.4 38.4 %copy-start.1 = (bf16[800,625]{1,0:T(8,128)(2,1)S(1)}, bf16[800,625]{1,0:T(8,128)(2,1)}, u32[]{:S(2)}) copy-start(bf16[800,625]{1,0:T(8,128)(2,1)} %constant.63.clone.matrix_ref) | copy-start | bytes 3000004
  57.4 43.4 %collective-permute-start.13 = (bf16[2,1600,384]{2,1,0:T(8,128)(2,1)}, bf16[2,1600,384]{2,1,0:T(8,128)(2,1)}, u32[]{:S(2)}, u32[]{:S(2)}) collective-permute-start(bf16[2,1600,384]{2,1,0:T(8,128)(2,1)} %shard_map.84.refs_4_), channel_id=1, source_target_pairs={{0,1},{1,0},{2,3},{3,2},{4,5},{5,4},{6,7},{7,6},{8,9},{9,8},{10,11... | collective-permute-start | bytes 7372808 | tf_op jit(solution)/shard_map/ppermute | solution.py:287
  65.5 31.8 %copy-start.5 = (s32[32,3]{0,1:T(4,128)S(1)}, s32[32,3]{0,1:T(4,128)}, u32[]{:S(2)}) copy-start(s32[32,3]{0,1:T(4,128)} %param.11) | copy-start | bytes 1156
  65.5 31.9 %copy-start.6 = (s32[32,4]{0,1:T(4,128)S(1)}, s32[32,4]{0,1:T(4,128)}, u32[]{:S(2)}) copy-start(s32[32,4]{0,1:T(4,128)} %param.12) | copy-start | bytes 1540
  65.5 35.3 %collective-permute-start.18 = (bf16[2,1600,384]{2,1,0:T(8,128)(2,1)}, bf16[2,1600,384]{2,1,0:T(8,128)(2,1)}, u32[]{:S(2)}, u32[]{:S(2)}) collective-permute-start(bf16[2,1600,384]{2,1,0:T(8,128)(2,1)} %shard_map.85.refs_6_), channel_id=1, source_target_pairs={{0,1},{1,0},{2,3},{3,2},{4,5},{5,4},{6,7},{7,6},{8,9},{9,8},{10,11... | collective-permute-start | bytes 7372808 | tf_op jit(solution)/shard_map/ppermute | solution.py:287
  65.5 18.9 %collective-permute-start.20 = (bf16[625,256]{1,0:T(8,128)(2,1)S(1)}, bf16[625,256]{1,0:T(8,128)(2,1)S(1)}, u32[]{:S(2)}, u32[]{:S(2)}) collective-permute-start(bf16[625,256]{1,0:T(8,128)(2,1)S(1)} %bitcast.25), channel_id=1, source_target_pairs={{0,4},{1,5},{2,6},{3,7},{4,0},{5,1},{6,2},{7,3},{8,12},{9,13},{10,... | collective-permute-start | bytes 960008 | tf_op jit(solution)/shard_map/ppermute | solution.py:290
  84.4 11.4 %collective-permute-start.19 = (bf16[625,256]{1,0:T(8,128)(2,1)S(1)}, bf16[625,256]{1,0:T(8,128)(2,1)S(1)}, u32[]{:S(2)}, u32[]{:S(2)}) collective-permute-start(bf16[625,256]{1,0:T(8,128)(2,1)S(1)} %bitcast.26), channel_id=1, source_target_pairs={{0,2},{1,3},{2,4},{3,5},{4,6},{5,7},{6,0},{7,1},{8,10},{9,11},{10,... | collective-permute-start | bytes 960008 | tf_op jit(solution)/shard_map/ppermute | solution.py:290
  97.2 3.6 %collective-permute-start.22 = (bf16[8,800,128]{2,1,0:T(8,128)(2,1)S(1)}, bf16[8,800,128]{2,1,0:T(8,128)(2,1)S(1)}, u32[]{:S(2)}, u32[]{:S(2)}) collective-permute-start(bf16[8,800,128]{2,1,0:T(8,128)(2,1)S(1)} %shard_map.86.refs_8_), channel_id=1, source_target_pairs={{0,1},{1,0},{2,3},{3,2},{4,5},{5,4},{6,7},{7,6},{8,9},{9,8},{10,11... | collective-permute-start | bytes 4915208 | tf_op jit(solution)/shard_map/ppermute | solution.py:287
  100.8 1.3 copy-start
  112.4 33.8 %collective-permute-start.24 = (bf16[2,625,128]{2,1,0:T(8,128)(2,1)S(1)}, bf16[2,625,128]{2,1,0:T(8,128)(2,1)S(1)}, u32[]{:S(2)}, u32[]{:S(2)}) collective-permute-start(bf16[2,625,128]{2,1,0:T(8,128)(2,1)S(1)} %bitcast.28), channel_id=1, source_target_pairs={{0,6},{1,7},{2,0},{3,1},{4,2},{5,3},{6,4},{7,5},{8,14},{9,15},{10,... | collective-permute-start | bytes 960008 | tf_op jit(solution)/shard_map/ppermute | solution.py:290
  124.8 23.9 %collective-permute-start.23 = (bf16[2,625,128]{2,1,0:T(8,128)(2,1)S(1)}, bf16[2,625,128]{2,1,0:T(8,128)(2,1)S(1)}, u32[]{:S(2)}, u32[]{:S(2)}) collective-permute-start(bf16[2,625,128]{2,1,0:T(8,128)(2,1)S(1)} %bitcast.29), channel_id=1, source_target_pairs={{0,4},{1,5},{2,6},{3,7},{4,0},{5,1},{6,2},{7,3},{8,12},{9,13},{10,... | collective-permute-start | bytes 960008 | tf_op jit(solution)/shard_map/ppermute | solution.py:290
  135.2 13.5 %copy-start.3 = (f32[2,128,625]{1,0,2:T(2,128)S(1)}, f32[2,128,625]{1,0,2:T(2,128)}, u32[]{:S(2)}) copy-start(f32[2,128,625]{1,0,2:T(2,128)} %param.10) | copy-start | bytes 1920004
  135.2 13.5 %collective-permute-start.25 = (bf16[2,625,128]{2,1,0:T(8,128)(2,1)S(1)}, bf16[2,625,128]{2,1,0:T(8,128)(2,1)S(1)}, u32[]{:S(2)}, u32[]{:S(2)}) collective-permute-start(bf16[2,625,128]{2,1,0:T(8,128)(2,1)S(1)} %bitcast.30), channel_id=1, source_target_pairs={{0,2},{1,3},{2,4},{3,5},{4,6},{5,7},{6,0},{7,1},{8,10},{9,11},{10,... | collective-permute-start | bytes 960008 | tf_op jit(solution)/shard_map/ppermute | solution.py:290

commit v6 on v5

--- a/solution.py
+++ b/solution.py
@@ -43,18 +43,18 @@
     return spread(PLACE[a] * PAD + b, ROWS).T
 
 
-def prepare_kernel(pieces, *refs):
-    tile_refs, matrix_ref = refs[:pieces], refs[pieces]
-    forms_ref, all_ref = refs[-2:]
+def prepare_kernel(column_ref, *refs):
+    tile_refs, matrix_ref, forms_ref, all_ref = refs[:4], refs[4], refs[5], refs[6]
     count, size, _ = tile_refs[0].shape
     depth = forms_ref.shape[2]
 
     @pl.when(pl.program_id(0) == 0)
     def _():
+        core = lax.rem(column_ref[0], 2)
         for m in range(count):
-            for i, ref in enumerate(tile_refs):
-                start = m * depth + i * size
-                all_ref[start : start + size, :] = ref[m]
+            for place, ref in zip((0, 1 + core, 2 - core, 3), tile_refs):
+                start = pl.multiple_of(m * depth + place * size, size)
+                all_ref[pl.ds(start, size), :] = ref[m]
 
     wide = count if depth % LANES == 0 else 1
     for first in range(0, count, wide):
@@ -68,48 +68,55 @@
             forms_ref[first + m] = made[:, m * depth : (m + 1) * depth]
 
 
-def prepare(parts, matrix):
+def prepare(parts, column, matrix):
     count, size, width = parts[0].shape
     depth = size * len(parts)
     rows = matrix.shape[0] // PREPARE_STEPS
-    in_specs = [pl.BlockSpec(part.shape, lambda i: (0, 0, 0)) for part in parts]
-    in_specs.append(pl.BlockSpec((rows, width), lambda i: (i, 0)))
+    in_specs = [pl.BlockSpec(part.shape, lambda i, column: (0, 0, 0)) for part in parts]
+    in_specs.append(pl.BlockSpec((rows, width), lambda i, column: (i, 0)))
     return pl.pallas_call(
-        functools.partial(prepare_kernel, len(parts)),
+        prepare_kernel,
         out_shape=jax.ShapeDtypeStruct((count, matrix.shape[0], depth), BF),
-        grid=(PREPARE_STEPS,),
-        in_specs=in_specs,
-        out_specs=pl.BlockSpec((count, rows, depth), lambda i: (0, i, 0)),
-        scratch_shapes=[pltpu.VMEM((count * depth, width), BF)],
+        grid_spec=pltpu.PrefetchScalarGridSpec(
+            num_scalar_prefetch=1,
+            grid=(PREPARE_STEPS,),
+            in_specs=in_specs,
+            out_specs=pl.BlockSpec((count, rows, depth), lambda i, column: (0, i, 0)),
+            scratch_shapes=[pltpu.VMEM((count * depth, width), BF)],
+        ),
         compiler_params=pltpu.CompilerParams(vmem_limit_bytes=VMEM_BYTES),
         cost_estimate=pl.CostEstimate(
             flops=2 * count * depth * width * matrix.shape[0],
             bytes_accessed=2 * count * depth * (width + matrix.shape[0]),
             transcendentals=0,
         ),
-    )(*parts, matrix)
-
-
-def amp_kernel(matrix_ref, *refs):
-    tile_refs, out_ref = refs[:-1], refs[-1]
-    blocks_here, pairs = out_ref.shape[0] // len(tile_refs), out_ref.shape[2]
-    for by, ref in enumerate(tile_refs):
-        made = jnp.dot(matrix_ref[...], ref[...], preferred_element_type=F32).astype(BF)
-        for m in range(blocks_here):
-            out_ref[by * blocks_here + m] = made[:, m * pairs : (m + 1) * pairs]
-
-
-def prepare_amps(parts, blocks_here, matrix):
-    levels, size = len(parts), parts[0].size
-    pairs = parts[0].shape[1] // blocks_here
+    )(column, *parts, matrix)
+
+
+def amp_kernel(matrix_ref, tiles_ref, out_ref):
+    pairs = out_ref.shape[2]
+    made = jnp.dot(matrix_ref[...], tiles_ref[0], preferred_element_type=F32).astype(BF)
+    for m in range(out_ref.shape[0]):
+        out_ref[m] = made[:, m * pairs : (m + 1) * pairs]
+
+
+def prepare_amps(tiles, blocks_here, matrix):
+    levels, entries, width = tiles.shape
+    pairs = width // blocks_here
     return pl.pallas_call(
         amp_kernel,
         out_shape=jax.ShapeDtypeStruct((levels * blocks_here, ROWS, pairs), BF),
+        grid=(levels,),
+        in_specs=[
+            pl.BlockSpec(matrix.shape, lambda i: (0, 0)),
+            pl.BlockSpec((1, entries, width), lambda i: (i, 0, 0)),
+        ],
+        out_specs=pl.BlockSpec((blocks_here, ROWS, pairs), lambda i: (i, 0, 0)),
         compiler_params=pltpu.CompilerParams(vmem_limit_bytes=VMEM_BYTES),
         cost_estimate=pl.CostEstimate(
-            flops=2 * levels * size * ROWS, bytes_accessed=4 * levels * size, transcendentals=0
-        ),
-    )(matrix, *parts)
+            flops=2 * tiles.size * ROWS, bytes_accessed=4 * tiles.size, transcendentals=0
+        ),
+    )(matrix, tiles)
 
 
 def turned(ref, groups, by):
@@ -229,8 +236,9 @@
             below, far, m = place(kind)
             return (below * 2 + far, m) if made else (0, (below * 2 + far) * blocks_here + m)
 
-        below, far, m = place(2)
-        return {"task": task, "row": factor(0), "col": factor(1), "amp": (far, below * blocks_here + m)}
+        _, far, m = place(2)
+        amp = owners_ref[task, 2] // 2 * blocks_here + m
+        return {"task": task, "row": factor(0), "col": factor(1), "amp": (far, amp)}
 
     anywhere = pl.BlockSpec(memory_space=pl.ANY)
     fixed = lambda shape: pl.BlockSpec(shape, lambda i, j, *tables: (0,) * len(shape))
@@ -268,8 +276,8 @@
     )(column, task_owners, task_local, *operands)
 
 
-def beside(x, bit, pair_count):
-    return lax.ppermute(x, "pair", [(p, p ^ bit) for p in range(pair_count)])
+def after(values, done):
+    return lax.optimization_barrier((values, done))[0]
 
 
 def per_device(factor_blocks, amplitudes, residual_in, task_owners, task_local):
@@ -289,28 +297,47 @@
     def around(x, by):
         return lax.ppermute(x, "task", [(c, (c + 2 * by) % task_count) for c in range(task_count)])
 
+    same_core = [[2 * z + k for z in range(levels)] for k in range(2)]
     slices = factor_blocks.reshape(blocks_here, levels, depth, -1)
     mine = [lax.dynamic_index_in_dim(slices, (level + by) % levels, 1, keepdims=False) for by in range(levels)]
-    parts = [mine[0]] + [around(mine[by], by) for by in range(1, levels)]
-    if pair_count == 4:
+    if pair_count == 4 and levels == 4:
+        sides = [
+            [(p * task_count + c, (p ^ (1 if c % 2 == turn else 2)) * task_count + c) for p in range(4) for c in range(task_count)]
+            for turn in range(2)
+        ]
+        first_side = lambda x: lax.ppermute(x, ("pair", "task"), sides[0])
+        second_side = lambda x: lax.ppermute(x, ("pair", "task"), sides[1])
+        part0 = mine[0]
+        a0, b0, part1, part3 = first_side(part0), second_side(part0), around(mine[1], 1), around(mine[3], 3)
+
+        a0, b0, part0, part1, part3, to2 = after((a0, b0, part0, part1, part3, mine[2]), ())
+        q0, a1, b1, a3, part2 = second_side(a0), first_side(part1), second_side(part1), first_side(part3), around(to2, 2)
+
         own = amplitudes.transpose(2, 0, 1).reshape(TV * TV, blocks_here * pairs)
-        (own,), _ = lax.optimization_barrier(((own,), parts[1:]))
-        amps = [own] + [around(own, by) for by in range(1, levels)]
-        amps = prepare_amps(amps, blocks_here, jnp.asarray(amp_matrix()))
-        held, flying = [], ()
-        for by, part in enumerate(parts):
-            part, flying = lax.optimization_barrier((part, flying))
-            across, along = beside(part, 1, pair_count), beside(part, 2, pair_count)
-            corner = beside(along, 1, pair_count) if by % 2 == 0 else beside(across, 2, pair_count)
-            flying = (across, along)
-            forms = prepare([part, across, along, corner], matrix)
-            held += [forms, other_core(forms)]
+        own = jnp.broadcast_to(own, (levels, *own.shape))
+        own, q0, a1, b1, a3, part2, part3 = after((own, q0, a1, b1, a3, part2, part3), ())
+        own = lax.all_to_all(own, "task", split_axis=0, concat_axis=0, axis_index_groups=same_core)
+        q1, b3, a2, b2 = second_side(a1), second_side(part3), first_side(part2), second_side(part2)
+        forms0 = prepare([part0, a0, b0, q0], column[None], matrix)
+        far0 = other_core(forms0)
+
+        q1, b3, a2, b2, a3 = after((q1, b3, a2, b2, a3), forms0)
+        q2, q3 = second_side(a2), second_side(a3)
+        forms1 = prepare([part1, a1, b1, q1], column[None], matrix)
+        far1 = other_core(after(forms1, far0))
+
+        q2, q3 = after((q2, q3), forms1)
+        forms3 = prepare([part3, a3, b3, q3], column[None], matrix)
+        far3 = other_core(after(forms3, far1))
+        forms2 = prepare([part2, a2, b2, q2], column[None], matrix)
+        far2 = other_core(after(forms2, far3))
+        amps = prepare_amps(own, blocks_here, jnp.asarray(amp_matrix()))
+        held = [forms0, far0, forms1, far1, forms2, far2, forms3, far3]
     else:
+        parts = [mine[0]] + [around(mine[by], by) for by in range(1, levels)]
         tiles = amplitudes.reshape(blocks_here, pairs, TV, TV).transpose(0, 3, 2, 1)
         tiles = jnp.pad(tiles, ((0, 0), (0, 0), (0, PAD - TV), (0, 0))).reshape(blocks_here, ROWS, pairs)
-        same_core = [[2 * z + k for z in range(levels)] for k in range(2)]
-        amps = lax.all_gather(tiles, "task", axis=0, axis_index_groups=same_core)
-        amps = amps[(level - jnp.arange(levels)) % levels].reshape(levels * blocks_here, ROWS, pairs)
+        amps = lax.all_gather(tiles, "task", axis=0, tiled=True, axis_index_groups=same_core)
         held = lax.all_gather(jnp.stack(parts), "pair", axis=2, tiled=True)
         held = [jnp.stack([held, other_core(held)], axis=1).reshape(total, depth * pair_count, -1)]
     amps = (amps, other_core(amps))

time: 150 us -> 161 us (1.073)
  waiting for transfers between devices: 51 us -> 61.8 us
  starting transfers between devices: 35.5 us -> 27.4 us
  local copies, waits for them, and re-layouts: 6.54 us -> 14.5 us
    all_to_all x0 -> x1, waiting for transfers between devices: none -> 22.7 us  [per_device(): lax.all_to_all(own, 'task', split_axis=0, concat_axis=0, axis_index_group...]
    ppermute x9 -> x6, waiting for transfers between devices: 40.1 us -> 19 us  [around(): lax.ppermute(x, 'task', [(c, (c + 2 * by) % task_count) for c in range(ta...]
    ppermute x9 -> x6, starting transfers between devices: 20.6 us -> 8.23 us  [around(): lax.ppermute(x, 'task', [(c, (c + 2 * by) % task_count) for c in range(ta...]
    ppermute x12, waiting for transfers between devices: 7.6 us -> 16.7 us  [the longest x8 16.7 us: per_device(): second_side = lambda x: lax.ppermute(x, ('pair', 'task'), sides[1])]
    unnamed x19 -> x47, local copies, waits for them, and re-layouts: 5.23 us -> 12 us
    all_to_all x0 -> x1, starting transfers between devices: none -> 4.86 us  [per_device(): lax.all_to_all(own, 'task', split_axis=0, concat_axis=0, axis_index_group...]
    pallas_call x4, Pallas kernels: 13.8 us -> 11.4 us  [prepare(): pl.pallas_call(prepare_kernel, out_shape=jax.ShapeDtypeStruct((count, mat...]
    pallas_call x1, Pallas kernels: 1.44 us -> 3.47 us  [prepare_amps(): pl.pallas_call(amp_kernel, out_shape=jax.ShapeDtypeStruct((levels * block...]
  transfers between devices with their start and end apart: 26 -> 24, of which waited for: 10 -> 12; matrix products, arithmetic and copies ran while one was open for 0% -> 0% of each run, Pallas kernels for 31% -> 27%
where the time goes in v6:
time: 161 us; the launch traced here: 160 us
  waiting for transfers between devices  61.8 us (38%)
  Pallas kernels  56.2 us (35%)
  starting transfers between devices  27.4 us (17%)
  local copies, waits for them, and re-layouts  14.5 us (9%)
    pallas_call x4, Pallas kernels, ladders(): pl.pallas_call(functools.partial(ladder_kernel, find, made, len(tiles)),...  41.4 us
    all_to_all x1, waiting for transfers between devices, per_device(): lax.all_to_all(own, 'task', split_axis=0, concat_axis=0, axis_index_group...  22.7 us
    ppermute x6, waiting for transfers between devices, around(): lax.ppermute(x, 'task', [(c, (c + 2 * by) % task_count) for c in range(ta...  19 us
    ppermute x8, waiting for transfers between devices, per_device(): second_side = lambda x: lax.ppermute(x, ('pair', 'task'), sides[1])  16.7 us
    unnamed x47, local copies, waits for them, and re-layouts  12 us
    pallas_call x4, Pallas kernels, prepare(): pl.pallas_call(prepare_kernel, out_shape=jax.ShapeDtypeStruct((count, mat...  11.4 us
    ppermute x8, starting transfers between devices, per_device(): second_side = lambda x: lax.ppermute(x, ('pair', 'task'), sides[1])  9.24 us
    ppermute x6, starting transfers between devices, around(): lax.ppermute(x, 'task', [(c, (c + 2 * by) % task_count) for c in range(ta...  8.23 us
  transfers between devices with their start and end apart: 24, of which 12 were waited for; matrix products, arithmetic and copies ran while one was open for 0% of the time, Pallas kernels for 27%

profile of v6, /device:TPU:0, one launch (start us, length us, event | category | flops | bytes accessed | tf_op | source)
XLA Modules:
  0.0 160.4 jit_solution(6480982476180214054)
XLA Ops:
  0.0 3.4 %copy.23 = bf16[2,384,625]{2,1,0:T(8,128)(2,1)S(1)} copy(bf16[2,384,625]{1,0,2:T(2,128)(2,1)} %param.8) | data formatting | bytes 1920000 | tf_op args[0]
  3.4 0.0 copy-start.13
  3.4 0.1 dynamic-slice_bitcast_fusion
  3.5 5.1 %collective-permute-start.3 = (bf16[2,96,625]{2,1,0:T(8,128)(2,1)S(1)}, bf16[2,96,625]{2,1,0:T(8,128)(2,1)S(1)}, u32[]{:S(2)}, u32[]{:S(2)}) collective-permute-start(bf16[2,96,625]{2,1,0:T(8,128)(2,1)S(1)} %get-tuple-element.52), channel_id=1, source_target_pairs={{0,6},{1,7},{2,0},{3,1},{4,2},{5,3},{6,4},{7,5},{8,14},{9,15},{10,... | collective-permute-start | bytes 720008 | tf_op jit(solution)/shard_map/ppermute | solution.py:298
  8.7 0.0 collective-permute-start.2
  8.7 1.5 collective-permute-start.1
  10.2 1.5 collective-permute-start
  11.7 3.3 %collective-permute-done.3.refs_0_ = bf16[2,96,625]{2,1,0:T(8,128)(2,1)S(1)} collective-permute-done((bf16[2,96,625]{2,1,0:T(8,128)(2,1)S(1)}, bf16[2,96,625]{2,1,0:T(8,128)(2,1)S(1)}, u32[]{:S(2)}, u32[]{:S(2)}) %collective-permute-start.3) | collective-permute-done | bytes 240032 | tf_op jit(solution)/shard_map/ppermute | solution.py:298
  15.0 5.0 %collective-permute-done.2.refs_0_ = bf16[2,96,625]{2,1,0:T(8,128)(2,1)S(1)} collective-permute-done((bf16[2,96,625]{2,1,0:T(8,128)(2,1)S(1)}, bf16[2,96,625]{2,1,0:T(8,128)(2,1)S(1)}, u32[]{:S(2)}, u32[]{:S(2)}) %collective-permute-start.2) | collective-permute-done | bytes 240032 | tf_op jit(solution)/shard_map/ppermute | solution.py:298
  20.0 0.0 collective-permute-done.refs_1_
  20.0 0.7 collective-permute-start.8
  20.8 1.5 collective-permute-start.4
  22.3 1.5 collective-permute-start.7
  23.8 0.5 collective-permute-start.6
  24.3 0.5 collective-permute-start.5
  24.8 0.3 pad
  25.1 7.9 %collective-permute-done.8.refs_0_ = bf16[2,96,625]{2,1,0:T(8,128)(2,1)S(1)} collective-permute-done((bf16[2,96,625]{2,1,0:T(8,128)(2,1)S(1)}, bf16[2,96,625]{2,1,0:T(8,128)(2,1)S(1)}, u32[]{:S(2)}, u32[]{:S(2)}) %collective-permute-start.8) | collective-permute-done | bytes 240032 | tf_op jit(solution)/shard_map/ppermute | solution.py:298
  33.0 0.0 collective-permute-done.7.refs_1_
  33.0 0.4 collective-permute-done.6.refs_2_
  33.5 1.1 broadcast_in_dim.5
  34.6 2.6 %shard_map.82.refs_0_ = bf16[2,1600,384]{2,1,0:T(8,128)(2,1)S(1)} custom-call(s32[1]{0:T(128)} %bitcast.column_ref, bf16[2,96,625]{2,1,0:T(8,128)(2,1)S(1)} %get-tuple-element.28.refs_0_, bf16[2,96,625]{2,1,0:T(8,128)(2,1)S(1)} %collective-permute-done.refs_1_, bf16[2,96,625]{2,1,0:T(8,128)(2,1)S(1)} %collective-permute-done.1.refs_2_, ...), custom_call_target="tpu_custom_call" | custom-call | flops 1536000000 | bytes 3417600 | tf_op jit(solution)/shard_map/pallas_call | solution.py:77
  37.3 0.0 copy-start.14
  37.3 0.1 collective-permute-start.9
  37.4 1.6 collective-permute-start.10
  39.0 0.5 collective-permute-start.11
  39.5 1.5 collective-permute-start.13
  41.0 1.1 collective-permute-start.12
  42.1 2.4 %collective-permute-done.10.refs_3_ = bf16[2,96,625]{2,1,0:T(8,128)(2,1)S(1)} collective-permute-done((bf16[2,96,625]{2,1,0:T(8,128)(2,1)S(1)}, bf16[2,96,625]{2,1,0:T(8,128)(2,1)S(1)}, u32[]{:S(2)}, u32[]{:S(2)}) %collective-permute-start.10) | collective-permute-done | bytes 240032 | tf_op jit(solution)/shard_map/ppermute | solution.py:309
  44.5 4.4 %collective-permute-done.11.refs_2_ = bf16[2,96,625]{2,1,0:T(8,128)(2,1)S(1)} collective-permute-done((bf16[2,96,625]{2,1,0:T(8,128)(2,1)S(1)}, bf16[2,96,625]{2,1,0:T(8,128)(2,1)S(1)}, u32[]{:S(2)}, u32[]{:S(2)}) %collective-permute-start.11) | collective-permute-done | bytes 240032 | tf_op jit(solution)/shard_map/ppermute | solution.py:309
  48.9 2.6 %collective-permute-done.13.refs_2_ = bf16[2,96,625]{2,1,0:T(8,128)(2,1)S(1)} collective-permute-done((bf16[2,96,625]{2,1,0:T(8,128)(2,1)S(1)}, bf16[2,96,625]{2,1,0:T(8,128)(2,1)S(1)}, u32[]{:S(2)}, u32[]{:S(2)}) %collective-permute-start.13) | collective-permute-done | bytes 240032 | tf_op jit(solution)/shard_map/ppermute | solution.py:309
  51.5 2.7 %shard_map.83.refs_2_ = bf16[2,1600,384]{2,1,0:T(8,128)(2,1)S(1)} custom-call(s32[1]{0:T(128)} %bitcast.column_ref, bf16[2,96,625]{2,1,0:T(8,128)(2,1)S(1)} %collective-permute-done.2.refs_0_, bf16[2,96,625]{2,1,0:T(8,128)(2,1)S(1)} %collective-permute-done.5.refs_1_, bf16[2,96,625]{2,1,0:T(8,128)(2,1)S(1)} %collective-permute-done.6.refs_2_, ...), custom_call_target="tpu_custom_call" | custom-call | flops 1536000000 | bytes 3417600 | tf_op jit(solution)/shard_map/pallas_call | solution.py:77
  54.3 0.1 collective-permute-start.14
  54.3 1.6 collective-permute-start.15
  55.9 0.5 collective-permute-start.16
  56.4 4.2 %collective-permute-done.15.refs_3_ = bf16[2,96,625]{2,1,0:T(8,128)(2,1)S(1)} collective-permute-done((bf16[2,96,625]{2,1,0:T(8,128)(2,1)S(1)}, bf16[2,96,625]{2,1,0:T(8,128)(2,1)S(1)}, u32[]{:S(2)}, u32[]{:S(2)}) %collective-permute-start.15) | collective-permute-done | bytes 240032 | tf_op jit(solution)/shard_map/ppermute | solution.py:309
  60.6 2.6 %collective-permute-done.16.refs_3_ = bf16[2,96,625]{2,1,0:T(8,128)(2,1)S(1)} collective-permute-done((bf16[2,96,625]{2,1,0:T(8,128)(2,1)S(1)}, bf16[2,96,625]{2,1,0:T(8,128)(2,1)S(1)}, u32[]{:S(2)}, u32[]{:S(2)}) %collective-permute-start.16) | collective-permute-done | bytes 240032 | tf_op jit(solution)/shard_map/ppermute | solution.py:309
  63.2 2.6 %shard_map.85.refs_6_ = bf16[2,1600,384]{2,1,0:T(8,128)(2,1)S(1)} custom-call(s32[1]{0:T(128)} %bitcast.column_ref, bf16[2,96,625]{2,1,0:T(8,128)(2,1)S(1)} %collective-permute-done.3.refs_0_, bf16[2,96,625]{2,1,0:T(8,128)(2,1)S(1)} %collective-permute-done.7.refs_1_, bf16[2,96,625]{2,1,0:T(8,128)(2,1)S(1)} %collective-permute-done.11.refs_2_, ...), custom_call_target="tpu_custom_call" | custom-call | flops 1536000000 | bytes 3417600 | tf_op jit(solution)/shard_map/pallas_call | solution.py:77
  65.9 1.5 copy-done.16
  67.5 4.9 %all-to-all-start = ((bf16[4,625,256]{2,1,0:T(8,128)(2,1)}), bf16[4,625,256]{2,1,0:T(8,128)(2,1)}, u32[]{:S(2)}, u32[]{:S(2)}) async-start(bf16[4,625,256]{2,1,0:T(8,128)(2,1)} %broadcast_in_dim.5), calls=%async_computation | async-start | bytes 2588672 | tf_op jit(solution)/shard_map/all_to_all | solution.py:319
  72.3 0.9 copy-done.6
  73.3 0.9 copy-done.8
  74.2 0.9 copy-done.10
  75.2 0.9 copy-done.12
  76.1 1.6 copy-done.15
  77.7 3.4 %shard_map.84.refs_4_ = bf16[2,1600,384]{2,1,0:T(8,128)(2,1)} custom-call(s32[1]{0:T(128)} %bitcast.column_ref, bf16[2,96,625]{2,1,0:T(8,128)(2,1)S(1)} %copy-done.6, bf16[2,96,625]{2,1,0:T(8,128)(2,1)S(1)} %copy-done.10, bf16[2,96,625]{2,1,0:T(8,128)(2,1)S(1)} %copy-done.8, bf16[2,96,625]{2,1,0:T(8,128)(2,1)S(1)} %copy-done.12, bf16[1600,625]{1,0:T(8,128)(2,1)S(1)} %copy-done.15), custom_call_target="tpu_custom_call" | custom-call | flops 1536000000 | bytes 3417600 | tf_op jit(solution)/shard_map/pallas_call | solution.py:77
  81.1 0.3 collective-permute-start.18
  81.4 22.7 %all-to-all-done.tiles_ref = bf16[4,625,256]{2,1,0:T(8,128)(2,1)} async-done(((bf16[4,625,256]{2,1,0:T(8,128)(2,1)}), bf16[4,625,256]{2,1,0:T(8,128)(2,1)}, u32[]{:S(2)}, u32[]{:S(2)}) %all-to-all-start) | async-done | bytes 1280032 | tf_op jit(solution)/shard_map/all_to_all | solution.py:319
  104.1 3.5 %shard_map.86.refs_8_ = bf16[8,800,128]{2,1,0:T(8,128)(2,1)S(1)} custom-call(bf16[800,625]{1,0:T(8,128)(2,1)S(1)} %copy-done.4, bf16[4,625,256]{2,1,0:T(8,128)(2,1)} %all-to-all-done.tiles_ref), custom_call_target="tpu_custom_call" | custom-call | flops 1024000000 | bytes 2560000 | tf_op jit(solution)/shard_map/pallas_call | solution.py:106
  107.6 0.1 collective-permute-start.19
  107.7 0.1 copy.24.owners_ref
  107.8 0.1 copy.25.local_ref
  107.8 3.3 %collective-permute-done.19.refs_9_ = bf16[8,800,128]{2,1,0:T(8,128)(2,1)S(1)} collective-permute-done((bf16[8,800,128]{2,1,0:T(8,128)(2,1)S(1)}, bf16[8,800,128]{2,1,0:T(8,128)(2,1)S(1)}, u32[]{:S(2)}, u32[]{:S(2)}) %collective-permute-start.19) | collective-permute-done | bytes 1638432 | tf_op jit(solution)/shard_map/ppermute | solution.py:295
  111.2 1.3 copy-done.3
  112.4 10.3 %shard_map.88 = bf16[1,2,625,128]{3,2,1,0:T(8,128)(2,1)S(1)} custom-call(s32[1]{0:T(128)} %bitcast.column_ref, s32[32,3]{1,0:T(8,128)S(1)} %copy.24.owners_ref, s32[32,4]{1,0:T(8,128)S(1)} %copy.25.local_ref, bf16[2,1600,384]{2,1,0:T(8,128)(2,1)} %copy-done, bf16[2,1600,384]{2,1,0:T(8,128)(2,1)} %collective-permute-done.9.refs_1_, ...), custom_call_target="tpu_custom_call" | custom-call | flops 2936012800 | bytes 6553600 | tf_op jit(solution)/shard_map/pallas_call | solution.py:260
  122.8 1.7 %collective-permute-start.21 = (bf16[2,625,128]{2,1,0:T(8,128)(2,1)S(1)}, bf16[2,625,128]{2,1,0:T(8,128)(2,1)S(1)}, u32[]{:S(2)}, u32[]{:S(2)}) collective-permute-start(bf16[2,625,128]{2,1,0:T(8,128)(2,1)S(1)} %bitcast.24), channel_id=1, source_target_pairs={{0,6},{1,7},{2,0},{3,1},{4,2},{5,3},{6,4},{7,5},{8,14},{9,15},{10,... | collective-permute-start | bytes 960008 | tf_op jit(solution)/shard_map/ppermute | solution.py:298
  124.5 10.3 %shard_map.87 = bf16[1,2,625,128]{3,2,1,0:T(8,128)(2,1)S(1)} custom-call(s32[1]{0:T(128)} %bitcast.column_ref, s32[32,3]{1,0:T(8,128)S(1)} %copy.24.owners_ref, s32[32,4]{1,0:T(8,128)S(1)} %copy.25.local_ref, bf16[2,1600,384]{2,1,0:T(8,128)(2,1)} %copy-done, bf16[2,1600,384]{2,1,0:T(8,128)(2,1)} %collective-permute-done.9.refs_1_, ...), custom_call_target="tpu_custom_call" | custom-call | flops 2936012800 | bytes 6553600 | tf_op jit(solution)/shard_map/pallas_call | solution.py:260
  134.8 0.1 collective-permute-start.20
  134.9 10.3 %shard_map.89 = bf16[1,2,625,128]{3,2,1,0:T(8,128)(2,1)S(1)} custom-call(s32[1]{0:T(128)} %bitcast.column_ref, s32[32,3]{1,0:T(8,128)S(1)} %copy.24.owners_ref, s32[32,4]{1,0:T(8,128)S(1)} %copy.25.local_ref, bf16[2,1600,384]{2,1,0:T(8,128)(2,1)} %copy-done, bf16[2,1600,384]{2,1,0:T(8,128)(2,1)} %collective-permute-done.9.refs_1_, ...), custom_call_target="tpu_custom_call" | custom-call | flops 2936012800 | bytes 6553600 | tf_op jit(solution)/shard_map/pallas_call | solution.py:260
  145.2 0.0 copy-start.17
  145.3 0.6 collective-permute-start.22
  145.9 10.3 %shard_map.90 = bf16[1,2,625,128]{3,2,1,0:T(8,128)(2,1)S(1)} custom-call(s32[1]{0:T(128)} %bitcast.column_ref, s32[32,3]{1,0:T(8,128)S(1)} %copy.24.owners_ref, s32[32,4]{1,0:T(8,128)S(1)} %copy.25.local_ref, bf16[2,1600,384]{2,1,0:T(8,128)(2,1)} %copy-done, bf16[2,1600,384]{2,1,0:T(8,128)(2,1)} %collective-permute-done.9.refs_1_, ...), custom_call_target="tpu_custom_call" | custom-call | flops 2936012800 | bytes 6553600 | tf_op jit(solution)/shard_map/pallas_call | solution.py:260
  156.2 2.8 %collective-permute-done.20 = bf16[2,625,128]{2,1,0:T(8,128)(2,1)S(1)} collective-permute-done((bf16[2,625,128]{2,1,0:T(8,128)(2,1)S(1)}, bf16[2,625,128]{2,1,0:T(8,128)(2,1)S(1)}, u32[]{:S(2)}, u32[]{:S(2)}) %collective-permute-start.20) | collective-permute-done | bytes 320032 | tf_op jit(solution)/shard_map/ppermute | solution.py:298
  159.0 0.2 fusion.1
  159.2 1.2 copy.33
  (44 shorter events, 0.1 us)
Async XLA Ops:
  0.0 24.8 %copy-start.18 = (bf16[2,128,625]{1,0,2:T(2,128)(2,1)S(1)}, bf16[2,128,625]{1,0,2:T(2,128)(2,1)}, u32[]{:S(2)}) copy-start(bf16[2,128,625]{1,0,2:T(2,128)(2,1)} %param.9) | copy-start | bytes 960004
  3.4 31.2 %copy-start.13 = (bf16[1600,625]{1,0:T(8,128)(2,1)S(1)}, bf16[1600,625]{1,0:T(8,128)(2,1)}, u32[]{:S(2)}) copy-start(bf16[1600,625]{1,0:T(8,128)(2,1)} %constant.61.clone.refs_4_) | copy-start | bytes 6000004
  3.5 11.5 %collective-permute-start.3 = (bf16[2,96,625]{2,1,0:T(8,128)(2,1)S(1)}, bf16[2,96,625]{2,1,0:T(8,128)(2,1)S(1)}, u32[]{:S(2)}, u32[]{:S(2)}) collective-permute-start(bf16[2,96,625]{2,1,0:T(8,128)(2,1)S(1)} %get-tuple-element.52), channel_id=1, source_target_pairs={{0,6},{1,7},{2,0},{3,1},{4,2},{5,3},{6,4},{7,5},{8,14},{9,15},{10,... | collective-permute-start | bytes 720008 | tf_op jit(solution)/shard_map/ppermute | solution.py:298
  8.7 11.4 %collective-permute-start.2 = (bf16[2,96,625]{2,1,0:T(8,128)(2,1)S(1)}, bf16[2,96,625]{2,1,0:T(8,128)(2,1)S(1)}, u32[]{:S(2)}, u32[]{:S(2)}) collective-permute-start(bf16[2,96,625]{2,1,0:T(8,128)(2,1)S(1)} %get-tuple-element.53), channel_id=1, source_target_pairs={{0,2},{1,3},{2,4},{3,5},{4,6},{5,7},{6,0},{7,1},{8,10},{9,11},{10,... | collective-permute-start | bytes 720008 | tf_op jit(solution)/shard_map/ppermute | solution.py:298
  8.7 11.4 %collective-permute-start.1 = (bf16[2,96,625]{2,1,0:T(8,128)(2,1)S(1)}, bf16[2,96,625]{2,1,0:T(8,128)(2,1)S(1)}, u32[]{:S(2)}, u32[]{:S(2)}) collective-permute-start(bf16[2,96,625]{2,1,0:T(8,128)(2,1)S(1)} %get-tuple-element.28.refs_0_), channel_id=1, source_target_pairs={{0,16},{1,9},{2,18},{3,11},{4,20},{5,13},{6,22},{7,15},{8,24},{9,1... | collective-permute-start | bytes 720008 | tf_op jit(solution)/shard_map/ppermute | solution.py:309
  10.2 9.9 %collective-permute-start = (bf16[2,96,625]{2,1,0:T(8,128)(2,1)S(1)}, bf16[2,96,625]{2,1,0:T(8,128)(2,1)S(1)}, u32[]{:S(2)}, u32[]{:S(2)}) collective-permute-start(bf16[2,96,625]{2,1,0:T(8,128)(2,1)S(1)} %get-tuple-element.28.refs_0_), channel_id=1, source_target_pairs={{0,8},{1,17},{2,10},{3,19},{4,12},{5,21},{6,14},{7,23},{8,0},{9,25... | collective-permute-start | bytes 720008 | tf_op jit(solution)/shard_map/ppermute | solution.py:308
  20.0 13.0 %collective-permute-start.8 = (bf16[2,96,625]{2,1,0:T(8,128)(2,1)S(1)}, bf16[2,96,625]{2,1,0:T(8,128)(2,1)S(1)}, u32[]{:S(2)}, u32[]{:S(2)}) collective-permute-start(bf16[2,96,625]{2,1,0:T(8,128)(2,1)S(1)} %get-tuple-element.33), channel_id=1, source_target_pairs={{0,4},{1,5},{2,6},{3,7},{4,0},{5,1},{6,2},{7,3},{8,12},{9,13},{10,... | collective-permute-start | bytes 720008 | tf_op jit(solution)/shard_map/ppermute | solution.py:298
  20.8 12.3 %collective-permute-start.4 = (bf16[2,96,625]{2,1,0:T(8,128)(2,1)S(1)}, bf16[2,96,625]{2,1,0:T(8,128)(2,1)S(1)}, u32[]{:S(2)}, u32[]{:S(2)}) collective-permute-start(bf16[2,96,625]{2,1,0:T(8,128)(2,1)S(1)} %collective-permute-done.refs_1_), channel_id=1, source_target_pairs={{0,16},{1,9},{2,18},{3,11},{4,20},{5,13},{6,22},{7,15},{8,24},{9,1... | collective-permute-start | bytes 720008 | tf_op jit(solution)/shard_map/ppermute | solution.py:309
  22.3 10.7 %collective-permute-start.7 = (bf16[2,96,625]{2,1,0:T(8,128)(2,1)S(1)}, bf16[2,96,625]{2,1,0:T(8,128)(2,1)S(1)}, u32[]{:S(2)}, u32[]{:S(2)}) collective-permute-start(bf16[2,96,625]{2,1,0:T(8,128)(2,1)S(1)} %collective-permute-done.3.refs_0_), channel_id=1, source_target_pairs={{0,8},{1,17},{2,10},{3,19},{4,12},{5,21},{6,14},{7,23},{8,0},{9,25... | collective-permute-start | bytes 720008 | tf_op jit(solution)/shard_map/ppermute | solution.py:308
  23.8 9.7 %collective-permute-start.6 = (bf16[2,96,625]{2,1,0:T(8,128)(2,1)S(1)}, bf16[2,96,625]{2,1,0:T(8,128)(2,1)S(1)}, u32[]{:S(2)}, u32[]{:S(2)}) collective-permute-start(bf16[2,96,625]{2,1,0:T(8,128)(2,1)S(1)} %collective-permute-done.2.refs_0_), channel_id=1, source_target_pairs={{0,16},{1,9},{2,18},{3,11},{4,20},{5,13},{6,22},{7,15},{8,24},{9,1... | collective-permute-start | bytes 720008 | tf_op jit(solution)/shard_map/ppermute | solution.py:309
  24.3 9.2 %collective-permute-start.5 = (bf16[2,96,625]{2,1,0:T(8,128)(2,1)S(1)}, bf16[2,96,625]{2,1,0:T(8,128)(2,1)S(1)}, u32[]{:S(2)}, u32[]{:S(2)}) collective-permute-start(bf16[2,96,625]{2,1,0:T(8,128)(2,1)S(1)} %collective-permute-done.2.refs_0_), channel_id=1, source_target_pairs={{0,8},{1,17},{2,10},{3,19},{4,12},{5,21},{6,14},{7,23},{8,0},{9,25... | collective-permute-start | bytes 720008 | tf_op jit(solution)/shard_map/ppermute | solution.py:308
  33.0 8.0 %copy-start.5 = (bf16[2,96,625]{2,1,0:T(8,128)(2,1)}, bf16[2,96,625]{2,1,0:T(8,128)(2,1)S(1)}, u32[]{:S(2)}) copy-start(bf16[2,96,625]{2,1,0:T(8,128)(2,1)S(1)} %collective-permute-done.8.refs_0_) | copy-start | bytes 720004
  37.3 16.9 %copy-start = (bf16[2,1600,384]{2,1,0:T(8,128)(2,1)}, bf16[2,1600,384]{2,1,0:T(8,128)(2,1)S(1)}, u32[]{:S(2)}) copy-start(bf16[2,1600,384]{2,1,0:T(8,128)(2,1)S(1)} %shard_map.82.refs_0_) | copy-start | bytes 7372804
  37.3 26.0 %copy-start.14 = (bf16[1600,625]{1,0:T(8,128)(2,1)S(1)}, bf16[1600,625]{1,0:T(8,128)(2,1)}, u32[]{:S(2)}) copy-start(bf16[1600,625]{1,0:T(8,128)(2,1)} %constant.61.clone.refs_4_) | copy-start | bytes 6000004
  37.3 16.9 %collective-permute-start.9 = (bf16[2,1600,384]{2,1,0:T(8,128)(2,1)S(1)}, bf16[2,1600,384]{2,1,0:T(8,128)(2,1)}, u32[]{:S(2)}, u32[]{:S(2)}) collective-permute-start(bf16[2,1600,384]{2,1,0:T(8,128)(2,1)S(1)} %shard_map.82.refs_0_), channel_id=1, source_target_pairs={{0,1},{1,0},{2,3},{3,2},{4,5},{5,4},{6,7},{7,6},{8,9},{9,8},{10,11... | collective-permute-start | bytes 7372808 | tf_op jit(solution)/shard_map/ppermute | solution.py:295
  37.4 7.1 %collective-permute-start.10 = (bf16[2,96,625]{2,1,0:T(8,128)(2,1)S(1)}, bf16[2,96,625]{2,1,0:T(8,128)(2,1)S(1)}, u32[]{:S(2)}, u32[]{:S(2)}) collective-permute-start(bf16[2,96,625]{2,1,0:T(8,128)(2,1)S(1)} %collective-permute-done.5.refs_1_), channel_id=1, source_target_pairs={{0,16},{1,9},{2,18},{3,11},{4,20},{5,13},{6,22},{7,15},{8,24},{9,1... | collective-permute-start | bytes 720008 | tf_op jit(solution)/shard_map/ppermute | solution.py:309
  39.0 10.0 %collective-permute-start.11 = (bf16[2,96,625]{2,1,0:T(8,128)(2,1)S(1)}, bf16[2,96,625]{2,1,0:T(8,128)(2,1)S(1)}, u32[]{:S(2)}, u32[]{:S(2)}) collective-permute-start(bf16[2,96,625]{2,1,0:T(8,128)(2,1)S(1)} %collective-permute-done.3.refs_0_), channel_id=1, source_target_pairs={{0,16},{1,9},{2,18},{3,11},{4,20},{5,13},{6,22},{7,15},{8,24},{9,1... | collective-permute-start | bytes 720008 | tf_op jit(solution)/shard_map/ppermute | solution.py:309
  39.5 12.1 %collective-permute-start.13 = (bf16[2,96,625]{2,1,0:T(8,128)(2,1)S(1)}, bf16[2,96,625]{2,1,0:T(8,128)(2,1)S(1)}, u32[]{:S(2)}, u32[]{:S(2)}) collective-permute-start(bf16[2,96,625]{2,1,0:T(8,128)(2,1)S(1)} %collective-permute-done.8.refs_0_), channel_id=1, source_target_pairs={{0,16},{1,9},{2,18},{3,11},{4,20},{5,13},{6,22},{7,15},{8,24},{9,1... | collective-permute-start | bytes 720008 | tf_op jit(solution)/shard_map/ppermute | solution.py:309
  41.0 10.6 %collective-permute-start.12 = (bf16[2,96,625]{2,1,0:T(8,128)(2,1)S(1)}, bf16[2,96,625]{2,1,0:T(8,128)(2,1)S(1)}, u32[]{:S(2)}, u32[]{:S(2)}) collective-permute-start(bf16[2,96,625]{2,1,0:T(8,128)(2,1)S(1)} %collective-permute-done.8.refs_0_), channel_id=1, source_target_pairs={{0,8},{1,17},{2,10},{3,19},{4,12},{5,21},{6,14},{7,23},{8,0},{9,25... | collective-permute-start | bytes 720008 | tf_op jit(solution)/shard_map/ppermute | solution.py:308
  51.5 2.7 %copy-start.7 = (bf16[2,96,625]{2,1,0:T(8,128)(2,1)}, bf16[2,96,625]{2,1,0:T(8,128)(2,1)S(1)}, u32[]{:S(2)}) copy-start(bf16[2,96,625]{2,1,0:T(8,128)(2,1)S(1)} %collective-permute-done.13.refs_2_) | copy-start | bytes 720004
  51.5 2.8 %copy-start.9 = (bf16[2,96,625]{2,1,0:T(8,128)(2,1)}, bf16[2,96,625]{2,1,0:T(8,128)(2,1)S(1)}, u32[]{:S(2)}) copy-start(bf16[2,96,625]{2,1,0:T(8,128)(2,1)S(1)} %collective-permute-done.12.refs_1_) | copy-start | bytes 720004
  54.2 11.7 %copy-start.1 = (bf16[2,1600,384]{2,1,0:T(8,128)(2,1)}, bf16[2,1600,384]{2,1,0:T(8,128)(2,1)S(1)}, u32[]{:S(2)}) copy-start(bf16[2,1600,384]{2,1,0:T(8,128)(2,1)S(1)} %shard_map.83.refs_2_) | copy-start | bytes 7372804
  54.3 11.7 %collective-permute-start.14 = (bf16[2,1600,384]{2,1,0:T(8,128)(2,1)S(1)}, bf16[2,1600,384]{2,1,0:T(8,128)(2,1)S(1)}, u32[]{:S(2)}, u32[]{:S(2)}) collective-permute-start(bf16[2,1600,384]{2,1,0:T(8,128)(2,1)S(1)} %shard_map.83.refs_2_), channel_id=1, source_target_pairs={{0,1},{1,0},{2,3},{3,2},{4,5},{5,4},{6,7},{7,6},{8,9},{9,8},{10,11... | collective-permute-start | bytes 7372808 | tf_op jit(solution)/shard_map/ppermute | solution.py:295
  54.3 6.3 %collective-permute-start.15 = (bf16[2,96,625]{2,1,0:T(8,128)(2,1)S(1)}, bf16[2,96,625]{2,1,0:T(8,128)(2,1)S(1)}, u32[]{:S(2)}, u32[]{:S(2)}) collective-permute-start(bf16[2,96,625]{2,1,0:T(8,128)(2,1)S(1)} %collective-permute-done.12.refs_1_), channel_id=1, source_target_pairs={{0,16},{1,9},{2,18},{3,11},{4,20},{5,13},{6,22},{7,15},{8,24},{9,1... | collective-permute-start | bytes 720008 | tf_op jit(solution)/shard_map/ppermute | solution.py:309
  55.9 7.3 %collective-permute-start.16 = (bf16[2,96,625]{2,1,0:T(8,128)(2,1)S(1)}, bf16[2,96,625]{2,1,0:T(8,128)(2,1)S(1)}, u32[]{:S(2)}, u32[]{:S(2)}) collective-permute-start(bf16[2,96,625]{2,1,0:T(8,128)(2,1)S(1)} %collective-permute-done.7.refs_1_), channel_id=1, source_target_pairs={{0,16},{1,9},{2,18},{3,11},{4,20},{5,13},{6,22},{7,15},{8,24},{9,1... | collective-permute-start | bytes 720008 | tf_op jit(solution)/shard_map/ppermute | solution.py:309
  60.6 5.3 %copy-start.11 = (bf16[2,96,625]{2,1,0:T(8,128)(2,1)}, bf16[2,96,625]{2,1,0:T(8,128)(2,1)S(1)}, u32[]{:S(2)}) copy-start(bf16[2,96,625]{2,1,0:T(8,128)(2,1)S(1)} %collective-permute-done.15.refs_3_) | copy-start | bytes 720004
  65.9 15.2 %copy-start.2 = (bf16[2,1600,384]{2,1,0:T(8,128)(2,1)}, bf16[2,1600,384]{2,1,0:T(8,128)(2,1)S(1)}, u32[]{:S(2)}) copy-start(bf16[2,1600,384]{2,1,0:T(8,128)(2,1)S(1)} %shard_map.85.refs_6_) | copy-start | bytes 7372804
  65.9 1.5 copy-start.16
  67.5 13.7 %collective-permute-start.17 = (bf16[2,1600,384]{2,1,0:T(8,128)(2,1)S(1)}, bf16[2,1600,384]{2,1,0:T(8,128)(2,1)}, u32[]{:S(2)}, u32[]{:S(2)}) collective-permute-start(bf16[2,1600,384]{2,1,0:T(8,128)(2,1)S(1)} %shard_map.85.refs_6_), channel_id=1, source_target_pairs={{0,1},{1,0},{2,3},{3,2},{4,5},{5,4},{6,7},{7,6},{8,9},{9,8},{10,11... | collective-permute-start | bytes 7372808 | tf_op jit(solution)/shard_map/ppermute | solution.py:295
  67.5 36.6 %all-to-all-start = ((bf16[4,625,256]{2,1,0:T(8,128)(2,1)}), bf16[4,625,256]{2,1,0:T(8,128)(2,1)}, u32[]{:S(2)}, u32[]{:S(2)}) async-start(bf16[4,625,256]{2,1,0:T(8,128)(2,1)} %broadcast_in_dim.5), calls=%async_computation | async-start | bytes 2588672 | tf_op jit(solution)/shard_map/all_to_all | solution.py:319
  72.3 0.9 copy-start.6
  73.3 0.9 copy-start.8
  74.2 0.9 copy-start.10
  75.2 0.9 copy-start.12
  76.1 1.6 copy-start.15
  77.7 26.4 %copy-start.4 = (bf16[800,625]{1,0:T(8,128)(2,1)S(1)}, bf16[800,625]{1,0:T(8,128)(2,1)}, u32[]{:S(2)}) copy-start(bf16[800,625]{1,0:T(8,128)(2,1)} %constant.63.clone.matrix_ref) | copy-start | bytes 3000004
  81.1 26.5 %copy-start.19 = (s32[32,3]{0,1:T(4,128)S(1)}, s32[32,3]{0,1:T(4,128)}, u32[]{:S(2)}) copy-start(s32[32,3]{0,1:T(4,128)} %param.11) | copy-start | bytes 1156
  81.1 26.6 %copy-start.20 = (s32[32,4]{0,1:T(4,128)S(1)}, s32[32,4]{0,1:T(4,128)}, u32[]{:S(2)}) copy-start(s32[32,4]{0,1:T(4,128)} %param.12) | copy-start | bytes 1540
  81.1 30.0 %collective-permute-start.18 = (bf16[2,1600,384]{2,1,0:T(8,128)(2,1)}, bf16[2,1600,384]{2,1,0:T(8,128)(2,1)}, u32[]{:S(2)}, u32[]{:S(2)}) collective-permute-start(bf16[2,1600,384]{2,1,0:T(8,128)(2,1)} %shard_map.84.refs_4_), channel_id=1, source_target_pairs={{0,1},{1,0},{2,3},{3,2},{4,5},{5,4},{6,7},{7,6},{8,9},{9,8},{10,11... | collective-permute-start | bytes 7372808 | tf_op jit(solution)/shard_map/ppermute | solution.py:295
  107.6 3.6 %collective-permute-start.19 = (bf16[8,800,128]{2,1,0:T(8,128)(2,1)S(1)}, bf16[8,800,128]{2,1,0:T(8,128)(2,1)S(1)}, u32[]{:S(2)}, u32[]{:S(2)}) collective-permute-start(bf16[8,800,128]{2,1,0:T(8,128)(2,1)S(1)} %shard_map.86.refs_8_), channel_id=1, source_target_pairs={{0,1},{1,0},{2,3},{3,2},{4,5},{5,4},{6,7},{7,6},{8,9},{9,8},{10,11... | collective-permute-start | bytes 4915208 | tf_op jit(solution)/shard_map/ppermute | solution.py:295
  111.2 1.3 copy-start.3
  122.8 33.5 %collective-permute-start.21 = (bf16[2,625,128]{2,1,0:T(8,128)(2,1)S(1)}, bf16[2,625,128]{2,1,0:T(8,128)(2,1)S(1)}, u32[]{:S(2)}, u32[]{:S(2)}) collective-permute-start(bf16[2,625,128]{2,1,0:T(8,128)(2,1)S(1)} %bitcast.24), channel_id=1, source_target_pairs={{0,6},{1,7},{2,0},{3,1},{4,2},{5,3},{6,4},{7,5},{8,14},{9,15},{10,... | collective-permute-start | bytes 960008 | tf_op jit(solution)/shard_map/ppermute | solution.py:298
  134.8 24.2 %collective-permute-start.20 = (bf16[2,625,128]{2,1,0:T(8,128)(2,1)S(1)}, bf16[2,625,128]{2,1,0:T(8,128)(2,1)S(1)}, u32[]{:S(2)}, u32[]{:S(2)}) collective-permute-start(bf16[2,625,128]{2,1,0:T(8,128)(2,1)S(1)} %bitcast.25), channel_id=1, source_target_pairs={{0,4},{1,5},{2,6},{3,7},{4,0},{5,1},{6,2},{7,3},{8,12},{9,13},{10,... | collective-permute-start | bytes 960008 | tf_op jit(solution)/shard_map/ppermute | solution.py:298
  145.2 13.8 %copy-start.17 = (f32[2,128,625]{1,0,2:T(2,128)S(1)}, f32[2,128,625]{1,0,2:T(2,128)}, u32[]{:S(2)}) copy-start(f32[2,128,625]{1,0,2:T(2,128)} %param.10) | copy-start | bytes 1920004
  145.3 13.8 %collective-permute-start.22 = (bf16[2,625,128]{2,1,0:T(8,128)(2,1)S(1)}, bf16[2,625,128]{2,1,0:T(8,128)(2,1)S(1)}, u32[]{:S(2)}, u32[]{:S(2)}) collective-permute-start(bf16[2,625,128]{2,1,0:T(8,128)(2,1)S(1)} %bitcast.26), channel_id=1, source_target_pairs={{0,2},{1,3},{2,4},{3,5},{4,6},{5,7},{6,0},{7,1},{8,10},{9,11},{10,... | collective-permute-start | bytes 960008 | tf_op jit(solution)/shard_map/ppermute | solution.py:298

commit v7 on v6

--- a/solution.py
+++ b/solution.py
@@ -56,7 +56,7 @@
                 start = pl.multiple_of(m * depth + place * size, size)
                 all_ref[pl.ds(start, size), :] = ref[m]
 
-    wide = count if depth % LANES == 0 else 1
+    wide = 2 if depth % LANES == 0 and count % 2 == 0 else 1
     for first in range(0, count, wide):
         made = lax.dot_general(
             matrix_ref[...],
@@ -93,30 +93,26 @@
     )(column, *parts, matrix)
 
 
-def amp_kernel(matrix_ref, tiles_ref, out_ref):
-    pairs = out_ref.shape[2]
-    made = jnp.dot(matrix_ref[...], tiles_ref[0], preferred_element_type=F32).astype(BF)
-    for m in range(out_ref.shape[0]):
-        out_ref[m] = made[:, m * pairs : (m + 1) * pairs]
-
-
-def prepare_amps(tiles, blocks_here, matrix):
-    levels, entries, width = tiles.shape
-    pairs = width // blocks_here
+def amp_kernel(matrix_ref, *refs):
+    tile_refs, out_ref = refs[:-1], refs[-1]
+    blocks_here, pairs = out_ref.shape[0] // len(tile_refs), out_ref.shape[2]
+    for by, ref in enumerate(tile_refs):
+        made = jnp.dot(matrix_ref[...], ref[...], preferred_element_type=F32).astype(BF)
+        for m in range(blocks_here):
+            out_ref[by * blocks_here + m] = made[:, m * pairs : (m + 1) * pairs]
+
+
+def prepare_amps(parts, blocks_here, matrix):
+    levels, size = len(parts), parts[0].size
+    pairs = parts[0].shape[1] // blocks_here
     return pl.pallas_call(
         amp_kernel,
         out_shape=jax.ShapeDtypeStruct((levels * blocks_here, ROWS, pairs), BF),
-        grid=(levels,),
-        in_specs=[
-            pl.BlockSpec(matrix.shape, lambda i: (0, 0)),
-            pl.BlockSpec((1, entries, width), lambda i: (i, 0, 0)),
-        ],
-        out_specs=pl.BlockSpec((blocks_here, ROWS, pairs), lambda i: (i, 0, 0)),
         compiler_params=pltpu.CompilerParams(vmem_limit_bytes=VMEM_BYTES),
         cost_estimate=pl.CostEstimate(
-            flops=2 * tiles.size * ROWS, bytes_accessed=4 * tiles.size, transcendentals=0
-        ),
-    )(matrix, tiles)
+            flops=2 * levels * size * ROWS, bytes_accessed=4 * levels * size, transcendentals=0
+        ),
+    )(matrix, *parts)
 
 
 def turned(ref, groups, by):
@@ -234,11 +230,13 @@
 
         def factor(kind):
             below, far, m = place(kind)
-            return (below * 2 + far, m) if made else (0, (below * 2 + far) * blocks_here + m)
-
-        _, far, m = place(2)
-        amp = owners_ref[task, 2] // 2 * blocks_here + m
-        return {"task": task, "row": factor(0), "col": factor(1), "amp": (far, amp)}
+            if not made:
+                return 0, (below * 2 + far) * blocks_here + m
+            chunk = jnp.where(below == 3, 1, below)
+            return chunk * 2 + far, m + jnp.where(below == 3, blocks_here, 0)
+
+        below, far, m = place(2)
+        return {"task": task, "row": factor(0), "col": factor(1), "amp": (far, below * blocks_here + m)}
 
     anywhere = pl.BlockSpec(memory_space=pl.ANY)
     fixed = lambda shape: pl.BlockSpec(shape, lambda i, j, *tables: (0,) * len(shape))
@@ -307,37 +305,37 @@
         ]
         first_side = lambda x: lax.ppermute(x, ("pair", "task"), sides[0])
         second_side = lambda x: lax.ppermute(x, ("pair", "task"), sides[1])
+        made_forms = lambda *parts: prepare(parts, column[None], matrix)
         part0 = mine[0]
         a0, b0, part1, part3 = first_side(part0), second_side(part0), around(mine[1], 1), around(mine[3], 3)
 
         a0, b0, part0, part1, part3, to2 = after((a0, b0, part0, part1, part3, mine[2]), ())
-        q0, a1, b1, a3, part2 = second_side(a0), first_side(part1), second_side(part1), first_side(part3), around(to2, 2)
+        part13 = jnp.concatenate([part1, part3], axis=0)
+        q0, a13, b13, part2 = second_side(a0), first_side(part13), second_side(part13), around(to2, 2)
 
         own = amplitudes.transpose(2, 0, 1).reshape(TV * TV, blocks_here * pairs)
-        own = jnp.broadcast_to(own, (levels, *own.shape))
-        own, q0, a1, b1, a3, part2, part3 = after((own, q0, a1, b1, a3, part2, part3), ())
-        own = lax.all_to_all(own, "task", split_axis=0, concat_axis=0, axis_index_groups=same_core)
-        q1, b3, a2, b2 = second_side(a1), second_side(part3), first_side(part2), second_side(part2)
-        forms0 = prepare([part0, a0, b0, q0], column[None], matrix)
+        own, q0, a13, b13, part2, part13 = after((own, q0, a13, b13, part2, part13), ())
+        q13, a2, b2, amp1 = second_side(a13), first_side(part2), second_side(part2), around(own, 1)
+        forms0 = made_forms(part0, a0, b0, q0)
         far0 = other_core(forms0)
 
-        q1, b3, a2, b2, a3 = after((q1, b3, a2, b2, a3), forms0)
-        q2, q3 = second_side(a2), second_side(a3)
-        forms1 = prepare([part1, a1, b1, q1], column[None], matrix)
-        far1 = other_core(after(forms1, far0))
-
-        q2, q3 = after((q2, q3), forms1)
-        forms3 = prepare([part3, a3, b3, q3], column[None], matrix)
-        far3 = other_core(after(forms3, far1))
-        forms2 = prepare([part2, a2, b2, q2], column[None], matrix)
-        far2 = other_core(after(forms2, far3))
-        amps = prepare_amps(own, blocks_here, jnp.asarray(amp_matrix()))
-        held = [forms0, far0, forms1, far1, forms2, far2, forms3, far3]
+        q13, a2, b2, amp1 = after((q13, a2, b2, amp1), forms0)
+        q2, amp2 = second_side(a2), around(amp1, 1)
+        forms13 = made_forms(part13, a13, b13, q13)
+        far13 = other_core(after(forms13, far0))
+
+        q2, amp2 = after((q2, amp2), forms13)
+        amp3 = around(amp2, 1)
+        forms2 = made_forms(part2, a2, b2, q2)
+        far2 = other_core(after(forms2, far13))
+        amps = prepare_amps([own, amp1, amp2, after(amp3, forms2)], blocks_here, jnp.asarray(amp_matrix()))
+        held = [forms0, far0, forms13, far13, forms2, far2]
     else:
         parts = [mine[0]] + [around(mine[by], by) for by in range(1, levels)]
         tiles = amplitudes.reshape(blocks_here, pairs, TV, TV).transpose(0, 3, 2, 1)
         tiles = jnp.pad(tiles, ((0, 0), (0, 0), (0, PAD - TV), (0, 0))).reshape(blocks_here, ROWS, pairs)
-        amps = lax.all_gather(tiles, "task", axis=0, tiled=True, axis_index_groups=same_core)
+        amps = lax.all_gather(tiles, "task", axis=0, axis_index_groups=same_core)
+        amps = amps[(level - jnp.arange(levels)) % levels].reshape(levels * blocks_here, ROWS, pairs)
         held = lax.all_gather(jnp.stack(parts), "pair", axis=2, tiled=True)
         held = [jnp.stack([held, other_core(held)], axis=1).reshape(total, depth * pair_count, -1)]
     amps = (amps, other_core(amps))

time: 161 us -> 140 us (0.87)
  local copies, waits for them, and re-layouts: 14.5 us -> 6.48 us
  waiting for transfers between devices: 61.8 us -> 54.9 us
  starting transfers between devices: 27.4 us -> 22.7 us
    all_to_all x1 -> x0, waiting for transfers between devices: 22.7 us -> none  [per_device(): lax.all_to_all(own, 'task', split_axis=0, concat_axis=0, axis_index_group...]
    ppermute x6 -> x9, waiting for transfers between devices: 19 us -> 36.5 us  [around(): lax.ppermute(x, 'task', [(c, (c + 2 * by) % task_count) for c in range(ta...]
    unnamed x47 -> x24, local copies, waits for them, and re-layouts: 12 us -> 5.17 us
    all_to_all x1 -> x0, starting transfers between devices: 4.86 us -> none  [per_device(): lax.all_to_all(own, 'task', split_axis=0, concat_axis=0, axis_index_group...]
    ppermute x6 -> x9, starting transfers between devices: 8.23 us -> 11.7 us  [around(): lax.ppermute(x, 'task', [(c, (c + 2 * by) % task_count) for c in range(ta...]
    pallas_call x1, Pallas kernels: 3.47 us -> 1.44 us  [prepare_amps(): pl.pallas_call(amp_kernel, out_shape=jax.ShapeDtypeStruct((levels * block...]
    ppermute x8 -> x6, starting transfers between devices: 9.24 us -> 7.22 us  [per_device(): second_side = lambda x: lax.ppermute(x, ('pair', 'task'), sides[1])]
    ppermute x8 -> x6, waiting for transfers between devices: 16.7 us -> 15 us  [per_device(): second_side = lambda x: lax.ppermute(x, ('pair', 'task'), sides[1])]
  transfers between devices with their start and end apart: 24 -> 22, of which waited for: 12 -> 10; matrix products, arithmetic and copies ran while one was open for 0% -> 0% of each run, Pallas kernels for 27% -> 30%
where the time goes in v7:
time: 140 us; the launch traced here: 139 us
  waiting for transfers between devices  54.9 us (39%)
  Pallas kernels  54.8 us (39%)
  starting transfers between devices  22.7 us (16%)
  local copies, waits for them, and re-layouts  6.48 us (5%)
    pallas_call x4, Pallas kernels, ladders(): pl.pallas_call(functools.partial(ladder_kernel, find, made, len(tiles)),...  41.4 us
    ppermute x9, waiting for transfers between devices, around(): lax.ppermute(x, 'task', [(c, (c + 2 * by) % task_count) for c in range(ta...  36.5 us
    ppermute x6, waiting for transfers between devices, per_device(): second_side = lambda x: lax.ppermute(x, ('pair', 'task'), sides[1])  15 us
    pallas_call x3, Pallas kernels, prepare(): pl.pallas_call(prepare_kernel, out_shape=jax.ShapeDtypeStruct((count, mat...  11.9 us
    ppermute x9, starting transfers between devices, around(): lax.ppermute(x, 'task', [(c, (c + 2 * by) % task_count) for c in range(ta...  11.7 us
    ppermute x6, starting transfers between devices, per_device(): second_side = lambda x: lax.ppermute(x, ('pair', 'task'), sides[1])  7.22 us
    unnamed x24, local copies, waits for them, and re-layouts  5.17 us
    ppermute x3, starting transfers between devices, per_device(): first_side = lambda x: lax.ppermute(x, ('pair', 'task'), sides[0])  3.54 us
  transfers between devices with their start and end apart: 22, of which 10 were waited for; matrix products, arithmetic and copies ran while one was open for 0% of the time, Pallas kernels for 30%

profile of v7, /device:TPU:0, one launch (start us, length us, event | category | flops | bytes accessed | tf_op | source)
XLA Modules:
  0.0 139.3 jit_solution(6995315424572212801)
XLA Ops:
  0.0 3.4 %copy.23 = bf16[2,384,625]{2,1,0:T(8,128)(2,1)S(1)} copy(bf16[2,384,625]{1,0,2:T(2,128)(2,1)} %param.8) | data formatting | bytes 1920000 | tf_op args[0]
  3.4 0.0 copy-start.3
  3.4 0.1 dynamic-slice_bitcast_fusion
  3.5 5.1 %collective-permute-start.3 = (bf16[2,96,625]{2,1,0:T(8,128)(2,1)S(1)}, bf16[2,96,625]{2,1,0:T(8,128)(2,1)S(1)}, u32[]{:S(2)}, u32[]{:S(2)}) collective-permute-start(bf16[2,96,625]{2,1,0:T(8,128)(2,1)S(1)} %get-tuple-element.48), channel_id=1, source_target_pairs={{0,6},{1,7},{2,0},{3,1},{4,2},{5,3},{6,4},{7,5},{8,14},{9,15},{10,... | collective-permute-start | bytes 720008 | tf_op jit(solution)/shard_map/ppermute | solution.py:296
  8.7 0.0 collective-permute-start.2
  8.7 1.5 %collective-permute-start.1 = (bf16[2,96,625]{2,1,0:T(8,128)(2,1)S(1)}, bf16[2,96,625]{2,1,0:T(8,128)(2,1)S(1)}, u32[]{:S(2)}, u32[]{:S(2)}) collective-permute-start(bf16[2,96,625]{2,1,0:T(8,128)(2,1)S(1)} %get-tuple-element.26.refs_0_), channel_id=1, source_target_pairs={{0,16},{1,9},{2,18},{3,11},{4,20},{5,13},{6,22},{7,15},{8,24},{9,1... | collective-permute-start | bytes 720008 | tf_op jit(solution)/shard_map/ppermute | solution.py:307
  10.2 1.5 %collective-permute-start = (bf16[2,96,625]{2,1,0:T(8,128)(2,1)S(1)}, bf16[2,96,625]{2,1,0:T(8,128)(2,1)S(1)}, u32[]{:S(2)}, u32[]{:S(2)}) collective-permute-start(bf16[2,96,625]{2,1,0:T(8,128)(2,1)S(1)} %get-tuple-element.26.refs_0_), channel_id=1, source_target_pairs={{0,8},{1,17},{2,10},{3,19},{4,12},{5,21},{6,14},{7,23},{8,0},{9,25... | collective-permute-start | bytes 720008 | tf_op jit(solution)/shard_map/ppermute | solution.py:306
  11.7 3.3 %collective-permute-done.3 = bf16[2,96,625]{2,1,0:T(8,128)(2,1)S(1)} collective-permute-done((bf16[2,96,625]{2,1,0:T(8,128)(2,1)S(1)}, bf16[2,96,625]{2,1,0:T(8,128)(2,1)S(1)}, u32[]{:S(2)}, u32[]{:S(2)}) %collective-permute-start.3) | collective-permute-done | bytes 240032 | tf_op jit(solution)/shard_map/ppermute | solution.py:296
  15.0 5.0 %collective-permute-done.2 = bf16[2,96,625]{2,1,0:T(8,128)(2,1)S(1)} collective-permute-done((bf16[2,96,625]{2,1,0:T(8,128)(2,1)S(1)}, bf16[2,96,625]{2,1,0:T(8,128)(2,1)S(1)}, u32[]{:S(2)}, u32[]{:S(2)}) %collective-permute-start.2) | collective-permute-done | bytes 240032 | tf_op jit(solution)/shard_map/ppermute | solution.py:296
  20.0 0.0 collective-permute-done.1.refs_2_
  20.0 0.0 collective-permute-done.refs_1_
  20.1 1.6 %collective-permute-start.6 = (bf16[4,96,625]{2,1,0:T(8,128)(2,1)S(1)}, bf16[4,96,625]{2,1,0:T(8,128)(2,1)S(1)}, u32[]{:S(2)}, u32[]{:S(2)}) collective-permute-start(bf16[4,96,625]{2,1,0:T(8,128)(2,1)S(1)} %constant_dynamic-update-slice_fusion.refs_0_), channel_id=1, source_target_pairs={{0,16},{1,9},{2,18},{3,11},{4,20},{5,13},{6,22},{7,15},{8,24},{9,1... | collective-permute-start | bytes 1440008 | tf_op jit(solution)/shard_map/ppermute | solution.py:307
  21.7 1.5 %collective-permute-start.5 = (bf16[4,96,625]{2,1,0:T(8,128)(2,1)S(1)}, bf16[4,96,625]{2,1,0:T(8,128)(2,1)S(1)}, u32[]{:S(2)}, u32[]{:S(2)}) collective-permute-start(bf16[4,96,625]{2,1,0:T(8,128)(2,1)S(1)} %constant_dynamic-update-slice_fusion.refs_0_), channel_id=1, source_target_pairs={{0,8},{1,17},{2,10},{3,19},{4,12},{5,21},{6,14},{7,23},{8,0},{9,25... | collective-permute-start | bytes 1440008 | tf_op jit(solution)/shard_map/ppermute | solution.py:306
  23.2 0.7 collective-permute-start.7
  23.9 0.5 collective-permute-start.4
  24.4 0.0 copy-done.6
  24.4 0.3 pad
  24.7 10.9 %collective-permute-done.7.refs_0_ = bf16[2,96,625]{2,1,0:T(8,128)(2,1)S(1)} collective-permute-done((bf16[2,96,625]{2,1,0:T(8,128)(2,1)S(1)}, bf16[2,96,625]{2,1,0:T(8,128)(2,1)S(1)}, u32[]{:S(2)}, u32[]{:S(2)}) %collective-permute-start.7) | collective-permute-done | bytes 240032 | tf_op jit(solution)/shard_map/ppermute | solution.py:296
  35.6 0.5 collective-permute-done.4.refs_3_
  36.1 0.0 collective-permute-done.6.refs_2_
  36.1 0.0 collective-permute-done.5.refs_1_
  36.1 2.7 %shard_map.82.refs_0_ = bf16[2,1600,384]{2,1,0:T(8,128)(2,1)S(1)} custom-call(s32[1]{0:T(128)} %bitcast.column_ref, bf16[2,96,625]{2,1,0:T(8,128)(2,1)S(1)} %get-tuple-element.26.refs_0_, bf16[2,96,625]{2,1,0:T(8,128)(2,1)S(1)} %collective-permute-done.refs_1_, bf16[2,96,625]{2,1,0:T(8,128)(2,1)S(1)} %collective-permute-done.1.refs_2_, ...), custom_call_target="tpu_custom_call" | custom-call | flops 1536000000 | bytes 3417600 | tf_op jit(solution)/shard_map/pallas_call | solution.py:77
  38.8 0.0 copy-start
  38.8 0.1 collective-permute-start.8
  38.9 1.6 %collective-permute-start.9 = (bf16[4,96,625]{2,1,0:T(8,128)(2,1)S(1)}, bf16[4,96,625]{2,1,0:T(8,128)(2,1)S(1)}, u32[]{:S(2)}, u32[]{:S(2)}) collective-permute-start(bf16[4,96,625]{2,1,0:T(8,128)(2,1)S(1)} %collective-permute-done.5.refs_1_), channel_id=1, source_target_pairs={{0,16},{1,9},{2,18},{3,11},{4,20},{5,13},{6,22},{7,15},{8,24},{9,1... | collective-permute-start | bytes 1440008 | tf_op jit(solution)/shard_map/ppermute | solution.py:307
  40.5 1.7 %collective-permute-start.12 = (bf16[625,256]{1,0:T(8,128)(2,1)S(1)}, bf16[625,256]{1,0:T(8,128)(2,1)S(1)}, u32[]{:S(2)}, u32[]{:S(2)}) collective-permute-start(bf16[625,256]{1,0:T(8,128)(2,1)S(1)} %bitcast.24), channel_id=1, source_target_pairs={{0,2},{1,3},{2,4},{3,5},{4,6},{5,7},{6,0},{7,1},{8,10},{9,11},{10,... | collective-permute-start | bytes 960008 | tf_op jit(solution)/shard_map/ppermute | solution.py:296
  42.1 0.5 collective-permute-start.11
  42.6 0.6 collective-permute-start.10
  43.2 9.9 %collective-permute-done.11.refs_2_ = bf16[2,96,625]{2,1,0:T(8,128)(2,1)S(1)} collective-permute-done((bf16[2,96,625]{2,1,0:T(8,128)(2,1)S(1)}, bf16[2,96,625]{2,1,0:T(8,128)(2,1)S(1)}, u32[]{:S(2)}, u32[]{:S(2)}) %collective-permute-start.11) | collective-permute-done | bytes 240032 | tf_op jit(solution)/shard_map/ppermute | solution.py:307
  53.0 0.0 collective-permute-done.10.refs_1_
  53.0 0.0 collective-permute-done.12.refs_1_
  53.0 0.0 collective-permute-done.9.refs_3_
  53.0 5.9 %shard_map.83.refs_2_ = bf16[4,1600,384]{2,1,0:T(8,128)(2,1)} custom-call(s32[1]{0:T(128)} %bitcast.column_ref, bf16[4,96,625]{2,1,0:T(8,128)(2,1)S(1)} %constant_dynamic-update-slice_fusion.refs_0_, bf16[4,96,625]{2,1,0:T(8,128)(2,1)S(1)} %collective-permute-done.5.refs_1_, bf16[4,96,625]{2,1,0:T(8,128)(2,1)S(1)} %collective-permute-done.6.refs_2_, ...), custom_call_target="tpu_custom_call" | custom-call | flops 3072000000 | bytes 6835200 | tf_op jit(solution)/shard_map/pallas_call | solution.py:77
  58.9 0.0 collective-permute-done.8.refs_1_
  58.9 0.1 collective-permute-start.13
  59.0 1.7 %collective-permute-start.15 = (bf16[625,256]{1,0:T(8,128)(2,1)S(1)}, bf16[625,256]{1,0:T(8,128)(2,1)S(1)}, u32[]{:S(2)}, u32[]{:S(2)}) collective-permute-start(bf16[625,256]{1,0:T(8,128)(2,1)S(1)} %collective-permute-done.12.refs_1_), channel_id=1, source_target_pairs={{0,2},{1,3},{2,4},{3,5},{4,6},{5,7},{6,0},{7,1},{8,10},{9,11},{10,... | collective-permute-start | bytes 960008 | tf_op jit(solution)/shard_map/ppermute | solution.py:296
  60.7 1.5 %collective-permute-start.14 = (bf16[2,96,625]{2,1,0:T(8,128)(2,1)S(1)}, bf16[2,96,625]{2,1,0:T(8,128)(2,1)S(1)}, u32[]{:S(2)}, u32[]{:S(2)}) collective-permute-start(bf16[2,96,625]{2,1,0:T(8,128)(2,1)S(1)} %collective-permute-done.10.refs_1_), channel_id=1, source_target_pairs={{0,16},{1,9},{2,18},{3,11},{4,20},{5,13},{6,22},{7,15},{8,24},{9,1... | collective-permute-start | bytes 720008 | tf_op jit(solution)/shard_map/ppermute | solution.py:307
  62.2 4.7 %collective-permute-done.14.refs_3_ = bf16[2,96,625]{2,1,0:T(8,128)(2,1)S(1)} collective-permute-done((bf16[2,96,625]{2,1,0:T(8,128)(2,1)S(1)}, bf16[2,96,625]{2,1,0:T(8,128)(2,1)S(1)}, u32[]{:S(2)}, u32[]{:S(2)}) %collective-permute-start.14) | collective-permute-done | bytes 240032 | tf_op jit(solution)/shard_map/ppermute | solution.py:307
  66.9 3.9 %collective-permute-done.15.refs_2_ = bf16[625,256]{1,0:T(8,128)(2,1)S(1)} collective-permute-done((bf16[625,256]{1,0:T(8,128)(2,1)S(1)}, bf16[625,256]{1,0:T(8,128)(2,1)S(1)}, u32[]{:S(2)}, u32[]{:S(2)}) %collective-permute-start.15) | collective-permute-done | bytes 320032 | tf_op jit(solution)/shard_map/ppermute | solution.py:296
  70.8 3.4 %shard_map.84.refs_4_ = bf16[2,1600,384]{2,1,0:T(8,128)(2,1)} custom-call(s32[1]{0:T(128)} %bitcast.column_ref, bf16[2,96,625]{2,1,0:T(8,128)(2,1)S(1)} %collective-permute-done.7.refs_0_, bf16[2,96,625]{2,1,0:T(8,128)(2,1)S(1)} %collective-permute-done.10.refs_1_, bf16[2,96,625]{2,1,0:T(8,128)(2,1)S(1)} %collective-permute-done.11.refs_2_, ...), custom_call_target="tpu_custom_call" | custom-call | flops 1536000000 | bytes 3417600 | tf_op jit(solution)/shard_map/pallas_call | solution.py:77
  74.3 0.0 collective-permute-done.13.refs_3_
  74.3 0.1 collective-permute-start.16
  74.3 0.1 collective-permute-start.17
  74.4 11.8 %collective-permute-done.17.refs_3_ = bf16[625,256]{1,0:T(8,128)(2,1)S(1)} collective-permute-done((bf16[625,256]{1,0:T(8,128)(2,1)S(1)}, bf16[625,256]{1,0:T(8,128)(2,1)S(1)}, u32[]{:S(2)}, u32[]{:S(2)}) %collective-permute-start.17) | collective-permute-done | bytes 320032 | tf_op jit(solution)/shard_map/ppermute | solution.py:296
  86.2 1.4 %shard_map.85.refs_6_ = bf16[8,800,128]{2,1,0:T(8,128)(2,1)S(1)} custom-call(bf16[800,625]{1,0:T(8,128)(2,1)S(1)} %copy-done.2, bf16[625,256]{1,0:T(8,128)(2,1)S(1)} %bitcast.25, bf16[625,256]{1,0:T(8,128)(2,1)S(1)} %collective-permute-done.12.refs_1_, bf16[625,256]{1,0:T(8,128)(2,1)S(1)} %collective-permute-done.15.refs_2_, ...), custom_call_target="tpu_custom_call" | custom-call | flops 1024000000 | bytes 2560000 | tf_op jit(solution)/shard_map/pallas_call | solution.py:108
  87.6 0.1 collective-permute-start.18
  87.7 0.1 copy.24.owners_ref
  87.8 0.1 copy.25.local_ref
  87.9 3.3 %collective-permute-done.18.refs_7_ = bf16[8,800,128]{2,1,0:T(8,128)(2,1)S(1)} collective-permute-done((bf16[8,800,128]{2,1,0:T(8,128)(2,1)S(1)}, bf16[8,800,128]{2,1,0:T(8,128)(2,1)S(1)}, u32[]{:S(2)}, u32[]{:S(2)}) %collective-permute-start.18) | collective-permute-done | bytes 1638432 | tf_op jit(solution)/shard_map/ppermute | solution.py:293
  91.2 0.0 collective-permute-done.16.refs_5_
  91.2 1.3 copy-done.1
  92.5 10.3 %shard_map.87 = bf16[1,2,625,128]{3,2,1,0:T(8,128)(2,1)S(1)} custom-call(s32[1]{0:T(128)} %bitcast.column_ref, s32[32,3]{1,0:T(8,128)S(1)} %copy.24.owners_ref, s32[32,4]{1,0:T(8,128)S(1)} %copy.25.local_ref, bf16[2,1600,384]{2,1,0:T(8,128)(2,1)} %copy-done, bf16[2,1600,384]{2,1,0:T(8,128)(2,1)} %collective-permute-done.8.refs_1_, ...), custom_call_target="tpu_custom_call" | custom-call | flops 2936012800 | bytes 6553600 | tf_op jit(solution)/shard_map/pallas_call | solution.py:258
  102.8 0.2 collective-permute-start.20
  103.1 10.3 %shard_map.86 = bf16[1,2,625,128]{3,2,1,0:T(8,128)(2,1)S(1)} custom-call(s32[1]{0:T(128)} %bitcast.column_ref, s32[32,3]{1,0:T(8,128)S(1)} %copy.24.owners_ref, s32[32,4]{1,0:T(8,128)S(1)} %copy.25.local_ref, bf16[2,1600,384]{2,1,0:T(8,128)(2,1)} %copy-done, bf16[2,1600,384]{2,1,0:T(8,128)(2,1)} %collective-permute-done.8.refs_1_, ...), custom_call_target="tpu_custom_call" | custom-call | flops 2936012800 | bytes 6553600 | tf_op jit(solution)/shard_map/pallas_call | solution.py:258
  113.4 0.1 collective-permute-start.19
  113.5 10.3 %shard_map.88 = bf16[1,2,625,128]{3,2,1,0:T(8,128)(2,1)S(1)} custom-call(s32[1]{0:T(128)} %bitcast.column_ref, s32[32,3]{1,0:T(8,128)S(1)} %copy.24.owners_ref, s32[32,4]{1,0:T(8,128)S(1)} %copy.25.local_ref, bf16[2,1600,384]{2,1,0:T(8,128)(2,1)} %copy-done, bf16[2,1600,384]{2,1,0:T(8,128)(2,1)} %collective-permute-done.8.refs_1_, ...), custom_call_target="tpu_custom_call" | custom-call | flops 2936012800 | bytes 6553600 | tf_op jit(solution)/shard_map/pallas_call | solution.py:258
  123.8 0.0 copy-start.5
  123.8 2.1 %collective-permute-start.21 = (bf16[2,625,128]{2,1,0:T(8,128)(2,1)S(1)}, bf16[2,625,128]{2,1,0:T(8,128)(2,1)S(1)}, u32[]{:S(2)}, u32[]{:S(2)}) collective-permute-start(bf16[2,625,128]{2,1,0:T(8,128)(2,1)S(1)} %bitcast.28), channel_id=1, source_target_pairs={{0,2},{1,3},{2,4},{3,5},{4,6},{5,7},{6,0},{7,1},{8,10},{9,11},{10,... | collective-permute-start | bytes 960008 | tf_op jit(solution)/shard_map/ppermute | solution.py:296
  125.9 10.3 %shard_map.89 = bf16[1,2,625,128]{3,2,1,0:T(8,128)(2,1)S(1)} custom-call(s32[1]{0:T(128)} %bitcast.column_ref, s32[32,3]{1,0:T(8,128)S(1)} %copy.24.owners_ref, s32[32,4]{1,0:T(8,128)S(1)} %copy.25.local_ref, bf16[2,1600,384]{2,1,0:T(8,128)(2,1)} %copy-done, bf16[2,1600,384]{2,1,0:T(8,128)(2,1)} %collective-permute-done.8.refs_1_, ...), custom_call_target="tpu_custom_call" | custom-call | flops 2936012800 | bytes 6553600 | tf_op jit(solution)/shard_map/pallas_call | solution.py:258
  136.3 0.0 collective-permute-done.20
  136.3 1.6 %collective-permute-done.19 = bf16[2,625,128]{2,1,0:T(8,128)(2,1)S(1)} collective-permute-done((bf16[2,625,128]{2,1,0:T(8,128)(2,1)S(1)}, bf16[2,625,128]{2,1,0:T(8,128)(2,1)S(1)}, u32[]{:S(2)}, u32[]{:S(2)}) %collective-permute-start.19) | collective-permute-done | bytes 320032 | tf_op jit(solution)/shard_map/ppermute | solution.py:296
  137.9 0.0 collective-permute-done.21
  137.9 0.2 fusion.1
  138.1 1.2 copy.33
  (16 shorter events, 0.1 us)
Async XLA Ops:
  0.0 24.4 %copy-start.6 = (bf16[2,128,625]{1,0,2:T(2,128)(2,1)S(1)}, bf16[2,128,625]{1,0,2:T(2,128)(2,1)}, u32[]{:S(2)}) copy-start(bf16[2,128,625]{1,0,2:T(2,128)(2,1)} %param.9) | copy-start | bytes 960004
  3.4 32.7 %copy-start.3 = (bf16[1600,625]{1,0:T(8,128)(2,1)S(1)}, bf16[1600,625]{1,0:T(8,128)(2,1)}, u32[]{:S(2)}) copy-start(bf16[1600,625]{1,0:T(8,128)(2,1)} %constant.61.clone.refs_4_) | copy-start | bytes 6000004
  3.5 11.5 %collective-permute-start.3 = (bf16[2,96,625]{2,1,0:T(8,128)(2,1)S(1)}, bf16[2,96,625]{2,1,0:T(8,128)(2,1)S(1)}, u32[]{:S(2)}, u32[]{:S(2)}) collective-permute-start(bf16[2,96,625]{2,1,0:T(8,128)(2,1)S(1)} %get-tuple-element.48), channel_id=1, source_target_pairs={{0,6},{1,7},{2,0},{3,1},{4,2},{5,3},{6,4},{7,5},{8,14},{9,15},{10,... | collective-permute-start | bytes 720008 | tf_op jit(solution)/shard_map/ppermute | solution.py:296
  8.7 11.4 %collective-permute-start.2 = (bf16[2,96,625]{2,1,0:T(8,128)(2,1)S(1)}, bf16[2,96,625]{2,1,0:T(8,128)(2,1)S(1)}, u32[]{:S(2)}, u32[]{:S(2)}) collective-permute-start(bf16[2,96,625]{2,1,0:T(8,128)(2,1)S(1)} %get-tuple-element.49), channel_id=1, source_target_pairs={{0,2},{1,3},{2,4},{3,5},{4,6},{5,7},{6,0},{7,1},{8,10},{9,11},{10,... | collective-permute-start | bytes 720008 | tf_op jit(solution)/shard_map/ppermute | solution.py:296
  8.7 11.4 %collective-permute-start.1 = (bf16[2,96,625]{2,1,0:T(8,128)(2,1)S(1)}, bf16[2,96,625]{2,1,0:T(8,128)(2,1)S(1)}, u32[]{:S(2)}, u32[]{:S(2)}) collective-permute-start(bf16[2,96,625]{2,1,0:T(8,128)(2,1)S(1)} %get-tuple-element.26.refs_0_), channel_id=1, source_target_pairs={{0,16},{1,9},{2,18},{3,11},{4,20},{5,13},{6,22},{7,15},{8,24},{9,1... | collective-permute-start | bytes 720008 | tf_op jit(solution)/shard_map/ppermute | solution.py:307
  10.2 9.9 %collective-permute-start = (bf16[2,96,625]{2,1,0:T(8,128)(2,1)S(1)}, bf16[2,96,625]{2,1,0:T(8,128)(2,1)S(1)}, u32[]{:S(2)}, u32[]{:S(2)}) collective-permute-start(bf16[2,96,625]{2,1,0:T(8,128)(2,1)S(1)} %get-tuple-element.26.refs_0_), channel_id=1, source_target_pairs={{0,8},{1,17},{2,10},{3,19},{4,12},{5,21},{6,14},{7,23},{8,0},{9,25... | collective-permute-start | bytes 720008 | tf_op jit(solution)/shard_map/ppermute | solution.py:306
  20.1 16.0 %collective-permute-start.6 = (bf16[4,96,625]{2,1,0:T(8,128)(2,1)S(1)}, bf16[4,96,625]{2,1,0:T(8,128)(2,1)S(1)}, u32[]{:S(2)}, u32[]{:S(2)}) collective-permute-start(bf16[4,96,625]{2,1,0:T(8,128)(2,1)S(1)} %constant_dynamic-update-slice_fusion.refs_0_), channel_id=1, source_target_pairs={{0,16},{1,9},{2,18},{3,11},{4,20},{5,13},{6,22},{7,15},{8,24},{9,1... | collective-permute-start | bytes 1440008 | tf_op jit(solution)/shard_map/ppermute | solution.py:307
  21.7 14.4 %collective-permute-start.5 = (bf16[4,96,625]{2,1,0:T(8,128)(2,1)S(1)}, bf16[4,96,625]{2,1,0:T(8,128)(2,1)S(1)}, u32[]{:S(2)}, u32[]{:S(2)}) collective-permute-start(bf16[4,96,625]{2,1,0:T(8,128)(2,1)S(1)} %constant_dynamic-update-slice_fusion.refs_0_), channel_id=1, source_target_pairs={{0,8},{1,17},{2,10},{3,19},{4,12},{5,21},{6,14},{7,23},{8,0},{9,25... | collective-permute-start | bytes 1440008 | tf_op jit(solution)/shard_map/ppermute | solution.py:306
  23.2 12.4 %collective-permute-start.7 = (bf16[2,96,625]{2,1,0:T(8,128)(2,1)S(1)}, bf16[2,96,625]{2,1,0:T(8,128)(2,1)S(1)}, u32[]{:S(2)}, u32[]{:S(2)}) collective-permute-start(bf16[2,96,625]{2,1,0:T(8,128)(2,1)S(1)} %get-tuple-element.31), channel_id=1, source_target_pairs={{0,4},{1,5},{2,6},{3,7},{4,0},{5,1},{6,2},{7,3},{8,12},{9,13},{10,... | collective-permute-start | bytes 720008 | tf_op jit(solution)/shard_map/ppermute | solution.py:296
  23.9 12.2 %collective-permute-start.4 = (bf16[2,96,625]{2,1,0:T(8,128)(2,1)S(1)}, bf16[2,96,625]{2,1,0:T(8,128)(2,1)S(1)}, u32[]{:S(2)}, u32[]{:S(2)}) collective-permute-start(bf16[2,96,625]{2,1,0:T(8,128)(2,1)S(1)} %collective-permute-done.refs_1_), channel_id=1, source_target_pairs={{0,16},{1,9},{2,18},{3,11},{4,20},{5,13},{6,22},{7,15},{8,24},{9,1... | collective-permute-start | bytes 720008 | tf_op jit(solution)/shard_map/ppermute | solution.py:307
  38.8 20.1 %copy-start = (bf16[2,1600,384]{2,1,0:T(8,128)(2,1)}, bf16[2,1600,384]{2,1,0:T(8,128)(2,1)S(1)}, u32[]{:S(2)}) copy-start(bf16[2,1600,384]{2,1,0:T(8,128)(2,1)S(1)} %shard_map.82.refs_0_) | copy-start | bytes 7372804
  38.8 20.1 %collective-permute-start.8 = (bf16[2,1600,384]{2,1,0:T(8,128)(2,1)S(1)}, bf16[2,1600,384]{2,1,0:T(8,128)(2,1)}, u32[]{:S(2)}, u32[]{:S(2)}) collective-permute-start(bf16[2,1600,384]{2,1,0:T(8,128)(2,1)S(1)} %shard_map.82.refs_0_), channel_id=1, source_target_pairs={{0,1},{1,0},{2,3},{3,2},{4,5},{5,4},{6,7},{7,6},{8,9},{9,8},{10,11... | collective-permute-start | bytes 7372808 | tf_op jit(solution)/shard_map/ppermute | solution.py:293
  38.9 14.2 %collective-permute-start.9 = (bf16[4,96,625]{2,1,0:T(8,128)(2,1)S(1)}, bf16[4,96,625]{2,1,0:T(8,128)(2,1)S(1)}, u32[]{:S(2)}, u32[]{:S(2)}) collective-permute-start(bf16[4,96,625]{2,1,0:T(8,128)(2,1)S(1)} %collective-permute-done.5.refs_1_), channel_id=1, source_target_pairs={{0,16},{1,9},{2,18},{3,11},{4,20},{5,13},{6,22},{7,15},{8,24},{9,1... | collective-permute-start | bytes 1440008 | tf_op jit(solution)/shard_map/ppermute | solution.py:307
  40.5 12.6 %collective-permute-start.12 = (bf16[625,256]{1,0:T(8,128)(2,1)S(1)}, bf16[625,256]{1,0:T(8,128)(2,1)S(1)}, u32[]{:S(2)}, u32[]{:S(2)}) collective-permute-start(bf16[625,256]{1,0:T(8,128)(2,1)S(1)} %bitcast.24), channel_id=1, source_target_pairs={{0,2},{1,3},{2,4},{3,5},{4,6},{5,7},{6,0},{7,1},{8,10},{9,11},{10,... | collective-permute-start | bytes 960008 | tf_op jit(solution)/shard_map/ppermute | solution.py:296
  42.1 10.9 %collective-permute-start.11 = (bf16[2,96,625]{2,1,0:T(8,128)(2,1)S(1)}, bf16[2,96,625]{2,1,0:T(8,128)(2,1)S(1)}, u32[]{:S(2)}, u32[]{:S(2)}) collective-permute-start(bf16[2,96,625]{2,1,0:T(8,128)(2,1)S(1)} %collective-permute-done.7.refs_0_), channel_id=1, source_target_pairs={{0,16},{1,9},{2,18},{3,11},{4,20},{5,13},{6,22},{7,15},{8,24},{9,1... | collective-permute-start | bytes 720008 | tf_op jit(solution)/shard_map/ppermute | solution.py:307
  42.6 10.4 %collective-permute-start.10 = (bf16[2,96,625]{2,1,0:T(8,128)(2,1)S(1)}, bf16[2,96,625]{2,1,0:T(8,128)(2,1)S(1)}, u32[]{:S(2)}, u32[]{:S(2)}) collective-permute-start(bf16[2,96,625]{2,1,0:T(8,128)(2,1)S(1)} %collective-permute-done.7.refs_0_), channel_id=1, source_target_pairs={{0,8},{1,17},{2,10},{3,19},{4,12},{5,21},{6,14},{7,23},{8,0},{9,25... | collective-permute-start | bytes 720008 | tf_op jit(solution)/shard_map/ppermute | solution.py:306
  58.9 27.3 %copy-start.2 = (bf16[800,625]{1,0:T(8,128)(2,1)S(1)}, bf16[800,625]{1,0:T(8,128)(2,1)}, u32[]{:S(2)}) copy-start(bf16[800,625]{1,0:T(8,128)(2,1)} %constant.63.clone.matrix_ref) | copy-start | bytes 3000004
  58.9 15.3 %collective-permute-start.13 = (bf16[4,1600,384]{2,1,0:T(8,128)(2,1)}, bf16[4,1600,384]{2,1,0:T(8,128)(2,1)S(1)}, u32[]{:S(2)}, u32[]{:S(2)}) collective-permute-start(bf16[4,1600,384]{2,1,0:T(8,128)(2,1)} %shard_map.83.refs_2_), channel_id=1, source_target_pairs={{0,1},{1,0},{2,3},{3,2},{4,5},{5,4},{6,7},{7,6},{8,9},{9,8},{10,11... | collective-permute-start | bytes 14745608 | tf_op jit(solution)/shard_map/ppermute | solution.py:293
  59.0 11.8 %collective-permute-start.15 = (bf16[625,256]{1,0:T(8,128)(2,1)S(1)}, bf16[625,256]{1,0:T(8,128)(2,1)S(1)}, u32[]{:S(2)}, u32[]{:S(2)}) collective-permute-start(bf16[625,256]{1,0:T(8,128)(2,1)S(1)} %collective-permute-done.12.refs_1_), channel_id=1, source_target_pairs={{0,2},{1,3},{2,4},{3,5},{4,6},{5,7},{6,0},{7,1},{8,10},{9,11},{10,... | collective-permute-start | bytes 960008 | tf_op jit(solution)/shard_map/ppermute | solution.py:296
  60.7 6.2 %collective-permute-start.14 = (bf16[2,96,625]{2,1,0:T(8,128)(2,1)S(1)}, bf16[2,96,625]{2,1,0:T(8,128)(2,1)S(1)}, u32[]{:S(2)}, u32[]{:S(2)}) collective-permute-start(bf16[2,96,625]{2,1,0:T(8,128)(2,1)S(1)} %collective-permute-done.10.refs_1_), channel_id=1, source_target_pairs={{0,16},{1,9},{2,18},{3,11},{4,20},{5,13},{6,22},{7,15},{8,24},{9,1... | collective-permute-start | bytes 720008 | tf_op jit(solution)/shard_map/ppermute | solution.py:307
  74.3 13.5 %copy-start.7 = (s32[32,3]{0,1:T(4,128)S(1)}, s32[32,3]{0,1:T(4,128)}, u32[]{:S(2)}) copy-start(s32[32,3]{0,1:T(4,128)} %param.11) | copy-start | bytes 1156
  74.3 13.6 %copy-start.8 = (s32[32,4]{0,1:T(4,128)S(1)}, s32[32,4]{0,1:T(4,128)}, u32[]{:S(2)}) copy-start(s32[32,4]{0,1:T(4,128)} %param.12) | copy-start | bytes 1540
  74.3 13.4 %copy-start.4 = (bf16[4,1600,384]{2,1,0:T(8,128)(2,1)}, bf16[4,1600,384]{2,1,0:T(8,128)(2,1)S(1)}, u32[]{:S(2)}) copy-start(bf16[4,1600,384]{2,1,0:T(8,128)(2,1)S(1)} %collective-permute-done.13.refs_3_) | copy-start | bytes 14745604
  74.3 16.9 %collective-permute-start.16 = (bf16[2,1600,384]{2,1,0:T(8,128)(2,1)}, bf16[2,1600,384]{2,1,0:T(8,128)(2,1)}, u32[]{:S(2)}, u32[]{:S(2)}) collective-permute-start(bf16[2,1600,384]{2,1,0:T(8,128)(2,1)} %shard_map.84.refs_4_), channel_id=1, source_target_pairs={{0,1},{1,0},{2,3},{3,2},{4,5},{5,4},{6,7},{7,6},{8,9},{9,8},{10,11... | collective-permute-start | bytes 7372808 | tf_op jit(solution)/shard_map/ppermute | solution.py:293
  74.3 11.8 %collective-permute-start.17 = (bf16[625,256]{1,0:T(8,128)(2,1)S(1)}, bf16[625,256]{1,0:T(8,128)(2,1)S(1)}, u32[]{:S(2)}, u32[]{:S(2)}) collective-permute-start(bf16[625,256]{1,0:T(8,128)(2,1)S(1)} %collective-permute-done.15.refs_2_), channel_id=1, source_target_pairs={{0,2},{1,3},{2,4},{3,5},{4,6},{5,7},{6,0},{7,1},{8,10},{9,11},{10,... | collective-permute-start | bytes 960008 | tf_op jit(solution)/shard_map/ppermute | solution.py:296
  87.6 3.6 %collective-permute-start.18 = (bf16[8,800,128]{2,1,0:T(8,128)(2,1)S(1)}, bf16[8,800,128]{2,1,0:T(8,128)(2,1)S(1)}, u32[]{:S(2)}, u32[]{:S(2)}) collective-permute-start(bf16[8,800,128]{2,1,0:T(8,128)(2,1)S(1)} %shard_map.85.refs_6_), channel_id=1, source_target_pairs={{0,1},{1,0},{2,3},{3,2},{4,5},{5,4},{6,7},{7,6},{8,9},{9,8},{10,11... | collective-permute-start | bytes 4915208 | tf_op jit(solution)/shard_map/ppermute | solution.py:293
  91.2 1.3 copy-start.1
  102.8 33.5 %collective-permute-start.20 = (bf16[2,625,128]{2,1,0:T(8,128)(2,1)S(1)}, bf16[2,625,128]{2,1,0:T(8,128)(2,1)S(1)}, u32[]{:S(2)}, u32[]{:S(2)}) collective-permute-start(bf16[2,625,128]{2,1,0:T(8,128)(2,1)S(1)} %bitcast.26), channel_id=1, source_target_pairs={{0,6},{1,7},{2,0},{3,1},{4,2},{5,3},{6,4},{7,5},{8,14},{9,15},{10,... | collective-permute-start | bytes 960008 | tf_op jit(solution)/shard_map/ppermute | solution.py:296
  113.4 24.5 %collective-permute-start.19 = (bf16[2,625,128]{2,1,0:T(8,128)(2,1)S(1)}, bf16[2,625,128]{2,1,0:T(8,128)(2,1)S(1)}, u32[]{:S(2)}, u32[]{:S(2)}) collective-permute-start(bf16[2,625,128]{2,1,0:T(8,128)(2,1)S(1)} %bitcast.27), channel_id=1, source_target_pairs={{0,4},{1,5},{2,6},{3,7},{4,0},{5,1},{6,2},{7,3},{8,12},{9,13},{10,... | collective-permute-start | bytes 960008 | tf_op jit(solution)/shard_map/ppermute | solution.py:296
  123.8 14.1 %copy-start.5 = (f32[2,128,625]{1,0,2:T(2,128)S(1)}, f32[2,128,625]{1,0,2:T(2,128)}, u32[]{:S(2)}) copy-start(f32[2,128,625]{1,0,2:T(2,128)} %param.10) | copy-start | bytes 1920004
  123.8 14.0 %collective-permute-start.21 = (bf16[2,625,128]{2,1,0:T(8,128)(2,1)S(1)}, bf16[2,625,128]{2,1,0:T(8,128)(2,1)S(1)}, u32[]{:S(2)}, u32[]{:S(2)}) collective-permute-start(bf16[2,625,128]{2,1,0:T(8,128)(2,1)S(1)} %bitcast.28), channel_id=1, source_target_pairs={{0,2},{1,3},{2,4},{3,5},{4,6},{5,7},{6,0},{7,1},{8,10},{9,11},{10,... | collective-permute-start | bytes 960008 | tf_op jit(solution)/shard_map/ppermute | solution.py:296

commit v8 on v7

--- a/solution.py
+++ b/solution.py
@@ -306,26 +306,26 @@
         first_side = lambda x: lax.ppermute(x, ("pair", "task"), sides[0])
         second_side = lambda x: lax.ppermute(x, ("pair", "task"), sides[1])
         made_forms = lambda *parts: prepare(parts, column[None], matrix)
+        own = amplitudes.transpose(2, 0, 1).reshape(TV * TV, blocks_here * pairs)
+        amp1 = around(own, 1)
         part0 = mine[0]
         a0, b0, part1, part3 = first_side(part0), second_side(part0), around(mine[1], 1), around(mine[3], 3)
 
-        a0, b0, part0, part1, part3, to2 = after((a0, b0, part0, part1, part3, mine[2]), ())
+        a0, b0, part0, part1, part3, amp1, to2 = after((a0, b0, part0, part1, part3, amp1, mine[2]), ())
         part13 = jnp.concatenate([part1, part3], axis=0)
         q0, a13, b13, part2 = second_side(a0), first_side(part13), second_side(part13), around(to2, 2)
 
-        own = amplitudes.transpose(2, 0, 1).reshape(TV * TV, blocks_here * pairs)
         own, q0, a13, b13, part2, part13 = after((own, q0, a13, b13, part2, part13), ())
-        q13, a2, b2, amp1 = second_side(a13), first_side(part2), second_side(part2), around(own, 1)
+        q13, a2, b2, amp2 = second_side(a13), first_side(part2), second_side(part2), around(own, 2)
         forms0 = made_forms(part0, a0, b0, q0)
         far0 = other_core(forms0)
 
-        q13, a2, b2, amp1 = after((q13, a2, b2, amp1), forms0)
-        q2, amp2 = second_side(a2), around(amp1, 1)
+        q13, a2, b2, own, amp2 = after((q13, a2, b2, own, amp2), forms0)
+        q2, amp3 = second_side(a2), around(own, 3)
         forms13 = made_forms(part13, a13, b13, q13)
         far13 = other_core(after(forms13, far0))
 
-        q2, amp2 = after((q2, amp2), forms13)
-        amp3 = around(amp2, 1)
+        q2 = after(q2, forms13)
         forms2 = made_forms(part2, a2, b2, q2)
         far2 = other_core(after(forms2, far13))
         amps = prepare_amps([own, amp1, amp2, after(amp3, forms2)], blocks_here, jnp.asarray(amp_matrix()))

time: 140 us -> 143 us (1.021)
  starting transfers between devices: 22.7 us -> 25.4 us
  local copies, waits for them, and re-layouts: 6.48 us -> 8.97 us
  waiting for transfers between devices: 54.9 us -> 53.2 us
    ppermute x9, waiting for transfers between devices: 36.5 us -> 32.9 us  [around(): lax.ppermute(x, 'task', [(c, (c + 2 * by) % task_count) for c in range(ta...]
    ppermute x9, starting transfers between devices: 11.7 us -> 14.2 us  [around(): lax.ppermute(x, 'task', [(c, (c + 2 * by) % task_count) for c in range(ta...]
    unnamed x24, local copies, waits for them, and re-layouts: 5.17 us -> 7.66 us
    ppermute x6, waiting for transfers between devices: 15 us -> 17 us  [per_device(): second_side = lambda x: lax.ppermute(x, ('pair', 'task'), sides[1])]
  transfers between devices with their start and end apart: 22 -> 22, of which waited for: 10 -> 10; matrix products, arithmetic and copies ran while one was open for 0% -> 3% of each run, Pallas kernels for 30% -> 29%
where the time goes in v8:
time: 143 us
  Pallas kernels  54.7 us (38%)
  waiting for transfers between devices  53.2 us (37%)
  starting transfers between devices  25.4 us (18%)
  local copies, waits for them, and re-layouts  8.97 us (6%)
    pallas_call x4, Pallas kernels, ladders(): pl.pallas_call(functools.partial(ladder_kernel, find, made, len(tiles)),...  41.4 us
    ppermute x9, waiting for transfers between devices, around(): lax.ppermute(x, 'task', [(c, (c + 2 * by) % task_count) for c in range(ta...  32.9 us
    ppermute x6, waiting for transfers between devices, per_device(): second_side = lambda x: lax.ppermute(x, ('pair', 'task'), sides[1])  17 us
    ppermute x9, starting transfers between devices, around(): lax.ppermute(x, 'task', [(c, (c + 2 * by) % task_count) for c in range(ta...  14.2 us
    pallas_call x3, Pallas kernels, prepare(): pl.pallas_call(prepare_kernel, out_shape=jax.ShapeDtypeStruct((count, mat...  11.9 us
    unnamed x24, local copies, waits for them, and re-layouts  7.66 us
    ppermute x6, starting transfers between devices, per_device(): second_side = lambda x: lax.ppermute(x, ('pair', 'task'), sides[1])  7.38 us
    ppermute x3, starting transfers between devices, per_device(): first_side = lambda x: lax.ppermute(x, ('pair', 'task'), sides[0])  3.52 us
  transfers between devices with their start and end apart: 22, of which 10 were waited for; matrix products, arithmetic and copies ran while one was open for 3% of the time, Pallas kernels for 29%

profile of v8, /device:TPU:0, one launch (start us, length us, event | category | flops | bytes accessed | tf_op | source)
XLA Modules:
  0.0 142.7 jit_solution(15809053869544904634)
XLA Ops:
  0.0 1.2 pad
  1.3 3.1 %collective-permute-start.4 = (bf16[625,256]{1,0:T(8,128)(2,1)S(1)}, bf16[625,256]{1,0:T(8,128)(2,1)S(1)}, u32[]{:S(2)}, u32[]{:S(2)}) collective-permute-start(bf16[625,256]{1,0:T(8,128)(2,1)S(1)} %bitcast.24), channel_id=1, source_target_pairs={{0,2},{1,3},{2,4},{3,5},{4,6},{5,7},{6,0},{7,1},{8,10},{9,11},{10,... | collective-permute-start | bytes 960008 | tf_op jit(solution)/shard_map/ppermute | solution.py:296
  4.4 3.3 %copy.23 = bf16[2,384,625]{2,1,0:T(8,128)(2,1)S(1)} copy(bf16[2,384,625]{1,0,2:T(2,128)(2,1)} %param.8) | data formatting | bytes 1920000 | tf_op args[0]
  7.7 0.1 dynamic-slice_bitcast_fusion
  7.8 2.2 %collective-permute-start.3 = (bf16[2,96,625]{2,1,0:T(8,128)(2,1)S(1)}, bf16[2,96,625]{2,1,0:T(8,128)(2,1)S(1)}, u32[]{:S(2)}, u32[]{:S(2)}) collective-permute-start(bf16[2,96,625]{2,1,0:T(8,128)(2,1)S(1)} %get-tuple-element.50), channel_id=1, source_target_pairs={{0,6},{1,7},{2,0},{3,1},{4,2},{5,3},{6,4},{7,5},{8,14},{9,15},{10,... | collective-permute-start | bytes 720008 | tf_op jit(solution)/shard_map/ppermute | solution.py:296
  10.0 0.0 collective-permute-start.2
  10.0 1.6 %collective-permute-start.1 = (bf16[2,96,625]{2,1,0:T(8,128)(2,1)S(1)}, bf16[2,96,625]{2,1,0:T(8,128)(2,1)S(1)}, u32[]{:S(2)}, u32[]{:S(2)}) collective-permute-start(bf16[2,96,625]{2,1,0:T(8,128)(2,1)S(1)} %get-tuple-element.27.refs_0_), channel_id=1, source_target_pairs={{0,16},{1,9},{2,18},{3,11},{4,20},{5,13},{6,22},{7,15},{8,24},{9,1... | collective-permute-start | bytes 720008 | tf_op jit(solution)/shard_map/ppermute | solution.py:307
  11.7 1.5 %collective-permute-start = (bf16[2,96,625]{2,1,0:T(8,128)(2,1)S(1)}, bf16[2,96,625]{2,1,0:T(8,128)(2,1)S(1)}, u32[]{:S(2)}, u32[]{:S(2)}) collective-permute-start(bf16[2,96,625]{2,1,0:T(8,128)(2,1)S(1)} %get-tuple-element.27.refs_0_), channel_id=1, source_target_pairs={{0,8},{1,17},{2,10},{3,19},{4,12},{5,21},{6,14},{7,23},{8,0},{9,25... | collective-permute-start | bytes 720008 | tf_op jit(solution)/shard_map/ppermute | solution.py:306
  13.2 6.9 %collective-permute-done.3 = bf16[2,96,625]{2,1,0:T(8,128)(2,1)S(1)} collective-permute-done((bf16[2,96,625]{2,1,0:T(8,128)(2,1)S(1)}, bf16[2,96,625]{2,1,0:T(8,128)(2,1)S(1)}, u32[]{:S(2)}, u32[]{:S(2)}) %collective-permute-start.3) | collective-permute-done | bytes 240032 | tf_op jit(solution)/shard_map/ppermute | solution.py:296
  20.1 4.5 %collective-permute-done.2 = bf16[2,96,625]{2,1,0:T(8,128)(2,1)S(1)} collective-permute-done((bf16[2,96,625]{2,1,0:T(8,128)(2,1)S(1)}, bf16[2,96,625]{2,1,0:T(8,128)(2,1)S(1)}, u32[]{:S(2)}, u32[]{:S(2)}) %collective-permute-start.2) | collective-permute-done | bytes 240032 | tf_op jit(solution)/shard_map/ppermute | solution.py:296
  24.6 0.0 collective-permute-done.1.refs_2_
  24.6 0.0 collective-permute-done.refs_1_
  24.6 0.0 collective-permute-done.4.refs_1_
  24.7 1.6 %collective-permute-start.7 = (bf16[4,96,625]{2,1,0:T(8,128)(2,1)S(1)}, bf16[4,96,625]{2,1,0:T(8,128)(2,1)S(1)}, u32[]{:S(2)}, u32[]{:S(2)}) collective-permute-start(bf16[4,96,625]{2,1,0:T(8,128)(2,1)S(1)} %constant_dynamic-update-slice_fusion.refs_0_), channel_id=1, source_target_pairs={{0,16},{1,9},{2,18},{3,11},{4,20},{5,13},{6,22},{7,15},{8,24},{9,1... | collective-permute-start | bytes 1440008 | tf_op jit(solution)/shard_map/ppermute | solution.py:307
  26.3 1.5 %collective-permute-start.6 = (bf16[4,96,625]{2,1,0:T(8,128)(2,1)S(1)}, bf16[4,96,625]{2,1,0:T(8,128)(2,1)S(1)}, u32[]{:S(2)}, u32[]{:S(2)}) collective-permute-start(bf16[4,96,625]{2,1,0:T(8,128)(2,1)S(1)} %constant_dynamic-update-slice_fusion.refs_0_), channel_id=1, source_target_pairs={{0,8},{1,17},{2,10},{3,19},{4,12},{5,21},{6,14},{7,23},{8,0},{9,25... | collective-permute-start | bytes 1440008 | tf_op jit(solution)/shard_map/ppermute | solution.py:306
  27.7 0.7 collective-permute-start.8
  28.4 0.5 collective-permute-start.5
  28.9 10.4 %collective-permute-done.8.refs_0_ = bf16[2,96,625]{2,1,0:T(8,128)(2,1)S(1)} collective-permute-done((bf16[2,96,625]{2,1,0:T(8,128)(2,1)S(1)}, bf16[2,96,625]{2,1,0:T(8,128)(2,1)S(1)}, u32[]{:S(2)}, u32[]{:S(2)}) %collective-permute-start.8) | collective-permute-done | bytes 240032 | tf_op jit(solution)/shard_map/ppermute | solution.py:296
  39.3 1.4 collective-permute-done.5.refs_3_
  40.7 0.0 collective-permute-done.7.refs_2_
  40.7 0.0 collective-permute-done.6.refs_1_
  40.7 1.6 %copy-done.3 = bf16[1600,625]{1,0:T(8,128)(2,1)S(1)} copy-done((bf16[1600,625]{1,0:T(8,128)(2,1)S(1)}, bf16[1600,625]{1,0:T(8,128)(2,1)}, u32[]{:S(2)}) %copy-start.3) | copy-done | bytes 2000024
  42.3 2.6 %shard_map.82.refs_0_ = bf16[2,1600,384]{2,1,0:T(8,128)(2,1)S(1)} custom-call(s32[1]{0:T(128)} %bitcast.column_ref, bf16[2,96,625]{2,1,0:T(8,128)(2,1)S(1)} %get-tuple-element.27.refs_0_, bf16[2,96,625]{2,1,0:T(8,128)(2,1)S(1)} %collective-permute-done.refs_1_, bf16[2,96,625]{2,1,0:T(8,128)(2,1)S(1)} %collective-permute-done.1.refs_2_, ...), custom_call_target="tpu_custom_call" | custom-call | flops 1536000000 | bytes 3417600 | tf_op jit(solution)/shard_map/pallas_call | solution.py:77
  45.0 0.1 collective-permute-start.9
  45.1 1.6 %collective-permute-start.10 = (bf16[4,96,625]{2,1,0:T(8,128)(2,1)S(1)}, bf16[4,96,625]{2,1,0:T(8,128)(2,1)S(1)}, u32[]{:S(2)}, u32[]{:S(2)}) collective-permute-start(bf16[4,96,625]{2,1,0:T(8,128)(2,1)S(1)} %collective-permute-done.6.refs_1_), channel_id=1, source_target_pairs={{0,16},{1,9},{2,18},{3,11},{4,20},{5,13},{6,22},{7,15},{8,24},{9,1... | collective-permute-start | bytes 1440008 | tf_op jit(solution)/shard_map/ppermute | solution.py:307
  46.6 0.6 collective-permute-start.13
  47.3 0.5 collective-permute-start.12
  47.8 0.5 collective-permute-start.11
  48.3 10.9 %collective-permute-done.12.refs_2_ = bf16[2,96,625]{2,1,0:T(8,128)(2,1)S(1)} collective-permute-done((bf16[2,96,625]{2,1,0:T(8,128)(2,1)S(1)}, bf16[2,96,625]{2,1,0:T(8,128)(2,1)S(1)}, u32[]{:S(2)}, u32[]{:S(2)}) %collective-permute-start.12) | collective-permute-done | bytes 240032 | tf_op jit(solution)/shard_map/ppermute | solution.py:307
  59.2 0.0 collective-permute-done.11.refs_1_
  59.2 3.0 %collective-permute-done.13.refs_2_ = bf16[625,256]{1,0:T(8,128)(2,1)S(1)} collective-permute-done((bf16[625,256]{1,0:T(8,128)(2,1)S(1)}, bf16[625,256]{1,0:T(8,128)(2,1)S(1)}, u32[]{:S(2)}, u32[]{:S(2)}) %collective-permute-start.13) | collective-permute-done | bytes 320032 | tf_op jit(solution)/shard_map/ppermute | solution.py:296
  62.3 0.0 collective-permute-done.10.refs_3_
  62.3 5.8 %shard_map.83.refs_2_ = bf16[4,1600,384]{2,1,0:T(8,128)(2,1)} custom-call(s32[1]{0:T(128)} %bitcast.column_ref, bf16[4,96,625]{2,1,0:T(8,128)(2,1)S(1)} %constant_dynamic-update-slice_fusion.refs_0_, bf16[4,96,625]{2,1,0:T(8,128)(2,1)S(1)} %collective-permute-done.6.refs_1_, bf16[4,96,625]{2,1,0:T(8,128)(2,1)S(1)} %collective-permute-done.7.refs_2_, ...), custom_call_target="tpu_custom_call" | custom-call | flops 3072000000 | bytes 6835200 | tf_op jit(solution)/shard_map/pallas_call | solution.py:77
  68.1 0.0 collective-permute-done.9.refs_1_
  68.1 0.1 collective-permute-start.14
  68.2 1.6 %collective-permute-start.15 = (bf16[2,96,625]{2,1,0:T(8,128)(2,1)S(1)}, bf16[2,96,625]{2,1,0:T(8,128)(2,1)S(1)}, u32[]{:S(2)}, u32[]{:S(2)}) collective-permute-start(bf16[2,96,625]{2,1,0:T(8,128)(2,1)S(1)} %collective-permute-done.11.refs_1_), channel_id=1, source_target_pairs={{0,16},{1,9},{2,18},{3,11},{4,20},{5,13},{6,22},{7,15},{8,24},{9,1... | collective-permute-start | bytes 720008 | tf_op jit(solution)/shard_map/ppermute | solution.py:307
  69.8 4.7 %collective-permute-done.15.refs_3_ = bf16[2,96,625]{2,1,0:T(8,128)(2,1)S(1)} collective-permute-done((bf16[2,96,625]{2,1,0:T(8,128)(2,1)S(1)}, bf16[2,96,625]{2,1,0:T(8,128)(2,1)S(1)}, u32[]{:S(2)}, u32[]{:S(2)}) %collective-permute-start.15) | collective-permute-done | bytes 240032 | tf_op jit(solution)/shard_map/ppermute | solution.py:307
  74.5 3.4 %shard_map.84.refs_4_ = bf16[2,1600,384]{2,1,0:T(8,128)(2,1)} custom-call(s32[1]{0:T(128)} %bitcast.column_ref, bf16[2,96,625]{2,1,0:T(8,128)(2,1)S(1)} %collective-permute-done.8.refs_0_, bf16[2,96,625]{2,1,0:T(8,128)(2,1)S(1)} %collective-permute-done.11.refs_1_, bf16[2,96,625]{2,1,0:T(8,128)(2,1)S(1)} %collective-permute-done.12.refs_2_, ...), custom_call_target="tpu_custom_call" | custom-call | flops 1536000000 | bytes 3417600 | tf_op jit(solution)/shard_map/pallas_call | solution.py:77
  77.9 0.0 copy-done.5
  77.9 0.0 collective-permute-done.14.refs_3_
  77.9 0.1 collective-permute-start.16
  78.0 2.5 %collective-permute-start.17 = (bf16[625,256]{1,0:T(8,128)(2,1)S(1)}, bf16[625,256]{1,0:T(8,128)(2,1)S(1)}, u32[]{:S(2)}, u32[]{:S(2)}) collective-permute-start(bf16[625,256]{1,0:T(8,128)(2,1)S(1)} %bitcast.26), channel_id=1, source_target_pairs={{0,6},{1,7},{2,0},{3,1},{4,2},{5,3},{6,4},{7,5},{8,14},{9,15},{10,... | collective-permute-start | bytes 960008 | tf_op jit(solution)/shard_map/ppermute | solution.py:296
  80.5 7.6 %collective-permute-done.17.refs_3_ = bf16[625,256]{1,0:T(8,128)(2,1)S(1)} collective-permute-done((bf16[625,256]{1,0:T(8,128)(2,1)S(1)}, bf16[625,256]{1,0:T(8,128)(2,1)S(1)}, u32[]{:S(2)}, u32[]{:S(2)}) %collective-permute-start.17) | collective-permute-done | bytes 320032 | tf_op jit(solution)/shard_map/ppermute | solution.py:296
  88.0 0.0 copy-done.2
  88.0 1.4 %shard_map.85.refs_6_ = bf16[8,800,128]{2,1,0:T(8,128)(2,1)S(1)} custom-call(bf16[800,625]{1,0:T(8,128)(2,1)S(1)} %copy-done.2, bf16[625,256]{1,0:T(8,128)(2,1)S(1)} %bitcast.27, bf16[625,256]{1,0:T(8,128)(2,1)S(1)} %collective-permute-done.4.refs_1_, bf16[625,256]{1,0:T(8,128)(2,1)S(1)} %collective-permute-done.13.refs_2_, ...), custom_call_target="tpu_custom_call" | custom-call | flops 1024000000 | bytes 2560000 | tf_op jit(solution)/shard_map/pallas_call | solution.py:108
  89.5 0.1 collective-permute-start.18
  89.6 0.1 copy.24.owners_ref
  89.6 0.1 copy.25.local_ref
  89.7 3.3 %collective-permute-done.18.refs_7_ = bf16[8,800,128]{2,1,0:T(8,128)(2,1)S(1)} collective-permute-done((bf16[8,800,128]{2,1,0:T(8,128)(2,1)S(1)}, bf16[8,800,128]{2,1,0:T(8,128)(2,1)S(1)}, u32[]{:S(2)}, u32[]{:S(2)}) %collective-permute-start.18) | collective-permute-done | bytes 1638432 | tf_op jit(solution)/shard_map/ppermute | solution.py:293
  93.0 0.0 collective-permute-done.16.refs_5_
  93.0 1.3 copy-done.1
  94.3 10.3 %shard_map.87 = bf16[1,2,625,128]{3,2,1,0:T(8,128)(2,1)S(1)} custom-call(s32[1]{0:T(128)} %bitcast.column_ref, s32[32,3]{1,0:T(8,128)S(1)} %copy.24.owners_ref, s32[32,4]{1,0:T(8,128)S(1)} %copy.25.local_ref, bf16[2,1600,384]{2,1,0:T(8,128)(2,1)} %copy-done, bf16[2,1600,384]{2,1,0:T(8,128)(2,1)} %copy-done.5, bf16[4,1600,384]{2,1,0:T(8,128)(2,1)} %shard_map.83.refs_2_, ...), custom_call_target="tpu_custom_call" | custom-call | flops 2936012800 | bytes 6553600 | tf_op jit(solution)/shard_map/pallas_call | solution.py:258
  104.6 4.5 %collective-permute-start.20 = (bf16[2,625,128]{2,1,0:T(8,128)(2,1)S(1)}, bf16[2,625,128]{2,1,0:T(8,128)(2,1)S(1)}, u32[]{:S(2)}, u32[]{:S(2)}) collective-permute-start(bf16[2,625,128]{2,1,0:T(8,128)(2,1)S(1)} %bitcast.28), channel_id=1, source_target_pairs={{0,6},{1,7},{2,0},{3,1},{4,2},{5,3},{6,4},{7,5},{8,14},{9,15},{10,... | collective-permute-start | bytes 960008 | tf_op jit(solution)/shard_map/ppermute | solution.py:296
  109.1 10.3 %shard_map.86 = bf16[1,2,625,128]{3,2,1,0:T(8,128)(2,1)S(1)} custom-call(s32[1]{0:T(128)} %bitcast.column_ref, s32[32,3]{1,0:T(8,128)S(1)} %copy.24.owners_ref, s32[32,4]{1,0:T(8,128)S(1)} %copy.25.local_ref, bf16[2,1600,384]{2,1,0:T(8,128)(2,1)} %copy-done, bf16[2,1600,384]{2,1,0:T(8,128)(2,1)} %copy-done.5, bf16[4,1600,384]{2,1,0:T(8,128)(2,1)} %shard_map.83.refs_2_, ...), custom_call_target="tpu_custom_call" | custom-call | flops 2936012800 | bytes 6553600 | tf_op jit(solution)/shard_map/pallas_call | solution.py:258
  119.4 0.1 collective-permute-start.19
  119.5 10.4 %shard_map.88 = bf16[1,2,625,128]{3,2,1,0:T(8,128)(2,1)S(1)} custom-call(s32[1]{0:T(128)} %bitcast.column_ref, s32[32,3]{1,0:T(8,128)S(1)} %copy.24.owners_ref, s32[32,4]{1,0:T(8,128)S(1)} %copy.25.local_ref, bf16[2,1600,384]{2,1,0:T(8,128)(2,1)} %copy-done, bf16[2,1600,384]{2,1,0:T(8,128)(2,1)} %copy-done.5, bf16[4,1600,384]{2,1,0:T(8,128)(2,1)} %shard_map.83.refs_2_, ...), custom_call_target="tpu_custom_call" | custom-call | flops 2936012800 | bytes 6553600 | tf_op jit(solution)/shard_map/pallas_call | solution.py:258
  129.9 0.0 copy-start.6
  129.9 0.6 collective-permute-start.21
  130.5 10.3 %shard_map.89 = bf16[1,2,625,128]{3,2,1,0:T(8,128)(2,1)S(1)} custom-call(s32[1]{0:T(128)} %bitcast.column_ref, s32[32,3]{1,0:T(8,128)S(1)} %copy.24.owners_ref, s32[32,4]{1,0:T(8,128)S(1)} %copy.25.local_ref, bf16[2,1600,384]{2,1,0:T(8,128)(2,1)} %copy-done, bf16[2,1600,384]{2,1,0:T(8,128)(2,1)} %copy-done.5, bf16[4,1600,384]{2,1,0:T(8,128)(2,1)} %shard_map.83.refs_2_, ...), custom_call_target="tpu_custom_call" | custom-call | flops 2936012800 | bytes 6553600 | tf_op jit(solution)/shard_map/pallas_call | solution.py:258
  140.8 0.0 collective-permute-done.20
  140.9 0.5 collective-permute-done.19
  141.3 0.0 collective-permute-done.21
  141.3 0.2 fusion.1
  141.5 1.2 copy.33
  (16 shorter events, 0.1 us)
Async XLA Ops:
  1.3 23.3 %collective-permute-start.4 = (bf16[625,256]{1,0:T(8,128)(2,1)S(1)}, bf16[625,256]{1,0:T(8,128)(2,1)S(1)}, u32[]{:S(2)}, u32[]{:S(2)}) collective-permute-start(bf16[625,256]{1,0:T(8,128)(2,1)S(1)} %bitcast.24), channel_id=1, source_target_pairs={{0,2},{1,3},{2,4},{3,5},{4,6},{5,7},{6,0},{7,1},{8,10},{9,11},{10,... | collective-permute-start | bytes 960008 | tf_op jit(solution)/shard_map/ppermute | solution.py:296
  7.8 12.2 %collective-permute-start.3 = (bf16[2,96,625]{2,1,0:T(8,128)(2,1)S(1)}, bf16[2,96,625]{2,1,0:T(8,128)(2,1)S(1)}, u32[]{:S(2)}, u32[]{:S(2)}) collective-permute-start(bf16[2,96,625]{2,1,0:T(8,128)(2,1)S(1)} %get-tuple-element.50), channel_id=1, source_target_pairs={{0,6},{1,7},{2,0},{3,1},{4,2},{5,3},{6,4},{7,5},{8,14},{9,15},{10,... | collective-permute-start | bytes 720008 | tf_op jit(solution)/shard_map/ppermute | solution.py:296
  10.0 14.5 %collective-permute-start.2 = (bf16[2,96,625]{2,1,0:T(8,128)(2,1)S(1)}, bf16[2,96,625]{2,1,0:T(8,128)(2,1)S(1)}, u32[]{:S(2)}, u32[]{:S(2)}) collective-permute-start(bf16[2,96,625]{2,1,0:T(8,128)(2,1)S(1)} %get-tuple-element.51), channel_id=1, source_target_pairs={{0,2},{1,3},{2,4},{3,5},{4,6},{5,7},{6,0},{7,1},{8,10},{9,11},{10,... | collective-permute-start | bytes 720008 | tf_op jit(solution)/shard_map/ppermute | solution.py:296
  10.0 14.5 %collective-permute-start.1 = (bf16[2,96,625]{2,1,0:T(8,128)(2,1)S(1)}, bf16[2,96,625]{2,1,0:T(8,128)(2,1)S(1)}, u32[]{:S(2)}, u32[]{:S(2)}) collective-permute-start(bf16[2,96,625]{2,1,0:T(8,128)(2,1)S(1)} %get-tuple-element.27.refs_0_), channel_id=1, source_target_pairs={{0,16},{1,9},{2,18},{3,11},{4,20},{5,13},{6,22},{7,15},{8,24},{9,1... | collective-permute-start | bytes 720008 | tf_op jit(solution)/shard_map/ppermute | solution.py:307
  11.7 12.9 %collective-permute-start = (bf16[2,96,625]{2,1,0:T(8,128)(2,1)S(1)}, bf16[2,96,625]{2,1,0:T(8,128)(2,1)S(1)}, u32[]{:S(2)}, u32[]{:S(2)}) collective-permute-start(bf16[2,96,625]{2,1,0:T(8,128)(2,1)S(1)} %get-tuple-element.27.refs_0_), channel_id=1, source_target_pairs={{0,8},{1,17},{2,10},{3,19},{4,12},{5,21},{6,14},{7,23},{8,0},{9,25... | collective-permute-start | bytes 720008 | tf_op jit(solution)/shard_map/ppermute | solution.py:306
  24.7 16.1 %collective-permute-start.7 = (bf16[4,96,625]{2,1,0:T(8,128)(2,1)S(1)}, bf16[4,96,625]{2,1,0:T(8,128)(2,1)S(1)}, u32[]{:S(2)}, u32[]{:S(2)}) collective-permute-start(bf16[4,96,625]{2,1,0:T(8,128)(2,1)S(1)} %constant_dynamic-update-slice_fusion.refs_0_), channel_id=1, source_target_pairs={{0,16},{1,9},{2,18},{3,11},{4,20},{5,13},{6,22},{7,15},{8,24},{9,1... | collective-permute-start | bytes 1440008 | tf_op jit(solution)/shard_map/ppermute | solution.py:307
  26.3 14.5 %collective-permute-start.6 = (bf16[4,96,625]{2,1,0:T(8,128)(2,1)S(1)}, bf16[4,96,625]{2,1,0:T(8,128)(2,1)S(1)}, u32[]{:S(2)}, u32[]{:S(2)}) collective-permute-start(bf16[4,96,625]{2,1,0:T(8,128)(2,1)S(1)} %constant_dynamic-update-slice_fusion.refs_0_), channel_id=1, source_target_pairs={{0,8},{1,17},{2,10},{3,19},{4,12},{5,21},{6,14},{7,23},{8,0},{9,25... | collective-permute-start | bytes 1440008 | tf_op jit(solution)/shard_map/ppermute | solution.py:306
  27.7 11.6 %collective-permute-start.8 = (bf16[2,96,625]{2,1,0:T(8,128)(2,1)S(1)}, bf16[2,96,625]{2,1,0:T(8,128)(2,1)S(1)}, u32[]{:S(2)}, u32[]{:S(2)}) collective-permute-start(bf16[2,96,625]{2,1,0:T(8,128)(2,1)S(1)} %get-tuple-element.32), channel_id=1, source_target_pairs={{0,4},{1,5},{2,6},{3,7},{4,0},{5,1},{6,2},{7,3},{8,12},{9,13},{10,... | collective-permute-start | bytes 720008 | tf_op jit(solution)/shard_map/ppermute | solution.py:296
  28.4 12.3 %collective-permute-start.5 = (bf16[2,96,625]{2,1,0:T(8,128)(2,1)S(1)}, bf16[2,96,625]{2,1,0:T(8,128)(2,1)S(1)}, u32[]{:S(2)}, u32[]{:S(2)}) collective-permute-start(bf16[2,96,625]{2,1,0:T(8,128)(2,1)S(1)} %collective-permute-done.refs_1_), channel_id=1, source_target_pairs={{0,16},{1,9},{2,18},{3,11},{4,20},{5,13},{6,22},{7,15},{8,24},{9,1... | collective-permute-start | bytes 720008 | tf_op jit(solution)/shard_map/ppermute | solution.py:307
  40.7 1.6 %copy-start.3 = (bf16[1600,625]{1,0:T(8,128)(2,1)S(1)}, bf16[1600,625]{1,0:T(8,128)(2,1)}, u32[]{:S(2)}) copy-start(bf16[1600,625]{1,0:T(8,128)(2,1)} %constant.61.clone.refs_4_) | copy-start | bytes 6000004
  42.3 19.9 %copy-start.4 = (bf16[1600,625]{1,0:T(8,128)(2,1)S(1)}, bf16[1600,625]{1,0:T(8,128)(2,1)}, u32[]{:S(2)}) copy-start(bf16[1600,625]{1,0:T(8,128)(2,1)} %constant.61.clone.refs_4_) | copy-start | bytes 6000004
  45.0 23.1 %copy-start = (bf16[2,1600,384]{2,1,0:T(8,128)(2,1)}, bf16[2,1600,384]{2,1,0:T(8,128)(2,1)S(1)}, u32[]{:S(2)}) copy-start(bf16[2,1600,384]{2,1,0:T(8,128)(2,1)S(1)} %shard_map.82.refs_0_) | copy-start | bytes 7372804
  45.0 23.1 %collective-permute-start.9 = (bf16[2,1600,384]{2,1,0:T(8,128)(2,1)S(1)}, bf16[2,1600,384]{2,1,0:T(8,128)(2,1)S(1)}, u32[]{:S(2)}, u32[]{:S(2)}) collective-permute-start(bf16[2,1600,384]{2,1,0:T(8,128)(2,1)S(1)} %shard_map.82.refs_0_), channel_id=1, source_target_pairs={{0,1},{1,0},{2,3},{3,2},{4,5},{5,4},{6,7},{7,6},{8,9},{9,8},{10,11... | collective-permute-start | bytes 7372808 | tf_op jit(solution)/shard_map/ppermute | solution.py:293
  45.1 17.2 %collective-permute-start.10 = (bf16[4,96,625]{2,1,0:T(8,128)(2,1)S(1)}, bf16[4,96,625]{2,1,0:T(8,128)(2,1)S(1)}, u32[]{:S(2)}, u32[]{:S(2)}) collective-permute-start(bf16[4,96,625]{2,1,0:T(8,128)(2,1)S(1)} %collective-permute-done.6.refs_1_), channel_id=1, source_target_pairs={{0,16},{1,9},{2,18},{3,11},{4,20},{5,13},{6,22},{7,15},{8,24},{9,1... | collective-permute-start | bytes 1440008 | tf_op jit(solution)/shard_map/ppermute | solution.py:307
  46.6 15.6 %collective-permute-start.13 = (bf16[625,256]{1,0:T(8,128)(2,1)S(1)}, bf16[625,256]{1,0:T(8,128)(2,1)S(1)}, u32[]{:S(2)}, u32[]{:S(2)}) collective-permute-start(bf16[625,256]{1,0:T(8,128)(2,1)S(1)} %bitcast.25), channel_id=1, source_target_pairs={{0,4},{1,5},{2,6},{3,7},{4,0},{5,1},{6,2},{7,3},{8,12},{9,13},{10,... | collective-permute-start | bytes 960008 | tf_op jit(solution)/shard_map/ppermute | solution.py:296
  47.3 12.0 %collective-permute-start.12 = (bf16[2,96,625]{2,1,0:T(8,128)(2,1)S(1)}, bf16[2,96,625]{2,1,0:T(8,128)(2,1)S(1)}, u32[]{:S(2)}, u32[]{:S(2)}) collective-permute-start(bf16[2,96,625]{2,1,0:T(8,128)(2,1)S(1)} %collective-permute-done.8.refs_0_), channel_id=1, source_target_pairs={{0,16},{1,9},{2,18},{3,11},{4,20},{5,13},{6,22},{7,15},{8,24},{9,1... | collective-permute-start | bytes 720008 | tf_op jit(solution)/shard_map/ppermute | solution.py:307
  47.8 11.5 %collective-permute-start.11 = (bf16[2,96,625]{2,1,0:T(8,128)(2,1)S(1)}, bf16[2,96,625]{2,1,0:T(8,128)(2,1)S(1)}, u32[]{:S(2)}, u32[]{:S(2)}) collective-permute-start(bf16[2,96,625]{2,1,0:T(8,128)(2,1)S(1)} %collective-permute-done.8.refs_0_), channel_id=1, source_target_pairs={{0,8},{1,17},{2,10},{3,19},{4,12},{5,21},{6,14},{7,23},{8,0},{9,25... | collective-permute-start | bytes 720008 | tf_op jit(solution)/shard_map/ppermute | solution.py:306
  68.1 19.9 %copy-start.2 = (bf16[800,625]{1,0:T(8,128)(2,1)S(1)}, bf16[800,625]{1,0:T(8,128)(2,1)}, u32[]{:S(2)}) copy-start(bf16[800,625]{1,0:T(8,128)(2,1)} %constant.63.clone.matrix_ref) | copy-start | bytes 3000004
  68.1 9.8 %copy-start.5 = (bf16[2,1600,384]{2,1,0:T(8,128)(2,1)}, bf16[2,1600,384]{2,1,0:T(8,128)(2,1)S(1)}, u32[]{:S(2)}) copy-start(bf16[2,1600,384]{2,1,0:T(8,128)(2,1)S(1)} %collective-permute-done.9.refs_1_) | copy-start | bytes 7372804
  68.1 9.8 %collective-permute-start.14 = (bf16[4,1600,384]{2,1,0:T(8,128)(2,1)}, bf16[4,1600,384]{2,1,0:T(8,128)(2,1)}, u32[]{:S(2)}, u32[]{:S(2)}) collective-permute-start(bf16[4,1600,384]{2,1,0:T(8,128)(2,1)} %shard_map.83.refs_2_), channel_id=1, source_target_pairs={{0,1},{1,0},{2,3},{3,2},{4,5},{5,4},{6,7},{7,6},{8,9},{9,8},{10,11... | collective-permute-start | bytes 14745608 | tf_op jit(solution)/shard_map/ppermute | solution.py:293
  68.2 6.3 %collective-permute-start.15 = (bf16[2,96,625]{2,1,0:T(8,128)(2,1)S(1)}, bf16[2,96,625]{2,1,0:T(8,128)(2,1)S(1)}, u32[]{:S(2)}, u32[]{:S(2)}) collective-permute-start(bf16[2,96,625]{2,1,0:T(8,128)(2,1)S(1)} %collective-permute-done.11.refs_1_), channel_id=1, source_target_pairs={{0,16},{1,9},{2,18},{3,11},{4,20},{5,13},{6,22},{7,15},{8,24},{9,1... | collective-permute-start | bytes 720008 | tf_op jit(solution)/shard_map/ppermute | solution.py:307
  77.9 11.6 %copy-start.7 = (s32[32,3]{0,1:T(4,128)S(1)}, s32[32,3]{0,1:T(4,128)}, u32[]{:S(2)}) copy-start(s32[32,3]{0,1:T(4,128)} %param.11) | copy-start | bytes 1156
  77.9 11.7 %copy-start.8 = (s32[32,4]{0,1:T(4,128)S(1)}, s32[32,4]{0,1:T(4,128)}, u32[]{:S(2)}) copy-start(s32[32,4]{0,1:T(4,128)} %param.12) | copy-start | bytes 1540
  77.9 15.1 %collective-permute-start.16 = (bf16[2,1600,384]{2,1,0:T(8,128)(2,1)}, bf16[2,1600,384]{2,1,0:T(8,128)(2,1)}, u32[]{:S(2)}, u32[]{:S(2)}) collective-permute-start(bf16[2,1600,384]{2,1,0:T(8,128)(2,1)} %shard_map.84.refs_4_), channel_id=1, source_target_pairs={{0,1},{1,0},{2,3},{3,2},{4,5},{5,4},{6,7},{7,6},{8,9},{9,8},{10,11... | collective-permute-start | bytes 7372808 | tf_op jit(solution)/shard_map/ppermute | solution.py:293
  78.0 10.0 %collective-permute-start.17 = (bf16[625,256]{1,0:T(8,128)(2,1)S(1)}, bf16[625,256]{1,0:T(8,128)(2,1)S(1)}, u32[]{:S(2)}, u32[]{:S(2)}) collective-permute-start(bf16[625,256]{1,0:T(8,128)(2,1)S(1)} %bitcast.26), channel_id=1, source_target_pairs={{0,6},{1,7},{2,0},{3,1},{4,2},{5,3},{6,4},{7,5},{8,14},{9,15},{10,... | collective-permute-start | bytes 960008 | tf_op jit(solution)/shard_map/ppermute | solution.py:296
  89.5 3.6 %collective-permute-start.18 = (bf16[8,800,128]{2,1,0:T(8,128)(2,1)S(1)}, bf16[8,800,128]{2,1,0:T(8,128)(2,1)S(1)}, u32[]{:S(2)}, u32[]{:S(2)}) collective-permute-start(bf16[8,800,128]{2,1,0:T(8,128)(2,1)S(1)} %shard_map.85.refs_6_), channel_id=1, source_target_pairs={{0,1},{1,0},{2,3},{3,2},{4,5},{5,4},{6,7},{7,6},{8,9},{9,8},{10,11... | collective-permute-start | bytes 4915208 | tf_op jit(solution)/shard_map/ppermute | solution.py:293
  93.0 1.3 copy-start.1
  104.6 36.2 %collective-permute-start.20 = (bf16[2,625,128]{2,1,0:T(8,128)(2,1)S(1)}, bf16[2,625,128]{2,1,0:T(8,128)(2,1)S(1)}, u32[]{:S(2)}, u32[]{:S(2)}) collective-permute-start(bf16[2,625,128]{2,1,0:T(8,128)(2,1)S(1)} %bitcast.28), channel_id=1, source_target_pairs={{0,6},{1,7},{2,0},{3,1},{4,2},{5,3},{6,4},{7,5},{8,14},{9,15},{10,... | collective-permute-start | bytes 960008 | tf_op jit(solution)/shard_map/ppermute | solution.py:296
  119.4 21.9 %collective-permute-start.19 = (bf16[2,625,128]{2,1,0:T(8,128)(2,1)S(1)}, bf16[2,625,128]{2,1,0:T(8,128)(2,1)S(1)}, u32[]{:S(2)}, u32[]{:S(2)}) collective-permute-start(bf16[2,625,128]{2,1,0:T(8,128)(2,1)S(1)} %bitcast.29), channel_id=1, source_target_pairs={{0,4},{1,5},{2,6},{3,7},{4,0},{5,1},{6,2},{7,3},{8,12},{9,13},{10,... | collective-permute-start | bytes 960008 | tf_op jit(solution)/shard_map/ppermute | solution.py:296
  129.9 11.4 %copy-start.6 = (f32[2,128,625]{1,0,2:T(2,128)S(1)}, f32[2,128,625]{1,0,2:T(2,128)}, u32[]{:S(2)}) copy-start(f32[2,128,625]{1,0,2:T(2,128)} %param.10) | copy-start | bytes 1920004
  129.9 11.4 %collective-permute-start.21 = (bf16[2,625,128]{2,1,0:T(8,128)(2,1)S(1)}, bf16[2,625,128]{2,1,0:T(8,128)(2,1)S(1)}, u32[]{:S(2)}, u32[]{:S(2)}) collective-permute-start(bf16[2,625,128]{2,1,0:T(8,128)(2,1)S(1)} %bitcast.30), channel_id=1, source_target_pairs={{0,2},{1,3},{2,4},{3,5},{4,6},{5,7},{6,0},{7,1},{8,10},{9,11},{10,... | collective-permute-start | bytes 960008 | tf_op jit(solution)/shard_map/ppermute | solution.py:296

commit v9 on v8

--- a/solution.py
+++ b/solution.py
@@ -314,21 +314,19 @@
         a0, b0, part0, part1, part3, amp1, to2 = after((a0, b0, part0, part1, part3, amp1, mine[2]), ())
         part13 = jnp.concatenate([part1, part3], axis=0)
         q0, a13, b13, part2 = second_side(a0), first_side(part13), second_side(part13), around(to2, 2)
-
-        own, q0, a13, b13, part2, part13 = after((own, q0, a13, b13, part2, part13), ())
+        forms0 = made_forms(part0, a0, b0, q0)
+
+        own, forms0, a13, b13, part2, part13 = after((own, forms0, a13, b13, part2, part13), ())
         q13, a2, b2, amp2 = second_side(a13), first_side(part2), second_side(part2), around(own, 2)
-        forms0 = made_forms(part0, a0, b0, q0)
         far0 = other_core(forms0)
-
-        q13, a2, b2, own, amp2 = after((q13, a2, b2, own, amp2), forms0)
+        forms13 = made_forms(part13, a13, b13, q13)
+
+        forms13, part2, a2, b2, own, amp2 = after((forms13, part2, a2, b2, own, amp2), ())
         q2, amp3 = second_side(a2), around(own, 3)
-        forms13 = made_forms(part13, a13, b13, q13)
         far13 = other_core(after(forms13, far0))
-
-        q2 = after(q2, forms13)
-        forms2 = made_forms(part2, a2, b2, q2)
+        amps = prepare_amps([own, amp1, amp2, amp3], blocks_here, jnp.asarray(amp_matrix()))
+        forms2 = made_forms(part2, a2, b2, after(q2, amps))
         far2 = other_core(after(forms2, far13))
-        amps = prepare_amps([own, amp1, amp2, after(amp3, forms2)], blocks_here, jnp.asarray(amp_matrix()))
         held = [forms0, far0, forms13, far13, forms2, far2]
     else:
         parts = [mine[0]] + [around(mine[by], by) for by in range(1, levels)]

time: 143 us -> 135 us (0.944)
  waiting for transfers between devices: 53.2 us -> 45 us
    ppermute x9, waiting for transfers between devices: 32.9 us -> 18.2 us  [around(): lax.ppermute(x, 'task', [(c, (c + 2 * by) % task_count) for c in range(ta...]
    ppermute x4, waiting for transfers between devices: 3.31 us -> 6.67 us  [per_device(): lax.ppermute(x, 'task', [(c, c ^ 1) for c in range(task_count)])]
    ppermute x6, waiting for transfers between devices: 17 us -> 20.1 us  [per_device(): second_side = lambda x: lax.ppermute(x, ('pair', 'task'), sides[1])]
  transfers between devices with their start and end apart: 22 -> 22, of which waited for: 10 -> 8; matrix products, arithmetic and copies ran while one was open for 3% -> 3% of each run, Pallas kernels for 29% -> 33%
where the time goes in v9:
time: 135 us; the launch traced here: 134 us
  Pallas kernels  54.7 us (41%)
  waiting for transfers between devices  45 us (33%)
  starting transfers between devices  25.2 us (19%)
  local copies, waits for them, and re-layouts  8.98 us (7%)
    pallas_call x4, Pallas kernels, ladders(): pl.pallas_call(functools.partial(ladder_kernel, find, made, len(tiles)),...  41.4 us
    ppermute x6, waiting for transfers between devices, per_device(): second_side = lambda x: lax.ppermute(x, ('pair', 'task'), sides[1])  20.1 us
    ppermute x9, waiting for transfers between devices, around(): lax.ppermute(x, 'task', [(c, (c + 2 * by) % task_count) for c in range(ta...  18.2 us
    ppermute x9, starting transfers between devices, around(): lax.ppermute(x, 'task', [(c, (c + 2 * by) % task_count) for c in range(ta...  13.7 us
    pallas_call x3, Pallas kernels, prepare(): pl.pallas_call(prepare_kernel, out_shape=jax.ShapeDtypeStruct((count, mat...  11.9 us
    unnamed x24, local copies, waits for them, and re-layouts  7.67 us
    ppermute x6, starting transfers between devices, per_device(): second_side = lambda x: lax.ppermute(x, ('pair', 'task'), sides[1])  7.33 us
    ppermute x4, waiting for transfers between devices, per_device(): lax.ppermute(x, 'task', [(c, c ^ 1) for c in range(task_count)])  6.67 us
  transfers between devices with their start and end apart: 22, of which 8 were waited for; matrix products, arithmetic and copies ran while one was open for 3% of the time, Pallas kernels for 33%

profile of v9, /device:TPU:0, one launch (start us, length us, event | category | flops | bytes accessed | tf_op | source)
XLA Modules:
  0.0 134.3 jit_solution(7266146018161870135)
XLA Ops:
  0.0 1.2 pad
  1.3 3.1 %collective-permute-start.4 = (bf16[625,256]{1,0:T(8,128)(2,1)S(1)}, bf16[625,256]{1,0:T(8,128)(2,1)S(1)}, u32[]{:S(2)}, u32[]{:S(2)}) collective-permute-start(bf16[625,256]{1,0:T(8,128)(2,1)S(1)} %bitcast.24), channel_id=1, source_target_pairs={{0,2},{1,3},{2,4},{3,5},{4,6},{5,7},{6,0},{7,1},{8,10},{9,11},{10,... | collective-permute-start | bytes 960008 | tf_op jit(solution)/shard_map/ppermute | solution.py:296
  4.4 3.3 %copy.23 = bf16[2,384,625]{2,1,0:T(8,128)(2,1)S(1)} copy(bf16[2,384,625]{1,0,2:T(2,128)(2,1)} %param.8) | data formatting | bytes 1920000 | tf_op args[0]
  7.7 0.1 dynamic-slice_bitcast_fusion
  7.8 2.2 %collective-permute-start.3 = (bf16[2,96,625]{2,1,0:T(8,128)(2,1)S(1)}, bf16[2,96,625]{2,1,0:T(8,128)(2,1)S(1)}, u32[]{:S(2)}, u32[]{:S(2)}) collective-permute-start(bf16[2,96,625]{2,1,0:T(8,128)(2,1)S(1)} %get-tuple-element.50), channel_id=1, source_target_pairs={{0,6},{1,7},{2,0},{3,1},{4,2},{5,3},{6,4},{7,5},{8,14},{9,15},{10,... | collective-permute-start | bytes 720008 | tf_op jit(solution)/shard_map/ppermute | solution.py:296
  10.0 0.0 collective-permute-start.2
  10.0 1.6 %collective-permute-start.1 = (bf16[2,96,625]{2,1,0:T(8,128)(2,1)S(1)}, bf16[2,96,625]{2,1,0:T(8,128)(2,1)S(1)}, u32[]{:S(2)}, u32[]{:S(2)}) collective-permute-start(bf16[2,96,625]{2,1,0:T(8,128)(2,1)S(1)} %get-tuple-element.27.refs_0_), channel_id=1, source_target_pairs={{0,16},{1,9},{2,18},{3,11},{4,20},{5,13},{6,22},{7,15},{8,24},{9,1... | collective-permute-start | bytes 720008 | tf_op jit(solution)/shard_map/ppermute | solution.py:307
  11.7 1.5 %collective-permute-start = (bf16[2,96,625]{2,1,0:T(8,128)(2,1)S(1)}, bf16[2,96,625]{2,1,0:T(8,128)(2,1)S(1)}, u32[]{:S(2)}, u32[]{:S(2)}) collective-permute-start(bf16[2,96,625]{2,1,0:T(8,128)(2,1)S(1)} %get-tuple-element.27.refs_0_), channel_id=1, source_target_pairs={{0,8},{1,17},{2,10},{3,19},{4,12},{5,21},{6,14},{7,23},{8,0},{9,25... | collective-permute-start | bytes 720008 | tf_op jit(solution)/shard_map/ppermute | solution.py:306
  13.2 6.9 %collective-permute-done.3 = bf16[2,96,625]{2,1,0:T(8,128)(2,1)S(1)} collective-permute-done((bf16[2,96,625]{2,1,0:T(8,128)(2,1)S(1)}, bf16[2,96,625]{2,1,0:T(8,128)(2,1)S(1)}, u32[]{:S(2)}, u32[]{:S(2)}) %collective-permute-start.3) | collective-permute-done | bytes 240032 | tf_op jit(solution)/shard_map/ppermute | solution.py:296
  20.1 4.5 %collective-permute-done.2 = bf16[2,96,625]{2,1,0:T(8,128)(2,1)S(1)} collective-permute-done((bf16[2,96,625]{2,1,0:T(8,128)(2,1)S(1)}, bf16[2,96,625]{2,1,0:T(8,128)(2,1)S(1)}, u32[]{:S(2)}, u32[]{:S(2)}) %collective-permute-start.2) | collective-permute-done | bytes 240032 | tf_op jit(solution)/shard_map/ppermute | solution.py:296
  24.6 0.0 collective-permute-done.1.refs_2_
  24.6 0.0 collective-permute-done.refs_1_
  24.6 0.0 collective-permute-done.4.refs_1_
  24.7 1.6 %collective-permute-start.7 = (bf16[4,96,625]{2,1,0:T(8,128)(2,1)S(1)}, bf16[4,96,625]{2,1,0:T(8,128)(2,1)S(1)}, u32[]{:S(2)}, u32[]{:S(2)}) collective-permute-start(bf16[4,96,625]{2,1,0:T(8,128)(2,1)S(1)} %constant_dynamic-update-slice_fusion.refs_0_), channel_id=1, source_target_pairs={{0,16},{1,9},{2,18},{3,11},{4,20},{5,13},{6,22},{7,15},{8,24},{9,1... | collective-permute-start | bytes 1440008 | tf_op jit(solution)/shard_map/ppermute | solution.py:307
  26.3 1.5 %collective-permute-start.6 = (bf16[4,96,625]{2,1,0:T(8,128)(2,1)S(1)}, bf16[4,96,625]{2,1,0:T(8,128)(2,1)S(1)}, u32[]{:S(2)}, u32[]{:S(2)}) collective-permute-start(bf16[4,96,625]{2,1,0:T(8,128)(2,1)S(1)} %constant_dynamic-update-slice_fusion.refs_0_), channel_id=1, source_target_pairs={{0,8},{1,17},{2,10},{3,19},{4,12},{5,21},{6,14},{7,23},{8,0},{9,25... | collective-permute-start | bytes 1440008 | tf_op jit(solution)/shard_map/ppermute | solution.py:306
  27.7 0.5 collective-permute-start.5
  28.2 0.7 collective-permute-start.8
  28.9 11.8 %collective-permute-done.5.refs_3_ = bf16[2,96,625]{2,1,0:T(8,128)(2,1)S(1)} collective-permute-done((bf16[2,96,625]{2,1,0:T(8,128)(2,1)S(1)}, bf16[2,96,625]{2,1,0:T(8,128)(2,1)S(1)}, u32[]{:S(2)}, u32[]{:S(2)}) %collective-permute-start.5) | collective-permute-done | bytes 240032 | tf_op jit(solution)/shard_map/ppermute | solution.py:307
  40.7 1.6 %copy-done.3 = bf16[1600,625]{1,0:T(8,128)(2,1)S(1)} copy-done((bf16[1600,625]{1,0:T(8,128)(2,1)S(1)}, bf16[1600,625]{1,0:T(8,128)(2,1)}, u32[]{:S(2)}) %copy-start.3) | copy-done | bytes 2000024
  42.3 2.6 %shard_map.82.refs_0_ = bf16[2,1600,384]{2,1,0:T(8,128)(2,1)S(1)} custom-call(s32[1]{0:T(128)} %bitcast.column_ref, bf16[2,96,625]{2,1,0:T(8,128)(2,1)S(1)} %get-tuple-element.27.refs_0_, bf16[2,96,625]{2,1,0:T(8,128)(2,1)S(1)} %collective-permute-done.refs_1_, bf16[2,96,625]{2,1,0:T(8,128)(2,1)S(1)} %collective-permute-done.1.refs_2_, ...), custom_call_target="tpu_custom_call" | custom-call | flops 1536000000 | bytes 3417600 | tf_op jit(solution)/shard_map/pallas_call | solution.py:77
  45.0 0.0 copy-start.2
  45.0 0.0 collective-permute-done.8.refs_0_
  45.0 0.0 collective-permute-done.7.refs_2_
  45.0 0.0 collective-permute-done.6.refs_1_
  45.0 0.1 collective-permute-start.9
  45.1 1.6 %collective-permute-start.10 = (bf16[4,96,625]{2,1,0:T(8,128)(2,1)S(1)}, bf16[4,96,625]{2,1,0:T(8,128)(2,1)S(1)}, u32[]{:S(2)}, u32[]{:S(2)}) collective-permute-start(bf16[4,96,625]{2,1,0:T(8,128)(2,1)S(1)} %collective-permute-done.6.refs_1_), channel_id=1, source_target_pairs={{0,16},{1,9},{2,18},{3,11},{4,20},{5,13},{6,22},{7,15},{8,24},{9,1... | collective-permute-start | bytes 1440008 | tf_op jit(solution)/shard_map/ppermute | solution.py:307
  46.7 0.6 collective-permute-start.13
  47.3 0.5 collective-permute-start.12
  47.8 0.5 collective-permute-start.11
  48.3 8.3 %collective-permute-done.10.refs_3_ = bf16[4,96,625]{2,1,0:T(8,128)(2,1)S(1)} collective-permute-done((bf16[4,96,625]{2,1,0:T(8,128)(2,1)S(1)}, bf16[4,96,625]{2,1,0:T(8,128)(2,1)S(1)}, u32[]{:S(2)}, u32[]{:S(2)}) %collective-permute-start.10) | collective-permute-done | bytes 480032 | tf_op jit(solution)/shard_map/ppermute | solution.py:307
  56.6 5.8 %shard_map.83.refs_2_ = bf16[4,1600,384]{2,1,0:T(8,128)(2,1)} custom-call(s32[1]{0:T(128)} %bitcast.column_ref, bf16[4,96,625]{2,1,0:T(8,128)(2,1)S(1)} %constant_dynamic-update-slice_fusion.refs_0_, bf16[4,96,625]{2,1,0:T(8,128)(2,1)S(1)} %collective-permute-done.6.refs_1_, bf16[4,96,625]{2,1,0:T(8,128)(2,1)S(1)} %collective-permute-done.7.refs_2_, ...), custom_call_target="tpu_custom_call" | custom-call | flops 3072000000 | bytes 6835200 | tf_op jit(solution)/shard_map/pallas_call | solution.py:77
  62.5 0.0 collective-permute-done.12.refs_2_
  62.5 0.0 collective-permute-done.11.refs_1_
  62.5 0.0 collective-permute-done.13.refs_2_
  62.5 0.0 collective-permute-done.9.refs_1_
  62.5 0.1 collective-permute-start.14
  62.6 2.2 %collective-permute-start.16 = (bf16[625,256]{1,0:T(8,128)(2,1)S(1)}, bf16[625,256]{1,0:T(8,128)(2,1)S(1)}, u32[]{:S(2)}, u32[]{:S(2)}) collective-permute-start(bf16[625,256]{1,0:T(8,128)(2,1)S(1)} %bitcast.26), channel_id=1, source_target_pairs={{0,6},{1,7},{2,0},{3,1},{4,2},{5,3},{6,4},{7,5},{8,14},{9,15},{10,... | collective-permute-start | bytes 960008 | tf_op jit(solution)/shard_map/ppermute | solution.py:296
  64.8 1.5 %collective-permute-start.15 = (bf16[2,96,625]{2,1,0:T(8,128)(2,1)S(1)}, bf16[2,96,625]{2,1,0:T(8,128)(2,1)S(1)}, u32[]{:S(2)}, u32[]{:S(2)}) collective-permute-start(bf16[2,96,625]{2,1,0:T(8,128)(2,1)S(1)} %collective-permute-done.11.refs_1_), channel_id=1, source_target_pairs={{0,16},{1,9},{2,18},{3,11},{4,20},{5,13},{6,22},{7,15},{8,24},{9,1... | collective-permute-start | bytes 720008 | tf_op jit(solution)/shard_map/ppermute | solution.py:307
  66.3 6.3 %collective-permute-done.16.refs_3_ = bf16[625,256]{1,0:T(8,128)(2,1)S(1)} collective-permute-done((bf16[625,256]{1,0:T(8,128)(2,1)S(1)}, bf16[625,256]{1,0:T(8,128)(2,1)S(1)}, u32[]{:S(2)}, u32[]{:S(2)}) %collective-permute-start.16) | collective-permute-done | bytes 320032 | tf_op jit(solution)/shard_map/ppermute | solution.py:296
  72.6 1.4 %shard_map.84.refs_6_ = bf16[8,800,128]{2,1,0:T(8,128)(2,1)S(1)} custom-call(bf16[800,625]{1,0:T(8,128)(2,1)S(1)} %copy-done.2, bf16[625,256]{1,0:T(8,128)(2,1)S(1)} %bitcast.27, bf16[625,256]{1,0:T(8,128)(2,1)S(1)} %collective-permute-done.4.refs_1_, bf16[625,256]{1,0:T(8,128)(2,1)S(1)} %collective-permute-done.13.refs_2_, ...), custom_call_target="tpu_custom_call" | custom-call | flops 1024000000 | bytes 2560000 | tf_op jit(solution)/shard_map/pallas_call | solution.py:108
  74.0 0.0 copy-start.7
  74.1 0.0 copy-start.8
  74.1 0.0 collective-permute-done.15.refs_3_
  74.1 3.5 %shard_map.85.refs_4_ = bf16[2,1600,384]{2,1,0:T(8,128)(2,1)} custom-call(s32[1]{0:T(128)} %bitcast.column_ref, bf16[2,96,625]{2,1,0:T(8,128)(2,1)S(1)} %collective-permute-done.8.refs_0_, bf16[2,96,625]{2,1,0:T(8,128)(2,1)S(1)} %collective-permute-done.11.refs_1_, bf16[2,96,625]{2,1,0:T(8,128)(2,1)S(1)} %collective-permute-done.12.refs_2_, ...), custom_call_target="tpu_custom_call" | custom-call | flops 1536000000 | bytes 3417600 | tf_op jit(solution)/shard_map/pallas_call | solution.py:77
  77.5 0.0 collective-permute-done.14.refs_3_
  77.5 0.0 collective-permute-start.17
  77.5 0.5 collective-permute-start.18
  78.1 0.1 copy.24.owners_ref
  78.1 0.1 copy.25.local_ref
  78.2 6.0 %collective-permute-done.18.refs_7_ = bf16[8,800,128]{2,1,0:T(8,128)(2,1)S(1)} collective-permute-done((bf16[8,800,128]{2,1,0:T(8,128)(2,1)S(1)}, bf16[8,800,128]{2,1,0:T(8,128)(2,1)S(1)}, u32[]{:S(2)}, u32[]{:S(2)}) %collective-permute-start.18) | collective-permute-done | bytes 1638432 | tf_op jit(solution)/shard_map/ppermute | solution.py:293
  84.2 0.7 collective-permute-done.17.refs_5_
  84.9 1.3 copy-done.1
  86.2 10.3 %shard_map.87 = bf16[1,2,625,128]{3,2,1,0:T(8,128)(2,1)S(1)} custom-call(s32[1]{0:T(128)} %bitcast.column_ref, s32[32,3]{1,0:T(8,128)S(1)} %copy.24.owners_ref, s32[32,4]{1,0:T(8,128)S(1)} %copy.25.local_ref, bf16[2,1600,384]{2,1,0:T(8,128)(2,1)} %copy-done, bf16[2,1600,384]{2,1,0:T(8,128)(2,1)} %copy-done.5, bf16[4,1600,384]{2,1,0:T(8,128)(2,1)} %shard_map.83.refs_2_, ...), custom_call_target="tpu_custom_call" | custom-call | flops 2936012800 | bytes 6553600 | tf_op jit(solution)/shard_map/pallas_call | solution.py:258
  96.5 4.2 %collective-permute-start.20 = (bf16[2,625,128]{2,1,0:T(8,128)(2,1)S(1)}, bf16[2,625,128]{2,1,0:T(8,128)(2,1)S(1)}, u32[]{:S(2)}, u32[]{:S(2)}) collective-permute-start(bf16[2,625,128]{2,1,0:T(8,128)(2,1)S(1)} %bitcast.28), channel_id=1, source_target_pairs={{0,6},{1,7},{2,0},{3,1},{4,2},{5,3},{6,4},{7,5},{8,14},{9,15},{10,... | collective-permute-start | bytes 960008 | tf_op jit(solution)/shard_map/ppermute | solution.py:296
  100.7 10.3 %shard_map.86 = bf16[1,2,625,128]{3,2,1,0:T(8,128)(2,1)S(1)} custom-call(s32[1]{0:T(128)} %bitcast.column_ref, s32[32,3]{1,0:T(8,128)S(1)} %copy.24.owners_ref, s32[32,4]{1,0:T(8,128)S(1)} %copy.25.local_ref, bf16[2,1600,384]{2,1,0:T(8,128)(2,1)} %copy-done, bf16[2,1600,384]{2,1,0:T(8,128)(2,1)} %copy-done.5, bf16[4,1600,384]{2,1,0:T(8,128)(2,1)} %shard_map.83.refs_2_, ...), custom_call_target="tpu_custom_call" | custom-call | flops 2936012800 | bytes 6553600 | tf_op jit(solution)/shard_map/pallas_call | solution.py:258
  111.1 0.1 collective-permute-start.19
  111.1 10.3 %shard_map.88 = bf16[1,2,625,128]{3,2,1,0:T(8,128)(2,1)S(1)} custom-call(s32[1]{0:T(128)} %bitcast.column_ref, s32[32,3]{1,0:T(8,128)S(1)} %copy.24.owners_ref, s32[32,4]{1,0:T(8,128)S(1)} %copy.25.local_ref, bf16[2,1600,384]{2,1,0:T(8,128)(2,1)} %copy-done, bf16[2,1600,384]{2,1,0:T(8,128)(2,1)} %copy-done.5, bf16[4,1600,384]{2,1,0:T(8,128)(2,1)} %shard_map.83.refs_2_, ...), custom_call_target="tpu_custom_call" | custom-call | flops 2936012800 | bytes 6553600 | tf_op jit(solution)/shard_map/pallas_call | solution.py:258
  121.5 0.0 copy-start.6
  121.5 0.6 collective-permute-start.21
  122.1 10.3 %shard_map.89 = bf16[1,2,625,128]{3,2,1,0:T(8,128)(2,1)S(1)} custom-call(s32[1]{0:T(128)} %bitcast.column_ref, s32[32,3]{1,0:T(8,128)S(1)} %copy.24.owners_ref, s32[32,4]{1,0:T(8,128)S(1)} %copy.25.local_ref, bf16[2,1600,384]{2,1,0:T(8,128)(2,1)} %copy-done, bf16[2,1600,384]{2,1,0:T(8,128)(2,1)} %copy-done.5, bf16[4,1600,384]{2,1,0:T(8,128)(2,1)} %shard_map.83.refs_2_, ...), custom_call_target="tpu_custom_call" | custom-call | flops 2936012800 | bytes 6553600 | tf_op jit(solution)/shard_map/pallas_call | solution.py:258
  132.5 0.0 collective-permute-done.20
  132.5 0.5 collective-permute-done.19
  132.9 0.2 fusion.1
  133.1 1.2 copy.33
  (16 shorter events, 0.1 us)
Async XLA Ops:
  1.3 23.3 %collective-permute-start.4 = (bf16[625,256]{1,0:T(8,128)(2,1)S(1)}, bf16[625,256]{1,0:T(8,128)(2,1)S(1)}, u32[]{:S(2)}, u32[]{:S(2)}) collective-permute-start(bf16[625,256]{1,0:T(8,128)(2,1)S(1)} %bitcast.24), channel_id=1, source_target_pairs={{0,2},{1,3},{2,4},{3,5},{4,6},{5,7},{6,0},{7,1},{8,10},{9,11},{10,... | collective-permute-start | bytes 960008 | tf_op jit(solution)/shard_map/ppermute | solution.py:296
  7.8 12.2 %collective-permute-start.3 = (bf16[2,96,625]{2,1,0:T(8,128)(2,1)S(1)}, bf16[2,96,625]{2,1,0:T(8,128)(2,1)S(1)}, u32[]{:S(2)}, u32[]{:S(2)}) collective-permute-start(bf16[2,96,625]{2,1,0:T(8,128)(2,1)S(1)} %get-tuple-element.50), channel_id=1, source_target_pairs={{0,6},{1,7},{2,0},{3,1},{4,2},{5,3},{6,4},{7,5},{8,14},{9,15},{10,... | collective-permute-start | bytes 720008 | tf_op jit(solution)/shard_map/ppermute | solution.py:296
  10.0 14.5 %collective-permute-start.2 = (bf16[2,96,625]{2,1,0:T(8,128)(2,1)S(1)}, bf16[2,96,625]{2,1,0:T(8,128)(2,1)S(1)}, u32[]{:S(2)}, u32[]{:S(2)}) collective-permute-start(bf16[2,96,625]{2,1,0:T(8,128)(2,1)S(1)} %get-tuple-element.51), channel_id=1, source_target_pairs={{0,2},{1,3},{2,4},{3,5},{4,6},{5,7},{6,0},{7,1},{8,10},{9,11},{10,... | collective-permute-start | bytes 720008 | tf_op jit(solution)/shard_map/ppermute | solution.py:296
  10.0 14.5 %collective-permute-start.1 = (bf16[2,96,625]{2,1,0:T(8,128)(2,1)S(1)}, bf16[2,96,625]{2,1,0:T(8,128)(2,1)S(1)}, u32[]{:S(2)}, u32[]{:S(2)}) collective-permute-start(bf16[2,96,625]{2,1,0:T(8,128)(2,1)S(1)} %get-tuple-element.27.refs_0_), channel_id=1, source_target_pairs={{0,16},{1,9},{2,18},{3,11},{4,20},{5,13},{6,22},{7,15},{8,24},{9,1... | collective-permute-start | bytes 720008 | tf_op jit(solution)/shard_map/ppermute | solution.py:307
  11.7 12.9 %collective-permute-start = (bf16[2,96,625]{2,1,0:T(8,128)(2,1)S(1)}, bf16[2,96,625]{2,1,0:T(8,128)(2,1)S(1)}, u32[]{:S(2)}, u32[]{:S(2)}) collective-permute-start(bf16[2,96,625]{2,1,0:T(8,128)(2,1)S(1)} %get-tuple-element.27.refs_0_), channel_id=1, source_target_pairs={{0,8},{1,17},{2,10},{3,19},{4,12},{5,21},{6,14},{7,23},{8,0},{9,25... | collective-permute-start | bytes 720008 | tf_op jit(solution)/shard_map/ppermute | solution.py:306
  24.7 20.3 %collective-permute-start.7 = (bf16[4,96,625]{2,1,0:T(8,128)(2,1)S(1)}, bf16[4,96,625]{2,1,0:T(8,128)(2,1)S(1)}, u32[]{:S(2)}, u32[]{:S(2)}) collective-permute-start(bf16[4,96,625]{2,1,0:T(8,128)(2,1)S(1)} %constant_dynamic-update-slice_fusion.refs_0_), channel_id=1, source_target_pairs={{0,16},{1,9},{2,18},{3,11},{4,20},{5,13},{6,22},{7,15},{8,24},{9,1... | collective-permute-start | bytes 1440008 | tf_op jit(solution)/shard_map/ppermute | solution.py:307
  26.3 18.8 %collective-permute-start.6 = (bf16[4,96,625]{2,1,0:T(8,128)(2,1)S(1)}, bf16[4,96,625]{2,1,0:T(8,128)(2,1)S(1)}, u32[]{:S(2)}, u32[]{:S(2)}) collective-permute-start(bf16[4,96,625]{2,1,0:T(8,128)(2,1)S(1)} %constant_dynamic-update-slice_fusion.refs_0_), channel_id=1, source_target_pairs={{0,8},{1,17},{2,10},{3,19},{4,12},{5,21},{6,14},{7,23},{8,0},{9,25... | collective-permute-start | bytes 1440008 | tf_op jit(solution)/shard_map/ppermute | solution.py:306
  27.7 13.0 %collective-permute-start.5 = (bf16[2,96,625]{2,1,0:T(8,128)(2,1)S(1)}, bf16[2,96,625]{2,1,0:T(8,128)(2,1)S(1)}, u32[]{:S(2)}, u32[]{:S(2)}) collective-permute-start(bf16[2,96,625]{2,1,0:T(8,128)(2,1)S(1)} %collective-permute-done.refs_1_), channel_id=1, source_target_pairs={{0,16},{1,9},{2,18},{3,11},{4,20},{5,13},{6,22},{7,15},{8,24},{9,1... | collective-permute-start | bytes 720008 | tf_op jit(solution)/shard_map/ppermute | solution.py:307
  28.2 16.7 %collective-permute-start.8 = (bf16[2,96,625]{2,1,0:T(8,128)(2,1)S(1)}, bf16[2,96,625]{2,1,0:T(8,128)(2,1)S(1)}, u32[]{:S(2)}, u32[]{:S(2)}) collective-permute-start(bf16[2,96,625]{2,1,0:T(8,128)(2,1)S(1)} %get-tuple-element.32), channel_id=1, source_target_pairs={{0,4},{1,5},{2,6},{3,7},{4,0},{5,1},{6,2},{7,3},{8,12},{9,13},{10,... | collective-permute-start | bytes 720008 | tf_op jit(solution)/shard_map/ppermute | solution.py:296
  40.7 1.6 %copy-start.3 = (bf16[1600,625]{1,0:T(8,128)(2,1)S(1)}, bf16[1600,625]{1,0:T(8,128)(2,1)}, u32[]{:S(2)}) copy-start(bf16[1600,625]{1,0:T(8,128)(2,1)} %constant.61.clone.refs_4_) | copy-start | bytes 6000004
  42.3 14.3 %copy-start.4 = (bf16[1600,625]{1,0:T(8,128)(2,1)S(1)}, bf16[1600,625]{1,0:T(8,128)(2,1)}, u32[]{:S(2)}) copy-start(bf16[1600,625]{1,0:T(8,128)(2,1)} %constant.61.clone.refs_4_) | copy-start | bytes 6000004
  45.0 17.5 %copy-start = (bf16[2,1600,384]{2,1,0:T(8,128)(2,1)}, bf16[2,1600,384]{2,1,0:T(8,128)(2,1)S(1)}, u32[]{:S(2)}) copy-start(bf16[2,1600,384]{2,1,0:T(8,128)(2,1)S(1)} %shard_map.82.refs_0_) | copy-start | bytes 7372804
  45.0 27.6 %copy-start.2 = (bf16[800,625]{1,0:T(8,128)(2,1)S(1)}, bf16[800,625]{1,0:T(8,128)(2,1)}, u32[]{:S(2)}) copy-start(bf16[800,625]{1,0:T(8,128)(2,1)} %constant.63.clone.matrix_ref) | copy-start | bytes 3000004
  45.0 17.5 %collective-permute-start.9 = (bf16[2,1600,384]{2,1,0:T(8,128)(2,1)S(1)}, bf16[2,1600,384]{2,1,0:T(8,128)(2,1)S(1)}, u32[]{:S(2)}, u32[]{:S(2)}) collective-permute-start(bf16[2,1600,384]{2,1,0:T(8,128)(2,1)S(1)} %shard_map.82.refs_0_), channel_id=1, source_target_pairs={{0,1},{1,0},{2,3},{3,2},{4,5},{5,4},{6,7},{7,6},{8,9},{9,8},{10,11... | collective-permute-start | bytes 7372808 | tf_op jit(solution)/shard_map/ppermute | solution.py:293
  45.1 11.5 %collective-permute-start.10 = (bf16[4,96,625]{2,1,0:T(8,128)(2,1)S(1)}, bf16[4,96,625]{2,1,0:T(8,128)(2,1)S(1)}, u32[]{:S(2)}, u32[]{:S(2)}) collective-permute-start(bf16[4,96,625]{2,1,0:T(8,128)(2,1)S(1)} %collective-permute-done.6.refs_1_), channel_id=1, source_target_pairs={{0,16},{1,9},{2,18},{3,11},{4,20},{5,13},{6,22},{7,15},{8,24},{9,1... | collective-permute-start | bytes 1440008 | tf_op jit(solution)/shard_map/ppermute | solution.py:307
  46.7 15.8 %collective-permute-start.13 = (bf16[625,256]{1,0:T(8,128)(2,1)S(1)}, bf16[625,256]{1,0:T(8,128)(2,1)S(1)}, u32[]{:S(2)}, u32[]{:S(2)}) collective-permute-start(bf16[625,256]{1,0:T(8,128)(2,1)S(1)} %bitcast.25), channel_id=1, source_target_pairs={{0,4},{1,5},{2,6},{3,7},{4,0},{5,1},{6,2},{7,3},{8,12},{9,13},{10,... | collective-permute-start | bytes 960008 | tf_op jit(solution)/shard_map/ppermute | solution.py:296
  47.3 15.2 %collective-permute-start.12 = (bf16[2,96,625]{2,1,0:T(8,128)(2,1)S(1)}, bf16[2,96,625]{2,1,0:T(8,128)(2,1)S(1)}, u32[]{:S(2)}, u32[]{:S(2)}) collective-permute-start(bf16[2,96,625]{2,1,0:T(8,128)(2,1)S(1)} %collective-permute-done.8.refs_0_), channel_id=1, source_target_pairs={{0,16},{1,9},{2,18},{3,11},{4,20},{5,13},{6,22},{7,15},{8,24},{9,1... | collective-permute-start | bytes 720008 | tf_op jit(solution)/shard_map/ppermute | solution.py:307
  47.8 14.7 %collective-permute-start.11 = (bf16[2,96,625]{2,1,0:T(8,128)(2,1)S(1)}, bf16[2,96,625]{2,1,0:T(8,128)(2,1)S(1)}, u32[]{:S(2)}, u32[]{:S(2)}) collective-permute-start(bf16[2,96,625]{2,1,0:T(8,128)(2,1)S(1)} %collective-permute-done.8.refs_0_), channel_id=1, source_target_pairs={{0,8},{1,17},{2,10},{3,19},{4,12},{5,21},{6,14},{7,23},{8,0},{9,25... | collective-permute-start | bytes 720008 | tf_op jit(solution)/shard_map/ppermute | solution.py:306
  62.5 3.8 %copy-start.5 = (bf16[2,1600,384]{2,1,0:T(8,128)(2,1)}, bf16[2,1600,384]{2,1,0:T(8,128)(2,1)S(1)}, u32[]{:S(2)}) copy-start(bf16[2,1600,384]{2,1,0:T(8,128)(2,1)S(1)} %collective-permute-done.9.refs_1_) | copy-start | bytes 7372804
  62.5 15.1 %collective-permute-start.14 = (bf16[4,1600,384]{2,1,0:T(8,128)(2,1)}, bf16[4,1600,384]{2,1,0:T(8,128)(2,1)}, u32[]{:S(2)}, u32[]{:S(2)}) collective-permute-start(bf16[4,1600,384]{2,1,0:T(8,128)(2,1)} %shard_map.83.refs_2_), channel_id=1, source_target_pairs={{0,1},{1,0},{2,3},{3,2},{4,5},{5,4},{6,7},{7,6},{8,9},{9,8},{10,11... | collective-permute-start | bytes 14745608 | tf_op jit(solution)/shard_map/ppermute | solution.py:293
  62.6 10.0 %collective-permute-start.16 = (bf16[625,256]{1,0:T(8,128)(2,1)S(1)}, bf16[625,256]{1,0:T(8,128)(2,1)S(1)}, u32[]{:S(2)}, u32[]{:S(2)}) collective-permute-start(bf16[625,256]{1,0:T(8,128)(2,1)S(1)} %bitcast.26), channel_id=1, source_target_pairs={{0,6},{1,7},{2,0},{3,1},{4,2},{5,3},{6,4},{7,5},{8,14},{9,15},{10,... | collective-permute-start | bytes 960008 | tf_op jit(solution)/shard_map/ppermute | solution.py:296
  64.8 9.3 %collective-permute-start.15 = (bf16[2,96,625]{2,1,0:T(8,128)(2,1)S(1)}, bf16[2,96,625]{2,1,0:T(8,128)(2,1)S(1)}, u32[]{:S(2)}, u32[]{:S(2)}) collective-permute-start(bf16[2,96,625]{2,1,0:T(8,128)(2,1)S(1)} %collective-permute-done.11.refs_1_), channel_id=1, source_target_pairs={{0,16},{1,9},{2,18},{3,11},{4,20},{5,13},{6,22},{7,15},{8,24},{9,1... | collective-permute-start | bytes 720008 | tf_op jit(solution)/shard_map/ppermute | solution.py:307
  74.0 4.0 %copy-start.7 = (s32[32,3]{0,1:T(4,128)S(1)}, s32[32,3]{0,1:T(4,128)}, u32[]{:S(2)}) copy-start(s32[32,3]{0,1:T(4,128)} %param.11) | copy-start | bytes 1156
  74.1 4.1 %copy-start.8 = (s32[32,4]{0,1:T(4,128)S(1)}, s32[32,4]{0,1:T(4,128)}, u32[]{:S(2)}) copy-start(s32[32,4]{0,1:T(4,128)} %param.12) | copy-start | bytes 1540
  77.5 7.4 %collective-permute-start.17 = (bf16[2,1600,384]{2,1,0:T(8,128)(2,1)}, bf16[2,1600,384]{2,1,0:T(8,128)(2,1)}, u32[]{:S(2)}, u32[]{:S(2)}) collective-permute-start(bf16[2,1600,384]{2,1,0:T(8,128)(2,1)} %shard_map.85.refs_4_), channel_id=1, source_target_pairs={{0,1},{1,0},{2,3},{3,2},{4,5},{5,4},{6,7},{7,6},{8,9},{9,8},{10,11... | collective-permute-start | bytes 7372808 | tf_op jit(solution)/shard_map/ppermute | solution.py:293
  77.5 6.6 %collective-permute-start.18 = (bf16[8,800,128]{2,1,0:T(8,128)(2,1)S(1)}, bf16[8,800,128]{2,1,0:T(8,128)(2,1)S(1)}, u32[]{:S(2)}, u32[]{:S(2)}) collective-permute-start(bf16[8,800,128]{2,1,0:T(8,128)(2,1)S(1)} %shard_map.84.refs_6_), channel_id=1, source_target_pairs={{0,1},{1,0},{2,3},{3,2},{4,5},{5,4},{6,7},{7,6},{8,9},{9,8},{10,11... | collective-permute-start | bytes 4915208 | tf_op jit(solution)/shard_map/ppermute | solution.py:293
  84.9 1.3 copy-start.1
  96.5 36.0 %collective-permute-start.20 = (bf16[2,625,128]{2,1,0:T(8,128)(2,1)S(1)}, bf16[2,625,128]{2,1,0:T(8,128)(2,1)S(1)}, u32[]{:S(2)}, u32[]{:S(2)}) collective-permute-start(bf16[2,625,128]{2,1,0:T(8,128)(2,1)S(1)} %bitcast.28), channel_id=1, source_target_pairs={{0,6},{1,7},{2,0},{3,1},{4,2},{5,3},{6,4},{7,5},{8,14},{9,15},{10,... | collective-permute-start | bytes 960008 | tf_op jit(solution)/shard_map/ppermute | solution.py:296
  111.1 21.9 %collective-permute-start.19 = (bf16[2,625,128]{2,1,0:T(8,128)(2,1)S(1)}, bf16[2,625,128]{2,1,0:T(8,128)(2,1)S(1)}, u32[]{:S(2)}, u32[]{:S(2)}) collective-permute-start(bf16[2,625,128]{2,1,0:T(8,128)(2,1)S(1)} %bitcast.29), channel_id=1, source_target_pairs={{0,4},{1,5},{2,6},{3,7},{4,0},{5,1},{6,2},{7,3},{8,12},{9,13},{10,... | collective-permute-start | bytes 960008 | tf_op jit(solution)/shard_map/ppermute | solution.py:296
  121.5 11.4 %copy-start.6 = (f32[2,128,625]{1,0,2:T(2,128)S(1)}, f32[2,128,625]{1,0,2:T(2,128)}, u32[]{:S(2)}) copy-start(f32[2,128,625]{1,0,2:T(2,128)} %param.10) | copy-start | bytes 1920004
  121.5 11.4 %collective-permute-start.21 = (bf16[2,625,128]{2,1,0:T(8,128)(2,1)S(1)}, bf16[2,625,128]{2,1,0:T(8,128)(2,1)S(1)}, u32[]{:S(2)}, u32[]{:S(2)}) collective-permute-start(bf16[2,625,128]{2,1,0:T(8,128)(2,1)S(1)} %bitcast.30), channel_id=1, source_target_pairs={{0,2},{1,3},{2,4},{3,5},{4,6},{5,7},{6,0},{7,1},{8,10},{9,11},{10,... | collective-permute-start | bytes 960008 | tf_op jit(solution)/shard_map/ppermute | solution.py:296

commit v10 on v9

--- a/solution.py
+++ b/solution.py
@@ -232,8 +232,7 @@
             below, far, m = place(kind)
             if not made:
                 return 0, (below * 2 + far) * blocks_here + m
-            chunk = jnp.where(below == 3, 1, below)
-            return chunk * 2 + far, m + jnp.where(below == 3, blocks_here, 0)
+            return below * 2 + far, m
 
         below, far, m = place(2)
         return {"task": task, "row": factor(0), "col": factor(1), "amp": (far, below * blocks_here + m)}
@@ -312,22 +311,26 @@
         a0, b0, part1, part3 = first_side(part0), second_side(part0), around(mine[1], 1), around(mine[3], 3)
 
         a0, b0, part0, part1, part3, amp1, to2 = after((a0, b0, part0, part1, part3, amp1, mine[2]), ())
-        part13 = jnp.concatenate([part1, part3], axis=0)
-        q0, a13, b13, part2 = second_side(a0), first_side(part13), second_side(part13), around(to2, 2)
+        q0, a1, b1, part2 = second_side(a0), first_side(part1), second_side(part1), around(to2, 2)
         forms0 = made_forms(part0, a0, b0, q0)
 
-        own, forms0, a13, b13, part2, part13 = after((own, forms0, a13, b13, part2, part13), ())
-        q13, a2, b2, amp2 = second_side(a13), first_side(part2), second_side(part2), around(own, 2)
+        forms0, part1, a1, b1, part2, part3, amp1 = after((forms0, part1, a1, b1, part2, part3, amp1), ())
+        q1, a3, b3, amp2 = second_side(a1), first_side(part3), second_side(part3), around(amp1, 1)
         far0 = other_core(forms0)
-        forms13 = made_forms(part13, a13, b13, q13)
-
-        forms13, part2, a2, b2, own, amp2 = after((forms13, part2, a2, b2, own, amp2), ())
-        q2, amp3 = second_side(a2), around(own, 3)
-        far13 = other_core(after(forms13, far0))
+        forms1 = made_forms(part1, a1, b1, q1)
+
+        forms1, part3, a3, b3, part2, amp2, far0 = after((forms1, part3, a3, b3, part2, amp2, far0), ())
+        q3, a2, b2, amp3 = second_side(a3), first_side(part2), second_side(part2), around(amp2, 1)
+        far1 = other_core(forms1)
+        forms3 = made_forms(part3, a3, b3, q3)
+
+        forms3, part2, a2, b2, amp3, far1 = after((forms3, part2, a2, b2, amp3, far1), ())
+        q2 = second_side(a2)
+        far3 = other_core(forms3)
         amps = prepare_amps([own, amp1, amp2, amp3], blocks_here, jnp.asarray(amp_matrix()))
         forms2 = made_forms(part2, a2, b2, after(q2, amps))
-        far2 = other_core(after(forms2, far13))
-        held = [forms0, far0, forms13, far13, forms2, far2]
+        far2 = other_core(after(forms2, far3))
+        held = [forms0, far0, forms1, far1, forms2, far2, forms3, far3]
     else:
         parts = [mine[0]] + [around(mine[by], by) for by in range(1, levels)]
         tiles = amplitudes.reshape(blocks_here, pairs, TV, TV).transpose(0, 3, 2, 1)

time: 135 us -> 129 us (0.956)
  waiting for transfers between devices: 45 us -> 41.1 us
  starting transfers between devices: 25.2 us -> 22.8 us
    ppermute x9, starting transfers between devices: 13.7 us -> 8.36 us  [around(): lax.ppermute(x, 'task', [(c, (c + 2 * by) % task_count) for c in range(ta...]
    ppermute x6 -> x8, starting transfers between devices: 7.33 us -> 9.35 us  [per_device(): second_side = lambda x: lax.ppermute(x, ('pair', 'task'), sides[1])]
    ppermute x9, waiting for transfers between devices: 18.2 us -> 16.4 us  [around(): lax.ppermute(x, 'task', [(c, (c + 2 * by) % task_count) for c in range(ta...]
    ppermute x3 -> x4, starting transfers between devices: 3.52 us -> 5.01 us  [per_device(): first_side = lambda x: lax.ppermute(x, ('pair', 'task'), sides[0])]
    unnamed x24 -> x29, local copies, waits for them, and re-layouts: 7.67 us -> 9.01 us
    ppermute x4 -> x5, waiting for transfers between devices: 6.67 us -> 5.48 us  [per_device(): lax.ppermute(x, 'task', [(c, c ^ 1) for c in range(task_count)])]
    ppermute x6 -> x8, waiting for transfers between devices: 20.1 us -> 19.2 us  [per_device(): second_side = lambda x: lax.ppermute(x, ('pair', 'task'), sides[1])]
    pallas_call x3 -> x4, Pallas kernels: 11.9 us -> 11.4 us  [prepare(): pl.pallas_call(prepare_kernel, out_shape=jax.ShapeDtypeStruct((count, mat...]
  transfers between devices with their start and end apart: 22 -> 26, of which waited for: 8 -> 13; matrix products, arithmetic and copies ran while one was open for 3% -> 3% of each run, Pallas kernels for 33% -> 34%
where the time goes in v10:
time: 129 us
  Pallas kernels  54.2 us (42%)
  waiting for transfers between devices  41.1 us (32%)
  starting transfers between devices  22.8 us (18%)
  local copies, waits for them, and re-layouts  10.3 us (8%)
    pallas_call x4, Pallas kernels, ladders(): pl.pallas_call(functools.partial(ladder_kernel, find, made, len(tiles)),...  41.4 us
    ppermute x8, waiting for transfers between devices, per_device(): second_side = lambda x: lax.ppermute(x, ('pair', 'task'), sides[1])  19.2 us
    ppermute x9, waiting for transfers between devices, around(): lax.ppermute(x, 'task', [(c, (c + 2 * by) % task_count) for c in range(ta...  16.4 us
    pallas_call x4, Pallas kernels, prepare(): pl.pallas_call(prepare_kernel, out_shape=jax.ShapeDtypeStruct((count, mat...  11.4 us
    ppermute x8, starting transfers between devices, per_device(): second_side = lambda x: lax.ppermute(x, ('pair', 'task'), sides[1])  9.35 us
    unnamed x29, local copies, waits for them, and re-layouts  9.01 us
    ppermute x9, starting transfers between devices, around(): lax.ppermute(x, 'task', [(c, (c + 2 * by) % task_count) for c in range(ta...  8.36 us
    ppermute x5, waiting for transfers between devices, per_device(): lax.ppermute(x, 'task', [(c, c ^ 1) for c in range(task_count)])  5.48 us
  transfers between devices with their start and end apart: 26, of which 13 were waited for; matrix products, arithmetic and copies ran while one was open for 3% of the time, Pallas kernels for 34%

profile of v10, /device:TPU:0, one launch (start us, length us, event | category | flops | bytes accessed | tf_op | source)
XLA Modules:
  0.0 128.8 jit_solution(17807743840846556070)
XLA Ops:
  0.0 1.2 pad
  1.3 3.1 %collective-permute-start.4 = (bf16[625,256]{1,0:T(8,128)(2,1)S(1)}, bf16[625,256]{1,0:T(8,128)(2,1)S(1)}, u32[]{:S(2)}, u32[]{:S(2)}) collective-permute-start(bf16[625,256]{1,0:T(8,128)(2,1)S(1)} %bitcast.24), channel_id=1, source_target_pairs={{0,2},{1,3},{2,4},{3,5},{4,6},{5,7},{6,0},{7,1},{8,10},{9,11},{10,... | collective-permute-start | bytes 960008 | tf_op jit(solution)/shard_map/ppermute | solution.py:295
  4.4 3.3 %copy.23 = bf16[2,384,625]{2,1,0:T(8,128)(2,1)S(1)} copy(bf16[2,384,625]{1,0,2:T(2,128)(2,1)} %param.8) | data formatting | bytes 1920000 | tf_op args[0]
  7.7 0.1 dynamic-slice_bitcast_fusion
  7.8 2.2 %collective-permute-start.3 = (bf16[2,96,625]{2,1,0:T(8,128)(2,1)S(1)}, bf16[2,96,625]{2,1,0:T(8,128)(2,1)S(1)}, u32[]{:S(2)}, u32[]{:S(2)}) collective-permute-start(bf16[2,96,625]{2,1,0:T(8,128)(2,1)S(1)} %get-tuple-element.64), channel_id=1, source_target_pairs={{0,6},{1,7},{2,0},{3,1},{4,2},{5,3},{6,4},{7,5},{8,14},{9,15},{10,... | collective-permute-start | bytes 720008 | tf_op jit(solution)/shard_map/ppermute | solution.py:295
  10.0 1.6 %collective-permute-start.1 = (bf16[2,96,625]{2,1,0:T(8,128)(2,1)S(1)}, bf16[2,96,625]{2,1,0:T(8,128)(2,1)S(1)}, u32[]{:S(2)}, u32[]{:S(2)}) collective-permute-start(bf16[2,96,625]{2,1,0:T(8,128)(2,1)S(1)} %get-tuple-element.34.refs_0_), channel_id=1, source_target_pairs={{0,16},{1,9},{2,18},{3,11},{4,20},{5,13},{6,22},{7,15},{8,24},{9,1... | collective-permute-start | bytes 720008 | tf_op jit(solution)/shard_map/ppermute | solution.py:306
  11.7 1.5 %collective-permute-start = (bf16[2,96,625]{2,1,0:T(8,128)(2,1)S(1)}, bf16[2,96,625]{2,1,0:T(8,128)(2,1)S(1)}, u32[]{:S(2)}, u32[]{:S(2)}) collective-permute-start(bf16[2,96,625]{2,1,0:T(8,128)(2,1)S(1)} %get-tuple-element.34.refs_0_), channel_id=1, source_target_pairs={{0,8},{1,17},{2,10},{3,19},{4,12},{5,21},{6,14},{7,23},{8,0},{9,25... | collective-permute-start | bytes 720008 | tf_op jit(solution)/shard_map/ppermute | solution.py:305
  13.2 6.9 %collective-permute-done.3.refs_0_ = bf16[2,96,625]{2,1,0:T(8,128)(2,1)S(1)} collective-permute-done((bf16[2,96,625]{2,1,0:T(8,128)(2,1)S(1)}, bf16[2,96,625]{2,1,0:T(8,128)(2,1)S(1)}, u32[]{:S(2)}, u32[]{:S(2)}) %collective-permute-start.3) | collective-permute-done | bytes 240032 | tf_op jit(solution)/shard_map/ppermute | solution.py:295
  20.1 4.5 %collective-permute-done.2.refs_0_ = bf16[2,96,625]{2,1,0:T(8,128)(2,1)S(1)} collective-permute-done((bf16[2,96,625]{2,1,0:T(8,128)(2,1)S(1)}, bf16[2,96,625]{2,1,0:T(8,128)(2,1)S(1)}, u32[]{:S(2)}, u32[]{:S(2)}) %collective-permute-start.2) | collective-permute-done | bytes 240032 | tf_op jit(solution)/shard_map/ppermute | solution.py:295
  24.6 0.0 collective-permute-done.1.refs_2_
  24.6 0.0 collective-permute-done.refs_1_
  24.6 0.0 collective-permute-done.4.refs_1_
  24.6 1.6 %collective-permute-start.5 = (bf16[2,96,625]{2,1,0:T(8,128)(2,1)S(1)}, bf16[2,96,625]{2,1,0:T(8,128)(2,1)S(1)}, u32[]{:S(2)}, u32[]{:S(2)}) collective-permute-start(bf16[2,96,625]{2,1,0:T(8,128)(2,1)S(1)} %collective-permute-done.refs_1_), channel_id=1, source_target_pairs={{0,16},{1,9},{2,18},{3,11},{4,20},{5,13},{6,22},{7,15},{8,24},{9,1... | collective-permute-start | bytes 720008 | tf_op jit(solution)/shard_map/ppermute | solution.py:306
  26.2 0.7 collective-permute-start.8
  26.9 0.5 collective-permute-start.7
  27.4 1.5 %collective-permute-start.6 = (bf16[2,96,625]{2,1,0:T(8,128)(2,1)S(1)}, bf16[2,96,625]{2,1,0:T(8,128)(2,1)S(1)}, u32[]{:S(2)}, u32[]{:S(2)}) collective-permute-start(bf16[2,96,625]{2,1,0:T(8,128)(2,1)S(1)} %collective-permute-done.2.refs_0_), channel_id=1, source_target_pairs={{0,8},{1,17},{2,10},{3,19},{4,12},{5,21},{6,14},{7,23},{8,0},{9,25... | collective-permute-start | bytes 720008 | tf_op jit(solution)/shard_map/ppermute | solution.py:305
  28.9 4.5 %collective-permute-done.5.refs_3_ = bf16[2,96,625]{2,1,0:T(8,128)(2,1)S(1)} collective-permute-done((bf16[2,96,625]{2,1,0:T(8,128)(2,1)S(1)}, bf16[2,96,625]{2,1,0:T(8,128)(2,1)S(1)}, u32[]{:S(2)}, u32[]{:S(2)}) %collective-permute-start.5) | collective-permute-done | bytes 240032 | tf_op jit(solution)/shard_map/ppermute | solution.py:306
  33.4 1.6 %copy-done.5 = bf16[1600,625]{1,0:T(8,128)(2,1)S(1)} copy-done((bf16[1600,625]{1,0:T(8,128)(2,1)S(1)}, bf16[1600,625]{1,0:T(8,128)(2,1)}, u32[]{:S(2)}) %copy-start.5) | copy-done | bytes 2000024
  34.9 2.6 %shard_map.82.refs_0_ = bf16[2,1600,384]{2,1,0:T(8,128)(2,1)S(1)} custom-call(s32[1]{0:T(128)} %bitcast.column_ref, bf16[2,96,625]{2,1,0:T(8,128)(2,1)S(1)} %get-tuple-element.34.refs_0_, bf16[2,96,625]{2,1,0:T(8,128)(2,1)S(1)} %collective-permute-done.refs_1_, bf16[2,96,625]{2,1,0:T(8,128)(2,1)S(1)} %collective-permute-done.1.refs_2_, ...), custom_call_target="tpu_custom_call" | custom-call | flops 1536000000 | bytes 3417600 | tf_op jit(solution)/shard_map/pallas_call | solution.py:77
  37.6 0.4 collective-permute-done.8.refs_0_
  38.0 0.0 collective-permute-start.13
  38.0 1.6 %collective-permute-start.9 = (bf16[2,96,625]{2,1,0:T(8,128)(2,1)S(1)}, bf16[2,96,625]{2,1,0:T(8,128)(2,1)S(1)}, u32[]{:S(2)}, u32[]{:S(2)}) collective-permute-start(bf16[2,96,625]{2,1,0:T(8,128)(2,1)S(1)} %collective-permute-done.6.refs_1_), channel_id=1, source_target_pairs={{0,16},{1,9},{2,18},{3,11},{4,20},{5,13},{6,22},{7,15},{8,24},{9,1... | collective-permute-start | bytes 720008 | tf_op jit(solution)/shard_map/ppermute | solution.py:306
  39.6 0.0 collective-permute-start.12
  39.6 0.5 collective-permute-start.11
  40.1 1.2 collective-permute-start.10
  41.3 4.7 %collective-permute-done.9.refs_3_ = bf16[2,96,625]{2,1,0:T(8,128)(2,1)S(1)} collective-permute-done((bf16[2,96,625]{2,1,0:T(8,128)(2,1)S(1)}, bf16[2,96,625]{2,1,0:T(8,128)(2,1)S(1)}, u32[]{:S(2)}, u32[]{:S(2)}) %collective-permute-start.9) | collective-permute-done | bytes 240032 | tf_op jit(solution)/shard_map/ppermute | solution.py:306
  46.0 2.6 %shard_map.83.refs_2_ = bf16[2,1600,384]{2,1,0:T(8,128)(2,1)S(1)} custom-call(s32[1]{0:T(128)} %bitcast.column_ref, bf16[2,96,625]{2,1,0:T(8,128)(2,1)S(1)} %collective-permute-done.2.refs_0_, bf16[2,96,625]{2,1,0:T(8,128)(2,1)S(1)} %collective-permute-done.6.refs_1_, bf16[2,96,625]{2,1,0:T(8,128)(2,1)S(1)} %collective-permute-done.7.refs_2_, ...), custom_call_target="tpu_custom_call" | custom-call | flops 1536000000 | bytes 3417600 | tf_op jit(solution)/shard_map/pallas_call | solution.py:77
  48.7 0.0 copy-start.4
  48.7 0.9 collective-permute-done.11.refs_2_
  49.6 0.0 collective-permute-done.10.refs_1_
  49.6 1.2 collective-permute-done.12.refs_2_
  50.7 0.0 collective-permute-done.13.refs_1_
  50.7 0.0 collective-permute-start.18
  50.7 1.5 %collective-permute-start.14 = (bf16[2,96,625]{2,1,0:T(8,128)(2,1)S(1)}, bf16[2,96,625]{2,1,0:T(8,128)(2,1)S(1)}, u32[]{:S(2)}, u32[]{:S(2)}) collective-permute-start(bf16[2,96,625]{2,1,0:T(8,128)(2,1)S(1)} %collective-permute-done.10.refs_1_), channel_id=1, source_target_pairs={{0,16},{1,9},{2,18},{3,11},{4,20},{5,13},{6,22},{7,15},{8,24},{9,1... | collective-permute-start | bytes 720008 | tf_op jit(solution)/shard_map/ppermute | solution.py:306
  52.3 0.5 collective-permute-start.16
  52.8 0.9 collective-permute-start.15
  53.6 4.9 %collective-permute-done.14.refs_3_ = bf16[2,96,625]{2,1,0:T(8,128)(2,1)S(1)} collective-permute-done((bf16[2,96,625]{2,1,0:T(8,128)(2,1)S(1)}, bf16[2,96,625]{2,1,0:T(8,128)(2,1)S(1)}, u32[]{:S(2)}, u32[]{:S(2)}) %collective-permute-start.14) | collective-permute-done | bytes 240032 | tf_op jit(solution)/shard_map/ppermute | solution.py:306
  58.6 2.6 %shard_map.84.refs_6_ = bf16[2,1600,384]{2,1,0:T(8,128)(2,1)S(1)} custom-call(s32[1]{0:T(128)} %bitcast.column_ref, bf16[2,96,625]{2,1,0:T(8,128)(2,1)S(1)} %collective-permute-done.3.refs_0_, bf16[2,96,625]{2,1,0:T(8,128)(2,1)S(1)} %collective-permute-done.10.refs_1_, bf16[2,96,625]{2,1,0:T(8,128)(2,1)S(1)} %collective-permute-done.11.refs_2_, ...), custom_call_target="tpu_custom_call" | custom-call | flops 1536000000 | bytes 3417600 | tf_op jit(solution)/shard_map/pallas_call | solution.py:77
  61.2 0.0 copy-start.7
  61.2 1.0 collective-permute-done.16.refs_2_
  62.2 1.0 collective-permute-done.17.refs_3_
  63.2 1.5 %collective-permute-start.19 = (bf16[2,96,625]{2,1,0:T(8,128)(2,1)S(1)}, bf16[2,96,625]{2,1,0:T(8,128)(2,1)S(1)}, u32[]{:S(2)}, u32[]{:S(2)}) collective-permute-start(bf16[2,96,625]{2,1,0:T(8,128)(2,1)S(1)} %collective-permute-done.15.refs_1_), channel_id=1, source_target_pairs={{0,16},{1,9},{2,18},{3,11},{4,20},{5,13},{6,22},{7,15},{8,24},{9,1... | collective-permute-start | bytes 720008 | tf_op jit(solution)/shard_map/ppermute | solution.py:306
  64.7 1.4 %shard_map.85.refs_8_ = bf16[8,800,128]{2,1,0:T(8,128)(2,1)S(1)} custom-call(bf16[800,625]{1,0:T(8,128)(2,1)S(1)} %copy-done.4, bf16[625,256]{1,0:T(8,128)(2,1)S(1)} %bitcast.25, bf16[625,256]{1,0:T(8,128)(2,1)S(1)} %collective-permute-done.4.refs_1_, bf16[625,256]{1,0:T(8,128)(2,1)S(1)} %collective-permute-done.12.refs_2_, ...), custom_call_target="tpu_custom_call" | custom-call | flops 1024000000 | bytes 2560000 | tf_op jit(solution)/shard_map/pallas_call | solution.py:108
  66.1 0.0 copy-start.10
  66.2 0.0 copy-start.11
  66.2 3.2 %collective-permute-done.19.refs_3_ = bf16[2,96,625]{2,1,0:T(8,128)(2,1)S(1)} collective-permute-done((bf16[2,96,625]{2,1,0:T(8,128)(2,1)S(1)}, bf16[2,96,625]{2,1,0:T(8,128)(2,1)S(1)}, u32[]{:S(2)}, u32[]{:S(2)}) %collective-permute-start.19) | collective-permute-done | bytes 240032 | tf_op jit(solution)/shard_map/ppermute | solution.py:306
  69.4 3.4 %shard_map.86.refs_4_ = bf16[2,1600,384]{2,1,0:T(8,128)(2,1)} custom-call(s32[1]{0:T(128)} %bitcast.column_ref, bf16[2,96,625]{2,1,0:T(8,128)(2,1)S(1)} %collective-permute-done.8.refs_0_, bf16[2,96,625]{2,1,0:T(8,128)(2,1)S(1)} %collective-permute-done.15.refs_1_, bf16[2,96,625]{2,1,0:T(8,128)(2,1)S(1)} %collective-permute-done.16.refs_2_, ...), custom_call_target="tpu_custom_call" | custom-call | flops 1536000000 | bytes 3417600 | tf_op jit(solution)/shard_map/pallas_call | solution.py:77
  72.8 0.1 collective-permute-start.21
  72.9 1.4 %copy-done.8 = bf16[2,1600,384]{2,1,0:T(8,128)(2,1)} copy-done((bf16[2,1600,384]{2,1,0:T(8,128)(2,1)}, bf16[2,1600,384]{2,1,0:T(8,128)(2,1)S(1)}, u32[]{:S(2)}) %copy-start.8) | copy-done | bytes 2457624
  74.3 0.1 copy.24.owners_ref
  74.4 0.1 copy.25.local_ref
  74.5 5.5 %collective-permute-done.22.refs_9_ = bf16[8,800,128]{2,1,0:T(8,128)(2,1)S(1)} collective-permute-done((bf16[8,800,128]{2,1,0:T(8,128)(2,1)S(1)}, bf16[8,800,128]{2,1,0:T(8,128)(2,1)S(1)}, u32[]{:S(2)}, u32[]{:S(2)}) %collective-permute-start.22) | collective-permute-done | bytes 1638432 | tf_op jit(solution)/shard_map/ppermute | solution.py:292
  79.9 1.3 copy-done.3
  81.2 10.4 %shard_map.88 = bf16[1,2,625,128]{3,2,1,0:T(8,128)(2,1)S(1)} custom-call(s32[1]{0:T(128)} %bitcast.column_ref, s32[32,3]{1,0:T(8,128)S(1)} %copy.24.owners_ref, s32[32,4]{1,0:T(8,128)S(1)} %copy.25.local_ref, bf16[2,1600,384]{2,1,0:T(8,128)(2,1)} %copy-done, bf16[2,1600,384]{2,1,0:T(8,128)(2,1)} %collective-permute-done.13.refs_1_, ...), custom_call_target="tpu_custom_call" | custom-call | flops 2936012800 | bytes 6553600 | tf_op jit(solution)/shard_map/pallas_call | solution.py:257
  91.5 1.3 %collective-permute-start.24 = (bf16[2,625,128]{2,1,0:T(8,128)(2,1)S(1)}, bf16[2,625,128]{2,1,0:T(8,128)(2,1)S(1)}, u32[]{:S(2)}, u32[]{:S(2)}) collective-permute-start(bf16[2,625,128]{2,1,0:T(8,128)(2,1)S(1)} %bitcast.26), channel_id=1, source_target_pairs={{0,6},{1,7},{2,0},{3,1},{4,2},{5,3},{6,4},{7,5},{8,14},{9,15},{10,... | collective-permute-start | bytes 960008 | tf_op jit(solution)/shard_map/ppermute | solution.py:295
  92.9 10.3 %shard_map.87 = bf16[1,2,625,128]{3,2,1,0:T(8,128)(2,1)S(1)} custom-call(s32[1]{0:T(128)} %bitcast.column_ref, s32[32,3]{1,0:T(8,128)S(1)} %copy.24.owners_ref, s32[32,4]{1,0:T(8,128)S(1)} %copy.25.local_ref, bf16[2,1600,384]{2,1,0:T(8,128)(2,1)} %copy-done, bf16[2,1600,384]{2,1,0:T(8,128)(2,1)} %collective-permute-done.13.refs_1_, ...), custom_call_target="tpu_custom_call" | custom-call | flops 2936012800 | bytes 6553600 | tf_op jit(solution)/shard_map/pallas_call | solution.py:257
  103.2 0.1 collective-permute-start.23
  103.3 10.4 %shard_map.89 = bf16[1,2,625,128]{3,2,1,0:T(8,128)(2,1)S(1)} custom-call(s32[1]{0:T(128)} %bitcast.column_ref, s32[32,3]{1,0:T(8,128)S(1)} %copy.24.owners_ref, s32[32,4]{1,0:T(8,128)S(1)} %copy.25.local_ref, bf16[2,1600,384]{2,1,0:T(8,128)(2,1)} %copy-done, bf16[2,1600,384]{2,1,0:T(8,128)(2,1)} %collective-permute-done.13.refs_1_, ...), custom_call_target="tpu_custom_call" | custom-call | flops 2936012800 | bytes 6553600 | tf_op jit(solution)/shard_map/pallas_call | solution.py:257
  113.7 0.0 copy-start.9
  113.7 1.0 collective-permute-start.25
  114.7 10.3 %shard_map.90 = bf16[1,2,625,128]{3,2,1,0:T(8,128)(2,1)S(1)} custom-call(s32[1]{0:T(128)} %bitcast.column_ref, s32[32,3]{1,0:T(8,128)S(1)} %copy.24.owners_ref, s32[32,4]{1,0:T(8,128)S(1)} %copy.25.local_ref, bf16[2,1600,384]{2,1,0:T(8,128)(2,1)} %copy-done, bf16[2,1600,384]{2,1,0:T(8,128)(2,1)} %collective-permute-done.13.refs_1_, ...), custom_call_target="tpu_custom_call" | custom-call | flops 2936012800 | bytes 6553600 | tf_op jit(solution)/shard_map/pallas_call | solution.py:257
  125.0 2.4 %collective-permute-done.23 = bf16[2,625,128]{2,1,0:T(8,128)(2,1)S(1)} collective-permute-done((bf16[2,625,128]{2,1,0:T(8,128)(2,1)S(1)}, bf16[2,625,128]{2,1,0:T(8,128)(2,1)S(1)}, u32[]{:S(2)}, u32[]{:S(2)}) %collective-permute-start.23) | collective-permute-done | bytes 320032 | tf_op jit(solution)/shard_map/ppermute | solution.py:295
  127.4 0.2 fusion.1
  127.6 1.2 copy.33
  (29 shorter events, 0.1 us)
Async XLA Ops:
  1.3 23.3 %collective-permute-start.4 = (bf16[625,256]{1,0:T(8,128)(2,1)S(1)}, bf16[625,256]{1,0:T(8,128)(2,1)S(1)}, u32[]{:S(2)}, u32[]{:S(2)}) collective-permute-start(bf16[625,256]{1,0:T(8,128)(2,1)S(1)} %bitcast.24), channel_id=1, source_target_pairs={{0,2},{1,3},{2,4},{3,5},{4,6},{5,7},{6,0},{7,1},{8,10},{9,11},{10,... | collective-permute-start | bytes 960008 | tf_op jit(solution)/shard_map/ppermute | solution.py:295
  7.8 12.2 %collective-permute-start.3 = (bf16[2,96,625]{2,1,0:T(8,128)(2,1)S(1)}, bf16[2,96,625]{2,1,0:T(8,128)(2,1)S(1)}, u32[]{:S(2)}, u32[]{:S(2)}) collective-permute-start(bf16[2,96,625]{2,1,0:T(8,128)(2,1)S(1)} %get-tuple-element.64), channel_id=1, source_target_pairs={{0,6},{1,7},{2,0},{3,1},{4,2},{5,3},{6,4},{7,5},{8,14},{9,15},{10,... | collective-permute-start | bytes 720008 | tf_op jit(solution)/shard_map/ppermute | solution.py:295
  10.0 14.5 %collective-permute-start.2 = (bf16[2,96,625]{2,1,0:T(8,128)(2,1)S(1)}, bf16[2,96,625]{2,1,0:T(8,128)(2,1)S(1)}, u32[]{:S(2)}, u32[]{:S(2)}) collective-permute-start(bf16[2,96,625]{2,1,0:T(8,128)(2,1)S(1)} %get-tuple-element.65), channel_id=1, source_target_pairs={{0,2},{1,3},{2,4},{3,5},{4,6},{5,7},{6,0},{7,1},{8,10},{9,11},{10,... | collective-permute-start | bytes 720008 | tf_op jit(solution)/shard_map/ppermute | solution.py:295
  10.0 14.5 %collective-permute-start.1 = (bf16[2,96,625]{2,1,0:T(8,128)(2,1)S(1)}, bf16[2,96,625]{2,1,0:T(8,128)(2,1)S(1)}, u32[]{:S(2)}, u32[]{:S(2)}) collective-permute-start(bf16[2,96,625]{2,1,0:T(8,128)(2,1)S(1)} %get-tuple-element.34.refs_0_), channel_id=1, source_target_pairs={{0,16},{1,9},{2,18},{3,11},{4,20},{5,13},{6,22},{7,15},{8,24},{9,1... | collective-permute-start | bytes 720008 | tf_op jit(solution)/shard_map/ppermute | solution.py:306
  11.7 12.9 %collective-permute-start = (bf16[2,96,625]{2,1,0:T(8,128)(2,1)S(1)}, bf16[2,96,625]{2,1,0:T(8,128)(2,1)S(1)}, u32[]{:S(2)}, u32[]{:S(2)}) collective-permute-start(bf16[2,96,625]{2,1,0:T(8,128)(2,1)S(1)} %get-tuple-element.34.refs_0_), channel_id=1, source_target_pairs={{0,8},{1,17},{2,10},{3,19},{4,12},{5,21},{6,14},{7,23},{8,0},{9,25... | collective-permute-start | bytes 720008 | tf_op jit(solution)/shard_map/ppermute | solution.py:305
  24.6 8.8 %collective-permute-start.5 = (bf16[2,96,625]{2,1,0:T(8,128)(2,1)S(1)}, bf16[2,96,625]{2,1,0:T(8,128)(2,1)S(1)}, u32[]{:S(2)}, u32[]{:S(2)}) collective-permute-start(bf16[2,96,625]{2,1,0:T(8,128)(2,1)S(1)} %collective-permute-done.refs_1_), channel_id=1, source_target_pairs={{0,16},{1,9},{2,18},{3,11},{4,20},{5,13},{6,22},{7,15},{8,24},{9,1... | collective-permute-start | bytes 720008 | tf_op jit(solution)/shard_map/ppermute | solution.py:306
  26.2 11.8 %collective-permute-start.8 = (bf16[2,96,625]{2,1,0:T(8,128)(2,1)S(1)}, bf16[2,96,625]{2,1,0:T(8,128)(2,1)S(1)}, u32[]{:S(2)}, u32[]{:S(2)}) collective-permute-start(bf16[2,96,625]{2,1,0:T(8,128)(2,1)S(1)} %get-tuple-element.38), channel_id=1, source_target_pairs={{0,4},{1,5},{2,6},{3,7},{4,0},{5,1},{6,2},{7,3},{8,12},{9,13},{10,... | collective-permute-start | bytes 720008 | tf_op jit(solution)/shard_map/ppermute | solution.py:295
  26.9 11.2 %collective-permute-start.7 = (bf16[2,96,625]{2,1,0:T(8,128)(2,1)S(1)}, bf16[2,96,625]{2,1,0:T(8,128)(2,1)S(1)}, u32[]{:S(2)}, u32[]{:S(2)}) collective-permute-start(bf16[2,96,625]{2,1,0:T(8,128)(2,1)S(1)} %collective-permute-done.2.refs_0_), channel_id=1, source_target_pairs={{0,16},{1,9},{2,18},{3,11},{4,20},{5,13},{6,22},{7,15},{8,24},{9,1... | collective-permute-start | bytes 720008 | tf_op jit(solution)/shard_map/ppermute | solution.py:306
  27.4 10.7 %collective-permute-start.6 = (bf16[2,96,625]{2,1,0:T(8,128)(2,1)S(1)}, bf16[2,96,625]{2,1,0:T(8,128)(2,1)S(1)}, u32[]{:S(2)}, u32[]{:S(2)}) collective-permute-start(bf16[2,96,625]{2,1,0:T(8,128)(2,1)S(1)} %collective-permute-done.2.refs_0_), channel_id=1, source_target_pairs={{0,8},{1,17},{2,10},{3,19},{4,12},{5,21},{6,14},{7,23},{8,0},{9,25... | collective-permute-start | bytes 720008 | tf_op jit(solution)/shard_map/ppermute | solution.py:305
  33.4 1.6 %copy-start.5 = (bf16[1600,625]{1,0:T(8,128)(2,1)S(1)}, bf16[1600,625]{1,0:T(8,128)(2,1)}, u32[]{:S(2)}) copy-start(bf16[1600,625]{1,0:T(8,128)(2,1)} %constant.61.clone.refs_4_) | copy-start | bytes 6000004
  34.9 11.1 %copy-start.6 = (bf16[1600,625]{1,0:T(8,128)(2,1)S(1)}, bf16[1600,625]{1,0:T(8,128)(2,1)}, u32[]{:S(2)}) copy-start(bf16[1600,625]{1,0:T(8,128)(2,1)} %constant.61.clone.refs_4_) | copy-start | bytes 6000004
  37.6 11.1 %copy-start = (bf16[2,1600,384]{2,1,0:T(8,128)(2,1)}, bf16[2,1600,384]{2,1,0:T(8,128)(2,1)S(1)}, u32[]{:S(2)}) copy-start(bf16[2,1600,384]{2,1,0:T(8,128)(2,1)S(1)} %shard_map.82.refs_0_) | copy-start | bytes 7372804
  38.0 12.7 %collective-permute-start.13 = (bf16[2,1600,384]{2,1,0:T(8,128)(2,1)S(1)}, bf16[2,1600,384]{2,1,0:T(8,128)(2,1)}, u32[]{:S(2)}, u32[]{:S(2)}) collective-permute-start(bf16[2,1600,384]{2,1,0:T(8,128)(2,1)S(1)} %shard_map.82.refs_0_), channel_id=1, source_target_pairs={{0,1},{1,0},{2,3},{3,2},{4,5},{5,4},{6,7},{7,6},{8,9},{9,8},{10,11... | collective-permute-start | bytes 7372808 | tf_op jit(solution)/shard_map/ppermute | solution.py:292
  38.0 8.0 %collective-permute-start.9 = (bf16[2,96,625]{2,1,0:T(8,128)(2,1)S(1)}, bf16[2,96,625]{2,1,0:T(8,128)(2,1)S(1)}, u32[]{:S(2)}, u32[]{:S(2)}) collective-permute-start(bf16[2,96,625]{2,1,0:T(8,128)(2,1)S(1)} %collective-permute-done.6.refs_1_), channel_id=1, source_target_pairs={{0,16},{1,9},{2,18},{3,11},{4,20},{5,13},{6,22},{7,15},{8,24},{9,1... | collective-permute-start | bytes 720008 | tf_op jit(solution)/shard_map/ppermute | solution.py:306
  39.6 11.1 %collective-permute-start.12 = (bf16[625,256]{1,0:T(8,128)(2,1)S(1)}, bf16[625,256]{1,0:T(8,128)(2,1)S(1)}, u32[]{:S(2)}, u32[]{:S(2)}) collective-permute-start(bf16[625,256]{1,0:T(8,128)(2,1)S(1)} %collective-permute-done.4.refs_1_), channel_id=1, source_target_pairs={{0,2},{1,3},{2,4},{3,5},{4,6},{5,7},{6,0},{7,1},{8,10},{9,11},{10,... | collective-permute-start | bytes 960008 | tf_op jit(solution)/shard_map/ppermute | solution.py:295
  39.6 9.9 %collective-permute-start.11 = (bf16[2,96,625]{2,1,0:T(8,128)(2,1)S(1)}, bf16[2,96,625]{2,1,0:T(8,128)(2,1)S(1)}, u32[]{:S(2)}, u32[]{:S(2)}) collective-permute-start(bf16[2,96,625]{2,1,0:T(8,128)(2,1)S(1)} %collective-permute-done.3.refs_0_), channel_id=1, source_target_pairs={{0,16},{1,9},{2,18},{3,11},{4,20},{5,13},{6,22},{7,15},{8,24},{9,1... | collective-permute-start | bytes 720008 | tf_op jit(solution)/shard_map/ppermute | solution.py:306
  40.1 9.4 %collective-permute-start.10 = (bf16[2,96,625]{2,1,0:T(8,128)(2,1)S(1)}, bf16[2,96,625]{2,1,0:T(8,128)(2,1)S(1)}, u32[]{:S(2)}, u32[]{:S(2)}) collective-permute-start(bf16[2,96,625]{2,1,0:T(8,128)(2,1)S(1)} %collective-permute-done.3.refs_0_), channel_id=1, source_target_pairs={{0,8},{1,17},{2,10},{3,19},{4,12},{5,21},{6,14},{7,23},{8,0},{9,25... | collective-permute-start | bytes 720008 | tf_op jit(solution)/shard_map/ppermute | solution.py:305
  48.7 12.6 %copy-start.1 = (bf16[2,1600,384]{2,1,0:T(8,128)(2,1)}, bf16[2,1600,384]{2,1,0:T(8,128)(2,1)S(1)}, u32[]{:S(2)}) copy-start(bf16[2,1600,384]{2,1,0:T(8,128)(2,1)S(1)} %shard_map.83.refs_2_) | copy-start | bytes 7372804
  48.7 16.0 %copy-start.4 = (bf16[800,625]{1,0:T(8,128)(2,1)S(1)}, bf16[800,625]{1,0:T(8,128)(2,1)}, u32[]{:S(2)}) copy-start(bf16[800,625]{1,0:T(8,128)(2,1)} %constant.63.clone.matrix_ref) | copy-start | bytes 3000004
  50.7 12.4 %collective-permute-start.18 = (bf16[2,1600,384]{2,1,0:T(8,128)(2,1)S(1)}, bf16[2,1600,384]{2,1,0:T(8,128)(2,1)}, u32[]{:S(2)}, u32[]{:S(2)}) collective-permute-start(bf16[2,1600,384]{2,1,0:T(8,128)(2,1)S(1)} %shard_map.83.refs_2_), channel_id=1, source_target_pairs={{0,1},{1,0},{2,3},{3,2},{4,5},{5,4},{6,7},{7,6},{8,9},{9,8},{10,11... | collective-permute-start | bytes 7372808 | tf_op jit(solution)/shard_map/ppermute | solution.py:292
  50.7 7.8 %collective-permute-start.14 = (bf16[2,96,625]{2,1,0:T(8,128)(2,1)S(1)}, bf16[2,96,625]{2,1,0:T(8,128)(2,1)S(1)}, u32[]{:S(2)}, u32[]{:S(2)}) collective-permute-start(bf16[2,96,625]{2,1,0:T(8,128)(2,1)S(1)} %collective-permute-done.10.refs_1_), channel_id=1, source_target_pairs={{0,16},{1,9},{2,18},{3,11},{4,20},{5,13},{6,22},{7,15},{8,24},{9,1... | collective-permute-start | bytes 720008 | tf_op jit(solution)/shard_map/ppermute | solution.py:306
  52.3 10.9 %collective-permute-start.17 = (bf16[625,256]{1,0:T(8,128)(2,1)S(1)}, bf16[625,256]{1,0:T(8,128)(2,1)S(1)}, u32[]{:S(2)}, u32[]{:S(2)}) collective-permute-start(bf16[625,256]{1,0:T(8,128)(2,1)S(1)} %collective-permute-done.12.refs_2_), channel_id=1, source_target_pairs={{0,2},{1,3},{2,4},{3,5},{4,6},{5,7},{6,0},{7,1},{8,10},{9,11},{10,... | collective-permute-start | bytes 960008 | tf_op jit(solution)/shard_map/ppermute | solution.py:295
  52.3 9.9 %collective-permute-start.16 = (bf16[2,96,625]{2,1,0:T(8,128)(2,1)S(1)}, bf16[2,96,625]{2,1,0:T(8,128)(2,1)S(1)}, u32[]{:S(2)}, u32[]{:S(2)}) collective-permute-start(bf16[2,96,625]{2,1,0:T(8,128)(2,1)S(1)} %collective-permute-done.8.refs_0_), channel_id=1, source_target_pairs={{0,16},{1,9},{2,18},{3,11},{4,20},{5,13},{6,22},{7,15},{8,24},{9,1... | collective-permute-start | bytes 720008 | tf_op jit(solution)/shard_map/ppermute | solution.py:306
  52.8 9.4 %collective-permute-start.15 = (bf16[2,96,625]{2,1,0:T(8,128)(2,1)S(1)}, bf16[2,96,625]{2,1,0:T(8,128)(2,1)S(1)}, u32[]{:S(2)}, u32[]{:S(2)}) collective-permute-start(bf16[2,96,625]{2,1,0:T(8,128)(2,1)S(1)} %collective-permute-done.8.refs_0_), channel_id=1, source_target_pairs={{0,8},{1,17},{2,10},{3,19},{4,12},{5,21},{6,14},{7,23},{8,0},{9,25... | collective-permute-start | bytes 720008 | tf_op jit(solution)/shard_map/ppermute | solution.py:305
  61.2 11.6 %copy-start.2 = (bf16[2,1600,384]{2,1,0:T(8,128)(2,1)}, bf16[2,1600,384]{2,1,0:T(8,128)(2,1)S(1)}, u32[]{:S(2)}) copy-start(bf16[2,1600,384]{2,1,0:T(8,128)(2,1)S(1)} %shard_map.84.refs_6_) | copy-start | bytes 7372804
  61.2 8.1 %copy-start.7 = (bf16[1600,625]{1,0:T(8,128)(2,1)S(1)}, bf16[1600,625]{1,0:T(8,128)(2,1)}, u32[]{:S(2)}) copy-start(bf16[1600,625]{1,0:T(8,128)(2,1)} %constant.61.clone.refs_4_) | copy-start | bytes 6000004
  63.2 9.7 %collective-permute-start.20 = (bf16[2,1600,384]{2,1,0:T(8,128)(2,1)S(1)}, bf16[2,1600,384]{2,1,0:T(8,128)(2,1)S(1)}, u32[]{:S(2)}, u32[]{:S(2)}) collective-permute-start(bf16[2,1600,384]{2,1,0:T(8,128)(2,1)S(1)} %shard_map.84.refs_6_), channel_id=1, source_target_pairs={{0,1},{1,0},{2,3},{3,2},{4,5},{5,4},{6,7},{7,6},{8,9},{9,8},{10,11... | collective-permute-start | bytes 7372808 | tf_op jit(solution)/shard_map/ppermute | solution.py:292
  63.2 6.2 %collective-permute-start.19 = (bf16[2,96,625]{2,1,0:T(8,128)(2,1)S(1)}, bf16[2,96,625]{2,1,0:T(8,128)(2,1)S(1)}, u32[]{:S(2)}, u32[]{:S(2)}) collective-permute-start(bf16[2,96,625]{2,1,0:T(8,128)(2,1)S(1)} %collective-permute-done.15.refs_1_), channel_id=1, source_target_pairs={{0,16},{1,9},{2,18},{3,11},{4,20},{5,13},{6,22},{7,15},{8,24},{9,1... | collective-permute-start | bytes 720008 | tf_op jit(solution)/shard_map/ppermute | solution.py:306
  66.1 8.1 %copy-start.10 = (s32[32,3]{0,1:T(4,128)S(1)}, s32[32,3]{0,1:T(4,128)}, u32[]{:S(2)}) copy-start(s32[32,3]{0,1:T(4,128)} %param.11) | copy-start | bytes 1156
  66.2 8.2 %copy-start.11 = (s32[32,4]{0,1:T(4,128)S(1)}, s32[32,4]{0,1:T(4,128)}, u32[]{:S(2)}) copy-start(s32[32,4]{0,1:T(4,128)} %param.12) | copy-start | bytes 1540
  72.8 1.4 %copy-start.8 = (bf16[2,1600,384]{2,1,0:T(8,128)(2,1)}, bf16[2,1600,384]{2,1,0:T(8,128)(2,1)S(1)}, u32[]{:S(2)}) copy-start(bf16[2,1600,384]{2,1,0:T(8,128)(2,1)S(1)} %collective-permute-done.20.refs_7_) | copy-start | bytes 7372804
  72.8 7.1 %collective-permute-start.21 = (bf16[2,1600,384]{2,1,0:T(8,128)(2,1)}, bf16[2,1600,384]{2,1,0:T(8,128)(2,1)}, u32[]{:S(2)}, u32[]{:S(2)}) collective-permute-start(bf16[2,1600,384]{2,1,0:T(8,128)(2,1)} %shard_map.86.refs_4_), channel_id=1, source_target_pairs={{0,1},{1,0},{2,3},{3,2},{4,5},{5,4},{6,7},{7,6},{8,9},{9,8},{10,11... | collective-permute-start | bytes 7372808 | tf_op jit(solution)/shard_map/ppermute | solution.py:292
  74.3 5.6 %collective-permute-start.22 = (bf16[8,800,128]{2,1,0:T(8,128)(2,1)S(1)}, bf16[8,800,128]{2,1,0:T(8,128)(2,1)S(1)}, u32[]{:S(2)}, u32[]{:S(2)}) collective-permute-start(bf16[8,800,128]{2,1,0:T(8,128)(2,1)S(1)} %shard_map.85.refs_8_), channel_id=1, source_target_pairs={{0,1},{1,0},{2,3},{3,2},{4,5},{5,4},{6,7},{7,6},{8,9},{9,8},{10,11... | collective-permute-start | bytes 4915208 | tf_op jit(solution)/shard_map/ppermute | solution.py:292
  79.9 1.3 copy-start.3
  91.5 33.5 %collective-permute-start.24 = (bf16[2,625,128]{2,1,0:T(8,128)(2,1)S(1)}, bf16[2,625,128]{2,1,0:T(8,128)(2,1)S(1)}, u32[]{:S(2)}, u32[]{:S(2)}) collective-permute-start(bf16[2,625,128]{2,1,0:T(8,128)(2,1)S(1)} %bitcast.26), channel_id=1, source_target_pairs={{0,6},{1,7},{2,0},{3,1},{4,2},{5,3},{6,4},{7,5},{8,14},{9,15},{10,... | collective-permute-start | bytes 960008 | tf_op jit(solution)/shard_map/ppermute | solution.py:295
  103.2 24.2 %collective-permute-start.23 = (bf16[2,625,128]{2,1,0:T(8,128)(2,1)S(1)}, bf16[2,625,128]{2,1,0:T(8,128)(2,1)S(1)}, u32[]{:S(2)}, u32[]{:S(2)}) collective-permute-start(bf16[2,625,128]{2,1,0:T(8,128)(2,1)S(1)} %bitcast.27), channel_id=1, source_target_pairs={{0,4},{1,5},{2,6},{3,7},{4,0},{5,1},{6,2},{7,3},{8,12},{9,13},{10,... | collective-permute-start | bytes 960008 | tf_op jit(solution)/shard_map/ppermute | solution.py:295
  113.7 13.8 %copy-start.9 = (f32[2,128,625]{1,0,2:T(2,128)S(1)}, f32[2,128,625]{1,0,2:T(2,128)}, u32[]{:S(2)}) copy-start(f32[2,128,625]{1,0,2:T(2,128)} %param.10) | copy-start | bytes 1920004
  113.7 13.8 %collective-permute-start.25 = (bf16[2,625,128]{2,1,0:T(8,128)(2,1)S(1)}, bf16[2,625,128]{2,1,0:T(8,128)(2,1)S(1)}, u32[]{:S(2)}, u32[]{:S(2)}) collective-permute-start(bf16[2,625,128]{2,1,0:T(8,128)(2,1)S(1)} %bitcast.28), channel_id=1, source_target_pairs={{0,2},{1,3},{2,4},{3,5},{4,6},{5,7},{6,0},{7,1},{8,10},{9,11},{10,... | collective-permute-start | bytes 960008 | tf_op jit(solution)/shard_map/ppermute | solution.py:295

commit v11 on v10

--- a/solution.py
+++ b/solution.py
@@ -308,28 +308,30 @@
         own = amplitudes.transpose(2, 0, 1).reshape(TV * TV, blocks_here * pairs)
         amp1 = around(own, 1)
         part0 = mine[0]
-        a0, b0, part1, part3 = first_side(part0), second_side(part0), around(mine[1], 1), around(mine[3], 3)
-
-        a0, b0, part0, part1, part3, amp1, to2 = after((a0, b0, part0, part1, part3, amp1, mine[2]), ())
-        q0, a1, b1, part2 = second_side(a0), first_side(part1), second_side(part1), around(to2, 2)
+        a0, b0, part1 = first_side(part0), second_side(part0), around(mine[1], 1)
+
+        a0, b0, part0, part1, amp1, to3 = after((a0, b0, part0, part1, amp1, mine[3]), ())
+        q0, a1, b1, part3 = second_side(a0), first_side(part1), second_side(part1), around(to3, 3)
         forms0 = made_forms(part0, a0, b0, q0)
 
-        forms0, part1, a1, b1, part2, part3, amp1 = after((forms0, part1, a1, b1, part2, part3, amp1), ())
-        q1, a3, b3, amp2 = second_side(a1), first_side(part3), second_side(part3), around(amp1, 1)
+        forms0, part1, a1, b1, part3, to2 = after((forms0, part1, a1, b1, part3, mine[2]), ())
+        q1, a3, b3, part2 = second_side(a1), first_side(part3), second_side(part3), around(to2, 2)
         far0 = other_core(forms0)
         forms1 = made_forms(part1, a1, b1, q1)
 
-        forms1, part3, a3, b3, part2, amp2, far0 = after((forms1, part3, a3, b3, part2, amp2, far0), ())
-        q3, a2, b2, amp3 = second_side(a3), first_side(part2), second_side(part2), around(amp2, 1)
+        forms1, part3, a3, b3, part2, amp1, far0 = after((forms1, part3, a3, b3, part2, amp1, far0), ())
+        q3, a2, b2, amp2 = second_side(a3), first_side(part2), second_side(part2), around(amp1, 1)
         far1 = other_core(forms1)
         forms3 = made_forms(part3, a3, b3, q3)
 
-        forms3, part2, a2, b2, amp3, far1 = after((forms3, part2, a2, b2, amp3, far1), ())
-        q2 = second_side(a2)
+        forms3, part2, a2, b2, amp2, far1 = after((forms3, part2, a2, b2, amp2, far1), ())
+        q2, amp3 = second_side(a2), around(amp2, 1)
         far3 = other_core(forms3)
+        forms2 = made_forms(part2, a2, b2, q2)
+
+        forms2, amp3, far3 = after((forms2, amp3, far3), ())
+        far2 = other_core(forms2)
         amps = prepare_amps([own, amp1, amp2, amp3], blocks_here, jnp.asarray(amp_matrix()))
-        forms2 = made_forms(part2, a2, b2, after(q2, amps))
-        far2 = other_core(after(forms2, far3))
         held = [forms0, far0, forms1, far1, forms2, far2, forms3, far3]
     else:
         parts = [mine[0]] + [around(mine[by], by) for by in range(1, levels)]

time: 129 us -> 128 us (level)
  waiting for transfers between devices: 41.1 us -> 38.1 us
  starting transfers between devices: 22.8 us -> 25.5 us
    ppermute x8, waiting for transfers between devices: 19.2 us -> 15.4 us  [per_device(): second_side = lambda x: lax.ppermute(x, ('pair', 'task'), sides[1])]
    ppermute x9, waiting for transfers between devices: 16.4 us -> 17.9 us  [around(): lax.ppermute(x, 'task', [(c, (c + 2 * by) % task_count) for c in range(ta...]
    ppermute x9, starting transfers between devices: 8.36 us -> 9.79 us  [around(): lax.ppermute(x, 'task', [(c, (c + 2 * by) % task_count) for c in range(ta...]
  transfers between devices with their start and end apart: 26 -> 26, of which waited for: 13 -> 11; matrix products, arithmetic and copies ran while one was open for 3% -> 3% of each run, Pallas kernels for 34% -> 34%
where the time goes in v11:
time: 128 us; the launch traced here: 127 us
  Pallas kernels  54.2 us (42%)
  waiting for transfers between devices  38.1 us (30%)
  starting transfers between devices  25.5 us (20%)
  local copies, waits for them, and re-layouts  9.07 us (7%)
    pallas_call x4, Pallas kernels, ladders(): pl.pallas_call(functools.partial(ladder_kernel, find, made, len(tiles)),...  41.4 us
    ppermute x9, waiting for transfers between devices, around(): lax.ppermute(x, 'task', [(c, (c + 2 * by) % task_count) for c in range(ta...  17.9 us
    ppermute x8, waiting for transfers between devices, per_device(): second_side = lambda x: lax.ppermute(x, ('pair', 'task'), sides[1])  15.4 us
    pallas_call x4, Pallas kernels, prepare(): pl.pallas_call(prepare_kernel, out_shape=jax.ShapeDtypeStruct((count, mat...  11.4 us
    ppermute x9, starting transfers between devices, around(): lax.ppermute(x, 'task', [(c, (c + 2 * by) % task_count) for c in range(ta...  9.79 us
    ppermute x8, starting transfers between devices, per_device(): second_side = lambda x: lax.ppermute(x, ('pair', 'task'), sides[1])  9.32 us
    unnamed x29, local copies, waits for them, and re-layouts  7.79 us
    ppermute x4, starting transfers between devices, per_device(): first_side = lambda x: lax.ppermute(x, ('pair', 'task'), sides[0])  5.66 us
  transfers between devices with their start and end apart: 26, of which 11 were waited for; matrix products, arithmetic and copies ran while one was open for 3% of the time, Pallas kernels for 34%

profile of v11, /device:TPU:0, one launch (start us, length us, event | category | flops | bytes accessed | tf_op | source)
XLA Modules:
  0.0 127.3 jit_solution(399207476199274747)
XLA Ops:
  0.0 1.2 pad
  1.3 3.1 %collective-permute-start.3 = (bf16[625,256]{1,0:T(8,128)(2,1)S(1)}, bf16[625,256]{1,0:T(8,128)(2,1)S(1)}, u32[]{:S(2)}, u32[]{:S(2)}) collective-permute-start(bf16[625,256]{1,0:T(8,128)(2,1)S(1)} %bitcast.24), channel_id=1, source_target_pairs={{0,2},{1,3},{2,4},{3,5},{4,6},{5,7},{6,0},{7,1},{8,10},{9,11},{10,... | collective-permute-start | bytes 960008 | tf_op jit(solution)/shard_map/ppermute | solution.py:295
  4.4 3.3 %copy.23 = bf16[2,384,625]{2,1,0:T(8,128)(2,1)S(1)} copy(bf16[2,384,625]{1,0,2:T(2,128)(2,1)} %param.8) | data formatting | bytes 1920000 | tf_op args[0]
  7.7 0.1 dynamic-slice_bitcast_fusion
  7.8 1.6 %collective-permute-start.2 = (bf16[2,96,625]{2,1,0:T(8,128)(2,1)S(1)}, bf16[2,96,625]{2,1,0:T(8,128)(2,1)S(1)}, u32[]{:S(2)}, u32[]{:S(2)}) collective-permute-start(bf16[2,96,625]{2,1,0:T(8,128)(2,1)S(1)} %get-tuple-element.63), channel_id=1, source_target_pairs={{0,2},{1,3},{2,4},{3,5},{4,6},{5,7},{6,0},{7,1},{8,10},{9,11},{10,... | collective-permute-start | bytes 720008 | tf_op jit(solution)/shard_map/ppermute | solution.py:295
  9.5 1.5 %collective-permute-start.1 = (bf16[2,96,625]{2,1,0:T(8,128)(2,1)S(1)}, bf16[2,96,625]{2,1,0:T(8,128)(2,1)S(1)}, u32[]{:S(2)}, u32[]{:S(2)}) collective-permute-start(bf16[2,96,625]{2,1,0:T(8,128)(2,1)S(1)} %get-tuple-element.33.refs_0_), channel_id=1, source_target_pairs={{0,16},{1,9},{2,18},{3,11},{4,20},{5,13},{6,22},{7,15},{8,24},{9,1... | collective-permute-start | bytes 720008 | tf_op jit(solution)/shard_map/ppermute | solution.py:306
  11.0 1.5 %collective-permute-start = (bf16[2,96,625]{2,1,0:T(8,128)(2,1)S(1)}, bf16[2,96,625]{2,1,0:T(8,128)(2,1)S(1)}, u32[]{:S(2)}, u32[]{:S(2)}) collective-permute-start(bf16[2,96,625]{2,1,0:T(8,128)(2,1)S(1)} %get-tuple-element.33.refs_0_), channel_id=1, source_target_pairs={{0,8},{1,17},{2,10},{3,19},{4,12},{5,21},{6,14},{7,23},{8,0},{9,25... | collective-permute-start | bytes 720008 | tf_op jit(solution)/shard_map/ppermute | solution.py:305
  12.5 6.8 %collective-permute-done.2.refs_0_ = bf16[2,96,625]{2,1,0:T(8,128)(2,1)S(1)} collective-permute-done((bf16[2,96,625]{2,1,0:T(8,128)(2,1)S(1)}, bf16[2,96,625]{2,1,0:T(8,128)(2,1)S(1)}, u32[]{:S(2)}, u32[]{:S(2)}) %collective-permute-start.2) | collective-permute-done | bytes 240032 | tf_op jit(solution)/shard_map/ppermute | solution.py:295
  19.3 0.0 collective-permute-done.1.refs_2_
  19.3 0.0 collective-permute-done.refs_1_
  19.3 1.6 %collective-permute-start.4 = (bf16[2,96,625]{2,1,0:T(8,128)(2,1)S(1)}, bf16[2,96,625]{2,1,0:T(8,128)(2,1)S(1)}, u32[]{:S(2)}, u32[]{:S(2)}) collective-permute-start(bf16[2,96,625]{2,1,0:T(8,128)(2,1)S(1)} %collective-permute-done.refs_1_), channel_id=1, source_target_pairs={{0,16},{1,9},{2,18},{3,11},{4,20},{5,13},{6,22},{7,15},{8,24},{9,1... | collective-permute-start | bytes 720008 | tf_op jit(solution)/shard_map/ppermute | solution.py:306
  20.9 1.7 %collective-permute-start.7 = (bf16[2,96,625]{2,1,0:T(8,128)(2,1)S(1)}, bf16[2,96,625]{2,1,0:T(8,128)(2,1)S(1)}, u32[]{:S(2)}, u32[]{:S(2)}) collective-permute-start(bf16[2,96,625]{2,1,0:T(8,128)(2,1)S(1)} %get-tuple-element.37), channel_id=1, source_target_pairs={{0,6},{1,7},{2,0},{3,1},{4,2},{5,3},{6,4},{7,5},{8,14},{9,15},{10,... | collective-permute-start | bytes 720008 | tf_op jit(solution)/shard_map/ppermute | solution.py:295
  22.6 0.5 collective-permute-start.6
  23.1 1.5 %collective-permute-start.5 = (bf16[2,96,625]{2,1,0:T(8,128)(2,1)S(1)}, bf16[2,96,625]{2,1,0:T(8,128)(2,1)S(1)}, u32[]{:S(2)}, u32[]{:S(2)}) collective-permute-start(bf16[2,96,625]{2,1,0:T(8,128)(2,1)S(1)} %collective-permute-done.2.refs_0_), channel_id=1, source_target_pairs={{0,8},{1,17},{2,10},{3,19},{4,12},{5,21},{6,14},{7,23},{8,0},{9,25... | collective-permute-start | bytes 720008 | tf_op jit(solution)/shard_map/ppermute | solution.py:305
  24.6 2.7 %collective-permute-done.4.refs_3_ = bf16[2,96,625]{2,1,0:T(8,128)(2,1)S(1)} collective-permute-done((bf16[2,96,625]{2,1,0:T(8,128)(2,1)S(1)}, bf16[2,96,625]{2,1,0:T(8,128)(2,1)S(1)}, u32[]{:S(2)}, u32[]{:S(2)}) %collective-permute-start.4) | collective-permute-done | bytes 240032 | tf_op jit(solution)/shard_map/ppermute | solution.py:306
  27.3 1.6 %copy-done.5 = bf16[1600,625]{1,0:T(8,128)(2,1)S(1)} copy-done((bf16[1600,625]{1,0:T(8,128)(2,1)S(1)}, bf16[1600,625]{1,0:T(8,128)(2,1)}, u32[]{:S(2)}) %copy-start.5) | copy-done | bytes 2000024
  28.8 2.6 %shard_map.82.refs_0_ = bf16[2,1600,384]{2,1,0:T(8,128)(2,1)S(1)} custom-call(s32[1]{0:T(128)} %bitcast.column_ref, bf16[2,96,625]{2,1,0:T(8,128)(2,1)S(1)} %get-tuple-element.33.refs_0_, bf16[2,96,625]{2,1,0:T(8,128)(2,1)S(1)} %collective-permute-done.refs_1_, bf16[2,96,625]{2,1,0:T(8,128)(2,1)S(1)} %collective-permute-done.1.refs_2_, ...), custom_call_target="tpu_custom_call" | custom-call | flops 1536000000 | bytes 3417600 | tf_op jit(solution)/shard_map/pallas_call | solution.py:77
  31.5 0.0 collective-permute-done.7.refs_0_
  31.5 0.0 collective-permute-done.6.refs_2_
  31.5 0.1 collective-permute-start.12
  31.6 1.6 %collective-permute-start.8 = (bf16[2,96,625]{2,1,0:T(8,128)(2,1)S(1)}, bf16[2,96,625]{2,1,0:T(8,128)(2,1)S(1)}, u32[]{:S(2)}, u32[]{:S(2)}) collective-permute-start(bf16[2,96,625]{2,1,0:T(8,128)(2,1)S(1)} %collective-permute-done.5.refs_1_), channel_id=1, source_target_pairs={{0,16},{1,9},{2,18},{3,11},{4,20},{5,13},{6,22},{7,15},{8,24},{9,1... | collective-permute-start | bytes 720008 | tf_op jit(solution)/shard_map/ppermute | solution.py:306
  33.2 1.0 collective-permute-start.11
  34.2 0.5 collective-permute-start.10
  34.7 1.8 %collective-permute-start.9 = (bf16[2,96,625]{2,1,0:T(8,128)(2,1)S(1)}, bf16[2,96,625]{2,1,0:T(8,128)(2,1)S(1)}, u32[]{:S(2)}, u32[]{:S(2)}) collective-permute-start(bf16[2,96,625]{2,1,0:T(8,128)(2,1)S(1)} %collective-permute-done.7.refs_0_), channel_id=1, source_target_pairs={{0,8},{1,17},{2,10},{3,19},{4,12},{5,21},{6,14},{7,23},{8,0},{9,25... | collective-permute-start | bytes 720008 | tf_op jit(solution)/shard_map/ppermute | solution.py:305
  36.5 2.3 %collective-permute-done.8.refs_3_ = bf16[2,96,625]{2,1,0:T(8,128)(2,1)S(1)} collective-permute-done((bf16[2,96,625]{2,1,0:T(8,128)(2,1)S(1)}, bf16[2,96,625]{2,1,0:T(8,128)(2,1)S(1)}, u32[]{:S(2)}, u32[]{:S(2)}) %collective-permute-start.8) | collective-permute-done | bytes 240032 | tf_op jit(solution)/shard_map/ppermute | solution.py:306
  38.8 2.6 %shard_map.83.refs_2_ = bf16[2,1600,384]{2,1,0:T(8,128)(2,1)S(1)} custom-call(s32[1]{0:T(128)} %bitcast.column_ref, bf16[2,96,625]{2,1,0:T(8,128)(2,1)S(1)} %collective-permute-done.2.refs_0_, bf16[2,96,625]{2,1,0:T(8,128)(2,1)S(1)} %collective-permute-done.5.refs_1_, bf16[2,96,625]{2,1,0:T(8,128)(2,1)S(1)} %collective-permute-done.6.refs_2_, ...), custom_call_target="tpu_custom_call" | custom-call | flops 1536000000 | bytes 3417600 | tf_op jit(solution)/shard_map/pallas_call | solution.py:77
  41.4 0.0 copy-start.6
  41.5 5.5 %collective-permute-done.11.refs_0_ = bf16[2,96,625]{2,1,0:T(8,128)(2,1)S(1)} collective-permute-done((bf16[2,96,625]{2,1,0:T(8,128)(2,1)S(1)}, bf16[2,96,625]{2,1,0:T(8,128)(2,1)S(1)}, u32[]{:S(2)}, u32[]{:S(2)}) %collective-permute-start.11) | collective-permute-done | bytes 240032 | tf_op jit(solution)/shard_map/ppermute | solution.py:295
  47.0 0.0 collective-permute-done.10.refs_2_
  47.0 0.0 collective-permute-done.9.refs_1_
  47.0 0.0 collective-permute-done.12.refs_1_
  47.0 0.1 collective-permute-start.17
  47.1 1.2 collective-permute-start.13
  48.3 0.1 copy-done.7
  48.5 0.0 collective-permute-start.16
  48.5 1.1 collective-permute-start.15
  49.6 0.9 collective-permute-start.14
  50.5 4.5 %collective-permute-done.13.refs_3_ = bf16[2,96,625]{2,1,0:T(8,128)(2,1)S(1)} collective-permute-done((bf16[2,96,625]{2,1,0:T(8,128)(2,1)S(1)}, bf16[2,96,625]{2,1,0:T(8,128)(2,1)S(1)}, u32[]{:S(2)}, u32[]{:S(2)}) %collective-permute-start.13) | collective-permute-done | bytes 240032 | tf_op jit(solution)/shard_map/ppermute | solution.py:306
  55.1 2.6 %shard_map.84.refs_6_ = bf16[2,1600,384]{2,1,0:T(8,128)(2,1)S(1)} custom-call(s32[1]{0:T(128)} %bitcast.column_ref, bf16[2,96,625]{2,1,0:T(8,128)(2,1)S(1)} %collective-permute-done.7.refs_0_, bf16[2,96,625]{2,1,0:T(8,128)(2,1)S(1)} %collective-permute-done.9.refs_1_, bf16[2,96,625]{2,1,0:T(8,128)(2,1)S(1)} %collective-permute-done.10.refs_2_, ...), custom_call_target="tpu_custom_call" | custom-call | flops 1536000000 | bytes 3417600 | tf_op jit(solution)/shard_map/pallas_call | solution.py:77
  57.7 0.0 copy-start.4
  57.7 0.9 collective-permute-done.15.refs_2_
  58.6 0.0 collective-permute-done.14.refs_1_
  58.6 1.2 collective-permute-done.16.refs_2_
  59.8 1.2 collective-permute-start.18
  61.1 5.0 %collective-permute-done.18.refs_3_ = bf16[2,96,625]{2,1,0:T(8,128)(2,1)S(1)} collective-permute-done((bf16[2,96,625]{2,1,0:T(8,128)(2,1)S(1)}, bf16[2,96,625]{2,1,0:T(8,128)(2,1)S(1)}, u32[]{:S(2)}, u32[]{:S(2)}) %collective-permute-start.18) | collective-permute-done | bytes 240032 | tf_op jit(solution)/shard_map/ppermute | solution.py:306
  66.1 3.4 %shard_map.85.refs_4_ = bf16[2,1600,384]{2,1,0:T(8,128)(2,1)} custom-call(s32[1]{0:T(128)} %bitcast.column_ref, bf16[2,96,625]{2,1,0:T(8,128)(2,1)S(1)} %collective-permute-done.11.refs_0_, bf16[2,96,625]{2,1,0:T(8,128)(2,1)S(1)} %collective-permute-done.14.refs_1_, bf16[2,96,625]{2,1,0:T(8,128)(2,1)S(1)} %collective-permute-done.15.refs_2_, ...), custom_call_target="tpu_custom_call" | custom-call | flops 1536000000 | bytes 3417600 | tf_op jit(solution)/shard_map/pallas_call | solution.py:77
  69.5 2.7 %collective-permute-done.19.refs_3_ = bf16[625,256]{1,0:T(8,128)(2,1)S(1)} collective-permute-done((bf16[625,256]{1,0:T(8,128)(2,1)S(1)}, bf16[625,256]{1,0:T(8,128)(2,1)S(1)}, u32[]{:S(2)}, u32[]{:S(2)}) %collective-permute-start.19) | collective-permute-done | bytes 320032 | tf_op jit(solution)/shard_map/ppermute | solution.py:295
  72.2 1.4 %shard_map.86.refs_8_ = bf16[8,800,128]{2,1,0:T(8,128)(2,1)S(1)} custom-call(bf16[800,625]{1,0:T(8,128)(2,1)S(1)} %copy-done.4, bf16[625,256]{1,0:T(8,128)(2,1)S(1)} %bitcast.25, bf16[625,256]{1,0:T(8,128)(2,1)S(1)} %collective-permute-done.3.refs_1_, bf16[625,256]{1,0:T(8,128)(2,1)S(1)} %collective-permute-done.16.refs_2_, ...), custom_call_target="tpu_custom_call" | custom-call | flops 1024000000 | bytes 2560000 | tf_op jit(solution)/shard_map/pallas_call | solution.py:108
  73.7 0.6 collective-permute-start.22
  74.3 0.1 copy.24.owners_ref
  74.4 0.1 copy.25.local_ref
  74.5 4.8 %collective-permute-done.22.refs_9_ = bf16[8,800,128]{2,1,0:T(8,128)(2,1)S(1)} collective-permute-done((bf16[8,800,128]{2,1,0:T(8,128)(2,1)S(1)}, bf16[8,800,128]{2,1,0:T(8,128)(2,1)S(1)}, u32[]{:S(2)}, u32[]{:S(2)}) %collective-permute-start.22) | collective-permute-done | bytes 1638432 | tf_op jit(solution)/shard_map/ppermute | solution.py:292
  79.3 1.3 copy-done.3
  80.5 10.4 %shard_map.88 = bf16[1,2,625,128]{3,2,1,0:T(8,128)(2,1)S(1)} custom-call(s32[1]{0:T(128)} %bitcast.column_ref, s32[32,3]{1,0:T(8,128)S(1)} %copy.24.owners_ref, s32[32,4]{1,0:T(8,128)S(1)} %copy.25.local_ref, bf16[2,1600,384]{2,1,0:T(8,128)(2,1)} %copy-done, bf16[2,1600,384]{2,1,0:T(8,128)(2,1)} %copy-done.7, bf16[2,1600,384]{2,1,0:T(8,128)(2,1)} %copy-done.1, ...), custom_call_target="tpu_custom_call" | custom-call | flops 2936012800 | bytes 6553600 | tf_op jit(solution)/shard_map/pallas_call | solution.py:257
  90.9 0.2 collective-permute-start.24
  91.1 10.4 %shard_map.87 = bf16[1,2,625,128]{3,2,1,0:T(8,128)(2,1)S(1)} custom-call(s32[1]{0:T(128)} %bitcast.column_ref, s32[32,3]{1,0:T(8,128)S(1)} %copy.24.owners_ref, s32[32,4]{1,0:T(8,128)S(1)} %copy.25.local_ref, bf16[2,1600,384]{2,1,0:T(8,128)(2,1)} %copy-done, bf16[2,1600,384]{2,1,0:T(8,128)(2,1)} %copy-done.7, bf16[2,1600,384]{2,1,0:T(8,128)(2,1)} %copy-done.1, ...), custom_call_target="tpu_custom_call" | custom-call | flops 2936012800 | bytes 6553600 | tf_op jit(solution)/shard_map/pallas_call | solution.py:257
  101.5 0.1 collective-permute-start.23
  101.6 10.4 %shard_map.89 = bf16[1,2,625,128]{3,2,1,0:T(8,128)(2,1)S(1)} custom-call(s32[1]{0:T(128)} %bitcast.column_ref, s32[32,3]{1,0:T(8,128)S(1)} %copy.24.owners_ref, s32[32,4]{1,0:T(8,128)S(1)} %copy.25.local_ref, bf16[2,1600,384]{2,1,0:T(8,128)(2,1)} %copy-done, bf16[2,1600,384]{2,1,0:T(8,128)(2,1)} %copy-done.7, bf16[2,1600,384]{2,1,0:T(8,128)(2,1)} %copy-done.1, ...), custom_call_target="tpu_custom_call" | custom-call | flops 2936012800 | bytes 6553600 | tf_op jit(solution)/shard_map/pallas_call | solution.py:257
  111.9 0.0 copy-start.9
  112.0 2.1 %collective-permute-start.25 = (bf16[2,625,128]{2,1,0:T(8,128)(2,1)S(1)}, bf16[2,625,128]{2,1,0:T(8,128)(2,1)S(1)}, u32[]{:S(2)}, u32[]{:S(2)}) collective-permute-start(bf16[2,625,128]{2,1,0:T(8,128)(2,1)S(1)} %bitcast.28), channel_id=1, source_target_pairs={{0,2},{1,3},{2,4},{3,5},{4,6},{5,7},{6,0},{7,1},{8,10},{9,11},{10,... | collective-permute-start | bytes 960008 | tf_op jit(solution)/shard_map/ppermute | solution.py:295
  114.0 10.3 %shard_map.90 = bf16[1,2,625,128]{3,2,1,0:T(8,128)(2,1)S(1)} custom-call(s32[1]{0:T(128)} %bitcast.column_ref, s32[32,3]{1,0:T(8,128)S(1)} %copy.24.owners_ref, s32[32,4]{1,0:T(8,128)S(1)} %copy.25.local_ref, bf16[2,1600,384]{2,1,0:T(8,128)(2,1)} %copy-done, bf16[2,1600,384]{2,1,0:T(8,128)(2,1)} %copy-done.7, bf16[2,1600,384]{2,1,0:T(8,128)(2,1)} %copy-done.1, ...), custom_call_target="tpu_custom_call" | custom-call | flops 2936012800 | bytes 6553600 | tf_op jit(solution)/shard_map/pallas_call | solution.py:257
  124.4 1.6 %collective-permute-done.23 = bf16[2,625,128]{2,1,0:T(8,128)(2,1)S(1)} collective-permute-done((bf16[2,625,128]{2,1,0:T(8,128)(2,1)S(1)}, bf16[2,625,128]{2,1,0:T(8,128)(2,1)S(1)}, u32[]{:S(2)}, u32[]{:S(2)}) %collective-permute-start.23) | collective-permute-done | bytes 320032 | tf_op jit(solution)/shard_map/ppermute | solution.py:295
  126.0 0.2 fusion.1
  126.2 1.2 copy.33
  (29 shorter events, 0.1 us)
Async XLA Ops:
  1.3 18.0 %collective-permute-start.3 = (bf16[625,256]{1,0:T(8,128)(2,1)S(1)}, bf16[625,256]{1,0:T(8,128)(2,1)S(1)}, u32[]{:S(2)}, u32[]{:S(2)}) collective-permute-start(bf16[625,256]{1,0:T(8,128)(2,1)S(1)} %bitcast.24), channel_id=1, source_target_pairs={{0,2},{1,3},{2,4},{3,5},{4,6},{5,7},{6,0},{7,1},{8,10},{9,11},{10,... | collective-permute-start | bytes 960008 | tf_op jit(solution)/shard_map/ppermute | solution.py:295
  7.8 11.4 %collective-permute-start.2 = (bf16[2,96,625]{2,1,0:T(8,128)(2,1)S(1)}, bf16[2,96,625]{2,1,0:T(8,128)(2,1)S(1)}, u32[]{:S(2)}, u32[]{:S(2)}) collective-permute-start(bf16[2,96,625]{2,1,0:T(8,128)(2,1)S(1)} %get-tuple-element.63), channel_id=1, source_target_pairs={{0,2},{1,3},{2,4},{3,5},{4,6},{5,7},{6,0},{7,1},{8,10},{9,11},{10,... | collective-permute-start | bytes 720008 | tf_op jit(solution)/shard_map/ppermute | solution.py:295
  9.5 9.8 %collective-permute-start.1 = (bf16[2,96,625]{2,1,0:T(8,128)(2,1)S(1)}, bf16[2,96,625]{2,1,0:T(8,128)(2,1)S(1)}, u32[]{:S(2)}, u32[]{:S(2)}) collective-permute-start(bf16[2,96,625]{2,1,0:T(8,128)(2,1)S(1)} %get-tuple-element.33.refs_0_), channel_id=1, source_target_pairs={{0,16},{1,9},{2,18},{3,11},{4,20},{5,13},{6,22},{7,15},{8,24},{9,1... | collective-permute-start | bytes 720008 | tf_op jit(solution)/shard_map/ppermute | solution.py:306
  11.0 8.3 %collective-permute-start = (bf16[2,96,625]{2,1,0:T(8,128)(2,1)S(1)}, bf16[2,96,625]{2,1,0:T(8,128)(2,1)S(1)}, u32[]{:S(2)}, u32[]{:S(2)}) collective-permute-start(bf16[2,96,625]{2,1,0:T(8,128)(2,1)S(1)} %get-tuple-element.33.refs_0_), channel_id=1, source_target_pairs={{0,8},{1,17},{2,10},{3,19},{4,12},{5,21},{6,14},{7,23},{8,0},{9,25... | collective-permute-start | bytes 720008 | tf_op jit(solution)/shard_map/ppermute | solution.py:305
  19.3 8.0 %collective-permute-start.4 = (bf16[2,96,625]{2,1,0:T(8,128)(2,1)S(1)}, bf16[2,96,625]{2,1,0:T(8,128)(2,1)S(1)}, u32[]{:S(2)}, u32[]{:S(2)}) collective-permute-start(bf16[2,96,625]{2,1,0:T(8,128)(2,1)S(1)} %collective-permute-done.refs_1_), channel_id=1, source_target_pairs={{0,16},{1,9},{2,18},{3,11},{4,20},{5,13},{6,22},{7,15},{8,24},{9,1... | collective-permute-start | bytes 720008 | tf_op jit(solution)/shard_map/ppermute | solution.py:306
  20.9 10.6 %collective-permute-start.7 = (bf16[2,96,625]{2,1,0:T(8,128)(2,1)S(1)}, bf16[2,96,625]{2,1,0:T(8,128)(2,1)S(1)}, u32[]{:S(2)}, u32[]{:S(2)}) collective-permute-start(bf16[2,96,625]{2,1,0:T(8,128)(2,1)S(1)} %get-tuple-element.37), channel_id=1, source_target_pairs={{0,6},{1,7},{2,0},{3,1},{4,2},{5,3},{6,4},{7,5},{8,14},{9,15},{10,... | collective-permute-start | bytes 720008 | tf_op jit(solution)/shard_map/ppermute | solution.py:295
  22.6 8.9 %collective-permute-start.6 = (bf16[2,96,625]{2,1,0:T(8,128)(2,1)S(1)}, bf16[2,96,625]{2,1,0:T(8,128)(2,1)S(1)}, u32[]{:S(2)}, u32[]{:S(2)}) collective-permute-start(bf16[2,96,625]{2,1,0:T(8,128)(2,1)S(1)} %collective-permute-done.2.refs_0_), channel_id=1, source_target_pairs={{0,16},{1,9},{2,18},{3,11},{4,20},{5,13},{6,22},{7,15},{8,24},{9,1... | collective-permute-start | bytes 720008 | tf_op jit(solution)/shard_map/ppermute | solution.py:306
  23.1 8.4 %collective-permute-start.5 = (bf16[2,96,625]{2,1,0:T(8,128)(2,1)S(1)}, bf16[2,96,625]{2,1,0:T(8,128)(2,1)S(1)}, u32[]{:S(2)}, u32[]{:S(2)}) collective-permute-start(bf16[2,96,625]{2,1,0:T(8,128)(2,1)S(1)} %collective-permute-done.2.refs_0_), channel_id=1, source_target_pairs={{0,8},{1,17},{2,10},{3,19},{4,12},{5,21},{6,14},{7,23},{8,0},{9,25... | collective-permute-start | bytes 720008 | tf_op jit(solution)/shard_map/ppermute | solution.py:305
  27.3 1.6 %copy-start.5 = (bf16[1600,625]{1,0:T(8,128)(2,1)S(1)}, bf16[1600,625]{1,0:T(8,128)(2,1)}, u32[]{:S(2)}) copy-start(bf16[1600,625]{1,0:T(8,128)(2,1)} %constant.61.clone.refs_4_) | copy-start | bytes 6000004
  31.5 9.9 %copy-start = (bf16[2,1600,384]{2,1,0:T(8,128)(2,1)}, bf16[2,1600,384]{2,1,0:T(8,128)(2,1)S(1)}, u32[]{:S(2)}) copy-start(bf16[2,1600,384]{2,1,0:T(8,128)(2,1)S(1)} %shard_map.82.refs_0_) | copy-start | bytes 7372804
  31.5 15.5 %collective-permute-start.12 = (bf16[2,1600,384]{2,1,0:T(8,128)(2,1)S(1)}, bf16[2,1600,384]{2,1,0:T(8,128)(2,1)S(1)}, u32[]{:S(2)}, u32[]{:S(2)}) collective-permute-start(bf16[2,1600,384]{2,1,0:T(8,128)(2,1)S(1)} %shard_map.82.refs_0_), channel_id=1, source_target_pairs={{0,1},{1,0},{2,3},{3,2},{4,5},{5,4},{6,7},{7,6},{8,9},{9,8},{10,11... | collective-permute-start | bytes 7372808 | tf_op jit(solution)/shard_map/ppermute | solution.py:292
  31.6 7.2 %collective-permute-start.8 = (bf16[2,96,625]{2,1,0:T(8,128)(2,1)S(1)}, bf16[2,96,625]{2,1,0:T(8,128)(2,1)S(1)}, u32[]{:S(2)}, u32[]{:S(2)}) collective-permute-start(bf16[2,96,625]{2,1,0:T(8,128)(2,1)S(1)} %collective-permute-done.5.refs_1_), channel_id=1, source_target_pairs={{0,16},{1,9},{2,18},{3,11},{4,20},{5,13},{6,22},{7,15},{8,24},{9,1... | collective-permute-start | bytes 720008 | tf_op jit(solution)/shard_map/ppermute | solution.py:306
  33.2 13.8 %collective-permute-start.11 = (bf16[2,96,625]{2,1,0:T(8,128)(2,1)S(1)}, bf16[2,96,625]{2,1,0:T(8,128)(2,1)S(1)}, u32[]{:S(2)}, u32[]{:S(2)}) collective-permute-start(bf16[2,96,625]{2,1,0:T(8,128)(2,1)S(1)} %get-tuple-element.43), channel_id=1, source_target_pairs={{0,4},{1,5},{2,6},{3,7},{4,0},{5,1},{6,2},{7,3},{8,12},{9,13},{10,... | collective-permute-start | bytes 720008 | tf_op jit(solution)/shard_map/ppermute | solution.py:295
  34.2 12.8 %collective-permute-start.10 = (bf16[2,96,625]{2,1,0:T(8,128)(2,1)S(1)}, bf16[2,96,625]{2,1,0:T(8,128)(2,1)S(1)}, u32[]{:S(2)}, u32[]{:S(2)}) collective-permute-start(bf16[2,96,625]{2,1,0:T(8,128)(2,1)S(1)} %collective-permute-done.7.refs_0_), channel_id=1, source_target_pairs={{0,16},{1,9},{2,18},{3,11},{4,20},{5,13},{6,22},{7,15},{8,24},{9,1... | collective-permute-start | bytes 720008 | tf_op jit(solution)/shard_map/ppermute | solution.py:306
  34.7 12.3 %collective-permute-start.9 = (bf16[2,96,625]{2,1,0:T(8,128)(2,1)S(1)}, bf16[2,96,625]{2,1,0:T(8,128)(2,1)S(1)}, u32[]{:S(2)}, u32[]{:S(2)}) collective-permute-start(bf16[2,96,625]{2,1,0:T(8,128)(2,1)S(1)} %collective-permute-done.7.refs_0_), channel_id=1, source_target_pairs={{0,8},{1,17},{2,10},{3,19},{4,12},{5,21},{6,14},{7,23},{8,0},{9,25... | collective-permute-start | bytes 720008 | tf_op jit(solution)/shard_map/ppermute | solution.py:305
  41.4 16.3 %copy-start.1 = (bf16[2,1600,384]{2,1,0:T(8,128)(2,1)}, bf16[2,1600,384]{2,1,0:T(8,128)(2,1)S(1)}, u32[]{:S(2)}) copy-start(bf16[2,1600,384]{2,1,0:T(8,128)(2,1)S(1)} %shard_map.83.refs_2_) | copy-start | bytes 7372804
  41.4 24.6 %copy-start.6 = (bf16[1600,625]{1,0:T(8,128)(2,1)S(1)}, bf16[1600,625]{1,0:T(8,128)(2,1)}, u32[]{:S(2)}) copy-start(bf16[1600,625]{1,0:T(8,128)(2,1)} %constant.61.clone.refs_4_) | copy-start | bytes 6000004
  47.0 1.5 %copy-start.7 = (bf16[2,1600,384]{2,1,0:T(8,128)(2,1)}, bf16[2,1600,384]{2,1,0:T(8,128)(2,1)S(1)}, u32[]{:S(2)}) copy-start(bf16[2,1600,384]{2,1,0:T(8,128)(2,1)S(1)} %collective-permute-done.12.refs_1_) | copy-start | bytes 7372804
  47.0 12.8 %collective-permute-start.17 = (bf16[2,1600,384]{2,1,0:T(8,128)(2,1)S(1)}, bf16[2,1600,384]{2,1,0:T(8,128)(2,1)}, u32[]{:S(2)}, u32[]{:S(2)}) collective-permute-start(bf16[2,1600,384]{2,1,0:T(8,128)(2,1)S(1)} %shard_map.83.refs_2_), channel_id=1, source_target_pairs={{0,1},{1,0},{2,3},{3,2},{4,5},{5,4},{6,7},{7,6},{8,9},{9,8},{10,11... | collective-permute-start | bytes 7372808 | tf_op jit(solution)/shard_map/ppermute | solution.py:292
  47.1 7.9 %collective-permute-start.13 = (bf16[2,96,625]{2,1,0:T(8,128)(2,1)S(1)}, bf16[2,96,625]{2,1,0:T(8,128)(2,1)S(1)}, u32[]{:S(2)}, u32[]{:S(2)}) collective-permute-start(bf16[2,96,625]{2,1,0:T(8,128)(2,1)S(1)} %collective-permute-done.9.refs_1_), channel_id=1, source_target_pairs={{0,16},{1,9},{2,18},{3,11},{4,20},{5,13},{6,22},{7,15},{8,24},{9,1... | collective-permute-start | bytes 720008 | tf_op jit(solution)/shard_map/ppermute | solution.py:306
  48.5 11.4 %collective-permute-start.16 = (bf16[625,256]{1,0:T(8,128)(2,1)S(1)}, bf16[625,256]{1,0:T(8,128)(2,1)S(1)}, u32[]{:S(2)}, u32[]{:S(2)}) collective-permute-start(bf16[625,256]{1,0:T(8,128)(2,1)S(1)} %collective-permute-done.3.refs_1_), channel_id=1, source_target_pairs={{0,2},{1,3},{2,4},{3,5},{4,6},{5,7},{6,0},{7,1},{8,10},{9,11},{10,... | collective-permute-start | bytes 960008 | tf_op jit(solution)/shard_map/ppermute | solution.py:295
  48.5 10.1 %collective-permute-start.15 = (bf16[2,96,625]{2,1,0:T(8,128)(2,1)S(1)}, bf16[2,96,625]{2,1,0:T(8,128)(2,1)S(1)}, u32[]{:S(2)}, u32[]{:S(2)}) collective-permute-start(bf16[2,96,625]{2,1,0:T(8,128)(2,1)S(1)} %collective-permute-done.11.refs_0_), channel_id=1, source_target_pairs={{0,16},{1,9},{2,18},{3,11},{4,20},{5,13},{6,22},{7,15},{8,24},{9,1... | collective-permute-start | bytes 720008 | tf_op jit(solution)/shard_map/ppermute | solution.py:306
  49.6 9.0 %collective-permute-start.14 = (bf16[2,96,625]{2,1,0:T(8,128)(2,1)S(1)}, bf16[2,96,625]{2,1,0:T(8,128)(2,1)S(1)}, u32[]{:S(2)}, u32[]{:S(2)}) collective-permute-start(bf16[2,96,625]{2,1,0:T(8,128)(2,1)S(1)} %collective-permute-done.11.refs_0_), channel_id=1, source_target_pairs={{0,8},{1,17},{2,10},{3,19},{4,12},{5,21},{6,14},{7,23},{8,0},{9,25... | collective-permute-start | bytes 720008 | tf_op jit(solution)/shard_map/ppermute | solution.py:305
  57.7 11.8 %copy-start.2 = (bf16[2,1600,384]{2,1,0:T(8,128)(2,1)}, bf16[2,1600,384]{2,1,0:T(8,128)(2,1)S(1)}, u32[]{:S(2)}) copy-start(bf16[2,1600,384]{2,1,0:T(8,128)(2,1)S(1)} %shard_map.84.refs_6_) | copy-start | bytes 7372804
  57.7 14.5 %copy-start.4 = (bf16[800,625]{1,0:T(8,128)(2,1)S(1)}, bf16[800,625]{1,0:T(8,128)(2,1)}, u32[]{:S(2)}) copy-start(bf16[800,625]{1,0:T(8,128)(2,1)} %constant.63.clone.matrix_ref) | copy-start | bytes 3000004
  59.8 12.4 %collective-permute-start.20 = (bf16[2,1600,384]{2,1,0:T(8,128)(2,1)S(1)}, bf16[2,1600,384]{2,1,0:T(8,128)(2,1)S(1)}, u32[]{:S(2)}, u32[]{:S(2)}) collective-permute-start(bf16[2,1600,384]{2,1,0:T(8,128)(2,1)S(1)} %shard_map.84.refs_6_), channel_id=1, source_target_pairs={{0,1},{1,0},{2,3},{3,2},{4,5},{5,4},{6,7},{7,6},{8,9},{9,8},{10,11... | collective-permute-start | bytes 7372808 | tf_op jit(solution)/shard_map/ppermute | solution.py:292
  59.8 6.2 %collective-permute-start.18 = (bf16[2,96,625]{2,1,0:T(8,128)(2,1)S(1)}, bf16[2,96,625]{2,1,0:T(8,128)(2,1)S(1)}, u32[]{:S(2)}, u32[]{:S(2)}) collective-permute-start(bf16[2,96,625]{2,1,0:T(8,128)(2,1)S(1)} %collective-permute-done.14.refs_1_), channel_id=1, source_target_pairs={{0,16},{1,9},{2,18},{3,11},{4,20},{5,13},{6,22},{7,15},{8,24},{9,1... | collective-permute-start | bytes 720008 | tf_op jit(solution)/shard_map/ppermute | solution.py:306
  61.1 11.1 %collective-permute-start.19 = (bf16[625,256]{1,0:T(8,128)(2,1)S(1)}, bf16[625,256]{1,0:T(8,128)(2,1)S(1)}, u32[]{:S(2)}, u32[]{:S(2)}) collective-permute-start(bf16[625,256]{1,0:T(8,128)(2,1)S(1)} %collective-permute-done.16.refs_2_), channel_id=1, source_target_pairs={{0,2},{1,3},{2,4},{3,5},{4,6},{5,7},{6,0},{7,1},{8,10},{9,11},{10,... | collective-permute-start | bytes 960008 | tf_op jit(solution)/shard_map/ppermute | solution.py:295
  69.5 4.8 %copy-start.10 = (s32[32,3]{0,1:T(4,128)S(1)}, s32[32,3]{0,1:T(4,128)}, u32[]{:S(2)}) copy-start(s32[32,3]{0,1:T(4,128)} %param.11) | copy-start | bytes 1156
  69.5 4.9 %copy-start.11 = (s32[32,4]{0,1:T(4,128)S(1)}, s32[32,4]{0,1:T(4,128)}, u32[]{:S(2)}) copy-start(s32[32,4]{0,1:T(4,128)} %param.12) | copy-start | bytes 1540
  72.2 1.5 %copy-start.8 = (bf16[2,1600,384]{2,1,0:T(8,128)(2,1)}, bf16[2,1600,384]{2,1,0:T(8,128)(2,1)S(1)}, u32[]{:S(2)}) copy-start(bf16[2,1600,384]{2,1,0:T(8,128)(2,1)S(1)} %collective-permute-done.20.refs_7_) | copy-start | bytes 7372804
  72.2 7.0 %collective-permute-start.21 = (bf16[2,1600,384]{2,1,0:T(8,128)(2,1)}, bf16[2,1600,384]{2,1,0:T(8,128)(2,1)}, u32[]{:S(2)}, u32[]{:S(2)}) collective-permute-start(bf16[2,1600,384]{2,1,0:T(8,128)(2,1)} %shard_map.85.refs_4_), channel_id=1, source_target_pairs={{0,1},{1,0},{2,3},{3,2},{4,5},{5,4},{6,7},{7,6},{8,9},{9,8},{10,11... | collective-permute-start | bytes 7372808 | tf_op jit(solution)/shard_map/ppermute | solution.py:292
  73.7 5.5 %collective-permute-start.22 = (bf16[8,800,128]{2,1,0:T(8,128)(2,1)S(1)}, bf16[8,800,128]{2,1,0:T(8,128)(2,1)S(1)}, u32[]{:S(2)}, u32[]{:S(2)}) collective-permute-start(bf16[8,800,128]{2,1,0:T(8,128)(2,1)S(1)} %shard_map.86.refs_8_), channel_id=1, source_target_pairs={{0,1},{1,0},{2,3},{3,2},{4,5},{5,4},{6,7},{7,6},{8,9},{9,8},{10,11... | collective-permute-start | bytes 4915208 | tf_op jit(solution)/shard_map/ppermute | solution.py:292
  79.3 1.3 copy-start.3
  90.9 33.5 %collective-permute-start.24 = (bf16[2,625,128]{2,1,0:T(8,128)(2,1)S(1)}, bf16[2,625,128]{2,1,0:T(8,128)(2,1)S(1)}, u32[]{:S(2)}, u32[]{:S(2)}) collective-permute-start(bf16[2,625,128]{2,1,0:T(8,128)(2,1)S(1)} %bitcast.26), channel_id=1, source_target_pairs={{0,6},{1,7},{2,0},{3,1},{4,2},{5,3},{6,4},{7,5},{8,14},{9,15},{10,... | collective-permute-start | bytes 960008 | tf_op jit(solution)/shard_map/ppermute | solution.py:295
  101.5 24.5 %collective-permute-start.23 = (bf16[2,625,128]{2,1,0:T(8,128)(2,1)S(1)}, bf16[2,625,128]{2,1,0:T(8,128)(2,1)S(1)}, u32[]{:S(2)}, u32[]{:S(2)}) collective-permute-start(bf16[2,625,128]{2,1,0:T(8,128)(2,1)S(1)} %bitcast.27), channel_id=1, source_target_pairs={{0,4},{1,5},{2,6},{3,7},{4,0},{5,1},{6,2},{7,3},{8,12},{9,13},{10,... | collective-permute-start | bytes 960008 | tf_op jit(solution)/shard_map/ppermute | solution.py:295
  111.9 14.0 %copy-start.9 = (f32[2,128,625]{1,0,2:T(2,128)S(1)}, f32[2,128,625]{1,0,2:T(2,128)}, u32[]{:S(2)}) copy-start(f32[2,128,625]{1,0,2:T(2,128)} %param.10) | copy-start | bytes 1920004
  112.0 14.0 %collective-permute-start.25 = (bf16[2,625,128]{2,1,0:T(8,128)(2,1)S(1)}, bf16[2,625,128]{2,1,0:T(8,128)(2,1)S(1)}, u32[]{:S(2)}, u32[]{:S(2)}) collective-permute-start(bf16[2,625,128]{2,1,0:T(8,128)(2,1)S(1)} %bitcast.28), channel_id=1, source_target_pairs={{0,2},{1,3},{2,4},{3,5},{4,6},{5,7},{6,0},{7,1},{8,10},{9,11},{10,... | collective-permute-start | bytes 960008 | tf_op jit(solution)/shard_map/ppermute | solution.py:295

commit v12 on v10

--- a/solution.py
+++ b/solution.py
@@ -22,6 +22,7 @@
 BF = jnp.bfloat16
 F32 = jnp.float32
 VMEM_BYTES = 48 * 1024 * 1024
+LADDER_VMEM_BYTES = 60 * 1024 * 1024
 
 
 def spread(spots, rows):
@@ -36,11 +37,6 @@
 def amp_matrix():
     c, d = np.divmod(np.arange(TV * TV), TV)
     return spread(d * PAD + c, ROWS)
-
-
-def back_matrix():
-    a, b = np.divmod(np.arange(TV * TV), TV)
-    return spread(PLACE[a] * PAD + b, ROWS).T
 
 
 def prepare_kernel(column_ref, *refs):
@@ -122,12 +118,12 @@
 
 def ladder_kernel(find, made, sources, column_ref, owners_ref, local_ref, *refs):
     factor_refs, amp_refs, refs = refs[:sources], refs[sources : sources + 2], refs[sources + 2 :]
-    back_ref, matrix_ref, refs = refs[0], None if made else refs[1], refs[1 if made else 2 :]
+    matrix_ref, refs = None if made else refs[0], refs[0 if made else 1 :]
     out_ref, v_ref, u_ref, acc_ref, c_buf, r_buf, amp_buf, sems = refs[:8]
     column, columns = pl.program_id(0), pl.num_programs(0)
     step, steps = pl.program_id(1), pl.num_programs(1)
     at = column * steps + step
-    slot = lax.rem(at, 2)
+    slot = at & 1
 
     def fetch(choices, source, index, part, buffer, to, sem):
         for n, ref in enumerate(choices):
@@ -204,14 +200,12 @@
 
     @pl.when(step == steps - 1)
     def _():
-        blocks_here, pairs = out_ref.shape[1], out_ref.shape[3]
-        sums = jnp.concatenate([acc_ref[m].astype(BF) for m in range(blocks_here)], axis=1)
-        sums = jnp.dot(back_ref[...], sums, preferred_element_type=F32).astype(BF)
-        for m in range(blocks_here):
-            out_ref[0, m] = sums[:, m * pairs : (m + 1) * pairs]
-
-
-def ladders(first, columns, levels, blocks_here, column, task_owners, task_local, tiles, amps, back, matrix):
+        for m in range(out_ref.shape[1]):
+            rows = [acc_ref[m, PLACE[a] * PAD : PLACE[a] * PAD + TV, :] for a in range(TV)]
+            out_ref[0, m] = jnp.concatenate(rows, axis=0).astype(BF)
+
+
+def ladders(first, columns, levels, blocks_here, column, task_owners, task_local, tiles, amps, matrix):
     tasks = task_owners.shape[0] // (2 * levels)
     pairs = amps[0].shape[2]
     made = tiles[0].shape[1] == 2 * ROWS
@@ -219,13 +213,15 @@
     held = (ROWS, depth) if made else tiles[0].shape[1:]
 
     def find(i, j, column_ref, owners_ref, local_ref):
-        level, core = column_ref[0] // 2, lax.rem(column_ref[0], 2)
-        task = (2 * lax.rem(level + first + i, levels) + core) * tasks + j
+        level, core = column_ref[0] >> 1, column_ref[0] & 1
+        above = level + first + i
+        task = (2 * jnp.where(above >= levels, above - levels, above) + core) * tasks + j
 
         def place(kind):
             owner = owners_ref[task, kind]
-            below = lax.rem(level - owner // 2 + levels, levels)
-            far = jnp.where(lax.rem(owner, 2) != core, 1, 0)
+            below = level - (owner >> 1)
+            below = jnp.where(below < 0, below + levels, below)
+            far = (owner & 1) ^ core
             return below, far, local_ref[task, kind]
 
         def factor(kind):
@@ -238,9 +234,8 @@
         return {"task": task, "row": factor(0), "col": factor(1), "amp": (far, below * blocks_here + m)}
 
     anywhere = pl.BlockSpec(memory_space=pl.ANY)
-    fixed = lambda shape: pl.BlockSpec(shape, lambda i, j, *tables: (0,) * len(shape))
-    operands = [*tiles, *amps, back]
-    in_specs = [anywhere] * (len(tiles) + 2) + [fixed(back.shape)]
+    operands = [*tiles, *amps]
+    in_specs = [anywhere] * (len(tiles) + 2)
     scratch = [
         pltpu.VMEM((ROWS, WIDE), F32),
         pltpu.VMEM((ROWS, WIDE), BF),
@@ -251,7 +246,7 @@
         pltpu.SemaphoreType.DMA((2, 3)),
     ]
     if not made:
-        in_specs.append(fixed(matrix.shape))
+        in_specs.append(pl.BlockSpec(matrix.shape, lambda i, j, *tables: (0, 0)))
         scratch.append(pltpu.VMEM((2, ROWS, depth), BF))
         operands.append(matrix)
     return pl.pallas_call(
@@ -264,7 +259,7 @@
             out_specs=pl.BlockSpec((1, blocks_here, TV * TV, pairs), lambda i, j, *tables: (i, 0, 0, 0)),
             scratch_shapes=scratch,
         ),
-        compiler_params=pltpu.CompilerParams(vmem_limit_bytes=VMEM_BYTES),
+        compiler_params=pltpu.CompilerParams(vmem_limit_bytes=LADDER_VMEM_BYTES),
         cost_estimate=pl.CostEstimate(
             flops=2 * columns * tasks * ROWS * WIDE * (depth + pairs),
             bytes_accessed=2 * columns * tasks * ROWS * 2 * (depth + pairs),
@@ -288,7 +283,6 @@
     depth = depth_here // levels
     total = 2 * levels * blocks_here
     matrix = jnp.asarray(forms_matrix())
-    back = jnp.asarray(back_matrix())
     other_core = lambda x: lax.ppermute(x, "task", [(c, c ^ 1) for c in range(task_count)])
 
     def around(x, by):
@@ -308,27 +302,26 @@
         own = amplitudes.transpose(2, 0, 1).reshape(TV * TV, blocks_here * pairs)
         amp1 = around(own, 1)
         part0 = mine[0]
-        a0, b0, part1, part3 = first_side(part0), second_side(part0), around(mine[1], 1), around(mine[3], 3)
-
-        a0, b0, part0, part1, part3, amp1, to2 = after((a0, b0, part0, part1, part3, amp1, mine[2]), ())
-        q0, a1, b1, part2 = second_side(a0), first_side(part1), second_side(part1), around(to2, 2)
+        a0, b0, part1 = first_side(part0), second_side(part0), around(mine[1], 1)
+
+        a0, b0, part0, part1, amp1, to3 = after((a0, b0, part0, part1, amp1, mine[3]), ())
+        q0, a1, b1, part3, amp2 = second_side(a0), first_side(part1), second_side(part1), around(to3, 3), around(amp1, 1)
         forms0 = made_forms(part0, a0, b0, q0)
 
-        forms0, part1, a1, b1, part2, part3, amp1 = after((forms0, part1, a1, b1, part2, part3, amp1), ())
-        q1, a3, b3, amp2 = second_side(a1), first_side(part3), second_side(part3), around(amp1, 1)
+        forms0, part1, a1, b1, part3, to2, amp2 = after((forms0, part1, a1, b1, part3, mine[2], amp2), ())
+        q1, a3, b3, part2 = second_side(a1), first_side(part3), second_side(part3), around(to2, 2)
         far0 = other_core(forms0)
         forms1 = made_forms(part1, a1, b1, q1)
 
-        forms1, part3, a3, b3, part2, amp2, far0 = after((forms1, part3, a3, b3, part2, amp2, far0), ())
+        forms1, part3, a3, b3, part2, far0, amp2 = after((forms1, part3, a3, b3, part2, far0, amp2), ())
         q3, a2, b2, amp3 = second_side(a3), first_side(part2), second_side(part2), around(amp2, 1)
         far1 = other_core(forms1)
         forms3 = made_forms(part3, a3, b3, q3)
 
         forms3, part2, a2, b2, amp3, far1 = after((forms3, part2, a2, b2, amp3, far1), ())
-        q2 = second_side(a2)
-        far3 = other_core(forms3)
+        q2, far3 = second_side(a2), other_core(forms3)
         amps = prepare_amps([own, amp1, amp2, amp3], blocks_here, jnp.asarray(amp_matrix()))
-        forms2 = made_forms(part2, a2, b2, after(q2, amps))
+        forms2 = made_forms(part2, a2, b2, q2)
         far2 = other_core(after(forms2, far3))
         held = [forms0, far0, forms1, far1, forms2, far2, forms3, far3]
     else:
@@ -347,9 +340,7 @@
     order = [2, 3, 1, 0] if calls == 4 else list(reversed(range(calls)))
     for call in order:
         first = call * width
-        sums = ladders(
-            first, width, levels, blocks_here, column[None], task_owners, task_local, held, amps, back, matrix
-        )
+        sums = ladders(first, width, levels, blocks_here, column[None], task_owners, task_local, held, amps, matrix)
         for i in range(width):
             term = (around(sums[i], first + i) if first + i else sums[i]).astype(F32)
             ladder = term if ladder is None else ladder + term

time: 129 us -> 130 us (level)
  starting transfers between devices: 22.8 us -> 29.1 us
  waiting for transfers between devices: 41.1 us -> 34.9 us
    ppermute x8, waiting for transfers between devices: 19.2 us -> 10.5 us  [per_device(): second_side = lambda x: lax.ppermute(x, ('pair', 'task'), sides[1])]
    ppermute x9, starting transfers between devices: 8.36 us -> 13.3 us  [around(): lax.ppermute(x, 'task', [(c, (c + 2 * by) % task_count) for c in range(ta...]
    ppermute x9, waiting for transfers between devices: 16.4 us -> 20.8 us  [around(): lax.ppermute(x, 'task', [(c, (c + 2 * by) % task_count) for c in range(ta...]
    ppermute x5, waiting for transfers between devices: 5.48 us -> 3.61 us  [per_device(): lax.ppermute(x, 'task', [(c, c ^ 1) for c in range(task_count)])]
    unnamed x29 -> x31, local copies, waits for them, and re-layouts: 9.01 us -> 8.82 us
  transfers between devices with their start and end apart: 26 -> 26, of which waited for: 13 -> 10; matrix products, arithmetic and copies ran while one was open for 3% -> 4% of each run, Pallas kernels for 34% -> 34%
where the time goes in v12:
time: 130 us; the launch traced here: 129 us
  Pallas kernels  53.3 us (41%)
  waiting for transfers between devices  34.9 us (27%)
  starting transfers between devices  29.1 us (22%)
  local copies, waits for them, and re-layouts  10.1 us (8%)
    pallas_call x4, Pallas kernels, ladders(): pl.pallas_call(functools.partial(ladder_kernel, find, made, len(tiles)),...  40.5 us
    ppermute x9, waiting for transfers between devices, around(): lax.ppermute(x, 'task', [(c, (c + 2 * by) % task_count) for c in range(ta...  20.8 us
    ppermute x9, starting transfers between devices, around(): lax.ppermute(x, 'task', [(c, (c + 2 * by) % task_count) for c in range(ta...  13.3 us
    pallas_call x4, Pallas kernels, prepare(): pl.pallas_call(prepare_kernel, out_shape=jax.ShapeDtypeStruct((count, mat...  11.3 us
    ppermute x8, waiting for transfers between devices, per_device(): second_side = lambda x: lax.ppermute(x, ('pair', 'task'), sides[1])  10.5 us
    ppermute x8, starting transfers between devices, per_device(): second_side = lambda x: lax.ppermute(x, ('pair', 'task'), sides[1])  10.1 us
    unnamed x31, local copies, waits for them, and re-layouts  8.82 us
    ppermute x4, starting transfers between devices, per_device(): first_side = lambda x: lax.ppermute(x, ('pair', 'task'), sides[0])  4.88 us
  transfers between devices with their start and end apart: 26, of which 10 were waited for; matrix products, arithmetic and copies ran while one was open for 4% of the time, Pallas kernels for 34%

profile of v12, /device:TPU:0, one launch (start us, length us, event | category | flops | bytes accessed | tf_op | source)
XLA Modules:
  0.0 128.9 jit_solution(11905303381318215735)
XLA Ops:
  0.0 1.2 pad
  1.3 3.1 %collective-permute-start.3 = (bf16[625,256]{1,0:T(8,128)(2,1)S(1)}, bf16[625,256]{1,0:T(8,128)(2,1)S(1)}, u32[]{:S(2)}, u32[]{:S(2)}) collective-permute-start(bf16[625,256]{1,0:T(8,128)(2,1)S(1)} %bitcast.24), channel_id=1, source_target_pairs={{0,2},{1,3},{2,4},{3,5},{4,6},{5,7},{6,0},{7,1},{8,10},{9,11},{10,... | collective-permute-start | bytes 960008 | tf_op jit(solution)/shard_map/ppermute | solution.py:289
  4.4 3.3 %copy.22 = bf16[2,384,625]{2,1,0:T(8,128)(2,1)S(1)} copy(bf16[2,384,625]{1,0,2:T(2,128)(2,1)} %param.7) | data formatting | bytes 1920000 | tf_op args[0]
  7.7 0.1 dynamic-slice_bitcast_fusion
  7.8 1.6 %collective-permute-start.2 = (bf16[2,96,625]{2,1,0:T(8,128)(2,1)S(1)}, bf16[2,96,625]{2,1,0:T(8,128)(2,1)S(1)}, u32[]{:S(2)}, u32[]{:S(2)}) collective-permute-start(bf16[2,96,625]{2,1,0:T(8,128)(2,1)S(1)} %get-tuple-element.61), channel_id=1, source_target_pairs={{0,2},{1,3},{2,4},{3,5},{4,6},{5,7},{6,0},{7,1},{8,10},{9,11},{10,... | collective-permute-start | bytes 720008 | tf_op jit(solution)/shard_map/ppermute | solution.py:289
  9.5 1.5 %collective-permute-start.1 = (bf16[2,96,625]{2,1,0:T(8,128)(2,1)S(1)}, bf16[2,96,625]{2,1,0:T(8,128)(2,1)S(1)}, u32[]{:S(2)}, u32[]{:S(2)}) collective-permute-start(bf16[2,96,625]{2,1,0:T(8,128)(2,1)S(1)} %get-tuple-element.32.refs_0_), channel_id=1, source_target_pairs={{0,16},{1,9},{2,18},{3,11},{4,20},{5,13},{6,22},{7,15},{8,24},{9,1... | collective-permute-start | bytes 720008 | tf_op jit(solution)/shard_map/ppermute | solution.py:300
  11.0 1.5 %collective-permute-start = (bf16[2,96,625]{2,1,0:T(8,128)(2,1)S(1)}, bf16[2,96,625]{2,1,0:T(8,128)(2,1)S(1)}, u32[]{:S(2)}, u32[]{:S(2)}) collective-permute-start(bf16[2,96,625]{2,1,0:T(8,128)(2,1)S(1)} %get-tuple-element.32.refs_0_), channel_id=1, source_target_pairs={{0,8},{1,17},{2,10},{3,19},{4,12},{5,21},{6,14},{7,23},{8,0},{9,25... | collective-permute-start | bytes 720008 | tf_op jit(solution)/shard_map/ppermute | solution.py:299
  12.5 6.8 %collective-permute-done.2.refs_0_ = bf16[2,96,625]{2,1,0:T(8,128)(2,1)S(1)} collective-permute-done((bf16[2,96,625]{2,1,0:T(8,128)(2,1)S(1)}, bf16[2,96,625]{2,1,0:T(8,128)(2,1)S(1)}, u32[]{:S(2)}, u32[]{:S(2)}) %collective-permute-start.2) | collective-permute-done | bytes 240032 | tf_op jit(solution)/shard_map/ppermute | solution.py:289
  19.3 0.0 collective-permute-done.1.refs_2_
  19.3 0.0 collective-permute-done.refs_1_
  19.3 1.6 %collective-permute-start.4 = (bf16[2,96,625]{2,1,0:T(8,128)(2,1)S(1)}, bf16[2,96,625]{2,1,0:T(8,128)(2,1)S(1)}, u32[]{:S(2)}, u32[]{:S(2)}) collective-permute-start(bf16[2,96,625]{2,1,0:T(8,128)(2,1)S(1)} %collective-permute-done.refs_1_), channel_id=1, source_target_pairs={{0,16},{1,9},{2,18},{3,11},{4,20},{5,13},{6,22},{7,15},{8,24},{9,1... | collective-permute-start | bytes 720008 | tf_op jit(solution)/shard_map/ppermute | solution.py:300
  20.9 0.1 collective-permute-start.8
  20.9 3.8 %collective-permute-start.7 = (bf16[2,96,625]{2,1,0:T(8,128)(2,1)S(1)}, bf16[2,96,625]{2,1,0:T(8,128)(2,1)S(1)}, u32[]{:S(2)}, u32[]{:S(2)}) collective-permute-start(bf16[2,96,625]{2,1,0:T(8,128)(2,1)S(1)} %get-tuple-element.36), channel_id=1, source_target_pairs={{0,6},{1,7},{2,0},{3,1},{4,2},{5,3},{6,4},{7,5},{8,14},{9,15},{10,... | collective-permute-start | bytes 720008 | tf_op jit(solution)/shard_map/ppermute | solution.py:289
  24.7 0.5 collective-permute-start.6
  25.2 1.5 %collective-permute-start.5 = (bf16[2,96,625]{2,1,0:T(8,128)(2,1)S(1)}, bf16[2,96,625]{2,1,0:T(8,128)(2,1)S(1)}, u32[]{:S(2)}, u32[]{:S(2)}) collective-permute-start(bf16[2,96,625]{2,1,0:T(8,128)(2,1)S(1)} %collective-permute-done.2.refs_0_), channel_id=1, source_target_pairs={{0,8},{1,17},{2,10},{3,19},{4,12},{5,21},{6,14},{7,23},{8,0},{9,25... | collective-permute-start | bytes 720008 | tf_op jit(solution)/shard_map/ppermute | solution.py:299
  26.7 1.6 %copy-done.5 = bf16[1600,625]{1,0:T(8,128)(2,1)S(1)} copy-done((bf16[1600,625]{1,0:T(8,128)(2,1)S(1)}, bf16[1600,625]{1,0:T(8,128)(2,1)}, u32[]{:S(2)}) %copy-start.5) | copy-done | bytes 2000024
  28.3 2.6 %shard_map.73.refs_0_ = bf16[2,1600,384]{2,1,0:T(8,128)(2,1)S(1)} custom-call(s32[1]{0:T(128)} %bitcast.column_ref, bf16[2,96,625]{2,1,0:T(8,128)(2,1)S(1)} %get-tuple-element.32.refs_0_, bf16[2,96,625]{2,1,0:T(8,128)(2,1)S(1)} %collective-permute-done.refs_1_, bf16[2,96,625]{2,1,0:T(8,128)(2,1)S(1)} %collective-permute-done.1.refs_2_, ...), custom_call_target="tpu_custom_call" | custom-call | flops 1536000000 | bytes 3417600 | tf_op jit(solution)/shard_map/pallas_call | solution.py:73
  30.9 3.5 %collective-permute-done.7.refs_0_ = bf16[2,96,625]{2,1,0:T(8,128)(2,1)S(1)} collective-permute-done((bf16[2,96,625]{2,1,0:T(8,128)(2,1)S(1)}, bf16[2,96,625]{2,1,0:T(8,128)(2,1)S(1)}, u32[]{:S(2)}, u32[]{:S(2)}) %collective-permute-start.7) | collective-permute-done | bytes 240032 | tf_op jit(solution)/shard_map/ppermute | solution.py:289
  34.4 0.0 collective-permute-done.6.refs_2_
  34.4 0.0 collective-permute-done.5.refs_1_
  34.4 0.0 collective-permute-done.8.refs_2_
  34.4 0.1 collective-permute-start.13
  34.5 1.6 %collective-permute-start.9 = (bf16[2,96,625]{2,1,0:T(8,128)(2,1)S(1)}, bf16[2,96,625]{2,1,0:T(8,128)(2,1)S(1)}, u32[]{:S(2)}, u32[]{:S(2)}) collective-permute-start(bf16[2,96,625]{2,1,0:T(8,128)(2,1)S(1)} %collective-permute-done.5.refs_1_), channel_id=1, source_target_pairs={{0,16},{1,9},{2,18},{3,11},{4,20},{5,13},{6,22},{7,15},{8,24},{9,1... | collective-permute-start | bytes 720008 | tf_op jit(solution)/shard_map/ppermute | solution.py:300
  36.1 2.4 %collective-permute-start.12 = (bf16[2,96,625]{2,1,0:T(8,128)(2,1)S(1)}, bf16[2,96,625]{2,1,0:T(8,128)(2,1)S(1)}, u32[]{:S(2)}, u32[]{:S(2)}) collective-permute-start(bf16[2,96,625]{2,1,0:T(8,128)(2,1)S(1)} %get-tuple-element.43), channel_id=1, source_target_pairs={{0,4},{1,5},{2,6},{3,7},{4,0},{5,1},{6,2},{7,3},{8,12},{9,13},{10,... | collective-permute-start | bytes 720008 | tf_op jit(solution)/shard_map/ppermute | solution.py:289
  38.5 0.5 collective-permute-start.11
  39.0 0.8 collective-permute-start.10
  39.8 1.0 collective-permute-done.9.refs_3_
  40.7 2.6 %shard_map.74.refs_2_ = bf16[2,1600,384]{2,1,0:T(8,128)(2,1)S(1)} custom-call(s32[1]{0:T(128)} %bitcast.column_ref, bf16[2,96,625]{2,1,0:T(8,128)(2,1)S(1)} %collective-permute-done.2.refs_0_, bf16[2,96,625]{2,1,0:T(8,128)(2,1)S(1)} %collective-permute-done.5.refs_1_, bf16[2,96,625]{2,1,0:T(8,128)(2,1)S(1)} %collective-permute-done.6.refs_2_, ...), custom_call_target="tpu_custom_call" | custom-call | flops 1536000000 | bytes 3417600 | tf_op jit(solution)/shard_map/pallas_call | solution.py:73
  43.4 0.0 copy-start.6
  43.4 6.3 %collective-permute-done.12.refs_0_ = bf16[2,96,625]{2,1,0:T(8,128)(2,1)S(1)} collective-permute-done((bf16[2,96,625]{2,1,0:T(8,128)(2,1)S(1)}, bf16[2,96,625]{2,1,0:T(8,128)(2,1)S(1)}, u32[]{:S(2)}, u32[]{:S(2)}) %collective-permute-start.12) | collective-permute-done | bytes 240032 | tf_op jit(solution)/shard_map/ppermute | solution.py:289
  49.7 0.0 collective-permute-done.11.refs_2_
  49.7 0.1 collective-permute-start.18
  49.8 1.5 %collective-permute-start.14 = (bf16[2,96,625]{2,1,0:T(8,128)(2,1)S(1)}, bf16[2,96,625]{2,1,0:T(8,128)(2,1)S(1)}, u32[]{:S(2)}, u32[]{:S(2)}) collective-permute-start(bf16[2,96,625]{2,1,0:T(8,128)(2,1)S(1)} %collective-permute-done.10.refs_1_), channel_id=1, source_target_pairs={{0,16},{1,9},{2,18},{3,11},{4,20},{5,13},{6,22},{7,15},{8,24},{9,1... | collective-permute-start | bytes 720008 | tf_op jit(solution)/shard_map/ppermute | solution.py:300
  51.3 0.0 collective-permute-start.17
  51.3 1.3 %collective-permute-start.16 = (bf16[2,96,625]{2,1,0:T(8,128)(2,1)S(1)}, bf16[2,96,625]{2,1,0:T(8,128)(2,1)S(1)}, u32[]{:S(2)}, u32[]{:S(2)}) collective-permute-start(bf16[2,96,625]{2,1,0:T(8,128)(2,1)S(1)} %collective-permute-done.12.refs_0_), channel_id=1, source_target_pairs={{0,16},{1,9},{2,18},{3,11},{4,20},{5,13},{6,22},{7,15},{8,24},{9,1... | collective-permute-start | bytes 720008 | tf_op jit(solution)/shard_map/ppermute | solution.py:300
  52.6 1.1 collective-permute-start.15
  53.8 4.0 %collective-permute-done.14.refs_3_ = bf16[2,96,625]{2,1,0:T(8,128)(2,1)S(1)} collective-permute-done((bf16[2,96,625]{2,1,0:T(8,128)(2,1)S(1)}, bf16[2,96,625]{2,1,0:T(8,128)(2,1)S(1)}, u32[]{:S(2)}, u32[]{:S(2)}) %collective-permute-start.14) | collective-permute-done | bytes 240032 | tf_op jit(solution)/shard_map/ppermute | solution.py:300
  57.8 2.6 %shard_map.75.refs_6_ = bf16[2,1600,384]{2,1,0:T(8,128)(2,1)S(1)} custom-call(s32[1]{0:T(128)} %bitcast.column_ref, bf16[2,96,625]{2,1,0:T(8,128)(2,1)S(1)} %collective-permute-done.7.refs_0_, bf16[2,96,625]{2,1,0:T(8,128)(2,1)S(1)} %collective-permute-done.10.refs_1_, bf16[2,96,625]{2,1,0:T(8,128)(2,1)S(1)} %collective-permute-done.11.refs_2_, ...), custom_call_target="tpu_custom_call" | custom-call | flops 1536000000 | bytes 3417600 | tf_op jit(solution)/shard_map/pallas_call | solution.py:73
  60.4 0.0 copy-start.4
  60.5 0.9 collective-permute-done.16.refs_2_
  61.3 0.0 collective-permute-done.15.refs_1_
  61.3 1.2 collective-permute-done.17.refs_3_
  62.5 1.6 %collective-permute-start.19 = (bf16[2,96,625]{2,1,0:T(8,128)(2,1)S(1)}, bf16[2,96,625]{2,1,0:T(8,128)(2,1)S(1)}, u32[]{:S(2)}, u32[]{:S(2)}) collective-permute-start(bf16[2,96,625]{2,1,0:T(8,128)(2,1)S(1)} %collective-permute-done.15.refs_1_), channel_id=1, source_target_pairs={{0,16},{1,9},{2,18},{3,11},{4,20},{5,13},{6,22},{7,15},{8,24},{9,1... | collective-permute-start | bytes 720008 | tf_op jit(solution)/shard_map/ppermute | solution.py:300
  64.1 4.6 %collective-permute-done.19.refs_3_ = bf16[2,96,625]{2,1,0:T(8,128)(2,1)S(1)} collective-permute-done((bf16[2,96,625]{2,1,0:T(8,128)(2,1)S(1)}, bf16[2,96,625]{2,1,0:T(8,128)(2,1)S(1)}, u32[]{:S(2)}, u32[]{:S(2)}) %collective-permute-start.19) | collective-permute-done | bytes 240032 | tf_op jit(solution)/shard_map/ppermute | solution.py:300
  68.7 3.4 %shard_map.76.refs_4_ = bf16[2,1600,384]{2,1,0:T(8,128)(2,1)} custom-call(s32[1]{0:T(128)} %bitcast.column_ref, bf16[2,96,625]{2,1,0:T(8,128)(2,1)S(1)} %collective-permute-done.12.refs_0_, bf16[2,96,625]{2,1,0:T(8,128)(2,1)S(1)} %collective-permute-done.15.refs_1_, bf16[2,96,625]{2,1,0:T(8,128)(2,1)S(1)} %collective-permute-done.16.refs_2_, ...), custom_call_target="tpu_custom_call" | custom-call | flops 1536000000 | bytes 3417600 | tf_op jit(solution)/shard_map/pallas_call | solution.py:73
  72.1 0.0 collective-permute-done.20.refs_7_
  72.2 0.1 collective-permute-start.21
  72.3 1.4 %shard_map.77.refs_8_ = bf16[8,800,128]{2,1,0:T(8,128)(2,1)S(1)} custom-call(bf16[800,625]{1,0:T(8,128)(2,1)S(1)} %copy-done.4, bf16[625,256]{1,0:T(8,128)(2,1)S(1)} %bitcast.25, bf16[625,256]{1,0:T(8,128)(2,1)S(1)} %collective-permute-done.3.refs_1_, bf16[625,256]{1,0:T(8,128)(2,1)S(1)} %collective-permute-done.8.refs_2_, ...), custom_call_target="tpu_custom_call" | custom-call | flops 1024000000 | bytes 2560000 | tf_op jit(solution)/shard_map/pallas_call | solution.py:104
  73.7 0.6 collective-permute-start.22
  74.3 0.7 copy.23.owners_ref
  75.0 0.7 copy.24.local_ref
  75.6 3.6 %collective-permute-done.22.refs_9_ = bf16[8,800,128]{2,1,0:T(8,128)(2,1)S(1)} collective-permute-done((bf16[8,800,128]{2,1,0:T(8,128)(2,1)S(1)}, bf16[8,800,128]{2,1,0:T(8,128)(2,1)S(1)}, u32[]{:S(2)}, u32[]{:S(2)}) %collective-permute-start.22) | collective-permute-done | bytes 1638432 | tf_op jit(solution)/shard_map/ppermute | solution.py:286
  79.3 1.2 copy-done.9
  80.5 10.1 %shard_map.79 = bf16[1,2,625,128]{3,2,1,0:T(8,128)(2,1)} custom-call(s32[1]{0:T(128)} %bitcast.column_ref, s32[32,3]{1,0:T(8,128)} %copy.23.owners_ref, s32[32,4]{1,0:T(8,128)} %copy.24.local_ref, bf16[2,1600,384]{2,1,0:T(8,128)(2,1)} %copy-done.1, bf16[2,1600,384]{2,1,0:T(8,128)(2,1)} %copy-done.7, bf16[2,1600,384]{2,1,0:T(8,128)(2,1)} %copy-done.2, ...), custom_call_target="tpu_custom_call" | custom-call | flops 2936012800 | bytes 6553600 | tf_op jit(solution)/shard_map/pallas_call | solution.py:252
  90.6 1.3 %collective-permute-start.24 = (bf16[2,625,128]{2,1,0:T(8,128)(2,1)}, bf16[2,625,128]{2,1,0:T(8,128)(2,1)S(1)}, u32[]{:S(2)}, u32[]{:S(2)}) collective-permute-start(bf16[2,625,128]{2,1,0:T(8,128)(2,1)} %bitcast.28), channel_id=1, source_target_pairs={{0,6},{1,7},{2,0},{3,1},{4,2},{5,3},{6,4},{7,5},{8,14},{9,15},{10,... | collective-permute-start | bytes 960008 | tf_op jit(solution)/shard_map/ppermute | solution.py:289
  91.9 10.1 %shard_map.78 = bf16[1,2,625,128]{3,2,1,0:T(8,128)(2,1)} custom-call(s32[1]{0:T(128)} %bitcast.column_ref, s32[32,3]{1,0:T(8,128)} %copy.23.owners_ref, s32[32,4]{1,0:T(8,128)} %copy.24.local_ref, bf16[2,1600,384]{2,1,0:T(8,128)(2,1)} %copy-done.1, bf16[2,1600,384]{2,1,0:T(8,128)(2,1)} %copy-done.7, bf16[2,1600,384]{2,1,0:T(8,128)(2,1)} %copy-done.2, ...), custom_call_target="tpu_custom_call" | custom-call | flops 2936012800 | bytes 6553600 | tf_op jit(solution)/shard_map/pallas_call | solution.py:252
  102.1 0.1 collective-permute-start.23
  102.2 10.1 %shard_map.80 = bf16[1,2,625,128]{3,2,1,0:T(8,128)(2,1)} custom-call(s32[1]{0:T(128)} %bitcast.column_ref, s32[32,3]{1,0:T(8,128)} %copy.23.owners_ref, s32[32,4]{1,0:T(8,128)} %copy.24.local_ref, bf16[2,1600,384]{2,1,0:T(8,128)(2,1)} %copy-done.1, bf16[2,1600,384]{2,1,0:T(8,128)(2,1)} %copy-done.7, bf16[2,1600,384]{2,1,0:T(8,128)(2,1)} %copy-done.2, ...), custom_call_target="tpu_custom_call" | custom-call | flops 2936012800 | bytes 6553600 | tf_op jit(solution)/shard_map/pallas_call | solution.py:252
  112.3 0.0 copy-start.10
  112.3 1.0 collective-permute-start.25
  113.3 10.1 %shard_map.81 = bf16[1,2,625,128]{3,2,1,0:T(8,128)(2,1)} custom-call(s32[1]{0:T(128)} %bitcast.column_ref, s32[32,3]{1,0:T(8,128)} %copy.23.owners_ref, s32[32,4]{1,0:T(8,128)} %copy.24.local_ref, bf16[2,1600,384]{2,1,0:T(8,128)(2,1)} %copy-done.1, bf16[2,1600,384]{2,1,0:T(8,128)(2,1)} %copy-done.7, bf16[2,1600,384]{2,1,0:T(8,128)(2,1)} %copy-done.2, ...), custom_call_target="tpu_custom_call" | custom-call | flops 2936012800 | bytes 6553600 | tf_op jit(solution)/shard_map/pallas_call | solution.py:252
  123.5 3.1 %collective-permute-done.23 = bf16[2,625,128]{2,1,0:T(8,128)(2,1)S(1)} collective-permute-done((bf16[2,625,128]{2,1,0:T(8,128)(2,1)}, bf16[2,625,128]{2,1,0:T(8,128)(2,1)S(1)}, u32[]{:S(2)}, u32[]{:S(2)}) %collective-permute-start.23) | collective-permute-done | bytes 320032 | tf_op jit(solution)/shard_map/ppermute | solution.py:289
  126.5 1.2 fusion.1
  127.7 1.2 copy.32
  (31 shorter events, 0.1 us)
Async XLA Ops:
  1.3 18.0 %collective-permute-start.3 = (bf16[625,256]{1,0:T(8,128)(2,1)S(1)}, bf16[625,256]{1,0:T(8,128)(2,1)S(1)}, u32[]{:S(2)}, u32[]{:S(2)}) collective-permute-start(bf16[625,256]{1,0:T(8,128)(2,1)S(1)} %bitcast.24), channel_id=1, source_target_pairs={{0,2},{1,3},{2,4},{3,5},{4,6},{5,7},{6,0},{7,1},{8,10},{9,11},{10,... | collective-permute-start | bytes 960008 | tf_op jit(solution)/shard_map/ppermute | solution.py:289
  7.8 11.4 %collective-permute-start.2 = (bf16[2,96,625]{2,1,0:T(8,128)(2,1)S(1)}, bf16[2,96,625]{2,1,0:T(8,128)(2,1)S(1)}, u32[]{:S(2)}, u32[]{:S(2)}) collective-permute-start(bf16[2,96,625]{2,1,0:T(8,128)(2,1)S(1)} %get-tuple-element.61), channel_id=1, source_target_pairs={{0,2},{1,3},{2,4},{3,5},{4,6},{5,7},{6,0},{7,1},{8,10},{9,11},{10,... | collective-permute-start | bytes 720008 | tf_op jit(solution)/shard_map/ppermute | solution.py:289
  9.5 9.8 %collective-permute-start.1 = (bf16[2,96,625]{2,1,0:T(8,128)(2,1)S(1)}, bf16[2,96,625]{2,1,0:T(8,128)(2,1)S(1)}, u32[]{:S(2)}, u32[]{:S(2)}) collective-permute-start(bf16[2,96,625]{2,1,0:T(8,128)(2,1)S(1)} %get-tuple-element.32.refs_0_), channel_id=1, source_target_pairs={{0,16},{1,9},{2,18},{3,11},{4,20},{5,13},{6,22},{7,15},{8,24},{9,1... | collective-permute-start | bytes 720008 | tf_op jit(solution)/shard_map/ppermute | solution.py:300
  11.0 8.3 %collective-permute-start = (bf16[2,96,625]{2,1,0:T(8,128)(2,1)S(1)}, bf16[2,96,625]{2,1,0:T(8,128)(2,1)S(1)}, u32[]{:S(2)}, u32[]{:S(2)}) collective-permute-start(bf16[2,96,625]{2,1,0:T(8,128)(2,1)S(1)} %get-tuple-element.32.refs_0_), channel_id=1, source_target_pairs={{0,8},{1,17},{2,10},{3,19},{4,12},{5,21},{6,14},{7,23},{8,0},{9,25... | collective-permute-start | bytes 720008 | tf_op jit(solution)/shard_map/ppermute | solution.py:299
  19.3 7.4 %collective-permute-start.4 = (bf16[2,96,625]{2,1,0:T(8,128)(2,1)S(1)}, bf16[2,96,625]{2,1,0:T(8,128)(2,1)S(1)}, u32[]{:S(2)}, u32[]{:S(2)}) collective-permute-start(bf16[2,96,625]{2,1,0:T(8,128)(2,1)S(1)} %collective-permute-done.refs_1_), channel_id=1, source_target_pairs={{0,16},{1,9},{2,18},{3,11},{4,20},{5,13},{6,22},{7,15},{8,24},{9,1... | collective-permute-start | bytes 720008 | tf_op jit(solution)/shard_map/ppermute | solution.py:300
  20.9 13.5 %collective-permute-start.8 = (bf16[625,256]{1,0:T(8,128)(2,1)S(1)}, bf16[625,256]{1,0:T(8,128)(2,1)S(1)}, u32[]{:S(2)}, u32[]{:S(2)}) collective-permute-start(bf16[625,256]{1,0:T(8,128)(2,1)S(1)} %collective-permute-done.3.refs_1_), channel_id=1, source_target_pairs={{0,2},{1,3},{2,4},{3,5},{4,6},{5,7},{6,0},{7,1},{8,10},{9,11},{10,... | collective-permute-start | bytes 960008 | tf_op jit(solution)/shard_map/ppermute | solution.py:289
  20.9 13.5 %collective-permute-start.7 = (bf16[2,96,625]{2,1,0:T(8,128)(2,1)S(1)}, bf16[2,96,625]{2,1,0:T(8,128)(2,1)S(1)}, u32[]{:S(2)}, u32[]{:S(2)}) collective-permute-start(bf16[2,96,625]{2,1,0:T(8,128)(2,1)S(1)} %get-tuple-element.36), channel_id=1, source_target_pairs={{0,6},{1,7},{2,0},{3,1},{4,2},{5,3},{6,4},{7,5},{8,14},{9,15},{10,... | collective-permute-start | bytes 720008 | tf_op jit(solution)/shard_map/ppermute | solution.py:289
  24.7 9.7 %collective-permute-start.6 = (bf16[2,96,625]{2,1,0:T(8,128)(2,1)S(1)}, bf16[2,96,625]{2,1,0:T(8,128)(2,1)S(1)}, u32[]{:S(2)}, u32[]{:S(2)}) collective-permute-start(bf16[2,96,625]{2,1,0:T(8,128)(2,1)S(1)} %collective-permute-done.2.refs_0_), channel_id=1, source_target_pairs={{0,16},{1,9},{2,18},{3,11},{4,20},{5,13},{6,22},{7,15},{8,24},{9,1... | collective-permute-start | bytes 720008 | tf_op jit(solution)/shard_map/ppermute | solution.py:300
  25.2 9.2 %collective-permute-start.5 = (bf16[2,96,625]{2,1,0:T(8,128)(2,1)S(1)}, bf16[2,96,625]{2,1,0:T(8,128)(2,1)S(1)}, u32[]{:S(2)}, u32[]{:S(2)}) collective-permute-start(bf16[2,96,625]{2,1,0:T(8,128)(2,1)S(1)} %collective-permute-done.2.refs_0_), channel_id=1, source_target_pairs={{0,8},{1,17},{2,10},{3,19},{4,12},{5,21},{6,14},{7,23},{8,0},{9,25... | collective-permute-start | bytes 720008 | tf_op jit(solution)/shard_map/ppermute | solution.py:299
  26.7 1.6 %copy-start.5 = (bf16[1600,625]{1,0:T(8,128)(2,1)S(1)}, bf16[1600,625]{1,0:T(8,128)(2,1)}, u32[]{:S(2)}) copy-start(bf16[1600,625]{1,0:T(8,128)(2,1)} %constant.59.clone.refs_4_) | copy-start | bytes 6000004
  30.9 12.5 %copy-start.1 = (bf16[2,1600,384]{2,1,0:T(8,128)(2,1)}, bf16[2,1600,384]{2,1,0:T(8,128)(2,1)S(1)}, u32[]{:S(2)}) copy-start(bf16[2,1600,384]{2,1,0:T(8,128)(2,1)S(1)} %shard_map.73.refs_0_) | copy-start | bytes 7372804
  34.4 15.3 %collective-permute-start.13 = (bf16[2,1600,384]{2,1,0:T(8,128)(2,1)S(1)}, bf16[2,1600,384]{2,1,0:T(8,128)(2,1)S(1)}, u32[]{:S(2)}, u32[]{:S(2)}) collective-permute-start(bf16[2,1600,384]{2,1,0:T(8,128)(2,1)S(1)} %shard_map.73.refs_0_), channel_id=1, source_target_pairs={{0,1},{1,0},{2,3},{3,2},{4,5},{5,4},{6,7},{7,6},{8,9},{9,8},{10,11... | collective-permute-start | bytes 7372808 | tf_op jit(solution)/shard_map/ppermute | solution.py:286
  34.5 6.3 %collective-permute-start.9 = (bf16[2,96,625]{2,1,0:T(8,128)(2,1)S(1)}, bf16[2,96,625]{2,1,0:T(8,128)(2,1)S(1)}, u32[]{:S(2)}, u32[]{:S(2)}) collective-permute-start(bf16[2,96,625]{2,1,0:T(8,128)(2,1)S(1)} %collective-permute-done.5.refs_1_), channel_id=1, source_target_pairs={{0,16},{1,9},{2,18},{3,11},{4,20},{5,13},{6,22},{7,15},{8,24},{9,1... | collective-permute-start | bytes 720008 | tf_op jit(solution)/shard_map/ppermute | solution.py:300
  36.1 13.6 %collective-permute-start.12 = (bf16[2,96,625]{2,1,0:T(8,128)(2,1)S(1)}, bf16[2,96,625]{2,1,0:T(8,128)(2,1)S(1)}, u32[]{:S(2)}, u32[]{:S(2)}) collective-permute-start(bf16[2,96,625]{2,1,0:T(8,128)(2,1)S(1)} %get-tuple-element.43), channel_id=1, source_target_pairs={{0,4},{1,5},{2,6},{3,7},{4,0},{5,1},{6,2},{7,3},{8,12},{9,13},{10,... | collective-permute-start | bytes 720008 | tf_op jit(solution)/shard_map/ppermute | solution.py:289
  38.5 11.2 %collective-permute-start.11 = (bf16[2,96,625]{2,1,0:T(8,128)(2,1)S(1)}, bf16[2,96,625]{2,1,0:T(8,128)(2,1)S(1)}, u32[]{:S(2)}, u32[]{:S(2)}) collective-permute-start(bf16[2,96,625]{2,1,0:T(8,128)(2,1)S(1)} %collective-permute-done.7.refs_0_), channel_id=1, source_target_pairs={{0,16},{1,9},{2,18},{3,11},{4,20},{5,13},{6,22},{7,15},{8,24},{9,1... | collective-permute-start | bytes 720008 | tf_op jit(solution)/shard_map/ppermute | solution.py:300
  39.0 10.7 %collective-permute-start.10 = (bf16[2,96,625]{2,1,0:T(8,128)(2,1)S(1)}, bf16[2,96,625]{2,1,0:T(8,128)(2,1)S(1)}, u32[]{:S(2)}, u32[]{:S(2)}) collective-permute-start(bf16[2,96,625]{2,1,0:T(8,128)(2,1)S(1)} %collective-permute-done.7.refs_0_), channel_id=1, source_target_pairs={{0,8},{1,17},{2,10},{3,19},{4,12},{5,21},{6,14},{7,23},{8,0},{9,25... | collective-permute-start | bytes 720008 | tf_op jit(solution)/shard_map/ppermute | solution.py:299
  43.4 17.0 %copy-start.2 = (bf16[2,1600,384]{2,1,0:T(8,128)(2,1)}, bf16[2,1600,384]{2,1,0:T(8,128)(2,1)S(1)}, u32[]{:S(2)}) copy-start(bf16[2,1600,384]{2,1,0:T(8,128)(2,1)S(1)} %shard_map.74.refs_2_) | copy-start | bytes 7372804
  43.4 25.3 %copy-start.6 = (bf16[1600,625]{1,0:T(8,128)(2,1)S(1)}, bf16[1600,625]{1,0:T(8,128)(2,1)}, u32[]{:S(2)}) copy-start(bf16[1600,625]{1,0:T(8,128)(2,1)} %constant.59.clone.refs_4_) | copy-start | bytes 6000004
  49.7 1.6 %copy-start.7 = (bf16[2,1600,384]{2,1,0:T(8,128)(2,1)}, bf16[2,1600,384]{2,1,0:T(8,128)(2,1)S(1)}, u32[]{:S(2)}) copy-start(bf16[2,1600,384]{2,1,0:T(8,128)(2,1)S(1)} %collective-permute-done.13.refs_1_) | copy-start | bytes 7372804
  49.7 12.8 %collective-permute-start.18 = (bf16[2,1600,384]{2,1,0:T(8,128)(2,1)S(1)}, bf16[2,1600,384]{2,1,0:T(8,128)(2,1)}, u32[]{:S(2)}, u32[]{:S(2)}) collective-permute-start(bf16[2,1600,384]{2,1,0:T(8,128)(2,1)S(1)} %shard_map.74.refs_2_), channel_id=1, source_target_pairs={{0,1},{1,0},{2,3},{3,2},{4,5},{5,4},{6,7},{7,6},{8,9},{9,8},{10,11... | collective-permute-start | bytes 7372808 | tf_op jit(solution)/shard_map/ppermute | solution.py:286
  49.8 8.0 %collective-permute-start.14 = (bf16[2,96,625]{2,1,0:T(8,128)(2,1)S(1)}, bf16[2,96,625]{2,1,0:T(8,128)(2,1)S(1)}, u32[]{:S(2)}, u32[]{:S(2)}) collective-permute-start(bf16[2,96,625]{2,1,0:T(8,128)(2,1)S(1)} %collective-permute-done.10.refs_1_), channel_id=1, source_target_pairs={{0,16},{1,9},{2,18},{3,11},{4,20},{5,13},{6,22},{7,15},{8,24},{9,1... | collective-permute-start | bytes 720008 | tf_op jit(solution)/shard_map/ppermute | solution.py:300
  51.3 11.2 %collective-permute-start.17 = (bf16[625,256]{1,0:T(8,128)(2,1)S(1)}, bf16[625,256]{1,0:T(8,128)(2,1)S(1)}, u32[]{:S(2)}, u32[]{:S(2)}) collective-permute-start(bf16[625,256]{1,0:T(8,128)(2,1)S(1)} %collective-permute-done.8.refs_2_), channel_id=1, source_target_pairs={{0,2},{1,3},{2,4},{3,5},{4,6},{5,7},{6,0},{7,1},{8,10},{9,11},{10,... | collective-permute-start | bytes 960008 | tf_op jit(solution)/shard_map/ppermute | solution.py:289
  51.3 10.0 %collective-permute-start.16 = (bf16[2,96,625]{2,1,0:T(8,128)(2,1)S(1)}, bf16[2,96,625]{2,1,0:T(8,128)(2,1)S(1)}, u32[]{:S(2)}, u32[]{:S(2)}) collective-permute-start(bf16[2,96,625]{2,1,0:T(8,128)(2,1)S(1)} %collective-permute-done.12.refs_0_), channel_id=1, source_target_pairs={{0,16},{1,9},{2,18},{3,11},{4,20},{5,13},{6,22},{7,15},{8,24},{9,1... | collective-permute-start | bytes 720008 | tf_op jit(solution)/shard_map/ppermute | solution.py:300
  52.6 8.7 %collective-permute-start.15 = (bf16[2,96,625]{2,1,0:T(8,128)(2,1)S(1)}, bf16[2,96,625]{2,1,0:T(8,128)(2,1)S(1)}, u32[]{:S(2)}, u32[]{:S(2)}) collective-permute-start(bf16[2,96,625]{2,1,0:T(8,128)(2,1)S(1)} %collective-permute-done.12.refs_0_), channel_id=1, source_target_pairs={{0,8},{1,17},{2,10},{3,19},{4,12},{5,21},{6,14},{7,23},{8,0},{9,25... | collective-permute-start | bytes 720008 | tf_op jit(solution)/shard_map/ppermute | solution.py:299
  60.4 11.7 %copy-start.3 = (bf16[2,1600,384]{2,1,0:T(8,128)(2,1)}, bf16[2,1600,384]{2,1,0:T(8,128)(2,1)S(1)}, u32[]{:S(2)}) copy-start(bf16[2,1600,384]{2,1,0:T(8,128)(2,1)S(1)} %shard_map.75.refs_6_) | copy-start | bytes 7372804
  60.4 11.8 %copy-start.4 = (bf16[800,625]{1,0:T(8,128)(2,1)S(1)}, bf16[800,625]{1,0:T(8,128)(2,1)}, u32[]{:S(2)}) copy-start(bf16[800,625]{1,0:T(8,128)(2,1)} %constant.60.clone.matrix_ref) | copy-start | bytes 3000004
  62.5 9.7 %collective-permute-start.20 = (bf16[2,1600,384]{2,1,0:T(8,128)(2,1)S(1)}, bf16[2,1600,384]{2,1,0:T(8,128)(2,1)S(1)}, u32[]{:S(2)}, u32[]{:S(2)}) collective-permute-start(bf16[2,1600,384]{2,1,0:T(8,128)(2,1)S(1)} %shard_map.75.refs_6_), channel_id=1, source_target_pairs={{0,1},{1,0},{2,3},{3,2},{4,5},{5,4},{6,7},{7,6},{8,9},{9,8},{10,11... | collective-permute-start | bytes 7372808 | tf_op jit(solution)/shard_map/ppermute | solution.py:286
  62.5 6.2 %collective-permute-start.19 = (bf16[2,96,625]{2,1,0:T(8,128)(2,1)S(1)}, bf16[2,96,625]{2,1,0:T(8,128)(2,1)S(1)}, u32[]{:S(2)}, u32[]{:S(2)}) collective-permute-start(bf16[2,96,625]{2,1,0:T(8,128)(2,1)S(1)} %collective-permute-done.15.refs_1_), channel_id=1, source_target_pairs={{0,16},{1,9},{2,18},{3,11},{4,20},{5,13},{6,22},{7,15},{8,24},{9,1... | collective-permute-start | bytes 720008 | tf_op jit(solution)/shard_map/ppermute | solution.py:300
  72.1 2.1 %copy-start.11 = (s32[32,3]{0,1:T(4,128)S(1)}, s32[32,3]{0,1:T(4,128)}, u32[]{:S(2)}) copy-start(s32[32,3]{0,1:T(4,128)} %param.10) | copy-start | bytes 1156
  72.1 2.8 %copy-start.12 = (s32[32,4]{0,1:T(4,128)S(1)}, s32[32,4]{0,1:T(4,128)}, u32[]{:S(2)}) copy-start(s32[32,4]{0,1:T(4,128)} %param.11) | copy-start | bytes 1540
  72.2 1.5 %copy-start.8 = (bf16[2,1600,384]{2,1,0:T(8,128)(2,1)}, bf16[2,1600,384]{2,1,0:T(8,128)(2,1)S(1)}, u32[]{:S(2)}) copy-start(bf16[2,1600,384]{2,1,0:T(8,128)(2,1)S(1)} %collective-permute-done.20.refs_7_) | copy-start | bytes 7372804
  72.2 7.1 %collective-permute-start.21 = (bf16[2,1600,384]{2,1,0:T(8,128)(2,1)}, bf16[2,1600,384]{2,1,0:T(8,128)(2,1)}, u32[]{:S(2)}, u32[]{:S(2)}) collective-permute-start(bf16[2,1600,384]{2,1,0:T(8,128)(2,1)} %shard_map.76.refs_4_), channel_id=1, source_target_pairs={{0,1},{1,0},{2,3},{3,2},{4,5},{5,4},{6,7},{7,6},{8,9},{9,8},{10,11... | collective-permute-start | bytes 7372808 | tf_op jit(solution)/shard_map/ppermute | solution.py:286
  73.7 5.5 %copy-start = (bf16[8,800,128]{2,1,0:T(8,128)(2,1)}, bf16[8,800,128]{2,1,0:T(8,128)(2,1)S(1)}, u32[]{:S(2)}) copy-start(bf16[8,800,128]{2,1,0:T(8,128)(2,1)S(1)} %shard_map.77.refs_8_) | copy-start | bytes 4915204
  73.7 5.5 %collective-permute-start.22 = (bf16[8,800,128]{2,1,0:T(8,128)(2,1)S(1)}, bf16[8,800,128]{2,1,0:T(8,128)(2,1)S(1)}, u32[]{:S(2)}, u32[]{:S(2)}) collective-permute-start(bf16[8,800,128]{2,1,0:T(8,128)(2,1)S(1)} %shard_map.77.refs_8_), channel_id=1, source_target_pairs={{0,1},{1,0},{2,3},{3,2},{4,5},{5,4},{6,7},{7,6},{8,9},{9,8},{10,11... | collective-permute-start | bytes 4915208 | tf_op jit(solution)/shard_map/ppermute | solution.py:286
  79.2 1.2 copy-start.9
  90.6 32.8 %collective-permute-start.24 = (bf16[2,625,128]{2,1,0:T(8,128)(2,1)}, bf16[2,625,128]{2,1,0:T(8,128)(2,1)S(1)}, u32[]{:S(2)}, u32[]{:S(2)}) collective-permute-start(bf16[2,625,128]{2,1,0:T(8,128)(2,1)} %bitcast.28), channel_id=1, source_target_pairs={{0,6},{1,7},{2,0},{3,1},{4,2},{5,3},{6,4},{7,5},{8,14},{9,15},{10,... | collective-permute-start | bytes 960008 | tf_op jit(solution)/shard_map/ppermute | solution.py:289
  102.1 24.4 %collective-permute-start.23 = (bf16[2,625,128]{2,1,0:T(8,128)(2,1)}, bf16[2,625,128]{2,1,0:T(8,128)(2,1)S(1)}, u32[]{:S(2)}, u32[]{:S(2)}) collective-permute-start(bf16[2,625,128]{2,1,0:T(8,128)(2,1)} %bitcast.29), channel_id=1, source_target_pairs={{0,4},{1,5},{2,6},{3,7},{4,0},{5,1},{6,2},{7,3},{8,12},{9,13},{10,... | collective-permute-start | bytes 960008 | tf_op jit(solution)/shard_map/ppermute | solution.py:289
  112.3 14.2 %copy-start.10 = (f32[2,128,625]{1,0,2:T(2,128)S(1)}, f32[2,128,625]{1,0,2:T(2,128)}, u32[]{:S(2)}) copy-start(f32[2,128,625]{1,0,2:T(2,128)} %param.9) | copy-start | bytes 1920004
  112.3 14.2 %collective-permute-start.25 = (bf16[2,625,128]{2,1,0:T(8,128)(2,1)}, bf16[2,625,128]{2,1,0:T(8,128)(2,1)S(1)}, u32[]{:S(2)}, u32[]{:S(2)}) collective-permute-start(bf16[2,625,128]{2,1,0:T(8,128)(2,1)} %bitcast.30), channel_id=1, source_target_pairs={{0,2},{1,3},{2,4},{3,5},{4,6},{5,7},{6,0},{7,1},{8,10},{9,11},{10,... | collective-permute-start | bytes 960008 | tf_op jit(solution)/shard_map/ppermute | solution.py:289

commit v13 on v12

--- a/solution.py
+++ b/solution.py
@@ -22,7 +22,6 @@
 BF = jnp.bfloat16
 F32 = jnp.float32
 VMEM_BYTES = 48 * 1024 * 1024
-LADDER_VMEM_BYTES = 60 * 1024 * 1024
 
 
 def spread(spots, rows):
@@ -137,7 +136,6 @@
         places = find(i, j, column_ref, owners_ref, local_ref)
         fetch(factor_refs, *places["col"], 0 if made else None, c_buf, to, sems.at[to, 0])
         fetch(factor_refs, *places["row"], 1 if made else None, r_buf, to, sems.at[to, 1])
-        fetch(amp_refs, *places["amp"], None, amp_buf, to, sems.at[to, 2])
 
     @pl.when(at == 0)
     def _():
@@ -152,9 +150,16 @@
     def _():
         acc_ref[...] = jnp.zeros_like(acc_ref)
 
-    for n, buffer in enumerate((c_buf, r_buf, amp_buf)):
+    here = find(column, step, column_ref, owners_ref, local_ref)
+    for core in range(2):
+
+        @pl.when(here["amp"][0] == core)
+        def _():
+            amp_buf[...] = amp_refs[core][here["amp"][1]]
+
+    for n, buffer in enumerate((c_buf, r_buf)):
         pltpu.make_async_copy(buffer.at[slot], buffer.at[slot], sems.at[slot, n]).wait()
-    c_form, r_form, amp_form = c_buf.at[slot], r_buf.at[slot], amp_buf.at[slot]
+    c_form, r_form, amp_form = c_buf.at[slot], r_buf.at[slot], amp_buf
     if not made:
         forms = refs[8]
         for i, tile in enumerate((c_form, r_form)):
@@ -192,7 +197,7 @@
                     for p in range(1, GROUP):
                         block = jnp.where(at_spot[p], blocks[(p - i) % GROUP], block)
                     u_ref[START[i] + A * PAD : START[i] + (A + 1) * PAD, D * LANES : (D + 1) * LANES] = block.astype(BF)
-    out = local_ref[find(column, step, column_ref, owners_ref, local_ref)["task"], 3]
+    out = local_ref[here["task"], 3]
     for i in range(GROUP):
         acc_ref[out, START[i] : START[i + 1], :] += jnp.dot(
             u_ref[START[i] : START[i + 1], :], turned(amp_form, range(GROUPS), i), preferred_element_type=F32
@@ -235,15 +240,15 @@
 
     anywhere = pl.BlockSpec(memory_space=pl.ANY)
     operands = [*tiles, *amps]
-    in_specs = [anywhere] * (len(tiles) + 2)
+    in_specs = [anywhere] * len(tiles) + [pl.BlockSpec(memory_space=pltpu.VMEM)] * 2
     scratch = [
         pltpu.VMEM((ROWS, WIDE), F32),
         pltpu.VMEM((ROWS, WIDE), BF),
         pltpu.VMEM((blocks_here, ROWS, pairs), F32),
         pltpu.VMEM((2, *held), BF),
         pltpu.VMEM((2, *held), BF),
-        pltpu.VMEM((2, ROWS, pairs), BF),
-        pltpu.SemaphoreType.DMA((2, 3)),
+        pltpu.VMEM((ROWS, pairs), BF),
+        pltpu.SemaphoreType.DMA((2, 2)),
     ]
     if not made:
         in_specs.append(pl.BlockSpec(matrix.shape, lambda i, j, *tables: (0, 0)))
@@ -259,7 +264,7 @@
             out_specs=pl.BlockSpec((1, blocks_here, TV * TV, pairs), lambda i, j, *tables: (i, 0, 0, 0)),
             scratch_shapes=scratch,
         ),
-        compiler_params=pltpu.CompilerParams(vmem_limit_bytes=LADDER_VMEM_BYTES),
+        compiler_params=pltpu.CompilerParams(vmem_limit_bytes=VMEM_BYTES),
         cost_estimate=pl.CostEstimate(
             flops=2 * columns * tasks * ROWS * WIDE * (depth + pairs),
             bytes_accessed=2 * columns * tasks * ROWS * 2 * (depth + pairs),
@@ -300,29 +305,31 @@
         second_side = lambda x: lax.ppermute(x, ("pair", "task"), sides[1])
         made_forms = lambda *parts: prepare(parts, column[None], matrix)
         own = amplitudes.transpose(2, 0, 1).reshape(TV * TV, blocks_here * pairs)
-        amp1 = around(own, 1)
         part0 = mine[0]
         a0, b0, part1 = first_side(part0), second_side(part0), around(mine[1], 1)
 
-        a0, b0, part0, part1, amp1, to3 = after((a0, b0, part0, part1, amp1, mine[3]), ())
-        q0, a1, b1, part3, amp2 = second_side(a0), first_side(part1), second_side(part1), around(to3, 3), around(amp1, 1)
+        a0, b0, part0, part1, own, to3 = after((a0, b0, part0, part1, own, mine[3]), ())
+        q0, a1, b1, part3, amp1 = second_side(a0), first_side(part1), second_side(part1), around(to3, 3), around(own, 1)
         forms0 = made_forms(part0, a0, b0, q0)
 
-        forms0, part1, a1, b1, part3, to2, amp2 = after((forms0, part1, a1, b1, part3, mine[2], amp2), ())
+        forms0, part1, a1, b1, part3, to2, amp1 = after((forms0, part1, a1, b1, part3, mine[2], amp1), ())
         q1, a3, b3, part2 = second_side(a1), first_side(part3), second_side(part3), around(to2, 2)
         far0 = other_core(forms0)
         forms1 = made_forms(part1, a1, b1, q1)
 
-        forms1, part3, a3, b3, part2, far0, amp2 = after((forms1, part3, a3, b3, part2, far0, amp2), ())
-        q3, a2, b2, amp3 = second_side(a3), first_side(part2), second_side(part2), around(amp2, 1)
+        forms1, part3, a3, b3, part2, amp1, far0 = after((forms1, part3, a3, b3, part2, amp1, far0), ())
+        q3, a2, b2, amp2 = second_side(a3), first_side(part2), second_side(part2), around(amp1, 1)
         far1 = other_core(forms1)
         forms3 = made_forms(part3, a3, b3, q3)
 
-        forms3, part2, a2, b2, amp3, far1 = after((forms3, part2, a2, b2, amp3, far1), ())
-        q2, far3 = second_side(a2), other_core(forms3)
+        forms3, part2, a2, b2, amp2, far1 = after((forms3, part2, a2, b2, amp2, far1), ())
+        q2, amp3 = second_side(a2), around(amp2, 1)
+        far3 = other_core(forms3)
+        forms2 = made_forms(part2, a2, b2, q2)
+
+        forms2, amp3, far3 = after((forms2, amp3, far3), ())
+        far2 = other_core(forms2)
         amps = prepare_amps([own, amp1, amp2, amp3], blocks_here, jnp.asarray(amp_matrix()))
-        forms2 = made_forms(part2, a2, b2, q2)
-        far2 = other_core(after(forms2, far3))
         held = [forms0, far0, forms1, far1, forms2, far2, forms3, far3]
     else:
         parts = [mine[0]] + [around(mine[by], by) for by in range(1, levels)]

time: 130 us -> 127 us (0.977)
  waiting for transfers between devices: 34.9 us -> 43.6 us
  starting transfers between devices: 29.1 us -> 25.1 us
  Pallas kernels: 53.3 us -> 50.1 us
  local copies, waits for them, and re-layouts: 10.1 us -> 6.98 us
    ppermute x9, waiting for transfers between devices: 20.8 us -> 25 us  [around(): lax.ppermute(x, 'task', [(c, (c + 2 * by) % task_count) for c in range(ta...]
    ppermute x8, waiting for transfers between devices: 10.5 us -> 13.8 us  [per_device(): second_side = lambda x: lax.ppermute(x, ('pair', 'task'), sides[1])]
    pallas_call x4, Pallas kernels: 40.5 us -> 37.4 us  [ladders(): pl.pallas_call(functools.partial(ladder_kernel, find, made, len(tiles)),...]
    unnamed x31 -> x29, local copies, waits for them, and re-layouts: 8.82 us -> 5.7 us
    ppermute x9, starting transfers between devices: 13.3 us -> 10.8 us  [around(): lax.ppermute(x, 'task', [(c, (c + 2 * by) % task_count) for c in range(ta...]
  transfers between devices with their start and end apart: 26 -> 26, of which waited for: 10 -> 12; matrix products, arithmetic and copies ran while one was open for 4% -> 0% of each run, Pallas kernels for 34% -> 32%
where the time goes in v13:
time: 127 us; the launch traced here: 126 us
  Pallas kernels  50.1 us (39%)
  waiting for transfers between devices  43.6 us (34%)
  starting transfers between devices  25.1 us (20%)
  local copies, waits for them, and re-layouts  6.98 us (5%)
    pallas_call x4, Pallas kernels, ladders(): pl.pallas_call(functools.partial(ladder_kernel, find, made, len(tiles)),...  37.4 us
    ppermute x9, waiting for transfers between devices, around(): lax.ppermute(x, 'task', [(c, (c + 2 * by) % task_count) for c in range(ta...  25 us
    ppermute x8, waiting for transfers between devices, per_device(): second_side = lambda x: lax.ppermute(x, ('pair', 'task'), sides[1])  13.8 us
    pallas_call x4, Pallas kernels, prepare(): pl.pallas_call(prepare_kernel, out_shape=jax.ShapeDtypeStruct((count, mat...  11.3 us
    ppermute x9, starting transfers between devices, around(): lax.ppermute(x, 'task', [(c, (c + 2 * by) % task_count) for c in range(ta...  10.8 us
    ppermute x8, starting transfers between devices, per_device(): second_side = lambda x: lax.ppermute(x, ('pair', 'task'), sides[1])  9.25 us
    unnamed x29, local copies, waits for them, and re-layouts  5.7 us
    ppermute x5, waiting for transfers between devices, per_device(): lax.ppermute(x, 'task', [(c, c ^ 1) for c in range(task_count)])  4.81 us
  transfers between devices with their start and end apart: 26, of which 12 were waited for; matrix products, arithmetic and copies ran while one was open for 0% of the time, Pallas kernels for 32%

profile of v13, /device:TPU:0, one launch (start us, length us, event | category | flops | bytes accessed | tf_op | source)
XLA Modules:
  0.0 126.3 jit_solution(16165794475947013316)
XLA Ops:
  0.0 3.5 %copy.22 = bf16[2,384,625]{2,1,0:T(8,128)(2,1)S(1)} copy(bf16[2,384,625]{1,0,2:T(2,128)(2,1)} %param.7) | data formatting | bytes 1920000 | tf_op args[0]
  3.5 0.1 dynamic-slice_bitcast_fusion
  3.6 3.1 %collective-permute-start.2 = (bf16[2,96,625]{2,1,0:T(8,128)(2,1)S(1)}, bf16[2,96,625]{2,1,0:T(8,128)(2,1)S(1)}, u32[]{:S(2)}, u32[]{:S(2)}) collective-permute-start(bf16[2,96,625]{2,1,0:T(8,128)(2,1)S(1)} %get-tuple-element.65), channel_id=1, source_target_pairs={{0,2},{1,3},{2,4},{3,5},{4,6},{5,7},{6,0},{7,1},{8,10},{9,11},{10,... | collective-permute-start | bytes 720008 | tf_op jit(solution)/shard_map/ppermute | solution.py:294
  6.7 1.5 %collective-permute-start.1 = (bf16[2,96,625]{2,1,0:T(8,128)(2,1)S(1)}, bf16[2,96,625]{2,1,0:T(8,128)(2,1)S(1)}, u32[]{:S(2)}, u32[]{:S(2)}) collective-permute-start(bf16[2,96,625]{2,1,0:T(8,128)(2,1)S(1)} %get-tuple-element.34.refs_0_), channel_id=1, source_target_pairs={{0,16},{1,9},{2,18},{3,11},{4,20},{5,13},{6,22},{7,15},{8,24},{9,1... | collective-permute-start | bytes 720008 | tf_op jit(solution)/shard_map/ppermute | solution.py:305
  8.2 1.5 %collective-permute-start = (bf16[2,96,625]{2,1,0:T(8,128)(2,1)S(1)}, bf16[2,96,625]{2,1,0:T(8,128)(2,1)S(1)}, u32[]{:S(2)}, u32[]{:S(2)}) collective-permute-start(bf16[2,96,625]{2,1,0:T(8,128)(2,1)S(1)} %get-tuple-element.34.refs_0_), channel_id=1, source_target_pairs={{0,8},{1,17},{2,10},{3,19},{4,12},{5,21},{6,14},{7,23},{8,0},{9,25... | collective-permute-start | bytes 720008 | tf_op jit(solution)/shard_map/ppermute | solution.py:304
  9.7 0.3 pad
  10.0 4.7 %collective-permute-done.2.refs_0_ = bf16[2,96,625]{2,1,0:T(8,128)(2,1)S(1)} collective-permute-done((bf16[2,96,625]{2,1,0:T(8,128)(2,1)S(1)}, bf16[2,96,625]{2,1,0:T(8,128)(2,1)S(1)}, u32[]{:S(2)}, u32[]{:S(2)}) %collective-permute-start.2) | collective-permute-done | bytes 240032 | tf_op jit(solution)/shard_map/ppermute | solution.py:294
  14.7 0.6 collective-permute-done.1.refs_2_
  15.3 0.0 collective-permute-done.refs_1_
  15.4 1.5 %collective-permute-start.3 = (bf16[2,96,625]{2,1,0:T(8,128)(2,1)S(1)}, bf16[2,96,625]{2,1,0:T(8,128)(2,1)S(1)}, u32[]{:S(2)}, u32[]{:S(2)}) collective-permute-start(bf16[2,96,625]{2,1,0:T(8,128)(2,1)S(1)} %collective-permute-done.refs_1_), channel_id=1, source_target_pairs={{0,16},{1,9},{2,18},{3,11},{4,20},{5,13},{6,22},{7,15},{8,24},{9,1... | collective-permute-start | bytes 720008 | tf_op jit(solution)/shard_map/ppermute | solution.py:305
  16.9 1.6 %collective-permute-start.7 = (bf16[625,256]{1,0:T(8,128)(2,1)S(1)}, bf16[625,256]{1,0:T(8,128)(2,1)S(1)}, u32[]{:S(2)}, u32[]{:S(2)}) collective-permute-start(bf16[625,256]{1,0:T(8,128)(2,1)S(1)} %bitcast.24), channel_id=1, source_target_pairs={{0,2},{1,3},{2,4},{3,5},{4,6},{5,7},{6,0},{7,1},{8,10},{9,11},{10,... | collective-permute-start | bytes 960008 | tf_op jit(solution)/shard_map/ppermute | solution.py:294
  18.5 2.2 %collective-permute-start.6 = (bf16[2,96,625]{2,1,0:T(8,128)(2,1)S(1)}, bf16[2,96,625]{2,1,0:T(8,128)(2,1)S(1)}, u32[]{:S(2)}, u32[]{:S(2)}) collective-permute-start(bf16[2,96,625]{2,1,0:T(8,128)(2,1)S(1)} %get-tuple-element.38), channel_id=1, source_target_pairs={{0,6},{1,7},{2,0},{3,1},{4,2},{5,3},{6,4},{7,5},{8,14},{9,15},{10,... | collective-permute-start | bytes 720008 | tf_op jit(solution)/shard_map/ppermute | solution.py:294
  20.7 0.5 collective-permute-start.5
  21.2 0.8 collective-permute-start.4
  22.1 0.0 collective-permute-done.3.refs_3_
  22.1 2.6 %shard_map.73.refs_0_ = bf16[2,1600,384]{2,1,0:T(8,128)(2,1)S(1)} custom-call(s32[1]{0:T(128)} %bitcast.column_ref, bf16[2,96,625]{2,1,0:T(8,128)(2,1)S(1)} %get-tuple-element.34.refs_0_, bf16[2,96,625]{2,1,0:T(8,128)(2,1)S(1)} %collective-permute-done.refs_1_, bf16[2,96,625]{2,1,0:T(8,128)(2,1)S(1)} %collective-permute-done.1.refs_2_, ...), custom_call_target="tpu_custom_call" | custom-call | flops 1536000000 | bytes 3417600 | tf_op jit(solution)/shard_map/pallas_call | solution.py:72
  24.7 6.6 %collective-permute-done.6.refs_0_ = bf16[2,96,625]{2,1,0:T(8,128)(2,1)S(1)} collective-permute-done((bf16[2,96,625]{2,1,0:T(8,128)(2,1)S(1)}, bf16[2,96,625]{2,1,0:T(8,128)(2,1)S(1)}, u32[]{:S(2)}, u32[]{:S(2)}) %collective-permute-start.6) | collective-permute-done | bytes 240032 | tf_op jit(solution)/shard_map/ppermute | solution.py:294
  31.4 0.0 collective-permute-done.5.refs_2_
  31.4 0.0 collective-permute-done.4.refs_1_
  31.4 0.0 collective-permute-done.7.refs_1_
  31.4 0.1 collective-permute-start.12
  31.4 1.6 %collective-permute-start.8 = (bf16[2,96,625]{2,1,0:T(8,128)(2,1)S(1)}, bf16[2,96,625]{2,1,0:T(8,128)(2,1)S(1)}, u32[]{:S(2)}, u32[]{:S(2)}) collective-permute-start(bf16[2,96,625]{2,1,0:T(8,128)(2,1)S(1)} %collective-permute-done.4.refs_1_), channel_id=1, source_target_pairs={{0,16},{1,9},{2,18},{3,11},{4,20},{5,13},{6,22},{7,15},{8,24},{9,1... | collective-permute-start | bytes 720008 | tf_op jit(solution)/shard_map/ppermute | solution.py:305
  33.0 1.1 collective-permute-start.11
  34.2 0.5 collective-permute-start.10
  34.7 1.7 %collective-permute-start.9 = (bf16[2,96,625]{2,1,0:T(8,128)(2,1)S(1)}, bf16[2,96,625]{2,1,0:T(8,128)(2,1)S(1)}, u32[]{:S(2)}, u32[]{:S(2)}) collective-permute-start(bf16[2,96,625]{2,1,0:T(8,128)(2,1)S(1)} %collective-permute-done.6.refs_0_), channel_id=1, source_target_pairs={{0,8},{1,17},{2,10},{3,19},{4,12},{5,21},{6,14},{7,23},{8,0},{9,25... | collective-permute-start | bytes 720008 | tf_op jit(solution)/shard_map/ppermute | solution.py:304
  36.4 2.0 %collective-permute-done.8.refs_3_ = bf16[2,96,625]{2,1,0:T(8,128)(2,1)S(1)} collective-permute-done((bf16[2,96,625]{2,1,0:T(8,128)(2,1)S(1)}, bf16[2,96,625]{2,1,0:T(8,128)(2,1)S(1)}, u32[]{:S(2)}, u32[]{:S(2)}) %collective-permute-start.8) | collective-permute-done | bytes 240032 | tf_op jit(solution)/shard_map/ppermute | solution.py:305
  38.4 2.6 %shard_map.74.refs_2_ = bf16[2,1600,384]{2,1,0:T(8,128)(2,1)S(1)} custom-call(s32[1]{0:T(128)} %bitcast.column_ref, bf16[2,96,625]{2,1,0:T(8,128)(2,1)S(1)} %collective-permute-done.2.refs_0_, bf16[2,96,625]{2,1,0:T(8,128)(2,1)S(1)} %collective-permute-done.4.refs_1_, bf16[2,96,625]{2,1,0:T(8,128)(2,1)S(1)} %collective-permute-done.5.refs_2_, ...), custom_call_target="tpu_custom_call" | custom-call | flops 1536000000 | bytes 3417600 | tf_op jit(solution)/shard_map/pallas_call | solution.py:72
  41.1 6.4 %collective-permute-done.11.refs_0_ = bf16[2,96,625]{2,1,0:T(8,128)(2,1)S(1)} collective-permute-done((bf16[2,96,625]{2,1,0:T(8,128)(2,1)S(1)}, bf16[2,96,625]{2,1,0:T(8,128)(2,1)S(1)}, u32[]{:S(2)}, u32[]{:S(2)}) %collective-permute-start.11) | collective-permute-done | bytes 240032 | tf_op jit(solution)/shard_map/ppermute | solution.py:294
  47.5 0.1 collective-permute-start.17
  47.5 0.9 collective-permute-start.13
  48.4 0.0 collective-permute-start.16
  48.4 1.2 collective-permute-start.15
  49.6 0.3 collective-permute-start.14
  49.9 5.6 %collective-permute-done.13.refs_3_ = bf16[2,96,625]{2,1,0:T(8,128)(2,1)S(1)} collective-permute-done((bf16[2,96,625]{2,1,0:T(8,128)(2,1)S(1)}, bf16[2,96,625]{2,1,0:T(8,128)(2,1)S(1)}, u32[]{:S(2)}, u32[]{:S(2)}) %collective-permute-start.13) | collective-permute-done | bytes 240032 | tf_op jit(solution)/shard_map/ppermute | solution.py:305
  55.5 2.6 %shard_map.75.refs_6_ = bf16[2,1600,384]{2,1,0:T(8,128)(2,1)S(1)} custom-call(s32[1]{0:T(128)} %bitcast.column_ref, bf16[2,96,625]{2,1,0:T(8,128)(2,1)S(1)} %collective-permute-done.6.refs_0_, bf16[2,96,625]{2,1,0:T(8,128)(2,1)S(1)} %collective-permute-done.9.refs_1_, bf16[2,96,625]{2,1,0:T(8,128)(2,1)S(1)} %collective-permute-done.10.refs_2_, ...), custom_call_target="tpu_custom_call" | custom-call | flops 1536000000 | bytes 3417600 | tf_op jit(solution)/shard_map/pallas_call | solution.py:72
  58.2 0.0 copy-start.4
  58.2 0.9 collective-permute-done.15.refs_2_
  59.1 0.3 collective-permute-done.16.refs_2_
  59.4 0.0 collective-permute-done.17.refs_3_
  59.4 0.0 collective-permute-start.20
  59.4 1.5 %collective-permute-start.18 = (bf16[2,96,625]{2,1,0:T(8,128)(2,1)S(1)}, bf16[2,96,625]{2,1,0:T(8,128)(2,1)S(1)}, u32[]{:S(2)}, u32[]{:S(2)}) collective-permute-start(bf16[2,96,625]{2,1,0:T(8,128)(2,1)S(1)} %collective-permute-done.14.refs_1_), channel_id=1, source_target_pairs={{0,16},{1,9},{2,18},{3,11},{4,20},{5,13},{6,22},{7,15},{8,24},{9,1... | collective-permute-start | bytes 720008 | tf_op jit(solution)/shard_map/ppermute | solution.py:305
  60.9 4.7 %collective-permute-done.18.refs_3_ = bf16[2,96,625]{2,1,0:T(8,128)(2,1)S(1)} collective-permute-done((bf16[2,96,625]{2,1,0:T(8,128)(2,1)S(1)}, bf16[2,96,625]{2,1,0:T(8,128)(2,1)S(1)}, u32[]{:S(2)}, u32[]{:S(2)}) %collective-permute-start.18) | collective-permute-done | bytes 240032 | tf_op jit(solution)/shard_map/ppermute | solution.py:305
  65.6 3.4 %shard_map.76.refs_4_ = bf16[2,1600,384]{2,1,0:T(8,128)(2,1)} custom-call(s32[1]{0:T(128)} %bitcast.column_ref, bf16[2,96,625]{2,1,0:T(8,128)(2,1)S(1)} %collective-permute-done.11.refs_0_, bf16[2,96,625]{2,1,0:T(8,128)(2,1)S(1)} %collective-permute-done.14.refs_1_, bf16[2,96,625]{2,1,0:T(8,128)(2,1)S(1)} %collective-permute-done.15.refs_2_, ...), custom_call_target="tpu_custom_call" | custom-call | flops 1536000000 | bytes 3417600 | tf_op jit(solution)/shard_map/pallas_call | solution.py:72
  69.0 3.7 %collective-permute-done.19.refs_3_ = bf16[625,256]{1,0:T(8,128)(2,1)S(1)} collective-permute-done((bf16[625,256]{1,0:T(8,128)(2,1)S(1)}, bf16[625,256]{1,0:T(8,128)(2,1)S(1)}, u32[]{:S(2)}, u32[]{:S(2)}) %collective-permute-start.19) | collective-permute-done | bytes 320032 | tf_op jit(solution)/shard_map/ppermute | solution.py:294
  72.7 0.0 collective-permute-done.20.refs_7_
  72.7 1.4 %shard_map.77.refs_8_ = bf16[8,800,128]{2,1,0:T(8,128)(2,1)S(1)} custom-call(bf16[800,625]{1,0:T(8,128)(2,1)S(1)} %copy-done.4, bf16[625,256]{1,0:T(8,128)(2,1)S(1)} %bitcast.25, bf16[625,256]{1,0:T(8,128)(2,1)S(1)} %collective-permute-done.7.refs_1_, bf16[625,256]{1,0:T(8,128)(2,1)S(1)} %collective-permute-done.16.refs_2_, ...), custom_call_target="tpu_custom_call" | custom-call | flops 1024000000 | bytes 2560000 | tf_op jit(solution)/shard_map/pallas_call | solution.py:103
  74.1 0.6 collective-permute-start.22
  74.7 0.1 copy.23.owners_ref
  74.8 0.1 copy.24.local_ref
  74.9 4.8 %collective-permute-done.22.refs_9_ = bf16[8,800,128]{2,1,0:T(8,128)(2,1)S(1)} collective-permute-done((bf16[8,800,128]{2,1,0:T(8,128)(2,1)S(1)}, bf16[8,800,128]{2,1,0:T(8,128)(2,1)S(1)}, u32[]{:S(2)}, u32[]{:S(2)}) %collective-permute-start.22) | collective-permute-done | bytes 1638432 | tf_op jit(solution)/shard_map/ppermute | solution.py:291
  79.7 1.7 %copy-done.1 = bf16[2,1600,384]{2,1,0:T(8,128)(2,1)S(1)} copy-done((bf16[2,1600,384]{2,1,0:T(8,128)(2,1)S(1)}, bf16[2,1600,384]{2,1,0:T(8,128)(2,1)}, u32[]{:S(2)}) %copy-start.1) | copy-done | bytes 2457624
  81.4 9.3 %shard_map.79 = bf16[1,2,625,128]{3,2,1,0:T(8,128)(2,1)S(1)} custom-call(s32[1]{0:T(128)} %bitcast.column_ref, s32[32,3]{1,0:T(8,128)S(1)} %copy.23.owners_ref, s32[32,4]{1,0:T(8,128)S(1)} %copy.24.local_ref, bf16[2,1600,384]{2,1,0:T(8,128)(2,1)S(1)} %copy-done.1, bf16[2,1600,384]{2,1,0:T(8,128)(2,1)} %copy-done.6, bf16[2,1600,384]{2,1,0:T(8,128)(2,1)} %copy-done.2, ...), custom_call_target="tpu_custom_call" | custom-call | flops 2936012800 | bytes 6553600 | tf_op jit(solution)/shard_map/pallas_call | solution.py:257
  90.7 0.2 collective-permute-start.24
  90.9 9.5 %shard_map.78 = bf16[1,2,625,128]{3,2,1,0:T(8,128)(2,1)S(1)} custom-call(s32[1]{0:T(128)} %bitcast.column_ref, s32[32,3]{1,0:T(8,128)S(1)} %copy.23.owners_ref, s32[32,4]{1,0:T(8,128)S(1)} %copy.24.local_ref, bf16[2,1600,384]{2,1,0:T(8,128)(2,1)S(1)} %copy-done.1, bf16[2,1600,384]{2,1,0:T(8,128)(2,1)} %copy-done.6, bf16[2,1600,384]{2,1,0:T(8,128)(2,1)} %copy-done.2, ...), custom_call_target="tpu_custom_call" | custom-call | flops 2936012800 | bytes 6553600 | tf_op jit(solution)/shard_map/pallas_call | solution.py:257
  100.4 0.3 collective-permute-start.23
  100.7 9.3 %shard_map.80 = bf16[1,2,625,128]{3,2,1,0:T(8,128)(2,1)S(1)} custom-call(s32[1]{0:T(128)} %bitcast.column_ref, s32[32,3]{1,0:T(8,128)S(1)} %copy.23.owners_ref, s32[32,4]{1,0:T(8,128)S(1)} %copy.24.local_ref, bf16[2,1600,384]{2,1,0:T(8,128)(2,1)S(1)} %copy-done.1, bf16[2,1600,384]{2,1,0:T(8,128)(2,1)} %copy-done.6, bf16[2,1600,384]{2,1,0:T(8,128)(2,1)} %copy-done.2, ...), custom_call_target="tpu_custom_call" | custom-call | flops 2936012800 | bytes 6553600 | tf_op jit(solution)/shard_map/pallas_call | solution.py:257
  110.0 0.0 copy-start.8
  110.0 2.2 %collective-permute-start.25 = (bf16[2,625,128]{2,1,0:T(8,128)(2,1)S(1)}, bf16[2,625,128]{2,1,0:T(8,128)(2,1)S(1)}, u32[]{:S(2)}, u32[]{:S(2)}) collective-permute-start(bf16[2,625,128]{2,1,0:T(8,128)(2,1)S(1)} %bitcast.28), channel_id=1, source_target_pairs={{0,2},{1,3},{2,4},{3,5},{4,6},{5,7},{6,0},{7,1},{8,10},{9,11},{10,... | collective-permute-start | bytes 960008 | tf_op jit(solution)/shard_map/ppermute | solution.py:294
  112.2 9.3 %shard_map.81 = bf16[1,2,625,128]{3,2,1,0:T(8,128)(2,1)S(1)} custom-call(s32[1]{0:T(128)} %bitcast.column_ref, s32[32,3]{1,0:T(8,128)S(1)} %copy.23.owners_ref, s32[32,4]{1,0:T(8,128)S(1)} %copy.24.local_ref, bf16[2,1600,384]{2,1,0:T(8,128)(2,1)S(1)} %copy-done.1, bf16[2,1600,384]{2,1,0:T(8,128)(2,1)} %copy-done.6, bf16[2,1600,384]{2,1,0:T(8,128)(2,1)} %copy-done.2, ...), custom_call_target="tpu_custom_call" | custom-call | flops 2936012800 | bytes 6553600 | tf_op jit(solution)/shard_map/pallas_call | solution.py:257
  121.5 0.0 collective-permute-done.24
  121.5 3.4 %collective-permute-done.23 = bf16[2,625,128]{2,1,0:T(8,128)(2,1)S(1)} collective-permute-done((bf16[2,625,128]{2,1,0:T(8,128)(2,1)S(1)}, bf16[2,625,128]{2,1,0:T(8,128)(2,1)S(1)}, u32[]{:S(2)}, u32[]{:S(2)}) %collective-permute-start.23) | collective-permute-done | bytes 320032 | tf_op jit(solution)/shard_map/ppermute | solution.py:294
  124.9 0.0 collective-permute-done.25
  124.9 0.2 fusion.1
  125.1 1.2 copy.32
  (29 shorter events, 0.1 us)
Async XLA Ops:
  0.0 9.7 %copy-start.9 = (bf16[2,128,625]{1,0,2:T(2,128)(2,1)S(1)}, bf16[2,128,625]{1,0,2:T(2,128)(2,1)}, u32[]{:S(2)}) copy-start(bf16[2,128,625]{1,0,2:T(2,128)(2,1)} %param.8) | copy-start | bytes 960004
  0.0 22.1 %copy-start.5 = (bf16[1600,625]{1,0:T(8,128)(2,1)S(1)}, bf16[1600,625]{1,0:T(8,128)(2,1)}, u32[]{:S(2)}) copy-start(bf16[1600,625]{1,0:T(8,128)(2,1)} %constant.59.clone.refs_4_) | copy-start | bytes 6000004
  3.6 11.1 %collective-permute-start.2 = (bf16[2,96,625]{2,1,0:T(8,128)(2,1)S(1)}, bf16[2,96,625]{2,1,0:T(8,128)(2,1)S(1)}, u32[]{:S(2)}, u32[]{:S(2)}) collective-permute-start(bf16[2,96,625]{2,1,0:T(8,128)(2,1)S(1)} %get-tuple-element.65), channel_id=1, source_target_pairs={{0,2},{1,3},{2,4},{3,5},{4,6},{5,7},{6,0},{7,1},{8,10},{9,11},{10,... | collective-permute-start | bytes 720008 | tf_op jit(solution)/shard_map/ppermute | solution.py:294
  6.7 8.6 %collective-permute-start.1 = (bf16[2,96,625]{2,1,0:T(8,128)(2,1)S(1)}, bf16[2,96,625]{2,1,0:T(8,128)(2,1)S(1)}, u32[]{:S(2)}, u32[]{:S(2)}) collective-permute-start(bf16[2,96,625]{2,1,0:T(8,128)(2,1)S(1)} %get-tuple-element.34.refs_0_), channel_id=1, source_target_pairs={{0,16},{1,9},{2,18},{3,11},{4,20},{5,13},{6,22},{7,15},{8,24},{9,1... | collective-permute-start | bytes 720008 | tf_op jit(solution)/shard_map/ppermute | solution.py:305
  8.2 7.1 %collective-permute-start = (bf16[2,96,625]{2,1,0:T(8,128)(2,1)S(1)}, bf16[2,96,625]{2,1,0:T(8,128)(2,1)S(1)}, u32[]{:S(2)}, u32[]{:S(2)}) collective-permute-start(bf16[2,96,625]{2,1,0:T(8,128)(2,1)S(1)} %get-tuple-element.34.refs_0_), channel_id=1, source_target_pairs={{0,8},{1,17},{2,10},{3,19},{4,12},{5,21},{6,14},{7,23},{8,0},{9,25... | collective-permute-start | bytes 720008 | tf_op jit(solution)/shard_map/ppermute | solution.py:304
  15.4 6.7 %collective-permute-start.3 = (bf16[2,96,625]{2,1,0:T(8,128)(2,1)S(1)}, bf16[2,96,625]{2,1,0:T(8,128)(2,1)S(1)}, u32[]{:S(2)}, u32[]{:S(2)}) collective-permute-start(bf16[2,96,625]{2,1,0:T(8,128)(2,1)S(1)} %collective-permute-done.refs_1_), channel_id=1, source_target_pairs={{0,16},{1,9},{2,18},{3,11},{4,20},{5,13},{6,22},{7,15},{8,24},{9,1... | collective-permute-start | bytes 720008 | tf_op jit(solution)/shard_map/ppermute | solution.py:305
  16.9 14.5 %collective-permute-start.7 = (bf16[625,256]{1,0:T(8,128)(2,1)S(1)}, bf16[625,256]{1,0:T(8,128)(2,1)S(1)}, u32[]{:S(2)}, u32[]{:S(2)}) collective-permute-start(bf16[625,256]{1,0:T(8,128)(2,1)S(1)} %bitcast.24), channel_id=1, source_target_pairs={{0,2},{1,3},{2,4},{3,5},{4,6},{5,7},{6,0},{7,1},{8,10},{9,11},{10,... | collective-permute-start | bytes 960008 | tf_op jit(solution)/shard_map/ppermute | solution.py:294
  18.5 12.9 %collective-permute-start.6 = (bf16[2,96,625]{2,1,0:T(8,128)(2,1)S(1)}, bf16[2,96,625]{2,1,0:T(8,128)(2,1)S(1)}, u32[]{:S(2)}, u32[]{:S(2)}) collective-permute-start(bf16[2,96,625]{2,1,0:T(8,128)(2,1)S(1)} %get-tuple-element.38), channel_id=1, source_target_pairs={{0,6},{1,7},{2,0},{3,1},{4,2},{5,3},{6,4},{7,5},{8,14},{9,15},{10,... | collective-permute-start | bytes 720008 | tf_op jit(solution)/shard_map/ppermute | solution.py:294
  20.7 10.7 %collective-permute-start.5 = (bf16[2,96,625]{2,1,0:T(8,128)(2,1)S(1)}, bf16[2,96,625]{2,1,0:T(8,128)(2,1)S(1)}, u32[]{:S(2)}, u32[]{:S(2)}) collective-permute-start(bf16[2,96,625]{2,1,0:T(8,128)(2,1)S(1)} %collective-permute-done.2.refs_0_), channel_id=1, source_target_pairs={{0,16},{1,9},{2,18},{3,11},{4,20},{5,13},{6,22},{7,15},{8,24},{9,1... | collective-permute-start | bytes 720008 | tf_op jit(solution)/shard_map/ppermute | solution.py:305
  21.2 10.2 %collective-permute-start.4 = (bf16[2,96,625]{2,1,0:T(8,128)(2,1)S(1)}, bf16[2,96,625]{2,1,0:T(8,128)(2,1)S(1)}, u32[]{:S(2)}, u32[]{:S(2)}) collective-permute-start(bf16[2,96,625]{2,1,0:T(8,128)(2,1)S(1)} %collective-permute-done.2.refs_0_), channel_id=1, source_target_pairs={{0,8},{1,17},{2,10},{3,19},{4,12},{5,21},{6,14},{7,23},{8,0},{9,25... | collective-permute-start | bytes 720008 | tf_op jit(solution)/shard_map/ppermute | solution.py:304
  24.7 16.4 %copy-start = (bf16[2,1600,384]{2,1,0:T(8,128)(2,1)}, bf16[2,1600,384]{2,1,0:T(8,128)(2,1)S(1)}, u32[]{:S(2)}) copy-start(bf16[2,1600,384]{2,1,0:T(8,128)(2,1)S(1)} %shard_map.73.refs_0_) | copy-start | bytes 7372804
  31.4 16.1 %collective-permute-start.12 = (bf16[2,1600,384]{2,1,0:T(8,128)(2,1)S(1)}, bf16[2,1600,384]{2,1,0:T(8,128)(2,1)S(1)}, u32[]{:S(2)}, u32[]{:S(2)}) collective-permute-start(bf16[2,1600,384]{2,1,0:T(8,128)(2,1)S(1)} %shard_map.73.refs_0_), channel_id=1, source_target_pairs={{0,1},{1,0},{2,3},{3,2},{4,5},{5,4},{6,7},{7,6},{8,9},{9,8},{10,11... | collective-permute-start | bytes 7372808 | tf_op jit(solution)/shard_map/ppermute | solution.py:291
  31.4 7.0 %collective-permute-start.8 = (bf16[2,96,625]{2,1,0:T(8,128)(2,1)S(1)}, bf16[2,96,625]{2,1,0:T(8,128)(2,1)S(1)}, u32[]{:S(2)}, u32[]{:S(2)}) collective-permute-start(bf16[2,96,625]{2,1,0:T(8,128)(2,1)S(1)} %collective-permute-done.4.refs_1_), channel_id=1, source_target_pairs={{0,16},{1,9},{2,18},{3,11},{4,20},{5,13},{6,22},{7,15},{8,24},{9,1... | collective-permute-start | bytes 720008 | tf_op jit(solution)/shard_map/ppermute | solution.py:305
  33.0 14.4 %collective-permute-start.11 = (bf16[2,96,625]{2,1,0:T(8,128)(2,1)S(1)}, bf16[2,96,625]{2,1,0:T(8,128)(2,1)S(1)}, u32[]{:S(2)}, u32[]{:S(2)}) collective-permute-start(bf16[2,96,625]{2,1,0:T(8,128)(2,1)S(1)} %get-tuple-element.45), channel_id=1, source_target_pairs={{0,4},{1,5},{2,6},{3,7},{4,0},{5,1},{6,2},{7,3},{8,12},{9,13},{10,... | collective-permute-start | bytes 720008 | tf_op jit(solution)/shard_map/ppermute | solution.py:294
  34.2 13.3 %collective-permute-start.10 = (bf16[2,96,625]{2,1,0:T(8,128)(2,1)S(1)}, bf16[2,96,625]{2,1,0:T(8,128)(2,1)S(1)}, u32[]{:S(2)}, u32[]{:S(2)}) collective-permute-start(bf16[2,96,625]{2,1,0:T(8,128)(2,1)S(1)} %collective-permute-done.6.refs_0_), channel_id=1, source_target_pairs={{0,16},{1,9},{2,18},{3,11},{4,20},{5,13},{6,22},{7,15},{8,24},{9,1... | collective-permute-start | bytes 720008 | tf_op jit(solution)/shard_map/ppermute | solution.py:305
  34.7 12.8 %collective-permute-start.9 = (bf16[2,96,625]{2,1,0:T(8,128)(2,1)S(1)}, bf16[2,96,625]{2,1,0:T(8,128)(2,1)S(1)}, u32[]{:S(2)}, u32[]{:S(2)}) collective-permute-start(bf16[2,96,625]{2,1,0:T(8,128)(2,1)S(1)} %collective-permute-done.6.refs_0_), channel_id=1, source_target_pairs={{0,8},{1,17},{2,10},{3,19},{4,12},{5,21},{6,14},{7,23},{8,0},{9,25... | collective-permute-start | bytes 720008 | tf_op jit(solution)/shard_map/ppermute | solution.py:304
  41.1 17.1 %copy-start.2 = (bf16[2,1600,384]{2,1,0:T(8,128)(2,1)}, bf16[2,1600,384]{2,1,0:T(8,128)(2,1)S(1)}, u32[]{:S(2)}) copy-start(bf16[2,1600,384]{2,1,0:T(8,128)(2,1)S(1)} %shard_map.74.refs_2_) | copy-start | bytes 7372804
  47.4 10.7 %copy-start.6 = (bf16[2,1600,384]{2,1,0:T(8,128)(2,1)}, bf16[2,1600,384]{2,1,0:T(8,128)(2,1)S(1)}, u32[]{:S(2)}) copy-start(bf16[2,1600,384]{2,1,0:T(8,128)(2,1)S(1)} %collective-permute-done.12.refs_1_) | copy-start | bytes 7372804
  47.5 11.9 %collective-permute-start.17 = (bf16[2,1600,384]{2,1,0:T(8,128)(2,1)S(1)}, bf16[2,1600,384]{2,1,0:T(8,128)(2,1)}, u32[]{:S(2)}, u32[]{:S(2)}) collective-permute-start(bf16[2,1600,384]{2,1,0:T(8,128)(2,1)S(1)} %shard_map.74.refs_2_), channel_id=1, source_target_pairs={{0,1},{1,0},{2,3},{3,2},{4,5},{5,4},{6,7},{7,6},{8,9},{9,8},{10,11... | collective-permute-start | bytes 7372808 | tf_op jit(solution)/shard_map/ppermute | solution.py:291
  47.5 8.0 %collective-permute-start.13 = (bf16[2,96,625]{2,1,0:T(8,128)(2,1)S(1)}, bf16[2,96,625]{2,1,0:T(8,128)(2,1)S(1)}, u32[]{:S(2)}, u32[]{:S(2)}) collective-permute-start(bf16[2,96,625]{2,1,0:T(8,128)(2,1)S(1)} %collective-permute-done.9.refs_1_), channel_id=1, source_target_pairs={{0,16},{1,9},{2,18},{3,11},{4,20},{5,13},{6,22},{7,15},{8,24},{9,1... | collective-permute-start | bytes 720008 | tf_op jit(solution)/shard_map/ppermute | solution.py:305
  48.4 10.9 %collective-permute-start.16 = (bf16[625,256]{1,0:T(8,128)(2,1)S(1)}, bf16[625,256]{1,0:T(8,128)(2,1)S(1)}, u32[]{:S(2)}, u32[]{:S(2)}) collective-permute-start(bf16[625,256]{1,0:T(8,128)(2,1)S(1)} %collective-permute-done.7.refs_1_), channel_id=1, source_target_pairs={{0,2},{1,3},{2,4},{3,5},{4,6},{5,7},{6,0},{7,1},{8,10},{9,11},{10,... | collective-permute-start | bytes 960008 | tf_op jit(solution)/shard_map/ppermute | solution.py:294
  48.4 10.6 %collective-permute-start.15 = (bf16[2,96,625]{2,1,0:T(8,128)(2,1)S(1)}, bf16[2,96,625]{2,1,0:T(8,128)(2,1)S(1)}, u32[]{:S(2)}, u32[]{:S(2)}) collective-permute-start(bf16[2,96,625]{2,1,0:T(8,128)(2,1)S(1)} %collective-permute-done.11.refs_0_), channel_id=1, source_target_pairs={{0,16},{1,9},{2,18},{3,11},{4,20},{5,13},{6,22},{7,15},{8,24},{9,1... | collective-permute-start | bytes 720008 | tf_op jit(solution)/shard_map/ppermute | solution.py:305
  49.6 9.4 %collective-permute-start.14 = (bf16[2,96,625]{2,1,0:T(8,128)(2,1)S(1)}, bf16[2,96,625]{2,1,0:T(8,128)(2,1)S(1)}, u32[]{:S(2)}, u32[]{:S(2)}) collective-permute-start(bf16[2,96,625]{2,1,0:T(8,128)(2,1)S(1)} %collective-permute-done.11.refs_0_), channel_id=1, source_target_pairs={{0,8},{1,17},{2,10},{3,19},{4,12},{5,21},{6,14},{7,23},{8,0},{9,25... | collective-permute-start | bytes 720008 | tf_op jit(solution)/shard_map/ppermute | solution.py:304
  58.2 10.8 %copy-start.3 = (bf16[2,1600,384]{2,1,0:T(8,128)(2,1)}, bf16[2,1600,384]{2,1,0:T(8,128)(2,1)S(1)}, u32[]{:S(2)}) copy-start(bf16[2,1600,384]{2,1,0:T(8,128)(2,1)S(1)} %shard_map.75.refs_6_) | copy-start | bytes 7372804
  58.2 14.5 %copy-start.4 = (bf16[800,625]{1,0:T(8,128)(2,1)S(1)}, bf16[800,625]{1,0:T(8,128)(2,1)}, u32[]{:S(2)}) copy-start(bf16[800,625]{1,0:T(8,128)(2,1)} %constant.60.clone.matrix_ref) | copy-start | bytes 3000004
  59.4 13.3 %collective-permute-start.20 = (bf16[2,1600,384]{2,1,0:T(8,128)(2,1)S(1)}, bf16[2,1600,384]{2,1,0:T(8,128)(2,1)S(1)}, u32[]{:S(2)}, u32[]{:S(2)}) collective-permute-start(bf16[2,1600,384]{2,1,0:T(8,128)(2,1)S(1)} %shard_map.75.refs_6_), channel_id=1, source_target_pairs={{0,1},{1,0},{2,3},{3,2},{4,5},{5,4},{6,7},{7,6},{8,9},{9,8},{10,11... | collective-permute-start | bytes 7372808 | tf_op jit(solution)/shard_map/ppermute | solution.py:291
  59.4 6.2 %collective-permute-start.18 = (bf16[2,96,625]{2,1,0:T(8,128)(2,1)S(1)}, bf16[2,96,625]{2,1,0:T(8,128)(2,1)S(1)}, u32[]{:S(2)}, u32[]{:S(2)}) collective-permute-start(bf16[2,96,625]{2,1,0:T(8,128)(2,1)S(1)} %collective-permute-done.14.refs_1_), channel_id=1, source_target_pairs={{0,16},{1,9},{2,18},{3,11},{4,20},{5,13},{6,22},{7,15},{8,24},{9,1... | collective-permute-start | bytes 720008 | tf_op jit(solution)/shard_map/ppermute | solution.py:305
  60.9 11.8 %collective-permute-start.19 = (bf16[625,256]{1,0:T(8,128)(2,1)S(1)}, bf16[625,256]{1,0:T(8,128)(2,1)S(1)}, u32[]{:S(2)}, u32[]{:S(2)}) collective-permute-start(bf16[625,256]{1,0:T(8,128)(2,1)S(1)} %collective-permute-done.16.refs_2_), channel_id=1, source_target_pairs={{0,2},{1,3},{2,4},{3,5},{4,6},{5,7},{6,0},{7,1},{8,10},{9,11},{10,... | collective-permute-start | bytes 960008 | tf_op jit(solution)/shard_map/ppermute | solution.py:294
  69.0 5.7 %copy-start.10 = (s32[32,3]{0,1:T(4,128)S(1)}, s32[32,3]{0,1:T(4,128)}, u32[]{:S(2)}) copy-start(s32[32,3]{0,1:T(4,128)} %param.10) | copy-start | bytes 1156
  69.0 5.8 %copy-start.11 = (s32[32,4]{0,1:T(4,128)S(1)}, s32[32,4]{0,1:T(4,128)}, u32[]{:S(2)}) copy-start(s32[32,4]{0,1:T(4,128)} %param.11) | copy-start | bytes 1540
  72.7 1.5 %copy-start.7 = (bf16[2,1600,384]{2,1,0:T(8,128)(2,1)}, bf16[2,1600,384]{2,1,0:T(8,128)(2,1)S(1)}, u32[]{:S(2)}) copy-start(bf16[2,1600,384]{2,1,0:T(8,128)(2,1)S(1)} %collective-permute-done.20.refs_7_) | copy-start | bytes 7372804
  72.7 7.0 %collective-permute-start.21 = (bf16[2,1600,384]{2,1,0:T(8,128)(2,1)}, bf16[2,1600,384]{2,1,0:T(8,128)(2,1)}, u32[]{:S(2)}, u32[]{:S(2)}) collective-permute-start(bf16[2,1600,384]{2,1,0:T(8,128)(2,1)} %shard_map.76.refs_4_), channel_id=1, source_target_pairs={{0,1},{1,0},{2,3},{3,2},{4,5},{5,4},{6,7},{7,6},{8,9},{9,8},{10,11... | collective-permute-start | bytes 7372808 | tf_op jit(solution)/shard_map/ppermute | solution.py:291
  74.1 5.5 %collective-permute-start.22 = (bf16[8,800,128]{2,1,0:T(8,128)(2,1)S(1)}, bf16[8,800,128]{2,1,0:T(8,128)(2,1)S(1)}, u32[]{:S(2)}, u32[]{:S(2)}) collective-permute-start(bf16[8,800,128]{2,1,0:T(8,128)(2,1)S(1)} %shard_map.77.refs_8_), channel_id=1, source_target_pairs={{0,1},{1,0},{2,3},{3,2},{4,5},{5,4},{6,7},{7,6},{8,9},{9,8},{10,11... | collective-permute-start | bytes 4915208 | tf_op jit(solution)/shard_map/ppermute | solution.py:291
  79.7 1.7 %copy-start.1 = (bf16[2,1600,384]{2,1,0:T(8,128)(2,1)S(1)}, bf16[2,1600,384]{2,1,0:T(8,128)(2,1)}, u32[]{:S(2)}) copy-start(bf16[2,1600,384]{2,1,0:T(8,128)(2,1)} %copy-done) | copy-start | bytes 7372804
  90.7 30.8 %collective-permute-start.24 = (bf16[2,625,128]{2,1,0:T(8,128)(2,1)S(1)}, bf16[2,625,128]{2,1,0:T(8,128)(2,1)S(1)}, u32[]{:S(2)}, u32[]{:S(2)}) collective-permute-start(bf16[2,625,128]{2,1,0:T(8,128)(2,1)S(1)} %bitcast.26), channel_id=1, source_target_pairs={{0,6},{1,7},{2,0},{3,1},{4,2},{5,3},{6,4},{7,5},{8,14},{9,15},{10,... | collective-permute-start | bytes 960008 | tf_op jit(solution)/shard_map/ppermute | solution.py:294
  100.4 24.5 %collective-permute-start.23 = (bf16[2,625,128]{2,1,0:T(8,128)(2,1)S(1)}, bf16[2,625,128]{2,1,0:T(8,128)(2,1)S(1)}, u32[]{:S(2)}, u32[]{:S(2)}) collective-permute-start(bf16[2,625,128]{2,1,0:T(8,128)(2,1)S(1)} %bitcast.27), channel_id=1, source_target_pairs={{0,4},{1,5},{2,6},{3,7},{4,0},{5,1},{6,2},{7,3},{8,12},{9,13},{10,... | collective-permute-start | bytes 960008 | tf_op jit(solution)/shard_map/ppermute | solution.py:294
  110.0 14.9 %copy-start.8 = (f32[2,128,625]{1,0,2:T(2,128)S(1)}, f32[2,128,625]{1,0,2:T(2,128)}, u32[]{:S(2)}) copy-start(f32[2,128,625]{1,0,2:T(2,128)} %param.9) | copy-start | bytes 1920004
  110.0 14.9 %collective-permute-start.25 = (bf16[2,625,128]{2,1,0:T(8,128)(2,1)S(1)}, bf16[2,625,128]{2,1,0:T(8,128)(2,1)S(1)}, u32[]{:S(2)}, u32[]{:S(2)}) collective-permute-start(bf16[2,625,128]{2,1,0:T(8,128)(2,1)S(1)} %bitcast.28), channel_id=1, source_target_pairs={{0,2},{1,3},{2,4},{3,5},{4,6},{5,7},{6,0},{7,1},{8,10},{9,11},{10,... | collective-permute-start | bytes 960008 | tf_op jit(solution)/shard_map/ppermute | solution.py:294

commit v14 on v13

--- a/solution.py
+++ b/solution.py
@@ -22,6 +22,7 @@
 BF = jnp.bfloat16
 F32 = jnp.float32
 VMEM_BYTES = 48 * 1024 * 1024
+LADDER_VMEM_BYTES = 56 * 1024 * 1024
 
 
 def spread(spots, rows):
@@ -264,7 +265,7 @@
             out_specs=pl.BlockSpec((1, blocks_here, TV * TV, pairs), lambda i, j, *tables: (i, 0, 0, 0)),
             scratch_shapes=scratch,
         ),
-        compiler_params=pltpu.CompilerParams(vmem_limit_bytes=VMEM_BYTES),
+        compiler_params=pltpu.CompilerParams(vmem_limit_bytes=LADDER_VMEM_BYTES),
         cost_estimate=pl.CostEstimate(
             flops=2 * columns * tasks * ROWS * WIDE * (depth + pairs),
             bytes_accessed=2 * columns * tasks * ROWS * 2 * (depth + pairs),
@@ -305,14 +306,16 @@
         second_side = lambda x: lax.ppermute(x, ("pair", "task"), sides[1])
         made_forms = lambda *parts: prepare(parts, column[None], matrix)
         own = amplitudes.transpose(2, 0, 1).reshape(TV * TV, blocks_here * pairs)
+        amp1 = around(own, 1)
         part0 = mine[0]
         a0, b0, part1 = first_side(part0), second_side(part0), around(mine[1], 1)
 
-        a0, b0, part0, part1, own, to3 = after((a0, b0, part0, part1, own, mine[3]), ())
-        q0, a1, b1, part3, amp1 = second_side(a0), first_side(part1), second_side(part1), around(to3, 3), around(own, 1)
+        a0, b0, part0, part1, amp1, own, to3 = after((a0, b0, part0, part1, amp1, own, mine[3]), ())
+        q0, a1, b1, part3 = second_side(a0), first_side(part1), second_side(part1), around(to3, 3)
+        far_own = other_core(own)
         forms0 = made_forms(part0, a0, b0, q0)
 
-        forms0, part1, a1, b1, part3, to2, amp1 = after((forms0, part1, a1, b1, part3, mine[2], amp1), ())
+        forms0, part1, a1, b1, part3, to2, far_own = after((forms0, part1, a1, b1, part3, mine[2], far_own), ())
         q1, a3, b3, part2 = second_side(a1), first_side(part3), second_side(part3), around(to2, 2)
         far0 = other_core(forms0)
         forms1 = made_forms(part1, a1, b1, q1)
@@ -322,14 +325,15 @@
         far1 = other_core(forms1)
         forms3 = made_forms(part3, a3, b3, q3)
 
-        forms3, part2, a2, b2, amp2, far1 = after((forms3, part2, a2, b2, amp2, far1), ())
+        forms3, part2, a2, b2, amp1, amp2, far1 = after((forms3, part2, a2, b2, amp1, amp2, far1), ())
         q2, amp3 = second_side(a2), around(amp2, 1)
-        far3 = other_core(forms3)
+        far3, far_amp1, far_amp2 = other_core(forms3), other_core(amp1), other_core(amp2)
         forms2 = made_forms(part2, a2, b2, q2)
 
-        forms2, amp3, far3 = after((forms2, amp3, far3), ())
-        far2 = other_core(forms2)
-        amps = prepare_amps([own, amp1, amp2, amp3], blocks_here, jnp.asarray(amp_matrix()))
+        forms2, amp3, far3, far_amp1, far_amp2 = after((forms2, amp3, far3, far_amp1, far_amp2), ())
+        far2, far_amp3 = other_core(forms2), other_core(amp3)
+        amps = [[own, amp1, amp2, amp3], [far_own, far_amp1, far_amp2, far_amp3]]
+        amps = [prepare_amps(tiles, blocks_here, jnp.asarray(amp_matrix())) for tiles in amps]
         held = [forms0, far0, forms1, far1, forms2, far2, forms3, far3]
     else:
         parts = [mine[0]] + [around(mine[by], by) for by in range(1, levels)]
@@ -338,16 +342,16 @@
         amps = lax.all_gather(tiles, "task", axis=0, axis_index_groups=same_core)
         amps = amps[(level - jnp.arange(levels)) % levels].reshape(levels * blocks_here, ROWS, pairs)
         held = lax.all_gather(jnp.stack(parts), "pair", axis=2, tiled=True)
+        amps = [amps, other_core(amps)]
         held = [jnp.stack([held, other_core(held)], axis=1).reshape(total, depth * pair_count, -1)]
-    amps = (amps, other_core(amps))
-
-    ladder = None
+    ladder, here = None, column[None]
     calls = min(levels, 4)
     width = levels // calls
     order = [2, 3, 1, 0] if calls == 4 else list(reversed(range(calls)))
     for call in order:
         first = call * width
-        sums = ladders(first, width, levels, blocks_here, column[None], task_owners, task_local, held, amps, matrix)
+        sums = ladders(first, width, levels, blocks_here, here, task_owners, task_local, held, amps, matrix)
+        here = after(here, sums)
         for i in range(width):
             term = (around(sums[i], first + i) if first + i else sums[i]).astype(F32)
             ladder = term if ladder is None else ladder + term

time: 127 us -> 152 us (1.20)
  Pallas kernels: 50.1 us -> 64.2 us
  local copies, waits for them, and re-layouts: 6.98 us -> 15.6 us
  starting transfers between devices: 25.1 us -> 26.8 us
    pallas_call x4, Pallas kernels: 37.4 us -> 48.9 us  [ladders(): pl.pallas_call(functools.partial(ladder_kernel, find, made, len(tiles)),...]
    unnamed x29 -> x51, local copies, waits for them, and re-layouts: 5.7 us -> 14.4 us
    ppermute x5 -> x8, waiting for transfers between devices: 4.81 us -> 0.02 us  [per_device(): lax.ppermute(x, 'task', [(c, c ^ 1) for c in range(task_count)])]
    pallas_call x1 -> x2, Pallas kernels: 1.44 us -> 4 us  [prepare_amps(): pl.pallas_call(amp_kernel, out_shape=jax.ShapeDtypeStruct((levels * block...]
    ppermute x9, waiting for transfers between devices: 25 us -> 27.5 us  [around(): lax.ppermute(x, 'task', [(c, (c + 2 * by) % task_count) for c in range(ta...]
    ppermute x8, waiting for transfers between devices: 13.8 us -> 15.5 us  [per_device(): second_side = lambda x: lax.ppermute(x, ('pair', 'task'), sides[1])]
  transfers between devices with their start and end apart: 26 -> 29, of which waited for: 12 -> 12; matrix products, arithmetic and copies ran while one was open for 0% -> 3% of each run, Pallas kernels for 32% -> 18%
where the time goes in v14:
time: 152 us; the launch traced here: 151 us
  Pallas kernels  64.2 us (42%)
  waiting for transfers between devices  43.1 us (28%)
  starting transfers between devices  26.8 us (18%)
  local copies, waits for them, and re-layouts  15.6 us (10%)
    pallas_call x4, Pallas kernels, ladders(): pl.pallas_call(functools.partial(ladder_kernel, find, made, len(tiles)),...  48.9 us
    ppermute x9, waiting for transfers between devices, around(): lax.ppermute(x, 'task', [(c, (c + 2 * by) % task_count) for c in range(ta...  27.5 us
    ppermute x8, waiting for transfers between devices, per_device(): second_side = lambda x: lax.ppermute(x, ('pair', 'task'), sides[1])  15.5 us
    unnamed x51, local copies, waits for them, and re-layouts  14.4 us
    ppermute x9, starting transfers between devices, around(): lax.ppermute(x, 'task', [(c, (c + 2 * by) % task_count) for c in range(ta...  11.4 us
    pallas_call x4, Pallas kernels, prepare(): pl.pallas_call(prepare_kernel, out_shape=jax.ShapeDtypeStruct((count, mat...  11.3 us
    ppermute x8, starting transfers between devices, per_device(): second_side = lambda x: lax.ppermute(x, ('pair', 'task'), sides[1])  8.54 us
    ppermute x4, starting transfers between devices, per_device(): first_side = lambda x: lax.ppermute(x, ('pair', 'task'), sides[0])  5.53 us
  transfers between devices with their start and end apart: 29, of which 12 were waited for; matrix products, arithmetic and copies ran while one was open for 3% of the time, Pallas kernels for 18%

profile of v14, /device:TPU:0, one launch (start us, length us, event | category | flops | bytes accessed | tf_op | source)
XLA Modules:
  0.0 151.2 jit_solution(14033433402254032156)
XLA Ops:
  0.0 1.2 pad
  1.3 0.0 copy-start.6
  1.3 3.1 %collective-permute-start.3 = (bf16[625,256]{1,0:T(8,128)(2,1)S(1)}, bf16[625,256]{1,0:T(8,128)(2,1)}, u32[]{:S(2)}, u32[]{:S(2)}) collective-permute-start(bf16[625,256]{1,0:T(8,128)(2,1)S(1)} %bitcast.24), channel_id=1, source_target_pairs={{0,2},{1,3},{2,4},{3,5},{4,6},{5,7},{6,0},{7,1},{8,10},{9,11},{10,... | collective-permute-start | bytes 960008 | tf_op jit(solution)/shard_map/ppermute | solution.py:295
  4.4 3.3 %copy.23 = bf16[2,384,625]{2,1,0:T(8,128)(2,1)S(1)} copy(bf16[2,384,625]{1,0,2:T(2,128)(2,1)} %param.8) | data formatting | bytes 1920000 | tf_op args[0]
  7.7 0.1 dynamic-slice_bitcast_fusion
  7.9 1.6 %collective-permute-start.2 = (bf16[2,96,625]{2,1,0:T(8,128)(2,1)S(1)}, bf16[2,96,625]{2,1,0:T(8,128)(2,1)S(1)}, u32[]{:S(2)}, u32[]{:S(2)}) collective-permute-start(bf16[2,96,625]{2,1,0:T(8,128)(2,1)S(1)} %get-tuple-element.79), channel_id=1, source_target_pairs={{0,2},{1,3},{2,4},{3,5},{4,6},{5,7},{6,0},{7,1},{8,10},{9,11},{10,... | collective-permute-start | bytes 720008 | tf_op jit(solution)/shard_map/ppermute | solution.py:295
  9.5 1.5 %collective-permute-start.1 = (bf16[2,96,625]{2,1,0:T(8,128)(2,1)S(1)}, bf16[2,96,625]{2,1,0:T(8,128)(2,1)S(1)}, u32[]{:S(2)}, u32[]{:S(2)}) collective-permute-start(bf16[2,96,625]{2,1,0:T(8,128)(2,1)S(1)} %get-tuple-element.41.refs_0_), channel_id=1, source_target_pairs={{0,16},{1,9},{2,18},{3,11},{4,20},{5,13},{6,22},{7,15},{8,24},{9,1... | collective-permute-start | bytes 720008 | tf_op jit(solution)/shard_map/ppermute | solution.py:306
  11.0 1.5 collective-permute-start
  12.5 6.8 %collective-permute-done.2.refs_0_ = bf16[2,96,625]{2,1,0:T(8,128)(2,1)S(1)} collective-permute-done((bf16[2,96,625]{2,1,0:T(8,128)(2,1)S(1)}, bf16[2,96,625]{2,1,0:T(8,128)(2,1)S(1)}, u32[]{:S(2)}, u32[]{:S(2)}) %collective-permute-start.2) | collective-permute-done | bytes 240032 | tf_op jit(solution)/shard_map/ppermute | solution.py:295
  19.3 1.6 %collective-permute-start.4 = (bf16[2,96,625]{2,1,0:T(8,128)(2,1)S(1)}, bf16[2,96,625]{2,1,0:T(8,128)(2,1)S(1)}, u32[]{:S(2)}, u32[]{:S(2)}) collective-permute-start(bf16[2,96,625]{2,1,0:T(8,128)(2,1)S(1)} %collective-permute-done.refs_1_), channel_id=1, source_target_pairs={{0,16},{1,9},{2,18},{3,11},{4,20},{5,13},{6,22},{7,15},{8,24},{9,1... | collective-permute-start | bytes 720008 | tf_op jit(solution)/shard_map/ppermute | solution.py:306
  20.9 1.7 %collective-permute-start.7 = (bf16[2,96,625]{2,1,0:T(8,128)(2,1)S(1)}, bf16[2,96,625]{2,1,0:T(8,128)(2,1)S(1)}, u32[]{:S(2)}, u32[]{:S(2)}) collective-permute-start(bf16[2,96,625]{2,1,0:T(8,128)(2,1)S(1)} %get-tuple-element.45), channel_id=1, source_target_pairs={{0,6},{1,7},{2,0},{3,1},{4,2},{5,3},{6,4},{7,5},{8,14},{9,15},{10,... | collective-permute-start | bytes 720008 | tf_op jit(solution)/shard_map/ppermute | solution.py:295
  22.6 0.5 collective-permute-start.6
  23.1 1.5 collective-permute-start.5
  24.6 0.9 collective-permute-done.4.refs_3_
  25.6 1.6 %copy-done.16 = bf16[1600,625]{1,0:T(8,128)(2,1)S(1)} copy-done((bf16[1600,625]{1,0:T(8,128)(2,1)S(1)}, bf16[1600,625]{1,0:T(8,128)(2,1)}, u32[]{:S(2)}) %copy-start.16) | copy-done | bytes 2000024
  27.1 2.6 %shard_map.82.refs_0_ = bf16[2,1600,384]{2,1,0:T(8,128)(2,1)S(1)} custom-call(s32[1]{0:T(128)} %bitcast.column_ref, bf16[2,96,625]{2,1,0:T(8,128)(2,1)S(1)} %get-tuple-element.41.refs_0_, bf16[2,96,625]{2,1,0:T(8,128)(2,1)S(1)} %collective-permute-done.refs_1_, bf16[2,96,625]{2,1,0:T(8,128)(2,1)S(1)} %collective-permute-done.1.refs_2_, ...), custom_call_target="tpu_custom_call" | custom-call | flops 1536000000 | bytes 3417600 | tf_op jit(solution)/shard_map/pallas_call | solution.py:73
  29.8 1.2 collective-permute-done.6.refs_2_
  31.1 0.2 collective-permute-start.13
  31.3 1.1 collective-permute-start.9
  32.3 1.0 collective-permute-start.12
  33.4 0.3 collective-permute-start.11
  33.7 1.9 %collective-permute-start.10 = (bf16[2,96,625]{2,1,0:T(8,128)(2,1)S(1)}, bf16[2,96,625]{2,1,0:T(8,128)(2,1)S(1)}, u32[]{:S(2)}, u32[]{:S(2)}) collective-permute-start(bf16[2,96,625]{2,1,0:T(8,128)(2,1)S(1)} %collective-permute-done.7.refs_0_), channel_id=1, source_target_pairs={{0,8},{1,17},{2,10},{3,19},{4,12},{5,21},{6,14},{7,23},{8,0},{9,25... | collective-permute-start | bytes 720008 | tf_op jit(solution)/shard_map/ppermute | solution.py:305
  35.7 2.9 %collective-permute-done.9.refs_3_ = bf16[2,96,625]{2,1,0:T(8,128)(2,1)S(1)} collective-permute-done((bf16[2,96,625]{2,1,0:T(8,128)(2,1)S(1)}, bf16[2,96,625]{2,1,0:T(8,128)(2,1)S(1)}, u32[]{:S(2)}, u32[]{:S(2)}) %collective-permute-start.9) | collective-permute-done | bytes 240032 | tf_op jit(solution)/shard_map/ppermute | solution.py:306
  38.6 2.6 %shard_map.83.refs_2_ = bf16[2,1600,384]{2,1,0:T(8,128)(2,1)S(1)} custom-call(s32[1]{0:T(128)} %bitcast.column_ref, bf16[2,96,625]{2,1,0:T(8,128)(2,1)S(1)} %collective-permute-done.2.refs_0_, bf16[2,96,625]{2,1,0:T(8,128)(2,1)S(1)} %collective-permute-done.5.refs_1_, bf16[2,96,625]{2,1,0:T(8,128)(2,1)S(1)} %collective-permute-done.6.refs_2_, ...), custom_call_target="tpu_custom_call" | custom-call | flops 1536000000 | bytes 3417600 | tf_op jit(solution)/shard_map/pallas_call | solution.py:73
  41.3 5.3 %collective-permute-done.12.refs_0_ = bf16[2,96,625]{2,1,0:T(8,128)(2,1)S(1)} collective-permute-done((bf16[2,96,625]{2,1,0:T(8,128)(2,1)S(1)}, bf16[2,96,625]{2,1,0:T(8,128)(2,1)S(1)}, u32[]{:S(2)}, u32[]{:S(2)}) %collective-permute-start.12) | collective-permute-done | bytes 240032 | tf_op jit(solution)/shard_map/ppermute | solution.py:295
  46.5 0.1 collective-permute-start.18
  46.7 1.6 %collective-permute-start.14 = (bf16[2,96,625]{2,1,0:T(8,128)(2,1)S(1)}, bf16[2,96,625]{2,1,0:T(8,128)(2,1)S(1)}, u32[]{:S(2)}, u32[]{:S(2)}) collective-permute-start(bf16[2,96,625]{2,1,0:T(8,128)(2,1)S(1)} %collective-permute-done.10.refs_1_), channel_id=1, source_target_pairs={{0,16},{1,9},{2,18},{3,11},{4,20},{5,13},{6,22},{7,15},{8,24},{9,1... | collective-permute-start | bytes 720008 | tf_op jit(solution)/shard_map/ppermute | solution.py:306
  48.2 0.5 collective-permute-start.16
  48.7 0.6 collective-permute-start.15
  49.3 5.3 %collective-permute-done.14.refs_3_ = bf16[2,96,625]{2,1,0:T(8,128)(2,1)S(1)} collective-permute-done((bf16[2,96,625]{2,1,0:T(8,128)(2,1)S(1)}, bf16[2,96,625]{2,1,0:T(8,128)(2,1)S(1)}, u32[]{:S(2)}, u32[]{:S(2)}) %collective-permute-start.14) | collective-permute-done | bytes 240032 | tf_op jit(solution)/shard_map/ppermute | solution.py:306
  54.6 2.6 %shard_map.84.refs_6_ = bf16[2,1600,384]{2,1,0:T(8,128)(2,1)S(1)} custom-call(s32[1]{0:T(128)} %bitcast.column_ref, bf16[2,96,625]{2,1,0:T(8,128)(2,1)S(1)} %collective-permute-done.7.refs_0_, bf16[2,96,625]{2,1,0:T(8,128)(2,1)S(1)} %collective-permute-done.10.refs_1_, bf16[2,96,625]{2,1,0:T(8,128)(2,1)S(1)} %collective-permute-done.11.refs_2_, ...), custom_call_target="tpu_custom_call" | custom-call | flops 1536000000 | bytes 3417600 | tf_op jit(solution)/shard_map/pallas_call | solution.py:73
  57.2 0.0 copy-start.21
  57.2 0.0 copy-start.22
  57.3 0.0 copy-start.5
  57.3 0.9 collective-permute-done.16.refs_2_
  58.1 0.8 collective-permute-done.17.refs_2_
  59.0 1.5 collective-permute-start.19
  60.5 0.2 collective-permute-start.22
  60.6 0.4 collective-permute-start.23
  61.0 4.3 %collective-permute-done.19.refs_3_ = bf16[2,96,625]{2,1,0:T(8,128)(2,1)S(1)} collective-permute-done((bf16[2,96,625]{2,1,0:T(8,128)(2,1)S(1)}, bf16[2,96,625]{2,1,0:T(8,128)(2,1)S(1)}, u32[]{:S(2)}, u32[]{:S(2)}) %collective-permute-start.19) | collective-permute-done | bytes 240032 | tf_op jit(solution)/shard_map/ppermute | solution.py:306
  65.3 3.4 %shard_map.85.refs_4_ = bf16[2,1600,384]{2,1,0:T(8,128)(2,1)} custom-call(s32[1]{0:T(128)} %bitcast.column_ref, bf16[2,96,625]{2,1,0:T(8,128)(2,1)S(1)} %collective-permute-done.12.refs_0_, bf16[2,96,625]{2,1,0:T(8,128)(2,1)S(1)} %collective-permute-done.15.refs_1_, bf16[2,96,625]{2,1,0:T(8,128)(2,1)S(1)} %collective-permute-done.16.refs_2_, ...), custom_call_target="tpu_custom_call" | custom-call | flops 1536000000 | bytes 3417600 | tf_op jit(solution)/shard_map/pallas_call | solution.py:73
  68.7 0.7 copy-done.12
  69.4 0.7 copy-done.14
  70.2 2.4 %collective-permute-done.20.refs_3_ = bf16[625,256]{1,0:T(8,128)(2,1)} collective-permute-done((bf16[625,256]{1,0:T(8,128)(2,1)S(1)}, bf16[625,256]{1,0:T(8,128)(2,1)}, u32[]{:S(2)}, u32[]{:S(2)}) %collective-permute-start.20) | collective-permute-done | bytes 320032 | tf_op jit(solution)/shard_map/ppermute | solution.py:295
  72.6 0.5 collective-permute-start.25
  73.1 0.7 copy.24.owners_ref
  73.8 0.7 copy.25.local_ref
  74.5 1.0 copy-done.7
  75.4 1.0 copy-done.11
  76.4 2.6 %shard_map.86.refs_8_ = bf16[8,800,128]{2,1,0:T(8,128)(2,1)S(1)} custom-call(bf16[800,625]{1,0:T(8,128)(2,1)S(1)} %copy-done.5, bf16[625,256]{1,0:T(8,128)(2,1)S(1)} %bitcast.26, bf16[625,256]{1,0:T(8,128)(2,1)} %collective-permute-done.3.refs_1_, bf16[625,256]{1,0:T(8,128)(2,1)S(1)} %copy-done.11, bf16[625,256]{1,0:T(8,128)(2,1)} %collective-permute-done.20.refs_3_), custom_call_target="tpu_custom_call" | custom-call | flops 1024000000 | bytes 2560000 | tf_op jit(solution)/shard_map/pallas_call | solution.py:104
  79.0 1.2 copy-done
  80.2 1.0 copy-done.9
  81.1 1.4 shard_map.87.refs_9_
  82.6 1.2 copy-done.1
  83.8 12.2 %shard_map.88 = bf16[1,2,625,128]{3,2,1,0:T(8,128)(2,1)} custom-call(s32[1]{0:T(128)} %bitcast.column_ref, s32[32,3]{1,0:T(8,128)} %copy.24.owners_ref, s32[32,4]{1,0:T(8,128)} %copy.25.local_ref, bf16[2,1600,384]{2,1,0:T(8,128)(2,1)} %copy-done.2, bf16[2,1600,384]{2,1,0:T(8,128)(2,1)} %collective-permute-done.13.refs_1_, bf16[2,1600,384]{2,1,0:T(8,128)(2,1)} %copy-done.3, ...), custom_call_target="tpu_custom_call" | custom-call | flops 2936012800 | bytes 6553600 | tf_op jit(solution)/shard_map/pallas_call | solution.py:258
  96.0 12.2 %shard_map.89 = bf16[1,2,625,128]{3,2,1,0:T(8,128)(2,1)} custom-call(s32[1]{0:T(128)} %bitcast.column_ref, s32[32,3]{1,0:T(8,128)} %copy.24.owners_ref, s32[32,4]{1,0:T(8,128)} %copy.25.local_ref, bf16[2,1600,384]{2,1,0:T(8,128)(2,1)} %copy-done.2, bf16[2,1600,384]{2,1,0:T(8,128)(2,1)} %collective-permute-done.13.refs_1_, bf16[2,1600,384]{2,1,0:T(8,128)(2,1)} %copy-done.3, ...), custom_call_target="tpu_custom_call" | custom-call | flops 2936012800 | bytes 6553600 | tf_op jit(solution)/shard_map/pallas_call | solution.py:258
  108.2 12.3 %shard_map.90 = bf16[1,2,625,128]{3,2,1,0:T(8,128)(2,1)} custom-call(s32[1]{0:T(128)} %bitcast.column_ref, s32[32,3]{1,0:T(8,128)} %copy.24.owners_ref, s32[32,4]{1,0:T(8,128)} %copy.25.local_ref, bf16[2,1600,384]{2,1,0:T(8,128)(2,1)} %copy-done.2, bf16[2,1600,384]{2,1,0:T(8,128)(2,1)} %collective-permute-done.13.refs_1_, bf16[2,1600,384]{2,1,0:T(8,128)(2,1)} %copy-done.3, ...), custom_call_target="tpu_custom_call" | custom-call | flops 2936012800 | bytes 6553600 | tf_op jit(solution)/shard_map/pallas_call | solution.py:258
  120.4 0.1 collective-permute-start.28
  120.5 3.8 %collective-permute-start.27 = (bf16[2,625,128]{2,1,0:T(8,128)(2,1)S(1)}, bf16[2,625,128]{2,1,0:T(8,128)(2,1)S(1)}, u32[]{:S(2)}, u32[]{:S(2)}) collective-permute-start(bf16[2,625,128]{2,1,0:T(8,128)(2,1)S(1)} %bitcast.30), channel_id=1, source_target_pairs={{0,6},{1,7},{2,0},{3,1},{4,2},{5,3},{6,4},{7,5},{8,14},{9,15},{10,... | collective-permute-start | bytes 960008 | tf_op jit(solution)/shard_map/ppermute | solution.py:295
  124.3 12.3 %shard_map.91 = bf16[1,2,625,128]{3,2,1,0:T(8,128)(2,1)} custom-call(s32[1]{0:T(128)} %bitcast.column_ref, s32[32,3]{1,0:T(8,128)} %copy.24.owners_ref, s32[32,4]{1,0:T(8,128)} %copy.25.local_ref, bf16[2,1600,384]{2,1,0:T(8,128)(2,1)} %copy-done.2, bf16[2,1600,384]{2,1,0:T(8,128)(2,1)} %collective-permute-done.13.refs_1_, bf16[2,1600,384]{2,1,0:T(8,128)(2,1)} %copy-done.3, ...), custom_call_target="tpu_custom_call" | custom-call | flops 2936012800 | bytes 6553600 | tf_op jit(solution)/shard_map/pallas_call | solution.py:258
  136.6 4.5 %collective-permute-done.27 = bf16[2,625,128]{2,1,0:T(8,128)(2,1)S(1)} collective-permute-done((bf16[2,625,128]{2,1,0:T(8,128)(2,1)S(1)}, bf16[2,625,128]{2,1,0:T(8,128)(2,1)S(1)}, u32[]{:S(2)}, u32[]{:S(2)}) %collective-permute-start.27) | collective-permute-done | bytes 320032 | tf_op jit(solution)/shard_map/ppermute | solution.py:295
  141.1 7.8 %collective-permute-done.26 = bf16[2,625,128]{2,1,0:T(8,128)(2,1)S(1)} collective-permute-done((bf16[2,625,128]{2,1,0:T(8,128)(2,1)S(1)}, bf16[2,625,128]{2,1,0:T(8,128)(2,1)S(1)}, u32[]{:S(2)}, u32[]{:S(2)}) %collective-permute-start.26) | collective-permute-done | bytes 320032 | tf_op jit(solution)/shard_map/ppermute | solution.py:295
  148.9 1.2 fusion.1
  150.1 1.2 copy.33
  (58 shorter events, 0.2 us)
Async XLA Ops:
  1.3 28.5 %copy-start.6 = (bf16[79,8,2,128]{3,1,2,0:T(8,128)(2,1)}, bf16[79,8,2,128]{3,1,2,0:T(8,128)(2,1)S(1)}, u32[]{:S(2)}) copy-start(bf16[79,8,2,128]{3,1,2,0:T(8,128)(2,1)S(1)} %copy.34) | copy-start | bytes 970756
  1.3 18.0 %collective-permute-start.3 = (bf16[625,256]{1,0:T(8,128)(2,1)S(1)}, bf16[625,256]{1,0:T(8,128)(2,1)}, u32[]{:S(2)}, u32[]{:S(2)}) collective-permute-start(bf16[625,256]{1,0:T(8,128)(2,1)S(1)} %bitcast.24), channel_id=1, source_target_pairs={{0,2},{1,3},{2,4},{3,5},{4,6},{5,7},{6,0},{7,1},{8,10},{9,11},{10,... | collective-permute-start | bytes 960008 | tf_op jit(solution)/shard_map/ppermute | solution.py:295
  7.9 11.4 %collective-permute-start.2 = (bf16[2,96,625]{2,1,0:T(8,128)(2,1)S(1)}, bf16[2,96,625]{2,1,0:T(8,128)(2,1)S(1)}, u32[]{:S(2)}, u32[]{:S(2)}) collective-permute-start(bf16[2,96,625]{2,1,0:T(8,128)(2,1)S(1)} %get-tuple-element.79), channel_id=1, source_target_pairs={{0,2},{1,3},{2,4},{3,5},{4,6},{5,7},{6,0},{7,1},{8,10},{9,11},{10,... | collective-permute-start | bytes 720008 | tf_op jit(solution)/shard_map/ppermute | solution.py:295
  9.5 9.8 %collective-permute-start.1 = (bf16[2,96,625]{2,1,0:T(8,128)(2,1)S(1)}, bf16[2,96,625]{2,1,0:T(8,128)(2,1)S(1)}, u32[]{:S(2)}, u32[]{:S(2)}) collective-permute-start(bf16[2,96,625]{2,1,0:T(8,128)(2,1)S(1)} %get-tuple-element.41.refs_0_), channel_id=1, source_target_pairs={{0,16},{1,9},{2,18},{3,11},{4,20},{5,13},{6,22},{7,15},{8,24},{9,1... | collective-permute-start | bytes 720008 | tf_op jit(solution)/shard_map/ppermute | solution.py:306
  11.0 8.3 %collective-permute-start = (bf16[2,96,625]{2,1,0:T(8,128)(2,1)S(1)}, bf16[2,96,625]{2,1,0:T(8,128)(2,1)S(1)}, u32[]{:S(2)}, u32[]{:S(2)}) collective-permute-start(bf16[2,96,625]{2,1,0:T(8,128)(2,1)S(1)} %get-tuple-element.41.refs_0_), channel_id=1, source_target_pairs={{0,8},{1,17},{2,10},{3,19},{4,12},{5,21},{6,14},{7,23},{8,0},{9,25... | collective-permute-start | bytes 720008 | tf_op jit(solution)/shard_map/ppermute | solution.py:305
  19.3 6.3 %collective-permute-start.4 = (bf16[2,96,625]{2,1,0:T(8,128)(2,1)S(1)}, bf16[2,96,625]{2,1,0:T(8,128)(2,1)S(1)}, u32[]{:S(2)}, u32[]{:S(2)}) collective-permute-start(bf16[2,96,625]{2,1,0:T(8,128)(2,1)S(1)} %collective-permute-done.refs_1_), channel_id=1, source_target_pairs={{0,16},{1,9},{2,18},{3,11},{4,20},{5,13},{6,22},{7,15},{8,24},{9,1... | collective-permute-start | bytes 720008 | tf_op jit(solution)/shard_map/ppermute | solution.py:306
  20.9 10.2 %collective-permute-start.8 = (bf16[625,256]{1,0:T(8,128)(2,1)S(1)}, bf16[625,256]{1,0:T(8,128)(2,1)S(1)}, u32[]{:S(2)}, u32[]{:S(2)}) collective-permute-start(bf16[625,256]{1,0:T(8,128)(2,1)S(1)} %bitcast.25), channel_id=1, source_target_pairs={{0,1},{1,0},{2,3},{3,2},{4,5},{5,4},{6,7},{7,6},{8,9},{9,8},{10,11... | collective-permute-start | bytes 960008 | tf_op jit(solution)/shard_map/ppermute | solution.py:292
  20.9 8.9 %collective-permute-start.7 = (bf16[2,96,625]{2,1,0:T(8,128)(2,1)S(1)}, bf16[2,96,625]{2,1,0:T(8,128)(2,1)S(1)}, u32[]{:S(2)}, u32[]{:S(2)}) collective-permute-start(bf16[2,96,625]{2,1,0:T(8,128)(2,1)S(1)} %get-tuple-element.45), channel_id=1, source_target_pairs={{0,6},{1,7},{2,0},{3,1},{4,2},{5,3},{6,4},{7,5},{8,14},{9,15},{10,... | collective-permute-start | bytes 720008 | tf_op jit(solution)/shard_map/ppermute | solution.py:295
  22.6 8.4 %collective-permute-start.6 = (bf16[2,96,625]{2,1,0:T(8,128)(2,1)S(1)}, bf16[2,96,625]{2,1,0:T(8,128)(2,1)S(1)}, u32[]{:S(2)}, u32[]{:S(2)}) collective-permute-start(bf16[2,96,625]{2,1,0:T(8,128)(2,1)S(1)} %collective-permute-done.2.refs_0_), channel_id=1, source_target_pairs={{0,16},{1,9},{2,18},{3,11},{4,20},{5,13},{6,22},{7,15},{8,24},{9,1... | collective-permute-start | bytes 720008 | tf_op jit(solution)/shard_map/ppermute | solution.py:306
  23.1 7.9 %collective-permute-start.5 = (bf16[2,96,625]{2,1,0:T(8,128)(2,1)S(1)}, bf16[2,96,625]{2,1,0:T(8,128)(2,1)S(1)}, u32[]{:S(2)}, u32[]{:S(2)}) collective-permute-start(bf16[2,96,625]{2,1,0:T(8,128)(2,1)S(1)} %collective-permute-done.2.refs_0_), channel_id=1, source_target_pairs={{0,8},{1,17},{2,10},{3,19},{4,12},{5,21},{6,14},{7,23},{8,0},{9,25... | collective-permute-start | bytes 720008 | tf_op jit(solution)/shard_map/ppermute | solution.py:305
  25.6 1.6 %copy-start.16 = (bf16[1600,625]{1,0:T(8,128)(2,1)S(1)}, bf16[1600,625]{1,0:T(8,128)(2,1)}, u32[]{:S(2)}) copy-start(bf16[1600,625]{1,0:T(8,128)(2,1)} %constant.59.clone.refs_4_) | copy-start | bytes 6000004
  27.1 11.5 %copy-start.17 = (bf16[1600,625]{1,0:T(8,128)(2,1)S(1)}, bf16[1600,625]{1,0:T(8,128)(2,1)}, u32[]{:S(2)}) copy-start(bf16[1600,625]{1,0:T(8,128)(2,1)} %constant.59.clone.refs_4_) | copy-start | bytes 6000004
  29.8 11.4 %copy-start.2 = (bf16[2,1600,384]{2,1,0:T(8,128)(2,1)}, bf16[2,1600,384]{2,1,0:T(8,128)(2,1)S(1)}, u32[]{:S(2)}) copy-start(bf16[2,1600,384]{2,1,0:T(8,128)(2,1)S(1)} %shard_map.82.refs_0_) | copy-start | bytes 7372804
  31.1 10.2 %copy-start.8 = (bf16[625,256]{1,0:T(8,128)(2,1)}, bf16[625,256]{1,0:T(8,128)(2,1)S(1)}, u32[]{:S(2)}) copy-start(bf16[625,256]{1,0:T(8,128)(2,1)S(1)} %collective-permute-done.8.refs_0_) | copy-start | bytes 960004
  31.1 15.5 %collective-permute-start.13 = (bf16[2,1600,384]{2,1,0:T(8,128)(2,1)S(1)}, bf16[2,1600,384]{2,1,0:T(8,128)(2,1)}, u32[]{:S(2)}, u32[]{:S(2)}) collective-permute-start(bf16[2,1600,384]{2,1,0:T(8,128)(2,1)S(1)} %shard_map.82.refs_0_), channel_id=1, source_target_pairs={{0,1},{1,0},{2,3},{3,2},{4,5},{5,4},{6,7},{7,6},{8,9},{9,8},{10,11... | collective-permute-start | bytes 7372808 | tf_op jit(solution)/shard_map/ppermute | solution.py:292
  31.3 7.3 %collective-permute-start.9 = (bf16[2,96,625]{2,1,0:T(8,128)(2,1)S(1)}, bf16[2,96,625]{2,1,0:T(8,128)(2,1)S(1)}, u32[]{:S(2)}, u32[]{:S(2)}) collective-permute-start(bf16[2,96,625]{2,1,0:T(8,128)(2,1)S(1)} %collective-permute-done.5.refs_1_), channel_id=1, source_target_pairs={{0,16},{1,9},{2,18},{3,11},{4,20},{5,13},{6,22},{7,15},{8,24},{9,1... | collective-permute-start | bytes 720008 | tf_op jit(solution)/shard_map/ppermute | solution.py:306
  32.3 14.2 %collective-permute-start.12 = (bf16[2,96,625]{2,1,0:T(8,128)(2,1)S(1)}, bf16[2,96,625]{2,1,0:T(8,128)(2,1)S(1)}, u32[]{:S(2)}, u32[]{:S(2)}) collective-permute-start(bf16[2,96,625]{2,1,0:T(8,128)(2,1)S(1)} %get-tuple-element.52), channel_id=1, source_target_pairs={{0,4},{1,5},{2,6},{3,7},{4,0},{5,1},{6,2},{7,3},{8,12},{9,13},{10,... | collective-permute-start | bytes 720008 | tf_op jit(solution)/shard_map/ppermute | solution.py:295
  33.4 13.1 %collective-permute-start.11 = (bf16[2,96,625]{2,1,0:T(8,128)(2,1)S(1)}, bf16[2,96,625]{2,1,0:T(8,128)(2,1)S(1)}, u32[]{:S(2)}, u32[]{:S(2)}) collective-permute-start(bf16[2,96,625]{2,1,0:T(8,128)(2,1)S(1)} %collective-permute-done.7.refs_0_), channel_id=1, source_target_pairs={{0,16},{1,9},{2,18},{3,11},{4,20},{5,13},{6,22},{7,15},{8,24},{9,1... | collective-permute-start | bytes 720008 | tf_op jit(solution)/shard_map/ppermute | solution.py:306
  33.7 12.8 %collective-permute-start.10 = (bf16[2,96,625]{2,1,0:T(8,128)(2,1)S(1)}, bf16[2,96,625]{2,1,0:T(8,128)(2,1)S(1)}, u32[]{:S(2)}, u32[]{:S(2)}) collective-permute-start(bf16[2,96,625]{2,1,0:T(8,128)(2,1)S(1)} %collective-permute-done.7.refs_0_), channel_id=1, source_target_pairs={{0,8},{1,17},{2,10},{3,19},{4,12},{5,21},{6,14},{7,23},{8,0},{9,25... | collective-permute-start | bytes 720008 | tf_op jit(solution)/shard_map/ppermute | solution.py:305
  41.2 16.0 %copy-start.3 = (bf16[2,1600,384]{2,1,0:T(8,128)(2,1)}, bf16[2,1600,384]{2,1,0:T(8,128)(2,1)S(1)}, u32[]{:S(2)}) copy-start(bf16[2,1600,384]{2,1,0:T(8,128)(2,1)S(1)} %shard_map.83.refs_2_) | copy-start | bytes 7372804
  46.5 12.5 %collective-permute-start.18 = (bf16[2,1600,384]{2,1,0:T(8,128)(2,1)S(1)}, bf16[2,1600,384]{2,1,0:T(8,128)(2,1)}, u32[]{:S(2)}, u32[]{:S(2)}) collective-permute-start(bf16[2,1600,384]{2,1,0:T(8,128)(2,1)S(1)} %shard_map.83.refs_2_), channel_id=1, source_target_pairs={{0,1},{1,0},{2,3},{3,2},{4,5},{5,4},{6,7},{7,6},{8,9},{9,8},{10,11... | collective-permute-start | bytes 7372808 | tf_op jit(solution)/shard_map/ppermute | solution.py:292
  46.7 7.9 %collective-permute-start.14 = (bf16[2,96,625]{2,1,0:T(8,128)(2,1)S(1)}, bf16[2,96,625]{2,1,0:T(8,128)(2,1)S(1)}, u32[]{:S(2)}, u32[]{:S(2)}) collective-permute-start(bf16[2,96,625]{2,1,0:T(8,128)(2,1)S(1)} %collective-permute-done.10.refs_1_), channel_id=1, source_target_pairs={{0,16},{1,9},{2,18},{3,11},{4,20},{5,13},{6,22},{7,15},{8,24},{9,1... | collective-permute-start | bytes 720008 | tf_op jit(solution)/shard_map/ppermute | solution.py:306
  48.2 10.8 %collective-permute-start.17 = (bf16[625,256]{1,0:T(8,128)(2,1)}, bf16[625,256]{1,0:T(8,128)(2,1)S(1)}, u32[]{:S(2)}, u32[]{:S(2)}) collective-permute-start(bf16[625,256]{1,0:T(8,128)(2,1)} %collective-permute-done.3.refs_1_), channel_id=1, source_target_pairs={{0,2},{1,3},{2,4},{3,5},{4,6},{5,7},{6,0},{7,1},{8,10},{9,11},{10,... | collective-permute-start | bytes 960008 | tf_op jit(solution)/shard_map/ppermute | solution.py:295
  48.2 9.9 %collective-permute-start.16 = (bf16[2,96,625]{2,1,0:T(8,128)(2,1)S(1)}, bf16[2,96,625]{2,1,0:T(8,128)(2,1)S(1)}, u32[]{:S(2)}, u32[]{:S(2)}) collective-permute-start(bf16[2,96,625]{2,1,0:T(8,128)(2,1)S(1)} %collective-permute-done.12.refs_0_), channel_id=1, source_target_pairs={{0,16},{1,9},{2,18},{3,11},{4,20},{5,13},{6,22},{7,15},{8,24},{9,1... | collective-permute-start | bytes 720008 | tf_op jit(solution)/shard_map/ppermute | solution.py:306
  48.7 9.4 %collective-permute-start.15 = (bf16[2,96,625]{2,1,0:T(8,128)(2,1)S(1)}, bf16[2,96,625]{2,1,0:T(8,128)(2,1)S(1)}, u32[]{:S(2)}, u32[]{:S(2)}) collective-permute-start(bf16[2,96,625]{2,1,0:T(8,128)(2,1)S(1)} %collective-permute-done.12.refs_0_), channel_id=1, source_target_pairs={{0,8},{1,17},{2,10},{3,19},{4,12},{5,21},{6,14},{7,23},{8,0},{9,25... | collective-permute-start | bytes 720008 | tf_op jit(solution)/shard_map/ppermute | solution.py:305
  57.2 11.5 %copy-start.4 = (bf16[2,1600,384]{2,1,0:T(8,128)(2,1)}, bf16[2,1600,384]{2,1,0:T(8,128)(2,1)S(1)}, u32[]{:S(2)}) copy-start(bf16[2,1600,384]{2,1,0:T(8,128)(2,1)S(1)} %shard_map.84.refs_6_) | copy-start | bytes 7372804
  57.2 15.8 %copy-start.21 = (s32[32,3]{0,1:T(4,128)S(1)}, s32[32,3]{0,1:T(4,128)}, u32[]{:S(2)}) copy-start(s32[32,3]{0,1:T(4,128)} %param.11) | copy-start | bytes 1156
  57.2 16.5 %copy-start.22 = (s32[32,4]{0,1:T(4,128)S(1)}, s32[32,4]{0,1:T(4,128)}, u32[]{:S(2)}) copy-start(s32[32,4]{0,1:T(4,128)} %param.12) | copy-start | bytes 1540
  57.3 17.2 %copy-start.5 = (bf16[800,625]{1,0:T(8,128)(2,1)S(1)}, bf16[800,625]{1,0:T(8,128)(2,1)}, u32[]{:S(2)}) copy-start(bf16[800,625]{1,0:T(8,128)(2,1)} %constant.60.clone.matrix_ref) | copy-start | bytes 3000004
  59.0 9.7 %copy-start.10 = (bf16[625,256]{1,0:T(8,128)(2,1)}, bf16[625,256]{1,0:T(8,128)(2,1)S(1)}, u32[]{:S(2)}) copy-start(bf16[625,256]{1,0:T(8,128)(2,1)S(1)} %collective-permute-done.17.refs_2_) | copy-start | bytes 960004
  59.0 13.6 %collective-permute-start.21 = (bf16[2,1600,384]{2,1,0:T(8,128)(2,1)S(1)}, bf16[2,1600,384]{2,1,0:T(8,128)(2,1)}, u32[]{:S(2)}, u32[]{:S(2)}) collective-permute-start(bf16[2,1600,384]{2,1,0:T(8,128)(2,1)S(1)} %shard_map.84.refs_6_), channel_id=1, source_target_pairs={{0,1},{1,0},{2,3},{3,2},{4,5},{5,4},{6,7},{7,6},{8,9},{9,8},{10,11... | collective-permute-start | bytes 7372808 | tf_op jit(solution)/shard_map/ppermute | solution.py:292
  59.0 6.3 %collective-permute-start.19 = (bf16[2,96,625]{2,1,0:T(8,128)(2,1)S(1)}, bf16[2,96,625]{2,1,0:T(8,128)(2,1)S(1)}, u32[]{:S(2)}, u32[]{:S(2)}) collective-permute-start(bf16[2,96,625]{2,1,0:T(8,128)(2,1)S(1)} %collective-permute-done.15.refs_1_), channel_id=1, source_target_pairs={{0,16},{1,9},{2,18},{3,11},{4,20},{5,13},{6,22},{7,15},{8,24},{9,1... | collective-permute-start | bytes 720008 | tf_op jit(solution)/shard_map/ppermute | solution.py:306
  60.5 8.2 %collective-permute-start.22 = (bf16[625,256]{1,0:T(8,128)(2,1)}, bf16[625,256]{1,0:T(8,128)(2,1)S(1)}, u32[]{:S(2)}, u32[]{:S(2)}) collective-permute-start(bf16[625,256]{1,0:T(8,128)(2,1)} %collective-permute-done.3.refs_1_), channel_id=1, source_target_pairs={{0,1},{1,0},{2,3},{3,2},{4,5},{5,4},{6,7},{7,6},{8,9},{9,8},{10,11... | collective-permute-start | bytes 960008 | tf_op jit(solution)/shard_map/ppermute | solution.py:292
  60.6 8.8 %collective-permute-start.23 = (bf16[625,256]{1,0:T(8,128)(2,1)S(1)}, bf16[625,256]{1,0:T(8,128)(2,1)S(1)}, u32[]{:S(2)}, u32[]{:S(2)}) collective-permute-start(bf16[625,256]{1,0:T(8,128)(2,1)S(1)} %collective-permute-done.17.refs_2_), channel_id=1, source_target_pairs={{0,1},{1,0},{2,3},{3,2},{4,5},{5,4},{6,7},{7,6},{8,9},{9,8},{10,11... | collective-permute-start | bytes 960008 | tf_op jit(solution)/shard_map/ppermute | solution.py:292
  61.0 11.6 %collective-permute-start.20 = (bf16[625,256]{1,0:T(8,128)(2,1)S(1)}, bf16[625,256]{1,0:T(8,128)(2,1)}, u32[]{:S(2)}, u32[]{:S(2)}) collective-permute-start(bf16[625,256]{1,0:T(8,128)(2,1)S(1)} %collective-permute-done.17.refs_2_), channel_id=1, source_target_pairs={{0,2},{1,3},{2,4},{3,5},{4,6},{5,7},{6,0},{7,1},{8,10},{9,11},{10,... | collective-permute-start | bytes 960008 | tf_op jit(solution)/shard_map/ppermute | solution.py:295
  68.7 0.7 copy-start.12
  69.4 0.7 copy-start.14
  72.6 11.2 %collective-permute-start.24 = (bf16[2,1600,384]{2,1,0:T(8,128)(2,1)}, bf16[2,1600,384]{2,1,0:T(8,128)(2,1)}, u32[]{:S(2)}, u32[]{:S(2)}) collective-permute-start(bf16[2,1600,384]{2,1,0:T(8,128)(2,1)} %shard_map.85.refs_4_), channel_id=1, source_target_pairs={{0,1},{1,0},{2,3},{3,2},{4,5},{5,4},{6,7},{7,6},{8,9},{9,8},{10,11... | collective-permute-start | bytes 7372808 | tf_op jit(solution)/shard_map/ppermute | solution.py:292
  72.6 7.6 %collective-permute-start.25 = (bf16[625,256]{1,0:T(8,128)(2,1)}, bf16[625,256]{1,0:T(8,128)(2,1)S(1)}, u32[]{:S(2)}, u32[]{:S(2)}) collective-permute-start(bf16[625,256]{1,0:T(8,128)(2,1)} %collective-permute-done.20.refs_3_), channel_id=1, source_target_pairs={{0,1},{1,0},{2,3},{3,2},{4,5},{5,4},{6,7},{7,6},{8,9},{9,8},{10,11... | collective-permute-start | bytes 960008 | tf_op jit(solution)/shard_map/ppermute | solution.py:292
  74.5 1.0 copy-start.7
  75.4 1.0 copy-start.11
  76.4 3.8 %copy-start.13 = (bf16[625,256]{1,0:T(8,128)(2,1)S(1)}, bf16[625,256]{1,0:T(8,128)(2,1)}, u32[]{:S(2)}) copy-start(bf16[625,256]{1,0:T(8,128)(2,1)} %copy-done.12) | copy-start | bytes 960004
  76.4 3.8 %copy-start.15 = (bf16[625,256]{1,0:T(8,128)(2,1)S(1)}, bf16[625,256]{1,0:T(8,128)(2,1)}, u32[]{:S(2)}) copy-start(bf16[625,256]{1,0:T(8,128)(2,1)} %copy-done.14) | copy-start | bytes 960004
  79.0 1.2 copy-start
  80.2 1.0 copy-start.9
  82.6 1.2 copy-start.1
  108.1 12.4 %copy-start.20 = (bf16[1,2,625,128]{3,2,1,0:T(8,128)(2,1)S(1)}, bf16[1,2,625,128]{3,2,1,0:T(8,128)(2,1)}, u32[]{:S(2)}) copy-start(bf16[1,2,625,128]{3,2,1,0:T(8,128)(2,1)} %shard_map.89) | copy-start | bytes 960004
  108.2 16.2 %copy-start.19 = (bf16[1,2,625,128]{3,2,1,0:T(8,128)(2,1)S(1)}, bf16[1,2,625,128]{3,2,1,0:T(8,128)(2,1)}, u32[]{:S(2)}) copy-start(bf16[1,2,625,128]{3,2,1,0:T(8,128)(2,1)} %shard_map.88) | copy-start | bytes 960004
  120.4 16.2 %collective-permute-start.28 = (bf16[2,625,128]{2,1,0:T(8,128)(2,1)}, bf16[2,625,128]{2,1,0:T(8,128)(2,1)S(1)}, u32[]{:S(2)}, u32[]{:S(2)}) collective-permute-start(bf16[2,625,128]{2,1,0:T(8,128)(2,1)} %bitcast.31), channel_id=1, source_target_pairs={{0,2},{1,3},{2,4},{3,5},{4,6},{5,7},{6,0},{7,1},{8,10},{9,11},{10,... | collective-permute-start | bytes 960008 | tf_op jit(solution)/shard_map/ppermute | solution.py:295
  120.5 20.6 %collective-permute-start.27 = (bf16[2,625,128]{2,1,0:T(8,128)(2,1)S(1)}, bf16[2,625,128]{2,1,0:T(8,128)(2,1)S(1)}, u32[]{:S(2)}, u32[]{:S(2)}) collective-permute-start(bf16[2,625,128]{2,1,0:T(8,128)(2,1)S(1)} %bitcast.30), channel_id=1, source_target_pairs={{0,6},{1,7},{2,0},{3,1},{4,2},{5,3},{6,4},{7,5},{8,14},{9,15},{10,... | collective-permute-start | bytes 960008 | tf_op jit(solution)/shard_map/ppermute | solution.py:295
  124.3 24.6 %copy-start.18 = (f32[2,128,625]{1,0,2:T(2,128)S(1)}, f32[2,128,625]{1,0,2:T(2,128)}, u32[]{:S(2)}) copy-start(f32[2,128,625]{1,0,2:T(2,128)} %param.10) | copy-start | bytes 1920004
  124.3 24.6 %collective-permute-start.26 = (bf16[2,625,128]{2,1,0:T(8,128)(2,1)S(1)}, bf16[2,625,128]{2,1,0:T(8,128)(2,1)S(1)}, u32[]{:S(2)}, u32[]{:S(2)}) collective-permute-start(bf16[2,625,128]{2,1,0:T(8,128)(2,1)S(1)} %bitcast.29), channel_id=1, source_target_pairs={{0,4},{1,5},{2,6},{3,7},{4,0},{5,1},{6,2},{7,3},{8,12},{9,13},{10,... | collective-permute-start | bytes 960008 | tf_op jit(solution)/shard_map/ppermute | solution.py:295

commit v15 on v13

--- a/solution.py
+++ b/solution.py
@@ -305,14 +305,15 @@
         second_side = lambda x: lax.ppermute(x, ("pair", "task"), sides[1])
         made_forms = lambda *parts: prepare(parts, column[None], matrix)
         own = amplitudes.transpose(2, 0, 1).reshape(TV * TV, blocks_here * pairs)
+        amp1 = around(own, 1)
         part0 = mine[0]
         a0, b0, part1 = first_side(part0), second_side(part0), around(mine[1], 1)
 
-        a0, b0, part0, part1, own, to3 = after((a0, b0, part0, part1, own, mine[3]), ())
-        q0, a1, b1, part3, amp1 = second_side(a0), first_side(part1), second_side(part1), around(to3, 3), around(own, 1)
+        a0, b0, part0, part1, amp1, to3 = after((a0, b0, part0, part1, amp1, mine[3]), ())
+        q0, a1, b1, part3 = second_side(a0), first_side(part1), second_side(part1), around(to3, 3)
         forms0 = made_forms(part0, a0, b0, q0)
 
-        forms0, part1, a1, b1, part3, to2, amp1 = after((forms0, part1, a1, b1, part3, mine[2], amp1), ())
+        forms0, part1, a1, b1, part3, to2 = after((forms0, part1, a1, b1, part3, mine[2]), ())
         q1, a3, b3, part2 = second_side(a1), first_side(part3), second_side(part3), around(to2, 2)
         far0 = other_core(forms0)
         forms1 = made_forms(part1, a1, b1, q1)
@@ -344,7 +345,7 @@
     ladder = None
     calls = min(levels, 4)
     width = levels // calls
-    order = [2, 3, 1, 0] if calls == 4 else list(reversed(range(calls)))
+    order = list(reversed(range(calls)))
     for call in order:
         first = call * width
         sums = ladders(first, width, levels, blocks_here, column[None], task_owners, task_local, held, amps, matrix)

time: 127 us -> 123 us (0.969)
  waiting for transfers between devices: 43.6 us -> 37.1 us
  local copies, waits for them, and re-layouts: 6.98 us -> 9.51 us
    ppermute x9, waiting for transfers between devices: 25 us -> 16.9 us  [around(): lax.ppermute(x, 'task', [(c, (c + 2 * by) % task_count) for c in range(ta...]
    unnamed x29, local copies, waits for them, and re-layouts: 5.7 us -> 8.23 us
    ppermute x8, waiting for transfers between devices: 13.8 us -> 15.4 us  [per_device(): second_side = lambda x: lax.ppermute(x, ('pair', 'task'), sides[1])]
    ppermute x4, starting transfers between devices: 4.37 us -> 5.66 us  [per_device(): first_side = lambda x: lax.ppermute(x, ('pair', 'task'), sides[0])]
  transfers between devices with their start and end apart: 26 -> 26, of which waited for: 12 -> 11; matrix products, arithmetic and copies ran while one was open for 0% -> 3% of each run, Pallas kernels for 32% -> 33%
where the time goes in v15:
time: 123 us
  Pallas kernels  50.1 us (41%)
  waiting for transfers between devices  37.1 us (30%)
  starting transfers between devices  25.7 us (21%)
  local copies, waits for them, and re-layouts  9.51 us (8%)
    pallas_call x4, Pallas kernels, ladders(): pl.pallas_call(functools.partial(ladder_kernel, find, made, len(tiles)),...  37.3 us
    ppermute x9, waiting for transfers between devices, around(): lax.ppermute(x, 'task', [(c, (c + 2 * by) % task_count) for c in range(ta...  16.9 us
    ppermute x8, waiting for transfers between devices, per_device(): second_side = lambda x: lax.ppermute(x, ('pair', 'task'), sides[1])  15.4 us
    pallas_call x4, Pallas kernels, prepare(): pl.pallas_call(prepare_kernel, out_shape=jax.ShapeDtypeStruct((count, mat...  11.4 us
    ppermute x9, starting transfers between devices, around(): lax.ppermute(x, 'task', [(c, (c + 2 * by) % task_count) for c in range(ta...  9.96 us
    ppermute x8, starting transfers between devices, per_device(): second_side = lambda x: lax.ppermute(x, ('pair', 'task'), sides[1])  9.32 us
    unnamed x29, local copies, waits for them, and re-layouts  8.23 us
    ppermute x4, starting transfers between devices, per_device(): first_side = lambda x: lax.ppermute(x, ('pair', 'task'), sides[0])  5.66 us
  transfers between devices with their start and end apart: 26, of which 11 were waited for; matrix products, arithmetic and copies ran while one was open for 3% of the time, Pallas kernels for 33%

profile of v15, /device:TPU:0, one launch (start us, length us, event | category | flops | bytes accessed | tf_op | source)
XLA Modules:
  0.0 122.8 jit_solution(6415205161882176794)
XLA Ops:
  0.0 1.2 pad
  1.3 3.1 %collective-permute-start.3 = (bf16[625,256]{1,0:T(8,128)(2,1)S(1)}, bf16[625,256]{1,0:T(8,128)(2,1)S(1)}, u32[]{:S(2)}, u32[]{:S(2)}) collective-permute-start(bf16[625,256]{1,0:T(8,128)(2,1)S(1)} %bitcast.24), channel_id=1, source_target_pairs={{0,2},{1,3},{2,4},{3,5},{4,6},{5,7},{6,0},{7,1},{8,10},{9,11},{10,... | collective-permute-start | bytes 960008 | tf_op jit(solution)/shard_map/ppermute | solution.py:294
  4.4 3.3 %copy.22 = bf16[2,384,625]{2,1,0:T(8,128)(2,1)S(1)} copy(bf16[2,384,625]{1,0,2:T(2,128)(2,1)} %param.7) | data formatting | bytes 1920000 | tf_op args[0]
  7.7 0.1 dynamic-slice_bitcast_fusion
  7.8 1.6 %collective-permute-start.2 = (bf16[2,96,625]{2,1,0:T(8,128)(2,1)S(1)}, bf16[2,96,625]{2,1,0:T(8,128)(2,1)S(1)}, u32[]{:S(2)}, u32[]{:S(2)}) collective-permute-start(bf16[2,96,625]{2,1,0:T(8,128)(2,1)S(1)} %get-tuple-element.63), channel_id=1, source_target_pairs={{0,2},{1,3},{2,4},{3,5},{4,6},{5,7},{6,0},{7,1},{8,10},{9,11},{10,... | collective-permute-start | bytes 720008 | tf_op jit(solution)/shard_map/ppermute | solution.py:294
  9.5 1.5 %collective-permute-start.1 = (bf16[2,96,625]{2,1,0:T(8,128)(2,1)S(1)}, bf16[2,96,625]{2,1,0:T(8,128)(2,1)S(1)}, u32[]{:S(2)}, u32[]{:S(2)}) collective-permute-start(bf16[2,96,625]{2,1,0:T(8,128)(2,1)S(1)} %get-tuple-element.33.refs_0_), channel_id=1, source_target_pairs={{0,16},{1,9},{2,18},{3,11},{4,20},{5,13},{6,22},{7,15},{8,24},{9,1... | collective-permute-start | bytes 720008 | tf_op jit(solution)/shard_map/ppermute | solution.py:305
  11.0 1.5 %collective-permute-start = (bf16[2,96,625]{2,1,0:T(8,128)(2,1)S(1)}, bf16[2,96,625]{2,1,0:T(8,128)(2,1)S(1)}, u32[]{:S(2)}, u32[]{:S(2)}) collective-permute-start(bf16[2,96,625]{2,1,0:T(8,128)(2,1)S(1)} %get-tuple-element.33.refs_0_), channel_id=1, source_target_pairs={{0,8},{1,17},{2,10},{3,19},{4,12},{5,21},{6,14},{7,23},{8,0},{9,25... | collective-permute-start | bytes 720008 | tf_op jit(solution)/shard_map/ppermute | solution.py:304
  12.5 6.8 %collective-permute-done.2.refs_0_ = bf16[2,96,625]{2,1,0:T(8,128)(2,1)S(1)} collective-permute-done((bf16[2,96,625]{2,1,0:T(8,128)(2,1)S(1)}, bf16[2,96,625]{2,1,0:T(8,128)(2,1)S(1)}, u32[]{:S(2)}, u32[]{:S(2)}) %collective-permute-start.2) | collective-permute-done | bytes 240032 | tf_op jit(solution)/shard_map/ppermute | solution.py:294
  19.3 0.0 collective-permute-done.1.refs_2_
  19.3 0.0 collective-permute-done.refs_1_
  19.3 0.0 collective-permute-done.3.refs_1_
  19.3 1.6 %collective-permute-start.4 = (bf16[2,96,625]{2,1,0:T(8,128)(2,1)S(1)}, bf16[2,96,625]{2,1,0:T(8,128)(2,1)S(1)}, u32[]{:S(2)}, u32[]{:S(2)}) collective-permute-start(bf16[2,96,625]{2,1,0:T(8,128)(2,1)S(1)} %collective-permute-done.refs_1_), channel_id=1, source_target_pairs={{0,16},{1,9},{2,18},{3,11},{4,20},{5,13},{6,22},{7,15},{8,24},{9,1... | collective-permute-start | bytes 720008 | tf_op jit(solution)/shard_map/ppermute | solution.py:305
  20.9 1.7 %collective-permute-start.7 = (bf16[2,96,625]{2,1,0:T(8,128)(2,1)S(1)}, bf16[2,96,625]{2,1,0:T(8,128)(2,1)S(1)}, u32[]{:S(2)}, u32[]{:S(2)}) collective-permute-start(bf16[2,96,625]{2,1,0:T(8,128)(2,1)S(1)} %get-tuple-element.37), channel_id=1, source_target_pairs={{0,6},{1,7},{2,0},{3,1},{4,2},{5,3},{6,4},{7,5},{8,14},{9,15},{10,... | collective-permute-start | bytes 720008 | tf_op jit(solution)/shard_map/ppermute | solution.py:294
  22.6 0.5 collective-permute-start.6
  23.1 1.5 %collective-permute-start.5 = (bf16[2,96,625]{2,1,0:T(8,128)(2,1)S(1)}, bf16[2,96,625]{2,1,0:T(8,128)(2,1)S(1)}, u32[]{:S(2)}, u32[]{:S(2)}) collective-permute-start(bf16[2,96,625]{2,1,0:T(8,128)(2,1)S(1)} %collective-permute-done.2.refs_0_), channel_id=1, source_target_pairs={{0,8},{1,17},{2,10},{3,19},{4,12},{5,21},{6,14},{7,23},{8,0},{9,25... | collective-permute-start | bytes 720008 | tf_op jit(solution)/shard_map/ppermute | solution.py:304
  24.6 2.7 %collective-permute-done.4.refs_3_ = bf16[2,96,625]{2,1,0:T(8,128)(2,1)S(1)} collective-permute-done((bf16[2,96,625]{2,1,0:T(8,128)(2,1)S(1)}, bf16[2,96,625]{2,1,0:T(8,128)(2,1)S(1)}, u32[]{:S(2)}, u32[]{:S(2)}) %collective-permute-start.4) | collective-permute-done | bytes 240032 | tf_op jit(solution)/shard_map/ppermute | solution.py:305
  27.3 1.6 %copy-done.5 = bf16[1600,625]{1,0:T(8,128)(2,1)S(1)} copy-done((bf16[1600,625]{1,0:T(8,128)(2,1)S(1)}, bf16[1600,625]{1,0:T(8,128)(2,1)}, u32[]{:S(2)}) %copy-start.5) | copy-done | bytes 2000024
  28.8 2.6 %shard_map.73.refs_0_ = bf16[2,1600,384]{2,1,0:T(8,128)(2,1)S(1)} custom-call(s32[1]{0:T(128)} %bitcast.column_ref, bf16[2,96,625]{2,1,0:T(8,128)(2,1)S(1)} %get-tuple-element.33.refs_0_, bf16[2,96,625]{2,1,0:T(8,128)(2,1)S(1)} %collective-permute-done.refs_1_, bf16[2,96,625]{2,1,0:T(8,128)(2,1)S(1)} %collective-permute-done.1.refs_2_, ...), custom_call_target="tpu_custom_call" | custom-call | flops 1536000000 | bytes 3417600 | tf_op jit(solution)/shard_map/pallas_call | solution.py:72
  31.5 0.0 collective-permute-done.7.refs_0_
  31.5 0.0 collective-permute-done.5.refs_1_
  31.5 0.1 collective-permute-start.12
  31.6 1.6 %collective-permute-start.8 = (bf16[2,96,625]{2,1,0:T(8,128)(2,1)S(1)}, bf16[2,96,625]{2,1,0:T(8,128)(2,1)S(1)}, u32[]{:S(2)}, u32[]{:S(2)}) collective-permute-start(bf16[2,96,625]{2,1,0:T(8,128)(2,1)S(1)} %collective-permute-done.5.refs_1_), channel_id=1, source_target_pairs={{0,16},{1,9},{2,18},{3,11},{4,20},{5,13},{6,22},{7,15},{8,24},{9,1... | collective-permute-start | bytes 720008 | tf_op jit(solution)/shard_map/ppermute | solution.py:305
  33.2 1.0 collective-permute-start.11
  34.2 0.5 collective-permute-start.10
  34.7 1.8 %collective-permute-start.9 = (bf16[2,96,625]{2,1,0:T(8,128)(2,1)S(1)}, bf16[2,96,625]{2,1,0:T(8,128)(2,1)S(1)}, u32[]{:S(2)}, u32[]{:S(2)}) collective-permute-start(bf16[2,96,625]{2,1,0:T(8,128)(2,1)S(1)} %collective-permute-done.7.refs_0_), channel_id=1, source_target_pairs={{0,8},{1,17},{2,10},{3,19},{4,12},{5,21},{6,14},{7,23},{8,0},{9,25... | collective-permute-start | bytes 720008 | tf_op jit(solution)/shard_map/ppermute | solution.py:304
  36.5 2.3 %collective-permute-done.8.refs_3_ = bf16[2,96,625]{2,1,0:T(8,128)(2,1)S(1)} collective-permute-done((bf16[2,96,625]{2,1,0:T(8,128)(2,1)S(1)}, bf16[2,96,625]{2,1,0:T(8,128)(2,1)S(1)}, u32[]{:S(2)}, u32[]{:S(2)}) %collective-permute-start.8) | collective-permute-done | bytes 240032 | tf_op jit(solution)/shard_map/ppermute | solution.py:305
  38.8 2.6 %shard_map.74.refs_2_ = bf16[2,1600,384]{2,1,0:T(8,128)(2,1)S(1)} custom-call(s32[1]{0:T(128)} %bitcast.column_ref, bf16[2,96,625]{2,1,0:T(8,128)(2,1)S(1)} %collective-permute-done.2.refs_0_, bf16[2,96,625]{2,1,0:T(8,128)(2,1)S(1)} %collective-permute-done.5.refs_1_, bf16[2,96,625]{2,1,0:T(8,128)(2,1)S(1)} %collective-permute-done.6.refs_2_, ...), custom_call_target="tpu_custom_call" | custom-call | flops 1536000000 | bytes 3417600 | tf_op jit(solution)/shard_map/pallas_call | solution.py:72
  41.4 0.0 copy-start.6
  41.5 5.5 %collective-permute-done.11.refs_0_ = bf16[2,96,625]{2,1,0:T(8,128)(2,1)S(1)} collective-permute-done((bf16[2,96,625]{2,1,0:T(8,128)(2,1)S(1)}, bf16[2,96,625]{2,1,0:T(8,128)(2,1)S(1)}, u32[]{:S(2)}, u32[]{:S(2)}) %collective-permute-start.11) | collective-permute-done | bytes 240032 | tf_op jit(solution)/shard_map/ppermute | solution.py:294
  47.0 0.0 collective-permute-done.12.refs_1_
  47.0 0.1 collective-permute-start.17
  47.1 1.2 %collective-permute-start.13 = (bf16[2,96,625]{2,1,0:T(8,128)(2,1)S(1)}, bf16[2,96,625]{2,1,0:T(8,128)(2,1)S(1)}, u32[]{:S(2)}, u32[]{:S(2)}) collective-permute-start(bf16[2,96,625]{2,1,0:T(8,128)(2,1)S(1)} %collective-permute-done.9.refs_1_), channel_id=1, source_target_pairs={{0,16},{1,9},{2,18},{3,11},{4,20},{5,13},{6,22},{7,15},{8,24},{9,1... | collective-permute-start | bytes 720008 | tf_op jit(solution)/shard_map/ppermute | solution.py:305
  48.3 0.1 copy-done.7
  48.5 1.1 collective-permute-start.15
  49.6 0.9 collective-permute-start.14
  50.5 4.5 %collective-permute-done.13.refs_3_ = bf16[2,96,625]{2,1,0:T(8,128)(2,1)S(1)} collective-permute-done((bf16[2,96,625]{2,1,0:T(8,128)(2,1)S(1)}, bf16[2,96,625]{2,1,0:T(8,128)(2,1)S(1)}, u32[]{:S(2)}, u32[]{:S(2)}) %collective-permute-start.13) | collective-permute-done | bytes 240032 | tf_op jit(solution)/shard_map/ppermute | solution.py:305
  55.1 2.6 %shard_map.75.refs_6_ = bf16[2,1600,384]{2,1,0:T(8,128)(2,1)S(1)} custom-call(s32[1]{0:T(128)} %bitcast.column_ref, bf16[2,96,625]{2,1,0:T(8,128)(2,1)S(1)} %collective-permute-done.7.refs_0_, bf16[2,96,625]{2,1,0:T(8,128)(2,1)S(1)} %collective-permute-done.9.refs_1_, bf16[2,96,625]{2,1,0:T(8,128)(2,1)S(1)} %collective-permute-done.10.refs_2_, ...), custom_call_target="tpu_custom_call" | custom-call | flops 1536000000 | bytes 3417600 | tf_op jit(solution)/shard_map/pallas_call | solution.py:72
  57.7 0.0 copy-start.4
  57.7 0.9 collective-permute-done.15.refs_2_
  58.6 1.2 collective-permute-done.16.refs_2_
  59.8 0.0 collective-permute-done.17.refs_3_
  59.8 1.2 %collective-permute-start.18 = (bf16[2,96,625]{2,1,0:T(8,128)(2,1)S(1)}, bf16[2,96,625]{2,1,0:T(8,128)(2,1)S(1)}, u32[]{:S(2)}, u32[]{:S(2)}) collective-permute-start(bf16[2,96,625]{2,1,0:T(8,128)(2,1)S(1)} %collective-permute-done.14.refs_1_), channel_id=1, source_target_pairs={{0,16},{1,9},{2,18},{3,11},{4,20},{5,13},{6,22},{7,15},{8,24},{9,1... | collective-permute-start | bytes 720008 | tf_op jit(solution)/shard_map/ppermute | solution.py:305
  61.1 0.0 collective-permute-start.19
  61.1 5.0 %collective-permute-done.18.refs_3_ = bf16[2,96,625]{2,1,0:T(8,128)(2,1)S(1)} collective-permute-done((bf16[2,96,625]{2,1,0:T(8,128)(2,1)S(1)}, bf16[2,96,625]{2,1,0:T(8,128)(2,1)S(1)}, u32[]{:S(2)}, u32[]{:S(2)}) %collective-permute-start.18) | collective-permute-done | bytes 240032 | tf_op jit(solution)/shard_map/ppermute | solution.py:305
  66.1 3.4 %shard_map.76.refs_4_ = bf16[2,1600,384]{2,1,0:T(8,128)(2,1)} custom-call(s32[1]{0:T(128)} %bitcast.column_ref, bf16[2,96,625]{2,1,0:T(8,128)(2,1)S(1)} %collective-permute-done.11.refs_0_, bf16[2,96,625]{2,1,0:T(8,128)(2,1)S(1)} %collective-permute-done.14.refs_1_, bf16[2,96,625]{2,1,0:T(8,128)(2,1)S(1)} %collective-permute-done.15.refs_2_, ...), custom_call_target="tpu_custom_call" | custom-call | flops 1536000000 | bytes 3417600 | tf_op jit(solution)/shard_map/pallas_call | solution.py:72
  69.5 2.7 %collective-permute-done.19.refs_3_ = bf16[625,256]{1,0:T(8,128)(2,1)S(1)} collective-permute-done((bf16[625,256]{1,0:T(8,128)(2,1)S(1)}, bf16[625,256]{1,0:T(8,128)(2,1)S(1)}, u32[]{:S(2)}, u32[]{:S(2)}) %collective-permute-start.19) | collective-permute-done | bytes 320032 | tf_op jit(solution)/shard_map/ppermute | solution.py:294
  72.2 0.0 collective-permute-start.21
  72.2 1.4 %shard_map.77.refs_8_ = bf16[8,800,128]{2,1,0:T(8,128)(2,1)S(1)} custom-call(bf16[800,625]{1,0:T(8,128)(2,1)S(1)} %copy-done.4, bf16[625,256]{1,0:T(8,128)(2,1)S(1)} %bitcast.25, bf16[625,256]{1,0:T(8,128)(2,1)S(1)} %collective-permute-done.3.refs_1_, bf16[625,256]{1,0:T(8,128)(2,1)S(1)} %collective-permute-done.16.refs_2_, ...), custom_call_target="tpu_custom_call" | custom-call | flops 1024000000 | bytes 2560000 | tf_op jit(solution)/shard_map/pallas_call | solution.py:103
  73.7 0.6 collective-permute-start.22
  74.3 0.1 copy.23.owners_ref
  74.4 0.1 copy.24.local_ref
  74.5 4.8 %collective-permute-done.22.refs_9_ = bf16[8,800,128]{2,1,0:T(8,128)(2,1)S(1)} collective-permute-done((bf16[8,800,128]{2,1,0:T(8,128)(2,1)S(1)}, bf16[8,800,128]{2,1,0:T(8,128)(2,1)S(1)}, u32[]{:S(2)}, u32[]{:S(2)}) %collective-permute-start.22) | collective-permute-done | bytes 1638432 | tf_op jit(solution)/shard_map/ppermute | solution.py:291
  79.3 1.7 %copy-done.1 = bf16[2,1600,384]{2,1,0:T(8,128)(2,1)S(1)} copy-done((bf16[2,1600,384]{2,1,0:T(8,128)(2,1)S(1)}, bf16[2,1600,384]{2,1,0:T(8,128)(2,1)}, u32[]{:S(2)}) %copy-start.1) | copy-done | bytes 2457624
  81.0 9.3 %shard_map.79 = bf16[1,2,625,128]{3,2,1,0:T(8,128)(2,1)S(1)} custom-call(s32[1]{0:T(128)} %bitcast.column_ref, s32[32,3]{1,0:T(8,128)S(1)} %copy.23.owners_ref, s32[32,4]{1,0:T(8,128)S(1)} %copy.24.local_ref, bf16[2,1600,384]{2,1,0:T(8,128)(2,1)S(1)} %copy-done.1, bf16[2,1600,384]{2,1,0:T(8,128)(2,1)} %copy-done.7, bf16[2,1600,384]{2,1,0:T(8,128)(2,1)} %copy-done.2, ...), custom_call_target="tpu_custom_call" | custom-call | flops 2936012800 | bytes 6553600 | tf_op jit(solution)/shard_map/pallas_call | solution.py:257
  90.3 0.1 collective-permute-start.24
  90.4 9.3 %shard_map.78 = bf16[1,2,625,128]{3,2,1,0:T(8,128)(2,1)S(1)} custom-call(s32[1]{0:T(128)} %bitcast.column_ref, s32[32,3]{1,0:T(8,128)S(1)} %copy.23.owners_ref, s32[32,4]{1,0:T(8,128)S(1)} %copy.24.local_ref, bf16[2,1600,384]{2,1,0:T(8,128)(2,1)S(1)} %copy-done.1, bf16[2,1600,384]{2,1,0:T(8,128)(2,1)} %copy-done.7, bf16[2,1600,384]{2,1,0:T(8,128)(2,1)} %copy-done.2, ...), custom_call_target="tpu_custom_call" | custom-call | flops 2936012800 | bytes 6553600 | tf_op jit(solution)/shard_map/pallas_call | solution.py:257
  99.7 1.2 collective-permute-start.23
  100.9 9.3 %shard_map.80 = bf16[1,2,625,128]{3,2,1,0:T(8,128)(2,1)S(1)} custom-call(s32[1]{0:T(128)} %bitcast.column_ref, s32[32,3]{1,0:T(8,128)S(1)} %copy.23.owners_ref, s32[32,4]{1,0:T(8,128)S(1)} %copy.24.local_ref, bf16[2,1600,384]{2,1,0:T(8,128)(2,1)S(1)} %copy-done.1, bf16[2,1600,384]{2,1,0:T(8,128)(2,1)} %copy-done.7, bf16[2,1600,384]{2,1,0:T(8,128)(2,1)} %copy-done.2, ...), custom_call_target="tpu_custom_call" | custom-call | flops 2936012800 | bytes 6553600 | tf_op jit(solution)/shard_map/pallas_call | solution.py:257
  110.2 0.0 copy-start.9
  110.2 1.3 %collective-permute-start.25 = (bf16[2,625,128]{2,1,0:T(8,128)(2,1)S(1)}, bf16[2,625,128]{2,1,0:T(8,128)(2,1)S(1)}, u32[]{:S(2)}, u32[]{:S(2)}) collective-permute-start(bf16[2,625,128]{2,1,0:T(8,128)(2,1)S(1)} %bitcast.28), channel_id=1, source_target_pairs={{0,2},{1,3},{2,4},{3,5},{4,6},{5,7},{6,0},{7,1},{8,10},{9,11},{10,... | collective-permute-start | bytes 960008 | tf_op jit(solution)/shard_map/ppermute | solution.py:294
  111.5 9.3 %shard_map.81 = bf16[1,2,625,128]{3,2,1,0:T(8,128)(2,1)S(1)} custom-call(s32[1]{0:T(128)} %bitcast.column_ref, s32[32,3]{1,0:T(8,128)S(1)} %copy.23.owners_ref, s32[32,4]{1,0:T(8,128)S(1)} %copy.24.local_ref, bf16[2,1600,384]{2,1,0:T(8,128)(2,1)S(1)} %copy-done.1, bf16[2,1600,384]{2,1,0:T(8,128)(2,1)} %copy-done.7, bf16[2,1600,384]{2,1,0:T(8,128)(2,1)} %copy-done.2, ...), custom_call_target="tpu_custom_call" | custom-call | flops 2936012800 | bytes 6553600 | tf_op jit(solution)/shard_map/pallas_call | solution.py:257
  120.8 0.6 collective-permute-done.25
  121.4 0.2 fusion.1
  121.6 1.2 copy.32
  (29 shorter events, 0.1 us)
Async XLA Ops:
  1.3 18.0 %collective-permute-start.3 = (bf16[625,256]{1,0:T(8,128)(2,1)S(1)}, bf16[625,256]{1,0:T(8,128)(2,1)S(1)}, u32[]{:S(2)}, u32[]{:S(2)}) collective-permute-start(bf16[625,256]{1,0:T(8,128)(2,1)S(1)} %bitcast.24), channel_id=1, source_target_pairs={{0,2},{1,3},{2,4},{3,5},{4,6},{5,7},{6,0},{7,1},{8,10},{9,11},{10,... | collective-permute-start | bytes 960008 | tf_op jit(solution)/shard_map/ppermute | solution.py:294
  7.8 11.4 %collective-permute-start.2 = (bf16[2,96,625]{2,1,0:T(8,128)(2,1)S(1)}, bf16[2,96,625]{2,1,0:T(8,128)(2,1)S(1)}, u32[]{:S(2)}, u32[]{:S(2)}) collective-permute-start(bf16[2,96,625]{2,1,0:T(8,128)(2,1)S(1)} %get-tuple-element.63), channel_id=1, source_target_pairs={{0,2},{1,3},{2,4},{3,5},{4,6},{5,7},{6,0},{7,1},{8,10},{9,11},{10,... | collective-permute-start | bytes 720008 | tf_op jit(solution)/shard_map/ppermute | solution.py:294
  9.5 9.8 %collective-permute-start.1 = (bf16[2,96,625]{2,1,0:T(8,128)(2,1)S(1)}, bf16[2,96,625]{2,1,0:T(8,128)(2,1)S(1)}, u32[]{:S(2)}, u32[]{:S(2)}) collective-permute-start(bf16[2,96,625]{2,1,0:T(8,128)(2,1)S(1)} %get-tuple-element.33.refs_0_), channel_id=1, source_target_pairs={{0,16},{1,9},{2,18},{3,11},{4,20},{5,13},{6,22},{7,15},{8,24},{9,1... | collective-permute-start | bytes 720008 | tf_op jit(solution)/shard_map/ppermute | solution.py:305
  11.0 8.3 %collective-permute-start = (bf16[2,96,625]{2,1,0:T(8,128)(2,1)S(1)}, bf16[2,96,625]{2,1,0:T(8,128)(2,1)S(1)}, u32[]{:S(2)}, u32[]{:S(2)}) collective-permute-start(bf16[2,96,625]{2,1,0:T(8,128)(2,1)S(1)} %get-tuple-element.33.refs_0_), channel_id=1, source_target_pairs={{0,8},{1,17},{2,10},{3,19},{4,12},{5,21},{6,14},{7,23},{8,0},{9,25... | collective-permute-start | bytes 720008 | tf_op jit(solution)/shard_map/ppermute | solution.py:304
  19.3 8.0 %collective-permute-start.4 = (bf16[2,96,625]{2,1,0:T(8,128)(2,1)S(1)}, bf16[2,96,625]{2,1,0:T(8,128)(2,1)S(1)}, u32[]{:S(2)}, u32[]{:S(2)}) collective-permute-start(bf16[2,96,625]{2,1,0:T(8,128)(2,1)S(1)} %collective-permute-done.refs_1_), channel_id=1, source_target_pairs={{0,16},{1,9},{2,18},{3,11},{4,20},{5,13},{6,22},{7,15},{8,24},{9,1... | collective-permute-start | bytes 720008 | tf_op jit(solution)/shard_map/ppermute | solution.py:305
  20.9 10.6 %collective-permute-start.7 = (bf16[2,96,625]{2,1,0:T(8,128)(2,1)S(1)}, bf16[2,96,625]{2,1,0:T(8,128)(2,1)S(1)}, u32[]{:S(2)}, u32[]{:S(2)}) collective-permute-start(bf16[2,96,625]{2,1,0:T(8,128)(2,1)S(1)} %get-tuple-element.37), channel_id=1, source_target_pairs={{0,6},{1,7},{2,0},{3,1},{4,2},{5,3},{6,4},{7,5},{8,14},{9,15},{10,... | collective-permute-start | bytes 720008 | tf_op jit(solution)/shard_map/ppermute | solution.py:294
  22.6 8.9 %collective-permute-start.6 = (bf16[2,96,625]{2,1,0:T(8,128)(2,1)S(1)}, bf16[2,96,625]{2,1,0:T(8,128)(2,1)S(1)}, u32[]{:S(2)}, u32[]{:S(2)}) collective-permute-start(bf16[2,96,625]{2,1,0:T(8,128)(2,1)S(1)} %collective-permute-done.2.refs_0_), channel_id=1, source_target_pairs={{0,16},{1,9},{2,18},{3,11},{4,20},{5,13},{6,22},{7,15},{8,24},{9,1... | collective-permute-start | bytes 720008 | tf_op jit(solution)/shard_map/ppermute | solution.py:305
  23.1 8.4 %collective-permute-start.5 = (bf16[2,96,625]{2,1,0:T(8,128)(2,1)S(1)}, bf16[2,96,625]{2,1,0:T(8,128)(2,1)S(1)}, u32[]{:S(2)}, u32[]{:S(2)}) collective-permute-start(bf16[2,96,625]{2,1,0:T(8,128)(2,1)S(1)} %collective-permute-done.2.refs_0_), channel_id=1, source_target_pairs={{0,8},{1,17},{2,10},{3,19},{4,12},{5,21},{6,14},{7,23},{8,0},{9,25... | collective-permute-start | bytes 720008 | tf_op jit(solution)/shard_map/ppermute | solution.py:304
  27.3 1.6 %copy-start.5 = (bf16[1600,625]{1,0:T(8,128)(2,1)S(1)}, bf16[1600,625]{1,0:T(8,128)(2,1)}, u32[]{:S(2)}) copy-start(bf16[1600,625]{1,0:T(8,128)(2,1)} %constant.59.clone.refs_4_) | copy-start | bytes 6000004
  31.5 9.9 %copy-start = (bf16[2,1600,384]{2,1,0:T(8,128)(2,1)}, bf16[2,1600,384]{2,1,0:T(8,128)(2,1)S(1)}, u32[]{:S(2)}) copy-start(bf16[2,1600,384]{2,1,0:T(8,128)(2,1)S(1)} %shard_map.73.refs_0_) | copy-start | bytes 7372804
  31.5 15.5 %collective-permute-start.12 = (bf16[2,1600,384]{2,1,0:T(8,128)(2,1)S(1)}, bf16[2,1600,384]{2,1,0:T(8,128)(2,1)S(1)}, u32[]{:S(2)}, u32[]{:S(2)}) collective-permute-start(bf16[2,1600,384]{2,1,0:T(8,128)(2,1)S(1)} %shard_map.73.refs_0_), channel_id=1, source_target_pairs={{0,1},{1,0},{2,3},{3,2},{4,5},{5,4},{6,7},{7,6},{8,9},{9,8},{10,11... | collective-permute-start | bytes 7372808 | tf_op jit(solution)/shard_map/ppermute | solution.py:291
  31.6 7.2 %collective-permute-start.8 = (bf16[2,96,625]{2,1,0:T(8,128)(2,1)S(1)}, bf16[2,96,625]{2,1,0:T(8,128)(2,1)S(1)}, u32[]{:S(2)}, u32[]{:S(2)}) collective-permute-start(bf16[2,96,625]{2,1,0:T(8,128)(2,1)S(1)} %collective-permute-done.5.refs_1_), channel_id=1, source_target_pairs={{0,16},{1,9},{2,18},{3,11},{4,20},{5,13},{6,22},{7,15},{8,24},{9,1... | collective-permute-start | bytes 720008 | tf_op jit(solution)/shard_map/ppermute | solution.py:305
  33.2 13.8 %collective-permute-start.11 = (bf16[2,96,625]{2,1,0:T(8,128)(2,1)S(1)}, bf16[2,96,625]{2,1,0:T(8,128)(2,1)S(1)}, u32[]{:S(2)}, u32[]{:S(2)}) collective-permute-start(bf16[2,96,625]{2,1,0:T(8,128)(2,1)S(1)} %get-tuple-element.43), channel_id=1, source_target_pairs={{0,4},{1,5},{2,6},{3,7},{4,0},{5,1},{6,2},{7,3},{8,12},{9,13},{10,... | collective-permute-start | bytes 720008 | tf_op jit(solution)/shard_map/ppermute | solution.py:294
  34.2 12.8 %collective-permute-start.10 = (bf16[2,96,625]{2,1,0:T(8,128)(2,1)S(1)}, bf16[2,96,625]{2,1,0:T(8,128)(2,1)S(1)}, u32[]{:S(2)}, u32[]{:S(2)}) collective-permute-start(bf16[2,96,625]{2,1,0:T(8,128)(2,1)S(1)} %collective-permute-done.7.refs_0_), channel_id=1, source_target_pairs={{0,16},{1,9},{2,18},{3,11},{4,20},{5,13},{6,22},{7,15},{8,24},{9,1... | collective-permute-start | bytes 720008 | tf_op jit(solution)/shard_map/ppermute | solution.py:305
  34.7 12.3 %collective-permute-start.9 = (bf16[2,96,625]{2,1,0:T(8,128)(2,1)S(1)}, bf16[2,96,625]{2,1,0:T(8,128)(2,1)S(1)}, u32[]{:S(2)}, u32[]{:S(2)}) collective-permute-start(bf16[2,96,625]{2,1,0:T(8,128)(2,1)S(1)} %collective-permute-done.7.refs_0_), channel_id=1, source_target_pairs={{0,8},{1,17},{2,10},{3,19},{4,12},{5,21},{6,14},{7,23},{8,0},{9,25... | collective-permute-start | bytes 720008 | tf_op jit(solution)/shard_map/ppermute | solution.py:304
  41.4 16.3 %copy-start.2 = (bf16[2,1600,384]{2,1,0:T(8,128)(2,1)}, bf16[2,1600,384]{2,1,0:T(8,128)(2,1)S(1)}, u32[]{:S(2)}) copy-start(bf16[2,1600,384]{2,1,0:T(8,128)(2,1)S(1)} %shard_map.74.refs_2_) | copy-start | bytes 7372804
  41.4 24.6 %copy-start.6 = (bf16[1600,625]{1,0:T(8,128)(2,1)S(1)}, bf16[1600,625]{1,0:T(8,128)(2,1)}, u32[]{:S(2)}) copy-start(bf16[1600,625]{1,0:T(8,128)(2,1)} %constant.59.clone.refs_4_) | copy-start | bytes 6000004
  47.0 1.5 %copy-start.7 = (bf16[2,1600,384]{2,1,0:T(8,128)(2,1)}, bf16[2,1600,384]{2,1,0:T(8,128)(2,1)S(1)}, u32[]{:S(2)}) copy-start(bf16[2,1600,384]{2,1,0:T(8,128)(2,1)S(1)} %collective-permute-done.12.refs_1_) | copy-start | bytes 7372804
  47.0 12.8 %collective-permute-start.17 = (bf16[2,1600,384]{2,1,0:T(8,128)(2,1)S(1)}, bf16[2,1600,384]{2,1,0:T(8,128)(2,1)}, u32[]{:S(2)}, u32[]{:S(2)}) collective-permute-start(bf16[2,1600,384]{2,1,0:T(8,128)(2,1)S(1)} %shard_map.74.refs_2_), channel_id=1, source_target_pairs={{0,1},{1,0},{2,3},{3,2},{4,5},{5,4},{6,7},{7,6},{8,9},{9,8},{10,11... | collective-permute-start | bytes 7372808 | tf_op jit(solution)/shard_map/ppermute | solution.py:291
  47.1 7.9 %collective-permute-start.13 = (bf16[2,96,625]{2,1,0:T(8,128)(2,1)S(1)}, bf16[2,96,625]{2,1,0:T(8,128)(2,1)S(1)}, u32[]{:S(2)}, u32[]{:S(2)}) collective-permute-start(bf16[2,96,625]{2,1,0:T(8,128)(2,1)S(1)} %collective-permute-done.9.refs_1_), channel_id=1, source_target_pairs={{0,16},{1,9},{2,18},{3,11},{4,20},{5,13},{6,22},{7,15},{8,24},{9,1... | collective-permute-start | bytes 720008 | tf_op jit(solution)/shard_map/ppermute | solution.py:305
  48.5 11.4 %collective-permute-start.16 = (bf16[625,256]{1,0:T(8,128)(2,1)S(1)}, bf16[625,256]{1,0:T(8,128)(2,1)S(1)}, u32[]{:S(2)}, u32[]{:S(2)}) collective-permute-start(bf16[625,256]{1,0:T(8,128)(2,1)S(1)} %collective-permute-done.3.refs_1_), channel_id=1, source_target_pairs={{0,2},{1,3},{2,4},{3,5},{4,6},{5,7},{6,0},{7,1},{8,10},{9,11},{10,... | collective-permute-start | bytes 960008 | tf_op jit(solution)/shard_map/ppermute | solution.py:294
  48.5 10.1 %collective-permute-start.15 = (bf16[2,96,625]{2,1,0:T(8,128)(2,1)S(1)}, bf16[2,96,625]{2,1,0:T(8,128)(2,1)S(1)}, u32[]{:S(2)}, u32[]{:S(2)}) collective-permute-start(bf16[2,96,625]{2,1,0:T(8,128)(2,1)S(1)} %collective-permute-done.11.refs_0_), channel_id=1, source_target_pairs={{0,16},{1,9},{2,18},{3,11},{4,20},{5,13},{6,22},{7,15},{8,24},{9,1... | collective-permute-start | bytes 720008 | tf_op jit(solution)/shard_map/ppermute | solution.py:305
  49.6 9.0 %collective-permute-start.14 = (bf16[2,96,625]{2,1,0:T(8,128)(2,1)S(1)}, bf16[2,96,625]{2,1,0:T(8,128)(2,1)S(1)}, u32[]{:S(2)}, u32[]{:S(2)}) collective-permute-start(bf16[2,96,625]{2,1,0:T(8,128)(2,1)S(1)} %collective-permute-done.11.refs_0_), channel_id=1, source_target_pairs={{0,8},{1,17},{2,10},{3,19},{4,12},{5,21},{6,14},{7,23},{8,0},{9,25... | collective-permute-start | bytes 720008 | tf_op jit(solution)/shard_map/ppermute | solution.py:304
  57.7 11.8 %copy-start.3 = (bf16[2,1600,384]{2,1,0:T(8,128)(2,1)}, bf16[2,1600,384]{2,1,0:T(8,128)(2,1)S(1)}, u32[]{:S(2)}) copy-start(bf16[2,1600,384]{2,1,0:T(8,128)(2,1)S(1)} %shard_map.75.refs_6_) | copy-start | bytes 7372804
  57.7 14.5 %copy-start.4 = (bf16[800,625]{1,0:T(8,128)(2,1)S(1)}, bf16[800,625]{1,0:T(8,128)(2,1)}, u32[]{:S(2)}) copy-start(bf16[800,625]{1,0:T(8,128)(2,1)} %constant.60.clone.matrix_ref) | copy-start | bytes 3000004
  59.8 12.4 %collective-permute-start.20 = (bf16[2,1600,384]{2,1,0:T(8,128)(2,1)S(1)}, bf16[2,1600,384]{2,1,0:T(8,128)(2,1)S(1)}, u32[]{:S(2)}, u32[]{:S(2)}) collective-permute-start(bf16[2,1600,384]{2,1,0:T(8,128)(2,1)S(1)} %shard_map.75.refs_6_), channel_id=1, source_target_pairs={{0,1},{1,0},{2,3},{3,2},{4,5},{5,4},{6,7},{7,6},{8,9},{9,8},{10,11... | collective-permute-start | bytes 7372808 | tf_op jit(solution)/shard_map/ppermute | solution.py:291
  59.8 6.2 %collective-permute-start.18 = (bf16[2,96,625]{2,1,0:T(8,128)(2,1)S(1)}, bf16[2,96,625]{2,1,0:T(8,128)(2,1)S(1)}, u32[]{:S(2)}, u32[]{:S(2)}) collective-permute-start(bf16[2,96,625]{2,1,0:T(8,128)(2,1)S(1)} %collective-permute-done.14.refs_1_), channel_id=1, source_target_pairs={{0,16},{1,9},{2,18},{3,11},{4,20},{5,13},{6,22},{7,15},{8,24},{9,1... | collective-permute-start | bytes 720008 | tf_op jit(solution)/shard_map/ppermute | solution.py:305
  61.1 11.1 %collective-permute-start.19 = (bf16[625,256]{1,0:T(8,128)(2,1)S(1)}, bf16[625,256]{1,0:T(8,128)(2,1)S(1)}, u32[]{:S(2)}, u32[]{:S(2)}) collective-permute-start(bf16[625,256]{1,0:T(8,128)(2,1)S(1)} %collective-permute-done.16.refs_2_), channel_id=1, source_target_pairs={{0,2},{1,3},{2,4},{3,5},{4,6},{5,7},{6,0},{7,1},{8,10},{9,11},{10,... | collective-permute-start | bytes 960008 | tf_op jit(solution)/shard_map/ppermute | solution.py:294
  69.5 4.8 %copy-start.10 = (s32[32,3]{0,1:T(4,128)S(1)}, s32[32,3]{0,1:T(4,128)}, u32[]{:S(2)}) copy-start(s32[32,3]{0,1:T(4,128)} %param.10) | copy-start | bytes 1156
  69.5 4.9 %copy-start.11 = (s32[32,4]{0,1:T(4,128)S(1)}, s32[32,4]{0,1:T(4,128)}, u32[]{:S(2)}) copy-start(s32[32,4]{0,1:T(4,128)} %param.11) | copy-start | bytes 1540
  72.2 1.5 %copy-start.8 = (bf16[2,1600,384]{2,1,0:T(8,128)(2,1)}, bf16[2,1600,384]{2,1,0:T(8,128)(2,1)S(1)}, u32[]{:S(2)}) copy-start(bf16[2,1600,384]{2,1,0:T(8,128)(2,1)S(1)} %collective-permute-done.20.refs_7_) | copy-start | bytes 7372804
  72.2 7.0 %collective-permute-start.21 = (bf16[2,1600,384]{2,1,0:T(8,128)(2,1)}, bf16[2,1600,384]{2,1,0:T(8,128)(2,1)}, u32[]{:S(2)}, u32[]{:S(2)}) collective-permute-start(bf16[2,1600,384]{2,1,0:T(8,128)(2,1)} %shard_map.76.refs_4_), channel_id=1, source_target_pairs={{0,1},{1,0},{2,3},{3,2},{4,5},{5,4},{6,7},{7,6},{8,9},{9,8},{10,11... | collective-permute-start | bytes 7372808 | tf_op jit(solution)/shard_map/ppermute | solution.py:291
  73.7 5.5 %collective-permute-start.22 = (bf16[8,800,128]{2,1,0:T(8,128)(2,1)S(1)}, bf16[8,800,128]{2,1,0:T(8,128)(2,1)S(1)}, u32[]{:S(2)}, u32[]{:S(2)}) collective-permute-start(bf16[8,800,128]{2,1,0:T(8,128)(2,1)S(1)} %shard_map.77.refs_8_), channel_id=1, source_target_pairs={{0,1},{1,0},{2,3},{3,2},{4,5},{5,4},{6,7},{7,6},{8,9},{9,8},{10,11... | collective-permute-start | bytes 4915208 | tf_op jit(solution)/shard_map/ppermute | solution.py:291
  79.3 1.7 %copy-start.1 = (bf16[2,1600,384]{2,1,0:T(8,128)(2,1)S(1)}, bf16[2,1600,384]{2,1,0:T(8,128)(2,1)}, u32[]{:S(2)}) copy-start(bf16[2,1600,384]{2,1,0:T(8,128)(2,1)} %copy-done) | copy-start | bytes 7372804
  90.3 30.5 %collective-permute-start.24 = (bf16[2,625,128]{2,1,0:T(8,128)(2,1)S(1)}, bf16[2,625,128]{2,1,0:T(8,128)(2,1)S(1)}, u32[]{:S(2)}, u32[]{:S(2)}) collective-permute-start(bf16[2,625,128]{2,1,0:T(8,128)(2,1)S(1)} %bitcast.26), channel_id=1, source_target_pairs={{0,4},{1,5},{2,6},{3,7},{4,0},{5,1},{6,2},{7,3},{8,12},{9,13},{10,... | collective-permute-start | bytes 960008 | tf_op jit(solution)/shard_map/ppermute | solution.py:294
  99.7 21.1 %collective-permute-start.23 = (bf16[2,625,128]{2,1,0:T(8,128)(2,1)S(1)}, bf16[2,625,128]{2,1,0:T(8,128)(2,1)S(1)}, u32[]{:S(2)}, u32[]{:S(2)}) collective-permute-start(bf16[2,625,128]{2,1,0:T(8,128)(2,1)S(1)} %bitcast.27), channel_id=1, source_target_pairs={{0,6},{1,7},{2,0},{3,1},{4,2},{5,3},{6,4},{7,5},{8,14},{9,15},{10,... | collective-permute-start | bytes 960008 | tf_op jit(solution)/shard_map/ppermute | solution.py:294
  110.2 11.2 %copy-start.9 = (f32[2,128,625]{1,0,2:T(2,128)S(1)}, f32[2,128,625]{1,0,2:T(2,128)}, u32[]{:S(2)}) copy-start(f32[2,128,625]{1,0,2:T(2,128)} %param.9) | copy-start | bytes 1920004
  110.2 11.2 %collective-permute-start.25 = (bf16[2,625,128]{2,1,0:T(8,128)(2,1)S(1)}, bf16[2,625,128]{2,1,0:T(8,128)(2,1)S(1)}, u32[]{:S(2)}, u32[]{:S(2)}) collective-permute-start(bf16[2,625,128]{2,1,0:T(8,128)(2,1)S(1)} %bitcast.28), channel_id=1, source_target_pairs={{0,2},{1,3},{2,4},{3,5},{4,6},{5,7},{6,0},{7,1},{8,10},{9,11},{10,... | collective-permute-start | bytes 960008 | tf_op jit(solution)/shard_map/ppermute | solution.py:294

commit v16 on v15

--- a/solution.py
+++ b/solution.py
@@ -309,27 +309,27 @@
         part0 = mine[0]
         a0, b0, part1 = first_side(part0), second_side(part0), around(mine[1], 1)
 
-        a0, b0, part0, part1, amp1, to3 = after((a0, b0, part0, part1, amp1, mine[3]), ())
-        q0, a1, b1, part3 = second_side(a0), first_side(part1), second_side(part1), around(to3, 3)
+        a0, b0, part0, part1, amp1, to2 = after((a0, b0, part0, part1, amp1, mine[2]), ())
+        q0, a1, b1, part2 = second_side(a0), first_side(part1), second_side(part1), around(to2, 2)
         forms0 = made_forms(part0, a0, b0, q0)
 
-        forms0, part1, a1, b1, part3, to2 = after((forms0, part1, a1, b1, part3, mine[2]), ())
-        q1, a3, b3, part2 = second_side(a1), first_side(part3), second_side(part3), around(to2, 2)
+        forms0, part1, a1, b1, part2, to3 = after((forms0, part1, a1, b1, part2, mine[3]), ())
+        q1, a2, b2, part3 = second_side(a1), first_side(part2), second_side(part2), around(to3, 3)
         far0 = other_core(forms0)
         forms1 = made_forms(part1, a1, b1, q1)
 
-        forms1, part3, a3, b3, part2, amp1, far0 = after((forms1, part3, a3, b3, part2, amp1, far0), ())
-        q3, a2, b2, amp2 = second_side(a3), first_side(part2), second_side(part2), around(amp1, 1)
+        forms1, part2, a2, b2, part3, amp1, far0 = after((forms1, part2, a2, b2, part3, amp1, far0), ())
+        q2, a3, b3, amp2 = second_side(a2), first_side(part3), second_side(part3), around(amp1, 1)
         far1 = other_core(forms1)
+        forms2 = made_forms(part2, a2, b2, q2)
+
+        forms2, part3, a3, b3, amp2, far1 = after((forms2, part3, a3, b3, amp2, far1), ())
+        q3, amp3 = second_side(a3), around(amp2, 1)
+        far2 = other_core(forms2)
         forms3 = made_forms(part3, a3, b3, q3)
 
-        forms3, part2, a2, b2, amp2, far1 = after((forms3, part2, a2, b2, amp2, far1), ())
-        q2, amp3 = second_side(a2), around(amp2, 1)
+        forms3, amp3, far2 = after((forms3, amp3, far2), ())
         far3 = other_core(forms3)
-        forms2 = made_forms(part2, a2, b2, q2)
-
-        forms2, amp3, far3 = after((forms2, amp3, far3), ())
-        far2 = other_core(forms2)
         amps = prepare_amps([own, amp1, amp2, amp3], blocks_here, jnp.asarray(amp_matrix()))
         held = [forms0, far0, forms1, far1, forms2, far2, forms3, far3]
     else:

time: 123 us -> 121 us (0.984)
  waiting for transfers between devices: 37.1 us -> 34.8 us
    ppermute x9, waiting for transfers between devices: 16.9 us -> 12.3 us  [around(): lax.ppermute(x, 'task', [(c, (c + 2 * by) % task_count) for c in range(ta...]
    ppermute x8, waiting for transfers between devices: 15.4 us -> 17.7 us  [per_device(): second_side = lambda x: lax.ppermute(x, ('pair', 'task'), sides[1])]
  transfers between devices with their start and end apart: 26 -> 26, of which waited for: 11 -> 13; matrix products, arithmetic and copies ran while one was open for 3% -> 3% of each run, Pallas kernels for 33% -> 34%
where the time goes in v16:
time: 121 us
  Pallas kernels  50.4 us (42%)
  waiting for transfers between devices  34.8 us (29%)
  starting transfers between devices  25.4 us (21%)
  local copies, waits for them, and re-layouts  9.5 us (8%)
    pallas_call x4, Pallas kernels, ladders(): pl.pallas_call(functools.partial(ladder_kernel, find, made, len(tiles)),...  37.5 us
    ppermute x8, waiting for transfers between devices, per_device(): second_side = lambda x: lax.ppermute(x, ('pair', 'task'), sides[1])  17.7 us
    ppermute x9, waiting for transfers between devices, around(): lax.ppermute(x, 'task', [(c, (c + 2 * by) % task_count) for c in range(ta...  12.3 us
    pallas_call x4, Pallas kernels, prepare(): pl.pallas_call(prepare_kernel, out_shape=jax.ShapeDtypeStruct((count, mat...  11.4 us
    ppermute x9, starting transfers between devices, around(): lax.ppermute(x, 'task', [(c, (c + 2 * by) % task_count) for c in range(ta...  10.3 us
    ppermute x8, starting transfers between devices, per_device(): second_side = lambda x: lax.ppermute(x, ('pair', 'task'), sides[1])  9.58 us
    unnamed x29, local copies, waits for them, and re-layouts  8.2 us
    ppermute x4, starting transfers between devices, per_device(): first_side = lambda x: lax.ppermute(x, ('pair', 'task'), sides[0])  4.93 us
  transfers between devices with their start and end apart: 26, of which 13 were waited for; matrix products, arithmetic and copies ran while one was open for 3% of the time, Pallas kernels for 34%

profile of v16, /device:TPU:0, one launch (start us, length us, event | category | flops | bytes accessed | tf_op | source)
XLA Modules:
  0.0 120.6 jit_solution(1066184729229310845)
XLA Ops:
  0.0 1.2 %pad = bf16[632,2,128]{2,1,0:T(2,128)(2,1)S(1)} pad(bf16[625,2,128]{2,1,0:T(2,128)(2,1)} %bitcast.31, bf16[]{:T(256)} %constant.64), padding=0_7x0_0x0_0 | pad | bytes 643586
  1.3 3.1 %collective-permute-start.3 = (bf16[625,256]{1,0:T(8,128)(2,1)S(1)}, bf16[625,256]{1,0:T(8,128)(2,1)S(1)}, u32[]{:S(2)}, u32[]{:S(2)}) collective-permute-start(bf16[625,256]{1,0:T(8,128)(2,1)S(1)} %bitcast.24), channel_id=1, source_target_pairs={{0,2},{1,3},{2,4},{3,5},{4,6},{5,7},{6,0},{7,1},{8,10},{9,11},{10,... | collective-permute-start | bytes 960008 | tf_op jit(solution)/shard_map/ppermute | solution.py:294
  4.4 3.3 %copy.22 = bf16[2,384,625]{2,1,0:T(8,128)(2,1)S(1)} copy(bf16[2,384,625]{1,0,2:T(2,128)(2,1)} %param.7) | data formatting | bytes 1920000 | tf_op args[0]
  7.7 0.1 dynamic-slice_bitcast_fusion
  7.9 1.6 %collective-permute-start.2 = (bf16[2,96,625]{2,1,0:T(8,128)(2,1)S(1)}, bf16[2,96,625]{2,1,0:T(8,128)(2,1)S(1)}, u32[]{:S(2)}, u32[]{:S(2)}) collective-permute-start(bf16[2,96,625]{2,1,0:T(8,128)(2,1)S(1)} %get-tuple-element.63), channel_id=1, source_target_pairs={{0,2},{1,3},{2,4},{3,5},{4,6},{5,7},{6,0},{7,1},{8,10},{9,11},{10,... | collective-permute-start | bytes 720008 | tf_op jit(solution)/shard_map/ppermute | solution.py:294
  9.5 1.5 %collective-permute-start.1 = (bf16[2,96,625]{2,1,0:T(8,128)(2,1)S(1)}, bf16[2,96,625]{2,1,0:T(8,128)(2,1)S(1)}, u32[]{:S(2)}, u32[]{:S(2)}) collective-permute-start(bf16[2,96,625]{2,1,0:T(8,128)(2,1)S(1)} %get-tuple-element.33.refs_0_), channel_id=1, source_target_pairs={{0,16},{1,9},{2,18},{3,11},{4,20},{5,13},{6,22},{7,15},{8,24},{9,1... | collective-permute-start | bytes 720008 | tf_op jit(solution)/shard_map/ppermute | solution.py:305
  11.0 1.5 %collective-permute-start = (bf16[2,96,625]{2,1,0:T(8,128)(2,1)S(1)}, bf16[2,96,625]{2,1,0:T(8,128)(2,1)S(1)}, u32[]{:S(2)}, u32[]{:S(2)}) collective-permute-start(bf16[2,96,625]{2,1,0:T(8,128)(2,1)S(1)} %get-tuple-element.33.refs_0_), channel_id=1, source_target_pairs={{0,8},{1,17},{2,10},{3,19},{4,12},{5,21},{6,14},{7,23},{8,0},{9,25... | collective-permute-start | bytes 720008 | tf_op jit(solution)/shard_map/ppermute | solution.py:304
  12.5 6.8 %collective-permute-done.2.refs_0_ = bf16[2,96,625]{2,1,0:T(8,128)(2,1)S(1)} collective-permute-done((bf16[2,96,625]{2,1,0:T(8,128)(2,1)S(1)}, bf16[2,96,625]{2,1,0:T(8,128)(2,1)S(1)}, u32[]{:S(2)}, u32[]{:S(2)}) %collective-permute-start.2) | collective-permute-done | bytes 240032 | tf_op jit(solution)/shard_map/ppermute | solution.py:294
  19.3 0.0 collective-permute-done.1.refs_2_
  19.3 1.6 %collective-permute-start.4 = (bf16[2,96,625]{2,1,0:T(8,128)(2,1)S(1)}, bf16[2,96,625]{2,1,0:T(8,128)(2,1)S(1)}, u32[]{:S(2)}, u32[]{:S(2)}) collective-permute-start(bf16[2,96,625]{2,1,0:T(8,128)(2,1)S(1)} %collective-permute-done.refs_1_), channel_id=1, source_target_pairs={{0,16},{1,9},{2,18},{3,11},{4,20},{5,13},{6,22},{7,15},{8,24},{9,1... | collective-permute-start | bytes 720008 | tf_op jit(solution)/shard_map/ppermute | solution.py:305
  20.9 0.7 collective-permute-start.7
  21.6 0.5 collective-permute-start.6
  22.1 1.5 %collective-permute-start.5 = (bf16[2,96,625]{2,1,0:T(8,128)(2,1)S(1)}, bf16[2,96,625]{2,1,0:T(8,128)(2,1)S(1)}, u32[]{:S(2)}, u32[]{:S(2)}) collective-permute-start(bf16[2,96,625]{2,1,0:T(8,128)(2,1)S(1)} %collective-permute-done.2.refs_0_), channel_id=1, source_target_pairs={{0,8},{1,17},{2,10},{3,19},{4,12},{5,21},{6,14},{7,23},{8,0},{9,25... | collective-permute-start | bytes 720008 | tf_op jit(solution)/shard_map/ppermute | solution.py:304
  23.6 4.6 %collective-permute-done.4.refs_3_ = bf16[2,96,625]{2,1,0:T(8,128)(2,1)S(1)} collective-permute-done((bf16[2,96,625]{2,1,0:T(8,128)(2,1)S(1)}, bf16[2,96,625]{2,1,0:T(8,128)(2,1)S(1)}, u32[]{:S(2)}, u32[]{:S(2)}) %collective-permute-start.4) | collective-permute-done | bytes 240032 | tf_op jit(solution)/shard_map/ppermute | solution.py:305
  28.2 1.6 %copy-done.5 = bf16[1600,625]{1,0:T(8,128)(2,1)S(1)} copy-done((bf16[1600,625]{1,0:T(8,128)(2,1)S(1)}, bf16[1600,625]{1,0:T(8,128)(2,1)}, u32[]{:S(2)}) %copy-start.5) | copy-done | bytes 2000024
  29.7 2.6 %shard_map.73.refs_0_ = bf16[2,1600,384]{2,1,0:T(8,128)(2,1)S(1)} custom-call(s32[1]{0:T(128)} %bitcast.column_ref, bf16[2,96,625]{2,1,0:T(8,128)(2,1)S(1)} %get-tuple-element.33.refs_0_, bf16[2,96,625]{2,1,0:T(8,128)(2,1)S(1)} %collective-permute-done.refs_1_, bf16[2,96,625]{2,1,0:T(8,128)(2,1)S(1)} %collective-permute-done.1.refs_2_, ...), custom_call_target="tpu_custom_call" | custom-call | flops 1536000000 | bytes 3417600 | tf_op jit(solution)/shard_map/pallas_call | solution.py:72
  32.4 0.3 collective-permute-done.7.refs_0_
  32.7 0.0 collective-permute-done.6.refs_2_
  32.7 0.0 collective-permute-start.12
  32.7 1.6 %collective-permute-start.8 = (bf16[2,96,625]{2,1,0:T(8,128)(2,1)S(1)}, bf16[2,96,625]{2,1,0:T(8,128)(2,1)S(1)}, u32[]{:S(2)}, u32[]{:S(2)}) collective-permute-start(bf16[2,96,625]{2,1,0:T(8,128)(2,1)S(1)} %collective-permute-done.5.refs_1_), channel_id=1, source_target_pairs={{0,16},{1,9},{2,18},{3,11},{4,20},{5,13},{6,22},{7,15},{8,24},{9,1... | collective-permute-start | bytes 720008 | tf_op jit(solution)/shard_map/ppermute | solution.py:305
  34.3 2.5 %collective-permute-start.11 = (bf16[2,96,625]{2,1,0:T(8,128)(2,1)S(1)}, bf16[2,96,625]{2,1,0:T(8,128)(2,1)S(1)}, u32[]{:S(2)}, u32[]{:S(2)}) collective-permute-start(bf16[2,96,625]{2,1,0:T(8,128)(2,1)S(1)} %get-tuple-element.43), channel_id=1, source_target_pairs={{0,6},{1,7},{2,0},{3,1},{4,2},{5,3},{6,4},{7,5},{8,14},{9,15},{10,... | collective-permute-start | bytes 720008 | tf_op jit(solution)/shard_map/ppermute | solution.py:294
  36.8 0.5 collective-permute-start.10
  37.3 0.6 collective-permute-start.9
  37.9 1.0 collective-permute-done.8.refs_3_
  39.0 2.6 %shard_map.74.refs_2_ = bf16[2,1600,384]{2,1,0:T(8,128)(2,1)S(1)} custom-call(s32[1]{0:T(128)} %bitcast.column_ref, bf16[2,96,625]{2,1,0:T(8,128)(2,1)S(1)} %collective-permute-done.2.refs_0_, bf16[2,96,625]{2,1,0:T(8,128)(2,1)S(1)} %collective-permute-done.5.refs_1_, bf16[2,96,625]{2,1,0:T(8,128)(2,1)S(1)} %collective-permute-done.6.refs_2_, ...), custom_call_target="tpu_custom_call" | custom-call | flops 1536000000 | bytes 3417600 | tf_op jit(solution)/shard_map/pallas_call | solution.py:72
  41.6 0.0 copy-start.6
  41.7 0.8 collective-permute-done.11.refs_0_
  42.4 2.3 %collective-permute-done.10.refs_2_ = bf16[2,96,625]{2,1,0:T(8,128)(2,1)S(1)} collective-permute-done((bf16[2,96,625]{2,1,0:T(8,128)(2,1)S(1)}, bf16[2,96,625]{2,1,0:T(8,128)(2,1)S(1)}, u32[]{:S(2)}, u32[]{:S(2)}) %collective-permute-start.10) | collective-permute-done | bytes 240032 | tf_op jit(solution)/shard_map/ppermute | solution.py:305
  44.7 0.0 collective-permute-done.9.refs_1_
  44.7 0.0 collective-permute-done.12.refs_1_
  44.8 0.1 collective-permute-start.17
  44.8 1.3 %collective-permute-start.13 = (bf16[2,96,625]{2,1,0:T(8,128)(2,1)S(1)}, bf16[2,96,625]{2,1,0:T(8,128)(2,1)S(1)}, u32[]{:S(2)}, u32[]{:S(2)}) collective-permute-start(bf16[2,96,625]{2,1,0:T(8,128)(2,1)S(1)} %collective-permute-done.9.refs_1_), channel_id=1, source_target_pairs={{0,16},{1,9},{2,18},{3,11},{4,20},{5,13},{6,22},{7,15},{8,24},{9,1... | collective-permute-start | bytes 720008 | tf_op jit(solution)/shard_map/ppermute | solution.py:305
  46.1 0.1 copy-done.7
  46.2 0.0 collective-permute-start.16
  46.2 1.2 %collective-permute-start.15 = (bf16[2,96,625]{2,1,0:T(8,128)(2,1)S(1)}, bf16[2,96,625]{2,1,0:T(8,128)(2,1)S(1)}, u32[]{:S(2)}, u32[]{:S(2)}) collective-permute-start(bf16[2,96,625]{2,1,0:T(8,128)(2,1)S(1)} %collective-permute-done.11.refs_0_), channel_id=1, source_target_pairs={{0,16},{1,9},{2,18},{3,11},{4,20},{5,13},{6,22},{7,15},{8,24},{9,1... | collective-permute-start | bytes 720008 | tf_op jit(solution)/shard_map/ppermute | solution.py:305
  47.5 1.3 %collective-permute-start.14 = (bf16[2,96,625]{2,1,0:T(8,128)(2,1)S(1)}, bf16[2,96,625]{2,1,0:T(8,128)(2,1)S(1)}, u32[]{:S(2)}, u32[]{:S(2)}) collective-permute-start(bf16[2,96,625]{2,1,0:T(8,128)(2,1)S(1)} %collective-permute-done.11.refs_0_), channel_id=1, source_target_pairs={{0,8},{1,17},{2,10},{3,19},{4,12},{5,21},{6,14},{7,23},{8,0},{9,25... | collective-permute-start | bytes 720008 | tf_op jit(solution)/shard_map/ppermute | solution.py:304
  48.8 4.0 %collective-permute-done.13.refs_3_ = bf16[2,96,625]{2,1,0:T(8,128)(2,1)S(1)} collective-permute-done((bf16[2,96,625]{2,1,0:T(8,128)(2,1)S(1)}, bf16[2,96,625]{2,1,0:T(8,128)(2,1)S(1)}, u32[]{:S(2)}, u32[]{:S(2)}) %collective-permute-start.13) | collective-permute-done | bytes 240032 | tf_op jit(solution)/shard_map/ppermute | solution.py:305
  52.8 2.6 %shard_map.75.refs_4_ = bf16[2,1600,384]{2,1,0:T(8,128)(2,1)S(1)} custom-call(s32[1]{0:T(128)} %bitcast.column_ref, bf16[2,96,625]{2,1,0:T(8,128)(2,1)S(1)} %collective-permute-done.7.refs_0_, bf16[2,96,625]{2,1,0:T(8,128)(2,1)S(1)} %collective-permute-done.9.refs_1_, bf16[2,96,625]{2,1,0:T(8,128)(2,1)S(1)} %collective-permute-done.10.refs_2_, ...), custom_call_target="tpu_custom_call" | custom-call | flops 1536000000 | bytes 3417600 | tf_op jit(solution)/shard_map/pallas_call | solution.py:72
  55.5 0.0 copy-start.4
  55.5 0.9 collective-permute-done.15.refs_2_
  56.4 0.0 collective-permute-done.14.refs_1_
  56.4 1.1 collective-permute-done.16.refs_2_
  57.5 0.0 collective-permute-done.17.refs_3_
  57.5 1.4 %collective-permute-start.18 = (bf16[2,96,625]{2,1,0:T(8,128)(2,1)S(1)}, bf16[2,96,625]{2,1,0:T(8,128)(2,1)S(1)}, u32[]{:S(2)}, u32[]{:S(2)}) collective-permute-start(bf16[2,96,625]{2,1,0:T(8,128)(2,1)S(1)} %collective-permute-done.14.refs_1_), channel_id=1, source_target_pairs={{0,16},{1,9},{2,18},{3,11},{4,20},{5,13},{6,22},{7,15},{8,24},{9,1... | collective-permute-start | bytes 720008 | tf_op jit(solution)/shard_map/ppermute | solution.py:305
  58.9 4.8 %collective-permute-done.18.refs_3_ = bf16[2,96,625]{2,1,0:T(8,128)(2,1)S(1)} collective-permute-done((bf16[2,96,625]{2,1,0:T(8,128)(2,1)S(1)}, bf16[2,96,625]{2,1,0:T(8,128)(2,1)S(1)}, u32[]{:S(2)}, u32[]{:S(2)}) %collective-permute-start.18) | collective-permute-done | bytes 240032 | tf_op jit(solution)/shard_map/ppermute | solution.py:305
  63.7 3.5 %shard_map.76.refs_6_ = bf16[2,1600,384]{2,1,0:T(8,128)(2,1)} custom-call(s32[1]{0:T(128)} %bitcast.column_ref, bf16[2,96,625]{2,1,0:T(8,128)(2,1)S(1)} %collective-permute-done.11.refs_0_, bf16[2,96,625]{2,1,0:T(8,128)(2,1)S(1)} %collective-permute-done.14.refs_1_, bf16[2,96,625]{2,1,0:T(8,128)(2,1)S(1)} %collective-permute-done.15.refs_2_, ...), custom_call_target="tpu_custom_call" | custom-call | flops 1536000000 | bytes 3417600 | tf_op jit(solution)/shard_map/pallas_call | solution.py:72
  67.2 2.8 %collective-permute-done.19.refs_3_ = bf16[625,256]{1,0:T(8,128)(2,1)S(1)} collective-permute-done((bf16[625,256]{1,0:T(8,128)(2,1)S(1)}, bf16[625,256]{1,0:T(8,128)(2,1)S(1)}, u32[]{:S(2)}, u32[]{:S(2)}) %collective-permute-start.19) | collective-permute-done | bytes 320032 | tf_op jit(solution)/shard_map/ppermute | solution.py:294
  70.0 1.4 %shard_map.77.refs_8_ = bf16[8,800,128]{2,1,0:T(8,128)(2,1)S(1)} custom-call(bf16[800,625]{1,0:T(8,128)(2,1)S(1)} %copy-done.4, bf16[625,256]{1,0:T(8,128)(2,1)S(1)} %bitcast.25, bf16[625,256]{1,0:T(8,128)(2,1)S(1)} %collective-permute-done.3.refs_1_, bf16[625,256]{1,0:T(8,128)(2,1)S(1)} %collective-permute-done.16.refs_2_, ...), custom_call_target="tpu_custom_call" | custom-call | flops 1024000000 | bytes 2560000 | tf_op jit(solution)/shard_map/pallas_call | solution.py:103
  71.4 0.6 collective-permute-start.22
  72.0 0.1 copy.23.owners_ref
  72.1 0.1 copy.24.local_ref
  72.2 4.8 %collective-permute-done.22.refs_9_ = bf16[8,800,128]{2,1,0:T(8,128)(2,1)S(1)} collective-permute-done((bf16[8,800,128]{2,1,0:T(8,128)(2,1)S(1)}, bf16[8,800,128]{2,1,0:T(8,128)(2,1)S(1)}, u32[]{:S(2)}, u32[]{:S(2)}) %collective-permute-start.22) | collective-permute-done | bytes 1638432 | tf_op jit(solution)/shard_map/ppermute | solution.py:291
  77.0 1.7 %copy-done.1 = bf16[2,1600,384]{2,1,0:T(8,128)(2,1)S(1)} copy-done((bf16[2,1600,384]{2,1,0:T(8,128)(2,1)S(1)}, bf16[2,1600,384]{2,1,0:T(8,128)(2,1)}, u32[]{:S(2)}) %copy-start.1) | copy-done | bytes 2457624
  78.7 9.3 %shard_map.79 = bf16[1,2,625,128]{3,2,1,0:T(8,128)(2,1)S(1)} custom-call(s32[1]{0:T(128)} %bitcast.column_ref, s32[32,3]{1,0:T(8,128)S(1)} %copy.23.owners_ref, s32[32,4]{1,0:T(8,128)S(1)} %copy.24.local_ref, bf16[2,1600,384]{2,1,0:T(8,128)(2,1)S(1)} %copy-done.1, bf16[2,1600,384]{2,1,0:T(8,128)(2,1)} %copy-done.7, bf16[2,1600,384]{2,1,0:T(8,128)(2,1)} %copy-done.2, ...), custom_call_target="tpu_custom_call" | custom-call | flops 2936012800 | bytes 6553600 | tf_op jit(solution)/shard_map/pallas_call | solution.py:257
  88.0 0.1 collective-permute-start.24
  88.1 9.6 %shard_map.78 = bf16[1,2,625,128]{3,2,1,0:T(8,128)(2,1)S(1)} custom-call(s32[1]{0:T(128)} %bitcast.column_ref, s32[32,3]{1,0:T(8,128)S(1)} %copy.23.owners_ref, s32[32,4]{1,0:T(8,128)S(1)} %copy.24.local_ref, bf16[2,1600,384]{2,1,0:T(8,128)(2,1)S(1)} %copy-done.1, bf16[2,1600,384]{2,1,0:T(8,128)(2,1)} %copy-done.7, bf16[2,1600,384]{2,1,0:T(8,128)(2,1)} %copy-done.2, ...), custom_call_target="tpu_custom_call" | custom-call | flops 2936012800 | bytes 6553600 | tf_op jit(solution)/shard_map/pallas_call | solution.py:257
  97.7 0.8 collective-permute-start.23
  98.4 9.3 %shard_map.80 = bf16[1,2,625,128]{3,2,1,0:T(8,128)(2,1)S(1)} custom-call(s32[1]{0:T(128)} %bitcast.column_ref, s32[32,3]{1,0:T(8,128)S(1)} %copy.23.owners_ref, s32[32,4]{1,0:T(8,128)S(1)} %copy.24.local_ref, bf16[2,1600,384]{2,1,0:T(8,128)(2,1)S(1)} %copy-done.1, bf16[2,1600,384]{2,1,0:T(8,128)(2,1)} %copy-done.7, bf16[2,1600,384]{2,1,0:T(8,128)(2,1)} %copy-done.2, ...), custom_call_target="tpu_custom_call" | custom-call | flops 2936012800 | bytes 6553600 | tf_op jit(solution)/shard_map/pallas_call | solution.py:257
  107.8 0.0 copy-start.9
  107.8 1.5 %collective-permute-start.25 = (bf16[2,625,128]{2,1,0:T(8,128)(2,1)S(1)}, bf16[2,625,128]{2,1,0:T(8,128)(2,1)S(1)}, u32[]{:S(2)}, u32[]{:S(2)}) collective-permute-start(bf16[2,625,128]{2,1,0:T(8,128)(2,1)S(1)} %bitcast.28), channel_id=1, source_target_pairs={{0,2},{1,3},{2,4},{3,5},{4,6},{5,7},{6,0},{7,1},{8,10},{9,11},{10,... | collective-permute-start | bytes 960008 | tf_op jit(solution)/shard_map/ppermute | solution.py:294
  109.3 9.3 %shard_map.81 = bf16[1,2,625,128]{3,2,1,0:T(8,128)(2,1)S(1)} custom-call(s32[1]{0:T(128)} %bitcast.column_ref, s32[32,3]{1,0:T(8,128)S(1)} %copy.23.owners_ref, s32[32,4]{1,0:T(8,128)S(1)} %copy.24.local_ref, bf16[2,1600,384]{2,1,0:T(8,128)(2,1)S(1)} %copy-done.1, bf16[2,1600,384]{2,1,0:T(8,128)(2,1)} %copy-done.7, bf16[2,1600,384]{2,1,0:T(8,128)(2,1)} %copy-done.2, ...), custom_call_target="tpu_custom_call" | custom-call | flops 2936012800 | bytes 6553600 | tf_op jit(solution)/shard_map/pallas_call | solution.py:257
  118.7 0.5 collective-permute-done.25
  119.2 0.2 fusion.1
  119.4 1.2 copy.32
  (29 shorter events, 0.1 us)
Async XLA Ops:
  1.3 18.0 %collective-permute-start.3 = (bf16[625,256]{1,0:T(8,128)(2,1)S(1)}, bf16[625,256]{1,0:T(8,128)(2,1)S(1)}, u32[]{:S(2)}, u32[]{:S(2)}) collective-permute-start(bf16[625,256]{1,0:T(8,128)(2,1)S(1)} %bitcast.24), channel_id=1, source_target_pairs={{0,2},{1,3},{2,4},{3,5},{4,6},{5,7},{6,0},{7,1},{8,10},{9,11},{10,... | collective-permute-start | bytes 960008 | tf_op jit(solution)/shard_map/ppermute | solution.py:294
  7.9 11.4 %collective-permute-start.2 = (bf16[2,96,625]{2,1,0:T(8,128)(2,1)S(1)}, bf16[2,96,625]{2,1,0:T(8,128)(2,1)S(1)}, u32[]{:S(2)}, u32[]{:S(2)}) collective-permute-start(bf16[2,96,625]{2,1,0:T(8,128)(2,1)S(1)} %get-tuple-element.63), channel_id=1, source_target_pairs={{0,2},{1,3},{2,4},{3,5},{4,6},{5,7},{6,0},{7,1},{8,10},{9,11},{10,... | collective-permute-start | bytes 720008 | tf_op jit(solution)/shard_map/ppermute | solution.py:294
  9.5 9.8 %collective-permute-start.1 = (bf16[2,96,625]{2,1,0:T(8,128)(2,1)S(1)}, bf16[2,96,625]{2,1,0:T(8,128)(2,1)S(1)}, u32[]{:S(2)}, u32[]{:S(2)}) collective-permute-start(bf16[2,96,625]{2,1,0:T(8,128)(2,1)S(1)} %get-tuple-element.33.refs_0_), channel_id=1, source_target_pairs={{0,16},{1,9},{2,18},{3,11},{4,20},{5,13},{6,22},{7,15},{8,24},{9,1... | collective-permute-start | bytes 720008 | tf_op jit(solution)/shard_map/ppermute | solution.py:305
  11.0 8.3 %collective-permute-start = (bf16[2,96,625]{2,1,0:T(8,128)(2,1)S(1)}, bf16[2,96,625]{2,1,0:T(8,128)(2,1)S(1)}, u32[]{:S(2)}, u32[]{:S(2)}) collective-permute-start(bf16[2,96,625]{2,1,0:T(8,128)(2,1)S(1)} %get-tuple-element.33.refs_0_), channel_id=1, source_target_pairs={{0,8},{1,17},{2,10},{3,19},{4,12},{5,21},{6,14},{7,23},{8,0},{9,25... | collective-permute-start | bytes 720008 | tf_op jit(solution)/shard_map/ppermute | solution.py:304
  19.3 8.9 %collective-permute-start.4 = (bf16[2,96,625]{2,1,0:T(8,128)(2,1)S(1)}, bf16[2,96,625]{2,1,0:T(8,128)(2,1)S(1)}, u32[]{:S(2)}, u32[]{:S(2)}) collective-permute-start(bf16[2,96,625]{2,1,0:T(8,128)(2,1)S(1)} %collective-permute-done.refs_1_), channel_id=1, source_target_pairs={{0,16},{1,9},{2,18},{3,11},{4,20},{5,13},{6,22},{7,15},{8,24},{9,1... | collective-permute-start | bytes 720008 | tf_op jit(solution)/shard_map/ppermute | solution.py:305
  20.9 11.8 %collective-permute-start.7 = (bf16[2,96,625]{2,1,0:T(8,128)(2,1)S(1)}, bf16[2,96,625]{2,1,0:T(8,128)(2,1)S(1)}, u32[]{:S(2)}, u32[]{:S(2)}) collective-permute-start(bf16[2,96,625]{2,1,0:T(8,128)(2,1)S(1)} %get-tuple-element.37), channel_id=1, source_target_pairs={{0,4},{1,5},{2,6},{3,7},{4,0},{5,1},{6,2},{7,3},{8,12},{9,13},{10,... | collective-permute-start | bytes 720008 | tf_op jit(solution)/shard_map/ppermute | solution.py:294
  21.6 11.1 %collective-permute-start.6 = (bf16[2,96,625]{2,1,0:T(8,128)(2,1)S(1)}, bf16[2,96,625]{2,1,0:T(8,128)(2,1)S(1)}, u32[]{:S(2)}, u32[]{:S(2)}) collective-permute-start(bf16[2,96,625]{2,1,0:T(8,128)(2,1)S(1)} %collective-permute-done.2.refs_0_), channel_id=1, source_target_pairs={{0,16},{1,9},{2,18},{3,11},{4,20},{5,13},{6,22},{7,15},{8,24},{9,1... | collective-permute-start | bytes 720008 | tf_op jit(solution)/shard_map/ppermute | solution.py:305
  22.1 10.6 %collective-permute-start.5 = (bf16[2,96,625]{2,1,0:T(8,128)(2,1)S(1)}, bf16[2,96,625]{2,1,0:T(8,128)(2,1)S(1)}, u32[]{:S(2)}, u32[]{:S(2)}) collective-permute-start(bf16[2,96,625]{2,1,0:T(8,128)(2,1)S(1)} %collective-permute-done.2.refs_0_), channel_id=1, source_target_pairs={{0,8},{1,17},{2,10},{3,19},{4,12},{5,21},{6,14},{7,23},{8,0},{9,25... | collective-permute-start | bytes 720008 | tf_op jit(solution)/shard_map/ppermute | solution.py:304
  28.2 1.6 %copy-start.5 = (bf16[1600,625]{1,0:T(8,128)(2,1)S(1)}, bf16[1600,625]{1,0:T(8,128)(2,1)}, u32[]{:S(2)}) copy-start(bf16[1600,625]{1,0:T(8,128)(2,1)} %constant.59.clone.refs_4_) | copy-start | bytes 6000004
  32.4 9.2 %copy-start = (bf16[2,1600,384]{2,1,0:T(8,128)(2,1)}, bf16[2,1600,384]{2,1,0:T(8,128)(2,1)S(1)}, u32[]{:S(2)}) copy-start(bf16[2,1600,384]{2,1,0:T(8,128)(2,1)S(1)} %shard_map.73.refs_0_) | copy-start | bytes 7372804
  32.7 12.0 %collective-permute-start.12 = (bf16[2,1600,384]{2,1,0:T(8,128)(2,1)S(1)}, bf16[2,1600,384]{2,1,0:T(8,128)(2,1)S(1)}, u32[]{:S(2)}, u32[]{:S(2)}) collective-permute-start(bf16[2,1600,384]{2,1,0:T(8,128)(2,1)S(1)} %shard_map.73.refs_0_), channel_id=1, source_target_pairs={{0,1},{1,0},{2,3},{3,2},{4,5},{5,4},{6,7},{7,6},{8,9},{9,8},{10,11... | collective-permute-start | bytes 7372808 | tf_op jit(solution)/shard_map/ppermute | solution.py:291
  32.7 6.3 %collective-permute-start.8 = (bf16[2,96,625]{2,1,0:T(8,128)(2,1)S(1)}, bf16[2,96,625]{2,1,0:T(8,128)(2,1)S(1)}, u32[]{:S(2)}, u32[]{:S(2)}) collective-permute-start(bf16[2,96,625]{2,1,0:T(8,128)(2,1)S(1)} %collective-permute-done.5.refs_1_), channel_id=1, source_target_pairs={{0,16},{1,9},{2,18},{3,11},{4,20},{5,13},{6,22},{7,15},{8,24},{9,1... | collective-permute-start | bytes 720008 | tf_op jit(solution)/shard_map/ppermute | solution.py:305
  34.3 8.1 %collective-permute-start.11 = (bf16[2,96,625]{2,1,0:T(8,128)(2,1)S(1)}, bf16[2,96,625]{2,1,0:T(8,128)(2,1)S(1)}, u32[]{:S(2)}, u32[]{:S(2)}) collective-permute-start(bf16[2,96,625]{2,1,0:T(8,128)(2,1)S(1)} %get-tuple-element.43), channel_id=1, source_target_pairs={{0,6},{1,7},{2,0},{3,1},{4,2},{5,3},{6,4},{7,5},{8,14},{9,15},{10,... | collective-permute-start | bytes 720008 | tf_op jit(solution)/shard_map/ppermute | solution.py:294
  36.8 8.0 %collective-permute-start.10 = (bf16[2,96,625]{2,1,0:T(8,128)(2,1)S(1)}, bf16[2,96,625]{2,1,0:T(8,128)(2,1)S(1)}, u32[]{:S(2)}, u32[]{:S(2)}) collective-permute-start(bf16[2,96,625]{2,1,0:T(8,128)(2,1)S(1)} %collective-permute-done.7.refs_0_), channel_id=1, source_target_pairs={{0,16},{1,9},{2,18},{3,11},{4,20},{5,13},{6,22},{7,15},{8,24},{9,1... | collective-permute-start | bytes 720008 | tf_op jit(solution)/shard_map/ppermute | solution.py:305
  37.3 7.5 %collective-permute-start.9 = (bf16[2,96,625]{2,1,0:T(8,128)(2,1)S(1)}, bf16[2,96,625]{2,1,0:T(8,128)(2,1)S(1)}, u32[]{:S(2)}, u32[]{:S(2)}) collective-permute-start(bf16[2,96,625]{2,1,0:T(8,128)(2,1)S(1)} %collective-permute-done.7.refs_0_), channel_id=1, source_target_pairs={{0,8},{1,17},{2,10},{3,19},{4,12},{5,21},{6,14},{7,23},{8,0},{9,25... | collective-permute-start | bytes 720008 | tf_op jit(solution)/shard_map/ppermute | solution.py:304
  41.6 13.8 %copy-start.2 = (bf16[2,1600,384]{2,1,0:T(8,128)(2,1)}, bf16[2,1600,384]{2,1,0:T(8,128)(2,1)S(1)}, u32[]{:S(2)}) copy-start(bf16[2,1600,384]{2,1,0:T(8,128)(2,1)S(1)} %shard_map.74.refs_2_) | copy-start | bytes 7372804
  41.6 22.1 %copy-start.6 = (bf16[1600,625]{1,0:T(8,128)(2,1)S(1)}, bf16[1600,625]{1,0:T(8,128)(2,1)}, u32[]{:S(2)}) copy-start(bf16[1600,625]{1,0:T(8,128)(2,1)} %constant.59.clone.refs_4_) | copy-start | bytes 6000004
  44.8 1.5 %copy-start.7 = (bf16[2,1600,384]{2,1,0:T(8,128)(2,1)}, bf16[2,1600,384]{2,1,0:T(8,128)(2,1)S(1)}, u32[]{:S(2)}) copy-start(bf16[2,1600,384]{2,1,0:T(8,128)(2,1)S(1)} %collective-permute-done.12.refs_1_) | copy-start | bytes 7372804
  44.8 12.8 %collective-permute-start.17 = (bf16[2,1600,384]{2,1,0:T(8,128)(2,1)S(1)}, bf16[2,1600,384]{2,1,0:T(8,128)(2,1)}, u32[]{:S(2)}, u32[]{:S(2)}) collective-permute-start(bf16[2,1600,384]{2,1,0:T(8,128)(2,1)S(1)} %shard_map.74.refs_2_), channel_id=1, source_target_pairs={{0,1},{1,0},{2,3},{3,2},{4,5},{5,4},{6,7},{7,6},{8,9},{9,8},{10,11... | collective-permute-start | bytes 7372808 | tf_op jit(solution)/shard_map/ppermute | solution.py:291
  44.8 8.0 %collective-permute-start.13 = (bf16[2,96,625]{2,1,0:T(8,128)(2,1)S(1)}, bf16[2,96,625]{2,1,0:T(8,128)(2,1)S(1)}, u32[]{:S(2)}, u32[]{:S(2)}) collective-permute-start(bf16[2,96,625]{2,1,0:T(8,128)(2,1)S(1)} %collective-permute-done.9.refs_1_), channel_id=1, source_target_pairs={{0,16},{1,9},{2,18},{3,11},{4,20},{5,13},{6,22},{7,15},{8,24},{9,1... | collective-permute-start | bytes 720008 | tf_op jit(solution)/shard_map/ppermute | solution.py:305
  46.2 11.3 %collective-permute-start.16 = (bf16[625,256]{1,0:T(8,128)(2,1)S(1)}, bf16[625,256]{1,0:T(8,128)(2,1)S(1)}, u32[]{:S(2)}, u32[]{:S(2)}) collective-permute-start(bf16[625,256]{1,0:T(8,128)(2,1)S(1)} %collective-permute-done.3.refs_1_), channel_id=1, source_target_pairs={{0,2},{1,3},{2,4},{3,5},{4,6},{5,7},{6,0},{7,1},{8,10},{9,11},{10,... | collective-permute-start | bytes 960008 | tf_op jit(solution)/shard_map/ppermute | solution.py:294
  46.2 10.1 %collective-permute-start.15 = (bf16[2,96,625]{2,1,0:T(8,128)(2,1)S(1)}, bf16[2,96,625]{2,1,0:T(8,128)(2,1)S(1)}, u32[]{:S(2)}, u32[]{:S(2)}) collective-permute-start(bf16[2,96,625]{2,1,0:T(8,128)(2,1)S(1)} %collective-permute-done.11.refs_0_), channel_id=1, source_target_pairs={{0,16},{1,9},{2,18},{3,11},{4,20},{5,13},{6,22},{7,15},{8,24},{9,1... | collective-permute-start | bytes 720008 | tf_op jit(solution)/shard_map/ppermute | solution.py:305
  47.5 8.9 %collective-permute-start.14 = (bf16[2,96,625]{2,1,0:T(8,128)(2,1)S(1)}, bf16[2,96,625]{2,1,0:T(8,128)(2,1)S(1)}, u32[]{:S(2)}, u32[]{:S(2)}) collective-permute-start(bf16[2,96,625]{2,1,0:T(8,128)(2,1)S(1)} %collective-permute-done.11.refs_0_), channel_id=1, source_target_pairs={{0,8},{1,17},{2,10},{3,19},{4,12},{5,21},{6,14},{7,23},{8,0},{9,25... | collective-permute-start | bytes 720008 | tf_op jit(solution)/shard_map/ppermute | solution.py:304
  55.5 11.7 %copy-start.3 = (bf16[2,1600,384]{2,1,0:T(8,128)(2,1)}, bf16[2,1600,384]{2,1,0:T(8,128)(2,1)S(1)}, u32[]{:S(2)}) copy-start(bf16[2,1600,384]{2,1,0:T(8,128)(2,1)S(1)} %shard_map.75.refs_4_) | copy-start | bytes 7372804
  55.5 14.5 %copy-start.4 = (bf16[800,625]{1,0:T(8,128)(2,1)S(1)}, bf16[800,625]{1,0:T(8,128)(2,1)}, u32[]{:S(2)}) copy-start(bf16[800,625]{1,0:T(8,128)(2,1)} %constant.60.clone.matrix_ref) | copy-start | bytes 3000004
  57.5 12.4 %collective-permute-start.20 = (bf16[2,1600,384]{2,1,0:T(8,128)(2,1)S(1)}, bf16[2,1600,384]{2,1,0:T(8,128)(2,1)S(1)}, u32[]{:S(2)}, u32[]{:S(2)}) collective-permute-start(bf16[2,1600,384]{2,1,0:T(8,128)(2,1)S(1)} %shard_map.75.refs_4_), channel_id=1, source_target_pairs={{0,1},{1,0},{2,3},{3,2},{4,5},{5,4},{6,7},{7,6},{8,9},{9,8},{10,11... | collective-permute-start | bytes 7372808 | tf_op jit(solution)/shard_map/ppermute | solution.py:291
  57.5 6.2 %collective-permute-start.18 = (bf16[2,96,625]{2,1,0:T(8,128)(2,1)S(1)}, bf16[2,96,625]{2,1,0:T(8,128)(2,1)S(1)}, u32[]{:S(2)}, u32[]{:S(2)}) collective-permute-start(bf16[2,96,625]{2,1,0:T(8,128)(2,1)S(1)} %collective-permute-done.14.refs_1_), channel_id=1, source_target_pairs={{0,16},{1,9},{2,18},{3,11},{4,20},{5,13},{6,22},{7,15},{8,24},{9,1... | collective-permute-start | bytes 720008 | tf_op jit(solution)/shard_map/ppermute | solution.py:305
  58.9 11.1 %collective-permute-start.19 = (bf16[625,256]{1,0:T(8,128)(2,1)S(1)}, bf16[625,256]{1,0:T(8,128)(2,1)S(1)}, u32[]{:S(2)}, u32[]{:S(2)}) collective-permute-start(bf16[625,256]{1,0:T(8,128)(2,1)S(1)} %collective-permute-done.16.refs_2_), channel_id=1, source_target_pairs={{0,2},{1,3},{2,4},{3,5},{4,6},{5,7},{6,0},{7,1},{8,10},{9,11},{10,... | collective-permute-start | bytes 960008 | tf_op jit(solution)/shard_map/ppermute | solution.py:294
  67.2 4.8 %copy-start.10 = (s32[32,3]{0,1:T(4,128)S(1)}, s32[32,3]{0,1:T(4,128)}, u32[]{:S(2)}) copy-start(s32[32,3]{0,1:T(4,128)} %param.10) | copy-start | bytes 1156
  67.2 4.9 %copy-start.11 = (s32[32,4]{0,1:T(4,128)S(1)}, s32[32,4]{0,1:T(4,128)}, u32[]{:S(2)}) copy-start(s32[32,4]{0,1:T(4,128)} %param.11) | copy-start | bytes 1540
  70.0 1.5 %copy-start.8 = (bf16[2,1600,384]{2,1,0:T(8,128)(2,1)}, bf16[2,1600,384]{2,1,0:T(8,128)(2,1)S(1)}, u32[]{:S(2)}) copy-start(bf16[2,1600,384]{2,1,0:T(8,128)(2,1)S(1)} %collective-permute-done.20.refs_5_) | copy-start | bytes 7372804
  70.0 7.0 %collective-permute-start.21 = (bf16[2,1600,384]{2,1,0:T(8,128)(2,1)}, bf16[2,1600,384]{2,1,0:T(8,128)(2,1)}, u32[]{:S(2)}, u32[]{:S(2)}) collective-permute-start(bf16[2,1600,384]{2,1,0:T(8,128)(2,1)} %shard_map.76.refs_6_), channel_id=1, source_target_pairs={{0,1},{1,0},{2,3},{3,2},{4,5},{5,4},{6,7},{7,6},{8,9},{9,8},{10,11... | collective-permute-start | bytes 7372808 | tf_op jit(solution)/shard_map/ppermute | solution.py:291
  71.4 5.5 %collective-permute-start.22 = (bf16[8,800,128]{2,1,0:T(8,128)(2,1)S(1)}, bf16[8,800,128]{2,1,0:T(8,128)(2,1)S(1)}, u32[]{:S(2)}, u32[]{:S(2)}) collective-permute-start(bf16[8,800,128]{2,1,0:T(8,128)(2,1)S(1)} %shard_map.77.refs_8_), channel_id=1, source_target_pairs={{0,1},{1,0},{2,3},{3,2},{4,5},{5,4},{6,7},{7,6},{8,9},{9,8},{10,11... | collective-permute-start | bytes 4915208 | tf_op jit(solution)/shard_map/ppermute | solution.py:291
  77.0 1.7 %copy-start.1 = (bf16[2,1600,384]{2,1,0:T(8,128)(2,1)S(1)}, bf16[2,1600,384]{2,1,0:T(8,128)(2,1)}, u32[]{:S(2)}) copy-start(bf16[2,1600,384]{2,1,0:T(8,128)(2,1)} %copy-done) | copy-start | bytes 7372804
  88.0 30.7 %collective-permute-start.24 = (bf16[2,625,128]{2,1,0:T(8,128)(2,1)S(1)}, bf16[2,625,128]{2,1,0:T(8,128)(2,1)S(1)}, u32[]{:S(2)}, u32[]{:S(2)}) collective-permute-start(bf16[2,625,128]{2,1,0:T(8,128)(2,1)S(1)} %bitcast.26), channel_id=1, source_target_pairs={{0,4},{1,5},{2,6},{3,7},{4,0},{5,1},{6,2},{7,3},{8,12},{9,13},{10,... | collective-permute-start | bytes 960008 | tf_op jit(solution)/shard_map/ppermute | solution.py:294
  97.7 21.0 %collective-permute-start.23 = (bf16[2,625,128]{2,1,0:T(8,128)(2,1)S(1)}, bf16[2,625,128]{2,1,0:T(8,128)(2,1)S(1)}, u32[]{:S(2)}, u32[]{:S(2)}) collective-permute-start(bf16[2,625,128]{2,1,0:T(8,128)(2,1)S(1)} %bitcast.27), channel_id=1, source_target_pairs={{0,6},{1,7},{2,0},{3,1},{4,2},{5,3},{6,4},{7,5},{8,14},{9,15},{10,... | collective-permute-start | bytes 960008 | tf_op jit(solution)/shard_map/ppermute | solution.py:294
  107.8 11.4 %copy-start.9 = (f32[2,128,625]{1,0,2:T(2,128)S(1)}, f32[2,128,625]{1,0,2:T(2,128)}, u32[]{:S(2)}) copy-start(f32[2,128,625]{1,0,2:T(2,128)} %param.9) | copy-start | bytes 1920004
  107.8 11.4 %collective-permute-start.25 = (bf16[2,625,128]{2,1,0:T(8,128)(2,1)S(1)}, bf16[2,625,128]{2,1,0:T(8,128)(2,1)S(1)}, u32[]{:S(2)}, u32[]{:S(2)}) collective-permute-start(bf16[2,625,128]{2,1,0:T(8,128)(2,1)S(1)} %bitcast.28), channel_id=1, source_target_pairs={{0,2},{1,3},{2,4},{3,5},{4,6},{5,7},{6,0},{7,1},{8,10},{9,11},{10,... | collective-permute-start | bytes 960008 | tf_op jit(solution)/shard_map/ppermute | solution.py:294

commit v17 on v16

--- a/solution.py
+++ b/solution.py
@@ -316,21 +316,21 @@
         forms0, part1, a1, b1, part2, to3 = after((forms0, part1, a1, b1, part2, mine[3]), ())
         q1, a2, b2, part3 = second_side(a1), first_side(part2), second_side(part2), around(to3, 3)
         far0 = other_core(forms0)
+        q1, amp1 = after((q1, amp1), ())
+        amp2 = around(amp1, 1)
         forms1 = made_forms(part1, a1, b1, q1)
 
-        forms1, part2, a2, b2, part3, amp1, far0 = after((forms1, part2, a2, b2, part3, amp1, far0), ())
-        q2, a3, b3, amp2 = second_side(a2), first_side(part3), second_side(part3), around(amp1, 1)
+        forms1, part2, a2, b2, part3, amp2, far0 = after((forms1, part2, a2, b2, part3, amp2, far0), ())
+        q2, a3, b3, amp3 = second_side(a2), first_side(part3), second_side(part3), around(amp2, 1)
         far1 = other_core(forms1)
         forms2 = made_forms(part2, a2, b2, q2)
 
-        forms2, part3, a3, b3, amp2, far1 = after((forms2, part3, a3, b3, amp2, far1), ())
-        q3, amp3 = second_side(a3), around(amp2, 1)
-        far2 = other_core(forms2)
+        forms2, part3, a3, b3, amp3, far1 = after((forms2, part3, a3, b3, amp3, far1), ())
+        q3, far2 = second_side(a3), other_core(forms2)
+        far_parts = [other_core(x) for x in (part3, a3, b3, q3)]
+        amps = prepare_amps([own, amp1, amp2, amp3], blocks_here, jnp.asarray(amp_matrix()))
         forms3 = made_forms(part3, a3, b3, q3)
-
-        forms3, amp3, far2 = after((forms3, amp3, far2), ())
-        far3 = other_core(forms3)
-        amps = prepare_amps([own, amp1, amp2, amp3], blocks_here, jnp.asarray(amp_matrix()))
+        far3 = prepare(far_parts, (column ^ 1)[None], matrix)
         held = [forms0, far0, forms1, far1, forms2, far2, forms3, far3]
     else:
         parts = [mine[0]] + [around(mine[by], by) for by in range(1, levels)]

time: 121 us -> 134 us (1.11)
  starting transfers between devices: 25.4 us -> 33.1 us
  waiting for transfers between devices: 34.8 us -> 28.8 us
  local copies, waits for them, and re-layouts: 9.5 us -> 14.8 us
  Pallas kernels: 50.4 us -> 55.6 us
    ppermute x9, starting transfers between devices: 10.3 us -> 15.8 us  [around(): lax.ppermute(x, 'task', [(c, (c + 2 * by) % task_count) for c in range(ta...]
    pallas_call x4 -> x5, Pallas kernels: 11.4 us -> 16.7 us  [prepare(): pl.pallas_call(prepare_kernel, out_shape=jax.ShapeDtypeStruct((count, mat...]
    unnamed x29 -> x37, local copies, waits for them, and re-layouts: 8.2 us -> 13.5 us
    ppermute x8, waiting for transfers between devices: 17.7 us -> 13.2 us  [per_device(): second_side = lambda x: lax.ppermute(x, ('pair', 'task'), sides[1])]
    ppermute x5 -> x8, starting transfers between devices: 0.66 us -> 2.21 us  [per_device(): lax.ppermute(x, 'task', [(c, c ^ 1) for c in range(task_count)])]
    ppermute x5 -> x8, waiting for transfers between devices: 4.81 us -> 3.33 us  [per_device(): lax.ppermute(x, 'task', [(c, c ^ 1) for c in range(task_count)])]
  transfers between devices with their start and end apart: 26 -> 29, of which waited for: 13 -> 10; matrix products, arithmetic and copies ran while one was open for 3% -> 3% of each run, Pallas kernels for 34% -> 35%
where the time goes in v17:
time: 134 us; the launch traced here: 133 us
  Pallas kernels  55.6 us (41%)
  starting transfers between devices  33.1 us (25%)
  waiting for transfers between devices  28.8 us (21%)
  local copies, waits for them, and re-layouts  14.8 us (11%)
    pallas_call x4, Pallas kernels, ladders(): pl.pallas_call(functools.partial(ladder_kernel, find, made, len(tiles)),...  37.5 us
    pallas_call x5, Pallas kernels, prepare(): pl.pallas_call(prepare_kernel, out_shape=jax.ShapeDtypeStruct((count, mat...  16.7 us
    ppermute x9, starting transfers between devices, around(): lax.ppermute(x, 'task', [(c, (c + 2 * by) % task_count) for c in range(ta...  15.8 us
    unnamed x37, local copies, waits for them, and re-layouts  13.5 us
    ppermute x8, waiting for transfers between devices, per_device(): second_side = lambda x: lax.ppermute(x, ('pair', 'task'), sides[1])  13.2 us
    ppermute x9, waiting for transfers between devices, around(): lax.ppermute(x, 'task', [(c, (c + 2 * by) % task_count) for c in range(ta...  12.3 us
    ppermute x8, starting transfers between devices, per_device(): second_side = lambda x: lax.ppermute(x, ('pair', 'task'), sides[1])  10.1 us
    ppermute x4, starting transfers between devices, per_device(): first_side = lambda x: lax.ppermute(x, ('pair', 'task'), sides[0])  5.09 us
  transfers between devices with their start and end apart: 29, of which 10 were waited for; matrix products, arithmetic and copies ran while one was open for 3% of the time, Pallas kernels for 35%

profile of v17, /device:TPU:0, one launch (start us, length us, event | category | flops | bytes accessed | tf_op | source)
XLA Modules:
  0.0 132.9 jit_solution(4739512290230048695)
XLA Ops:
  0.0 1.2 pad
  1.3 3.1 %collective-permute-start.3 = (bf16[625,256]{1,0:T(8,128)(2,1)S(1)}, bf16[625,256]{1,0:T(8,128)(2,1)S(1)}, u32[]{:S(2)}, u32[]{:S(2)}) collective-permute-start(bf16[625,256]{1,0:T(8,128)(2,1)S(1)} %bitcast.25), channel_id=1, source_target_pairs={{0,2},{1,3},{2,4},{3,5},{4,6},{5,7},{6,0},{7,1},{8,10},{9,11},{10,... | collective-permute-start | bytes 960008 | tf_op jit(solution)/shard_map/ppermute | solution.py:294
  4.4 3.3 %copy.22 = bf16[2,384,625]{2,1,0:T(8,128)(2,1)S(1)} copy(bf16[2,384,625]{1,0,2:T(2,128)(2,1)} %param.7) | data formatting | bytes 1920000 | tf_op args[0]
  7.7 0.1 dynamic-slice_bitcast_fusion
  7.9 1.6 %collective-permute-start.2 = (bf16[2,96,625]{2,1,0:T(8,128)(2,1)S(1)}, bf16[2,96,625]{2,1,0:T(8,128)(2,1)S(1)}, u32[]{:S(2)}, u32[]{:S(2)}) collective-permute-start(bf16[2,96,625]{2,1,0:T(8,128)(2,1)S(1)} %get-tuple-element.61), channel_id=1, source_target_pairs={{0,2},{1,3},{2,4},{3,5},{4,6},{5,7},{6,0},{7,1},{8,10},{9,11},{10,... | collective-permute-start | bytes 720008 | tf_op jit(solution)/shard_map/ppermute | solution.py:294
  9.5 1.5 %collective-permute-start.1 = (bf16[2,96,625]{2,1,0:T(8,128)(2,1)S(1)}, bf16[2,96,625]{2,1,0:T(8,128)(2,1)S(1)}, u32[]{:S(2)}, u32[]{:S(2)}) collective-permute-start(bf16[2,96,625]{2,1,0:T(8,128)(2,1)S(1)} %get-tuple-element.32.refs_0_), channel_id=1, source_target_pairs={{0,16},{1,9},{2,18},{3,11},{4,20},{5,13},{6,22},{7,15},{8,24},{9,1... | collective-permute-start | bytes 720008 | tf_op jit(solution)/shard_map/ppermute | solution.py:305
  11.0 1.5 %collective-permute-start = (bf16[2,96,625]{2,1,0:T(8,128)(2,1)S(1)}, bf16[2,96,625]{2,1,0:T(8,128)(2,1)S(1)}, u32[]{:S(2)}, u32[]{:S(2)}) collective-permute-start(bf16[2,96,625]{2,1,0:T(8,128)(2,1)S(1)} %get-tuple-element.32.refs_0_), channel_id=1, source_target_pairs={{0,8},{1,17},{2,10},{3,19},{4,12},{5,21},{6,14},{7,23},{8,0},{9,25... | collective-permute-start | bytes 720008 | tf_op jit(solution)/shard_map/ppermute | solution.py:304
  12.5 6.8 %collective-permute-done.2.refs_0_ = bf16[2,96,625]{2,1,0:T(8,128)(2,1)S(1)} collective-permute-done((bf16[2,96,625]{2,1,0:T(8,128)(2,1)S(1)}, bf16[2,96,625]{2,1,0:T(8,128)(2,1)S(1)}, u32[]{:S(2)}, u32[]{:S(2)}) %collective-permute-start.2) | collective-permute-done | bytes 240032 | tf_op jit(solution)/shard_map/ppermute | solution.py:294
  19.3 0.0 collective-permute-done.refs_1_
  19.3 1.6 %collective-permute-start.4 = (bf16[2,96,625]{2,1,0:T(8,128)(2,1)S(1)}, bf16[2,96,625]{2,1,0:T(8,128)(2,1)S(1)}, u32[]{:S(2)}, u32[]{:S(2)}) collective-permute-start(bf16[2,96,625]{2,1,0:T(8,128)(2,1)S(1)} %collective-permute-done.refs_1_), channel_id=1, source_target_pairs={{0,16},{1,9},{2,18},{3,11},{4,20},{5,13},{6,22},{7,15},{8,24},{9,1... | collective-permute-start | bytes 720008 | tf_op jit(solution)/shard_map/ppermute | solution.py:305
  20.9 0.7 collective-permute-start.7
  21.6 0.5 collective-permute-start.6
  22.1 1.5 %collective-permute-start.5 = (bf16[2,96,625]{2,1,0:T(8,128)(2,1)S(1)}, bf16[2,96,625]{2,1,0:T(8,128)(2,1)S(1)}, u32[]{:S(2)}, u32[]{:S(2)}) collective-permute-start(bf16[2,96,625]{2,1,0:T(8,128)(2,1)S(1)} %collective-permute-done.2.refs_0_), channel_id=1, source_target_pairs={{0,8},{1,17},{2,10},{3,19},{4,12},{5,21},{6,14},{7,23},{8,0},{9,25... | collective-permute-start | bytes 720008 | tf_op jit(solution)/shard_map/ppermute | solution.py:304
  23.6 4.6 %collective-permute-done.4.refs_3_ = bf16[2,96,625]{2,1,0:T(8,128)(2,1)S(1)} collective-permute-done((bf16[2,96,625]{2,1,0:T(8,128)(2,1)S(1)}, bf16[2,96,625]{2,1,0:T(8,128)(2,1)S(1)}, u32[]{:S(2)}, u32[]{:S(2)}) %collective-permute-start.4) | collective-permute-done | bytes 240032 | tf_op jit(solution)/shard_map/ppermute | solution.py:305
  28.2 1.6 %copy-done.8 = bf16[1600,625]{1,0:T(8,128)(2,1)S(1)} copy-done((bf16[1600,625]{1,0:T(8,128)(2,1)S(1)}, bf16[1600,625]{1,0:T(8,128)(2,1)}, u32[]{:S(2)}) %copy-start.8) | copy-done | bytes 2000024
  29.7 2.6 %shard_map.73.refs_0_ = bf16[2,1600,384]{2,1,0:T(8,128)(2,1)S(1)} custom-call(s32[1]{0:T(128)} %bitcast.column_ref, bf16[2,96,625]{2,1,0:T(8,128)(2,1)S(1)} %get-tuple-element.32.refs_0_, bf16[2,96,625]{2,1,0:T(8,128)(2,1)S(1)} %collective-permute-done.refs_1_, bf16[2,96,625]{2,1,0:T(8,128)(2,1)S(1)} %collective-permute-done.1.refs_2_, ...), custom_call_target="tpu_custom_call" | custom-call | flops 1536000000 | bytes 3417600 | tf_op jit(solution)/shard_map/pallas_call | solution.py:72
  32.4 0.3 collective-permute-done.7.refs_0_
  32.7 0.1 collective-permute-start.13
  32.8 1.6 %collective-permute-start.8 = (bf16[2,96,625]{2,1,0:T(8,128)(2,1)S(1)}, bf16[2,96,625]{2,1,0:T(8,128)(2,1)S(1)}, u32[]{:S(2)}, u32[]{:S(2)}) collective-permute-start(bf16[2,96,625]{2,1,0:T(8,128)(2,1)S(1)} %collective-permute-done.5.refs_1_), channel_id=1, source_target_pairs={{0,16},{1,9},{2,18},{3,11},{4,20},{5,13},{6,22},{7,15},{8,24},{9,1... | collective-permute-start | bytes 720008 | tf_op jit(solution)/shard_map/ppermute | solution.py:305
  34.4 4.7 %collective-permute-done.8.refs_3_ = bf16[2,96,625]{2,1,0:T(8,128)(2,1)S(1)} collective-permute-done((bf16[2,96,625]{2,1,0:T(8,128)(2,1)S(1)}, bf16[2,96,625]{2,1,0:T(8,128)(2,1)S(1)}, u32[]{:S(2)}, u32[]{:S(2)}) %collective-permute-start.8) | collective-permute-done | bytes 240032 | tf_op jit(solution)/shard_map/ppermute | solution.py:305
  39.1 3.8 %collective-permute-start.11 = (bf16[2,96,625]{2,1,0:T(8,128)(2,1)S(1)}, bf16[2,96,625]{2,1,0:T(8,128)(2,1)S(1)}, u32[]{:S(2)}, u32[]{:S(2)}) collective-permute-start(bf16[2,96,625]{2,1,0:T(8,128)(2,1)S(1)} %get-tuple-element.44), channel_id=1, source_target_pairs={{0,6},{1,7},{2,0},{3,1},{4,2},{5,3},{6,4},{7,5},{8,14},{9,15},{10,... | collective-permute-start | bytes 720008 | tf_op jit(solution)/shard_map/ppermute | solution.py:294
  42.9 1.5 %collective-permute-start.10 = (bf16[2,96,625]{2,1,0:T(8,128)(2,1)S(1)}, bf16[2,96,625]{2,1,0:T(8,128)(2,1)S(1)}, u32[]{:S(2)}, u32[]{:S(2)}) collective-permute-start(bf16[2,96,625]{2,1,0:T(8,128)(2,1)S(1)} %collective-permute-done.7.refs_0_), channel_id=1, source_target_pairs={{0,16},{1,9},{2,18},{3,11},{4,20},{5,13},{6,22},{7,15},{8,24},{9,1... | collective-permute-start | bytes 720008 | tf_op jit(solution)/shard_map/ppermute | solution.py:305
  44.4 1.5 %collective-permute-start.9 = (bf16[2,96,625]{2,1,0:T(8,128)(2,1)S(1)}, bf16[2,96,625]{2,1,0:T(8,128)(2,1)S(1)}, u32[]{:S(2)}, u32[]{:S(2)}) collective-permute-start(bf16[2,96,625]{2,1,0:T(8,128)(2,1)S(1)} %collective-permute-done.7.refs_0_), channel_id=1, source_target_pairs={{0,8},{1,17},{2,10},{3,19},{4,12},{5,21},{6,14},{7,23},{8,0},{9,25... | collective-permute-start | bytes 720008 | tf_op jit(solution)/shard_map/ppermute | solution.py:304
  45.9 2.6 %shard_map.74.refs_2_ = bf16[2,1600,384]{2,1,0:T(8,128)(2,1)S(1)} custom-call(s32[1]{0:T(128)} %bitcast.column_ref, bf16[2,96,625]{2,1,0:T(8,128)(2,1)S(1)} %collective-permute-done.2.refs_0_, bf16[2,96,625]{2,1,0:T(8,128)(2,1)S(1)} %collective-permute-done.5.refs_1_, bf16[2,96,625]{2,1,0:T(8,128)(2,1)S(1)} %collective-permute-done.6.refs_2_, ...), custom_call_target="tpu_custom_call" | custom-call | flops 1536000000 | bytes 3417600 | tf_op jit(solution)/shard_map/pallas_call | solution.py:72
  48.5 0.0 copy-start.5
  48.5 4.9 %collective-permute-done.11.refs_0_ = bf16[2,96,625]{2,1,0:T(8,128)(2,1)S(1)} collective-permute-done((bf16[2,96,625]{2,1,0:T(8,128)(2,1)S(1)}, bf16[2,96,625]{2,1,0:T(8,128)(2,1)S(1)}, u32[]{:S(2)}, u32[]{:S(2)}) %collective-permute-start.11) | collective-permute-done | bytes 240032 | tf_op jit(solution)/shard_map/ppermute | solution.py:294
  53.5 0.1 collective-permute-start.18
  53.5 1.4 %copy-done.12 = bf16[2,1600,384]{2,1,0:T(8,128)(2,1)} copy-done((bf16[2,1600,384]{2,1,0:T(8,128)(2,1)}, bf16[2,1600,384]{2,1,0:T(8,128)(2,1)S(1)}, u32[]{:S(2)}) %copy-start.12) | copy-done | bytes 2457624
  54.9 1.5 %collective-permute-start.14 = (bf16[2,96,625]{2,1,0:T(8,128)(2,1)S(1)}, bf16[2,96,625]{2,1,0:T(8,128)(2,1)S(1)}, u32[]{:S(2)}, u32[]{:S(2)}) collective-permute-start(bf16[2,96,625]{2,1,0:T(8,128)(2,1)S(1)} %collective-permute-done.9.refs_1_), channel_id=1, source_target_pairs={{0,16},{1,9},{2,18},{3,11},{4,20},{5,13},{6,22},{7,15},{8,24},{9,1... | collective-permute-start | bytes 720008 | tf_op jit(solution)/shard_map/ppermute | solution.py:305
  56.4 1.6 %collective-permute-start.17 = (bf16[625,256]{1,0:T(8,128)(2,1)S(1)}, bf16[625,256]{1,0:T(8,128)(2,1)S(1)}, u32[]{:S(2)}, u32[]{:S(2)}) collective-permute-start(bf16[625,256]{1,0:T(8,128)(2,1)S(1)} %collective-permute-done.12.refs_2_), channel_id=1, source_target_pairs={{0,2},{1,3},{2,4},{3,5},{4,6},{5,7},{6,0},{7,1},{8,10},{9,11},{10,... | collective-permute-start | bytes 960008 | tf_op jit(solution)/shard_map/ppermute | solution.py:294
  58.0 0.5 collective-permute-start.16
  58.5 0.6 collective-permute-start.15
  59.1 3.6 %collective-permute-done.14.refs_3_ = bf16[2,96,625]{2,1,0:T(8,128)(2,1)S(1)} collective-permute-done((bf16[2,96,625]{2,1,0:T(8,128)(2,1)S(1)}, bf16[2,96,625]{2,1,0:T(8,128)(2,1)S(1)}, u32[]{:S(2)}, u32[]{:S(2)}) %collective-permute-start.14) | collective-permute-done | bytes 240032 | tf_op jit(solution)/shard_map/ppermute | solution.py:305
  62.8 3.4 %shard_map.75.refs_4_ = bf16[2,1600,384]{2,1,0:T(8,128)(2,1)} custom-call(s32[1]{0:T(128)} %bitcast.column_ref, bf16[2,96,625]{2,1,0:T(8,128)(2,1)S(1)} %collective-permute-done.7.refs_0_, bf16[2,96,625]{2,1,0:T(8,128)(2,1)S(1)} %collective-permute-done.9.refs_1_, bf16[2,96,625]{2,1,0:T(8,128)(2,1)S(1)} %collective-permute-done.10.refs_2_, ...), custom_call_target="tpu_custom_call" | custom-call | flops 1536000000 | bytes 3417600 | tf_op jit(solution)/shard_map/pallas_call | solution.py:72
  66.2 0.3 collective-permute-done.16.refs_2_
  66.5 0.3 collective-permute-done.17.refs_3_
  66.7 1.4 %shard_map.78.refs_8_ = bf16[8,800,128]{2,1,0:T(8,128)(2,1)S(1)} custom-call(bf16[800,625]{1,0:T(8,128)(2,1)S(1)} %copy-done.5, bf16[625,256]{1,0:T(8,128)(2,1)S(1)} %bitcast.26, bf16[625,256]{1,0:T(8,128)(2,1)S(1)} %collective-permute-done.3.refs_1_, bf16[625,256]{1,0:T(8,128)(2,1)S(1)} %collective-permute-done.12.refs_2_, ...), custom_call_target="tpu_custom_call" | custom-call | flops 1024000000 | bytes 2560000 | tf_op jit(solution)/shard_map/pallas_call | solution.py:103
  68.2 0.6 collective-permute-start.25
  68.8 0.1 collective-permute-start.21
  68.8 1.3 %collective-permute-start.20 = (bf16[2,96,625]{2,1,0:T(8,128)(2,1)}, bf16[2,96,625]{2,1,0:T(8,128)(2,1)}, u32[]{:S(2)}, u32[]{:S(2)}) collective-permute-start(bf16[2,96,625]{2,1,0:T(8,128)(2,1)} %collective-permute-done.15.refs_1_), channel_id=1, source_target_pairs={{0,16},{1,9},{2,18},{3,11},{4,20},{5,13},{6,22},{7,15},{8,24},{9,1... | collective-permute-start | bytes 720008 | tf_op jit(solution)/shard_map/ppermute | solution.py:305
  70.2 1.0 collective-permute-start.22
  71.1 3.3 %collective-permute-done.21.refs_0_ = bf16[2,96,625]{2,1,0:T(8,128)(2,1)S(1)} collective-permute-done((bf16[2,96,625]{2,1,0:T(8,128)(2,1)S(1)}, bf16[2,96,625]{2,1,0:T(8,128)(2,1)S(1)}, u32[]{:S(2)}, u32[]{:S(2)}) %collective-permute-start.21) | collective-permute-done | bytes 240032 | tf_op jit(solution)/shard_map/ppermute | solution.py:291
  74.5 0.7 copy-done.6
  75.1 0.1 collective-permute-start.23
  75.3 0.1 collective-permute-done.20.refs_3_
  75.3 0.3 collective-permute-start.24
  75.7 0.1 copy.23.owners_ref
  75.8 0.8 copy.24.local_ref
  76.5 1.6 %copy-done.10 = bf16[1600,625]{1,0:T(8,128)(2,1)S(1)} copy-done((bf16[1600,625]{1,0:T(8,128)(2,1)S(1)}, bf16[1600,625]{1,0:T(8,128)(2,1)}, u32[]{:S(2)}) %copy-start.10) | copy-done | bytes 2000024
  78.1 4.0 %shard_map.76.refs_6_ = bf16[2,1600,384]{2,1,0:T(8,128)(2,1)S(1)} custom-call(s32[1]{0:T(128)} %bitcast.column_ref, bf16[2,96,625]{2,1,0:T(8,128)(2,1)S(1)} %collective-permute-done.11.refs_0_, bf16[2,96,625]{2,1,0:T(8,128)(2,1)} %collective-permute-done.15.refs_1_, bf16[2,96,625]{2,1,0:T(8,128)(2,1)} %collective-permute-done.16.refs_2_, ...), custom_call_target="tpu_custom_call" | custom-call | flops 1536000000 | bytes 3417600 | tf_op jit(solution)/shard_map/pallas_call | solution.py:72
  82.1 1.4 %copy-done.3 = bf16[2,1600,384]{2,1,0:T(8,128)(2,1)} copy-done((bf16[2,1600,384]{2,1,0:T(8,128)(2,1)}, bf16[2,1600,384]{2,1,0:T(8,128)(2,1)S(1)}, u32[]{:S(2)}) %copy-start.3) | copy-done | bytes 2457624
  83.5 4.0 %shard_map.77.refs_7_ = bf16[2,1600,384]{2,1,0:T(8,128)(2,1)S(1)} custom-call(s32[1]{0:T(128)} %bitcast.7.column_ref, bf16[2,96,625]{2,1,0:T(8,128)(2,1)S(1)} %copy-done.7, bf16[2,96,625]{2,1,0:T(8,128)(2,1)} %collective-permute-done.22.refs_1_, bf16[2,96,625]{2,1,0:T(8,128)(2,1)} %collective-permute-done.23.refs_2_, ...), custom_call_target="tpu_custom_call" | custom-call | flops 1536000000 | bytes 3417600 | tf_op jit(solution)/shard_map/pallas_call | solution.py:72
  87.5 1.4 %copy-done.4 = bf16[2,1600,384]{2,1,0:T(8,128)(2,1)} copy-done((bf16[2,1600,384]{2,1,0:T(8,128)(2,1)}, bf16[2,1600,384]{2,1,0:T(8,128)(2,1)S(1)}, u32[]{:S(2)}) %copy-start.4) | copy-done | bytes 2457624
  89.0 9.3 %shard_map.80 = bf16[1,2,625,128]{3,2,1,0:T(8,128)(2,1)S(1)} custom-call(s32[1]{0:T(128)} %bitcast.column_ref, s32[32,3]{1,0:T(8,128)S(1)} %copy.23.owners_ref, s32[32,4]{1,0:T(8,128)S(1)} %copy.24.local_ref, bf16[2,1600,384]{2,1,0:T(8,128)(2,1)S(1)} %copy-done.1, bf16[2,1600,384]{2,1,0:T(8,128)(2,1)} %copy-done.12, bf16[2,1600,384]{2,1,0:T(8,128)(2,1)} %copy-done.2, ...), custom_call_target="tpu_custom_call" | custom-call | flops 2936012800 | bytes 6553600 | tf_op jit(solution)/shard_map/pallas_call | solution.py:257
  98.3 3.0 %collective-permute-start.27 = (bf16[2,625,128]{2,1,0:T(8,128)(2,1)S(1)}, bf16[2,625,128]{2,1,0:T(8,128)(2,1)S(1)}, u32[]{:S(2)}, u32[]{:S(2)}) collective-permute-start(bf16[2,625,128]{2,1,0:T(8,128)(2,1)S(1)} %bitcast.27), channel_id=1, source_target_pairs={{0,4},{1,5},{2,6},{3,7},{4,0},{5,1},{6,2},{7,3},{8,12},{9,13},{10,... | collective-permute-start | bytes 960008 | tf_op jit(solution)/shard_map/ppermute | solution.py:294
  101.2 9.4 %shard_map.79 = bf16[1,2,625,128]{3,2,1,0:T(8,128)(2,1)S(1)} custom-call(s32[1]{0:T(128)} %bitcast.column_ref, s32[32,3]{1,0:T(8,128)S(1)} %copy.23.owners_ref, s32[32,4]{1,0:T(8,128)S(1)} %copy.24.local_ref, bf16[2,1600,384]{2,1,0:T(8,128)(2,1)S(1)} %copy-done.1, bf16[2,1600,384]{2,1,0:T(8,128)(2,1)} %copy-done.12, bf16[2,1600,384]{2,1,0:T(8,128)(2,1)} %copy-done.2, ...), custom_call_target="tpu_custom_call" | custom-call | flops 2936012800 | bytes 6553600 | tf_op jit(solution)/shard_map/pallas_call | solution.py:257
  110.7 1.3 collective-permute-start.26
  112.0 9.3 %shard_map.81 = bf16[1,2,625,128]{3,2,1,0:T(8,128)(2,1)S(1)} custom-call(s32[1]{0:T(128)} %bitcast.column_ref, s32[32,3]{1,0:T(8,128)S(1)} %copy.23.owners_ref, s32[32,4]{1,0:T(8,128)S(1)} %copy.24.local_ref, bf16[2,1600,384]{2,1,0:T(8,128)(2,1)S(1)} %copy-done.1, bf16[2,1600,384]{2,1,0:T(8,128)(2,1)} %copy-done.12, bf16[2,1600,384]{2,1,0:T(8,128)(2,1)} %copy-done.2, ...), custom_call_target="tpu_custom_call" | custom-call | flops 2936012800 | bytes 6553600 | tf_op jit(solution)/shard_map/pallas_call | solution.py:257
  121.2 0.0 copy-start.14
  121.3 0.7 collective-permute-start.28
  122.0 9.5 %shard_map.82 = bf16[1,2,625,128]{3,2,1,0:T(8,128)(2,1)S(1)} custom-call(s32[1]{0:T(128)} %bitcast.column_ref, s32[32,3]{1,0:T(8,128)S(1)} %copy.23.owners_ref, s32[32,4]{1,0:T(8,128)S(1)} %copy.24.local_ref, bf16[2,1600,384]{2,1,0:T(8,128)(2,1)S(1)} %copy-done.1, bf16[2,1600,384]{2,1,0:T(8,128)(2,1)} %copy-done.12, bf16[2,1600,384]{2,1,0:T(8,128)(2,1)} %copy-done.2, ...), custom_call_target="tpu_custom_call" | custom-call | flops 2936012800 | bytes 6553600 | tf_op jit(solution)/shard_map/pallas_call | solution.py:257
  131.5 0.0 collective-permute-done.28
  131.5 0.2 fusion.1
  131.7 1.2 copy.32
  (44 shorter events, 0.1 us)
Async XLA Ops:
  1.3 18.0 %collective-permute-start.3 = (bf16[625,256]{1,0:T(8,128)(2,1)S(1)}, bf16[625,256]{1,0:T(8,128)(2,1)S(1)}, u32[]{:S(2)}, u32[]{:S(2)}) collective-permute-start(bf16[625,256]{1,0:T(8,128)(2,1)S(1)} %bitcast.25), channel_id=1, source_target_pairs={{0,2},{1,3},{2,4},{3,5},{4,6},{5,7},{6,0},{7,1},{8,10},{9,11},{10,... | collective-permute-start | bytes 960008 | tf_op jit(solution)/shard_map/ppermute | solution.py:294
  7.9 11.4 %collective-permute-start.2 = (bf16[2,96,625]{2,1,0:T(8,128)(2,1)S(1)}, bf16[2,96,625]{2,1,0:T(8,128)(2,1)S(1)}, u32[]{:S(2)}, u32[]{:S(2)}) collective-permute-start(bf16[2,96,625]{2,1,0:T(8,128)(2,1)S(1)} %get-tuple-element.61), channel_id=1, source_target_pairs={{0,2},{1,3},{2,4},{3,5},{4,6},{5,7},{6,0},{7,1},{8,10},{9,11},{10,... | collective-permute-start | bytes 720008 | tf_op jit(solution)/shard_map/ppermute | solution.py:294
  9.5 9.8 %collective-permute-start.1 = (bf16[2,96,625]{2,1,0:T(8,128)(2,1)S(1)}, bf16[2,96,625]{2,1,0:T(8,128)(2,1)S(1)}, u32[]{:S(2)}, u32[]{:S(2)}) collective-permute-start(bf16[2,96,625]{2,1,0:T(8,128)(2,1)S(1)} %get-tuple-element.32.refs_0_), channel_id=1, source_target_pairs={{0,16},{1,9},{2,18},{3,11},{4,20},{5,13},{6,22},{7,15},{8,24},{9,1... | collective-permute-start | bytes 720008 | tf_op jit(solution)/shard_map/ppermute | solution.py:305
  11.0 8.3 %collective-permute-start = (bf16[2,96,625]{2,1,0:T(8,128)(2,1)S(1)}, bf16[2,96,625]{2,1,0:T(8,128)(2,1)S(1)}, u32[]{:S(2)}, u32[]{:S(2)}) collective-permute-start(bf16[2,96,625]{2,1,0:T(8,128)(2,1)S(1)} %get-tuple-element.32.refs_0_), channel_id=1, source_target_pairs={{0,8},{1,17},{2,10},{3,19},{4,12},{5,21},{6,14},{7,23},{8,0},{9,25... | collective-permute-start | bytes 720008 | tf_op jit(solution)/shard_map/ppermute | solution.py:304
  19.3 8.9 %collective-permute-start.4 = (bf16[2,96,625]{2,1,0:T(8,128)(2,1)S(1)}, bf16[2,96,625]{2,1,0:T(8,128)(2,1)S(1)}, u32[]{:S(2)}, u32[]{:S(2)}) collective-permute-start(bf16[2,96,625]{2,1,0:T(8,128)(2,1)S(1)} %collective-permute-done.refs_1_), channel_id=1, source_target_pairs={{0,16},{1,9},{2,18},{3,11},{4,20},{5,13},{6,22},{7,15},{8,24},{9,1... | collective-permute-start | bytes 720008 | tf_op jit(solution)/shard_map/ppermute | solution.py:305
  20.9 11.8 %collective-permute-start.7 = (bf16[2,96,625]{2,1,0:T(8,128)(2,1)S(1)}, bf16[2,96,625]{2,1,0:T(8,128)(2,1)S(1)}, u32[]{:S(2)}, u32[]{:S(2)}) collective-permute-start(bf16[2,96,625]{2,1,0:T(8,128)(2,1)S(1)} %get-tuple-element.36), channel_id=1, source_target_pairs={{0,4},{1,5},{2,6},{3,7},{4,0},{5,1},{6,2},{7,3},{8,12},{9,13},{10,... | collective-permute-start | bytes 720008 | tf_op jit(solution)/shard_map/ppermute | solution.py:294
  21.6 11.1 %collective-permute-start.6 = (bf16[2,96,625]{2,1,0:T(8,128)(2,1)S(1)}, bf16[2,96,625]{2,1,0:T(8,128)(2,1)S(1)}, u32[]{:S(2)}, u32[]{:S(2)}) collective-permute-start(bf16[2,96,625]{2,1,0:T(8,128)(2,1)S(1)} %collective-permute-done.2.refs_0_), channel_id=1, source_target_pairs={{0,16},{1,9},{2,18},{3,11},{4,20},{5,13},{6,22},{7,15},{8,24},{9,1... | collective-permute-start | bytes 720008 | tf_op jit(solution)/shard_map/ppermute | solution.py:305
  22.1 10.6 %collective-permute-start.5 = (bf16[2,96,625]{2,1,0:T(8,128)(2,1)S(1)}, bf16[2,96,625]{2,1,0:T(8,128)(2,1)S(1)}, u32[]{:S(2)}, u32[]{:S(2)}) collective-permute-start(bf16[2,96,625]{2,1,0:T(8,128)(2,1)S(1)} %collective-permute-done.2.refs_0_), channel_id=1, source_target_pairs={{0,8},{1,17},{2,10},{3,19},{4,12},{5,21},{6,14},{7,23},{8,0},{9,25... | collective-permute-start | bytes 720008 | tf_op jit(solution)/shard_map/ppermute | solution.py:304
  28.2 1.6 %copy-start.8 = (bf16[1600,625]{1,0:T(8,128)(2,1)S(1)}, bf16[1600,625]{1,0:T(8,128)(2,1)}, u32[]{:S(2)}) copy-start(bf16[1600,625]{1,0:T(8,128)(2,1)} %constant.59.clone.refs_4_) | copy-start | bytes 6000004
  32.4 16.1 %copy-start = (bf16[2,1600,384]{2,1,0:T(8,128)(2,1)}, bf16[2,1600,384]{2,1,0:T(8,128)(2,1)S(1)}, u32[]{:S(2)}) copy-start(bf16[2,1600,384]{2,1,0:T(8,128)(2,1)S(1)} %shard_map.73.refs_0_) | copy-start | bytes 7372804
  32.7 30.0 %copy-start.9 = (bf16[1600,625]{1,0:T(8,128)(2,1)S(1)}, bf16[1600,625]{1,0:T(8,128)(2,1)}, u32[]{:S(2)}) copy-start(bf16[1600,625]{1,0:T(8,128)(2,1)} %constant.59.clone.refs_4_) | copy-start | bytes 6000004
  32.7 20.7 %collective-permute-start.13 = (bf16[2,1600,384]{2,1,0:T(8,128)(2,1)S(1)}, bf16[2,1600,384]{2,1,0:T(8,128)(2,1)S(1)}, u32[]{:S(2)}, u32[]{:S(2)}) collective-permute-start(bf16[2,1600,384]{2,1,0:T(8,128)(2,1)S(1)} %shard_map.73.refs_0_), channel_id=1, source_target_pairs={{0,1},{1,0},{2,3},{3,2},{4,5},{5,4},{6,7},{7,6},{8,9},{9,8},{10,11... | collective-permute-start | bytes 7372808 | tf_op jit(solution)/shard_map/ppermute | solution.py:291
  32.8 6.3 %collective-permute-start.8 = (bf16[2,96,625]{2,1,0:T(8,128)(2,1)S(1)}, bf16[2,96,625]{2,1,0:T(8,128)(2,1)S(1)}, u32[]{:S(2)}, u32[]{:S(2)}) collective-permute-start(bf16[2,96,625]{2,1,0:T(8,128)(2,1)S(1)} %collective-permute-done.5.refs_1_), channel_id=1, source_target_pairs={{0,16},{1,9},{2,18},{3,11},{4,20},{5,13},{6,22},{7,15},{8,24},{9,1... | collective-permute-start | bytes 720008 | tf_op jit(solution)/shard_map/ppermute | solution.py:305
  39.1 14.4 %collective-permute-start.12 = (bf16[625,256]{1,0:T(8,128)(2,1)S(1)}, bf16[625,256]{1,0:T(8,128)(2,1)S(1)}, u32[]{:S(2)}, u32[]{:S(2)}) collective-permute-start(bf16[625,256]{1,0:T(8,128)(2,1)S(1)} %collective-permute-done.3.refs_1_), channel_id=1, source_target_pairs={{0,2},{1,3},{2,4},{3,5},{4,6},{5,7},{6,0},{7,1},{8,10},{9,11},{10,... | collective-permute-start | bytes 960008 | tf_op jit(solution)/shard_map/ppermute | solution.py:294
  39.1 14.4 %collective-permute-start.11 = (bf16[2,96,625]{2,1,0:T(8,128)(2,1)S(1)}, bf16[2,96,625]{2,1,0:T(8,128)(2,1)S(1)}, u32[]{:S(2)}, u32[]{:S(2)}) collective-permute-start(bf16[2,96,625]{2,1,0:T(8,128)(2,1)S(1)} %get-tuple-element.44), channel_id=1, source_target_pairs={{0,6},{1,7},{2,0},{3,1},{4,2},{5,3},{6,4},{7,5},{8,14},{9,15},{10,... | collective-permute-start | bytes 720008 | tf_op jit(solution)/shard_map/ppermute | solution.py:294
  42.9 10.6 %collective-permute-start.10 = (bf16[2,96,625]{2,1,0:T(8,128)(2,1)S(1)}, bf16[2,96,625]{2,1,0:T(8,128)(2,1)S(1)}, u32[]{:S(2)}, u32[]{:S(2)}) collective-permute-start(bf16[2,96,625]{2,1,0:T(8,128)(2,1)S(1)} %collective-permute-done.7.refs_0_), channel_id=1, source_target_pairs={{0,16},{1,9},{2,18},{3,11},{4,20},{5,13},{6,22},{7,15},{8,24},{9,1... | collective-permute-start | bytes 720008 | tf_op jit(solution)/shard_map/ppermute | solution.py:305
  44.4 9.0 %collective-permute-start.9 = (bf16[2,96,625]{2,1,0:T(8,128)(2,1)S(1)}, bf16[2,96,625]{2,1,0:T(8,128)(2,1)S(1)}, u32[]{:S(2)}, u32[]{:S(2)}) collective-permute-start(bf16[2,96,625]{2,1,0:T(8,128)(2,1)S(1)} %collective-permute-done.7.refs_0_), channel_id=1, source_target_pairs={{0,8},{1,17},{2,10},{3,19},{4,12},{5,21},{6,14},{7,23},{8,0},{9,25... | collective-permute-start | bytes 720008 | tf_op jit(solution)/shard_map/ppermute | solution.py:304
  48.5 17.7 %copy-start.2 = (bf16[2,1600,384]{2,1,0:T(8,128)(2,1)}, bf16[2,1600,384]{2,1,0:T(8,128)(2,1)S(1)}, u32[]{:S(2)}) copy-start(bf16[2,1600,384]{2,1,0:T(8,128)(2,1)S(1)} %shard_map.74.refs_2_) | copy-start | bytes 7372804
  48.5 18.2 %copy-start.5 = (bf16[800,625]{1,0:T(8,128)(2,1)S(1)}, bf16[800,625]{1,0:T(8,128)(2,1)}, u32[]{:S(2)}) copy-start(bf16[800,625]{1,0:T(8,128)(2,1)} %constant.60.clone.matrix_ref) | copy-start | bytes 3000004
  53.5 1.4 %copy-start.12 = (bf16[2,1600,384]{2,1,0:T(8,128)(2,1)}, bf16[2,1600,384]{2,1,0:T(8,128)(2,1)S(1)}, u32[]{:S(2)}) copy-start(bf16[2,1600,384]{2,1,0:T(8,128)(2,1)S(1)} %collective-permute-done.13.refs_1_) | copy-start | bytes 7372804
  53.5 13.3 %collective-permute-start.18 = (bf16[2,1600,384]{2,1,0:T(8,128)(2,1)S(1)}, bf16[2,1600,384]{2,1,0:T(8,128)(2,1)S(1)}, u32[]{:S(2)}, u32[]{:S(2)}) collective-permute-start(bf16[2,1600,384]{2,1,0:T(8,128)(2,1)S(1)} %shard_map.74.refs_2_), channel_id=1, source_target_pairs={{0,1},{1,0},{2,3},{3,2},{4,5},{5,4},{6,7},{7,6},{8,9},{9,8},{10,11... | collective-permute-start | bytes 7372808 | tf_op jit(solution)/shard_map/ppermute | solution.py:291
  54.9 7.9 %collective-permute-start.14 = (bf16[2,96,625]{2,1,0:T(8,128)(2,1)S(1)}, bf16[2,96,625]{2,1,0:T(8,128)(2,1)S(1)}, u32[]{:S(2)}, u32[]{:S(2)}) collective-permute-start(bf16[2,96,625]{2,1,0:T(8,128)(2,1)S(1)} %collective-permute-done.9.refs_1_), channel_id=1, source_target_pairs={{0,16},{1,9},{2,18},{3,11},{4,20},{5,13},{6,22},{7,15},{8,24},{9,1... | collective-permute-start | bytes 720008 | tf_op jit(solution)/shard_map/ppermute | solution.py:305
  56.4 10.3 %collective-permute-start.17 = (bf16[625,256]{1,0:T(8,128)(2,1)S(1)}, bf16[625,256]{1,0:T(8,128)(2,1)S(1)}, u32[]{:S(2)}, u32[]{:S(2)}) collective-permute-start(bf16[625,256]{1,0:T(8,128)(2,1)S(1)} %collective-permute-done.12.refs_2_), channel_id=1, source_target_pairs={{0,2},{1,3},{2,4},{3,5},{4,6},{5,7},{6,0},{7,1},{8,10},{9,11},{10,... | collective-permute-start | bytes 960008 | tf_op jit(solution)/shard_map/ppermute | solution.py:294
  58.0 8.5 %collective-permute-start.16 = (bf16[2,96,625]{2,1,0:T(8,128)(2,1)S(1)}, bf16[2,96,625]{2,1,0:T(8,128)(2,1)}, u32[]{:S(2)}, u32[]{:S(2)}) collective-permute-start(bf16[2,96,625]{2,1,0:T(8,128)(2,1)S(1)} %collective-permute-done.11.refs_0_), channel_id=1, source_target_pairs={{0,16},{1,9},{2,18},{3,11},{4,20},{5,13},{6,22},{7,15},{8,24},{9,1... | collective-permute-start | bytes 720008 | tf_op jit(solution)/shard_map/ppermute | solution.py:305
  58.5 8.0 %collective-permute-start.15 = (bf16[2,96,625]{2,1,0:T(8,128)(2,1)S(1)}, bf16[2,96,625]{2,1,0:T(8,128)(2,1)}, u32[]{:S(2)}, u32[]{:S(2)}) collective-permute-start(bf16[2,96,625]{2,1,0:T(8,128)(2,1)S(1)} %collective-permute-done.11.refs_0_), channel_id=1, source_target_pairs={{0,8},{1,17},{2,10},{3,19},{4,12},{5,21},{6,14},{7,23},{8,0},{9,25... | collective-permute-start | bytes 720008 | tf_op jit(solution)/shard_map/ppermute | solution.py:304
  66.2 9.5 %copy-start.15 = (s32[32,3]{0,1:T(4,128)S(1)}, s32[32,3]{0,1:T(4,128)}, u32[]{:S(2)}) copy-start(s32[32,3]{0,1:T(4,128)} %param.10) | copy-start | bytes 1156
  66.7 7.7 %copy-start.13 = (bf16[2,1600,384]{2,1,0:T(8,128)(2,1)}, bf16[2,1600,384]{2,1,0:T(8,128)(2,1)S(1)}, u32[]{:S(2)}) copy-start(bf16[2,1600,384]{2,1,0:T(8,128)(2,1)S(1)} %collective-permute-done.18.refs_3_) | copy-start | bytes 7372804
  66.7 22.2 %collective-permute-start.19 = (bf16[2,1600,384]{2,1,0:T(8,128)(2,1)}, bf16[2,1600,384]{2,1,0:T(8,128)(2,1)}, u32[]{:S(2)}, u32[]{:S(2)}) collective-permute-start(bf16[2,1600,384]{2,1,0:T(8,128)(2,1)} %shard_map.75.refs_4_), channel_id=1, source_target_pairs={{0,1},{1,0},{2,3},{3,2},{4,5},{5,4},{6,7},{7,6},{8,9},{9,8},{10,11... | collective-permute-start | bytes 7372808 | tf_op jit(solution)/shard_map/ppermute | solution.py:291
  68.2 20.8 %collective-permute-start.25 = (bf16[8,800,128]{2,1,0:T(8,128)(2,1)S(1)}, bf16[8,800,128]{2,1,0:T(8,128)(2,1)S(1)}, u32[]{:S(2)}, u32[]{:S(2)}) collective-permute-start(bf16[8,800,128]{2,1,0:T(8,128)(2,1)S(1)} %shard_map.78.refs_8_), channel_id=1, source_target_pairs={{0,1},{1,0},{2,3},{3,2},{4,5},{5,4},{6,7},{7,6},{8,9},{9,8},{10,11... | collective-permute-start | bytes 4915208 | tf_op jit(solution)/shard_map/ppermute | solution.py:291
  68.8 5.7 %collective-permute-start.21 = (bf16[2,96,625]{2,1,0:T(8,128)(2,1)S(1)}, bf16[2,96,625]{2,1,0:T(8,128)(2,1)S(1)}, u32[]{:S(2)}, u32[]{:S(2)}) collective-permute-start(bf16[2,96,625]{2,1,0:T(8,128)(2,1)S(1)} %collective-permute-done.11.refs_0_), channel_id=1, source_target_pairs={{0,1},{1,0},{2,3},{3,2},{4,5},{5,4},{6,7},{7,6},{8,9},{9,8},{10,11... | collective-permute-start | bytes 720008 | tf_op jit(solution)/shard_map/ppermute | solution.py:291
  68.8 6.5 %collective-permute-start.20 = (bf16[2,96,625]{2,1,0:T(8,128)(2,1)}, bf16[2,96,625]{2,1,0:T(8,128)(2,1)}, u32[]{:S(2)}, u32[]{:S(2)}) collective-permute-start(bf16[2,96,625]{2,1,0:T(8,128)(2,1)} %collective-permute-done.15.refs_1_), channel_id=1, source_target_pairs={{0,16},{1,9},{2,18},{3,11},{4,20},{5,13},{6,22},{7,15},{8,24},{9,1... | collective-permute-start | bytes 720008 | tf_op jit(solution)/shard_map/ppermute | solution.py:305
  70.2 13.3 %collective-permute-start.22 = (bf16[2,96,625]{2,1,0:T(8,128)(2,1)}, bf16[2,96,625]{2,1,0:T(8,128)(2,1)}, u32[]{:S(2)}, u32[]{:S(2)}) collective-permute-start(bf16[2,96,625]{2,1,0:T(8,128)(2,1)} %collective-permute-done.15.refs_1_), channel_id=1, source_target_pairs={{0,1},{1,0},{2,3},{3,2},{4,5},{5,4},{6,7},{7,6},{8,9},{9,8},{10,11... | collective-permute-start | bytes 720008 | tf_op jit(solution)/shard_map/ppermute | solution.py:291
  74.5 0.7 copy-start.6
  75.1 8.3 %collective-permute-start.23 = (bf16[2,96,625]{2,1,0:T(8,128)(2,1)}, bf16[2,96,625]{2,1,0:T(8,128)(2,1)}, u32[]{:S(2)}, u32[]{:S(2)}) collective-permute-start(bf16[2,96,625]{2,1,0:T(8,128)(2,1)} %collective-permute-done.16.refs_2_), channel_id=1, source_target_pairs={{0,1},{1,0},{2,3},{3,2},{4,5},{5,4},{6,7},{7,6},{8,9},{9,8},{10,11... | collective-permute-start | bytes 720008 | tf_op jit(solution)/shard_map/ppermute | solution.py:291
  75.3 8.1 %collective-permute-start.24 = (bf16[2,96,625]{2,1,0:T(8,128)(2,1)}, bf16[2,96,625]{2,1,0:T(8,128)(2,1)}, u32[]{:S(2)}, u32[]{:S(2)}) collective-permute-start(bf16[2,96,625]{2,1,0:T(8,128)(2,1)} %collective-permute-done.20.refs_3_), channel_id=1, source_target_pairs={{0,1},{1,0},{2,3},{3,2},{4,5},{5,4},{6,7},{7,6},{8,9},{9,8},{10,11... | collective-permute-start | bytes 720008 | tf_op jit(solution)/shard_map/ppermute | solution.py:291
  76.5 1.6 %copy-start.10 = (bf16[1600,625]{1,0:T(8,128)(2,1)S(1)}, bf16[1600,625]{1,0:T(8,128)(2,1)}, u32[]{:S(2)}) copy-start(bf16[1600,625]{1,0:T(8,128)(2,1)} %constant.59.clone.refs_4_) | copy-start | bytes 6000004
  78.1 5.4 %copy-start.7 = (bf16[2,96,625]{2,1,0:T(8,128)(2,1)S(1)}, bf16[2,96,625]{2,1,0:T(8,128)(2,1)}, u32[]{:S(2)}) copy-start(bf16[2,96,625]{2,1,0:T(8,128)(2,1)} %copy-done.6) | copy-start | bytes 720004
  78.1 5.4 %copy-start.11 = (bf16[1600,625]{1,0:T(8,128)(2,1)S(1)}, bf16[1600,625]{1,0:T(8,128)(2,1)}, u32[]{:S(2)}) copy-start(bf16[1600,625]{1,0:T(8,128)(2,1)} %constant.59.clone.refs_4_) | copy-start | bytes 6000004
  82.1 1.4 %copy-start.3 = (bf16[2,1600,384]{2,1,0:T(8,128)(2,1)}, bf16[2,1600,384]{2,1,0:T(8,128)(2,1)S(1)}, u32[]{:S(2)}) copy-start(bf16[2,1600,384]{2,1,0:T(8,128)(2,1)S(1)} %shard_map.76.refs_6_) | copy-start | bytes 7372804
  83.5 5.4 %copy-start.1 = (bf16[2,1600,384]{2,1,0:T(8,128)(2,1)S(1)}, bf16[2,1600,384]{2,1,0:T(8,128)(2,1)}, u32[]{:S(2)}) copy-start(bf16[2,1600,384]{2,1,0:T(8,128)(2,1)} %copy-done) | copy-start | bytes 7372804
  87.5 1.4 %copy-start.4 = (bf16[2,1600,384]{2,1,0:T(8,128)(2,1)}, bf16[2,1600,384]{2,1,0:T(8,128)(2,1)S(1)}, u32[]{:S(2)}) copy-start(bf16[2,1600,384]{2,1,0:T(8,128)(2,1)S(1)} %shard_map.77.refs_7_) | copy-start | bytes 7372804
  98.3 33.2 %collective-permute-start.27 = (bf16[2,625,128]{2,1,0:T(8,128)(2,1)S(1)}, bf16[2,625,128]{2,1,0:T(8,128)(2,1)S(1)}, u32[]{:S(2)}, u32[]{:S(2)}) collective-permute-start(bf16[2,625,128]{2,1,0:T(8,128)(2,1)S(1)} %bitcast.27), channel_id=1, source_target_pairs={{0,4},{1,5},{2,6},{3,7},{4,0},{5,1},{6,2},{7,3},{8,12},{9,13},{10,... | collective-permute-start | bytes 960008 | tf_op jit(solution)/shard_map/ppermute | solution.py:294
  110.7 20.8 %collective-permute-start.26 = (bf16[2,625,128]{2,1,0:T(8,128)(2,1)S(1)}, bf16[2,625,128]{2,1,0:T(8,128)(2,1)S(1)}, u32[]{:S(2)}, u32[]{:S(2)}) collective-permute-start(bf16[2,625,128]{2,1,0:T(8,128)(2,1)S(1)} %bitcast.28), channel_id=1, source_target_pairs={{0,6},{1,7},{2,0},{3,1},{4,2},{5,3},{6,4},{7,5},{8,14},{9,15},{10,... | collective-permute-start | bytes 960008 | tf_op jit(solution)/shard_map/ppermute | solution.py:294
  121.2 10.3 %copy-start.14 = (f32[2,128,625]{1,0,2:T(2,128)S(1)}, f32[2,128,625]{1,0,2:T(2,128)}, u32[]{:S(2)}) copy-start(f32[2,128,625]{1,0,2:T(2,128)} %param.9) | copy-start | bytes 1920004
  121.3 10.2 %collective-permute-start.28 = (bf16[2,625,128]{2,1,0:T(8,128)(2,1)S(1)}, bf16[2,625,128]{2,1,0:T(8,128)(2,1)S(1)}, u32[]{:S(2)}, u32[]{:S(2)}) collective-permute-start(bf16[2,625,128]{2,1,0:T(8,128)(2,1)S(1)} %bitcast.29), channel_id=1, source_target_pairs={{0,2},{1,3},{2,4},{3,5},{4,6},{5,7},{6,0},{7,1},{8,10},{9,11},{10,... | collective-permute-start | bytes 960008 | tf_op jit(solution)/shard_map/ppermute | solution.py:294

commit v18 on v16

--- a/solution.py
+++ b/solution.py
@@ -115,8 +115,16 @@
     return jnp.concatenate([ref[x * PAD : (x + 1) * PAD, :] for x in numbers], axis=0)
 
 
+def pick_blocks(blocks, low, even):
+    b0, b1, b2, b3 = blocks
+    x, y = jnp.where(low, b0, b2), jnp.where(low, b2, b0)
+    z, w = jnp.where(low, b1, b3), jnp.where(low, b3, b1)
+    return jnp.where(even, x, z), jnp.where(even, w, x), jnp.where(even, y, w), jnp.where(even, z, y)
+
+
 def ladder_kernel(find, made, sources, column_ref, owners_ref, local_ref, *refs):
-    factor_refs, amp_refs, refs = refs[:sources], refs[sources : sources + 2], refs[sources + 2 :]
+    factors, both = sources
+    factor_refs, amp_refs, refs = refs[:factors], refs[factors:both], refs[both:]
     matrix_ref, refs = None if made else refs[0], refs[0 if made else 1 :]
     out_ref, v_ref, u_ref, acc_ref, c_buf, r_buf, amp_buf, sems = refs[:8]
     column, columns = pl.program_id(0), pl.num_programs(0)
@@ -151,11 +159,11 @@
         acc_ref[...] = jnp.zeros_like(acc_ref)
 
     here = find(column, step, column_ref, owners_ref, local_ref)
-    for core in range(2):
-
-        @pl.when(here["amp"][0] == core)
+    for n, ref in enumerate(amp_refs):
+
+        @pl.when(here["amp"][0] == n)
         def _():
-            amp_buf[...] = amp_refs[core][here["amp"][1]]
+            amp_buf[...] = ref[here["amp"][1]]
 
     for n, buffer in enumerate((c_buf, r_buf)):
         pltpu.make_async_copy(buffer.at[slot], buffer.at[slot], sems.at[slot, n]).wait()
@@ -172,7 +180,7 @@
         c_form, r_form = forms.at[0], forms.at[1]
 
     spot = lax.broadcasted_iota(jnp.int32, (PAD, LANES), 1) // PAD
-    at_spot = [spot == p for p in range(GROUP)]
+    low, even = spot < 2, spot % 2 == 0
     nothing = jnp.zeros((PAD, LANES), F32)
     for first in range(0, GROUPS, 2):
         groups = range(first, min(first + 2, GROUPS))
@@ -192,10 +200,7 @@
                     else nothing
                     for g in range(GROUP)
                 ]
-                for i in range(min(GROUP, TV - A * GROUP)):
-                    block = blocks[-i % GROUP]
-                    for p in range(1, GROUP):
-                        block = jnp.where(at_spot[p], blocks[(p - i) % GROUP], block)
+                for i, block in enumerate(pick_blocks(blocks, low, even)[: TV - A * GROUP]):
                     u_ref[START[i] + A * PAD : START[i] + (A + 1) * PAD, D * LANES : (D + 1) * LANES] = block.astype(BF)
     out = local_ref[here["task"], 3]
     for i in range(GROUP):
@@ -236,11 +241,15 @@
             return below * 2 + far, m
 
         below, far, m = place(2)
-        return {"task": task, "row": factor(0), "col": factor(1), "amp": (far, below * blocks_here + m)}
+        if len(amps) == 4:
+            amp = ((below >> 1) * 2 + far, (below & 1) * blocks_here + m)
+        else:
+            amp = (far, below * blocks_here + m)
+        return {"task": task, "row": factor(0), "col": factor(1), "amp": amp}
 
     anywhere = pl.BlockSpec(memory_space=pl.ANY)
     operands = [*tiles, *amps]
-    in_specs = [anywhere] * len(tiles) + [pl.BlockSpec(memory_space=pltpu.VMEM)] * 2
+    in_specs = [anywhere] * len(tiles) + [pl.BlockSpec(memory_space=pltpu.VMEM)] * len(amps)
     scratch = [
         pltpu.VMEM((ROWS, WIDE), F32),
         pltpu.VMEM((ROWS, WIDE), BF),
@@ -255,7 +264,7 @@
         scratch.append(pltpu.VMEM((2, ROWS, depth), BF))
         operands.append(matrix)
     return pl.pallas_call(
-        functools.partial(ladder_kernel, find, made, len(tiles)),
+        functools.partial(ladder_kernel, find, made, (len(tiles), len(tiles) + len(amps))),
         out_shape=jax.ShapeDtypeStruct((columns, blocks_here, TV * TV, pairs), BF),
         grid_spec=pltpu.PrefetchScalarGridSpec(
             num_scalar_prefetch=3,
@@ -305,6 +314,7 @@
         second_side = lambda x: lax.ppermute(x, ("pair", "task"), sides[1])
         made_forms = lambda *parts: prepare(parts, column[None], matrix)
         own = amplitudes.transpose(2, 0, 1).reshape(TV * TV, blocks_here * pairs)
+        amp_rows = jnp.asarray(amp_matrix())
         amp1 = around(own, 1)
         part0 = mine[0]
         a0, b0, part1 = first_side(part0), second_side(part0), around(mine[1], 1)
@@ -322,15 +332,17 @@
         q2, a3, b3, amp2 = second_side(a2), first_side(part3), second_side(part3), around(amp1, 1)
         far1 = other_core(forms1)
         forms2 = made_forms(part2, a2, b2, q2)
-
-        forms2, part3, a3, b3, amp2, far1 = after((forms2, part3, a3, b3, amp2, far1), ())
+        near = prepare_amps([own, amp1], blocks_here, amp_rows)
+
+        forms2, part3, a3, b3, amp2, far1, near = after((forms2, part3, a3, b3, amp2, far1, near), ())
         q3, amp3 = second_side(a3), around(amp2, 1)
-        far2 = other_core(forms2)
+        far2, far_near = other_core(forms2), other_core(near)
         forms3 = made_forms(part3, a3, b3, q3)
 
-        forms3, amp3, far2 = after((forms3, amp3, far2), ())
+        forms3, amp3, far2, far_near = after((forms3, amp3, far2, far_near), ())
         far3 = other_core(forms3)
-        amps = prepare_amps([own, amp1, amp2, amp3], blocks_here, jnp.asarray(amp_matrix()))
+        rest = prepare_amps([amp2, amp3], blocks_here, amp_rows)
+        amps = [near, far_near, rest, other_core(rest)]
         held = [forms0, far0, forms1, far1, forms2, far2, forms3, far3]
     else:
         parts = [mine[0]] + [around(mine[by], by) for by in range(1, levels)]
@@ -339,9 +351,8 @@
         amps = lax.all_gather(tiles, "task", axis=0, axis_index_groups=same_core)
         amps = amps[(level - jnp.arange(levels)) % levels].reshape(levels * blocks_here, ROWS, pairs)
         held = lax.all_gather(jnp.stack(parts), "pair", axis=2, tiled=True)
+        amps = [amps, other_core(amps)]
         held = [jnp.stack([held, other_core(held)], axis=1).reshape(total, depth * pair_count, -1)]
-    amps = (amps, other_core(amps))
-
     ladder = None
     calls = min(levels, 4)
     width = levels // calls

time: 121 us -> 126 us (1.041)
  Pallas kernels: 50.4 us -> 57.9 us
  waiting for transfers between devices: 34.8 us -> 31.9 us
    pallas_call x4, Pallas kernels: 37.5 us -> 43 us  [ladders(): pl.pallas_call(functools.partial(ladder_kernel, find, made, (len(tiles),...]
    pallas_call x1 -> x2, Pallas kernels: 1.44 us -> 3.52 us  [prepare_amps(): pl.pallas_call(amp_kernel, out_shape=jax.ShapeDtypeStruct((levels * block...]
    ppermute x5 -> x6, waiting for transfers between devices: 4.81 us -> 3.77 us  [per_device(): lax.ppermute(x, 'task', [(c, c ^ 1) for c in range(task_count)])]
    unnamed x29 -> x33, local copies, waits for them, and re-layouts: 8.2 us -> 8.46 us
  transfers between devices with their start and end apart: 26 -> 27, of which waited for: 13 -> 12; matrix products, arithmetic and copies ran while one was open for 3% -> 3% of each run, Pallas kernels for 34% -> 38%
where the time goes in v18:
time: 126 us; the launch traced here: 125 us
  Pallas kernels  57.9 us (46%)
  waiting for transfers between devices  31.9 us (25%)
  starting transfers between devices  25.2 us (20%)
  local copies, waits for them, and re-layouts  9.76 us (8%)
    pallas_call x4, Pallas kernels, ladders(): pl.pallas_call(functools.partial(ladder_kernel, find, made, (len(tiles),...  43 us
    ppermute x8, waiting for transfers between devices, per_device(): second_side = lambda x: lax.ppermute(x, ('pair', 'task'), sides[1])  16.5 us
    ppermute x9, waiting for transfers between devices, around(): lax.ppermute(x, 'task', [(c, (c + 2 * by) % task_count) for c in range(ta...  11.5 us
    pallas_call x4, Pallas kernels, prepare(): pl.pallas_call(prepare_kernel, out_shape=jax.ShapeDtypeStruct((count, mat...  11.4 us
    ppermute x9, starting transfers between devices, around(): lax.ppermute(x, 'task', [(c, (c + 2 * by) % task_count) for c in range(ta...  10.1 us
    ppermute x8, starting transfers between devices, per_device(): second_side = lambda x: lax.ppermute(x, ('pair', 'task'), sides[1])  9.13 us
    unnamed x33, local copies, waits for them, and re-layouts  8.46 us
    ppermute x4, starting transfers between devices, per_device(): first_side = lambda x: lax.ppermute(x, ('pair', 'task'), sides[0])  4.81 us
  transfers between devices with their start and end apart: 27, of which 12 were waited for; matrix products, arithmetic and copies ran while one was open for 3% of the time, Pallas kernels for 38%

profile of v18, /device:TPU:0, one launch (start us, length us, event | category | flops | bytes accessed | tf_op | source)
XLA Modules:
  0.0 125.1 jit_solution(14869596296642691638)
XLA Ops:
  0.0 1.2 pad
  1.3 0.0 copy-start.5
  1.3 3.1 %collective-permute-start.3 = (bf16[625,256]{1,0:T(8,128)(2,1)S(1)}, bf16[625,256]{1,0:T(8,128)(2,1)}, u32[]{:S(2)}, u32[]{:S(2)}) collective-permute-start(bf16[625,256]{1,0:T(8,128)(2,1)S(1)} %bitcast.24), channel_id=1, source_target_pairs={{0,2},{1,3},{2,4},{3,5},{4,6},{5,7},{6,0},{7,1},{8,10},{9,11},{10,... | collective-permute-start | bytes 960008 | tf_op jit(solution)/shard_map/ppermute | solution.py:303
  4.4 3.3 %copy.22 = bf16[2,384,625]{2,1,0:T(8,128)(2,1)S(1)} copy(bf16[2,384,625]{1,0,2:T(2,128)(2,1)} %param.7) | data formatting | bytes 1920000 | tf_op args[0]
  7.7 0.1 dynamic-slice_bitcast_fusion
  7.9 1.6 %collective-permute-start.2 = (bf16[2,96,625]{2,1,0:T(8,128)(2,1)S(1)}, bf16[2,96,625]{2,1,0:T(8,128)(2,1)S(1)}, u32[]{:S(2)}, u32[]{:S(2)}) collective-permute-start(bf16[2,96,625]{2,1,0:T(8,128)(2,1)S(1)} %get-tuple-element.67), channel_id=1, source_target_pairs={{0,2},{1,3},{2,4},{3,5},{4,6},{5,7},{6,0},{7,1},{8,10},{9,11},{10,... | collective-permute-start | bytes 720008 | tf_op jit(solution)/shard_map/ppermute | solution.py:303
  9.5 1.5 %collective-permute-start.1 = (bf16[2,96,625]{2,1,0:T(8,128)(2,1)S(1)}, bf16[2,96,625]{2,1,0:T(8,128)(2,1)S(1)}, u32[]{:S(2)}, u32[]{:S(2)}) collective-permute-start(bf16[2,96,625]{2,1,0:T(8,128)(2,1)S(1)} %get-tuple-element.35.refs_0_), channel_id=1, source_target_pairs={{0,16},{1,9},{2,18},{3,11},{4,20},{5,13},{6,22},{7,15},{8,24},{9,1... | collective-permute-start | bytes 720008 | tf_op jit(solution)/shard_map/ppermute | solution.py:314
  11.0 1.5 %collective-permute-start = (bf16[2,96,625]{2,1,0:T(8,128)(2,1)S(1)}, bf16[2,96,625]{2,1,0:T(8,128)(2,1)S(1)}, u32[]{:S(2)}, u32[]{:S(2)}) collective-permute-start(bf16[2,96,625]{2,1,0:T(8,128)(2,1)S(1)} %get-tuple-element.35.refs_0_), channel_id=1, source_target_pairs={{0,8},{1,17},{2,10},{3,19},{4,12},{5,21},{6,14},{7,23},{8,0},{9,25... | collective-permute-start | bytes 720008 | tf_op jit(solution)/shard_map/ppermute | solution.py:313
  12.5 6.8 %collective-permute-done.2.refs_0_ = bf16[2,96,625]{2,1,0:T(8,128)(2,1)S(1)} collective-permute-done((bf16[2,96,625]{2,1,0:T(8,128)(2,1)S(1)}, bf16[2,96,625]{2,1,0:T(8,128)(2,1)S(1)}, u32[]{:S(2)}, u32[]{:S(2)}) %collective-permute-start.2) | collective-permute-done | bytes 240032 | tf_op jit(solution)/shard_map/ppermute | solution.py:303
  19.3 1.6 %collective-permute-start.4 = (bf16[2,96,625]{2,1,0:T(8,128)(2,1)S(1)}, bf16[2,96,625]{2,1,0:T(8,128)(2,1)S(1)}, u32[]{:S(2)}, u32[]{:S(2)}) collective-permute-start(bf16[2,96,625]{2,1,0:T(8,128)(2,1)S(1)} %collective-permute-done.refs_1_), channel_id=1, source_target_pairs={{0,16},{1,9},{2,18},{3,11},{4,20},{5,13},{6,22},{7,15},{8,24},{9,1... | collective-permute-start | bytes 720008 | tf_op jit(solution)/shard_map/ppermute | solution.py:314
  20.9 0.7 collective-permute-start.7
  21.6 0.5 collective-permute-start.6
  22.1 1.5 %collective-permute-start.5 = (bf16[2,96,625]{2,1,0:T(8,128)(2,1)S(1)}, bf16[2,96,625]{2,1,0:T(8,128)(2,1)S(1)}, u32[]{:S(2)}, u32[]{:S(2)}) collective-permute-start(bf16[2,96,625]{2,1,0:T(8,128)(2,1)S(1)} %collective-permute-done.2.refs_0_), channel_id=1, source_target_pairs={{0,8},{1,17},{2,10},{3,19},{4,12},{5,21},{6,14},{7,23},{8,0},{9,25... | collective-permute-start | bytes 720008 | tf_op jit(solution)/shard_map/ppermute | solution.py:313
  23.6 4.6 %collective-permute-done.4.refs_3_ = bf16[2,96,625]{2,1,0:T(8,128)(2,1)S(1)} collective-permute-done((bf16[2,96,625]{2,1,0:T(8,128)(2,1)S(1)}, bf16[2,96,625]{2,1,0:T(8,128)(2,1)S(1)}, u32[]{:S(2)}, u32[]{:S(2)}) %collective-permute-start.4) | collective-permute-done | bytes 240032 | tf_op jit(solution)/shard_map/ppermute | solution.py:314
  28.2 1.6 %copy-done.7 = bf16[1600,625]{1,0:T(8,128)(2,1)S(1)} copy-done((bf16[1600,625]{1,0:T(8,128)(2,1)S(1)}, bf16[1600,625]{1,0:T(8,128)(2,1)}, u32[]{:S(2)}) %copy-start.7) | copy-done | bytes 2000024
  29.7 2.6 %shard_map.73.refs_0_ = bf16[2,1600,384]{2,1,0:T(8,128)(2,1)S(1)} custom-call(s32[1]{0:T(128)} %bitcast.column_ref, bf16[2,96,625]{2,1,0:T(8,128)(2,1)S(1)} %get-tuple-element.35.refs_0_, bf16[2,96,625]{2,1,0:T(8,128)(2,1)S(1)} %collective-permute-done.refs_1_, bf16[2,96,625]{2,1,0:T(8,128)(2,1)S(1)} %collective-permute-done.1.refs_2_, ...), custom_call_target="tpu_custom_call" | custom-call | flops 1536000000 | bytes 3417600 | tf_op jit(solution)/shard_map/pallas_call | solution.py:72
  32.4 0.3 collective-permute-done.7.refs_0_
  32.7 0.0 collective-permute-done.6.refs_2_
  32.7 0.0 collective-permute-done.5.refs_1_
  32.7 0.0 copy-start.6
  32.7 0.1 collective-permute-start.12
  32.8 1.6 %collective-permute-start.8 = (bf16[2,96,625]{2,1,0:T(8,128)(2,1)S(1)}, bf16[2,96,625]{2,1,0:T(8,128)(2,1)S(1)}, u32[]{:S(2)}, u32[]{:S(2)}) collective-permute-start(bf16[2,96,625]{2,1,0:T(8,128)(2,1)S(1)} %collective-permute-done.5.refs_1_), channel_id=1, source_target_pairs={{0,16},{1,9},{2,18},{3,11},{4,20},{5,13},{6,22},{7,15},{8,24},{9,1... | collective-permute-start | bytes 720008 | tf_op jit(solution)/shard_map/ppermute | solution.py:314
  34.4 2.5 %collective-permute-start.11 = (bf16[2,96,625]{2,1,0:T(8,128)(2,1)S(1)}, bf16[2,96,625]{2,1,0:T(8,128)(2,1)S(1)}, u32[]{:S(2)}, u32[]{:S(2)}) collective-permute-start(bf16[2,96,625]{2,1,0:T(8,128)(2,1)S(1)} %get-tuple-element.45), channel_id=1, source_target_pairs={{0,6},{1,7},{2,0},{3,1},{4,2},{5,3},{6,4},{7,5},{8,14},{9,15},{10,... | collective-permute-start | bytes 720008 | tf_op jit(solution)/shard_map/ppermute | solution.py:303
  36.9 0.5 collective-permute-start.10
  37.4 0.6 collective-permute-start.9
  38.0 1.0 collective-permute-done.8.refs_3_
  39.1 2.6 %shard_map.74.refs_2_ = bf16[2,1600,384]{2,1,0:T(8,128)(2,1)S(1)} custom-call(s32[1]{0:T(128)} %bitcast.column_ref, bf16[2,96,625]{2,1,0:T(8,128)(2,1)S(1)} %collective-permute-done.2.refs_0_, bf16[2,96,625]{2,1,0:T(8,128)(2,1)S(1)} %collective-permute-done.5.refs_1_, bf16[2,96,625]{2,1,0:T(8,128)(2,1)S(1)} %collective-permute-done.6.refs_2_, ...), custom_call_target="tpu_custom_call" | custom-call | flops 1536000000 | bytes 3417600 | tf_op jit(solution)/shard_map/pallas_call | solution.py:72
  41.7 0.0 copy-start.9
  41.8 0.8 collective-permute-done.11.refs_0_
  42.5 2.3 %collective-permute-done.10.refs_2_ = bf16[2,96,625]{2,1,0:T(8,128)(2,1)S(1)} collective-permute-done((bf16[2,96,625]{2,1,0:T(8,128)(2,1)S(1)}, bf16[2,96,625]{2,1,0:T(8,128)(2,1)S(1)}, u32[]{:S(2)}, u32[]{:S(2)}) %collective-permute-start.10) | collective-permute-done | bytes 240032 | tf_op jit(solution)/shard_map/ppermute | solution.py:314
  44.8 0.0 collective-permute-done.9.refs_1_
  44.8 0.0 collective-permute-done.12.refs_1_
  44.8 0.0 collective-permute-start.17
  44.9 1.3 %collective-permute-start.13 = (bf16[2,96,625]{2,1,0:T(8,128)(2,1)S(1)}, bf16[2,96,625]{2,1,0:T(8,128)(2,1)S(1)}, u32[]{:S(2)}, u32[]{:S(2)}) collective-permute-start(bf16[2,96,625]{2,1,0:T(8,128)(2,1)S(1)} %collective-permute-done.9.refs_1_), channel_id=1, source_target_pairs={{0,16},{1,9},{2,18},{3,11},{4,20},{5,13},{6,22},{7,15},{8,24},{9,1... | collective-permute-start | bytes 720008 | tf_op jit(solution)/shard_map/ppermute | solution.py:314
  46.2 0.8 collective-permute-start.15
  46.9 1.2 collective-permute-start.14
  48.1 1.8 %shard_map.76.refs_8_ = bf16[4,800,128]{2,1,0:T(8,128)(2,1)S(1)} custom-call(bf16[800,625]{1,0:T(8,128)(2,1)S(1)} %copy-done.4, bf16[625,256]{1,0:T(8,128)(2,1)S(1)} %bitcast.25, bf16[625,256]{1,0:T(8,128)(2,1)} %collective-permute-done.3.refs_1_), custom_call_target="tpu_custom_call" | custom-call | flops 512000000 | bytes 1280000 | tf_op jit(solution)/shard_map/pallas_call | solution.py:103
  49.9 0.0 copy-start.10
  49.9 2.9 %collective-permute-done.13.refs_3_ = bf16[2,96,625]{2,1,0:T(8,128)(2,1)S(1)} collective-permute-done((bf16[2,96,625]{2,1,0:T(8,128)(2,1)S(1)}, bf16[2,96,625]{2,1,0:T(8,128)(2,1)S(1)}, u32[]{:S(2)}, u32[]{:S(2)}) %collective-permute-start.13) | collective-permute-done | bytes 240032 | tf_op jit(solution)/shard_map/ppermute | solution.py:314
  52.8 2.6 %shard_map.75.refs_4_ = bf16[2,1600,384]{2,1,0:T(8,128)(2,1)S(1)} custom-call(s32[1]{0:T(128)} %bitcast.column_ref, bf16[2,96,625]{2,1,0:T(8,128)(2,1)S(1)} %collective-permute-done.7.refs_0_, bf16[2,96,625]{2,1,0:T(8,128)(2,1)S(1)} %collective-permute-done.9.refs_1_, bf16[2,96,625]{2,1,0:T(8,128)(2,1)S(1)} %collective-permute-done.10.refs_2_, ...), custom_call_target="tpu_custom_call" | custom-call | flops 1536000000 | bytes 3417600 | tf_op jit(solution)/shard_map/pallas_call | solution.py:72
  55.5 0.9 collective-permute-done.15.refs_2_
  56.4 1.4 %collective-permute-done.16.refs_0_ = bf16[625,256]{1,0:T(8,128)(2,1)S(1)} collective-permute-done((bf16[625,256]{1,0:T(8,128)(2,1)}, bf16[625,256]{1,0:T(8,128)(2,1)S(1)}, u32[]{:S(2)}, u32[]{:S(2)}) %collective-permute-start.16) | collective-permute-done | bytes 320032 | tf_op jit(solution)/shard_map/ppermute | solution.py:303
  57.8 0.5 collective-permute-start.21
  58.3 1.3 %collective-permute-start.18 = (bf16[2,96,625]{2,1,0:T(8,128)(2,1)S(1)}, bf16[2,96,625]{2,1,0:T(8,128)(2,1)S(1)}, u32[]{:S(2)}, u32[]{:S(2)}) collective-permute-start(bf16[2,96,625]{2,1,0:T(8,128)(2,1)S(1)} %collective-permute-done.14.refs_1_), channel_id=1, source_target_pairs={{0,16},{1,9},{2,18},{3,11},{4,20},{5,13},{6,22},{7,15},{8,24},{9,1... | collective-permute-start | bytes 720008 | tf_op jit(solution)/shard_map/ppermute | solution.py:314
  59.6 4.9 %collective-permute-done.18.refs_3_ = bf16[2,96,625]{2,1,0:T(8,128)(2,1)S(1)} collective-permute-done((bf16[2,96,625]{2,1,0:T(8,128)(2,1)S(1)}, bf16[2,96,625]{2,1,0:T(8,128)(2,1)S(1)}, u32[]{:S(2)}, u32[]{:S(2)}) %collective-permute-start.18) | collective-permute-done | bytes 240032 | tf_op jit(solution)/shard_map/ppermute | solution.py:314
  64.5 3.4 %shard_map.77.refs_6_ = bf16[2,1600,384]{2,1,0:T(8,128)(2,1)} custom-call(s32[1]{0:T(128)} %bitcast.column_ref, bf16[2,96,625]{2,1,0:T(8,128)(2,1)S(1)} %collective-permute-done.11.refs_0_, bf16[2,96,625]{2,1,0:T(8,128)(2,1)S(1)} %collective-permute-done.14.refs_1_, bf16[2,96,625]{2,1,0:T(8,128)(2,1)S(1)} %collective-permute-done.15.refs_2_, ...), custom_call_target="tpu_custom_call" | custom-call | flops 1536000000 | bytes 3417600 | tf_op jit(solution)/shard_map/pallas_call | solution.py:72
  67.9 2.3 %collective-permute-done.19.refs_1_ = bf16[625,256]{1,0:T(8,128)(2,1)S(1)} collective-permute-done((bf16[625,256]{1,0:T(8,128)(2,1)S(1)}, bf16[625,256]{1,0:T(8,128)(2,1)S(1)}, u32[]{:S(2)}, u32[]{:S(2)}) %collective-permute-start.19) | collective-permute-done | bytes 320032 | tf_op jit(solution)/shard_map/ppermute | solution.py:303
  70.2 0.9 copy-done.2
  71.1 1.7 %shard_map.78.refs_10_ = bf16[4,800,128]{2,1,0:T(8,128)(2,1)} custom-call(bf16[800,625]{1,0:T(8,128)(2,1)S(1)} %copy-done.4, bf16[625,256]{1,0:T(8,128)(2,1)S(1)} %collective-permute-done.16.refs_0_, bf16[625,256]{1,0:T(8,128)(2,1)S(1)} %collective-permute-done.19.refs_1_), custom_call_target="tpu_custom_call" | custom-call | flops 512000000 | bytes 1280000 | tf_op jit(solution)/shard_map/pallas_call | solution.py:103
  72.9 0.5 collective-permute-start.23
  73.4 0.1 copy.23.owners_ref
  73.5 0.1 copy.24.local_ref
  73.5 3.8 %collective-permute-done.23.refs_11_ = bf16[4,800,128]{2,1,0:T(8,128)(2,1)} collective-permute-done((bf16[4,800,128]{2,1,0:T(8,128)(2,1)}, bf16[4,800,128]{2,1,0:T(8,128)(2,1)}, u32[]{:S(2)}, u32[]{:S(2)}) %collective-permute-start.23) | collective-permute-done | bytes 819232 | tf_op jit(solution)/shard_map/ppermute | solution.py:300
  77.3 1.1 copy-done.3
  78.5 10.7 %shard_map.80 = bf16[1,2,625,128]{3,2,1,0:T(8,128)(2,1)S(1)} custom-call(s32[1]{0:T(128)} %bitcast.column_ref, s32[32,3]{1,0:T(8,128)S(1)} %copy.23.owners_ref, s32[32,4]{1,0:T(8,128)S(1)} %copy.24.local_ref, bf16[2,1600,384]{2,1,0:T(8,128)(2,1)S(1)} %shard_map.73.refs_0_, bf16[2,1600,384]{2,1,0:T(8,128)(2,1)} %collective-permute-done.12.refs_1_, ...), custom_call_target="tpu_custom_call" | custom-call | flops 2936012800 | bytes 6553600 | tf_op jit(solution)/shard_map/pallas_call | solution.py:266
  89.2 0.1 collective-permute-start.25
  89.3 10.7 %shard_map.79 = bf16[1,2,625,128]{3,2,1,0:T(8,128)(2,1)S(1)} custom-call(s32[1]{0:T(128)} %bitcast.column_ref, s32[32,3]{1,0:T(8,128)S(1)} %copy.23.owners_ref, s32[32,4]{1,0:T(8,128)S(1)} %copy.24.local_ref, bf16[2,1600,384]{2,1,0:T(8,128)(2,1)S(1)} %shard_map.73.refs_0_, bf16[2,1600,384]{2,1,0:T(8,128)(2,1)} %collective-permute-done.12.refs_1_, ...), custom_call_target="tpu_custom_call" | custom-call | flops 2936012800 | bytes 6553600 | tf_op jit(solution)/shard_map/pallas_call | solution.py:266
  100.0 1.2 collective-permute-start.24
  101.2 10.9 %shard_map.81 = bf16[1,2,625,128]{3,2,1,0:T(8,128)(2,1)S(1)} custom-call(s32[1]{0:T(128)} %bitcast.column_ref, s32[32,3]{1,0:T(8,128)S(1)} %copy.23.owners_ref, s32[32,4]{1,0:T(8,128)S(1)} %copy.24.local_ref, bf16[2,1600,384]{2,1,0:T(8,128)(2,1)S(1)} %shard_map.73.refs_0_, bf16[2,1600,384]{2,1,0:T(8,128)(2,1)} %collective-permute-done.12.refs_1_, ...), custom_call_target="tpu_custom_call" | custom-call | flops 2936012800 | bytes 6553600 | tf_op jit(solution)/shard_map/pallas_call | solution.py:266
  112.1 0.0 copy-start.11
  112.1 1.0 collective-permute-start.26
  113.0 10.7 %shard_map.82 = bf16[1,2,625,128]{3,2,1,0:T(8,128)(2,1)S(1)} custom-call(s32[1]{0:T(128)} %bitcast.column_ref, s32[32,3]{1,0:T(8,128)S(1)} %copy.23.owners_ref, s32[32,4]{1,0:T(8,128)S(1)} %copy.24.local_ref, bf16[2,1600,384]{2,1,0:T(8,128)(2,1)S(1)} %shard_map.73.refs_0_, bf16[2,1600,384]{2,1,0:T(8,128)(2,1)} %collective-permute-done.12.refs_1_, ...), custom_call_target="tpu_custom_call" | custom-call | flops 2936012800 | bytes 6553600 | tf_op jit(solution)/shard_map/pallas_call | solution.py:266
  123.8 0.2 fusion.1
  124.0 1.2 copy.32
  (36 shorter events, 0.1 us)
Async XLA Ops:
  1.3 26.9 %copy-start.5 = (bf16[79,8,2,128]{3,1,2,0:T(8,128)(2,1)}, bf16[79,8,2,128]{3,1,2,0:T(8,128)(2,1)S(1)}, u32[]{:S(2)}) copy-start(bf16[79,8,2,128]{3,1,2,0:T(8,128)(2,1)S(1)} %copy.33) | copy-start | bytes 970756
  1.3 18.0 %collective-permute-start.3 = (bf16[625,256]{1,0:T(8,128)(2,1)S(1)}, bf16[625,256]{1,0:T(8,128)(2,1)}, u32[]{:S(2)}, u32[]{:S(2)}) collective-permute-start(bf16[625,256]{1,0:T(8,128)(2,1)S(1)} %bitcast.24), channel_id=1, source_target_pairs={{0,2},{1,3},{2,4},{3,5},{4,6},{5,7},{6,0},{7,1},{8,10},{9,11},{10,... | collective-permute-start | bytes 960008 | tf_op jit(solution)/shard_map/ppermute | solution.py:303
  7.9 11.4 %collective-permute-start.2 = (bf16[2,96,625]{2,1,0:T(8,128)(2,1)S(1)}, bf16[2,96,625]{2,1,0:T(8,128)(2,1)S(1)}, u32[]{:S(2)}, u32[]{:S(2)}) collective-permute-start(bf16[2,96,625]{2,1,0:T(8,128)(2,1)S(1)} %get-tuple-element.67), channel_id=1, source_target_pairs={{0,2},{1,3},{2,4},{3,5},{4,6},{5,7},{6,0},{7,1},{8,10},{9,11},{10,... | collective-permute-start | bytes 720008 | tf_op jit(solution)/shard_map/ppermute | solution.py:303
  9.5 9.8 %collective-permute-start.1 = (bf16[2,96,625]{2,1,0:T(8,128)(2,1)S(1)}, bf16[2,96,625]{2,1,0:T(8,128)(2,1)S(1)}, u32[]{:S(2)}, u32[]{:S(2)}) collective-permute-start(bf16[2,96,625]{2,1,0:T(8,128)(2,1)S(1)} %get-tuple-element.35.refs_0_), channel_id=1, source_target_pairs={{0,16},{1,9},{2,18},{3,11},{4,20},{5,13},{6,22},{7,15},{8,24},{9,1... | collective-permute-start | bytes 720008 | tf_op jit(solution)/shard_map/ppermute | solution.py:314
  11.0 8.3 %collective-permute-start = (bf16[2,96,625]{2,1,0:T(8,128)(2,1)S(1)}, bf16[2,96,625]{2,1,0:T(8,128)(2,1)S(1)}, u32[]{:S(2)}, u32[]{:S(2)}) collective-permute-start(bf16[2,96,625]{2,1,0:T(8,128)(2,1)S(1)} %get-tuple-element.35.refs_0_), channel_id=1, source_target_pairs={{0,8},{1,17},{2,10},{3,19},{4,12},{5,21},{6,14},{7,23},{8,0},{9,25... | collective-permute-start | bytes 720008 | tf_op jit(solution)/shard_map/ppermute | solution.py:313
  19.3 8.9 %collective-permute-start.4 = (bf16[2,96,625]{2,1,0:T(8,128)(2,1)S(1)}, bf16[2,96,625]{2,1,0:T(8,128)(2,1)S(1)}, u32[]{:S(2)}, u32[]{:S(2)}) collective-permute-start(bf16[2,96,625]{2,1,0:T(8,128)(2,1)S(1)} %collective-permute-done.refs_1_), channel_id=1, source_target_pairs={{0,16},{1,9},{2,18},{3,11},{4,20},{5,13},{6,22},{7,15},{8,24},{9,1... | collective-permute-start | bytes 720008 | tf_op jit(solution)/shard_map/ppermute | solution.py:314
  20.9 11.8 %collective-permute-start.7 = (bf16[2,96,625]{2,1,0:T(8,128)(2,1)S(1)}, bf16[2,96,625]{2,1,0:T(8,128)(2,1)S(1)}, u32[]{:S(2)}, u32[]{:S(2)}) collective-permute-start(bf16[2,96,625]{2,1,0:T(8,128)(2,1)S(1)} %get-tuple-element.39), channel_id=1, source_target_pairs={{0,4},{1,5},{2,6},{3,7},{4,0},{5,1},{6,2},{7,3},{8,12},{9,13},{10,... | collective-permute-start | bytes 720008 | tf_op jit(solution)/shard_map/ppermute | solution.py:303
  21.6 11.1 %collective-permute-start.6 = (bf16[2,96,625]{2,1,0:T(8,128)(2,1)S(1)}, bf16[2,96,625]{2,1,0:T(8,128)(2,1)S(1)}, u32[]{:S(2)}, u32[]{:S(2)}) collective-permute-start(bf16[2,96,625]{2,1,0:T(8,128)(2,1)S(1)} %collective-permute-done.2.refs_0_), channel_id=1, source_target_pairs={{0,16},{1,9},{2,18},{3,11},{4,20},{5,13},{6,22},{7,15},{8,24},{9,1... | collective-permute-start | bytes 720008 | tf_op jit(solution)/shard_map/ppermute | solution.py:314
  22.1 10.6 %collective-permute-start.5 = (bf16[2,96,625]{2,1,0:T(8,128)(2,1)S(1)}, bf16[2,96,625]{2,1,0:T(8,128)(2,1)S(1)}, u32[]{:S(2)}, u32[]{:S(2)}) collective-permute-start(bf16[2,96,625]{2,1,0:T(8,128)(2,1)S(1)} %collective-permute-done.2.refs_0_), channel_id=1, source_target_pairs={{0,8},{1,17},{2,10},{3,19},{4,12},{5,21},{6,14},{7,23},{8,0},{9,25... | collective-permute-start | bytes 720008 | tf_op jit(solution)/shard_map/ppermute | solution.py:313
  28.2 1.6 %copy-start.7 = (bf16[1600,625]{1,0:T(8,128)(2,1)S(1)}, bf16[1600,625]{1,0:T(8,128)(2,1)}, u32[]{:S(2)}) copy-start(bf16[1600,625]{1,0:T(8,128)(2,1)} %constant.59.clone.refs_4_) | copy-start | bytes 6000004
  29.7 9.3 %copy-start.8 = (bf16[1600,625]{1,0:T(8,128)(2,1)S(1)}, bf16[1600,625]{1,0:T(8,128)(2,1)}, u32[]{:S(2)}) copy-start(bf16[1600,625]{1,0:T(8,128)(2,1)} %constant.59.clone.refs_4_) | copy-start | bytes 6000004
  32.7 15.4 %copy-start.4 = (bf16[800,625]{1,0:T(8,128)(2,1)S(1)}, bf16[800,625]{1,0:T(8,128)(2,1)}, u32[]{:S(2)}) copy-start(bf16[800,625]{1,0:T(8,128)(2,1)} %constant.60.clone.matrix_ref) | copy-start | bytes 3000004
  32.7 15.4 %copy-start.6 = (bf16[79,8,2,128]{3,1,2,0:T(8,128)(2,1)S(1)}, bf16[79,8,2,128]{3,1,2,0:T(8,128)(2,1)}, u32[]{:S(2)}) copy-start(bf16[79,8,2,128]{3,1,2,0:T(8,128)(2,1)} %copy-done.5) | copy-start | bytes 970756
  32.7 12.1 %collective-permute-start.12 = (bf16[2,1600,384]{2,1,0:T(8,128)(2,1)S(1)}, bf16[2,1600,384]{2,1,0:T(8,128)(2,1)}, u32[]{:S(2)}, u32[]{:S(2)}) collective-permute-start(bf16[2,1600,384]{2,1,0:T(8,128)(2,1)S(1)} %shard_map.73.refs_0_), channel_id=1, source_target_pairs={{0,1},{1,0},{2,3},{3,2},{4,5},{5,4},{6,7},{7,6},{8,9},{9,8},{10,11... | collective-permute-start | bytes 7372808 | tf_op jit(solution)/shard_map/ppermute | solution.py:300
  32.8 6.3 %collective-permute-start.8 = (bf16[2,96,625]{2,1,0:T(8,128)(2,1)S(1)}, bf16[2,96,625]{2,1,0:T(8,128)(2,1)S(1)}, u32[]{:S(2)}, u32[]{:S(2)}) collective-permute-start(bf16[2,96,625]{2,1,0:T(8,128)(2,1)S(1)} %collective-permute-done.5.refs_1_), channel_id=1, source_target_pairs={{0,16},{1,9},{2,18},{3,11},{4,20},{5,13},{6,22},{7,15},{8,24},{9,1... | collective-permute-start | bytes 720008 | tf_op jit(solution)/shard_map/ppermute | solution.py:314
  34.4 8.1 %collective-permute-start.11 = (bf16[2,96,625]{2,1,0:T(8,128)(2,1)S(1)}, bf16[2,96,625]{2,1,0:T(8,128)(2,1)S(1)}, u32[]{:S(2)}, u32[]{:S(2)}) collective-permute-start(bf16[2,96,625]{2,1,0:T(8,128)(2,1)S(1)} %get-tuple-element.45), channel_id=1, source_target_pairs={{0,6},{1,7},{2,0},{3,1},{4,2},{5,3},{6,4},{7,5},{8,14},{9,15},{10,... | collective-permute-start | bytes 720008 | tf_op jit(solution)/shard_map/ppermute | solution.py:303
  36.9 8.0 %collective-permute-start.10 = (bf16[2,96,625]{2,1,0:T(8,128)(2,1)S(1)}, bf16[2,96,625]{2,1,0:T(8,128)(2,1)S(1)}, u32[]{:S(2)}, u32[]{:S(2)}) collective-permute-start(bf16[2,96,625]{2,1,0:T(8,128)(2,1)S(1)} %collective-permute-done.7.refs_0_), channel_id=1, source_target_pairs={{0,16},{1,9},{2,18},{3,11},{4,20},{5,13},{6,22},{7,15},{8,24},{9,1... | collective-permute-start | bytes 720008 | tf_op jit(solution)/shard_map/ppermute | solution.py:314
  37.4 7.5 %collective-permute-start.9 = (bf16[2,96,625]{2,1,0:T(8,128)(2,1)S(1)}, bf16[2,96,625]{2,1,0:T(8,128)(2,1)S(1)}, u32[]{:S(2)}, u32[]{:S(2)}) collective-permute-start(bf16[2,96,625]{2,1,0:T(8,128)(2,1)S(1)} %collective-permute-done.7.refs_0_), channel_id=1, source_target_pairs={{0,8},{1,17},{2,10},{3,19},{4,12},{5,21},{6,14},{7,23},{8,0},{9,25... | collective-permute-start | bytes 720008 | tf_op jit(solution)/shard_map/ppermute | solution.py:313
  41.7 13.7 %copy-start = (bf16[2,1600,384]{2,1,0:T(8,128)(2,1)}, bf16[2,1600,384]{2,1,0:T(8,128)(2,1)S(1)}, u32[]{:S(2)}) copy-start(bf16[2,1600,384]{2,1,0:T(8,128)(2,1)S(1)} %shard_map.74.refs_2_) | copy-start | bytes 7372804
  41.7 11.1 %copy-start.9 = (bf16[1600,625]{1,0:T(8,128)(2,1)S(1)}, bf16[1600,625]{1,0:T(8,128)(2,1)}, u32[]{:S(2)}) copy-start(bf16[1600,625]{1,0:T(8,128)(2,1)} %constant.59.clone.refs_4_) | copy-start | bytes 6000004
  44.8 12.9 %collective-permute-start.17 = (bf16[2,1600,384]{2,1,0:T(8,128)(2,1)S(1)}, bf16[2,1600,384]{2,1,0:T(8,128)(2,1)}, u32[]{:S(2)}, u32[]{:S(2)}) collective-permute-start(bf16[2,1600,384]{2,1,0:T(8,128)(2,1)S(1)} %shard_map.74.refs_2_), channel_id=1, source_target_pairs={{0,1},{1,0},{2,3},{3,2},{4,5},{5,4},{6,7},{7,6},{8,9},{9,8},{10,11... | collective-permute-start | bytes 7372808 | tf_op jit(solution)/shard_map/ppermute | solution.py:300
  44.9 8.0 %collective-permute-start.13 = (bf16[2,96,625]{2,1,0:T(8,128)(2,1)S(1)}, bf16[2,96,625]{2,1,0:T(8,128)(2,1)S(1)}, u32[]{:S(2)}, u32[]{:S(2)}) collective-permute-start(bf16[2,96,625]{2,1,0:T(8,128)(2,1)S(1)} %collective-permute-done.9.refs_1_), channel_id=1, source_target_pairs={{0,16},{1,9},{2,18},{3,11},{4,20},{5,13},{6,22},{7,15},{8,24},{9,1... | collective-permute-start | bytes 720008 | tf_op jit(solution)/shard_map/ppermute | solution.py:314
  46.2 11.6 %collective-permute-start.16 = (bf16[625,256]{1,0:T(8,128)(2,1)}, bf16[625,256]{1,0:T(8,128)(2,1)S(1)}, u32[]{:S(2)}, u32[]{:S(2)}) collective-permute-start(bf16[625,256]{1,0:T(8,128)(2,1)} %collective-permute-done.3.refs_1_), channel_id=1, source_target_pairs={{0,2},{1,3},{2,4},{3,5},{4,6},{5,7},{6,0},{7,1},{8,10},{9,11},{10,... | collective-permute-start | bytes 960008 | tf_op jit(solution)/shard_map/ppermute | solution.py:303
  46.2 10.2 %collective-permute-start.15 = (bf16[2,96,625]{2,1,0:T(8,128)(2,1)S(1)}, bf16[2,96,625]{2,1,0:T(8,128)(2,1)S(1)}, u32[]{:S(2)}, u32[]{:S(2)}) collective-permute-start(bf16[2,96,625]{2,1,0:T(8,128)(2,1)S(1)} %collective-permute-done.11.refs_0_), channel_id=1, source_target_pairs={{0,16},{1,9},{2,18},{3,11},{4,20},{5,13},{6,22},{7,15},{8,24},{9,1... | collective-permute-start | bytes 720008 | tf_op jit(solution)/shard_map/ppermute | solution.py:314
  46.9 9.4 %collective-permute-start.14 = (bf16[2,96,625]{2,1,0:T(8,128)(2,1)S(1)}, bf16[2,96,625]{2,1,0:T(8,128)(2,1)S(1)}, u32[]{:S(2)}, u32[]{:S(2)}) collective-permute-start(bf16[2,96,625]{2,1,0:T(8,128)(2,1)S(1)} %collective-permute-done.11.refs_0_), channel_id=1, source_target_pairs={{0,8},{1,17},{2,10},{3,19},{4,12},{5,21},{6,14},{7,23},{8,0},{9,25... | collective-permute-start | bytes 720008 | tf_op jit(solution)/shard_map/ppermute | solution.py:313
  49.9 14.5 %copy-start.10 = (bf16[1600,625]{1,0:T(8,128)(2,1)S(1)}, bf16[1600,625]{1,0:T(8,128)(2,1)}, u32[]{:S(2)}) copy-start(bf16[1600,625]{1,0:T(8,128)(2,1)} %constant.59.clone.refs_4_) | copy-start | bytes 6000004
  55.5 12.4 %copy-start.1 = (bf16[2,1600,384]{2,1,0:T(8,128)(2,1)}, bf16[2,1600,384]{2,1,0:T(8,128)(2,1)S(1)}, u32[]{:S(2)}) copy-start(bf16[2,1600,384]{2,1,0:T(8,128)(2,1)S(1)} %shard_map.75.refs_4_) | copy-start | bytes 7372804
  57.8 13.4 %collective-permute-start.20 = (bf16[2,1600,384]{2,1,0:T(8,128)(2,1)S(1)}, bf16[2,1600,384]{2,1,0:T(8,128)(2,1)}, u32[]{:S(2)}, u32[]{:S(2)}) collective-permute-start(bf16[2,1600,384]{2,1,0:T(8,128)(2,1)S(1)} %shard_map.75.refs_4_), channel_id=1, source_target_pairs={{0,1},{1,0},{2,3},{3,2},{4,5},{5,4},{6,7},{7,6},{8,9},{9,8},{10,11... | collective-permute-start | bytes 7372808 | tf_op jit(solution)/shard_map/ppermute | solution.py:300
  57.8 12.4 %collective-permute-start.21 = (bf16[4,800,128]{2,1,0:T(8,128)(2,1)S(1)}, bf16[4,800,128]{2,1,0:T(8,128)(2,1)S(1)}, u32[]{:S(2)}, u32[]{:S(2)}) collective-permute-start(bf16[4,800,128]{2,1,0:T(8,128)(2,1)S(1)} %shard_map.76.refs_8_), channel_id=1, source_target_pairs={{0,1},{1,0},{2,3},{3,2},{4,5},{5,4},{6,7},{7,6},{8,9},{9,8},{10,11... | collective-permute-start | bytes 2457608 | tf_op jit(solution)/shard_map/ppermute | solution.py:300
  58.3 6.2 %collective-permute-start.18 = (bf16[2,96,625]{2,1,0:T(8,128)(2,1)S(1)}, bf16[2,96,625]{2,1,0:T(8,128)(2,1)S(1)}, u32[]{:S(2)}, u32[]{:S(2)}) collective-permute-start(bf16[2,96,625]{2,1,0:T(8,128)(2,1)S(1)} %collective-permute-done.14.refs_1_), channel_id=1, source_target_pairs={{0,16},{1,9},{2,18},{3,11},{4,20},{5,13},{6,22},{7,15},{8,24},{9,1... | collective-permute-start | bytes 720008 | tf_op jit(solution)/shard_map/ppermute | solution.py:314
  59.6 10.6 %collective-permute-start.19 = (bf16[625,256]{1,0:T(8,128)(2,1)S(1)}, bf16[625,256]{1,0:T(8,128)(2,1)S(1)}, u32[]{:S(2)}, u32[]{:S(2)}) collective-permute-start(bf16[625,256]{1,0:T(8,128)(2,1)S(1)} %collective-permute-done.16.refs_0_), channel_id=1, source_target_pairs={{0,2},{1,3},{2,4},{3,5},{4,6},{5,7},{6,0},{7,1},{8,10},{9,11},{10,... | collective-permute-start | bytes 960008 | tf_op jit(solution)/shard_map/ppermute | solution.py:303
  67.9 5.5 %copy-start.12 = (s32[32,3]{0,1:T(4,128)S(1)}, s32[32,3]{0,1:T(4,128)}, u32[]{:S(2)}) copy-start(s32[32,3]{0,1:T(4,128)} %param.10) | copy-start | bytes 1156
  67.9 5.5 %copy-start.13 = (s32[32,4]{0,1:T(4,128)S(1)}, s32[32,4]{0,1:T(4,128)}, u32[]{:S(2)}) copy-start(s32[32,4]{0,1:T(4,128)} %param.11) | copy-start | bytes 1540
  70.2 0.9 copy-start.2
  71.1 6.2 %collective-permute-start.22 = (bf16[2,1600,384]{2,1,0:T(8,128)(2,1)}, bf16[2,1600,384]{2,1,0:T(8,128)(2,1)}, u32[]{:S(2)}, u32[]{:S(2)}) collective-permute-start(bf16[2,1600,384]{2,1,0:T(8,128)(2,1)} %shard_map.77.refs_6_), channel_id=1, source_target_pairs={{0,1},{1,0},{2,3},{3,2},{4,5},{5,4},{6,7},{7,6},{8,9},{9,8},{10,11... | collective-permute-start | bytes 7372808 | tf_op jit(solution)/shard_map/ppermute | solution.py:300
  72.9 4.4 %collective-permute-start.23 = (bf16[4,800,128]{2,1,0:T(8,128)(2,1)}, bf16[4,800,128]{2,1,0:T(8,128)(2,1)}, u32[]{:S(2)}, u32[]{:S(2)}) collective-permute-start(bf16[4,800,128]{2,1,0:T(8,128)(2,1)} %shard_map.78.refs_10_), channel_id=1, source_target_pairs={{0,1},{1,0},{2,3},{3,2},{4,5},{5,4},{6,7},{7,6},{8,9},{9,8},{10,11... | collective-permute-start | bytes 2457608 | tf_op jit(solution)/shard_map/ppermute | solution.py:300
  77.3 1.1 copy-start.3
  89.2 34.6 %collective-permute-start.25 = (bf16[2,625,128]{2,1,0:T(8,128)(2,1)S(1)}, bf16[2,625,128]{2,1,0:T(8,128)(2,1)S(1)}, u32[]{:S(2)}, u32[]{:S(2)}) collective-permute-start(bf16[2,625,128]{2,1,0:T(8,128)(2,1)S(1)} %bitcast.26), channel_id=1, source_target_pairs={{0,4},{1,5},{2,6},{3,7},{4,0},{5,1},{6,2},{7,3},{8,12},{9,13},{10,... | collective-permute-start | bytes 960008 | tf_op jit(solution)/shard_map/ppermute | solution.py:303
  100.0 23.8 %collective-permute-start.24 = (bf16[2,625,128]{2,1,0:T(8,128)(2,1)S(1)}, bf16[2,625,128]{2,1,0:T(8,128)(2,1)S(1)}, u32[]{:S(2)}, u32[]{:S(2)}) collective-permute-start(bf16[2,625,128]{2,1,0:T(8,128)(2,1)S(1)} %bitcast.27), channel_id=1, source_target_pairs={{0,6},{1,7},{2,0},{3,1},{4,2},{5,3},{6,4},{7,5},{8,14},{9,15},{10,... | collective-permute-start | bytes 960008 | tf_op jit(solution)/shard_map/ppermute | solution.py:303
  112.1 11.7 %copy-start.11 = (f32[2,128,625]{1,0,2:T(2,128)S(1)}, f32[2,128,625]{1,0,2:T(2,128)}, u32[]{:S(2)}) copy-start(f32[2,128,625]{1,0,2:T(2,128)} %param.9) | copy-start | bytes 1920004
  112.1 11.7 %collective-permute-start.26 = (bf16[2,625,128]{2,1,0:T(8,128)(2,1)S(1)}, bf16[2,625,128]{2,1,0:T(8,128)(2,1)S(1)}, u32[]{:S(2)}, u32[]{:S(2)}) collective-permute-start(bf16[2,625,128]{2,1,0:T(8,128)(2,1)S(1)} %bitcast.28), channel_id=1, source_target_pairs={{0,2},{1,3},{2,4},{3,5},{4,6},{5,7},{6,0},{7,1},{8,10},{9,11},{10,... | collective-permute-start | bytes 960008 | tf_op jit(solution)/shard_map/ppermute | solution.py:303

commit v19 on v16

--- a/solution.py
+++ b/solution.py
@@ -22,6 +22,7 @@
 BF = jnp.bfloat16
 F32 = jnp.float32
 VMEM_BYTES = 48 * 1024 * 1024
+LADDER_VMEM_BYTES = 54 * 1024 * 1024
 
 
 def spread(spots, rows):
@@ -115,6 +116,13 @@
     return jnp.concatenate([ref[x * PAD : (x + 1) * PAD, :] for x in numbers], axis=0)
 
 
+def pick_blocks(blocks, low, even):
+    b0, b1, b2, b3 = blocks
+    x, y = jnp.where(low, b0, b2), jnp.where(low, b2, b0)
+    z, w = jnp.where(low, b1, b3), jnp.where(low, b3, b1)
+    return jnp.where(even, x, z), jnp.where(even, w, x), jnp.where(even, y, w), jnp.where(even, z, y)
+
+
 def ladder_kernel(find, made, sources, column_ref, owners_ref, local_ref, *refs):
     factor_refs, amp_refs, refs = refs[:sources], refs[sources : sources + 2], refs[sources + 2 :]
     matrix_ref, refs = None if made else refs[0], refs[0 if made else 1 :]
@@ -172,7 +180,7 @@
         c_form, r_form = forms.at[0], forms.at[1]
 
     spot = lax.broadcasted_iota(jnp.int32, (PAD, LANES), 1) // PAD
-    at_spot = [spot == p for p in range(GROUP)]
+    low, even = spot < 2, spot % 2 == 0
     nothing = jnp.zeros((PAD, LANES), F32)
     for first in range(0, GROUPS, 2):
         groups = range(first, min(first + 2, GROUPS))
@@ -192,10 +200,7 @@
                     else nothing
                     for g in range(GROUP)
                 ]
-                for i in range(min(GROUP, TV - A * GROUP)):
-                    block = blocks[-i % GROUP]
-                    for p in range(1, GROUP):
-                        block = jnp.where(at_spot[p], blocks[(p - i) % GROUP], block)
+                for i, block in enumerate(pick_blocks(blocks, low, even)[: TV - A * GROUP]):
                     u_ref[START[i] + A * PAD : START[i] + (A + 1) * PAD, D * LANES : (D + 1) * LANES] = block.astype(BF)
     out = local_ref[here["task"], 3]
     for i in range(GROUP):
@@ -264,7 +269,7 @@
             out_specs=pl.BlockSpec((1, blocks_here, TV * TV, pairs), lambda i, j, *tables: (i, 0, 0, 0)),
             scratch_shapes=scratch,
         ),
-        compiler_params=pltpu.CompilerParams(vmem_limit_bytes=VMEM_BYTES),
+        compiler_params=pltpu.CompilerParams(vmem_limit_bytes=LADDER_VMEM_BYTES),
         cost_estimate=pl.CostEstimate(
             flops=2 * columns * tasks * ROWS * WIDE * (depth + pairs),
             bytes_accessed=2 * columns * tasks * ROWS * 2 * (depth + pairs),
@@ -325,10 +330,10 @@
 
         forms2, part3, a3, b3, amp2, far1 = after((forms2, part3, a3, b3, amp2, far1), ())
         q3, amp3 = second_side(a3), around(amp2, 1)
-        far2 = other_core(forms2)
+        far2 = other_core(after(forms2, q3))
         forms3 = made_forms(part3, a3, b3, q3)
 
-        forms3, amp3, far2 = after((forms3, amp3, far2), ())
+        forms3, amp3 = after((forms3, amp3), ())
         far3 = other_core(forms3)
         amps = prepare_amps([own, amp1, amp2, amp3], blocks_here, jnp.asarray(amp_matrix()))
         held = [forms0, far0, forms1, far1, forms2, far2, forms3, far3]

time: 121 us -> 130 us (1.074)
  Pallas kernels: 50.4 us -> 62 us
  waiting for transfers between devices: 34.8 us -> 31.3 us
    pallas_call x4, Pallas kernels: 37.5 us -> 48.3 us  [ladders(): pl.pallas_call(functools.partial(ladder_kernel, find, made, len(tiles)),...]
    ppermute x9, waiting for transfers between devices: 12.3 us -> 10.1 us  [around(): lax.ppermute(x, 'task', [(c, (c + 2 * by) % task_count) for c in range(ta...]
    unnamed x29 -> x25, local copies, waits for them, and re-layouts: 8.2 us -> 8.77 us
  transfers between devices with their start and end apart: 26 -> 26, of which waited for: 13 -> 12; matrix products, arithmetic and copies ran while one was open for 3% -> 4% of each run, Pallas kernels for 34% -> 38%
where the time goes in v19:
time: 130 us
  Pallas kernels  62 us (48%)
  waiting for transfers between devices  31.3 us (24%)
  starting transfers between devices  24.8 us (19%)
  local copies, waits for them, and re-layouts  10.1 us (8%)
    pallas_call x4, Pallas kernels, ladders(): pl.pallas_call(functools.partial(ladder_kernel, find, made, len(tiles)),...  48.3 us
    ppermute x8, waiting for transfers between devices, per_device(): second_side = lambda x: lax.ppermute(x, ('pair', 'task'), sides[1])  17.6 us
    pallas_call x4, Pallas kernels, prepare(): pl.pallas_call(prepare_kernel, out_shape=jax.ShapeDtypeStruct((count, mat...  12.2 us
    ppermute x9, starting transfers between devices, around(): lax.ppermute(x, 'task', [(c, (c + 2 * by) % task_count) for c in range(ta...  10.3 us
    ppermute x9, waiting for transfers between devices, around(): lax.ppermute(x, 'task', [(c, (c + 2 * by) % task_count) for c in range(ta...  10.1 us
    ppermute x8, starting transfers between devices, per_device(): second_side = lambda x: lax.ppermute(x, ('pair', 'task'), sides[1])  9.13 us
    unnamed x25, local copies, waits for them, and re-layouts  8.77 us
    ppermute x4, starting transfers between devices, per_device(): first_side = lambda x: lax.ppermute(x, ('pair', 'task'), sides[0])  4.81 us
  transfers between devices with their start and end apart: 26, of which 12 were waited for; matrix products, arithmetic and copies ran while one was open for 4% of the time, Pallas kernels for 38%

profile of v19, /device:TPU:0, one launch (start us, length us, event | category | flops | bytes accessed | tf_op | source)
XLA Modules:
  0.0 129.6 jit_solution(14085959086804453065)
XLA Ops:
  0.0 1.2 pad
  1.3 3.1 %collective-permute-start.3 = (bf16[625,256]{1,0:T(8,128)(2,1)S(1)}, bf16[625,256]{1,0:T(8,128)(2,1)S(1)}, u32[]{:S(2)}, u32[]{:S(2)}) collective-permute-start(bf16[625,256]{1,0:T(8,128)(2,1)S(1)} %bitcast.24), channel_id=1, source_target_pairs={{0,2},{1,3},{2,4},{3,5},{4,6},{5,7},{6,0},{7,1},{8,10},{9,11},{10,... | collective-permute-start | bytes 960008 | tf_op jit(solution)/shard_map/ppermute | solution.py:299
  4.4 3.3 %copy.22 = bf16[2,384,625]{2,1,0:T(8,128)(2,1)S(1)} copy(bf16[2,384,625]{1,0,2:T(2,128)(2,1)} %param.7) | data formatting | bytes 1920000 | tf_op args[0]
  7.7 0.1 dynamic-slice_bitcast_fusion
  7.9 1.6 %collective-permute-start.2 = (bf16[2,96,625]{2,1,0:T(8,128)(2,1)S(1)}, bf16[2,96,625]{2,1,0:T(8,128)(2,1)S(1)}, u32[]{:S(2)}, u32[]{:S(2)}) collective-permute-start(bf16[2,96,625]{2,1,0:T(8,128)(2,1)S(1)} %get-tuple-element.63), channel_id=1, source_target_pairs={{0,2},{1,3},{2,4},{3,5},{4,6},{5,7},{6,0},{7,1},{8,10},{9,11},{10,... | collective-permute-start | bytes 720008 | tf_op jit(solution)/shard_map/ppermute | solution.py:299
  9.5 1.5 %collective-permute-start.1 = (bf16[2,96,625]{2,1,0:T(8,128)(2,1)S(1)}, bf16[2,96,625]{2,1,0:T(8,128)(2,1)S(1)}, u32[]{:S(2)}, u32[]{:S(2)}) collective-permute-start(bf16[2,96,625]{2,1,0:T(8,128)(2,1)S(1)} %get-tuple-element.33.refs_0_), channel_id=1, source_target_pairs={{0,16},{1,9},{2,18},{3,11},{4,20},{5,13},{6,22},{7,15},{8,24},{9,1... | collective-permute-start | bytes 720008 | tf_op jit(solution)/shard_map/ppermute | solution.py:310
  11.0 1.5 %collective-permute-start = (bf16[2,96,625]{2,1,0:T(8,128)(2,1)S(1)}, bf16[2,96,625]{2,1,0:T(8,128)(2,1)S(1)}, u32[]{:S(2)}, u32[]{:S(2)}) collective-permute-start(bf16[2,96,625]{2,1,0:T(8,128)(2,1)S(1)} %get-tuple-element.33.refs_0_), channel_id=1, source_target_pairs={{0,8},{1,17},{2,10},{3,19},{4,12},{5,21},{6,14},{7,23},{8,0},{9,25... | collective-permute-start | bytes 720008 | tf_op jit(solution)/shard_map/ppermute | solution.py:309
  12.5 6.8 %collective-permute-done.2.refs_0_ = bf16[2,96,625]{2,1,0:T(8,128)(2,1)S(1)} collective-permute-done((bf16[2,96,625]{2,1,0:T(8,128)(2,1)S(1)}, bf16[2,96,625]{2,1,0:T(8,128)(2,1)S(1)}, u32[]{:S(2)}, u32[]{:S(2)}) %collective-permute-start.2) | collective-permute-done | bytes 240032 | tf_op jit(solution)/shard_map/ppermute | solution.py:299
  19.3 0.0 collective-permute-done.1.refs_2_
  19.3 0.0 collective-permute-done.refs_1_
  19.3 0.0 collective-permute-done.3.refs_1_
  19.3 1.6 %collective-permute-start.4 = (bf16[2,96,625]{2,1,0:T(8,128)(2,1)S(1)}, bf16[2,96,625]{2,1,0:T(8,128)(2,1)S(1)}, u32[]{:S(2)}, u32[]{:S(2)}) collective-permute-start(bf16[2,96,625]{2,1,0:T(8,128)(2,1)S(1)} %collective-permute-done.refs_1_), channel_id=1, source_target_pairs={{0,16},{1,9},{2,18},{3,11},{4,20},{5,13},{6,22},{7,15},{8,24},{9,1... | collective-permute-start | bytes 720008 | tf_op jit(solution)/shard_map/ppermute | solution.py:310
  20.9 0.7 collective-permute-start.7
  21.6 0.5 collective-permute-start.6
  22.1 1.5 %collective-permute-start.5 = (bf16[2,96,625]{2,1,0:T(8,128)(2,1)S(1)}, bf16[2,96,625]{2,1,0:T(8,128)(2,1)S(1)}, u32[]{:S(2)}, u32[]{:S(2)}) collective-permute-start(bf16[2,96,625]{2,1,0:T(8,128)(2,1)S(1)} %collective-permute-done.2.refs_0_), channel_id=1, source_target_pairs={{0,8},{1,17},{2,10},{3,19},{4,12},{5,21},{6,14},{7,23},{8,0},{9,25... | collective-permute-start | bytes 720008 | tf_op jit(solution)/shard_map/ppermute | solution.py:309
  23.6 4.6 %collective-permute-done.4.refs_3_ = bf16[2,96,625]{2,1,0:T(8,128)(2,1)S(1)} collective-permute-done((bf16[2,96,625]{2,1,0:T(8,128)(2,1)S(1)}, bf16[2,96,625]{2,1,0:T(8,128)(2,1)S(1)}, u32[]{:S(2)}, u32[]{:S(2)}) %collective-permute-start.4) | collective-permute-done | bytes 240032 | tf_op jit(solution)/shard_map/ppermute | solution.py:310
  28.2 1.6 %copy-done.4 = bf16[1600,625]{1,0:T(8,128)(2,1)S(1)} copy-done((bf16[1600,625]{1,0:T(8,128)(2,1)S(1)}, bf16[1600,625]{1,0:T(8,128)(2,1)}, u32[]{:S(2)}) %copy-start.4) | copy-done | bytes 2000024
  29.7 2.6 %shard_map.73.refs_0_ = bf16[2,1600,384]{2,1,0:T(8,128)(2,1)S(1)} custom-call(s32[1]{0:T(128)} %bitcast.column_ref, bf16[2,96,625]{2,1,0:T(8,128)(2,1)S(1)} %get-tuple-element.33.refs_0_, bf16[2,96,625]{2,1,0:T(8,128)(2,1)S(1)} %collective-permute-done.refs_1_, bf16[2,96,625]{2,1,0:T(8,128)(2,1)S(1)} %collective-permute-done.1.refs_2_, ...), custom_call_target="tpu_custom_call" | custom-call | flops 1536000000 | bytes 3417600 | tf_op jit(solution)/shard_map/pallas_call | solution.py:73
  32.4 0.3 collective-permute-done.7.refs_0_
  32.7 0.0 collective-permute-done.6.refs_2_
  32.7 0.0 collective-permute-done.5.refs_1_
  32.7 0.0 collective-permute-start.12
  32.7 1.6 %collective-permute-start.8 = (bf16[2,96,625]{2,1,0:T(8,128)(2,1)S(1)}, bf16[2,96,625]{2,1,0:T(8,128)(2,1)S(1)}, u32[]{:S(2)}, u32[]{:S(2)}) collective-permute-start(bf16[2,96,625]{2,1,0:T(8,128)(2,1)S(1)} %collective-permute-done.5.refs_1_), channel_id=1, source_target_pairs={{0,16},{1,9},{2,18},{3,11},{4,20},{5,13},{6,22},{7,15},{8,24},{9,1... | collective-permute-start | bytes 720008 | tf_op jit(solution)/shard_map/ppermute | solution.py:310
  34.3 2.5 %collective-permute-start.11 = (bf16[2,96,625]{2,1,0:T(8,128)(2,1)S(1)}, bf16[2,96,625]{2,1,0:T(8,128)(2,1)S(1)}, u32[]{:S(2)}, u32[]{:S(2)}) collective-permute-start(bf16[2,96,625]{2,1,0:T(8,128)(2,1)S(1)} %get-tuple-element.43), channel_id=1, source_target_pairs={{0,6},{1,7},{2,0},{3,1},{4,2},{5,3},{6,4},{7,5},{8,14},{9,15},{10,... | collective-permute-start | bytes 720008 | tf_op jit(solution)/shard_map/ppermute | solution.py:299
  36.8 0.5 collective-permute-start.10
  37.3 0.6 collective-permute-start.9
  37.9 1.0 collective-permute-done.8.refs_3_
  39.0 2.6 %shard_map.74.refs_2_ = bf16[2,1600,384]{2,1,0:T(8,128)(2,1)S(1)} custom-call(s32[1]{0:T(128)} %bitcast.column_ref, bf16[2,96,625]{2,1,0:T(8,128)(2,1)S(1)} %collective-permute-done.2.refs_0_, bf16[2,96,625]{2,1,0:T(8,128)(2,1)S(1)} %collective-permute-done.5.refs_1_, bf16[2,96,625]{2,1,0:T(8,128)(2,1)S(1)} %collective-permute-done.6.refs_2_, ...), custom_call_target="tpu_custom_call" | custom-call | flops 1536000000 | bytes 3417600 | tf_op jit(solution)/shard_map/pallas_call | solution.py:73
  41.7 0.8 collective-permute-done.11.refs_0_
  42.4 2.3 %collective-permute-done.10.refs_2_ = bf16[2,96,625]{2,1,0:T(8,128)(2,1)S(1)} collective-permute-done((bf16[2,96,625]{2,1,0:T(8,128)(2,1)S(1)}, bf16[2,96,625]{2,1,0:T(8,128)(2,1)S(1)}, u32[]{:S(2)}, u32[]{:S(2)}) %collective-permute-start.10) | collective-permute-done | bytes 240032 | tf_op jit(solution)/shard_map/ppermute | solution.py:310
  44.7 0.0 collective-permute-done.9.refs_1_
  44.7 0.0 collective-permute-done.12.refs_1_
  44.8 0.0 collective-permute-start.17
  44.8 1.3 %collective-permute-start.13 = (bf16[2,96,625]{2,1,0:T(8,128)(2,1)S(1)}, bf16[2,96,625]{2,1,0:T(8,128)(2,1)S(1)}, u32[]{:S(2)}, u32[]{:S(2)}) collective-permute-start(bf16[2,96,625]{2,1,0:T(8,128)(2,1)S(1)} %collective-permute-done.9.refs_1_), channel_id=1, source_target_pairs={{0,16},{1,9},{2,18},{3,11},{4,20},{5,13},{6,22},{7,15},{8,24},{9,1... | collective-permute-start | bytes 720008 | tf_op jit(solution)/shard_map/ppermute | solution.py:310
  46.1 0.0 collective-permute-start.16
  46.1 0.8 collective-permute-start.15
  46.9 1.2 collective-permute-start.14
  48.0 4.7 %collective-permute-done.13.refs_3_ = bf16[2,96,625]{2,1,0:T(8,128)(2,1)S(1)} collective-permute-done((bf16[2,96,625]{2,1,0:T(8,128)(2,1)S(1)}, bf16[2,96,625]{2,1,0:T(8,128)(2,1)S(1)}, u32[]{:S(2)}, u32[]{:S(2)}) %collective-permute-start.13) | collective-permute-done | bytes 240032 | tf_op jit(solution)/shard_map/ppermute | solution.py:310
  52.7 3.4 %shard_map.75.refs_4_ = bf16[2,1600,384]{2,1,0:T(8,128)(2,1)} custom-call(s32[1]{0:T(128)} %bitcast.column_ref, bf16[2,96,625]{2,1,0:T(8,128)(2,1)S(1)} %collective-permute-done.7.refs_0_, bf16[2,96,625]{2,1,0:T(8,128)(2,1)S(1)} %collective-permute-done.9.refs_1_, bf16[2,96,625]{2,1,0:T(8,128)(2,1)S(1)} %collective-permute-done.10.refs_2_, ...), custom_call_target="tpu_custom_call" | custom-call | flops 1536000000 | bytes 3417600 | tf_op jit(solution)/shard_map/pallas_call | solution.py:73
  56.2 0.1 collective-permute-done.15.refs_2_
  56.3 0.0 collective-permute-done.14.refs_1_
  56.3 1.2 collective-permute-done.16.refs_2_
  57.4 0.0 collective-permute-done.17.refs_3_
  57.5 1.3 %collective-permute-start.18 = (bf16[2,96,625]{2,1,0:T(8,128)(2,1)S(1)}, bf16[2,96,625]{2,1,0:T(8,128)(2,1)S(1)}, u32[]{:S(2)}, u32[]{:S(2)}) collective-permute-start(bf16[2,96,625]{2,1,0:T(8,128)(2,1)S(1)} %collective-permute-done.14.refs_1_), channel_id=1, source_target_pairs={{0,16},{1,9},{2,18},{3,11},{4,20},{5,13},{6,22},{7,15},{8,24},{9,1... | collective-permute-start | bytes 720008 | tf_op jit(solution)/shard_map/ppermute | solution.py:310
  58.8 4.9 %collective-permute-done.18.refs_3_ = bf16[2,96,625]{2,1,0:T(8,128)(2,1)S(1)} collective-permute-done((bf16[2,96,625]{2,1,0:T(8,128)(2,1)S(1)}, bf16[2,96,625]{2,1,0:T(8,128)(2,1)S(1)}, u32[]{:S(2)}, u32[]{:S(2)}) %collective-permute-start.18) | collective-permute-done | bytes 240032 | tf_op jit(solution)/shard_map/ppermute | solution.py:310
  63.7 3.5 %shard_map.76.refs_6_ = bf16[2,1600,384]{2,1,0:T(8,128)(2,1)} custom-call(s32[1]{0:T(128)} %bitcast.column_ref, bf16[2,96,625]{2,1,0:T(8,128)(2,1)S(1)} %collective-permute-done.11.refs_0_, bf16[2,96,625]{2,1,0:T(8,128)(2,1)S(1)} %collective-permute-done.14.refs_1_, bf16[2,96,625]{2,1,0:T(8,128)(2,1)S(1)} %collective-permute-done.15.refs_2_, ...), custom_call_target="tpu_custom_call" | custom-call | flops 1536000000 | bytes 3417600 | tf_op jit(solution)/shard_map/pallas_call | solution.py:73
  67.1 1.1 collective-permute-done.20.refs_3_
  68.2 1.4 %shard_map.77.refs_8_ = bf16[8,800,128]{2,1,0:T(8,128)(2,1)S(1)} custom-call(bf16[800,625]{1,0:T(8,128)(2,1)S(1)} %copy-done.3, bf16[625,256]{1,0:T(8,128)(2,1)S(1)} %bitcast.25, bf16[625,256]{1,0:T(8,128)(2,1)S(1)} %collective-permute-done.3.refs_1_, bf16[625,256]{1,0:T(8,128)(2,1)S(1)} %collective-permute-done.16.refs_2_, ...), custom_call_target="tpu_custom_call" | custom-call | flops 1024000000 | bytes 2560000 | tf_op jit(solution)/shard_map/pallas_call | solution.py:104
  69.7 0.6 collective-permute-start.22
  70.2 0.7 copy.23.owners_ref
  70.9 0.7 copy.24.local_ref
  71.6 3.6 %collective-permute-done.22.refs_9_ = bf16[8,800,128]{2,1,0:T(8,128)(2,1)S(1)} collective-permute-done((bf16[8,800,128]{2,1,0:T(8,128)(2,1)S(1)}, bf16[8,800,128]{2,1,0:T(8,128)(2,1)S(1)}, u32[]{:S(2)}, u32[]{:S(2)}) %collective-permute-start.22) | collective-permute-done | bytes 1638432 | tf_op jit(solution)/shard_map/ppermute | solution.py:296
  75.2 1.2 copy-done.6
  76.4 12.1 %shard_map.79 = bf16[1,2,625,128]{3,2,1,0:T(8,128)(2,1)} custom-call(s32[1]{0:T(128)} %bitcast.column_ref, s32[32,3]{1,0:T(8,128)} %copy.23.owners_ref, s32[32,4]{1,0:T(8,128)} %copy.24.local_ref, bf16[2,1600,384]{2,1,0:T(8,128)(2,1)} %copy-done.1, bf16[2,1600,384]{2,1,0:T(8,128)(2,1)} %collective-permute-done.12.refs_1_, bf16[2,1600,384]{2,1,0:T(8,128)(2,1)} %copy-done.2, ...), custom_call_target="tpu_custom_call" | custom-call | flops 2936012800 | bytes 6553600 | tf_op jit(solution)/shard_map/pallas_call | solution.py:262
  88.5 0.1 collective-permute-start.24
  88.6 12.1 %shard_map.78 = bf16[1,2,625,128]{3,2,1,0:T(8,128)(2,1)} custom-call(s32[1]{0:T(128)} %bitcast.column_ref, s32[32,3]{1,0:T(8,128)} %copy.23.owners_ref, s32[32,4]{1,0:T(8,128)} %copy.24.local_ref, bf16[2,1600,384]{2,1,0:T(8,128)(2,1)} %copy-done.1, bf16[2,1600,384]{2,1,0:T(8,128)(2,1)} %collective-permute-done.12.refs_1_, bf16[2,1600,384]{2,1,0:T(8,128)(2,1)} %copy-done.2, ...), custom_call_target="tpu_custom_call" | custom-call | flops 2936012800 | bytes 6553600 | tf_op jit(solution)/shard_map/pallas_call | solution.py:262
  100.7 1.1 collective-permute-start.23
  101.8 12.1 %shard_map.80 = bf16[1,2,625,128]{3,2,1,0:T(8,128)(2,1)} custom-call(s32[1]{0:T(128)} %bitcast.column_ref, s32[32,3]{1,0:T(8,128)} %copy.23.owners_ref, s32[32,4]{1,0:T(8,128)} %copy.24.local_ref, bf16[2,1600,384]{2,1,0:T(8,128)(2,1)} %copy-done.1, bf16[2,1600,384]{2,1,0:T(8,128)(2,1)} %collective-permute-done.12.refs_1_, bf16[2,1600,384]{2,1,0:T(8,128)(2,1)} %copy-done.2, ...), custom_call_target="tpu_custom_call" | custom-call | flops 2936012800 | bytes 6553600 | tf_op jit(solution)/shard_map/pallas_call | solution.py:262
  113.9 0.0 copy-start.7
  113.9 1.2 collective-permute-start.25
  115.1 12.1 %shard_map.81 = bf16[1,2,625,128]{3,2,1,0:T(8,128)(2,1)} custom-call(s32[1]{0:T(128)} %bitcast.column_ref, s32[32,3]{1,0:T(8,128)} %copy.23.owners_ref, s32[32,4]{1,0:T(8,128)} %copy.24.local_ref, bf16[2,1600,384]{2,1,0:T(8,128)(2,1)} %copy-done.1, bf16[2,1600,384]{2,1,0:T(8,128)(2,1)} %collective-permute-done.12.refs_1_, bf16[2,1600,384]{2,1,0:T(8,128)(2,1)} %copy-done.2, ...), custom_call_target="tpu_custom_call" | custom-call | flops 2936012800 | bytes 6553600 | tf_op jit(solution)/shard_map/pallas_call | solution.py:262
  127.2 0.0 collective-permute-done.25
  127.2 1.2 fusion.1
  128.4 1.2 copy.32
  (25 shorter events, 0.1 us)
Async XLA Ops:
  1.3 18.0 %collective-permute-start.3 = (bf16[625,256]{1,0:T(8,128)(2,1)S(1)}, bf16[625,256]{1,0:T(8,128)(2,1)S(1)}, u32[]{:S(2)}, u32[]{:S(2)}) collective-permute-start(bf16[625,256]{1,0:T(8,128)(2,1)S(1)} %bitcast.24), channel_id=1, source_target_pairs={{0,2},{1,3},{2,4},{3,5},{4,6},{5,7},{6,0},{7,1},{8,10},{9,11},{10,... | collective-permute-start | bytes 960008 | tf_op jit(solution)/shard_map/ppermute | solution.py:299
  7.9 11.4 %collective-permute-start.2 = (bf16[2,96,625]{2,1,0:T(8,128)(2,1)S(1)}, bf16[2,96,625]{2,1,0:T(8,128)(2,1)S(1)}, u32[]{:S(2)}, u32[]{:S(2)}) collective-permute-start(bf16[2,96,625]{2,1,0:T(8,128)(2,1)S(1)} %get-tuple-element.63), channel_id=1, source_target_pairs={{0,2},{1,3},{2,4},{3,5},{4,6},{5,7},{6,0},{7,1},{8,10},{9,11},{10,... | collective-permute-start | bytes 720008 | tf_op jit(solution)/shard_map/ppermute | solution.py:299
  9.5 9.8 %collective-permute-start.1 = (bf16[2,96,625]{2,1,0:T(8,128)(2,1)S(1)}, bf16[2,96,625]{2,1,0:T(8,128)(2,1)S(1)}, u32[]{:S(2)}, u32[]{:S(2)}) collective-permute-start(bf16[2,96,625]{2,1,0:T(8,128)(2,1)S(1)} %get-tuple-element.33.refs_0_), channel_id=1, source_target_pairs={{0,16},{1,9},{2,18},{3,11},{4,20},{5,13},{6,22},{7,15},{8,24},{9,1... | collective-permute-start | bytes 720008 | tf_op jit(solution)/shard_map/ppermute | solution.py:310
  11.0 8.3 %collective-permute-start = (bf16[2,96,625]{2,1,0:T(8,128)(2,1)S(1)}, bf16[2,96,625]{2,1,0:T(8,128)(2,1)S(1)}, u32[]{:S(2)}, u32[]{:S(2)}) collective-permute-start(bf16[2,96,625]{2,1,0:T(8,128)(2,1)S(1)} %get-tuple-element.33.refs_0_), channel_id=1, source_target_pairs={{0,8},{1,17},{2,10},{3,19},{4,12},{5,21},{6,14},{7,23},{8,0},{9,25... | collective-permute-start | bytes 720008 | tf_op jit(solution)/shard_map/ppermute | solution.py:309
  19.3 8.9 %collective-permute-start.4 = (bf16[2,96,625]{2,1,0:T(8,128)(2,1)S(1)}, bf16[2,96,625]{2,1,0:T(8,128)(2,1)S(1)}, u32[]{:S(2)}, u32[]{:S(2)}) collective-permute-start(bf16[2,96,625]{2,1,0:T(8,128)(2,1)S(1)} %collective-permute-done.refs_1_), channel_id=1, source_target_pairs={{0,16},{1,9},{2,18},{3,11},{4,20},{5,13},{6,22},{7,15},{8,24},{9,1... | collective-permute-start | bytes 720008 | tf_op jit(solution)/shard_map/ppermute | solution.py:310
  20.9 11.8 %collective-permute-start.7 = (bf16[2,96,625]{2,1,0:T(8,128)(2,1)S(1)}, bf16[2,96,625]{2,1,0:T(8,128)(2,1)S(1)}, u32[]{:S(2)}, u32[]{:S(2)}) collective-permute-start(bf16[2,96,625]{2,1,0:T(8,128)(2,1)S(1)} %get-tuple-element.37), channel_id=1, source_target_pairs={{0,4},{1,5},{2,6},{3,7},{4,0},{5,1},{6,2},{7,3},{8,12},{9,13},{10,... | collective-permute-start | bytes 720008 | tf_op jit(solution)/shard_map/ppermute | solution.py:299
  21.6 11.1 %collective-permute-start.6 = (bf16[2,96,625]{2,1,0:T(8,128)(2,1)S(1)}, bf16[2,96,625]{2,1,0:T(8,128)(2,1)S(1)}, u32[]{:S(2)}, u32[]{:S(2)}) collective-permute-start(bf16[2,96,625]{2,1,0:T(8,128)(2,1)S(1)} %collective-permute-done.2.refs_0_), channel_id=1, source_target_pairs={{0,16},{1,9},{2,18},{3,11},{4,20},{5,13},{6,22},{7,15},{8,24},{9,1... | collective-permute-start | bytes 720008 | tf_op jit(solution)/shard_map/ppermute | solution.py:310
  22.1 10.6 %collective-permute-start.5 = (bf16[2,96,625]{2,1,0:T(8,128)(2,1)S(1)}, bf16[2,96,625]{2,1,0:T(8,128)(2,1)S(1)}, u32[]{:S(2)}, u32[]{:S(2)}) collective-permute-start(bf16[2,96,625]{2,1,0:T(8,128)(2,1)S(1)} %collective-permute-done.2.refs_0_), channel_id=1, source_target_pairs={{0,8},{1,17},{2,10},{3,19},{4,12},{5,21},{6,14},{7,23},{8,0},{9,25... | collective-permute-start | bytes 720008 | tf_op jit(solution)/shard_map/ppermute | solution.py:309
  28.2 1.6 %copy-start.4 = (bf16[1600,625]{1,0:T(8,128)(2,1)S(1)}, bf16[1600,625]{1,0:T(8,128)(2,1)}, u32[]{:S(2)}) copy-start(bf16[1600,625]{1,0:T(8,128)(2,1)} %constant.59.clone.refs_4_) | copy-start | bytes 6000004
  29.7 9.3 %copy-start.5 = (bf16[1600,625]{1,0:T(8,128)(2,1)S(1)}, bf16[1600,625]{1,0:T(8,128)(2,1)}, u32[]{:S(2)}) copy-start(bf16[1600,625]{1,0:T(8,128)(2,1)} %constant.59.clone.refs_4_) | copy-start | bytes 6000004
  32.4 9.3 %copy-start.1 = (bf16[2,1600,384]{2,1,0:T(8,128)(2,1)}, bf16[2,1600,384]{2,1,0:T(8,128)(2,1)S(1)}, u32[]{:S(2)}) copy-start(bf16[2,1600,384]{2,1,0:T(8,128)(2,1)S(1)} %shard_map.73.refs_0_) | copy-start | bytes 7372804
  32.7 12.0 %collective-permute-start.12 = (bf16[2,1600,384]{2,1,0:T(8,128)(2,1)S(1)}, bf16[2,1600,384]{2,1,0:T(8,128)(2,1)}, u32[]{:S(2)}, u32[]{:S(2)}) collective-permute-start(bf16[2,1600,384]{2,1,0:T(8,128)(2,1)S(1)} %shard_map.73.refs_0_), channel_id=1, source_target_pairs={{0,1},{1,0},{2,3},{3,2},{4,5},{5,4},{6,7},{7,6},{8,9},{9,8},{10,11... | collective-permute-start | bytes 7372808 | tf_op jit(solution)/shard_map/ppermute | solution.py:296
  32.7 6.3 %collective-permute-start.8 = (bf16[2,96,625]{2,1,0:T(8,128)(2,1)S(1)}, bf16[2,96,625]{2,1,0:T(8,128)(2,1)S(1)}, u32[]{:S(2)}, u32[]{:S(2)}) collective-permute-start(bf16[2,96,625]{2,1,0:T(8,128)(2,1)S(1)} %collective-permute-done.5.refs_1_), channel_id=1, source_target_pairs={{0,16},{1,9},{2,18},{3,11},{4,20},{5,13},{6,22},{7,15},{8,24},{9,1... | collective-permute-start | bytes 720008 | tf_op jit(solution)/shard_map/ppermute | solution.py:310
  34.3 8.1 %collective-permute-start.11 = (bf16[2,96,625]{2,1,0:T(8,128)(2,1)S(1)}, bf16[2,96,625]{2,1,0:T(8,128)(2,1)S(1)}, u32[]{:S(2)}, u32[]{:S(2)}) collective-permute-start(bf16[2,96,625]{2,1,0:T(8,128)(2,1)S(1)} %get-tuple-element.43), channel_id=1, source_target_pairs={{0,6},{1,7},{2,0},{3,1},{4,2},{5,3},{6,4},{7,5},{8,14},{9,15},{10,... | collective-permute-start | bytes 720008 | tf_op jit(solution)/shard_map/ppermute | solution.py:299
  36.8 8.0 %collective-permute-start.10 = (bf16[2,96,625]{2,1,0:T(8,128)(2,1)S(1)}, bf16[2,96,625]{2,1,0:T(8,128)(2,1)S(1)}, u32[]{:S(2)}, u32[]{:S(2)}) collective-permute-start(bf16[2,96,625]{2,1,0:T(8,128)(2,1)S(1)} %collective-permute-done.7.refs_0_), channel_id=1, source_target_pairs={{0,16},{1,9},{2,18},{3,11},{4,20},{5,13},{6,22},{7,15},{8,24},{9,1... | collective-permute-start | bytes 720008 | tf_op jit(solution)/shard_map/ppermute | solution.py:310
  37.3 7.5 %collective-permute-start.9 = (bf16[2,96,625]{2,1,0:T(8,128)(2,1)S(1)}, bf16[2,96,625]{2,1,0:T(8,128)(2,1)S(1)}, u32[]{:S(2)}, u32[]{:S(2)}) collective-permute-start(bf16[2,96,625]{2,1,0:T(8,128)(2,1)S(1)} %collective-permute-done.7.refs_0_), channel_id=1, source_target_pairs={{0,8},{1,17},{2,10},{3,19},{4,12},{5,21},{6,14},{7,23},{8,0},{9,25... | collective-permute-start | bytes 720008 | tf_op jit(solution)/shard_map/ppermute | solution.py:309
  41.6 14.5 %copy-start.2 = (bf16[2,1600,384]{2,1,0:T(8,128)(2,1)}, bf16[2,1600,384]{2,1,0:T(8,128)(2,1)S(1)}, u32[]{:S(2)}) copy-start(bf16[2,1600,384]{2,1,0:T(8,128)(2,1)S(1)} %shard_map.74.refs_2_) | copy-start | bytes 7372804
  44.8 12.7 %collective-permute-start.17 = (bf16[2,1600,384]{2,1,0:T(8,128)(2,1)S(1)}, bf16[2,1600,384]{2,1,0:T(8,128)(2,1)}, u32[]{:S(2)}, u32[]{:S(2)}) collective-permute-start(bf16[2,1600,384]{2,1,0:T(8,128)(2,1)S(1)} %shard_map.74.refs_2_), channel_id=1, source_target_pairs={{0,1},{1,0},{2,3},{3,2},{4,5},{5,4},{6,7},{7,6},{8,9},{9,8},{10,11... | collective-permute-start | bytes 7372808 | tf_op jit(solution)/shard_map/ppermute | solution.py:296
  44.8 8.0 %collective-permute-start.13 = (bf16[2,96,625]{2,1,0:T(8,128)(2,1)S(1)}, bf16[2,96,625]{2,1,0:T(8,128)(2,1)S(1)}, u32[]{:S(2)}, u32[]{:S(2)}) collective-permute-start(bf16[2,96,625]{2,1,0:T(8,128)(2,1)S(1)} %collective-permute-done.9.refs_1_), channel_id=1, source_target_pairs={{0,16},{1,9},{2,18},{3,11},{4,20},{5,13},{6,22},{7,15},{8,24},{9,1... | collective-permute-start | bytes 720008 | tf_op jit(solution)/shard_map/ppermute | solution.py:310
  46.1 11.4 %collective-permute-start.16 = (bf16[625,256]{1,0:T(8,128)(2,1)S(1)}, bf16[625,256]{1,0:T(8,128)(2,1)S(1)}, u32[]{:S(2)}, u32[]{:S(2)}) collective-permute-start(bf16[625,256]{1,0:T(8,128)(2,1)S(1)} %collective-permute-done.3.refs_1_), channel_id=1, source_target_pairs={{0,2},{1,3},{2,4},{3,5},{4,6},{5,7},{6,0},{7,1},{8,10},{9,11},{10,... | collective-permute-start | bytes 960008 | tf_op jit(solution)/shard_map/ppermute | solution.py:299
  46.1 10.2 %collective-permute-start.15 = (bf16[2,96,625]{2,1,0:T(8,128)(2,1)S(1)}, bf16[2,96,625]{2,1,0:T(8,128)(2,1)S(1)}, u32[]{:S(2)}, u32[]{:S(2)}) collective-permute-start(bf16[2,96,625]{2,1,0:T(8,128)(2,1)S(1)} %collective-permute-done.11.refs_0_), channel_id=1, source_target_pairs={{0,16},{1,9},{2,18},{3,11},{4,20},{5,13},{6,22},{7,15},{8,24},{9,1... | collective-permute-start | bytes 720008 | tf_op jit(solution)/shard_map/ppermute | solution.py:310
  46.9 9.4 %collective-permute-start.14 = (bf16[2,96,625]{2,1,0:T(8,128)(2,1)S(1)}, bf16[2,96,625]{2,1,0:T(8,128)(2,1)S(1)}, u32[]{:S(2)}, u32[]{:S(2)}) collective-permute-start(bf16[2,96,625]{2,1,0:T(8,128)(2,1)S(1)} %collective-permute-done.11.refs_0_), channel_id=1, source_target_pairs={{0,8},{1,17},{2,10},{3,19},{4,12},{5,21},{6,14},{7,23},{8,0},{9,25... | collective-permute-start | bytes 720008 | tf_op jit(solution)/shard_map/ppermute | solution.py:309
  56.2 12.0 %copy-start.3 = (bf16[800,625]{1,0:T(8,128)(2,1)S(1)}, bf16[800,625]{1,0:T(8,128)(2,1)}, u32[]{:S(2)}) copy-start(bf16[800,625]{1,0:T(8,128)(2,1)} %constant.60.clone.matrix_ref) | copy-start | bytes 3000004
  57.5 6.2 %collective-permute-start.18 = (bf16[2,96,625]{2,1,0:T(8,128)(2,1)S(1)}, bf16[2,96,625]{2,1,0:T(8,128)(2,1)S(1)}, u32[]{:S(2)}, u32[]{:S(2)}) collective-permute-start(bf16[2,96,625]{2,1,0:T(8,128)(2,1)S(1)} %collective-permute-done.14.refs_1_), channel_id=1, source_target_pairs={{0,16},{1,9},{2,18},{3,11},{4,20},{5,13},{6,22},{7,15},{8,24},{9,1... | collective-permute-start | bytes 720008 | tf_op jit(solution)/shard_map/ppermute | solution.py:310
  58.8 9.4 %collective-permute-start.20 = (bf16[625,256]{1,0:T(8,128)(2,1)S(1)}, bf16[625,256]{1,0:T(8,128)(2,1)S(1)}, u32[]{:S(2)}, u32[]{:S(2)}) collective-permute-start(bf16[625,256]{1,0:T(8,128)(2,1)S(1)} %collective-permute-done.16.refs_2_), channel_id=1, source_target_pairs={{0,2},{1,3},{2,4},{3,5},{4,6},{5,7},{6,0},{7,1},{8,10},{9,11},{10,... | collective-permute-start | bytes 960008 | tf_op jit(solution)/shard_map/ppermute | solution.py:299
  63.6 11.6 %collective-permute-start.19 = (bf16[2,1600,384]{2,1,0:T(8,128)(2,1)}, bf16[2,1600,384]{2,1,0:T(8,128)(2,1)}, u32[]{:S(2)}, u32[]{:S(2)}) collective-permute-start(bf16[2,1600,384]{2,1,0:T(8,128)(2,1)} %shard_map.75.refs_4_), channel_id=1, source_target_pairs={{0,1},{1,0},{2,3},{3,2},{4,5},{5,4},{6,7},{7,6},{8,9},{9,8},{10,11... | collective-permute-start | bytes 7372808 | tf_op jit(solution)/shard_map/ppermute | solution.py:296
  67.1 3.1 %copy-start.8 = (s32[32,3]{0,1:T(4,128)S(1)}, s32[32,3]{0,1:T(4,128)}, u32[]{:S(2)}) copy-start(s32[32,3]{0,1:T(4,128)} %param.10) | copy-start | bytes 1156
  67.1 3.8 %copy-start.9 = (s32[32,4]{0,1:T(4,128)S(1)}, s32[32,4]{0,1:T(4,128)}, u32[]{:S(2)}) copy-start(s32[32,4]{0,1:T(4,128)} %param.11) | copy-start | bytes 1540
  68.2 7.0 %collective-permute-start.21 = (bf16[2,1600,384]{2,1,0:T(8,128)(2,1)}, bf16[2,1600,384]{2,1,0:T(8,128)(2,1)}, u32[]{:S(2)}, u32[]{:S(2)}) collective-permute-start(bf16[2,1600,384]{2,1,0:T(8,128)(2,1)} %shard_map.76.refs_6_), channel_id=1, source_target_pairs={{0,1},{1,0},{2,3},{3,2},{4,5},{5,4},{6,7},{7,6},{8,9},{9,8},{10,11... | collective-permute-start | bytes 7372808 | tf_op jit(solution)/shard_map/ppermute | solution.py:296
  69.7 5.6 %copy-start = (bf16[8,800,128]{2,1,0:T(8,128)(2,1)}, bf16[8,800,128]{2,1,0:T(8,128)(2,1)S(1)}, u32[]{:S(2)}) copy-start(bf16[8,800,128]{2,1,0:T(8,128)(2,1)S(1)} %shard_map.77.refs_8_) | copy-start | bytes 4915204
  69.7 5.6 %collective-permute-start.22 = (bf16[8,800,128]{2,1,0:T(8,128)(2,1)S(1)}, bf16[8,800,128]{2,1,0:T(8,128)(2,1)S(1)}, u32[]{:S(2)}, u32[]{:S(2)}) collective-permute-start(bf16[8,800,128]{2,1,0:T(8,128)(2,1)S(1)} %shard_map.77.refs_8_), channel_id=1, source_target_pairs={{0,1},{1,0},{2,3},{3,2},{4,5},{5,4},{6,7},{7,6},{8,9},{9,8},{10,11... | collective-permute-start | bytes 4915208 | tf_op jit(solution)/shard_map/ppermute | solution.py:296
  75.2 1.2 copy-start.6
  88.5 38.7 %collective-permute-start.24 = (bf16[2,625,128]{2,1,0:T(8,128)(2,1)}, bf16[2,625,128]{2,1,0:T(8,128)(2,1)S(1)}, u32[]{:S(2)}, u32[]{:S(2)}) collective-permute-start(bf16[2,625,128]{2,1,0:T(8,128)(2,1)} %bitcast.28), channel_id=1, source_target_pairs={{0,4},{1,5},{2,6},{3,7},{4,0},{5,1},{6,2},{7,3},{8,12},{9,13},{10,... | collective-permute-start | bytes 960008 | tf_op jit(solution)/shard_map/ppermute | solution.py:299
  100.7 26.5 %collective-permute-start.23 = (bf16[2,625,128]{2,1,0:T(8,128)(2,1)}, bf16[2,625,128]{2,1,0:T(8,128)(2,1)S(1)}, u32[]{:S(2)}, u32[]{:S(2)}) collective-permute-start(bf16[2,625,128]{2,1,0:T(8,128)(2,1)} %bitcast.29), channel_id=1, source_target_pairs={{0,6},{1,7},{2,0},{3,1},{4,2},{5,3},{6,4},{7,5},{8,14},{9,15},{10,... | collective-permute-start | bytes 960008 | tf_op jit(solution)/shard_map/ppermute | solution.py:299
  113.9 13.4 %copy-start.7 = (f32[2,128,625]{1,0,2:T(2,128)S(1)}, f32[2,128,625]{1,0,2:T(2,128)}, u32[]{:S(2)}) copy-start(f32[2,128,625]{1,0,2:T(2,128)} %param.9) | copy-start | bytes 1920004
  113.9 13.3 %collective-permute-start.25 = (bf16[2,625,128]{2,1,0:T(8,128)(2,1)}, bf16[2,625,128]{2,1,0:T(8,128)(2,1)S(1)}, u32[]{:S(2)}, u32[]{:S(2)}) collective-permute-start(bf16[2,625,128]{2,1,0:T(8,128)(2,1)} %bitcast.30), channel_id=1, source_target_pairs={{0,2},{1,3},{2,4},{3,5},{4,6},{5,7},{6,0},{7,1},{8,10},{9,11},{10,... | collective-permute-start | bytes 960008 | tf_op jit(solution)/shard_map/ppermute | solution.py:299

commit v20 on v19

--- a/solution.py
+++ b/solution.py
@@ -22,7 +22,7 @@
 BF = jnp.bfloat16
 F32 = jnp.float32
 VMEM_BYTES = 48 * 1024 * 1024
-LADDER_VMEM_BYTES = 54 * 1024 * 1024
+LADDER_VMEM_BYTES = 48 * 1024 * 1024
 
 
 def spread(spots, rows):

time: 130 us -> 119 us (0.915)
  Pallas kernels: 62 us -> 50.7 us
  waiting for transfers between devices: 31.3 us -> 33.3 us
    pallas_call x4, Pallas kernels: 48.3 us -> 37.1 us  [ladders(): pl.pallas_call(functools.partial(ladder_kernel, find, made, len(tiles)),...]
    unnamed x25 -> x23, local copies, waits for them, and re-layouts: 8.77 us -> 8.07 us
  transfers between devices with their start and end apart: 26 -> 26, of which waited for: 12 -> 13; matrix products, arithmetic and copies ran while one was open for 4% -> 3% of each run, Pallas kernels for 38% -> 35%
where the time goes in v20:
time: 119 us
  Pallas kernels  50.7 us (43%)
  waiting for transfers between devices  33.3 us (28%)
  starting transfers between devices  24.8 us (21%)
  local copies, waits for them, and re-layouts  9.38 us (8%)
    pallas_call x4, Pallas kernels, ladders(): pl.pallas_call(functools.partial(ladder_kernel, find, made, len(tiles)),...  37.1 us
    ppermute x8, waiting for transfers between devices, per_device(): second_side = lambda x: lax.ppermute(x, ('pair', 'task'), sides[1])  17.6 us
    pallas_call x4, Pallas kernels, prepare(): pl.pallas_call(prepare_kernel, out_shape=jax.ShapeDtypeStruct((count, mat...  12.2 us
    ppermute x9, waiting for transfers between devices, around(): lax.ppermute(x, 'task', [(c, (c + 2 * by) % task_count) for c in range(ta...  10.8 us
    ppermute x9, starting transfers between devices, around(): lax.ppermute(x, 'task', [(c, (c + 2 * by) % task_count) for c in range(ta...  10.3 us
    ppermute x8, starting transfers between devices, per_device(): second_side = lambda x: lax.ppermute(x, ('pair', 'task'), sides[1])  9.13 us
    unnamed x23, local copies, waits for them, and re-layouts  8.07 us
    ppermute x5, waiting for transfers between devices, per_device(): lax.ppermute(x, 'task', [(c, c ^ 1) for c in range(task_count)])  4.82 us
  transfers between devices with their start and end apart: 26, of which 13 were waited for; matrix products, arithmetic and copies ran while one was open for 3% of the time, Pallas kernels for 35%

profile of v20, /device:TPU:0, one launch (start us, length us, event | category | flops | bytes accessed | tf_op | source)
XLA Modules:
  0.0 118.6 jit_solution(9674756564587705122)
XLA Ops:
  0.0 1.2 %pad = bf16[632,2,128]{2,1,0:T(2,128)(2,1)S(1)} pad(bf16[625,2,128]{2,1,0:T(2,128)(2,1)} %bitcast.31, bf16[]{:T(256)} %constant.64), padding=0_7x0_0x0_0 | pad | bytes 643586
  1.3 3.1 %collective-permute-start.3 = (bf16[625,256]{1,0:T(8,128)(2,1)S(1)}, bf16[625,256]{1,0:T(8,128)(2,1)S(1)}, u32[]{:S(2)}, u32[]{:S(2)}) collective-permute-start(bf16[625,256]{1,0:T(8,128)(2,1)S(1)} %bitcast.24), channel_id=1, source_target_pairs={{0,2},{1,3},{2,4},{3,5},{4,6},{5,7},{6,0},{7,1},{8,10},{9,11},{10,... | collective-permute-start | bytes 960008 | tf_op jit(solution)/shard_map/ppermute | solution.py:299
  4.4 3.3 %copy.22 = bf16[2,384,625]{2,1,0:T(8,128)(2,1)S(1)} copy(bf16[2,384,625]{1,0,2:T(2,128)(2,1)} %param.7) | data formatting | bytes 1920000 | tf_op args[0]
  7.7 0.1 dynamic-slice_bitcast_fusion
  7.9 1.6 %collective-permute-start.2 = (bf16[2,96,625]{2,1,0:T(8,128)(2,1)S(1)}, bf16[2,96,625]{2,1,0:T(8,128)(2,1)S(1)}, u32[]{:S(2)}, u32[]{:S(2)}) collective-permute-start(bf16[2,96,625]{2,1,0:T(8,128)(2,1)S(1)} %get-tuple-element.63), channel_id=1, source_target_pairs={{0,2},{1,3},{2,4},{3,5},{4,6},{5,7},{6,0},{7,1},{8,10},{9,11},{10,... | collective-permute-start | bytes 720008 | tf_op jit(solution)/shard_map/ppermute | solution.py:299
  9.5 1.5 %collective-permute-start.1 = (bf16[2,96,625]{2,1,0:T(8,128)(2,1)S(1)}, bf16[2,96,625]{2,1,0:T(8,128)(2,1)S(1)}, u32[]{:S(2)}, u32[]{:S(2)}) collective-permute-start(bf16[2,96,625]{2,1,0:T(8,128)(2,1)S(1)} %get-tuple-element.33.refs_0_), channel_id=1, source_target_pairs={{0,16},{1,9},{2,18},{3,11},{4,20},{5,13},{6,22},{7,15},{8,24},{9,1... | collective-permute-start | bytes 720008 | tf_op jit(solution)/shard_map/ppermute | solution.py:310
  11.0 1.5 %collective-permute-start = (bf16[2,96,625]{2,1,0:T(8,128)(2,1)S(1)}, bf16[2,96,625]{2,1,0:T(8,128)(2,1)S(1)}, u32[]{:S(2)}, u32[]{:S(2)}) collective-permute-start(bf16[2,96,625]{2,1,0:T(8,128)(2,1)S(1)} %get-tuple-element.33.refs_0_), channel_id=1, source_target_pairs={{0,8},{1,17},{2,10},{3,19},{4,12},{5,21},{6,14},{7,23},{8,0},{9,25... | collective-permute-start | bytes 720008 | tf_op jit(solution)/shard_map/ppermute | solution.py:309
  12.5 6.8 %collective-permute-done.2.refs_0_ = bf16[2,96,625]{2,1,0:T(8,128)(2,1)S(1)} collective-permute-done((bf16[2,96,625]{2,1,0:T(8,128)(2,1)S(1)}, bf16[2,96,625]{2,1,0:T(8,128)(2,1)S(1)}, u32[]{:S(2)}, u32[]{:S(2)}) %collective-permute-start.2) | collective-permute-done | bytes 240032 | tf_op jit(solution)/shard_map/ppermute | solution.py:299
  19.3 0.0 collective-permute-done.1.refs_2_
  19.3 0.0 collective-permute-done.refs_1_
  19.3 0.0 collective-permute-done.3.refs_1_
  19.3 1.6 %collective-permute-start.4 = (bf16[2,96,625]{2,1,0:T(8,128)(2,1)S(1)}, bf16[2,96,625]{2,1,0:T(8,128)(2,1)S(1)}, u32[]{:S(2)}, u32[]{:S(2)}) collective-permute-start(bf16[2,96,625]{2,1,0:T(8,128)(2,1)S(1)} %collective-permute-done.refs_1_), channel_id=1, source_target_pairs={{0,16},{1,9},{2,18},{3,11},{4,20},{5,13},{6,22},{7,15},{8,24},{9,1... | collective-permute-start | bytes 720008 | tf_op jit(solution)/shard_map/ppermute | solution.py:310
  20.9 0.7 collective-permute-start.7
  21.6 0.5 collective-permute-start.6
  22.1 1.5 %collective-permute-start.5 = (bf16[2,96,625]{2,1,0:T(8,128)(2,1)S(1)}, bf16[2,96,625]{2,1,0:T(8,128)(2,1)S(1)}, u32[]{:S(2)}, u32[]{:S(2)}) collective-permute-start(bf16[2,96,625]{2,1,0:T(8,128)(2,1)S(1)} %collective-permute-done.2.refs_0_), channel_id=1, source_target_pairs={{0,8},{1,17},{2,10},{3,19},{4,12},{5,21},{6,14},{7,23},{8,0},{9,25... | collective-permute-start | bytes 720008 | tf_op jit(solution)/shard_map/ppermute | solution.py:309
  23.6 4.6 %collective-permute-done.4.refs_3_ = bf16[2,96,625]{2,1,0:T(8,128)(2,1)S(1)} collective-permute-done((bf16[2,96,625]{2,1,0:T(8,128)(2,1)S(1)}, bf16[2,96,625]{2,1,0:T(8,128)(2,1)S(1)}, u32[]{:S(2)}, u32[]{:S(2)}) %collective-permute-start.4) | collective-permute-done | bytes 240032 | tf_op jit(solution)/shard_map/ppermute | solution.py:310
  28.2 1.6 %copy-done.4 = bf16[1600,625]{1,0:T(8,128)(2,1)S(1)} copy-done((bf16[1600,625]{1,0:T(8,128)(2,1)S(1)}, bf16[1600,625]{1,0:T(8,128)(2,1)}, u32[]{:S(2)}) %copy-start.4) | copy-done | bytes 2000024
  29.7 2.6 %shard_map.73.refs_0_ = bf16[2,1600,384]{2,1,0:T(8,128)(2,1)S(1)} custom-call(s32[1]{0:T(128)} %bitcast.column_ref, bf16[2,96,625]{2,1,0:T(8,128)(2,1)S(1)} %get-tuple-element.33.refs_0_, bf16[2,96,625]{2,1,0:T(8,128)(2,1)S(1)} %collective-permute-done.refs_1_, bf16[2,96,625]{2,1,0:T(8,128)(2,1)S(1)} %collective-permute-done.1.refs_2_, ...), custom_call_target="tpu_custom_call" | custom-call | flops 1536000000 | bytes 3417600 | tf_op jit(solution)/shard_map/pallas_call | solution.py:73
  32.4 0.3 collective-permute-done.7.refs_0_
  32.7 0.0 collective-permute-done.6.refs_2_
  32.7 0.0 collective-permute-done.5.refs_1_
  32.7 0.0 collective-permute-start.12
  32.7 1.6 %collective-permute-start.8 = (bf16[2,96,625]{2,1,0:T(8,128)(2,1)S(1)}, bf16[2,96,625]{2,1,0:T(8,128)(2,1)S(1)}, u32[]{:S(2)}, u32[]{:S(2)}) collective-permute-start(bf16[2,96,625]{2,1,0:T(8,128)(2,1)S(1)} %collective-permute-done.5.refs_1_), channel_id=1, source_target_pairs={{0,16},{1,9},{2,18},{3,11},{4,20},{5,13},{6,22},{7,15},{8,24},{9,1... | collective-permute-start | bytes 720008 | tf_op jit(solution)/shard_map/ppermute | solution.py:310
  34.3 2.5 %collective-permute-start.11 = (bf16[2,96,625]{2,1,0:T(8,128)(2,1)S(1)}, bf16[2,96,625]{2,1,0:T(8,128)(2,1)S(1)}, u32[]{:S(2)}, u32[]{:S(2)}) collective-permute-start(bf16[2,96,625]{2,1,0:T(8,128)(2,1)S(1)} %get-tuple-element.43), channel_id=1, source_target_pairs={{0,6},{1,7},{2,0},{3,1},{4,2},{5,3},{6,4},{7,5},{8,14},{9,15},{10,... | collective-permute-start | bytes 720008 | tf_op jit(solution)/shard_map/ppermute | solution.py:299
  36.8 0.5 collective-permute-start.10
  37.3 0.6 collective-permute-start.9
  37.9 1.0 collective-permute-done.8.refs_3_
  39.0 2.6 %shard_map.74.refs_2_ = bf16[2,1600,384]{2,1,0:T(8,128)(2,1)S(1)} custom-call(s32[1]{0:T(128)} %bitcast.column_ref, bf16[2,96,625]{2,1,0:T(8,128)(2,1)S(1)} %collective-permute-done.2.refs_0_, bf16[2,96,625]{2,1,0:T(8,128)(2,1)S(1)} %collective-permute-done.5.refs_1_, bf16[2,96,625]{2,1,0:T(8,128)(2,1)S(1)} %collective-permute-done.6.refs_2_, ...), custom_call_target="tpu_custom_call" | custom-call | flops 1536000000 | bytes 3417600 | tf_op jit(solution)/shard_map/pallas_call | solution.py:73
  41.7 0.8 collective-permute-done.11.refs_0_
  42.4 2.3 %collective-permute-done.10.refs_2_ = bf16[2,96,625]{2,1,0:T(8,128)(2,1)S(1)} collective-permute-done((bf16[2,96,625]{2,1,0:T(8,128)(2,1)S(1)}, bf16[2,96,625]{2,1,0:T(8,128)(2,1)S(1)}, u32[]{:S(2)}, u32[]{:S(2)}) %collective-permute-start.10) | collective-permute-done | bytes 240032 | tf_op jit(solution)/shard_map/ppermute | solution.py:310
  44.7 0.0 collective-permute-done.9.refs_1_
  44.7 0.0 collective-permute-done.12.refs_1_
  44.8 0.0 collective-permute-start.17
  44.8 1.3 %collective-permute-start.13 = (bf16[2,96,625]{2,1,0:T(8,128)(2,1)S(1)}, bf16[2,96,625]{2,1,0:T(8,128)(2,1)S(1)}, u32[]{:S(2)}, u32[]{:S(2)}) collective-permute-start(bf16[2,96,625]{2,1,0:T(8,128)(2,1)S(1)} %collective-permute-done.9.refs_1_), channel_id=1, source_target_pairs={{0,16},{1,9},{2,18},{3,11},{4,20},{5,13},{6,22},{7,15},{8,24},{9,1... | collective-permute-start | bytes 720008 | tf_op jit(solution)/shard_map/ppermute | solution.py:310
  46.1 0.8 collective-permute-start.15
  46.9 1.2 collective-permute-start.14
  48.0 4.7 %collective-permute-done.13.refs_3_ = bf16[2,96,625]{2,1,0:T(8,128)(2,1)S(1)} collective-permute-done((bf16[2,96,625]{2,1,0:T(8,128)(2,1)S(1)}, bf16[2,96,625]{2,1,0:T(8,128)(2,1)S(1)}, u32[]{:S(2)}, u32[]{:S(2)}) %collective-permute-start.13) | collective-permute-done | bytes 240032 | tf_op jit(solution)/shard_map/ppermute | solution.py:310
  52.7 3.4 %shard_map.75.refs_4_ = bf16[2,1600,384]{2,1,0:T(8,128)(2,1)} custom-call(s32[1]{0:T(128)} %bitcast.column_ref, bf16[2,96,625]{2,1,0:T(8,128)(2,1)S(1)} %collective-permute-done.7.refs_0_, bf16[2,96,625]{2,1,0:T(8,128)(2,1)S(1)} %collective-permute-done.9.refs_1_, bf16[2,96,625]{2,1,0:T(8,128)(2,1)S(1)} %collective-permute-done.10.refs_2_, ...), custom_call_target="tpu_custom_call" | custom-call | flops 1536000000 | bytes 3417600 | tf_op jit(solution)/shard_map/pallas_call | solution.py:73
  56.2 0.1 collective-permute-done.15.refs_2_
  56.3 1.2 collective-permute-done.16.refs_2_
  57.4 0.0 collective-permute-done.17.refs_3_
  57.5 1.3 %collective-permute-start.18 = (bf16[2,96,625]{2,1,0:T(8,128)(2,1)S(1)}, bf16[2,96,625]{2,1,0:T(8,128)(2,1)S(1)}, u32[]{:S(2)}, u32[]{:S(2)}) collective-permute-start(bf16[2,96,625]{2,1,0:T(8,128)(2,1)S(1)} %collective-permute-done.14.refs_1_), channel_id=1, source_target_pairs={{0,16},{1,9},{2,18},{3,11},{4,20},{5,13},{6,22},{7,15},{8,24},{9,1... | collective-permute-start | bytes 720008 | tf_op jit(solution)/shard_map/ppermute | solution.py:310
  58.8 4.9 %collective-permute-done.18.refs_3_ = bf16[2,96,625]{2,1,0:T(8,128)(2,1)S(1)} collective-permute-done((bf16[2,96,625]{2,1,0:T(8,128)(2,1)S(1)}, bf16[2,96,625]{2,1,0:T(8,128)(2,1)S(1)}, u32[]{:S(2)}, u32[]{:S(2)}) %collective-permute-start.18) | collective-permute-done | bytes 240032 | tf_op jit(solution)/shard_map/ppermute | solution.py:310
  63.7 3.5 %shard_map.76.refs_6_ = bf16[2,1600,384]{2,1,0:T(8,128)(2,1)} custom-call(s32[1]{0:T(128)} %bitcast.column_ref, bf16[2,96,625]{2,1,0:T(8,128)(2,1)S(1)} %collective-permute-done.11.refs_0_, bf16[2,96,625]{2,1,0:T(8,128)(2,1)S(1)} %collective-permute-done.14.refs_1_, bf16[2,96,625]{2,1,0:T(8,128)(2,1)S(1)} %collective-permute-done.15.refs_2_, ...), custom_call_target="tpu_custom_call" | custom-call | flops 1536000000 | bytes 3417600 | tf_op jit(solution)/shard_map/pallas_call | solution.py:73
  67.1 1.1 collective-permute-done.20.refs_3_
  68.2 1.4 %shard_map.77.refs_8_ = bf16[8,800,128]{2,1,0:T(8,128)(2,1)S(1)} custom-call(bf16[800,625]{1,0:T(8,128)(2,1)S(1)} %copy-done.3, bf16[625,256]{1,0:T(8,128)(2,1)S(1)} %bitcast.25, bf16[625,256]{1,0:T(8,128)(2,1)S(1)} %collective-permute-done.3.refs_1_, bf16[625,256]{1,0:T(8,128)(2,1)S(1)} %collective-permute-done.16.refs_2_, ...), custom_call_target="tpu_custom_call" | custom-call | flops 1024000000 | bytes 2560000 | tf_op jit(solution)/shard_map/pallas_call | solution.py:104
  69.7 0.6 collective-permute-start.22
  70.2 0.1 copy.23.owners_ref
  70.3 0.1 copy.24.local_ref
  70.4 4.8 %collective-permute-done.22.refs_9_ = bf16[8,800,128]{2,1,0:T(8,128)(2,1)S(1)} collective-permute-done((bf16[8,800,128]{2,1,0:T(8,128)(2,1)S(1)}, bf16[8,800,128]{2,1,0:T(8,128)(2,1)S(1)}, u32[]{:S(2)}, u32[]{:S(2)}) %collective-permute-start.22) | collective-permute-done | bytes 1638432 | tf_op jit(solution)/shard_map/ppermute | solution.py:296
  75.2 0.0 collective-permute-done.21.refs_7_
  75.2 1.7 %copy-done.1 = bf16[2,1600,384]{2,1,0:T(8,128)(2,1)S(1)} copy-done((bf16[2,1600,384]{2,1,0:T(8,128)(2,1)S(1)}, bf16[2,1600,384]{2,1,0:T(8,128)(2,1)}, u32[]{:S(2)}) %copy-start.1) | copy-done | bytes 2457624
  76.9 9.1 %shard_map.79 = bf16[1,2,625,128]{3,2,1,0:T(8,128)(2,1)S(1)} custom-call(s32[1]{0:T(128)} %bitcast.column_ref, s32[32,3]{1,0:T(8,128)S(1)} %copy.23.owners_ref, s32[32,4]{1,0:T(8,128)S(1)} %copy.24.local_ref, bf16[2,1600,384]{2,1,0:T(8,128)(2,1)S(1)} %copy-done.1, bf16[2,1600,384]{2,1,0:T(8,128)(2,1)} %collective-permute-done.12.refs_1_, ...), custom_call_target="tpu_custom_call" | custom-call | flops 2936012800 | bytes 6553600 | tf_op jit(solution)/shard_map/pallas_call | solution.py:262
  86.0 0.1 collective-permute-start.24
  86.1 9.3 %shard_map.78 = bf16[1,2,625,128]{3,2,1,0:T(8,128)(2,1)S(1)} custom-call(s32[1]{0:T(128)} %bitcast.column_ref, s32[32,3]{1,0:T(8,128)S(1)} %copy.23.owners_ref, s32[32,4]{1,0:T(8,128)S(1)} %copy.24.local_ref, bf16[2,1600,384]{2,1,0:T(8,128)(2,1)S(1)} %copy-done.1, bf16[2,1600,384]{2,1,0:T(8,128)(2,1)} %collective-permute-done.12.refs_1_, ...), custom_call_target="tpu_custom_call" | custom-call | flops 2936012800 | bytes 6553600 | tf_op jit(solution)/shard_map/pallas_call | solution.py:262
  95.4 1.3 %collective-permute-start.23 = (bf16[2,625,128]{2,1,0:T(8,128)(2,1)S(1)}, bf16[2,625,128]{2,1,0:T(8,128)(2,1)S(1)}, u32[]{:S(2)}, u32[]{:S(2)}) collective-permute-start(bf16[2,625,128]{2,1,0:T(8,128)(2,1)S(1)} %bitcast.27), channel_id=1, source_target_pairs={{0,6},{1,7},{2,0},{3,1},{4,2},{5,3},{6,4},{7,5},{8,14},{9,15},{10,... | collective-permute-start | bytes 960008 | tf_op jit(solution)/shard_map/ppermute | solution.py:299
  96.7 9.4 %shard_map.80 = bf16[1,2,625,128]{3,2,1,0:T(8,128)(2,1)S(1)} custom-call(s32[1]{0:T(128)} %bitcast.column_ref, s32[32,3]{1,0:T(8,128)S(1)} %copy.23.owners_ref, s32[32,4]{1,0:T(8,128)S(1)} %copy.24.local_ref, bf16[2,1600,384]{2,1,0:T(8,128)(2,1)S(1)} %copy-done.1, bf16[2,1600,384]{2,1,0:T(8,128)(2,1)} %collective-permute-done.12.refs_1_, ...), custom_call_target="tpu_custom_call" | custom-call | flops 2936012800 | bytes 6553600 | tf_op jit(solution)/shard_map/pallas_call | solution.py:262
  106.1 0.0 copy-start.6
  106.1 1.1 collective-permute-start.25
  107.2 9.3 %shard_map.81 = bf16[1,2,625,128]{3,2,1,0:T(8,128)(2,1)S(1)} custom-call(s32[1]{0:T(128)} %bitcast.column_ref, s32[32,3]{1,0:T(8,128)S(1)} %copy.23.owners_ref, s32[32,4]{1,0:T(8,128)S(1)} %copy.24.local_ref, bf16[2,1600,384]{2,1,0:T(8,128)(2,1)S(1)} %copy-done.1, bf16[2,1600,384]{2,1,0:T(8,128)(2,1)} %collective-permute-done.12.refs_1_, ...), custom_call_target="tpu_custom_call" | custom-call | flops 2936012800 | bytes 6553600 | tf_op jit(solution)/shard_map/pallas_call | solution.py:262
  116.5 0.0 collective-permute-done.24
  116.5 0.7 collective-permute-done.25
  117.2 0.2 fusion.1
  117.4 1.2 copy.32
  (23 shorter events, 0.1 us)
Async XLA Ops:
  1.3 18.0 %collective-permute-start.3 = (bf16[625,256]{1,0:T(8,128)(2,1)S(1)}, bf16[625,256]{1,0:T(8,128)(2,1)S(1)}, u32[]{:S(2)}, u32[]{:S(2)}) collective-permute-start(bf16[625,256]{1,0:T(8,128)(2,1)S(1)} %bitcast.24), channel_id=1, source_target_pairs={{0,2},{1,3},{2,4},{3,5},{4,6},{5,7},{6,0},{7,1},{8,10},{9,11},{10,... | collective-permute-start | bytes 960008 | tf_op jit(solution)/shard_map/ppermute | solution.py:299
  7.9 11.4 %collective-permute-start.2 = (bf16[2,96,625]{2,1,0:T(8,128)(2,1)S(1)}, bf16[2,96,625]{2,1,0:T(8,128)(2,1)S(1)}, u32[]{:S(2)}, u32[]{:S(2)}) collective-permute-start(bf16[2,96,625]{2,1,0:T(8,128)(2,1)S(1)} %get-tuple-element.63), channel_id=1, source_target_pairs={{0,2},{1,3},{2,4},{3,5},{4,6},{5,7},{6,0},{7,1},{8,10},{9,11},{10,... | collective-permute-start | bytes 720008 | tf_op jit(solution)/shard_map/ppermute | solution.py:299
  9.5 9.8 %collective-permute-start.1 = (bf16[2,96,625]{2,1,0:T(8,128)(2,1)S(1)}, bf16[2,96,625]{2,1,0:T(8,128)(2,1)S(1)}, u32[]{:S(2)}, u32[]{:S(2)}) collective-permute-start(bf16[2,96,625]{2,1,0:T(8,128)(2,1)S(1)} %get-tuple-element.33.refs_0_), channel_id=1, source_target_pairs={{0,16},{1,9},{2,18},{3,11},{4,20},{5,13},{6,22},{7,15},{8,24},{9,1... | collective-permute-start | bytes 720008 | tf_op jit(solution)/shard_map/ppermute | solution.py:310
  11.0 8.3 %collective-permute-start = (bf16[2,96,625]{2,1,0:T(8,128)(2,1)S(1)}, bf16[2,96,625]{2,1,0:T(8,128)(2,1)S(1)}, u32[]{:S(2)}, u32[]{:S(2)}) collective-permute-start(bf16[2,96,625]{2,1,0:T(8,128)(2,1)S(1)} %get-tuple-element.33.refs_0_), channel_id=1, source_target_pairs={{0,8},{1,17},{2,10},{3,19},{4,12},{5,21},{6,14},{7,23},{8,0},{9,25... | collective-permute-start | bytes 720008 | tf_op jit(solution)/shard_map/ppermute | solution.py:309
  19.3 8.9 %collective-permute-start.4 = (bf16[2,96,625]{2,1,0:T(8,128)(2,1)S(1)}, bf16[2,96,625]{2,1,0:T(8,128)(2,1)S(1)}, u32[]{:S(2)}, u32[]{:S(2)}) collective-permute-start(bf16[2,96,625]{2,1,0:T(8,128)(2,1)S(1)} %collective-permute-done.refs_1_), channel_id=1, source_target_pairs={{0,16},{1,9},{2,18},{3,11},{4,20},{5,13},{6,22},{7,15},{8,24},{9,1... | collective-permute-start | bytes 720008 | tf_op jit(solution)/shard_map/ppermute | solution.py:310
  20.9 11.8 %collective-permute-start.7 = (bf16[2,96,625]{2,1,0:T(8,128)(2,1)S(1)}, bf16[2,96,625]{2,1,0:T(8,128)(2,1)S(1)}, u32[]{:S(2)}, u32[]{:S(2)}) collective-permute-start(bf16[2,96,625]{2,1,0:T(8,128)(2,1)S(1)} %get-tuple-element.37), channel_id=1, source_target_pairs={{0,4},{1,5},{2,6},{3,7},{4,0},{5,1},{6,2},{7,3},{8,12},{9,13},{10,... | collective-permute-start | bytes 720008 | tf_op jit(solution)/shard_map/ppermute | solution.py:299
  21.6 11.1 %collective-permute-start.6 = (bf16[2,96,625]{2,1,0:T(8,128)(2,1)S(1)}, bf16[2,96,625]{2,1,0:T(8,128)(2,1)S(1)}, u32[]{:S(2)}, u32[]{:S(2)}) collective-permute-start(bf16[2,96,625]{2,1,0:T(8,128)(2,1)S(1)} %collective-permute-done.2.refs_0_), channel_id=1, source_target_pairs={{0,16},{1,9},{2,18},{3,11},{4,20},{5,13},{6,22},{7,15},{8,24},{9,1... | collective-permute-start | bytes 720008 | tf_op jit(solution)/shard_map/ppermute | solution.py:310
  22.1 10.6 %collective-permute-start.5 = (bf16[2,96,625]{2,1,0:T(8,128)(2,1)S(1)}, bf16[2,96,625]{2,1,0:T(8,128)(2,1)S(1)}, u32[]{:S(2)}, u32[]{:S(2)}) collective-permute-start(bf16[2,96,625]{2,1,0:T(8,128)(2,1)S(1)} %collective-permute-done.2.refs_0_), channel_id=1, source_target_pairs={{0,8},{1,17},{2,10},{3,19},{4,12},{5,21},{6,14},{7,23},{8,0},{9,25... | collective-permute-start | bytes 720008 | tf_op jit(solution)/shard_map/ppermute | solution.py:309
  28.2 1.6 %copy-start.4 = (bf16[1600,625]{1,0:T(8,128)(2,1)S(1)}, bf16[1600,625]{1,0:T(8,128)(2,1)}, u32[]{:S(2)}) copy-start(bf16[1600,625]{1,0:T(8,128)(2,1)} %constant.59.clone.refs_4_) | copy-start | bytes 6000004
  29.7 9.3 %copy-start.5 = (bf16[1600,625]{1,0:T(8,128)(2,1)S(1)}, bf16[1600,625]{1,0:T(8,128)(2,1)}, u32[]{:S(2)}) copy-start(bf16[1600,625]{1,0:T(8,128)(2,1)} %constant.59.clone.refs_4_) | copy-start | bytes 6000004
  32.4 9.3 %copy-start = (bf16[2,1600,384]{2,1,0:T(8,128)(2,1)}, bf16[2,1600,384]{2,1,0:T(8,128)(2,1)S(1)}, u32[]{:S(2)}) copy-start(bf16[2,1600,384]{2,1,0:T(8,128)(2,1)S(1)} %shard_map.73.refs_0_) | copy-start | bytes 7372804
  32.7 12.0 %collective-permute-start.12 = (bf16[2,1600,384]{2,1,0:T(8,128)(2,1)S(1)}, bf16[2,1600,384]{2,1,0:T(8,128)(2,1)}, u32[]{:S(2)}, u32[]{:S(2)}) collective-permute-start(bf16[2,1600,384]{2,1,0:T(8,128)(2,1)S(1)} %shard_map.73.refs_0_), channel_id=1, source_target_pairs={{0,1},{1,0},{2,3},{3,2},{4,5},{5,4},{6,7},{7,6},{8,9},{9,8},{10,11... | collective-permute-start | bytes 7372808 | tf_op jit(solution)/shard_map/ppermute | solution.py:296
  32.7 6.3 %collective-permute-start.8 = (bf16[2,96,625]{2,1,0:T(8,128)(2,1)S(1)}, bf16[2,96,625]{2,1,0:T(8,128)(2,1)S(1)}, u32[]{:S(2)}, u32[]{:S(2)}) collective-permute-start(bf16[2,96,625]{2,1,0:T(8,128)(2,1)S(1)} %collective-permute-done.5.refs_1_), channel_id=1, source_target_pairs={{0,16},{1,9},{2,18},{3,11},{4,20},{5,13},{6,22},{7,15},{8,24},{9,1... | collective-permute-start | bytes 720008 | tf_op jit(solution)/shard_map/ppermute | solution.py:310
  34.3 8.1 %collective-permute-start.11 = (bf16[2,96,625]{2,1,0:T(8,128)(2,1)S(1)}, bf16[2,96,625]{2,1,0:T(8,128)(2,1)S(1)}, u32[]{:S(2)}, u32[]{:S(2)}) collective-permute-start(bf16[2,96,625]{2,1,0:T(8,128)(2,1)S(1)} %get-tuple-element.43), channel_id=1, source_target_pairs={{0,6},{1,7},{2,0},{3,1},{4,2},{5,3},{6,4},{7,5},{8,14},{9,15},{10,... | collective-permute-start | bytes 720008 | tf_op jit(solution)/shard_map/ppermute | solution.py:299
  36.8 8.0 %collective-permute-start.10 = (bf16[2,96,625]{2,1,0:T(8,128)(2,1)S(1)}, bf16[2,96,625]{2,1,0:T(8,128)(2,1)S(1)}, u32[]{:S(2)}, u32[]{:S(2)}) collective-permute-start(bf16[2,96,625]{2,1,0:T(8,128)(2,1)S(1)} %collective-permute-done.7.refs_0_), channel_id=1, source_target_pairs={{0,16},{1,9},{2,18},{3,11},{4,20},{5,13},{6,22},{7,15},{8,24},{9,1... | collective-permute-start | bytes 720008 | tf_op jit(solution)/shard_map/ppermute | solution.py:310
  37.3 7.5 %collective-permute-start.9 = (bf16[2,96,625]{2,1,0:T(8,128)(2,1)S(1)}, bf16[2,96,625]{2,1,0:T(8,128)(2,1)S(1)}, u32[]{:S(2)}, u32[]{:S(2)}) collective-permute-start(bf16[2,96,625]{2,1,0:T(8,128)(2,1)S(1)} %collective-permute-done.7.refs_0_), channel_id=1, source_target_pairs={{0,8},{1,17},{2,10},{3,19},{4,12},{5,21},{6,14},{7,23},{8,0},{9,25... | collective-permute-start | bytes 720008 | tf_op jit(solution)/shard_map/ppermute | solution.py:309
  41.6 14.5 %copy-start.2 = (bf16[2,1600,384]{2,1,0:T(8,128)(2,1)}, bf16[2,1600,384]{2,1,0:T(8,128)(2,1)S(1)}, u32[]{:S(2)}) copy-start(bf16[2,1600,384]{2,1,0:T(8,128)(2,1)S(1)} %shard_map.74.refs_2_) | copy-start | bytes 7372804
  44.8 12.7 %collective-permute-start.17 = (bf16[2,1600,384]{2,1,0:T(8,128)(2,1)S(1)}, bf16[2,1600,384]{2,1,0:T(8,128)(2,1)}, u32[]{:S(2)}, u32[]{:S(2)}) collective-permute-start(bf16[2,1600,384]{2,1,0:T(8,128)(2,1)S(1)} %shard_map.74.refs_2_), channel_id=1, source_target_pairs={{0,1},{1,0},{2,3},{3,2},{4,5},{5,4},{6,7},{7,6},{8,9},{9,8},{10,11... | collective-permute-start | bytes 7372808 | tf_op jit(solution)/shard_map/ppermute | solution.py:296
  44.8 8.0 %collective-permute-start.13 = (bf16[2,96,625]{2,1,0:T(8,128)(2,1)S(1)}, bf16[2,96,625]{2,1,0:T(8,128)(2,1)S(1)}, u32[]{:S(2)}, u32[]{:S(2)}) collective-permute-start(bf16[2,96,625]{2,1,0:T(8,128)(2,1)S(1)} %collective-permute-done.9.refs_1_), channel_id=1, source_target_pairs={{0,16},{1,9},{2,18},{3,11},{4,20},{5,13},{6,22},{7,15},{8,24},{9,1... | collective-permute-start | bytes 720008 | tf_op jit(solution)/shard_map/ppermute | solution.py:310
  46.1 11.4 %collective-permute-start.16 = (bf16[625,256]{1,0:T(8,128)(2,1)S(1)}, bf16[625,256]{1,0:T(8,128)(2,1)S(1)}, u32[]{:S(2)}, u32[]{:S(2)}) collective-permute-start(bf16[625,256]{1,0:T(8,128)(2,1)S(1)} %collective-permute-done.3.refs_1_), channel_id=1, source_target_pairs={{0,2},{1,3},{2,4},{3,5},{4,6},{5,7},{6,0},{7,1},{8,10},{9,11},{10,... | collective-permute-start | bytes 960008 | tf_op jit(solution)/shard_map/ppermute | solution.py:299
  46.1 10.2 %collective-permute-start.15 = (bf16[2,96,625]{2,1,0:T(8,128)(2,1)S(1)}, bf16[2,96,625]{2,1,0:T(8,128)(2,1)S(1)}, u32[]{:S(2)}, u32[]{:S(2)}) collective-permute-start(bf16[2,96,625]{2,1,0:T(8,128)(2,1)S(1)} %collective-permute-done.11.refs_0_), channel_id=1, source_target_pairs={{0,16},{1,9},{2,18},{3,11},{4,20},{5,13},{6,22},{7,15},{8,24},{9,1... | collective-permute-start | bytes 720008 | tf_op jit(solution)/shard_map/ppermute | solution.py:310
  46.9 9.4 %collective-permute-start.14 = (bf16[2,96,625]{2,1,0:T(8,128)(2,1)S(1)}, bf16[2,96,625]{2,1,0:T(8,128)(2,1)S(1)}, u32[]{:S(2)}, u32[]{:S(2)}) collective-permute-start(bf16[2,96,625]{2,1,0:T(8,128)(2,1)S(1)} %collective-permute-done.11.refs_0_), channel_id=1, source_target_pairs={{0,8},{1,17},{2,10},{3,19},{4,12},{5,21},{6,14},{7,23},{8,0},{9,25... | collective-permute-start | bytes 720008 | tf_op jit(solution)/shard_map/ppermute | solution.py:309
  56.2 12.0 %copy-start.3 = (bf16[800,625]{1,0:T(8,128)(2,1)S(1)}, bf16[800,625]{1,0:T(8,128)(2,1)}, u32[]{:S(2)}) copy-start(bf16[800,625]{1,0:T(8,128)(2,1)} %constant.60.clone.matrix_ref) | copy-start | bytes 3000004
  57.5 6.2 %collective-permute-start.18 = (bf16[2,96,625]{2,1,0:T(8,128)(2,1)S(1)}, bf16[2,96,625]{2,1,0:T(8,128)(2,1)S(1)}, u32[]{:S(2)}, u32[]{:S(2)}) collective-permute-start(bf16[2,96,625]{2,1,0:T(8,128)(2,1)S(1)} %collective-permute-done.14.refs_1_), channel_id=1, source_target_pairs={{0,16},{1,9},{2,18},{3,11},{4,20},{5,13},{6,22},{7,15},{8,24},{9,1... | collective-permute-start | bytes 720008 | tf_op jit(solution)/shard_map/ppermute | solution.py:310
  58.8 9.4 %collective-permute-start.20 = (bf16[625,256]{1,0:T(8,128)(2,1)S(1)}, bf16[625,256]{1,0:T(8,128)(2,1)S(1)}, u32[]{:S(2)}, u32[]{:S(2)}) collective-permute-start(bf16[625,256]{1,0:T(8,128)(2,1)S(1)} %collective-permute-done.16.refs_2_), channel_id=1, source_target_pairs={{0,2},{1,3},{2,4},{3,5},{4,6},{5,7},{6,0},{7,1},{8,10},{9,11},{10,... | collective-permute-start | bytes 960008 | tf_op jit(solution)/shard_map/ppermute | solution.py:299
  63.6 11.6 %collective-permute-start.19 = (bf16[2,1600,384]{2,1,0:T(8,128)(2,1)}, bf16[2,1600,384]{2,1,0:T(8,128)(2,1)}, u32[]{:S(2)}, u32[]{:S(2)}) collective-permute-start(bf16[2,1600,384]{2,1,0:T(8,128)(2,1)} %shard_map.75.refs_4_), channel_id=1, source_target_pairs={{0,1},{1,0},{2,3},{3,2},{4,5},{5,4},{6,7},{7,6},{8,9},{9,8},{10,11... | collective-permute-start | bytes 7372808 | tf_op jit(solution)/shard_map/ppermute | solution.py:296
  67.1 3.1 %copy-start.7 = (s32[32,3]{0,1:T(4,128)S(1)}, s32[32,3]{0,1:T(4,128)}, u32[]{:S(2)}) copy-start(s32[32,3]{0,1:T(4,128)} %param.10) | copy-start | bytes 1156
  67.1 3.2 %copy-start.8 = (s32[32,4]{0,1:T(4,128)S(1)}, s32[32,4]{0,1:T(4,128)}, u32[]{:S(2)}) copy-start(s32[32,4]{0,1:T(4,128)} %param.11) | copy-start | bytes 1540
  68.2 7.0 %collective-permute-start.21 = (bf16[2,1600,384]{2,1,0:T(8,128)(2,1)}, bf16[2,1600,384]{2,1,0:T(8,128)(2,1)}, u32[]{:S(2)}, u32[]{:S(2)}) collective-permute-start(bf16[2,1600,384]{2,1,0:T(8,128)(2,1)} %shard_map.76.refs_6_), channel_id=1, source_target_pairs={{0,1},{1,0},{2,3},{3,2},{4,5},{5,4},{6,7},{7,6},{8,9},{9,8},{10,11... | collective-permute-start | bytes 7372808 | tf_op jit(solution)/shard_map/ppermute | solution.py:296
  69.7 5.6 %collective-permute-start.22 = (bf16[8,800,128]{2,1,0:T(8,128)(2,1)S(1)}, bf16[8,800,128]{2,1,0:T(8,128)(2,1)S(1)}, u32[]{:S(2)}, u32[]{:S(2)}) collective-permute-start(bf16[8,800,128]{2,1,0:T(8,128)(2,1)S(1)} %shard_map.77.refs_8_), channel_id=1, source_target_pairs={{0,1},{1,0},{2,3},{3,2},{4,5},{5,4},{6,7},{7,6},{8,9},{9,8},{10,11... | collective-permute-start | bytes 4915208 | tf_op jit(solution)/shard_map/ppermute | solution.py:296
  75.2 1.7 %copy-start.1 = (bf16[2,1600,384]{2,1,0:T(8,128)(2,1)S(1)}, bf16[2,1600,384]{2,1,0:T(8,128)(2,1)}, u32[]{:S(2)}) copy-start(bf16[2,1600,384]{2,1,0:T(8,128)(2,1)} %copy-done) | copy-start | bytes 7372804
  86.0 30.4 %collective-permute-start.24 = (bf16[2,625,128]{2,1,0:T(8,128)(2,1)S(1)}, bf16[2,625,128]{2,1,0:T(8,128)(2,1)S(1)}, u32[]{:S(2)}, u32[]{:S(2)}) collective-permute-start(bf16[2,625,128]{2,1,0:T(8,128)(2,1)S(1)} %bitcast.26), channel_id=1, source_target_pairs={{0,4},{1,5},{2,6},{3,7},{4,0},{5,1},{6,2},{7,3},{8,12},{9,13},{10,... | collective-permute-start | bytes 960008 | tf_op jit(solution)/shard_map/ppermute | solution.py:299
  95.4 21.1 %collective-permute-start.23 = (bf16[2,625,128]{2,1,0:T(8,128)(2,1)S(1)}, bf16[2,625,128]{2,1,0:T(8,128)(2,1)S(1)}, u32[]{:S(2)}, u32[]{:S(2)}) collective-permute-start(bf16[2,625,128]{2,1,0:T(8,128)(2,1)S(1)} %bitcast.27), channel_id=1, source_target_pairs={{0,6},{1,7},{2,0},{3,1},{4,2},{5,3},{6,4},{7,5},{8,14},{9,15},{10,... | collective-permute-start | bytes 960008 | tf_op jit(solution)/shard_map/ppermute | solution.py:299
  106.1 11.1 %copy-start.6 = (f32[2,128,625]{1,0,2:T(2,128)S(1)}, f32[2,128,625]{1,0,2:T(2,128)}, u32[]{:S(2)}) copy-start(f32[2,128,625]{1,0,2:T(2,128)} %param.9) | copy-start | bytes 1920004
  106.1 11.1 %collective-permute-start.25 = (bf16[2,625,128]{2,1,0:T(8,128)(2,1)S(1)}, bf16[2,625,128]{2,1,0:T(8,128)(2,1)S(1)}, u32[]{:S(2)}, u32[]{:S(2)}) collective-permute-start(bf16[2,625,128]{2,1,0:T(8,128)(2,1)S(1)} %bitcast.28), channel_id=1, source_target_pairs={{0,2},{1,3},{2,4},{3,5},{4,6},{5,7},{6,0},{7,1},{8,10},{9,11},{10,... | collective-permute-start | bytes 960008 | tf_op jit(solution)/shard_map/ppermute | solution.py:299

commit v21 on v20

--- a/solution.py
+++ b/solution.py
@@ -22,7 +22,7 @@
 BF = jnp.bfloat16
 F32 = jnp.float32
 VMEM_BYTES = 48 * 1024 * 1024
-LADDER_VMEM_BYTES = 48 * 1024 * 1024
+LADDER_VMEM_BYTES = 52 * 1024 * 1024
 
 
 def spread(spots, rows):

time: 119 us -> 123 us (1.034)
  Pallas kernels: 50.7 us -> 56.4 us
    pallas_call x4, Pallas kernels: 37.1 us -> 42.8 us  [ladders(): pl.pallas_call(functools.partial(ladder_kernel, find, made, len(tiles)),...]
  transfers between devices with their start and end apart: 26 -> 26, of which waited for: 13 -> 12; matrix products, arithmetic and copies ran while one was open for 3% -> 3% of each run, Pallas kernels for 35% -> 37%
where the time goes in v21:
time: 123 us
  Pallas kernels  56.4 us (46%)
  waiting for transfers between devices  32.5 us (26%)
  starting transfers between devices  24.8 us (20%)
  local copies, waits for them, and re-layouts  8.87 us (7%)
    pallas_call x4, Pallas kernels, ladders(): pl.pallas_call(functools.partial(ladder_kernel, find, made, len(tiles)),...  42.8 us
    ppermute x8, waiting for transfers between devices, per_device(): second_side = lambda x: lax.ppermute(x, ('pair', 'task'), sides[1])  17.6 us
    pallas_call x4, Pallas kernels, prepare(): pl.pallas_call(prepare_kernel, out_shape=jax.ShapeDtypeStruct((count, mat...  12.2 us
    ppermute x9, starting transfers between devices, around(): lax.ppermute(x, 'task', [(c, (c + 2 * by) % task_count) for c in range(ta...  10.3 us
    ppermute x9, waiting for transfers between devices, around(): lax.ppermute(x, 'task', [(c, (c + 2 * by) % task_count) for c in range(ta...  10.1 us
    ppermute x8, starting transfers between devices, per_device(): second_side = lambda x: lax.ppermute(x, ('pair', 'task'), sides[1])  9.13 us
    unnamed x23, local copies, waits for them, and re-layouts  7.57 us
    ppermute x5, waiting for transfers between devices, per_device(): lax.ppermute(x, 'task', [(c, c ^ 1) for c in range(task_count)])  4.82 us
  transfers between devices with their start and end apart: 26, of which 12 were waited for; matrix products, arithmetic and copies ran while one was open for 3% of the time, Pallas kernels for 37%

profile of v21, /device:TPU:0, one launch (start us, length us, event | category | flops | bytes accessed | tf_op | source)
XLA Modules:
  0.0 123.1 jit_solution(4977667983591987394)
XLA Ops:
  0.0 1.2 pad
  1.3 3.1 %collective-permute-start.3 = (bf16[625,256]{1,0:T(8,128)(2,1)S(1)}, bf16[625,256]{1,0:T(8,128)(2,1)S(1)}, u32[]{:S(2)}, u32[]{:S(2)}) collective-permute-start(bf16[625,256]{1,0:T(8,128)(2,1)S(1)} %bitcast.24), channel_id=1, source_target_pairs={{0,2},{1,3},{2,4},{3,5},{4,6},{5,7},{6,0},{7,1},{8,10},{9,11},{10,... | collective-permute-start | bytes 960008 | tf_op jit(solution)/shard_map/ppermute | solution.py:299
  4.4 3.3 %copy.22 = bf16[2,384,625]{2,1,0:T(8,128)(2,1)S(1)} copy(bf16[2,384,625]{1,0,2:T(2,128)(2,1)} %param.7) | data formatting | bytes 1920000 | tf_op args[0]
  7.7 0.1 dynamic-slice_bitcast_fusion
  7.9 1.6 %collective-permute-start.2 = (bf16[2,96,625]{2,1,0:T(8,128)(2,1)S(1)}, bf16[2,96,625]{2,1,0:T(8,128)(2,1)S(1)}, u32[]{:S(2)}, u32[]{:S(2)}) collective-permute-start(bf16[2,96,625]{2,1,0:T(8,128)(2,1)S(1)} %get-tuple-element.63), channel_id=1, source_target_pairs={{0,2},{1,3},{2,4},{3,5},{4,6},{5,7},{6,0},{7,1},{8,10},{9,11},{10,... | collective-permute-start | bytes 720008 | tf_op jit(solution)/shard_map/ppermute | solution.py:299
  9.5 1.5 %collective-permute-start.1 = (bf16[2,96,625]{2,1,0:T(8,128)(2,1)S(1)}, bf16[2,96,625]{2,1,0:T(8,128)(2,1)S(1)}, u32[]{:S(2)}, u32[]{:S(2)}) collective-permute-start(bf16[2,96,625]{2,1,0:T(8,128)(2,1)S(1)} %get-tuple-element.33.refs_0_), channel_id=1, source_target_pairs={{0,16},{1,9},{2,18},{3,11},{4,20},{5,13},{6,22},{7,15},{8,24},{9,1... | collective-permute-start | bytes 720008 | tf_op jit(solution)/shard_map/ppermute | solution.py:310
  11.0 1.5 %collective-permute-start = (bf16[2,96,625]{2,1,0:T(8,128)(2,1)S(1)}, bf16[2,96,625]{2,1,0:T(8,128)(2,1)S(1)}, u32[]{:S(2)}, u32[]{:S(2)}) collective-permute-start(bf16[2,96,625]{2,1,0:T(8,128)(2,1)S(1)} %get-tuple-element.33.refs_0_), channel_id=1, source_target_pairs={{0,8},{1,17},{2,10},{3,19},{4,12},{5,21},{6,14},{7,23},{8,0},{9,25... | collective-permute-start | bytes 720008 | tf_op jit(solution)/shard_map/ppermute | solution.py:309
  12.5 6.8 %collective-permute-done.2.refs_0_ = bf16[2,96,625]{2,1,0:T(8,128)(2,1)S(1)} collective-permute-done((bf16[2,96,625]{2,1,0:T(8,128)(2,1)S(1)}, bf16[2,96,625]{2,1,0:T(8,128)(2,1)S(1)}, u32[]{:S(2)}, u32[]{:S(2)}) %collective-permute-start.2) | collective-permute-done | bytes 240032 | tf_op jit(solution)/shard_map/ppermute | solution.py:299
  19.3 0.0 collective-permute-done.1.refs_2_
  19.3 0.0 collective-permute-done.refs_1_
  19.3 0.0 collective-permute-done.3.refs_1_
  19.3 1.6 %collective-permute-start.4 = (bf16[2,96,625]{2,1,0:T(8,128)(2,1)S(1)}, bf16[2,96,625]{2,1,0:T(8,128)(2,1)S(1)}, u32[]{:S(2)}, u32[]{:S(2)}) collective-permute-start(bf16[2,96,625]{2,1,0:T(8,128)(2,1)S(1)} %collective-permute-done.refs_1_), channel_id=1, source_target_pairs={{0,16},{1,9},{2,18},{3,11},{4,20},{5,13},{6,22},{7,15},{8,24},{9,1... | collective-permute-start | bytes 720008 | tf_op jit(solution)/shard_map/ppermute | solution.py:310
  20.9 0.7 collective-permute-start.7
  21.6 0.5 collective-permute-start.6
  22.1 1.5 %collective-permute-start.5 = (bf16[2,96,625]{2,1,0:T(8,128)(2,1)S(1)}, bf16[2,96,625]{2,1,0:T(8,128)(2,1)S(1)}, u32[]{:S(2)}, u32[]{:S(2)}) collective-permute-start(bf16[2,96,625]{2,1,0:T(8,128)(2,1)S(1)} %collective-permute-done.2.refs_0_), channel_id=1, source_target_pairs={{0,8},{1,17},{2,10},{3,19},{4,12},{5,21},{6,14},{7,23},{8,0},{9,25... | collective-permute-start | bytes 720008 | tf_op jit(solution)/shard_map/ppermute | solution.py:309
  23.6 4.6 %collective-permute-done.4.refs_3_ = bf16[2,96,625]{2,1,0:T(8,128)(2,1)S(1)} collective-permute-done((bf16[2,96,625]{2,1,0:T(8,128)(2,1)S(1)}, bf16[2,96,625]{2,1,0:T(8,128)(2,1)S(1)}, u32[]{:S(2)}, u32[]{:S(2)}) %collective-permute-start.4) | collective-permute-done | bytes 240032 | tf_op jit(solution)/shard_map/ppermute | solution.py:310
  28.2 1.6 %copy-done.3 = bf16[1600,625]{1,0:T(8,128)(2,1)S(1)} copy-done((bf16[1600,625]{1,0:T(8,128)(2,1)S(1)}, bf16[1600,625]{1,0:T(8,128)(2,1)}, u32[]{:S(2)}) %copy-start.3) | copy-done | bytes 2000024
  29.7 2.6 %shard_map.73.refs_0_ = bf16[2,1600,384]{2,1,0:T(8,128)(2,1)S(1)} custom-call(s32[1]{0:T(128)} %bitcast.column_ref, bf16[2,96,625]{2,1,0:T(8,128)(2,1)S(1)} %get-tuple-element.33.refs_0_, bf16[2,96,625]{2,1,0:T(8,128)(2,1)S(1)} %collective-permute-done.refs_1_, bf16[2,96,625]{2,1,0:T(8,128)(2,1)S(1)} %collective-permute-done.1.refs_2_, ...), custom_call_target="tpu_custom_call" | custom-call | flops 1536000000 | bytes 3417600 | tf_op jit(solution)/shard_map/pallas_call | solution.py:73
  32.4 0.3 collective-permute-done.7.refs_0_
  32.7 0.0 collective-permute-done.6.refs_2_
  32.7 0.0 collective-permute-start.12
  32.7 1.6 %collective-permute-start.8 = (bf16[2,96,625]{2,1,0:T(8,128)(2,1)S(1)}, bf16[2,96,625]{2,1,0:T(8,128)(2,1)S(1)}, u32[]{:S(2)}, u32[]{:S(2)}) collective-permute-start(bf16[2,96,625]{2,1,0:T(8,128)(2,1)S(1)} %collective-permute-done.5.refs_1_), channel_id=1, source_target_pairs={{0,16},{1,9},{2,18},{3,11},{4,20},{5,13},{6,22},{7,15},{8,24},{9,1... | collective-permute-start | bytes 720008 | tf_op jit(solution)/shard_map/ppermute | solution.py:310
  34.3 2.5 %collective-permute-start.11 = (bf16[2,96,625]{2,1,0:T(8,128)(2,1)S(1)}, bf16[2,96,625]{2,1,0:T(8,128)(2,1)S(1)}, u32[]{:S(2)}, u32[]{:S(2)}) collective-permute-start(bf16[2,96,625]{2,1,0:T(8,128)(2,1)S(1)} %get-tuple-element.43), channel_id=1, source_target_pairs={{0,6},{1,7},{2,0},{3,1},{4,2},{5,3},{6,4},{7,5},{8,14},{9,15},{10,... | collective-permute-start | bytes 720008 | tf_op jit(solution)/shard_map/ppermute | solution.py:299
  36.8 0.5 collective-permute-start.10
  37.3 0.6 collective-permute-start.9
  37.9 1.0 collective-permute-done.8.refs_3_
  39.0 2.6 %shard_map.74.refs_2_ = bf16[2,1600,384]{2,1,0:T(8,128)(2,1)S(1)} custom-call(s32[1]{0:T(128)} %bitcast.column_ref, bf16[2,96,625]{2,1,0:T(8,128)(2,1)S(1)} %collective-permute-done.2.refs_0_, bf16[2,96,625]{2,1,0:T(8,128)(2,1)S(1)} %collective-permute-done.5.refs_1_, bf16[2,96,625]{2,1,0:T(8,128)(2,1)S(1)} %collective-permute-done.6.refs_2_, ...), custom_call_target="tpu_custom_call" | custom-call | flops 1536000000 | bytes 3417600 | tf_op jit(solution)/shard_map/pallas_call | solution.py:73
  41.7 0.8 collective-permute-done.11.refs_0_
  42.4 2.3 %collective-permute-done.10.refs_2_ = bf16[2,96,625]{2,1,0:T(8,128)(2,1)S(1)} collective-permute-done((bf16[2,96,625]{2,1,0:T(8,128)(2,1)S(1)}, bf16[2,96,625]{2,1,0:T(8,128)(2,1)S(1)}, u32[]{:S(2)}, u32[]{:S(2)}) %collective-permute-start.10) | collective-permute-done | bytes 240032 | tf_op jit(solution)/shard_map/ppermute | solution.py:310
  44.7 0.0 collective-permute-done.9.refs_1_
  44.7 0.0 collective-permute-done.12.refs_1_
  44.8 1.3 %collective-permute-start.13 = (bf16[2,96,625]{2,1,0:T(8,128)(2,1)S(1)}, bf16[2,96,625]{2,1,0:T(8,128)(2,1)S(1)}, u32[]{:S(2)}, u32[]{:S(2)}) collective-permute-start(bf16[2,96,625]{2,1,0:T(8,128)(2,1)S(1)} %collective-permute-done.9.refs_1_), channel_id=1, source_target_pairs={{0,16},{1,9},{2,18},{3,11},{4,20},{5,13},{6,22},{7,15},{8,24},{9,1... | collective-permute-start | bytes 720008 | tf_op jit(solution)/shard_map/ppermute | solution.py:310
  46.1 0.0 collective-permute-start.16
  46.1 0.8 collective-permute-start.15
  46.9 1.2 collective-permute-start.14
  48.0 4.7 %collective-permute-done.13.refs_3_ = bf16[2,96,625]{2,1,0:T(8,128)(2,1)S(1)} collective-permute-done((bf16[2,96,625]{2,1,0:T(8,128)(2,1)S(1)}, bf16[2,96,625]{2,1,0:T(8,128)(2,1)S(1)}, u32[]{:S(2)}, u32[]{:S(2)}) %collective-permute-start.13) | collective-permute-done | bytes 240032 | tf_op jit(solution)/shard_map/ppermute | solution.py:310
  52.7 3.4 %shard_map.75.refs_4_ = bf16[2,1600,384]{2,1,0:T(8,128)(2,1)} custom-call(s32[1]{0:T(128)} %bitcast.column_ref, bf16[2,96,625]{2,1,0:T(8,128)(2,1)S(1)} %collective-permute-done.7.refs_0_, bf16[2,96,625]{2,1,0:T(8,128)(2,1)S(1)} %collective-permute-done.9.refs_1_, bf16[2,96,625]{2,1,0:T(8,128)(2,1)S(1)} %collective-permute-done.10.refs_2_, ...), custom_call_target="tpu_custom_call" | custom-call | flops 1536000000 | bytes 3417600 | tf_op jit(solution)/shard_map/pallas_call | solution.py:73
  56.2 0.1 collective-permute-done.15.refs_2_
  56.3 1.2 collective-permute-done.16.refs_2_
  57.5 1.3 %collective-permute-start.18 = (bf16[2,96,625]{2,1,0:T(8,128)(2,1)S(1)}, bf16[2,96,625]{2,1,0:T(8,128)(2,1)S(1)}, u32[]{:S(2)}, u32[]{:S(2)}) collective-permute-start(bf16[2,96,625]{2,1,0:T(8,128)(2,1)S(1)} %collective-permute-done.14.refs_1_), channel_id=1, source_target_pairs={{0,16},{1,9},{2,18},{3,11},{4,20},{5,13},{6,22},{7,15},{8,24},{9,1... | collective-permute-start | bytes 720008 | tf_op jit(solution)/shard_map/ppermute | solution.py:310
  58.8 0.0 collective-permute-start.20
  58.8 4.9 %collective-permute-done.18.refs_3_ = bf16[2,96,625]{2,1,0:T(8,128)(2,1)S(1)} collective-permute-done((bf16[2,96,625]{2,1,0:T(8,128)(2,1)S(1)}, bf16[2,96,625]{2,1,0:T(8,128)(2,1)S(1)}, u32[]{:S(2)}, u32[]{:S(2)}) %collective-permute-start.18) | collective-permute-done | bytes 240032 | tf_op jit(solution)/shard_map/ppermute | solution.py:310
  63.7 3.5 %shard_map.76.refs_6_ = bf16[2,1600,384]{2,1,0:T(8,128)(2,1)} custom-call(s32[1]{0:T(128)} %bitcast.column_ref, bf16[2,96,625]{2,1,0:T(8,128)(2,1)S(1)} %collective-permute-done.11.refs_0_, bf16[2,96,625]{2,1,0:T(8,128)(2,1)S(1)} %collective-permute-done.14.refs_1_, bf16[2,96,625]{2,1,0:T(8,128)(2,1)S(1)} %collective-permute-done.15.refs_2_, ...), custom_call_target="tpu_custom_call" | custom-call | flops 1536000000 | bytes 3417600 | tf_op jit(solution)/shard_map/pallas_call | solution.py:73
  67.1 1.1 collective-permute-done.20.refs_3_
  68.2 1.4 %shard_map.77.refs_8_ = bf16[8,800,128]{2,1,0:T(8,128)(2,1)S(1)} custom-call(bf16[800,625]{1,0:T(8,128)(2,1)S(1)} %copy-done.2, bf16[625,256]{1,0:T(8,128)(2,1)S(1)} %bitcast.25, bf16[625,256]{1,0:T(8,128)(2,1)S(1)} %collective-permute-done.3.refs_1_, bf16[625,256]{1,0:T(8,128)(2,1)S(1)} %collective-permute-done.16.refs_2_, ...), custom_call_target="tpu_custom_call" | custom-call | flops 1024000000 | bytes 2560000 | tf_op jit(solution)/shard_map/pallas_call | solution.py:104
  69.7 0.6 collective-permute-start.22
  70.2 0.1 copy.23.owners_ref
  70.3 0.1 copy.24.local_ref
  70.4 4.8 %collective-permute-done.22.refs_9_ = bf16[8,800,128]{2,1,0:T(8,128)(2,1)S(1)} collective-permute-done((bf16[8,800,128]{2,1,0:T(8,128)(2,1)S(1)}, bf16[8,800,128]{2,1,0:T(8,128)(2,1)S(1)}, u32[]{:S(2)}, u32[]{:S(2)}) %collective-permute-start.22) | collective-permute-done | bytes 1638432 | tf_op jit(solution)/shard_map/ppermute | solution.py:296
  75.2 0.0 collective-permute-done.19.refs_5_
  75.2 0.0 collective-permute-done.21.refs_7_
  75.2 1.2 copy-done.5
  76.4 10.7 %shard_map.79 = bf16[1,2,625,128]{3,2,1,0:T(8,128)(2,1)S(1)} custom-call(s32[1]{0:T(128)} %bitcast.column_ref, s32[32,3]{1,0:T(8,128)S(1)} %copy.23.owners_ref, s32[32,4]{1,0:T(8,128)S(1)} %copy.24.local_ref, bf16[2,1600,384]{2,1,0:T(8,128)(2,1)} %copy-done, bf16[2,1600,384]{2,1,0:T(8,128)(2,1)} %collective-permute-done.12.refs_1_, ...), custom_call_target="tpu_custom_call" | custom-call | flops 2936012800 | bytes 6553600 | tf_op jit(solution)/shard_map/pallas_call | solution.py:262
  87.1 0.1 collective-permute-start.24
  87.2 10.7 %shard_map.78 = bf16[1,2,625,128]{3,2,1,0:T(8,128)(2,1)S(1)} custom-call(s32[1]{0:T(128)} %bitcast.column_ref, s32[32,3]{1,0:T(8,128)S(1)} %copy.23.owners_ref, s32[32,4]{1,0:T(8,128)S(1)} %copy.24.local_ref, bf16[2,1600,384]{2,1,0:T(8,128)(2,1)} %copy-done, bf16[2,1600,384]{2,1,0:T(8,128)(2,1)} %collective-permute-done.12.refs_1_, ...), custom_call_target="tpu_custom_call" | custom-call | flops 2936012800 | bytes 6553600 | tf_op jit(solution)/shard_map/pallas_call | solution.py:262
  97.9 1.1 collective-permute-start.23
  99.0 10.7 %shard_map.80 = bf16[1,2,625,128]{3,2,1,0:T(8,128)(2,1)S(1)} custom-call(s32[1]{0:T(128)} %bitcast.column_ref, s32[32,3]{1,0:T(8,128)S(1)} %copy.23.owners_ref, s32[32,4]{1,0:T(8,128)S(1)} %copy.24.local_ref, bf16[2,1600,384]{2,1,0:T(8,128)(2,1)} %copy-done, bf16[2,1600,384]{2,1,0:T(8,128)(2,1)} %collective-permute-done.12.refs_1_, ...), custom_call_target="tpu_custom_call" | custom-call | flops 2936012800 | bytes 6553600 | tf_op jit(solution)/shard_map/pallas_call | solution.py:262
  109.7 0.0 copy-start.6
  109.7 1.3 %collective-permute-start.25 = (bf16[2,625,128]{2,1,0:T(8,128)(2,1)S(1)}, bf16[2,625,128]{2,1,0:T(8,128)(2,1)S(1)}, u32[]{:S(2)}, u32[]{:S(2)}) collective-permute-start(bf16[2,625,128]{2,1,0:T(8,128)(2,1)S(1)} %bitcast.28), channel_id=1, source_target_pairs={{0,2},{1,3},{2,4},{3,5},{4,6},{5,7},{6,0},{7,1},{8,10},{9,11},{10,... | collective-permute-start | bytes 960008 | tf_op jit(solution)/shard_map/ppermute | solution.py:299
  110.9 10.7 %shard_map.81 = bf16[1,2,625,128]{3,2,1,0:T(8,128)(2,1)S(1)} custom-call(s32[1]{0:T(128)} %bitcast.column_ref, s32[32,3]{1,0:T(8,128)S(1)} %copy.23.owners_ref, s32[32,4]{1,0:T(8,128)S(1)} %copy.24.local_ref, bf16[2,1600,384]{2,1,0:T(8,128)(2,1)} %copy-done, bf16[2,1600,384]{2,1,0:T(8,128)(2,1)} %collective-permute-done.12.refs_1_, ...), custom_call_target="tpu_custom_call" | custom-call | flops 2936012800 | bytes 6553600 | tf_op jit(solution)/shard_map/pallas_call | solution.py:262
  121.7 0.0 collective-permute-done.23
  121.7 0.0 collective-permute-done.25
  121.7 0.2 fusion.1
  121.9 1.2 copy.32
  (23 shorter events, 0.1 us)
Async XLA Ops:
  1.3 18.0 %collective-permute-start.3 = (bf16[625,256]{1,0:T(8,128)(2,1)S(1)}, bf16[625,256]{1,0:T(8,128)(2,1)S(1)}, u32[]{:S(2)}, u32[]{:S(2)}) collective-permute-start(bf16[625,256]{1,0:T(8,128)(2,1)S(1)} %bitcast.24), channel_id=1, source_target_pairs={{0,2},{1,3},{2,4},{3,5},{4,6},{5,7},{6,0},{7,1},{8,10},{9,11},{10,... | collective-permute-start | bytes 960008 | tf_op jit(solution)/shard_map/ppermute | solution.py:299
  7.9 11.4 %collective-permute-start.2 = (bf16[2,96,625]{2,1,0:T(8,128)(2,1)S(1)}, bf16[2,96,625]{2,1,0:T(8,128)(2,1)S(1)}, u32[]{:S(2)}, u32[]{:S(2)}) collective-permute-start(bf16[2,96,625]{2,1,0:T(8,128)(2,1)S(1)} %get-tuple-element.63), channel_id=1, source_target_pairs={{0,2},{1,3},{2,4},{3,5},{4,6},{5,7},{6,0},{7,1},{8,10},{9,11},{10,... | collective-permute-start | bytes 720008 | tf_op jit(solution)/shard_map/ppermute | solution.py:299
  9.5 9.8 %collective-permute-start.1 = (bf16[2,96,625]{2,1,0:T(8,128)(2,1)S(1)}, bf16[2,96,625]{2,1,0:T(8,128)(2,1)S(1)}, u32[]{:S(2)}, u32[]{:S(2)}) collective-permute-start(bf16[2,96,625]{2,1,0:T(8,128)(2,1)S(1)} %get-tuple-element.33.refs_0_), channel_id=1, source_target_pairs={{0,16},{1,9},{2,18},{3,11},{4,20},{5,13},{6,22},{7,15},{8,24},{9,1... | collective-permute-start | bytes 720008 | tf_op jit(solution)/shard_map/ppermute | solution.py:310
  11.0 8.3 %collective-permute-start = (bf16[2,96,625]{2,1,0:T(8,128)(2,1)S(1)}, bf16[2,96,625]{2,1,0:T(8,128)(2,1)S(1)}, u32[]{:S(2)}, u32[]{:S(2)}) collective-permute-start(bf16[2,96,625]{2,1,0:T(8,128)(2,1)S(1)} %get-tuple-element.33.refs_0_), channel_id=1, source_target_pairs={{0,8},{1,17},{2,10},{3,19},{4,12},{5,21},{6,14},{7,23},{8,0},{9,25... | collective-permute-start | bytes 720008 | tf_op jit(solution)/shard_map/ppermute | solution.py:309
  19.3 8.9 %collective-permute-start.4 = (bf16[2,96,625]{2,1,0:T(8,128)(2,1)S(1)}, bf16[2,96,625]{2,1,0:T(8,128)(2,1)S(1)}, u32[]{:S(2)}, u32[]{:S(2)}) collective-permute-start(bf16[2,96,625]{2,1,0:T(8,128)(2,1)S(1)} %collective-permute-done.refs_1_), channel_id=1, source_target_pairs={{0,16},{1,9},{2,18},{3,11},{4,20},{5,13},{6,22},{7,15},{8,24},{9,1... | collective-permute-start | bytes 720008 | tf_op jit(solution)/shard_map/ppermute | solution.py:310
  20.9 11.8 %collective-permute-start.7 = (bf16[2,96,625]{2,1,0:T(8,128)(2,1)S(1)}, bf16[2,96,625]{2,1,0:T(8,128)(2,1)S(1)}, u32[]{:S(2)}, u32[]{:S(2)}) collective-permute-start(bf16[2,96,625]{2,1,0:T(8,128)(2,1)S(1)} %get-tuple-element.37), channel_id=1, source_target_pairs={{0,4},{1,5},{2,6},{3,7},{4,0},{5,1},{6,2},{7,3},{8,12},{9,13},{10,... | collective-permute-start | bytes 720008 | tf_op jit(solution)/shard_map/ppermute | solution.py:299
  21.6 11.1 %collective-permute-start.6 = (bf16[2,96,625]{2,1,0:T(8,128)(2,1)S(1)}, bf16[2,96,625]{2,1,0:T(8,128)(2,1)S(1)}, u32[]{:S(2)}, u32[]{:S(2)}) collective-permute-start(bf16[2,96,625]{2,1,0:T(8,128)(2,1)S(1)} %collective-permute-done.2.refs_0_), channel_id=1, source_target_pairs={{0,16},{1,9},{2,18},{3,11},{4,20},{5,13},{6,22},{7,15},{8,24},{9,1... | collective-permute-start | bytes 720008 | tf_op jit(solution)/shard_map/ppermute | solution.py:310
  22.1 10.6 %collective-permute-start.5 = (bf16[2,96,625]{2,1,0:T(8,128)(2,1)S(1)}, bf16[2,96,625]{2,1,0:T(8,128)(2,1)S(1)}, u32[]{:S(2)}, u32[]{:S(2)}) collective-permute-start(bf16[2,96,625]{2,1,0:T(8,128)(2,1)S(1)} %collective-permute-done.2.refs_0_), channel_id=1, source_target_pairs={{0,8},{1,17},{2,10},{3,19},{4,12},{5,21},{6,14},{7,23},{8,0},{9,25... | collective-permute-start | bytes 720008 | tf_op jit(solution)/shard_map/ppermute | solution.py:309
  28.2 1.6 %copy-start.3 = (bf16[1600,625]{1,0:T(8,128)(2,1)S(1)}, bf16[1600,625]{1,0:T(8,128)(2,1)}, u32[]{:S(2)}) copy-start(bf16[1600,625]{1,0:T(8,128)(2,1)} %constant.59.clone.refs_4_) | copy-start | bytes 6000004
  29.7 9.3 %copy-start.4 = (bf16[1600,625]{1,0:T(8,128)(2,1)S(1)}, bf16[1600,625]{1,0:T(8,128)(2,1)}, u32[]{:S(2)}) copy-start(bf16[1600,625]{1,0:T(8,128)(2,1)} %constant.59.clone.refs_4_) | copy-start | bytes 6000004
  32.4 9.3 %copy-start = (bf16[2,1600,384]{2,1,0:T(8,128)(2,1)}, bf16[2,1600,384]{2,1,0:T(8,128)(2,1)S(1)}, u32[]{:S(2)}) copy-start(bf16[2,1600,384]{2,1,0:T(8,128)(2,1)S(1)} %shard_map.73.refs_0_) | copy-start | bytes 7372804
  32.7 12.0 %collective-permute-start.12 = (bf16[2,1600,384]{2,1,0:T(8,128)(2,1)S(1)}, bf16[2,1600,384]{2,1,0:T(8,128)(2,1)}, u32[]{:S(2)}, u32[]{:S(2)}) collective-permute-start(bf16[2,1600,384]{2,1,0:T(8,128)(2,1)S(1)} %shard_map.73.refs_0_), channel_id=1, source_target_pairs={{0,1},{1,0},{2,3},{3,2},{4,5},{5,4},{6,7},{7,6},{8,9},{9,8},{10,11... | collective-permute-start | bytes 7372808 | tf_op jit(solution)/shard_map/ppermute | solution.py:296
  32.7 6.3 %collective-permute-start.8 = (bf16[2,96,625]{2,1,0:T(8,128)(2,1)S(1)}, bf16[2,96,625]{2,1,0:T(8,128)(2,1)S(1)}, u32[]{:S(2)}, u32[]{:S(2)}) collective-permute-start(bf16[2,96,625]{2,1,0:T(8,128)(2,1)S(1)} %collective-permute-done.5.refs_1_), channel_id=1, source_target_pairs={{0,16},{1,9},{2,18},{3,11},{4,20},{5,13},{6,22},{7,15},{8,24},{9,1... | collective-permute-start | bytes 720008 | tf_op jit(solution)/shard_map/ppermute | solution.py:310
  34.3 8.1 %collective-permute-start.11 = (bf16[2,96,625]{2,1,0:T(8,128)(2,1)S(1)}, bf16[2,96,625]{2,1,0:T(8,128)(2,1)S(1)}, u32[]{:S(2)}, u32[]{:S(2)}) collective-permute-start(bf16[2,96,625]{2,1,0:T(8,128)(2,1)S(1)} %get-tuple-element.43), channel_id=1, source_target_pairs={{0,6},{1,7},{2,0},{3,1},{4,2},{5,3},{6,4},{7,5},{8,14},{9,15},{10,... | collective-permute-start | bytes 720008 | tf_op jit(solution)/shard_map/ppermute | solution.py:299
  36.8 8.0 %collective-permute-start.10 = (bf16[2,96,625]{2,1,0:T(8,128)(2,1)S(1)}, bf16[2,96,625]{2,1,0:T(8,128)(2,1)S(1)}, u32[]{:S(2)}, u32[]{:S(2)}) collective-permute-start(bf16[2,96,625]{2,1,0:T(8,128)(2,1)S(1)} %collective-permute-done.7.refs_0_), channel_id=1, source_target_pairs={{0,16},{1,9},{2,18},{3,11},{4,20},{5,13},{6,22},{7,15},{8,24},{9,1... | collective-permute-start | bytes 720008 | tf_op jit(solution)/shard_map/ppermute | solution.py:310
  37.3 7.5 %collective-permute-start.9 = (bf16[2,96,625]{2,1,0:T(8,128)(2,1)S(1)}, bf16[2,96,625]{2,1,0:T(8,128)(2,1)S(1)}, u32[]{:S(2)}, u32[]{:S(2)}) collective-permute-start(bf16[2,96,625]{2,1,0:T(8,128)(2,1)S(1)} %collective-permute-done.7.refs_0_), channel_id=1, source_target_pairs={{0,8},{1,17},{2,10},{3,19},{4,12},{5,21},{6,14},{7,23},{8,0},{9,25... | collective-permute-start | bytes 720008 | tf_op jit(solution)/shard_map/ppermute | solution.py:309
  41.6 14.5 %copy-start.1 = (bf16[2,1600,384]{2,1,0:T(8,128)(2,1)}, bf16[2,1600,384]{2,1,0:T(8,128)(2,1)S(1)}, u32[]{:S(2)}) copy-start(bf16[2,1600,384]{2,1,0:T(8,128)(2,1)S(1)} %shard_map.74.refs_2_) | copy-start | bytes 7372804
  44.8 12.7 %collective-permute-start.17 = (bf16[2,1600,384]{2,1,0:T(8,128)(2,1)S(1)}, bf16[2,1600,384]{2,1,0:T(8,128)(2,1)}, u32[]{:S(2)}, u32[]{:S(2)}) collective-permute-start(bf16[2,1600,384]{2,1,0:T(8,128)(2,1)S(1)} %shard_map.74.refs_2_), channel_id=1, source_target_pairs={{0,1},{1,0},{2,3},{3,2},{4,5},{5,4},{6,7},{7,6},{8,9},{9,8},{10,11... | collective-permute-start | bytes 7372808 | tf_op jit(solution)/shard_map/ppermute | solution.py:296
  44.8 8.0 %collective-permute-start.13 = (bf16[2,96,625]{2,1,0:T(8,128)(2,1)S(1)}, bf16[2,96,625]{2,1,0:T(8,128)(2,1)S(1)}, u32[]{:S(2)}, u32[]{:S(2)}) collective-permute-start(bf16[2,96,625]{2,1,0:T(8,128)(2,1)S(1)} %collective-permute-done.9.refs_1_), channel_id=1, source_target_pairs={{0,16},{1,9},{2,18},{3,11},{4,20},{5,13},{6,22},{7,15},{8,24},{9,1... | collective-permute-start | bytes 720008 | tf_op jit(solution)/shard_map/ppermute | solution.py:310
  46.1 11.4 %collective-permute-start.16 = (bf16[625,256]{1,0:T(8,128)(2,1)S(1)}, bf16[625,256]{1,0:T(8,128)(2,1)S(1)}, u32[]{:S(2)}, u32[]{:S(2)}) collective-permute-start(bf16[625,256]{1,0:T(8,128)(2,1)S(1)} %collective-permute-done.3.refs_1_), channel_id=1, source_target_pairs={{0,2},{1,3},{2,4},{3,5},{4,6},{5,7},{6,0},{7,1},{8,10},{9,11},{10,... | collective-permute-start | bytes 960008 | tf_op jit(solution)/shard_map/ppermute | solution.py:299
  46.1 10.2 %collective-permute-start.15 = (bf16[2,96,625]{2,1,0:T(8,128)(2,1)S(1)}, bf16[2,96,625]{2,1,0:T(8,128)(2,1)S(1)}, u32[]{:S(2)}, u32[]{:S(2)}) collective-permute-start(bf16[2,96,625]{2,1,0:T(8,128)(2,1)S(1)} %collective-permute-done.11.refs_0_), channel_id=1, source_target_pairs={{0,16},{1,9},{2,18},{3,11},{4,20},{5,13},{6,22},{7,15},{8,24},{9,1... | collective-permute-start | bytes 720008 | tf_op jit(solution)/shard_map/ppermute | solution.py:310
  46.9 9.4 %collective-permute-start.14 = (bf16[2,96,625]{2,1,0:T(8,128)(2,1)S(1)}, bf16[2,96,625]{2,1,0:T(8,128)(2,1)S(1)}, u32[]{:S(2)}, u32[]{:S(2)}) collective-permute-start(bf16[2,96,625]{2,1,0:T(8,128)(2,1)S(1)} %collective-permute-done.11.refs_0_), channel_id=1, source_target_pairs={{0,8},{1,17},{2,10},{3,19},{4,12},{5,21},{6,14},{7,23},{8,0},{9,25... | collective-permute-start | bytes 720008 | tf_op jit(solution)/shard_map/ppermute | solution.py:309
  56.2 12.0 %copy-start.2 = (bf16[800,625]{1,0:T(8,128)(2,1)S(1)}, bf16[800,625]{1,0:T(8,128)(2,1)}, u32[]{:S(2)}) copy-start(bf16[800,625]{1,0:T(8,128)(2,1)} %constant.60.clone.matrix_ref) | copy-start | bytes 3000004
  57.5 6.2 %collective-permute-start.18 = (bf16[2,96,625]{2,1,0:T(8,128)(2,1)S(1)}, bf16[2,96,625]{2,1,0:T(8,128)(2,1)S(1)}, u32[]{:S(2)}, u32[]{:S(2)}) collective-permute-start(bf16[2,96,625]{2,1,0:T(8,128)(2,1)S(1)} %collective-permute-done.14.refs_1_), channel_id=1, source_target_pairs={{0,16},{1,9},{2,18},{3,11},{4,20},{5,13},{6,22},{7,15},{8,24},{9,1... | collective-permute-start | bytes 720008 | tf_op jit(solution)/shard_map/ppermute | solution.py:310
  58.8 9.4 %collective-permute-start.20 = (bf16[625,256]{1,0:T(8,128)(2,1)S(1)}, bf16[625,256]{1,0:T(8,128)(2,1)S(1)}, u32[]{:S(2)}, u32[]{:S(2)}) collective-permute-start(bf16[625,256]{1,0:T(8,128)(2,1)S(1)} %collective-permute-done.16.refs_2_), channel_id=1, source_target_pairs={{0,2},{1,3},{2,4},{3,5},{4,6},{5,7},{6,0},{7,1},{8,10},{9,11},{10,... | collective-permute-start | bytes 960008 | tf_op jit(solution)/shard_map/ppermute | solution.py:299
  63.6 11.6 %collective-permute-start.19 = (bf16[2,1600,384]{2,1,0:T(8,128)(2,1)}, bf16[2,1600,384]{2,1,0:T(8,128)(2,1)}, u32[]{:S(2)}, u32[]{:S(2)}) collective-permute-start(bf16[2,1600,384]{2,1,0:T(8,128)(2,1)} %shard_map.75.refs_4_), channel_id=1, source_target_pairs={{0,1},{1,0},{2,3},{3,2},{4,5},{5,4},{6,7},{7,6},{8,9},{9,8},{10,11... | collective-permute-start | bytes 7372808 | tf_op jit(solution)/shard_map/ppermute | solution.py:296
  67.1 3.1 %copy-start.7 = (s32[32,3]{0,1:T(4,128)S(1)}, s32[32,3]{0,1:T(4,128)}, u32[]{:S(2)}) copy-start(s32[32,3]{0,1:T(4,128)} %param.10) | copy-start | bytes 1156
  67.1 3.2 %copy-start.8 = (s32[32,4]{0,1:T(4,128)S(1)}, s32[32,4]{0,1:T(4,128)}, u32[]{:S(2)}) copy-start(s32[32,4]{0,1:T(4,128)} %param.11) | copy-start | bytes 1540
  68.2 7.0 %collective-permute-start.21 = (bf16[2,1600,384]{2,1,0:T(8,128)(2,1)}, bf16[2,1600,384]{2,1,0:T(8,128)(2,1)}, u32[]{:S(2)}, u32[]{:S(2)}) collective-permute-start(bf16[2,1600,384]{2,1,0:T(8,128)(2,1)} %shard_map.76.refs_6_), channel_id=1, source_target_pairs={{0,1},{1,0},{2,3},{3,2},{4,5},{5,4},{6,7},{7,6},{8,9},{9,8},{10,11... | collective-permute-start | bytes 7372808 | tf_op jit(solution)/shard_map/ppermute | solution.py:296
  69.7 5.6 %collective-permute-start.22 = (bf16[8,800,128]{2,1,0:T(8,128)(2,1)S(1)}, bf16[8,800,128]{2,1,0:T(8,128)(2,1)S(1)}, u32[]{:S(2)}, u32[]{:S(2)}) collective-permute-start(bf16[8,800,128]{2,1,0:T(8,128)(2,1)S(1)} %shard_map.77.refs_8_), channel_id=1, source_target_pairs={{0,1},{1,0},{2,3},{3,2},{4,5},{5,4},{6,7},{7,6},{8,9},{9,8},{10,11... | collective-permute-start | bytes 4915208 | tf_op jit(solution)/shard_map/ppermute | solution.py:296
  75.2 1.2 copy-start.5
  87.1 34.5 %collective-permute-start.24 = (bf16[2,625,128]{2,1,0:T(8,128)(2,1)S(1)}, bf16[2,625,128]{2,1,0:T(8,128)(2,1)S(1)}, u32[]{:S(2)}, u32[]{:S(2)}) collective-permute-start(bf16[2,625,128]{2,1,0:T(8,128)(2,1)S(1)} %bitcast.26), channel_id=1, source_target_pairs={{0,4},{1,5},{2,6},{3,7},{4,0},{5,1},{6,2},{7,3},{8,12},{9,13},{10,... | collective-permute-start | bytes 960008 | tf_op jit(solution)/shard_map/ppermute | solution.py:299
  97.9 23.8 %collective-permute-start.23 = (bf16[2,625,128]{2,1,0:T(8,128)(2,1)S(1)}, bf16[2,625,128]{2,1,0:T(8,128)(2,1)S(1)}, u32[]{:S(2)}, u32[]{:S(2)}) collective-permute-start(bf16[2,625,128]{2,1,0:T(8,128)(2,1)S(1)} %bitcast.27), channel_id=1, source_target_pairs={{0,6},{1,7},{2,0},{3,1},{4,2},{5,3},{6,4},{7,5},{8,14},{9,15},{10,... | collective-permute-start | bytes 960008 | tf_op jit(solution)/shard_map/ppermute | solution.py:299
  109.7 12.0 %copy-start.6 = (f32[2,128,625]{1,0,2:T(2,128)S(1)}, f32[2,128,625]{1,0,2:T(2,128)}, u32[]{:S(2)}) copy-start(f32[2,128,625]{1,0,2:T(2,128)} %param.9) | copy-start | bytes 1920004
  109.7 12.0 %collective-permute-start.25 = (bf16[2,625,128]{2,1,0:T(8,128)(2,1)S(1)}, bf16[2,625,128]{2,1,0:T(8,128)(2,1)S(1)}, u32[]{:S(2)}, u32[]{:S(2)}) collective-permute-start(bf16[2,625,128]{2,1,0:T(8,128)(2,1)S(1)} %bitcast.28), channel_id=1, source_target_pairs={{0,2},{1,3},{2,4},{3,5},{4,6},{5,7},{6,0},{7,1},{8,10},{9,11},{10,... | collective-permute-start | bytes 960008 | tf_op jit(solution)/shard_map/ppermute | solution.py:299

commit v22 on v21

--- a/solution.py
+++ b/solution.py
@@ -22,7 +22,7 @@
 BF = jnp.bfloat16
 F32 = jnp.float32
 VMEM_BYTES = 48 * 1024 * 1024
-LADDER_VMEM_BYTES = 52 * 1024 * 1024
+LADDER_VMEM_BYTES = 50 * 1024 * 1024
 
 
 def spread(spots, rows):

time: 123 us -> 117 us (0.951)
  Pallas kernels: 56.4 us -> 50.7 us
    pallas_call x4, Pallas kernels: 42.8 us -> 37.1 us  [ladders(): pl.pallas_call(functools.partial(ladder_kernel, find, made, len(tiles)),...]
    unnamed x23 -> x21, local copies, waits for them, and re-layouts: 7.57 us -> 6.38 us
  transfers between devices with their start and end apart: 26 -> 26, of which waited for: 12 -> 13; matrix products, arithmetic and copies ran while one was open for 3% -> 3% of each run, Pallas kernels for 37% -> 36%
where the time goes in v22:
time: 117 us
  Pallas kernels  50.7 us (43%)
  waiting for transfers between devices  32.9 us (28%)
  starting transfers between devices  24.8 us (21%)
  local copies, waits for them, and re-layouts  7.68 us (7%)
    pallas_call x4, Pallas kernels, ladders(): pl.pallas_call(functools.partial(ladder_kernel, find, made, len(tiles)),...  37.1 us
    ppermute x8, waiting for transfers between devices, per_device(): second_side = lambda x: lax.ppermute(x, ('pair', 'task'), sides[1])  17.6 us
    pallas_call x4, Pallas kernels, prepare(): pl.pallas_call(prepare_kernel, out_shape=jax.ShapeDtypeStruct((count, mat...  12.2 us
    ppermute x9, waiting for transfers between devices, around(): lax.ppermute(x, 'task', [(c, (c + 2 * by) % task_count) for c in range(ta...  10.6 us
    ppermute x9, starting transfers between devices, around(): lax.ppermute(x, 'task', [(c, (c + 2 * by) % task_count) for c in range(ta...  10.3 us
    ppermute x8, starting transfers between devices, per_device(): second_side = lambda x: lax.ppermute(x, ('pair', 'task'), sides[1])  9.13 us
    unnamed x21, local copies, waits for them, and re-layouts  6.38 us
    ppermute x5, waiting for transfers between devices, per_device(): lax.ppermute(x, 'task', [(c, c ^ 1) for c in range(task_count)])  4.82 us
  transfers between devices with their start and end apart: 26, of which 13 were waited for; matrix products, arithmetic and copies ran while one was open for 3% of the time, Pallas kernels for 36%

profile of v22, /device:TPU:0, one launch (start us, length us, event | category | flops | bytes accessed | tf_op | source)
XLA Modules:
  0.0 116.6 jit_solution(8511113852481325471)
XLA Ops:
  0.0 1.2 %pad = bf16[632,2,128]{2,1,0:T(2,128)(2,1)S(1)} pad(bf16[625,2,128]{2,1,0:T(2,128)(2,1)} %bitcast.31, bf16[]{:T(256)} %constant.64), padding=0_7x0_0x0_0 | pad | bytes 643586
  1.3 3.1 %collective-permute-start.3 = (bf16[625,256]{1,0:T(8,128)(2,1)S(1)}, bf16[625,256]{1,0:T(8,128)(2,1)S(1)}, u32[]{:S(2)}, u32[]{:S(2)}) collective-permute-start(bf16[625,256]{1,0:T(8,128)(2,1)S(1)} %bitcast.24), channel_id=1, source_target_pairs={{0,2},{1,3},{2,4},{3,5},{4,6},{5,7},{6,0},{7,1},{8,10},{9,11},{10,... | collective-permute-start | bytes 960008 | tf_op jit(solution)/shard_map/ppermute | solution.py:299
  4.4 3.3 %copy.22 = bf16[2,384,625]{2,1,0:T(8,128)(2,1)S(1)} copy(bf16[2,384,625]{1,0,2:T(2,128)(2,1)} %param.7) | data formatting | bytes 1920000 | tf_op args[0]
  7.7 0.1 dynamic-slice_bitcast_fusion
  7.9 1.6 %collective-permute-start.2 = (bf16[2,96,625]{2,1,0:T(8,128)(2,1)S(1)}, bf16[2,96,625]{2,1,0:T(8,128)(2,1)S(1)}, u32[]{:S(2)}, u32[]{:S(2)}) collective-permute-start(bf16[2,96,625]{2,1,0:T(8,128)(2,1)S(1)} %get-tuple-element.63), channel_id=1, source_target_pairs={{0,2},{1,3},{2,4},{3,5},{4,6},{5,7},{6,0},{7,1},{8,10},{9,11},{10,... | collective-permute-start | bytes 720008 | tf_op jit(solution)/shard_map/ppermute | solution.py:299
  9.5 1.5 %collective-permute-start.1 = (bf16[2,96,625]{2,1,0:T(8,128)(2,1)S(1)}, bf16[2,96,625]{2,1,0:T(8,128)(2,1)S(1)}, u32[]{:S(2)}, u32[]{:S(2)}) collective-permute-start(bf16[2,96,625]{2,1,0:T(8,128)(2,1)S(1)} %get-tuple-element.33.refs_0_), channel_id=1, source_target_pairs={{0,16},{1,9},{2,18},{3,11},{4,20},{5,13},{6,22},{7,15},{8,24},{9,1... | collective-permute-start | bytes 720008 | tf_op jit(solution)/shard_map/ppermute | solution.py:310
  11.0 1.5 %collective-permute-start = (bf16[2,96,625]{2,1,0:T(8,128)(2,1)S(1)}, bf16[2,96,625]{2,1,0:T(8,128)(2,1)S(1)}, u32[]{:S(2)}, u32[]{:S(2)}) collective-permute-start(bf16[2,96,625]{2,1,0:T(8,128)(2,1)S(1)} %get-tuple-element.33.refs_0_), channel_id=1, source_target_pairs={{0,8},{1,17},{2,10},{3,19},{4,12},{5,21},{6,14},{7,23},{8,0},{9,25... | collective-permute-start | bytes 720008 | tf_op jit(solution)/shard_map/ppermute | solution.py:309
  12.5 6.8 %collective-permute-done.2.refs_0_ = bf16[2,96,625]{2,1,0:T(8,128)(2,1)S(1)} collective-permute-done((bf16[2,96,625]{2,1,0:T(8,128)(2,1)S(1)}, bf16[2,96,625]{2,1,0:T(8,128)(2,1)S(1)}, u32[]{:S(2)}, u32[]{:S(2)}) %collective-permute-start.2) | collective-permute-done | bytes 240032 | tf_op jit(solution)/shard_map/ppermute | solution.py:299
  19.3 0.0 collective-permute-done.1.refs_2_
  19.3 0.0 collective-permute-done.refs_1_
  19.3 0.0 collective-permute-done.3.refs_1_
  19.3 1.6 %collective-permute-start.4 = (bf16[2,96,625]{2,1,0:T(8,128)(2,1)S(1)}, bf16[2,96,625]{2,1,0:T(8,128)(2,1)S(1)}, u32[]{:S(2)}, u32[]{:S(2)}) collective-permute-start(bf16[2,96,625]{2,1,0:T(8,128)(2,1)S(1)} %collective-permute-done.refs_1_), channel_id=1, source_target_pairs={{0,16},{1,9},{2,18},{3,11},{4,20},{5,13},{6,22},{7,15},{8,24},{9,1... | collective-permute-start | bytes 720008 | tf_op jit(solution)/shard_map/ppermute | solution.py:310
  20.9 0.7 collective-permute-start.7
  21.6 0.5 collective-permute-start.6
  22.1 1.5 %collective-permute-start.5 = (bf16[2,96,625]{2,1,0:T(8,128)(2,1)S(1)}, bf16[2,96,625]{2,1,0:T(8,128)(2,1)S(1)}, u32[]{:S(2)}, u32[]{:S(2)}) collective-permute-start(bf16[2,96,625]{2,1,0:T(8,128)(2,1)S(1)} %collective-permute-done.2.refs_0_), channel_id=1, source_target_pairs={{0,8},{1,17},{2,10},{3,19},{4,12},{5,21},{6,14},{7,23},{8,0},{9,25... | collective-permute-start | bytes 720008 | tf_op jit(solution)/shard_map/ppermute | solution.py:309
  23.6 4.6 %collective-permute-done.4.refs_3_ = bf16[2,96,625]{2,1,0:T(8,128)(2,1)S(1)} collective-permute-done((bf16[2,96,625]{2,1,0:T(8,128)(2,1)S(1)}, bf16[2,96,625]{2,1,0:T(8,128)(2,1)S(1)}, u32[]{:S(2)}, u32[]{:S(2)}) %collective-permute-start.4) | collective-permute-done | bytes 240032 | tf_op jit(solution)/shard_map/ppermute | solution.py:310
  28.2 1.6 %copy-done.3 = bf16[1600,625]{1,0:T(8,128)(2,1)S(1)} copy-done((bf16[1600,625]{1,0:T(8,128)(2,1)S(1)}, bf16[1600,625]{1,0:T(8,128)(2,1)}, u32[]{:S(2)}) %copy-start.3) | copy-done | bytes 2000024
  29.7 2.6 %shard_map.73.refs_0_ = bf16[2,1600,384]{2,1,0:T(8,128)(2,1)S(1)} custom-call(s32[1]{0:T(128)} %bitcast.column_ref, bf16[2,96,625]{2,1,0:T(8,128)(2,1)S(1)} %get-tuple-element.33.refs_0_, bf16[2,96,625]{2,1,0:T(8,128)(2,1)S(1)} %collective-permute-done.refs_1_, bf16[2,96,625]{2,1,0:T(8,128)(2,1)S(1)} %collective-permute-done.1.refs_2_, ...), custom_call_target="tpu_custom_call" | custom-call | flops 1536000000 | bytes 3417600 | tf_op jit(solution)/shard_map/pallas_call | solution.py:73
  32.4 0.3 collective-permute-done.7.refs_0_
  32.7 0.0 collective-permute-done.6.refs_2_
  32.7 0.0 collective-permute-start.12
  32.7 1.6 %collective-permute-start.8 = (bf16[2,96,625]{2,1,0:T(8,128)(2,1)S(1)}, bf16[2,96,625]{2,1,0:T(8,128)(2,1)S(1)}, u32[]{:S(2)}, u32[]{:S(2)}) collective-permute-start(bf16[2,96,625]{2,1,0:T(8,128)(2,1)S(1)} %collective-permute-done.5.refs_1_), channel_id=1, source_target_pairs={{0,16},{1,9},{2,18},{3,11},{4,20},{5,13},{6,22},{7,15},{8,24},{9,1... | collective-permute-start | bytes 720008 | tf_op jit(solution)/shard_map/ppermute | solution.py:310
  34.3 2.5 %collective-permute-start.11 = (bf16[2,96,625]{2,1,0:T(8,128)(2,1)S(1)}, bf16[2,96,625]{2,1,0:T(8,128)(2,1)S(1)}, u32[]{:S(2)}, u32[]{:S(2)}) collective-permute-start(bf16[2,96,625]{2,1,0:T(8,128)(2,1)S(1)} %get-tuple-element.43), channel_id=1, source_target_pairs={{0,6},{1,7},{2,0},{3,1},{4,2},{5,3},{6,4},{7,5},{8,14},{9,15},{10,... | collective-permute-start | bytes 720008 | tf_op jit(solution)/shard_map/ppermute | solution.py:299
  36.8 0.5 collective-permute-start.10
  37.3 0.6 collective-permute-start.9
  37.9 1.0 collective-permute-done.8.refs_3_
  39.0 2.6 %shard_map.74.refs_2_ = bf16[2,1600,384]{2,1,0:T(8,128)(2,1)S(1)} custom-call(s32[1]{0:T(128)} %bitcast.column_ref, bf16[2,96,625]{2,1,0:T(8,128)(2,1)S(1)} %collective-permute-done.2.refs_0_, bf16[2,96,625]{2,1,0:T(8,128)(2,1)S(1)} %collective-permute-done.5.refs_1_, bf16[2,96,625]{2,1,0:T(8,128)(2,1)S(1)} %collective-permute-done.6.refs_2_, ...), custom_call_target="tpu_custom_call" | custom-call | flops 1536000000 | bytes 3417600 | tf_op jit(solution)/shard_map/pallas_call | solution.py:73
  41.7 0.8 collective-permute-done.11.refs_0_
  42.4 2.3 %collective-permute-done.10.refs_2_ = bf16[2,96,625]{2,1,0:T(8,128)(2,1)S(1)} collective-permute-done((bf16[2,96,625]{2,1,0:T(8,128)(2,1)S(1)}, bf16[2,96,625]{2,1,0:T(8,128)(2,1)S(1)}, u32[]{:S(2)}, u32[]{:S(2)}) %collective-permute-start.10) | collective-permute-done | bytes 240032 | tf_op jit(solution)/shard_map/ppermute | solution.py:310
  44.7 0.0 collective-permute-done.9.refs_1_
  44.7 0.0 collective-permute-done.12.refs_1_
  44.8 0.0 collective-permute-start.17
  44.8 1.3 %collective-permute-start.13 = (bf16[2,96,625]{2,1,0:T(8,128)(2,1)S(1)}, bf16[2,96,625]{2,1,0:T(8,128)(2,1)S(1)}, u32[]{:S(2)}, u32[]{:S(2)}) collective-permute-start(bf16[2,96,625]{2,1,0:T(8,128)(2,1)S(1)} %collective-permute-done.9.refs_1_), channel_id=1, source_target_pairs={{0,16},{1,9},{2,18},{3,11},{4,20},{5,13},{6,22},{7,15},{8,24},{9,1... | collective-permute-start | bytes 720008 | tf_op jit(solution)/shard_map/ppermute | solution.py:310
  46.1 0.0 collective-permute-start.16
  46.1 0.8 collective-permute-start.15
  46.9 1.2 %collective-permute-start.14 = (bf16[2,96,625]{2,1,0:T(8,128)(2,1)S(1)}, bf16[2,96,625]{2,1,0:T(8,128)(2,1)S(1)}, u32[]{:S(2)}, u32[]{:S(2)}) collective-permute-start(bf16[2,96,625]{2,1,0:T(8,128)(2,1)S(1)} %collective-permute-done.11.refs_0_), channel_id=1, source_target_pairs={{0,8},{1,17},{2,10},{3,19},{4,12},{5,21},{6,14},{7,23},{8,0},{9,25... | collective-permute-start | bytes 720008 | tf_op jit(solution)/shard_map/ppermute | solution.py:309
  48.0 4.7 %collective-permute-done.13.refs_3_ = bf16[2,96,625]{2,1,0:T(8,128)(2,1)S(1)} collective-permute-done((bf16[2,96,625]{2,1,0:T(8,128)(2,1)S(1)}, bf16[2,96,625]{2,1,0:T(8,128)(2,1)S(1)}, u32[]{:S(2)}, u32[]{:S(2)}) %collective-permute-start.13) | collective-permute-done | bytes 240032 | tf_op jit(solution)/shard_map/ppermute | solution.py:310
  52.7 3.5 %shard_map.75.refs_4_ = bf16[2,1600,384]{2,1,0:T(8,128)(2,1)} custom-call(s32[1]{0:T(128)} %bitcast.column_ref, bf16[2,96,625]{2,1,0:T(8,128)(2,1)S(1)} %collective-permute-done.7.refs_0_, bf16[2,96,625]{2,1,0:T(8,128)(2,1)S(1)} %collective-permute-done.9.refs_1_, bf16[2,96,625]{2,1,0:T(8,128)(2,1)S(1)} %collective-permute-done.10.refs_2_, ...), custom_call_target="tpu_custom_call" | custom-call | flops 1536000000 | bytes 3417600 | tf_op jit(solution)/shard_map/pallas_call | solution.py:73
  56.2 0.1 collective-permute-done.15.refs_2_
  56.3 1.2 collective-permute-done.16.refs_2_
  57.5 1.3 %collective-permute-start.18 = (bf16[2,96,625]{2,1,0:T(8,128)(2,1)S(1)}, bf16[2,96,625]{2,1,0:T(8,128)(2,1)S(1)}, u32[]{:S(2)}, u32[]{:S(2)}) collective-permute-start(bf16[2,96,625]{2,1,0:T(8,128)(2,1)S(1)} %collective-permute-done.14.refs_1_), channel_id=1, source_target_pairs={{0,16},{1,9},{2,18},{3,11},{4,20},{5,13},{6,22},{7,15},{8,24},{9,1... | collective-permute-start | bytes 720008 | tf_op jit(solution)/shard_map/ppermute | solution.py:310
  58.8 4.9 %collective-permute-done.18.refs_3_ = bf16[2,96,625]{2,1,0:T(8,128)(2,1)S(1)} collective-permute-done((bf16[2,96,625]{2,1,0:T(8,128)(2,1)S(1)}, bf16[2,96,625]{2,1,0:T(8,128)(2,1)S(1)}, u32[]{:S(2)}, u32[]{:S(2)}) %collective-permute-start.18) | collective-permute-done | bytes 240032 | tf_op jit(solution)/shard_map/ppermute | solution.py:310
  63.7 3.4 %shard_map.76.refs_6_ = bf16[2,1600,384]{2,1,0:T(8,128)(2,1)} custom-call(s32[1]{0:T(128)} %bitcast.column_ref, bf16[2,96,625]{2,1,0:T(8,128)(2,1)S(1)} %collective-permute-done.11.refs_0_, bf16[2,96,625]{2,1,0:T(8,128)(2,1)S(1)} %collective-permute-done.14.refs_1_, bf16[2,96,625]{2,1,0:T(8,128)(2,1)S(1)} %collective-permute-done.15.refs_2_, ...), custom_call_target="tpu_custom_call" | custom-call | flops 1536000000 | bytes 3417600 | tf_op jit(solution)/shard_map/pallas_call | solution.py:73
  67.1 1.1 collective-permute-done.20.refs_3_
  68.2 1.4 %shard_map.77.refs_8_ = bf16[8,800,128]{2,1,0:T(8,128)(2,1)S(1)} custom-call(bf16[800,625]{1,0:T(8,128)(2,1)S(1)} %copy-done.2, bf16[625,256]{1,0:T(8,128)(2,1)S(1)} %bitcast.25, bf16[625,256]{1,0:T(8,128)(2,1)S(1)} %collective-permute-done.3.refs_1_, bf16[625,256]{1,0:T(8,128)(2,1)S(1)} %collective-permute-done.16.refs_2_, ...), custom_call_target="tpu_custom_call" | custom-call | flops 1024000000 | bytes 2560000 | tf_op jit(solution)/shard_map/pallas_call | solution.py:104
  69.7 0.6 collective-permute-start.22
  70.2 0.1 copy.23.owners_ref
  70.3 0.1 copy.24.local_ref
  70.4 4.8 %collective-permute-done.22.refs_9_ = bf16[8,800,128]{2,1,0:T(8,128)(2,1)S(1)} collective-permute-done((bf16[8,800,128]{2,1,0:T(8,128)(2,1)S(1)}, bf16[8,800,128]{2,1,0:T(8,128)(2,1)S(1)}, u32[]{:S(2)}, u32[]{:S(2)}) %collective-permute-start.22) | collective-permute-done | bytes 1638432 | tf_op jit(solution)/shard_map/ppermute | solution.py:296
  75.2 0.0 collective-permute-done.19.refs_5_
  75.2 0.0 collective-permute-done.21.refs_7_
  75.2 9.3 %shard_map.79 = bf16[1,2,625,128]{3,2,1,0:T(8,128)(2,1)S(1)} custom-call(s32[1]{0:T(128)} %bitcast.column_ref, s32[32,3]{1,0:T(8,128)S(1)} %copy.23.owners_ref, s32[32,4]{1,0:T(8,128)S(1)} %copy.24.local_ref, bf16[2,1600,384]{2,1,0:T(8,128)(2,1)} %copy-done, bf16[2,1600,384]{2,1,0:T(8,128)(2,1)} %collective-permute-done.12.refs_1_, ...), custom_call_target="tpu_custom_call" | custom-call | flops 2936012800 | bytes 6553600 | tf_op jit(solution)/shard_map/pallas_call | solution.py:262
  84.5 0.1 collective-permute-start.24
  84.6 9.3 %shard_map.78 = bf16[1,2,625,128]{3,2,1,0:T(8,128)(2,1)S(1)} custom-call(s32[1]{0:T(128)} %bitcast.column_ref, s32[32,3]{1,0:T(8,128)S(1)} %copy.23.owners_ref, s32[32,4]{1,0:T(8,128)S(1)} %copy.24.local_ref, bf16[2,1600,384]{2,1,0:T(8,128)(2,1)} %copy-done, bf16[2,1600,384]{2,1,0:T(8,128)(2,1)} %collective-permute-done.12.refs_1_, ...), custom_call_target="tpu_custom_call" | custom-call | flops 2936012800 | bytes 6553600 | tf_op jit(solution)/shard_map/pallas_call | solution.py:262
  93.9 1.1 collective-permute-start.23
  94.9 9.3 %shard_map.80 = bf16[1,2,625,128]{3,2,1,0:T(8,128)(2,1)S(1)} custom-call(s32[1]{0:T(128)} %bitcast.column_ref, s32[32,3]{1,0:T(8,128)S(1)} %copy.23.owners_ref, s32[32,4]{1,0:T(8,128)S(1)} %copy.24.local_ref, bf16[2,1600,384]{2,1,0:T(8,128)(2,1)} %copy-done, bf16[2,1600,384]{2,1,0:T(8,128)(2,1)} %collective-permute-done.12.refs_1_, ...), custom_call_target="tpu_custom_call" | custom-call | flops 2936012800 | bytes 6553600 | tf_op jit(solution)/shard_map/pallas_call | solution.py:262
  104.2 0.0 copy-start.5
  104.2 1.3 %collective-permute-start.25 = (bf16[2,625,128]{2,1,0:T(8,128)(2,1)S(1)}, bf16[2,625,128]{2,1,0:T(8,128)(2,1)S(1)}, u32[]{:S(2)}, u32[]{:S(2)}) collective-permute-start(bf16[2,625,128]{2,1,0:T(8,128)(2,1)S(1)} %bitcast.28), channel_id=1, source_target_pairs={{0,2},{1,3},{2,4},{3,5},{4,6},{5,7},{6,0},{7,1},{8,10},{9,11},{10,... | collective-permute-start | bytes 960008 | tf_op jit(solution)/shard_map/ppermute | solution.py:299
  105.5 9.3 %shard_map.81 = bf16[1,2,625,128]{3,2,1,0:T(8,128)(2,1)S(1)} custom-call(s32[1]{0:T(128)} %bitcast.column_ref, s32[32,3]{1,0:T(8,128)S(1)} %copy.23.owners_ref, s32[32,4]{1,0:T(8,128)S(1)} %copy.24.local_ref, bf16[2,1600,384]{2,1,0:T(8,128)(2,1)} %copy-done, bf16[2,1600,384]{2,1,0:T(8,128)(2,1)} %collective-permute-done.12.refs_1_, ...), custom_call_target="tpu_custom_call" | custom-call | flops 2936012800 | bytes 6553600 | tf_op jit(solution)/shard_map/pallas_call | solution.py:262
  114.8 0.0 collective-permute-done.24
  114.8 0.0 collective-permute-done.23
  114.8 0.4 collective-permute-done.25
  115.2 0.2 fusion.1
  115.4 1.2 copy.32
  (21 shorter events, 0.1 us)
Async XLA Ops:
  1.3 18.0 %collective-permute-start.3 = (bf16[625,256]{1,0:T(8,128)(2,1)S(1)}, bf16[625,256]{1,0:T(8,128)(2,1)S(1)}, u32[]{:S(2)}, u32[]{:S(2)}) collective-permute-start(bf16[625,256]{1,0:T(8,128)(2,1)S(1)} %bitcast.24), channel_id=1, source_target_pairs={{0,2},{1,3},{2,4},{3,5},{4,6},{5,7},{6,0},{7,1},{8,10},{9,11},{10,... | collective-permute-start | bytes 960008 | tf_op jit(solution)/shard_map/ppermute | solution.py:299
  7.9 11.4 %collective-permute-start.2 = (bf16[2,96,625]{2,1,0:T(8,128)(2,1)S(1)}, bf16[2,96,625]{2,1,0:T(8,128)(2,1)S(1)}, u32[]{:S(2)}, u32[]{:S(2)}) collective-permute-start(bf16[2,96,625]{2,1,0:T(8,128)(2,1)S(1)} %get-tuple-element.63), channel_id=1, source_target_pairs={{0,2},{1,3},{2,4},{3,5},{4,6},{5,7},{6,0},{7,1},{8,10},{9,11},{10,... | collective-permute-start | bytes 720008 | tf_op jit(solution)/shard_map/ppermute | solution.py:299
  9.5 9.8 %collective-permute-start.1 = (bf16[2,96,625]{2,1,0:T(8,128)(2,1)S(1)}, bf16[2,96,625]{2,1,0:T(8,128)(2,1)S(1)}, u32[]{:S(2)}, u32[]{:S(2)}) collective-permute-start(bf16[2,96,625]{2,1,0:T(8,128)(2,1)S(1)} %get-tuple-element.33.refs_0_), channel_id=1, source_target_pairs={{0,16},{1,9},{2,18},{3,11},{4,20},{5,13},{6,22},{7,15},{8,24},{9,1... | collective-permute-start | bytes 720008 | tf_op jit(solution)/shard_map/ppermute | solution.py:310
  11.0 8.3 %collective-permute-start = (bf16[2,96,625]{2,1,0:T(8,128)(2,1)S(1)}, bf16[2,96,625]{2,1,0:T(8,128)(2,1)S(1)}, u32[]{:S(2)}, u32[]{:S(2)}) collective-permute-start(bf16[2,96,625]{2,1,0:T(8,128)(2,1)S(1)} %get-tuple-element.33.refs_0_), channel_id=1, source_target_pairs={{0,8},{1,17},{2,10},{3,19},{4,12},{5,21},{6,14},{7,23},{8,0},{9,25... | collective-permute-start | bytes 720008 | tf_op jit(solution)/shard_map/ppermute | solution.py:309
  19.3 8.9 %collective-permute-start.4 = (bf16[2,96,625]{2,1,0:T(8,128)(2,1)S(1)}, bf16[2,96,625]{2,1,0:T(8,128)(2,1)S(1)}, u32[]{:S(2)}, u32[]{:S(2)}) collective-permute-start(bf16[2,96,625]{2,1,0:T(8,128)(2,1)S(1)} %collective-permute-done.refs_1_), channel_id=1, source_target_pairs={{0,16},{1,9},{2,18},{3,11},{4,20},{5,13},{6,22},{7,15},{8,24},{9,1... | collective-permute-start | bytes 720008 | tf_op jit(solution)/shard_map/ppermute | solution.py:310
  20.9 11.8 %collective-permute-start.7 = (bf16[2,96,625]{2,1,0:T(8,128)(2,1)S(1)}, bf16[2,96,625]{2,1,0:T(8,128)(2,1)S(1)}, u32[]{:S(2)}, u32[]{:S(2)}) collective-permute-start(bf16[2,96,625]{2,1,0:T(8,128)(2,1)S(1)} %get-tuple-element.37), channel_id=1, source_target_pairs={{0,4},{1,5},{2,6},{3,7},{4,0},{5,1},{6,2},{7,3},{8,12},{9,13},{10,... | collective-permute-start | bytes 720008 | tf_op jit(solution)/shard_map/ppermute | solution.py:299
  21.6 11.1 %collective-permute-start.6 = (bf16[2,96,625]{2,1,0:T(8,128)(2,1)S(1)}, bf16[2,96,625]{2,1,0:T(8,128)(2,1)S(1)}, u32[]{:S(2)}, u32[]{:S(2)}) collective-permute-start(bf16[2,96,625]{2,1,0:T(8,128)(2,1)S(1)} %collective-permute-done.2.refs_0_), channel_id=1, source_target_pairs={{0,16},{1,9},{2,18},{3,11},{4,20},{5,13},{6,22},{7,15},{8,24},{9,1... | collective-permute-start | bytes 720008 | tf_op jit(solution)/shard_map/ppermute | solution.py:310
  22.1 10.6 %collective-permute-start.5 = (bf16[2,96,625]{2,1,0:T(8,128)(2,1)S(1)}, bf16[2,96,625]{2,1,0:T(8,128)(2,1)S(1)}, u32[]{:S(2)}, u32[]{:S(2)}) collective-permute-start(bf16[2,96,625]{2,1,0:T(8,128)(2,1)S(1)} %collective-permute-done.2.refs_0_), channel_id=1, source_target_pairs={{0,8},{1,17},{2,10},{3,19},{4,12},{5,21},{6,14},{7,23},{8,0},{9,25... | collective-permute-start | bytes 720008 | tf_op jit(solution)/shard_map/ppermute | solution.py:309
  28.2 1.6 %copy-start.3 = (bf16[1600,625]{1,0:T(8,128)(2,1)S(1)}, bf16[1600,625]{1,0:T(8,128)(2,1)}, u32[]{:S(2)}) copy-start(bf16[1600,625]{1,0:T(8,128)(2,1)} %constant.59.clone.refs_4_) | copy-start | bytes 6000004
  29.7 9.3 %copy-start.4 = (bf16[1600,625]{1,0:T(8,128)(2,1)S(1)}, bf16[1600,625]{1,0:T(8,128)(2,1)}, u32[]{:S(2)}) copy-start(bf16[1600,625]{1,0:T(8,128)(2,1)} %constant.59.clone.refs_4_) | copy-start | bytes 6000004
  32.4 9.3 %copy-start = (bf16[2,1600,384]{2,1,0:T(8,128)(2,1)}, bf16[2,1600,384]{2,1,0:T(8,128)(2,1)S(1)}, u32[]{:S(2)}) copy-start(bf16[2,1600,384]{2,1,0:T(8,128)(2,1)S(1)} %shard_map.73.refs_0_) | copy-start | bytes 7372804
  32.7 12.0 %collective-permute-start.12 = (bf16[2,1600,384]{2,1,0:T(8,128)(2,1)S(1)}, bf16[2,1600,384]{2,1,0:T(8,128)(2,1)}, u32[]{:S(2)}, u32[]{:S(2)}) collective-permute-start(bf16[2,1600,384]{2,1,0:T(8,128)(2,1)S(1)} %shard_map.73.refs_0_), channel_id=1, source_target_pairs={{0,1},{1,0},{2,3},{3,2},{4,5},{5,4},{6,7},{7,6},{8,9},{9,8},{10,11... | collective-permute-start | bytes 7372808 | tf_op jit(solution)/shard_map/ppermute | solution.py:296
  32.7 6.3 %collective-permute-start.8 = (bf16[2,96,625]{2,1,0:T(8,128)(2,1)S(1)}, bf16[2,96,625]{2,1,0:T(8,128)(2,1)S(1)}, u32[]{:S(2)}, u32[]{:S(2)}) collective-permute-start(bf16[2,96,625]{2,1,0:T(8,128)(2,1)S(1)} %collective-permute-done.5.refs_1_), channel_id=1, source_target_pairs={{0,16},{1,9},{2,18},{3,11},{4,20},{5,13},{6,22},{7,15},{8,24},{9,1... | collective-permute-start | bytes 720008 | tf_op jit(solution)/shard_map/ppermute | solution.py:310
  34.3 8.1 %collective-permute-start.11 = (bf16[2,96,625]{2,1,0:T(8,128)(2,1)S(1)}, bf16[2,96,625]{2,1,0:T(8,128)(2,1)S(1)}, u32[]{:S(2)}, u32[]{:S(2)}) collective-permute-start(bf16[2,96,625]{2,1,0:T(8,128)(2,1)S(1)} %get-tuple-element.43), channel_id=1, source_target_pairs={{0,6},{1,7},{2,0},{3,1},{4,2},{5,3},{6,4},{7,5},{8,14},{9,15},{10,... | collective-permute-start | bytes 720008 | tf_op jit(solution)/shard_map/ppermute | solution.py:299
  36.8 8.0 %collective-permute-start.10 = (bf16[2,96,625]{2,1,0:T(8,128)(2,1)S(1)}, bf16[2,96,625]{2,1,0:T(8,128)(2,1)S(1)}, u32[]{:S(2)}, u32[]{:S(2)}) collective-permute-start(bf16[2,96,625]{2,1,0:T(8,128)(2,1)S(1)} %collective-permute-done.7.refs_0_), channel_id=1, source_target_pairs={{0,16},{1,9},{2,18},{3,11},{4,20},{5,13},{6,22},{7,15},{8,24},{9,1... | collective-permute-start | bytes 720008 | tf_op jit(solution)/shard_map/ppermute | solution.py:310
  37.3 7.5 %collective-permute-start.9 = (bf16[2,96,625]{2,1,0:T(8,128)(2,1)S(1)}, bf16[2,96,625]{2,1,0:T(8,128)(2,1)S(1)}, u32[]{:S(2)}, u32[]{:S(2)}) collective-permute-start(bf16[2,96,625]{2,1,0:T(8,128)(2,1)S(1)} %collective-permute-done.7.refs_0_), channel_id=1, source_target_pairs={{0,8},{1,17},{2,10},{3,19},{4,12},{5,21},{6,14},{7,23},{8,0},{9,25... | collective-permute-start | bytes 720008 | tf_op jit(solution)/shard_map/ppermute | solution.py:309
  41.6 14.5 %copy-start.1 = (bf16[2,1600,384]{2,1,0:T(8,128)(2,1)}, bf16[2,1600,384]{2,1,0:T(8,128)(2,1)S(1)}, u32[]{:S(2)}) copy-start(bf16[2,1600,384]{2,1,0:T(8,128)(2,1)S(1)} %shard_map.74.refs_2_) | copy-start | bytes 7372804
  44.8 12.7 %collective-permute-start.17 = (bf16[2,1600,384]{2,1,0:T(8,128)(2,1)S(1)}, bf16[2,1600,384]{2,1,0:T(8,128)(2,1)}, u32[]{:S(2)}, u32[]{:S(2)}) collective-permute-start(bf16[2,1600,384]{2,1,0:T(8,128)(2,1)S(1)} %shard_map.74.refs_2_), channel_id=1, source_target_pairs={{0,1},{1,0},{2,3},{3,2},{4,5},{5,4},{6,7},{7,6},{8,9},{9,8},{10,11... | collective-permute-start | bytes 7372808 | tf_op jit(solution)/shard_map/ppermute | solution.py:296
  44.8 8.0 %collective-permute-start.13 = (bf16[2,96,625]{2,1,0:T(8,128)(2,1)S(1)}, bf16[2,96,625]{2,1,0:T(8,128)(2,1)S(1)}, u32[]{:S(2)}, u32[]{:S(2)}) collective-permute-start(bf16[2,96,625]{2,1,0:T(8,128)(2,1)S(1)} %collective-permute-done.9.refs_1_), channel_id=1, source_target_pairs={{0,16},{1,9},{2,18},{3,11},{4,20},{5,13},{6,22},{7,15},{8,24},{9,1... | collective-permute-start | bytes 720008 | tf_op jit(solution)/shard_map/ppermute | solution.py:310
  46.1 11.4 %collective-permute-start.16 = (bf16[625,256]{1,0:T(8,128)(2,1)S(1)}, bf16[625,256]{1,0:T(8,128)(2,1)S(1)}, u32[]{:S(2)}, u32[]{:S(2)}) collective-permute-start(bf16[625,256]{1,0:T(8,128)(2,1)S(1)} %collective-permute-done.3.refs_1_), channel_id=1, source_target_pairs={{0,2},{1,3},{2,4},{3,5},{4,6},{5,7},{6,0},{7,1},{8,10},{9,11},{10,... | collective-permute-start | bytes 960008 | tf_op jit(solution)/shard_map/ppermute | solution.py:299
  46.1 10.2 %collective-permute-start.15 = (bf16[2,96,625]{2,1,0:T(8,128)(2,1)S(1)}, bf16[2,96,625]{2,1,0:T(8,128)(2,1)S(1)}, u32[]{:S(2)}, u32[]{:S(2)}) collective-permute-start(bf16[2,96,625]{2,1,0:T(8,128)(2,1)S(1)} %collective-permute-done.11.refs_0_), channel_id=1, source_target_pairs={{0,16},{1,9},{2,18},{3,11},{4,20},{5,13},{6,22},{7,15},{8,24},{9,1... | collective-permute-start | bytes 720008 | tf_op jit(solution)/shard_map/ppermute | solution.py:310
  46.9 9.4 %collective-permute-start.14 = (bf16[2,96,625]{2,1,0:T(8,128)(2,1)S(1)}, bf16[2,96,625]{2,1,0:T(8,128)(2,1)S(1)}, u32[]{:S(2)}, u32[]{:S(2)}) collective-permute-start(bf16[2,96,625]{2,1,0:T(8,128)(2,1)S(1)} %collective-permute-done.11.refs_0_), channel_id=1, source_target_pairs={{0,8},{1,17},{2,10},{3,19},{4,12},{5,21},{6,14},{7,23},{8,0},{9,25... | collective-permute-start | bytes 720008 | tf_op jit(solution)/shard_map/ppermute | solution.py:309
  56.2 12.0 %copy-start.2 = (bf16[800,625]{1,0:T(8,128)(2,1)S(1)}, bf16[800,625]{1,0:T(8,128)(2,1)}, u32[]{:S(2)}) copy-start(bf16[800,625]{1,0:T(8,128)(2,1)} %constant.60.clone.matrix_ref) | copy-start | bytes 3000004
  57.5 6.2 %collective-permute-start.18 = (bf16[2,96,625]{2,1,0:T(8,128)(2,1)S(1)}, bf16[2,96,625]{2,1,0:T(8,128)(2,1)S(1)}, u32[]{:S(2)}, u32[]{:S(2)}) collective-permute-start(bf16[2,96,625]{2,1,0:T(8,128)(2,1)S(1)} %collective-permute-done.14.refs_1_), channel_id=1, source_target_pairs={{0,16},{1,9},{2,18},{3,11},{4,20},{5,13},{6,22},{7,15},{8,24},{9,1... | collective-permute-start | bytes 720008 | tf_op jit(solution)/shard_map/ppermute | solution.py:310
  58.8 9.4 %collective-permute-start.20 = (bf16[625,256]{1,0:T(8,128)(2,1)S(1)}, bf16[625,256]{1,0:T(8,128)(2,1)S(1)}, u32[]{:S(2)}, u32[]{:S(2)}) collective-permute-start(bf16[625,256]{1,0:T(8,128)(2,1)S(1)} %collective-permute-done.16.refs_2_), channel_id=1, source_target_pairs={{0,2},{1,3},{2,4},{3,5},{4,6},{5,7},{6,0},{7,1},{8,10},{9,11},{10,... | collective-permute-start | bytes 960008 | tf_op jit(solution)/shard_map/ppermute | solution.py:299
  63.6 11.6 %collective-permute-start.19 = (bf16[2,1600,384]{2,1,0:T(8,128)(2,1)}, bf16[2,1600,384]{2,1,0:T(8,128)(2,1)}, u32[]{:S(2)}, u32[]{:S(2)}) collective-permute-start(bf16[2,1600,384]{2,1,0:T(8,128)(2,1)} %shard_map.75.refs_4_), channel_id=1, source_target_pairs={{0,1},{1,0},{2,3},{3,2},{4,5},{5,4},{6,7},{7,6},{8,9},{9,8},{10,11... | collective-permute-start | bytes 7372808 | tf_op jit(solution)/shard_map/ppermute | solution.py:296
  67.1 3.1 %copy-start.6 = (s32[32,3]{0,1:T(4,128)S(1)}, s32[32,3]{0,1:T(4,128)}, u32[]{:S(2)}) copy-start(s32[32,3]{0,1:T(4,128)} %param.10) | copy-start | bytes 1156
  67.1 3.2 %copy-start.7 = (s32[32,4]{0,1:T(4,128)S(1)}, s32[32,4]{0,1:T(4,128)}, u32[]{:S(2)}) copy-start(s32[32,4]{0,1:T(4,128)} %param.11) | copy-start | bytes 1540
  68.2 7.0 %collective-permute-start.21 = (bf16[2,1600,384]{2,1,0:T(8,128)(2,1)}, bf16[2,1600,384]{2,1,0:T(8,128)(2,1)}, u32[]{:S(2)}, u32[]{:S(2)}) collective-permute-start(bf16[2,1600,384]{2,1,0:T(8,128)(2,1)} %shard_map.76.refs_6_), channel_id=1, source_target_pairs={{0,1},{1,0},{2,3},{3,2},{4,5},{5,4},{6,7},{7,6},{8,9},{9,8},{10,11... | collective-permute-start | bytes 7372808 | tf_op jit(solution)/shard_map/ppermute | solution.py:296
  69.7 5.6 %collective-permute-start.22 = (bf16[8,800,128]{2,1,0:T(8,128)(2,1)S(1)}, bf16[8,800,128]{2,1,0:T(8,128)(2,1)S(1)}, u32[]{:S(2)}, u32[]{:S(2)}) collective-permute-start(bf16[8,800,128]{2,1,0:T(8,128)(2,1)S(1)} %shard_map.77.refs_8_), channel_id=1, source_target_pairs={{0,1},{1,0},{2,3},{3,2},{4,5},{5,4},{6,7},{7,6},{8,9},{9,8},{10,11... | collective-permute-start | bytes 4915208 | tf_op jit(solution)/shard_map/ppermute | solution.py:296
  84.5 30.3 %collective-permute-start.24 = (bf16[2,625,128]{2,1,0:T(8,128)(2,1)S(1)}, bf16[2,625,128]{2,1,0:T(8,128)(2,1)S(1)}, u32[]{:S(2)}, u32[]{:S(2)}) collective-permute-start(bf16[2,625,128]{2,1,0:T(8,128)(2,1)S(1)} %bitcast.26), channel_id=1, source_target_pairs={{0,4},{1,5},{2,6},{3,7},{4,0},{5,1},{6,2},{7,3},{8,12},{9,13},{10,... | collective-permute-start | bytes 960008 | tf_op jit(solution)/shard_map/ppermute | solution.py:299
  93.9 20.9 %collective-permute-start.23 = (bf16[2,625,128]{2,1,0:T(8,128)(2,1)S(1)}, bf16[2,625,128]{2,1,0:T(8,128)(2,1)S(1)}, u32[]{:S(2)}, u32[]{:S(2)}) collective-permute-start(bf16[2,625,128]{2,1,0:T(8,128)(2,1)S(1)} %bitcast.27), channel_id=1, source_target_pairs={{0,6},{1,7},{2,0},{3,1},{4,2},{5,3},{6,4},{7,5},{8,14},{9,15},{10,... | collective-permute-start | bytes 960008 | tf_op jit(solution)/shard_map/ppermute | solution.py:299
  104.2 11.0 %copy-start.5 = (f32[2,128,625]{1,0,2:T(2,128)S(1)}, f32[2,128,625]{1,0,2:T(2,128)}, u32[]{:S(2)}) copy-start(f32[2,128,625]{1,0,2:T(2,128)} %param.9) | copy-start | bytes 1920004
  104.2 11.0 %collective-permute-start.25 = (bf16[2,625,128]{2,1,0:T(8,128)(2,1)S(1)}, bf16[2,625,128]{2,1,0:T(8,128)(2,1)S(1)}, u32[]{:S(2)}, u32[]{:S(2)}) collective-permute-start(bf16[2,625,128]{2,1,0:T(8,128)(2,1)S(1)} %bitcast.28), channel_id=1, source_target_pairs={{0,2},{1,3},{2,4},{3,5},{4,6},{5,7},{6,0},{7,1},{8,10},{9,11},{10,... | collective-permute-start | bytes 960008 | tf_op jit(solution)/shard_map/ppermute | solution.py:299

commit v23 on v22

--- a/solution.py
+++ b/solution.py
@@ -21,7 +21,7 @@
 PREPARE_STEPS = 2
 BF = jnp.bfloat16
 F32 = jnp.float32
-VMEM_BYTES = 48 * 1024 * 1024
+VMEM_BYTES = 32 * 1024 * 1024
 LADDER_VMEM_BYTES = 50 * 1024 * 1024
 
 

time: 117 us -> 117 us (level)
    unnamed x21 -> x25, local copies, waits for them, and re-layouts: 6.38 us -> 6.39 us
where the time goes in v23:
time: 117 us
  Pallas kernels  50.7 us (43%)
  waiting for transfers between devices  32.9 us (28%)
  starting transfers between devices  24.9 us (21%)
  local copies, waits for them, and re-layouts  7.69 us (7%)
    pallas_call x4, Pallas kernels, ladders(): pl.pallas_call(functools.partial(ladder_kernel, find, made, len(tiles)),...  37.1 us
    ppermute x8, waiting for transfers between devices, per_device(): second_side = lambda x: lax.ppermute(x, ('pair', 'task'), sides[1])  17.6 us
    pallas_call x4, Pallas kernels, prepare(): pl.pallas_call(prepare_kernel, out_shape=jax.ShapeDtypeStruct((count, mat...  12.2 us
    ppermute x9, waiting for transfers between devices, around(): lax.ppermute(x, 'task', [(c, (c + 2 * by) % task_count) for c in range(ta...  10.5 us
    ppermute x9, starting transfers between devices, around(): lax.ppermute(x, 'task', [(c, (c + 2 * by) % task_count) for c in range(ta...  10.3 us
    ppermute x8, starting transfers between devices, per_device(): second_side = lambda x: lax.ppermute(x, ('pair', 'task'), sides[1])  9.12 us
    unnamed x25, local copies, waits for them, and re-layouts  6.39 us
    ppermute x5, waiting for transfers between devices, per_device(): lax.ppermute(x, 'task', [(c, c ^ 1) for c in range(task_count)])  4.82 us
  transfers between devices with their start and end apart: 26, of which 13 were waited for; matrix products, arithmetic and copies ran while one was open for 3% of the time, Pallas kernels for 36%

profile of v23, /device:TPU:0, one launch (start us, length us, event | category | flops | bytes accessed | tf_op | source)
XLA Modules:
  0.0 116.6 jit_solution(7967011541730325857)
XLA Ops:
  0.0 1.2 %pad = bf16[632,2,128]{2,1,0:T(2,128)(2,1)S(1)} pad(bf16[625,2,128]{2,1,0:T(2,128)(2,1)} %bitcast.31, bf16[]{:T(256)} %constant.64), padding=0_7x0_0x0_0 | pad | bytes 643586
  1.3 3.1 %collective-permute-start.3 = (bf16[625,256]{1,0:T(8,128)(2,1)S(1)}, bf16[625,256]{1,0:T(8,128)(2,1)S(1)}, u32[]{:S(2)}, u32[]{:S(2)}) collective-permute-start(bf16[625,256]{1,0:T(8,128)(2,1)S(1)} %bitcast.24), channel_id=1, source_target_pairs={{0,2},{1,3},{2,4},{3,5},{4,6},{5,7},{6,0},{7,1},{8,10},{9,11},{10,... | collective-permute-start | bytes 960008 | tf_op jit(solution)/shard_map/ppermute | solution.py:299
  4.4 3.3 %copy.22 = bf16[2,384,625]{2,1,0:T(8,128)(2,1)S(1)} copy(bf16[2,384,625]{1,0,2:T(2,128)(2,1)} %param.7) | data formatting | bytes 1920000 | tf_op args[0]
  7.7 0.1 dynamic-slice_bitcast_fusion
  7.9 1.6 %collective-permute-start.2 = (bf16[2,96,625]{2,1,0:T(8,128)(2,1)S(1)}, bf16[2,96,625]{2,1,0:T(8,128)(2,1)S(1)}, u32[]{:S(2)}, u32[]{:S(2)}) collective-permute-start(bf16[2,96,625]{2,1,0:T(8,128)(2,1)S(1)} %get-tuple-element.63), channel_id=1, source_target_pairs={{0,2},{1,3},{2,4},{3,5},{4,6},{5,7},{6,0},{7,1},{8,10},{9,11},{10,... | collective-permute-start | bytes 720008 | tf_op jit(solution)/shard_map/ppermute | solution.py:299
  9.5 1.5 %collective-permute-start.1 = (bf16[2,96,625]{2,1,0:T(8,128)(2,1)S(1)}, bf16[2,96,625]{2,1,0:T(8,128)(2,1)S(1)}, u32[]{:S(2)}, u32[]{:S(2)}) collective-permute-start(bf16[2,96,625]{2,1,0:T(8,128)(2,1)S(1)} %get-tuple-element.33.refs_0_), channel_id=1, source_target_pairs={{0,16},{1,9},{2,18},{3,11},{4,20},{5,13},{6,22},{7,15},{8,24},{9,1... | collective-permute-start | bytes 720008 | tf_op jit(solution)/shard_map/ppermute | solution.py:310
  11.0 1.5 %collective-permute-start = (bf16[2,96,625]{2,1,0:T(8,128)(2,1)S(1)}, bf16[2,96,625]{2,1,0:T(8,128)(2,1)S(1)}, u32[]{:S(2)}, u32[]{:S(2)}) collective-permute-start(bf16[2,96,625]{2,1,0:T(8,128)(2,1)S(1)} %get-tuple-element.33.refs_0_), channel_id=1, source_target_pairs={{0,8},{1,17},{2,10},{3,19},{4,12},{5,21},{6,14},{7,23},{8,0},{9,25... | collective-permute-start | bytes 720008 | tf_op jit(solution)/shard_map/ppermute | solution.py:309
  12.5 6.8 %collective-permute-done.2.refs_0_ = bf16[2,96,625]{2,1,0:T(8,128)(2,1)S(1)} collective-permute-done((bf16[2,96,625]{2,1,0:T(8,128)(2,1)S(1)}, bf16[2,96,625]{2,1,0:T(8,128)(2,1)S(1)}, u32[]{:S(2)}, u32[]{:S(2)}) %collective-permute-start.2) | collective-permute-done | bytes 240032 | tf_op jit(solution)/shard_map/ppermute | solution.py:299
  19.3 0.0 collective-permute-done.1.refs_2_
  19.3 0.0 collective-permute-done.refs_1_
  19.3 0.0 collective-permute-done.3.refs_1_
  19.3 1.6 %collective-permute-start.4 = (bf16[2,96,625]{2,1,0:T(8,128)(2,1)S(1)}, bf16[2,96,625]{2,1,0:T(8,128)(2,1)S(1)}, u32[]{:S(2)}, u32[]{:S(2)}) collective-permute-start(bf16[2,96,625]{2,1,0:T(8,128)(2,1)S(1)} %collective-permute-done.refs_1_), channel_id=1, source_target_pairs={{0,16},{1,9},{2,18},{3,11},{4,20},{5,13},{6,22},{7,15},{8,24},{9,1... | collective-permute-start | bytes 720008 | tf_op jit(solution)/shard_map/ppermute | solution.py:310
  20.9 0.7 collective-permute-start.7
  21.6 0.5 collective-permute-start.6
  22.1 1.5 %collective-permute-start.5 = (bf16[2,96,625]{2,1,0:T(8,128)(2,1)S(1)}, bf16[2,96,625]{2,1,0:T(8,128)(2,1)S(1)}, u32[]{:S(2)}, u32[]{:S(2)}) collective-permute-start(bf16[2,96,625]{2,1,0:T(8,128)(2,1)S(1)} %collective-permute-done.2.refs_0_), channel_id=1, source_target_pairs={{0,8},{1,17},{2,10},{3,19},{4,12},{5,21},{6,14},{7,23},{8,0},{9,25... | collective-permute-start | bytes 720008 | tf_op jit(solution)/shard_map/ppermute | solution.py:309
  23.6 4.6 %collective-permute-done.4.refs_3_ = bf16[2,96,625]{2,1,0:T(8,128)(2,1)S(1)} collective-permute-done((bf16[2,96,625]{2,1,0:T(8,128)(2,1)S(1)}, bf16[2,96,625]{2,1,0:T(8,128)(2,1)S(1)}, u32[]{:S(2)}, u32[]{:S(2)}) %collective-permute-start.4) | collective-permute-done | bytes 240032 | tf_op jit(solution)/shard_map/ppermute | solution.py:310
  28.2 1.6 %copy-done.3 = bf16[1600,625]{1,0:T(8,128)(2,1)S(1)} copy-done((bf16[1600,625]{1,0:T(8,128)(2,1)S(1)}, bf16[1600,625]{1,0:T(8,128)(2,1)}, u32[]{:S(2)}) %copy-start.3) | copy-done | bytes 2000024
  29.7 2.6 %shard_map.73.refs_0_ = bf16[2,1600,384]{2,1,0:T(8,128)(2,1)S(1)} custom-call(s32[1]{0:T(128)} %bitcast.column_ref, bf16[2,96,625]{2,1,0:T(8,128)(2,1)S(1)} %get-tuple-element.33.refs_0_, bf16[2,96,625]{2,1,0:T(8,128)(2,1)S(1)} %collective-permute-done.refs_1_, bf16[2,96,625]{2,1,0:T(8,128)(2,1)S(1)} %collective-permute-done.1.refs_2_, ...), custom_call_target="tpu_custom_call" | custom-call | flops 1536000000 | bytes 3417600 | tf_op jit(solution)/shard_map/pallas_call | solution.py:73
  32.4 0.3 collective-permute-done.7.refs_0_
  32.7 0.0 collective-permute-done.6.refs_2_
  32.7 0.0 collective-permute-start.12
  32.7 1.6 %collective-permute-start.8 = (bf16[2,96,625]{2,1,0:T(8,128)(2,1)S(1)}, bf16[2,96,625]{2,1,0:T(8,128)(2,1)S(1)}, u32[]{:S(2)}, u32[]{:S(2)}) collective-permute-start(bf16[2,96,625]{2,1,0:T(8,128)(2,1)S(1)} %collective-permute-done.5.refs_1_), channel_id=1, source_target_pairs={{0,16},{1,9},{2,18},{3,11},{4,20},{5,13},{6,22},{7,15},{8,24},{9,1... | collective-permute-start | bytes 720008 | tf_op jit(solution)/shard_map/ppermute | solution.py:310
  34.3 2.5 %collective-permute-start.11 = (bf16[2,96,625]{2,1,0:T(8,128)(2,1)S(1)}, bf16[2,96,625]{2,1,0:T(8,128)(2,1)S(1)}, u32[]{:S(2)}, u32[]{:S(2)}) collective-permute-start(bf16[2,96,625]{2,1,0:T(8,128)(2,1)S(1)} %get-tuple-element.43), channel_id=1, source_target_pairs={{0,6},{1,7},{2,0},{3,1},{4,2},{5,3},{6,4},{7,5},{8,14},{9,15},{10,... | collective-permute-start | bytes 720008 | tf_op jit(solution)/shard_map/ppermute | solution.py:299
  36.8 0.5 collective-permute-start.10
  37.3 0.6 collective-permute-start.9
  37.9 1.0 collective-permute-done.8.refs_3_
  39.0 2.6 %shard_map.74.refs_2_ = bf16[2,1600,384]{2,1,0:T(8,128)(2,1)S(1)} custom-call(s32[1]{0:T(128)} %bitcast.column_ref, bf16[2,96,625]{2,1,0:T(8,128)(2,1)S(1)} %collective-permute-done.2.refs_0_, bf16[2,96,625]{2,1,0:T(8,128)(2,1)S(1)} %collective-permute-done.5.refs_1_, bf16[2,96,625]{2,1,0:T(8,128)(2,1)S(1)} %collective-permute-done.6.refs_2_, ...), custom_call_target="tpu_custom_call" | custom-call | flops 1536000000 | bytes 3417600 | tf_op jit(solution)/shard_map/pallas_call | solution.py:73
  41.7 0.8 collective-permute-done.11.refs_0_
  42.4 2.3 %collective-permute-done.10.refs_2_ = bf16[2,96,625]{2,1,0:T(8,128)(2,1)S(1)} collective-permute-done((bf16[2,96,625]{2,1,0:T(8,128)(2,1)S(1)}, bf16[2,96,625]{2,1,0:T(8,128)(2,1)S(1)}, u32[]{:S(2)}, u32[]{:S(2)}) %collective-permute-start.10) | collective-permute-done | bytes 240032 | tf_op jit(solution)/shard_map/ppermute | solution.py:310
  44.7 0.0 collective-permute-done.9.refs_1_
  44.7 0.0 collective-permute-done.12.refs_1_
  44.8 0.1 collective-permute-start.17
  44.8 1.3 %collective-permute-start.13 = (bf16[2,96,625]{2,1,0:T(8,128)(2,1)S(1)}, bf16[2,96,625]{2,1,0:T(8,128)(2,1)S(1)}, u32[]{:S(2)}, u32[]{:S(2)}) collective-permute-start(bf16[2,96,625]{2,1,0:T(8,128)(2,1)S(1)} %collective-permute-done.9.refs_1_), channel_id=1, source_target_pairs={{0,16},{1,9},{2,18},{3,11},{4,20},{5,13},{6,22},{7,15},{8,24},{9,1... | collective-permute-start | bytes 720008 | tf_op jit(solution)/shard_map/ppermute | solution.py:310
  46.1 0.8 collective-permute-start.15
  46.9 1.2 %collective-permute-start.14 = (bf16[2,96,625]{2,1,0:T(8,128)(2,1)S(1)}, bf16[2,96,625]{2,1,0:T(8,128)(2,1)S(1)}, u32[]{:S(2)}, u32[]{:S(2)}) collective-permute-start(bf16[2,96,625]{2,1,0:T(8,128)(2,1)S(1)} %collective-permute-done.11.refs_0_), channel_id=1, source_target_pairs={{0,8},{1,17},{2,10},{3,19},{4,12},{5,21},{6,14},{7,23},{8,0},{9,25... | collective-permute-start | bytes 720008 | tf_op jit(solution)/shard_map/ppermute | solution.py:309
  48.1 4.7 %collective-permute-done.13.refs_3_ = bf16[2,96,625]{2,1,0:T(8,128)(2,1)S(1)} collective-permute-done((bf16[2,96,625]{2,1,0:T(8,128)(2,1)S(1)}, bf16[2,96,625]{2,1,0:T(8,128)(2,1)S(1)}, u32[]{:S(2)}, u32[]{:S(2)}) %collective-permute-start.13) | collective-permute-done | bytes 240032 | tf_op jit(solution)/shard_map/ppermute | solution.py:310
  52.8 3.4 %shard_map.75.refs_4_ = bf16[2,1600,384]{2,1,0:T(8,128)(2,1)} custom-call(s32[1]{0:T(128)} %bitcast.column_ref, bf16[2,96,625]{2,1,0:T(8,128)(2,1)S(1)} %collective-permute-done.7.refs_0_, bf16[2,96,625]{2,1,0:T(8,128)(2,1)S(1)} %collective-permute-done.9.refs_1_, bf16[2,96,625]{2,1,0:T(8,128)(2,1)S(1)} %collective-permute-done.10.refs_2_, ...), custom_call_target="tpu_custom_call" | custom-call | flops 1536000000 | bytes 3417600 | tf_op jit(solution)/shard_map/pallas_call | solution.py:73
  56.3 0.1 collective-permute-done.15.refs_2_
  56.4 1.1 collective-permute-done.16.refs_2_
  57.5 1.3 %collective-permute-start.18 = (bf16[2,96,625]{2,1,0:T(8,128)(2,1)S(1)}, bf16[2,96,625]{2,1,0:T(8,128)(2,1)S(1)}, u32[]{:S(2)}, u32[]{:S(2)}) collective-permute-start(bf16[2,96,625]{2,1,0:T(8,128)(2,1)S(1)} %collective-permute-done.14.refs_1_), channel_id=1, source_target_pairs={{0,16},{1,9},{2,18},{3,11},{4,20},{5,13},{6,22},{7,15},{8,24},{9,1... | collective-permute-start | bytes 720008 | tf_op jit(solution)/shard_map/ppermute | solution.py:310
  58.9 4.9 %collective-permute-done.18.refs_3_ = bf16[2,96,625]{2,1,0:T(8,128)(2,1)S(1)} collective-permute-done((bf16[2,96,625]{2,1,0:T(8,128)(2,1)S(1)}, bf16[2,96,625]{2,1,0:T(8,128)(2,1)S(1)}, u32[]{:S(2)}, u32[]{:S(2)}) %collective-permute-start.18) | collective-permute-done | bytes 240032 | tf_op jit(solution)/shard_map/ppermute | solution.py:310
  63.7 0.0 collective-permute-start.19
  63.7 3.5 %shard_map.76.refs_6_ = bf16[2,1600,384]{2,1,0:T(8,128)(2,1)} custom-call(s32[1]{0:T(128)} %bitcast.column_ref, bf16[2,96,625]{2,1,0:T(8,128)(2,1)S(1)} %collective-permute-done.11.refs_0_, bf16[2,96,625]{2,1,0:T(8,128)(2,1)S(1)} %collective-permute-done.14.refs_1_, bf16[2,96,625]{2,1,0:T(8,128)(2,1)S(1)} %collective-permute-done.15.refs_2_, ...), custom_call_target="tpu_custom_call" | custom-call | flops 1536000000 | bytes 3417600 | tf_op jit(solution)/shard_map/pallas_call | solution.py:73
  67.2 1.1 collective-permute-done.20.refs_3_
  68.3 0.0 collective-permute-start.21
  68.3 1.4 %shard_map.77.refs_8_ = bf16[8,800,128]{2,1,0:T(8,128)(2,1)S(1)} custom-call(bf16[800,625]{1,0:T(8,128)(2,1)S(1)} %copy-done.2, bf16[625,256]{1,0:T(8,128)(2,1)S(1)} %bitcast.25, bf16[625,256]{1,0:T(8,128)(2,1)S(1)} %collective-permute-done.3.refs_1_, bf16[625,256]{1,0:T(8,128)(2,1)S(1)} %collective-permute-done.16.refs_2_, ...), custom_call_target="tpu_custom_call" | custom-call | flops 1024000000 | bytes 2560000 | tf_op jit(solution)/shard_map/pallas_call | solution.py:104
  69.7 0.6 collective-permute-start.22
  70.3 0.1 copy.23.owners_ref
  70.4 0.1 copy.24.local_ref
  70.5 4.8 %collective-permute-done.22.refs_9_ = bf16[8,800,128]{2,1,0:T(8,128)(2,1)S(1)} collective-permute-done((bf16[8,800,128]{2,1,0:T(8,128)(2,1)S(1)}, bf16[8,800,128]{2,1,0:T(8,128)(2,1)S(1)}, u32[]{:S(2)}, u32[]{:S(2)}) %collective-permute-start.22) | collective-permute-done | bytes 1638432 | tf_op jit(solution)/shard_map/ppermute | solution.py:296
  75.3 0.0 collective-permute-done.19.refs_5_
  75.3 0.0 collective-permute-done.21.refs_7_
  75.3 9.3 %shard_map.79 = bf16[1,2,625,128]{3,2,1,0:T(8,128)(2,1)S(1)} custom-call(s32[1]{0:T(128)} %bitcast.column_ref, s32[32,3]{1,0:T(8,128)S(1)} %copy.23.owners_ref, s32[32,4]{1,0:T(8,128)S(1)} %copy.24.local_ref, bf16[2,1600,384]{2,1,0:T(8,128)(2,1)} %copy-done, bf16[2,1600,384]{2,1,0:T(8,128)(2,1)} %copy-done.5, bf16[2,1600,384]{2,1,0:T(8,128)(2,1)} %copy-done.1, ...), custom_call_target="tpu_custom_call" | custom-call | flops 2936012800 | bytes 6553600 | tf_op jit(solution)/shard_map/pallas_call | solution.py:262
  84.6 0.1 collective-permute-start.24
  84.7 9.3 %shard_map.78 = bf16[1,2,625,128]{3,2,1,0:T(8,128)(2,1)S(1)} custom-call(s32[1]{0:T(128)} %bitcast.column_ref, s32[32,3]{1,0:T(8,128)S(1)} %copy.23.owners_ref, s32[32,4]{1,0:T(8,128)S(1)} %copy.24.local_ref, bf16[2,1600,384]{2,1,0:T(8,128)(2,1)} %copy-done, bf16[2,1600,384]{2,1,0:T(8,128)(2,1)} %copy-done.5, bf16[2,1600,384]{2,1,0:T(8,128)(2,1)} %copy-done.1, ...), custom_call_target="tpu_custom_call" | custom-call | flops 2936012800 | bytes 6553600 | tf_op jit(solution)/shard_map/pallas_call | solution.py:262
  93.9 1.1 collective-permute-start.23
  95.0 9.3 %shard_map.80 = bf16[1,2,625,128]{3,2,1,0:T(8,128)(2,1)S(1)} custom-call(s32[1]{0:T(128)} %bitcast.column_ref, s32[32,3]{1,0:T(8,128)S(1)} %copy.23.owners_ref, s32[32,4]{1,0:T(8,128)S(1)} %copy.24.local_ref, bf16[2,1600,384]{2,1,0:T(8,128)(2,1)} %copy-done, bf16[2,1600,384]{2,1,0:T(8,128)(2,1)} %copy-done.5, bf16[2,1600,384]{2,1,0:T(8,128)(2,1)} %copy-done.1, ...), custom_call_target="tpu_custom_call" | custom-call | flops 2936012800 | bytes 6553600 | tf_op jit(solution)/shard_map/pallas_call | solution.py:262
  104.3 0.0 copy-start.7
  104.3 1.2 %collective-permute-start.25 = (bf16[2,625,128]{2,1,0:T(8,128)(2,1)S(1)}, bf16[2,625,128]{2,1,0:T(8,128)(2,1)S(1)}, u32[]{:S(2)}, u32[]{:S(2)}) collective-permute-start(bf16[2,625,128]{2,1,0:T(8,128)(2,1)S(1)} %bitcast.28), channel_id=1, source_target_pairs={{0,2},{1,3},{2,4},{3,5},{4,6},{5,7},{6,0},{7,1},{8,10},{9,11},{10,... | collective-permute-start | bytes 960008 | tf_op jit(solution)/shard_map/ppermute | solution.py:299
  105.5 9.3 %shard_map.81 = bf16[1,2,625,128]{3,2,1,0:T(8,128)(2,1)S(1)} custom-call(s32[1]{0:T(128)} %bitcast.column_ref, s32[32,3]{1,0:T(8,128)S(1)} %copy.23.owners_ref, s32[32,4]{1,0:T(8,128)S(1)} %copy.24.local_ref, bf16[2,1600,384]{2,1,0:T(8,128)(2,1)} %copy-done, bf16[2,1600,384]{2,1,0:T(8,128)(2,1)} %copy-done.5, bf16[2,1600,384]{2,1,0:T(8,128)(2,1)} %copy-done.1, ...), custom_call_target="tpu_custom_call" | custom-call | flops 2936012800 | bytes 6553600 | tf_op jit(solution)/shard_map/pallas_call | solution.py:262
  114.8 0.0 collective-permute-done.24
  114.8 0.4 collective-permute-done.25
  115.3 0.2 fusion.1
  115.5 1.2 copy.32
  (25 shorter events, 0.1 us)
Async XLA Ops:
  1.3 18.0 %collective-permute-start.3 = (bf16[625,256]{1,0:T(8,128)(2,1)S(1)}, bf16[625,256]{1,0:T(8,128)(2,1)S(1)}, u32[]{:S(2)}, u32[]{:S(2)}) collective-permute-start(bf16[625,256]{1,0:T(8,128)(2,1)S(1)} %bitcast.24), channel_id=1, source_target_pairs={{0,2},{1,3},{2,4},{3,5},{4,6},{5,7},{6,0},{7,1},{8,10},{9,11},{10,... | collective-permute-start | bytes 960008 | tf_op jit(solution)/shard_map/ppermute | solution.py:299
  7.9 11.4 %collective-permute-start.2 = (bf16[2,96,625]{2,1,0:T(8,128)(2,1)S(1)}, bf16[2,96,625]{2,1,0:T(8,128)(2,1)S(1)}, u32[]{:S(2)}, u32[]{:S(2)}) collective-permute-start(bf16[2,96,625]{2,1,0:T(8,128)(2,1)S(1)} %get-tuple-element.63), channel_id=1, source_target_pairs={{0,2},{1,3},{2,4},{3,5},{4,6},{5,7},{6,0},{7,1},{8,10},{9,11},{10,... | collective-permute-start | bytes 720008 | tf_op jit(solution)/shard_map/ppermute | solution.py:299
  9.5 9.8 %collective-permute-start.1 = (bf16[2,96,625]{2,1,0:T(8,128)(2,1)S(1)}, bf16[2,96,625]{2,1,0:T(8,128)(2,1)S(1)}, u32[]{:S(2)}, u32[]{:S(2)}) collective-permute-start(bf16[2,96,625]{2,1,0:T(8,128)(2,1)S(1)} %get-tuple-element.33.refs_0_), channel_id=1, source_target_pairs={{0,16},{1,9},{2,18},{3,11},{4,20},{5,13},{6,22},{7,15},{8,24},{9,1... | collective-permute-start | bytes 720008 | tf_op jit(solution)/shard_map/ppermute | solution.py:310
  11.0 8.3 %collective-permute-start = (bf16[2,96,625]{2,1,0:T(8,128)(2,1)S(1)}, bf16[2,96,625]{2,1,0:T(8,128)(2,1)S(1)}, u32[]{:S(2)}, u32[]{:S(2)}) collective-permute-start(bf16[2,96,625]{2,1,0:T(8,128)(2,1)S(1)} %get-tuple-element.33.refs_0_), channel_id=1, source_target_pairs={{0,8},{1,17},{2,10},{3,19},{4,12},{5,21},{6,14},{7,23},{8,0},{9,25... | collective-permute-start | bytes 720008 | tf_op jit(solution)/shard_map/ppermute | solution.py:309
  19.3 8.9 %collective-permute-start.4 = (bf16[2,96,625]{2,1,0:T(8,128)(2,1)S(1)}, bf16[2,96,625]{2,1,0:T(8,128)(2,1)S(1)}, u32[]{:S(2)}, u32[]{:S(2)}) collective-permute-start(bf16[2,96,625]{2,1,0:T(8,128)(2,1)S(1)} %collective-permute-done.refs_1_), channel_id=1, source_target_pairs={{0,16},{1,9},{2,18},{3,11},{4,20},{5,13},{6,22},{7,15},{8,24},{9,1... | collective-permute-start | bytes 720008 | tf_op jit(solution)/shard_map/ppermute | solution.py:310
  20.9 11.8 %collective-permute-start.7 = (bf16[2,96,625]{2,1,0:T(8,128)(2,1)S(1)}, bf16[2,96,625]{2,1,0:T(8,128)(2,1)S(1)}, u32[]{:S(2)}, u32[]{:S(2)}) collective-permute-start(bf16[2,96,625]{2,1,0:T(8,128)(2,1)S(1)} %get-tuple-element.37), channel_id=1, source_target_pairs={{0,4},{1,5},{2,6},{3,7},{4,0},{5,1},{6,2},{7,3},{8,12},{9,13},{10,... | collective-permute-start | bytes 720008 | tf_op jit(solution)/shard_map/ppermute | solution.py:299
  21.6 11.1 %collective-permute-start.6 = (bf16[2,96,625]{2,1,0:T(8,128)(2,1)S(1)}, bf16[2,96,625]{2,1,0:T(8,128)(2,1)S(1)}, u32[]{:S(2)}, u32[]{:S(2)}) collective-permute-start(bf16[2,96,625]{2,1,0:T(8,128)(2,1)S(1)} %collective-permute-done.2.refs_0_), channel_id=1, source_target_pairs={{0,16},{1,9},{2,18},{3,11},{4,20},{5,13},{6,22},{7,15},{8,24},{9,1... | collective-permute-start | bytes 720008 | tf_op jit(solution)/shard_map/ppermute | solution.py:310
  22.1 10.6 %collective-permute-start.5 = (bf16[2,96,625]{2,1,0:T(8,128)(2,1)S(1)}, bf16[2,96,625]{2,1,0:T(8,128)(2,1)S(1)}, u32[]{:S(2)}, u32[]{:S(2)}) collective-permute-start(bf16[2,96,625]{2,1,0:T(8,128)(2,1)S(1)} %collective-permute-done.2.refs_0_), channel_id=1, source_target_pairs={{0,8},{1,17},{2,10},{3,19},{4,12},{5,21},{6,14},{7,23},{8,0},{9,25... | collective-permute-start | bytes 720008 | tf_op jit(solution)/shard_map/ppermute | solution.py:309
  28.2 1.6 %copy-start.3 = (bf16[1600,625]{1,0:T(8,128)(2,1)S(1)}, bf16[1600,625]{1,0:T(8,128)(2,1)}, u32[]{:S(2)}) copy-start(bf16[1600,625]{1,0:T(8,128)(2,1)} %constant.59.clone.refs_4_) | copy-start | bytes 6000004
  29.7 9.3 %copy-start.4 = (bf16[1600,625]{1,0:T(8,128)(2,1)S(1)}, bf16[1600,625]{1,0:T(8,128)(2,1)}, u32[]{:S(2)}) copy-start(bf16[1600,625]{1,0:T(8,128)(2,1)} %constant.59.clone.refs_4_) | copy-start | bytes 6000004
  32.4 9.3 %copy-start = (bf16[2,1600,384]{2,1,0:T(8,128)(2,1)}, bf16[2,1600,384]{2,1,0:T(8,128)(2,1)S(1)}, u32[]{:S(2)}) copy-start(bf16[2,1600,384]{2,1,0:T(8,128)(2,1)S(1)} %shard_map.73.refs_0_) | copy-start | bytes 7372804
  32.7 12.0 %collective-permute-start.12 = (bf16[2,1600,384]{2,1,0:T(8,128)(2,1)S(1)}, bf16[2,1600,384]{2,1,0:T(8,128)(2,1)S(1)}, u32[]{:S(2)}, u32[]{:S(2)}) collective-permute-start(bf16[2,1600,384]{2,1,0:T(8,128)(2,1)S(1)} %shard_map.73.refs_0_), channel_id=1, source_target_pairs={{0,1},{1,0},{2,3},{3,2},{4,5},{5,4},{6,7},{7,6},{8,9},{9,8},{10,11... | collective-permute-start | bytes 7372808 | tf_op jit(solution)/shard_map/ppermute | solution.py:296
  32.7 6.3 %collective-permute-start.8 = (bf16[2,96,625]{2,1,0:T(8,128)(2,1)S(1)}, bf16[2,96,625]{2,1,0:T(8,128)(2,1)S(1)}, u32[]{:S(2)}, u32[]{:S(2)}) collective-permute-start(bf16[2,96,625]{2,1,0:T(8,128)(2,1)S(1)} %collective-permute-done.5.refs_1_), channel_id=1, source_target_pairs={{0,16},{1,9},{2,18},{3,11},{4,20},{5,13},{6,22},{7,15},{8,24},{9,1... | collective-permute-start | bytes 720008 | tf_op jit(solution)/shard_map/ppermute | solution.py:310
  34.3 8.1 %collective-permute-start.11 = (bf16[2,96,625]{2,1,0:T(8,128)(2,1)S(1)}, bf16[2,96,625]{2,1,0:T(8,128)(2,1)S(1)}, u32[]{:S(2)}, u32[]{:S(2)}) collective-permute-start(bf16[2,96,625]{2,1,0:T(8,128)(2,1)S(1)} %get-tuple-element.43), channel_id=1, source_target_pairs={{0,6},{1,7},{2,0},{3,1},{4,2},{5,3},{6,4},{7,5},{8,14},{9,15},{10,... | collective-permute-start | bytes 720008 | tf_op jit(solution)/shard_map/ppermute | solution.py:299
  36.8 8.0 %collective-permute-start.10 = (bf16[2,96,625]{2,1,0:T(8,128)(2,1)S(1)}, bf16[2,96,625]{2,1,0:T(8,128)(2,1)S(1)}, u32[]{:S(2)}, u32[]{:S(2)}) collective-permute-start(bf16[2,96,625]{2,1,0:T(8,128)(2,1)S(1)} %collective-permute-done.7.refs_0_), channel_id=1, source_target_pairs={{0,16},{1,9},{2,18},{3,11},{4,20},{5,13},{6,22},{7,15},{8,24},{9,1... | collective-permute-start | bytes 720008 | tf_op jit(solution)/shard_map/ppermute | solution.py:310
  37.3 7.5 %collective-permute-start.9 = (bf16[2,96,625]{2,1,0:T(8,128)(2,1)S(1)}, bf16[2,96,625]{2,1,0:T(8,128)(2,1)S(1)}, u32[]{:S(2)}, u32[]{:S(2)}) collective-permute-start(bf16[2,96,625]{2,1,0:T(8,128)(2,1)S(1)} %collective-permute-done.7.refs_0_), channel_id=1, source_target_pairs={{0,8},{1,17},{2,10},{3,19},{4,12},{5,21},{6,14},{7,23},{8,0},{9,25... | collective-permute-start | bytes 720008 | tf_op jit(solution)/shard_map/ppermute | solution.py:309
  41.6 14.6 %copy-start.1 = (bf16[2,1600,384]{2,1,0:T(8,128)(2,1)}, bf16[2,1600,384]{2,1,0:T(8,128)(2,1)S(1)}, u32[]{:S(2)}) copy-start(bf16[2,1600,384]{2,1,0:T(8,128)(2,1)S(1)} %shard_map.74.refs_2_) | copy-start | bytes 7372804
  44.8 11.5 %copy-start.5 = (bf16[2,1600,384]{2,1,0:T(8,128)(2,1)}, bf16[2,1600,384]{2,1,0:T(8,128)(2,1)S(1)}, u32[]{:S(2)}) copy-start(bf16[2,1600,384]{2,1,0:T(8,128)(2,1)S(1)} %collective-permute-done.12.refs_1_) | copy-start | bytes 7372804
  44.8 12.8 %collective-permute-start.17 = (bf16[2,1600,384]{2,1,0:T(8,128)(2,1)S(1)}, bf16[2,1600,384]{2,1,0:T(8,128)(2,1)S(1)}, u32[]{:S(2)}, u32[]{:S(2)}) collective-permute-start(bf16[2,1600,384]{2,1,0:T(8,128)(2,1)S(1)} %shard_map.74.refs_2_), channel_id=1, source_target_pairs={{0,1},{1,0},{2,3},{3,2},{4,5},{5,4},{6,7},{7,6},{8,9},{9,8},{10,11... | collective-permute-start | bytes 7372808 | tf_op jit(solution)/shard_map/ppermute | solution.py:296
  44.8 8.0 %collective-permute-start.13 = (bf16[2,96,625]{2,1,0:T(8,128)(2,1)S(1)}, bf16[2,96,625]{2,1,0:T(8,128)(2,1)S(1)}, u32[]{:S(2)}, u32[]{:S(2)}) collective-permute-start(bf16[2,96,625]{2,1,0:T(8,128)(2,1)S(1)} %collective-permute-done.9.refs_1_), channel_id=1, source_target_pairs={{0,16},{1,9},{2,18},{3,11},{4,20},{5,13},{6,22},{7,15},{8,24},{9,1... | collective-permute-start | bytes 720008 | tf_op jit(solution)/shard_map/ppermute | solution.py:310
  46.1 11.4 %collective-permute-start.16 = (bf16[625,256]{1,0:T(8,128)(2,1)S(1)}, bf16[625,256]{1,0:T(8,128)(2,1)S(1)}, u32[]{:S(2)}, u32[]{:S(2)}) collective-permute-start(bf16[625,256]{1,0:T(8,128)(2,1)S(1)} %collective-permute-done.3.refs_1_), channel_id=1, source_target_pairs={{0,2},{1,3},{2,4},{3,5},{4,6},{5,7},{6,0},{7,1},{8,10},{9,11},{10,... | collective-permute-start | bytes 960008 | tf_op jit(solution)/shard_map/ppermute | solution.py:299
  46.1 10.2 %collective-permute-start.15 = (bf16[2,96,625]{2,1,0:T(8,128)(2,1)S(1)}, bf16[2,96,625]{2,1,0:T(8,128)(2,1)S(1)}, u32[]{:S(2)}, u32[]{:S(2)}) collective-permute-start(bf16[2,96,625]{2,1,0:T(8,128)(2,1)S(1)} %collective-permute-done.11.refs_0_), channel_id=1, source_target_pairs={{0,16},{1,9},{2,18},{3,11},{4,20},{5,13},{6,22},{7,15},{8,24},{9,1... | collective-permute-start | bytes 720008 | tf_op jit(solution)/shard_map/ppermute | solution.py:310
  46.9 9.4 %collective-permute-start.14 = (bf16[2,96,625]{2,1,0:T(8,128)(2,1)S(1)}, bf16[2,96,625]{2,1,0:T(8,128)(2,1)S(1)}, u32[]{:S(2)}, u32[]{:S(2)}) collective-permute-start(bf16[2,96,625]{2,1,0:T(8,128)(2,1)S(1)} %collective-permute-done.11.refs_0_), channel_id=1, source_target_pairs={{0,8},{1,17},{2,10},{3,19},{4,12},{5,21},{6,14},{7,23},{8,0},{9,25... | collective-permute-start | bytes 720008 | tf_op jit(solution)/shard_map/ppermute | solution.py:309
  56.3 12.0 %copy-start.2 = (bf16[800,625]{1,0:T(8,128)(2,1)S(1)}, bf16[800,625]{1,0:T(8,128)(2,1)}, u32[]{:S(2)}) copy-start(bf16[800,625]{1,0:T(8,128)(2,1)} %constant.60.clone.matrix_ref) | copy-start | bytes 3000004
  57.5 9.7 %copy-start.6 = (bf16[2,1600,384]{2,1,0:T(8,128)(2,1)}, bf16[2,1600,384]{2,1,0:T(8,128)(2,1)S(1)}, u32[]{:S(2)}) copy-start(bf16[2,1600,384]{2,1,0:T(8,128)(2,1)S(1)} %collective-permute-done.17.refs_3_) | copy-start | bytes 7372804
  57.5 6.2 %collective-permute-start.18 = (bf16[2,96,625]{2,1,0:T(8,128)(2,1)S(1)}, bf16[2,96,625]{2,1,0:T(8,128)(2,1)S(1)}, u32[]{:S(2)}, u32[]{:S(2)}) collective-permute-start(bf16[2,96,625]{2,1,0:T(8,128)(2,1)S(1)} %collective-permute-done.14.refs_1_), channel_id=1, source_target_pairs={{0,16},{1,9},{2,18},{3,11},{4,20},{5,13},{6,22},{7,15},{8,24},{9,1... | collective-permute-start | bytes 720008 | tf_op jit(solution)/shard_map/ppermute | solution.py:310
  58.9 9.4 %collective-permute-start.20 = (bf16[625,256]{1,0:T(8,128)(2,1)S(1)}, bf16[625,256]{1,0:T(8,128)(2,1)S(1)}, u32[]{:S(2)}, u32[]{:S(2)}) collective-permute-start(bf16[625,256]{1,0:T(8,128)(2,1)S(1)} %collective-permute-done.16.refs_2_), channel_id=1, source_target_pairs={{0,2},{1,3},{2,4},{3,5},{4,6},{5,7},{6,0},{7,1},{8,10},{9,11},{10,... | collective-permute-start | bytes 960008 | tf_op jit(solution)/shard_map/ppermute | solution.py:299
  63.7 11.6 %collective-permute-start.19 = (bf16[2,1600,384]{2,1,0:T(8,128)(2,1)}, bf16[2,1600,384]{2,1,0:T(8,128)(2,1)}, u32[]{:S(2)}, u32[]{:S(2)}) collective-permute-start(bf16[2,1600,384]{2,1,0:T(8,128)(2,1)} %shard_map.75.refs_4_), channel_id=1, source_target_pairs={{0,1},{1,0},{2,3},{3,2},{4,5},{5,4},{6,7},{7,6},{8,9},{9,8},{10,11... | collective-permute-start | bytes 7372808 | tf_op jit(solution)/shard_map/ppermute | solution.py:296
  67.2 3.1 %copy-start.8 = (s32[32,3]{0,1:T(4,128)S(1)}, s32[32,3]{0,1:T(4,128)}, u32[]{:S(2)}) copy-start(s32[32,3]{0,1:T(4,128)} %param.10) | copy-start | bytes 1156
  67.2 3.2 %copy-start.9 = (s32[32,4]{0,1:T(4,128)S(1)}, s32[32,4]{0,1:T(4,128)}, u32[]{:S(2)}) copy-start(s32[32,4]{0,1:T(4,128)} %param.11) | copy-start | bytes 1540
  68.3 7.0 %collective-permute-start.21 = (bf16[2,1600,384]{2,1,0:T(8,128)(2,1)}, bf16[2,1600,384]{2,1,0:T(8,128)(2,1)}, u32[]{:S(2)}, u32[]{:S(2)}) collective-permute-start(bf16[2,1600,384]{2,1,0:T(8,128)(2,1)} %shard_map.76.refs_6_), channel_id=1, source_target_pairs={{0,1},{1,0},{2,3},{3,2},{4,5},{5,4},{6,7},{7,6},{8,9},{9,8},{10,11... | collective-permute-start | bytes 7372808 | tf_op jit(solution)/shard_map/ppermute | solution.py:296
  69.7 5.6 %collective-permute-start.22 = (bf16[8,800,128]{2,1,0:T(8,128)(2,1)S(1)}, bf16[8,800,128]{2,1,0:T(8,128)(2,1)S(1)}, u32[]{:S(2)}, u32[]{:S(2)}) collective-permute-start(bf16[8,800,128]{2,1,0:T(8,128)(2,1)S(1)} %shard_map.77.refs_8_), channel_id=1, source_target_pairs={{0,1},{1,0},{2,3},{3,2},{4,5},{5,4},{6,7},{7,6},{8,9},{9,8},{10,11... | collective-permute-start | bytes 4915208 | tf_op jit(solution)/shard_map/ppermute | solution.py:296
  84.6 30.2 %collective-permute-start.24 = (bf16[2,625,128]{2,1,0:T(8,128)(2,1)S(1)}, bf16[2,625,128]{2,1,0:T(8,128)(2,1)S(1)}, u32[]{:S(2)}, u32[]{:S(2)}) collective-permute-start(bf16[2,625,128]{2,1,0:T(8,128)(2,1)S(1)} %bitcast.26), channel_id=1, source_target_pairs={{0,4},{1,5},{2,6},{3,7},{4,0},{5,1},{6,2},{7,3},{8,12},{9,13},{10,... | collective-permute-start | bytes 960008 | tf_op jit(solution)/shard_map/ppermute | solution.py:299
  93.9 20.9 %collective-permute-start.23 = (bf16[2,625,128]{2,1,0:T(8,128)(2,1)S(1)}, bf16[2,625,128]{2,1,0:T(8,128)(2,1)S(1)}, u32[]{:S(2)}, u32[]{:S(2)}) collective-permute-start(bf16[2,625,128]{2,1,0:T(8,128)(2,1)S(1)} %bitcast.27), channel_id=1, source_target_pairs={{0,6},{1,7},{2,0},{3,1},{4,2},{5,3},{6,4},{7,5},{8,14},{9,15},{10,... | collective-permute-start | bytes 960008 | tf_op jit(solution)/shard_map/ppermute | solution.py:299
  104.3 11.0 %copy-start.7 = (f32[2,128,625]{1,0,2:T(2,128)S(1)}, f32[2,128,625]{1,0,2:T(2,128)}, u32[]{:S(2)}) copy-start(f32[2,128,625]{1,0,2:T(2,128)} %param.9) | copy-start | bytes 1920004
  104.3 10.9 %collective-permute-start.25 = (bf16[2,625,128]{2,1,0:T(8,128)(2,1)S(1)}, bf16[2,625,128]{2,1,0:T(8,128)(2,1)S(1)}, u32[]{:S(2)}, u32[]{:S(2)}) collective-permute-start(bf16[2,625,128]{2,1,0:T(8,128)(2,1)S(1)} %bitcast.28), channel_id=1, source_target_pairs={{0,2},{1,3},{2,4},{3,5},{4,6},{5,7},{6,0},{7,1},{8,10},{9,11},{10,... | collective-permute-start | bytes 960008 | tf_op jit(solution)/shard_map/ppermute | solution.py:299

commit v24 on v22

--- a/solution.py
+++ b/solution.py
@@ -320,12 +320,12 @@
 
         forms0, part1, a1, b1, part2, to3 = after((forms0, part1, a1, b1, part2, mine[3]), ())
         q1, a2, b2, part3 = second_side(a1), first_side(part2), second_side(part2), around(to3, 3)
-        far0 = other_core(forms0)
+        far0 = other_core(after(forms0, q1))
         forms1 = made_forms(part1, a1, b1, q1)
 
         forms1, part2, a2, b2, part3, amp1, far0 = after((forms1, part2, a2, b2, part3, amp1, far0), ())
         q2, a3, b3, amp2 = second_side(a2), first_side(part3), second_side(part3), around(amp1, 1)
-        far1 = other_core(forms1)
+        far1 = other_core(after(forms1, q2))
         forms2 = made_forms(part2, a2, b2, q2)
 
         forms2, part3, a3, b3, amp2, far1 = after((forms2, part3, a3, b3, amp2, far1), ())

time: 117 us -> 128 us (1.094)
  waiting for transfers between devices: 32.9 us -> 42.7 us
  starting transfers between devices: 24.8 us -> 26.3 us
    ppermute x8, waiting for transfers between devices: 17.6 us -> 24.3 us  [per_device(): second_side = lambda x: lax.ppermute(x, ('pair', 'task'), sides[1])]
    ppermute x9, waiting for transfers between devices: 10.6 us -> 13.6 us  [around(): lax.ppermute(x, 'task', [(c, (c + 2 * by) % task_count) for c in range(ta...]
    ppermute x8, starting transfers between devices: 9.13 us -> 10.9 us  [per_device(): second_side = lambda x: lax.ppermute(x, ('pair', 'task'), sides[1])]
  transfers between devices with their start and end apart: 26 -> 26, of which waited for: 13 -> 13; matrix products, arithmetic and copies ran while one was open for 3% -> 3% of each run, Pallas kernels for 36% -> 32%
where the time goes in v24:
time: 128 us
  Pallas kernels  50.7 us (40%)
  waiting for transfers between devices  42.7 us (33%)
  starting transfers between devices  26.3 us (21%)
  local copies, waits for them, and re-layouts  7.68 us (6%)
    pallas_call x4, Pallas kernels, ladders(): pl.pallas_call(functools.partial(ladder_kernel, find, made, len(tiles)),...  37.1 us
    ppermute x8, waiting for transfers between devices, per_device(): second_side = lambda x: lax.ppermute(x, ('pair', 'task'), sides[1])  24.3 us
    ppermute x9, waiting for transfers between devices, around(): lax.ppermute(x, 'task', [(c, (c + 2 * by) % task_count) for c in range(ta...  13.6 us
    pallas_call x4, Pallas kernels, prepare(): pl.pallas_call(prepare_kernel, out_shape=jax.ShapeDtypeStruct((count, mat...  12.2 us
    ppermute x8, starting transfers between devices, per_device(): second_side = lambda x: lax.ppermute(x, ('pair', 'task'), sides[1])  10.9 us
    ppermute x9, starting transfers between devices, around(): lax.ppermute(x, 'task', [(c, (c + 2 * by) % task_count) for c in range(ta...  10.3 us
    unnamed x21, local copies, waits for them, and re-layouts  6.38 us
    ppermute x5, waiting for transfers between devices, per_device(): lax.ppermute(x, 'task', [(c, c ^ 1) for c in range(task_count)])  4.82 us
  transfers between devices with their start and end apart: 26, of which 13 were waited for; matrix products, arithmetic and copies ran while one was open for 3% of the time, Pallas kernels for 32%

profile of v24, /device:TPU:0, one launch (start us, length us, event | category | flops | bytes accessed | tf_op | source)
XLA Modules:
  0.0 127.8 jit_solution(6384496184528806217)
XLA Ops:
  0.0 1.2 pad
  1.3 3.1 %collective-permute-start.3 = (bf16[625,256]{1,0:T(8,128)(2,1)S(1)}, bf16[625,256]{1,0:T(8,128)(2,1)S(1)}, u32[]{:S(2)}, u32[]{:S(2)}) collective-permute-start(bf16[625,256]{1,0:T(8,128)(2,1)S(1)} %bitcast.24), channel_id=1, source_target_pairs={{0,2},{1,3},{2,4},{3,5},{4,6},{5,7},{6,0},{7,1},{8,10},{9,11},{10,... | collective-permute-start | bytes 960008 | tf_op jit(solution)/shard_map/ppermute | solution.py:299
  4.4 3.3 %copy.22 = bf16[2,384,625]{2,1,0:T(8,128)(2,1)S(1)} copy(bf16[2,384,625]{1,0,2:T(2,128)(2,1)} %param.7) | data formatting | bytes 1920000 | tf_op args[0]
  7.7 0.1 dynamic-slice_bitcast_fusion
  7.9 1.6 %collective-permute-start.2 = (bf16[2,96,625]{2,1,0:T(8,128)(2,1)S(1)}, bf16[2,96,625]{2,1,0:T(8,128)(2,1)S(1)}, u32[]{:S(2)}, u32[]{:S(2)}) collective-permute-start(bf16[2,96,625]{2,1,0:T(8,128)(2,1)S(1)} %get-tuple-element.67), channel_id=1, source_target_pairs={{0,2},{1,3},{2,4},{3,5},{4,6},{5,7},{6,0},{7,1},{8,10},{9,11},{10,... | collective-permute-start | bytes 720008 | tf_op jit(solution)/shard_map/ppermute | solution.py:299
  9.5 1.5 %collective-permute-start.1 = (bf16[2,96,625]{2,1,0:T(8,128)(2,1)S(1)}, bf16[2,96,625]{2,1,0:T(8,128)(2,1)S(1)}, u32[]{:S(2)}, u32[]{:S(2)}) collective-permute-start(bf16[2,96,625]{2,1,0:T(8,128)(2,1)S(1)} %get-tuple-element.35.refs_0_), channel_id=1, source_target_pairs={{0,16},{1,9},{2,18},{3,11},{4,20},{5,13},{6,22},{7,15},{8,24},{9,1... | collective-permute-start | bytes 720008 | tf_op jit(solution)/shard_map/ppermute | solution.py:310
  11.0 1.5 %collective-permute-start = (bf16[2,96,625]{2,1,0:T(8,128)(2,1)S(1)}, bf16[2,96,625]{2,1,0:T(8,128)(2,1)S(1)}, u32[]{:S(2)}, u32[]{:S(2)}) collective-permute-start(bf16[2,96,625]{2,1,0:T(8,128)(2,1)S(1)} %get-tuple-element.35.refs_0_), channel_id=1, source_target_pairs={{0,8},{1,17},{2,10},{3,19},{4,12},{5,21},{6,14},{7,23},{8,0},{9,25... | collective-permute-start | bytes 720008 | tf_op jit(solution)/shard_map/ppermute | solution.py:309
  12.5 6.8 %collective-permute-done.2.refs_0_ = bf16[2,96,625]{2,1,0:T(8,128)(2,1)S(1)} collective-permute-done((bf16[2,96,625]{2,1,0:T(8,128)(2,1)S(1)}, bf16[2,96,625]{2,1,0:T(8,128)(2,1)S(1)}, u32[]{:S(2)}, u32[]{:S(2)}) %collective-permute-start.2) | collective-permute-done | bytes 240032 | tf_op jit(solution)/shard_map/ppermute | solution.py:299
  19.3 0.0 collective-permute-done.1.refs_2_
  19.3 0.0 collective-permute-done.refs_1_
  19.3 0.0 collective-permute-done.3.refs_1_
  19.3 1.6 %collective-permute-start.4 = (bf16[2,96,625]{2,1,0:T(8,128)(2,1)S(1)}, bf16[2,96,625]{2,1,0:T(8,128)(2,1)S(1)}, u32[]{:S(2)}, u32[]{:S(2)}) collective-permute-start(bf16[2,96,625]{2,1,0:T(8,128)(2,1)S(1)} %collective-permute-done.refs_1_), channel_id=1, source_target_pairs={{0,16},{1,9},{2,18},{3,11},{4,20},{5,13},{6,22},{7,15},{8,24},{9,1... | collective-permute-start | bytes 720008 | tf_op jit(solution)/shard_map/ppermute | solution.py:310
  20.9 0.7 collective-permute-start.7
  21.6 0.5 collective-permute-start.6
  22.1 1.5 %collective-permute-start.5 = (bf16[2,96,625]{2,1,0:T(8,128)(2,1)S(1)}, bf16[2,96,625]{2,1,0:T(8,128)(2,1)S(1)}, u32[]{:S(2)}, u32[]{:S(2)}) collective-permute-start(bf16[2,96,625]{2,1,0:T(8,128)(2,1)S(1)} %collective-permute-done.2.refs_0_), channel_id=1, source_target_pairs={{0,8},{1,17},{2,10},{3,19},{4,12},{5,21},{6,14},{7,23},{8,0},{9,25... | collective-permute-start | bytes 720008 | tf_op jit(solution)/shard_map/ppermute | solution.py:309
  23.6 4.6 %collective-permute-done.4.refs_3_ = bf16[2,96,625]{2,1,0:T(8,128)(2,1)S(1)} collective-permute-done((bf16[2,96,625]{2,1,0:T(8,128)(2,1)S(1)}, bf16[2,96,625]{2,1,0:T(8,128)(2,1)S(1)}, u32[]{:S(2)}, u32[]{:S(2)}) %collective-permute-start.4) | collective-permute-done | bytes 240032 | tf_op jit(solution)/shard_map/ppermute | solution.py:310
  28.2 1.6 %copy-done.3 = bf16[1600,625]{1,0:T(8,128)(2,1)S(1)} copy-done((bf16[1600,625]{1,0:T(8,128)(2,1)S(1)}, bf16[1600,625]{1,0:T(8,128)(2,1)}, u32[]{:S(2)}) %copy-start.3) | copy-done | bytes 2000024
  29.7 2.6 %shard_map.73.refs_0_ = bf16[2,1600,384]{2,1,0:T(8,128)(2,1)S(1)} custom-call(s32[1]{0:T(128)} %bitcast.column_ref, bf16[2,96,625]{2,1,0:T(8,128)(2,1)S(1)} %get-tuple-element.35.refs_0_, bf16[2,96,625]{2,1,0:T(8,128)(2,1)S(1)} %collective-permute-done.refs_1_, bf16[2,96,625]{2,1,0:T(8,128)(2,1)S(1)} %collective-permute-done.1.refs_2_, ...), custom_call_target="tpu_custom_call" | custom-call | flops 1536000000 | bytes 3417600 | tf_op jit(solution)/shard_map/pallas_call | solution.py:73
  32.4 0.3 collective-permute-done.7.refs_0_
  32.7 1.5 %collective-permute-start.8 = (bf16[2,96,625]{2,1,0:T(8,128)(2,1)S(1)}, bf16[2,96,625]{2,1,0:T(8,128)(2,1)S(1)}, u32[]{:S(2)}, u32[]{:S(2)}) collective-permute-start(bf16[2,96,625]{2,1,0:T(8,128)(2,1)S(1)} %collective-permute-done.5.refs_1_), channel_id=1, source_target_pairs={{0,16},{1,9},{2,18},{3,11},{4,20},{5,13},{6,22},{7,15},{8,24},{9,1... | collective-permute-start | bytes 720008 | tf_op jit(solution)/shard_map/ppermute | solution.py:310
  34.2 4.7 %collective-permute-done.8.refs_3_ = bf16[2,96,625]{2,1,0:T(8,128)(2,1)S(1)} collective-permute-done((bf16[2,96,625]{2,1,0:T(8,128)(2,1)S(1)}, bf16[2,96,625]{2,1,0:T(8,128)(2,1)S(1)}, u32[]{:S(2)}, u32[]{:S(2)}) %collective-permute-start.8) | collective-permute-done | bytes 240032 | tf_op jit(solution)/shard_map/ppermute | solution.py:310
  38.9 0.0 collective-permute-start.12
  38.9 2.5 %collective-permute-start.11 = (bf16[2,96,625]{2,1,0:T(8,128)(2,1)S(1)}, bf16[2,96,625]{2,1,0:T(8,128)(2,1)S(1)}, u32[]{:S(2)}, u32[]{:S(2)}) collective-permute-start(bf16[2,96,625]{2,1,0:T(8,128)(2,1)S(1)} %get-tuple-element.45), channel_id=1, source_target_pairs={{0,6},{1,7},{2,0},{3,1},{4,2},{5,3},{6,4},{7,5},{8,14},{9,15},{10,... | collective-permute-start | bytes 720008 | tf_op jit(solution)/shard_map/ppermute | solution.py:299
  41.4 1.5 %collective-permute-start.10 = (bf16[2,96,625]{2,1,0:T(8,128)(2,1)S(1)}, bf16[2,96,625]{2,1,0:T(8,128)(2,1)S(1)}, u32[]{:S(2)}, u32[]{:S(2)}) collective-permute-start(bf16[2,96,625]{2,1,0:T(8,128)(2,1)S(1)} %collective-permute-done.7.refs_0_), channel_id=1, source_target_pairs={{0,16},{1,9},{2,18},{3,11},{4,20},{5,13},{6,22},{7,15},{8,24},{9,1... | collective-permute-start | bytes 720008 | tf_op jit(solution)/shard_map/ppermute | solution.py:310
  42.9 0.5 collective-permute-start.9
  43.5 2.6 %shard_map.74.refs_2_ = bf16[2,1600,384]{2,1,0:T(8,128)(2,1)S(1)} custom-call(s32[1]{0:T(128)} %bitcast.column_ref, bf16[2,96,625]{2,1,0:T(8,128)(2,1)S(1)} %collective-permute-done.2.refs_0_, bf16[2,96,625]{2,1,0:T(8,128)(2,1)S(1)} %collective-permute-done.5.refs_1_, bf16[2,96,625]{2,1,0:T(8,128)(2,1)S(1)} %collective-permute-done.6.refs_2_, ...), custom_call_target="tpu_custom_call" | custom-call | flops 1536000000 | bytes 3417600 | tf_op jit(solution)/shard_map/pallas_call | solution.py:73
  46.1 1.2 collective-permute-done.11.refs_0_
  47.3 2.6 %collective-permute-done.10.refs_2_ = bf16[2,96,625]{2,1,0:T(8,128)(2,1)S(1)} collective-permute-done((bf16[2,96,625]{2,1,0:T(8,128)(2,1)S(1)}, bf16[2,96,625]{2,1,0:T(8,128)(2,1)S(1)}, u32[]{:S(2)}, u32[]{:S(2)}) %collective-permute-start.10) | collective-permute-done | bytes 240032 | tf_op jit(solution)/shard_map/ppermute | solution.py:310
  49.8 1.4 %collective-permute-start.13 = (bf16[2,96,625]{2,1,0:T(8,128)(2,1)S(1)}, bf16[2,96,625]{2,1,0:T(8,128)(2,1)S(1)}, u32[]{:S(2)}, u32[]{:S(2)}) collective-permute-start(bf16[2,96,625]{2,1,0:T(8,128)(2,1)S(1)} %collective-permute-done.9.refs_1_), channel_id=1, source_target_pairs={{0,16},{1,9},{2,18},{3,11},{4,20},{5,13},{6,22},{7,15},{8,24},{9,1... | collective-permute-start | bytes 720008 | tf_op jit(solution)/shard_map/ppermute | solution.py:310
  51.3 4.8 %collective-permute-done.13.refs_3_ = bf16[2,96,625]{2,1,0:T(8,128)(2,1)S(1)} collective-permute-done((bf16[2,96,625]{2,1,0:T(8,128)(2,1)S(1)}, bf16[2,96,625]{2,1,0:T(8,128)(2,1)S(1)}, u32[]{:S(2)}, u32[]{:S(2)}) %collective-permute-start.13) | collective-permute-done | bytes 240032 | tf_op jit(solution)/shard_map/ppermute | solution.py:310
  56.0 0.0 collective-permute-start.17
  56.1 0.0 collective-permute-start.16
  56.1 1.4 %collective-permute-start.15 = (bf16[2,96,625]{2,1,0:T(8,128)(2,1)S(1)}, bf16[2,96,625]{2,1,0:T(8,128)(2,1)S(1)}, u32[]{:S(2)}, u32[]{:S(2)}) collective-permute-start(bf16[2,96,625]{2,1,0:T(8,128)(2,1)S(1)} %collective-permute-done.11.refs_0_), channel_id=1, source_target_pairs={{0,16},{1,9},{2,18},{3,11},{4,20},{5,13},{6,22},{7,15},{8,24},{9,1... | collective-permute-start | bytes 720008 | tf_op jit(solution)/shard_map/ppermute | solution.py:310
  57.5 1.0 collective-permute-start.14
  58.5 3.5 %shard_map.75.refs_4_ = bf16[2,1600,384]{2,1,0:T(8,128)(2,1)} custom-call(s32[1]{0:T(128)} %bitcast.column_ref, bf16[2,96,625]{2,1,0:T(8,128)(2,1)S(1)} %collective-permute-done.7.refs_0_, bf16[2,96,625]{2,1,0:T(8,128)(2,1)S(1)} %collective-permute-done.9.refs_1_, bf16[2,96,625]{2,1,0:T(8,128)(2,1)S(1)} %collective-permute-done.10.refs_2_, ...), custom_call_target="tpu_custom_call" | custom-call | flops 1536000000 | bytes 3417600 | tf_op jit(solution)/shard_map/pallas_call | solution.py:73
  62.0 2.9 %collective-permute-done.15.refs_2_ = bf16[2,96,625]{2,1,0:T(8,128)(2,1)S(1)} collective-permute-done((bf16[2,96,625]{2,1,0:T(8,128)(2,1)S(1)}, bf16[2,96,625]{2,1,0:T(8,128)(2,1)S(1)}, u32[]{:S(2)}, u32[]{:S(2)}) %collective-permute-start.15) | collective-permute-done | bytes 240032 | tf_op jit(solution)/shard_map/ppermute | solution.py:310
  64.9 0.0 collective-permute-done.14.refs_1_
  64.9 3.0 %collective-permute-done.16.refs_2_ = bf16[625,256]{1,0:T(8,128)(2,1)S(1)} collective-permute-done((bf16[625,256]{1,0:T(8,128)(2,1)S(1)}, bf16[625,256]{1,0:T(8,128)(2,1)S(1)}, u32[]{:S(2)}, u32[]{:S(2)}) %collective-permute-start.16) | collective-permute-done | bytes 320032 | tf_op jit(solution)/shard_map/ppermute | solution.py:299
  67.9 0.0 collective-permute-done.17.refs_3_
  67.9 1.4 %collective-permute-start.18 = (bf16[2,96,625]{2,1,0:T(8,128)(2,1)S(1)}, bf16[2,96,625]{2,1,0:T(8,128)(2,1)S(1)}, u32[]{:S(2)}, u32[]{:S(2)}) collective-permute-start(bf16[2,96,625]{2,1,0:T(8,128)(2,1)S(1)} %collective-permute-done.14.refs_1_), channel_id=1, source_target_pairs={{0,16},{1,9},{2,18},{3,11},{4,20},{5,13},{6,22},{7,15},{8,24},{9,1... | collective-permute-start | bytes 720008 | tf_op jit(solution)/shard_map/ppermute | solution.py:310
  69.3 0.0 collective-permute-start.20
  69.3 4.8 %collective-permute-done.18.refs_3_ = bf16[2,96,625]{2,1,0:T(8,128)(2,1)S(1)} collective-permute-done((bf16[2,96,625]{2,1,0:T(8,128)(2,1)S(1)}, bf16[2,96,625]{2,1,0:T(8,128)(2,1)S(1)}, u32[]{:S(2)}, u32[]{:S(2)}) %collective-permute-start.18) | collective-permute-done | bytes 240032 | tf_op jit(solution)/shard_map/ppermute | solution.py:310
  74.1 0.0 collective-permute-start.19
  74.1 3.4 %shard_map.76.refs_6_ = bf16[2,1600,384]{2,1,0:T(8,128)(2,1)} custom-call(s32[1]{0:T(128)} %bitcast.column_ref, bf16[2,96,625]{2,1,0:T(8,128)(2,1)S(1)} %collective-permute-done.11.refs_0_, bf16[2,96,625]{2,1,0:T(8,128)(2,1)S(1)} %collective-permute-done.14.refs_1_, bf16[2,96,625]{2,1,0:T(8,128)(2,1)S(1)} %collective-permute-done.15.refs_2_, ...), custom_call_target="tpu_custom_call" | custom-call | flops 1536000000 | bytes 3417600 | tf_op jit(solution)/shard_map/pallas_call | solution.py:73
  77.5 1.9 %collective-permute-done.20.refs_3_ = bf16[625,256]{1,0:T(8,128)(2,1)S(1)} collective-permute-done((bf16[625,256]{1,0:T(8,128)(2,1)S(1)}, bf16[625,256]{1,0:T(8,128)(2,1)S(1)}, u32[]{:S(2)}, u32[]{:S(2)}) %collective-permute-start.20) | collective-permute-done | bytes 320032 | tf_op jit(solution)/shard_map/ppermute | solution.py:299
  79.4 0.0 collective-permute-start.21
  79.4 1.4 %shard_map.77.refs_8_ = bf16[8,800,128]{2,1,0:T(8,128)(2,1)S(1)} custom-call(bf16[800,625]{1,0:T(8,128)(2,1)S(1)} %copy-done.2, bf16[625,256]{1,0:T(8,128)(2,1)S(1)} %bitcast.25, bf16[625,256]{1,0:T(8,128)(2,1)S(1)} %collective-permute-done.3.refs_1_, bf16[625,256]{1,0:T(8,128)(2,1)S(1)} %collective-permute-done.16.refs_2_, ...), custom_call_target="tpu_custom_call" | custom-call | flops 1024000000 | bytes 2560000 | tf_op jit(solution)/shard_map/pallas_call | solution.py:104
  80.9 0.6 collective-permute-start.22
  81.5 0.1 copy.23.owners_ref
  81.5 0.1 copy.24.local_ref
  81.6 4.8 %collective-permute-done.22.refs_9_ = bf16[8,800,128]{2,1,0:T(8,128)(2,1)S(1)} collective-permute-done((bf16[8,800,128]{2,1,0:T(8,128)(2,1)S(1)}, bf16[8,800,128]{2,1,0:T(8,128)(2,1)S(1)}, u32[]{:S(2)}, u32[]{:S(2)}) %collective-permute-start.22) | collective-permute-done | bytes 1638432 | tf_op jit(solution)/shard_map/ppermute | solution.py:296
  86.4 9.3 %shard_map.79 = bf16[1,2,625,128]{3,2,1,0:T(8,128)(2,1)S(1)} custom-call(s32[1]{0:T(128)} %bitcast.column_ref, s32[32,3]{1,0:T(8,128)S(1)} %copy.23.owners_ref, s32[32,4]{1,0:T(8,128)S(1)} %copy.24.local_ref, bf16[2,1600,384]{2,1,0:T(8,128)(2,1)} %copy-done, bf16[2,1600,384]{2,1,0:T(8,128)(2,1)} %collective-permute-done.12.refs_1_, ...), custom_call_target="tpu_custom_call" | custom-call | flops 2936012800 | bytes 6553600 | tf_op jit(solution)/shard_map/pallas_call | solution.py:262
  95.7 0.1 collective-permute-start.24
  95.8 9.3 %shard_map.78 = bf16[1,2,625,128]{3,2,1,0:T(8,128)(2,1)S(1)} custom-call(s32[1]{0:T(128)} %bitcast.column_ref, s32[32,3]{1,0:T(8,128)S(1)} %copy.23.owners_ref, s32[32,4]{1,0:T(8,128)S(1)} %copy.24.local_ref, bf16[2,1600,384]{2,1,0:T(8,128)(2,1)} %copy-done, bf16[2,1600,384]{2,1,0:T(8,128)(2,1)} %collective-permute-done.12.refs_1_, ...), custom_call_target="tpu_custom_call" | custom-call | flops 2936012800 | bytes 6553600 | tf_op jit(solution)/shard_map/pallas_call | solution.py:262
  105.1 1.1 collective-permute-start.23
  106.2 9.3 %shard_map.80 = bf16[1,2,625,128]{3,2,1,0:T(8,128)(2,1)S(1)} custom-call(s32[1]{0:T(128)} %bitcast.column_ref, s32[32,3]{1,0:T(8,128)S(1)} %copy.23.owners_ref, s32[32,4]{1,0:T(8,128)S(1)} %copy.24.local_ref, bf16[2,1600,384]{2,1,0:T(8,128)(2,1)} %copy-done, bf16[2,1600,384]{2,1,0:T(8,128)(2,1)} %collective-permute-done.12.refs_1_, ...), custom_call_target="tpu_custom_call" | custom-call | flops 2936012800 | bytes 6553600 | tf_op jit(solution)/shard_map/pallas_call | solution.py:262
  115.5 0.0 copy-start.5
  115.5 1.3 collective-permute-start.25
  116.7 9.3 %shard_map.81 = bf16[1,2,625,128]{3,2,1,0:T(8,128)(2,1)S(1)} custom-call(s32[1]{0:T(128)} %bitcast.column_ref, s32[32,3]{1,0:T(8,128)S(1)} %copy.23.owners_ref, s32[32,4]{1,0:T(8,128)S(1)} %copy.24.local_ref, bf16[2,1600,384]{2,1,0:T(8,128)(2,1)} %copy-done, bf16[2,1600,384]{2,1,0:T(8,128)(2,1)} %collective-permute-done.12.refs_1_, ...), custom_call_target="tpu_custom_call" | custom-call | flops 2936012800 | bytes 6553600 | tf_op jit(solution)/shard_map/pallas_call | solution.py:262
  126.0 0.0 collective-permute-done.24
  126.0 0.0 collective-permute-done.23
  126.0 0.4 collective-permute-done.25
  126.4 0.2 fusion.1
  126.6 1.2 copy.32
  (21 shorter events, 0.1 us)
Async XLA Ops:
  1.3 18.0 %collective-permute-start.3 = (bf16[625,256]{1,0:T(8,128)(2,1)S(1)}, bf16[625,256]{1,0:T(8,128)(2,1)S(1)}, u32[]{:S(2)}, u32[]{:S(2)}) collective-permute-start(bf16[625,256]{1,0:T(8,128)(2,1)S(1)} %bitcast.24), channel_id=1, source_target_pairs={{0,2},{1,3},{2,4},{3,5},{4,6},{5,7},{6,0},{7,1},{8,10},{9,11},{10,... | collective-permute-start | bytes 960008 | tf_op jit(solution)/shard_map/ppermute | solution.py:299
  7.9 11.4 %collective-permute-start.2 = (bf16[2,96,625]{2,1,0:T(8,128)(2,1)S(1)}, bf16[2,96,625]{2,1,0:T(8,128)(2,1)S(1)}, u32[]{:S(2)}, u32[]{:S(2)}) collective-permute-start(bf16[2,96,625]{2,1,0:T(8,128)(2,1)S(1)} %get-tuple-element.67), channel_id=1, source_target_pairs={{0,2},{1,3},{2,4},{3,5},{4,6},{5,7},{6,0},{7,1},{8,10},{9,11},{10,... | collective-permute-start | bytes 720008 | tf_op jit(solution)/shard_map/ppermute | solution.py:299
  9.5 9.8 %collective-permute-start.1 = (bf16[2,96,625]{2,1,0:T(8,128)(2,1)S(1)}, bf16[2,96,625]{2,1,0:T(8,128)(2,1)S(1)}, u32[]{:S(2)}, u32[]{:S(2)}) collective-permute-start(bf16[2,96,625]{2,1,0:T(8,128)(2,1)S(1)} %get-tuple-element.35.refs_0_), channel_id=1, source_target_pairs={{0,16},{1,9},{2,18},{3,11},{4,20},{5,13},{6,22},{7,15},{8,24},{9,1... | collective-permute-start | bytes 720008 | tf_op jit(solution)/shard_map/ppermute | solution.py:310
  11.0 8.3 %collective-permute-start = (bf16[2,96,625]{2,1,0:T(8,128)(2,1)S(1)}, bf16[2,96,625]{2,1,0:T(8,128)(2,1)S(1)}, u32[]{:S(2)}, u32[]{:S(2)}) collective-permute-start(bf16[2,96,625]{2,1,0:T(8,128)(2,1)S(1)} %get-tuple-element.35.refs_0_), channel_id=1, source_target_pairs={{0,8},{1,17},{2,10},{3,19},{4,12},{5,21},{6,14},{7,23},{8,0},{9,25... | collective-permute-start | bytes 720008 | tf_op jit(solution)/shard_map/ppermute | solution.py:309
  19.3 8.9 %collective-permute-start.4 = (bf16[2,96,625]{2,1,0:T(8,128)(2,1)S(1)}, bf16[2,96,625]{2,1,0:T(8,128)(2,1)S(1)}, u32[]{:S(2)}, u32[]{:S(2)}) collective-permute-start(bf16[2,96,625]{2,1,0:T(8,128)(2,1)S(1)} %collective-permute-done.refs_1_), channel_id=1, source_target_pairs={{0,16},{1,9},{2,18},{3,11},{4,20},{5,13},{6,22},{7,15},{8,24},{9,1... | collective-permute-start | bytes 720008 | tf_op jit(solution)/shard_map/ppermute | solution.py:310
  20.9 11.8 %collective-permute-start.7 = (bf16[2,96,625]{2,1,0:T(8,128)(2,1)S(1)}, bf16[2,96,625]{2,1,0:T(8,128)(2,1)S(1)}, u32[]{:S(2)}, u32[]{:S(2)}) collective-permute-start(bf16[2,96,625]{2,1,0:T(8,128)(2,1)S(1)} %get-tuple-element.39), channel_id=1, source_target_pairs={{0,4},{1,5},{2,6},{3,7},{4,0},{5,1},{6,2},{7,3},{8,12},{9,13},{10,... | collective-permute-start | bytes 720008 | tf_op jit(solution)/shard_map/ppermute | solution.py:299
  21.6 11.1 %collective-permute-start.6 = (bf16[2,96,625]{2,1,0:T(8,128)(2,1)S(1)}, bf16[2,96,625]{2,1,0:T(8,128)(2,1)S(1)}, u32[]{:S(2)}, u32[]{:S(2)}) collective-permute-start(bf16[2,96,625]{2,1,0:T(8,128)(2,1)S(1)} %collective-permute-done.2.refs_0_), channel_id=1, source_target_pairs={{0,16},{1,9},{2,18},{3,11},{4,20},{5,13},{6,22},{7,15},{8,24},{9,1... | collective-permute-start | bytes 720008 | tf_op jit(solution)/shard_map/ppermute | solution.py:310
  22.1 10.6 %collective-permute-start.5 = (bf16[2,96,625]{2,1,0:T(8,128)(2,1)S(1)}, bf16[2,96,625]{2,1,0:T(8,128)(2,1)S(1)}, u32[]{:S(2)}, u32[]{:S(2)}) collective-permute-start(bf16[2,96,625]{2,1,0:T(8,128)(2,1)S(1)} %collective-permute-done.2.refs_0_), channel_id=1, source_target_pairs={{0,8},{1,17},{2,10},{3,19},{4,12},{5,21},{6,14},{7,23},{8,0},{9,25... | collective-permute-start | bytes 720008 | tf_op jit(solution)/shard_map/ppermute | solution.py:309
  28.2 1.6 %copy-start.3 = (bf16[1600,625]{1,0:T(8,128)(2,1)S(1)}, bf16[1600,625]{1,0:T(8,128)(2,1)}, u32[]{:S(2)}) copy-start(bf16[1600,625]{1,0:T(8,128)(2,1)} %constant.59.clone.refs_4_) | copy-start | bytes 6000004
  29.7 13.7 %copy-start.4 = (bf16[1600,625]{1,0:T(8,128)(2,1)S(1)}, bf16[1600,625]{1,0:T(8,128)(2,1)}, u32[]{:S(2)}) copy-start(bf16[1600,625]{1,0:T(8,128)(2,1)} %constant.59.clone.refs_4_) | copy-start | bytes 6000004
  32.4 13.7 %copy-start = (bf16[2,1600,384]{2,1,0:T(8,128)(2,1)}, bf16[2,1600,384]{2,1,0:T(8,128)(2,1)S(1)}, u32[]{:S(2)}) copy-start(bf16[2,1600,384]{2,1,0:T(8,128)(2,1)S(1)} %shard_map.73.refs_0_) | copy-start | bytes 7372804
  32.7 6.2 %collective-permute-start.8 = (bf16[2,96,625]{2,1,0:T(8,128)(2,1)S(1)}, bf16[2,96,625]{2,1,0:T(8,128)(2,1)S(1)}, u32[]{:S(2)}, u32[]{:S(2)}) collective-permute-start(bf16[2,96,625]{2,1,0:T(8,128)(2,1)S(1)} %collective-permute-done.5.refs_1_), channel_id=1, source_target_pairs={{0,16},{1,9},{2,18},{3,11},{4,20},{5,13},{6,22},{7,15},{8,24},{9,1... | collective-permute-start | bytes 720008 | tf_op jit(solution)/shard_map/ppermute | solution.py:310
  38.9 10.9 %collective-permute-start.12 = (bf16[2,1600,384]{2,1,0:T(8,128)(2,1)S(1)}, bf16[2,1600,384]{2,1,0:T(8,128)(2,1)}, u32[]{:S(2)}, u32[]{:S(2)}) collective-permute-start(bf16[2,1600,384]{2,1,0:T(8,128)(2,1)S(1)} %shard_map.73.refs_0_), channel_id=1, source_target_pairs={{0,1},{1,0},{2,3},{3,2},{4,5},{5,4},{6,7},{7,6},{8,9},{9,8},{10,11... | collective-permute-start | bytes 7372808 | tf_op jit(solution)/shard_map/ppermute | solution.py:296
  38.9 8.4 %collective-permute-start.11 = (bf16[2,96,625]{2,1,0:T(8,128)(2,1)S(1)}, bf16[2,96,625]{2,1,0:T(8,128)(2,1)S(1)}, u32[]{:S(2)}, u32[]{:S(2)}) collective-permute-start(bf16[2,96,625]{2,1,0:T(8,128)(2,1)S(1)} %get-tuple-element.45), channel_id=1, source_target_pairs={{0,6},{1,7},{2,0},{3,1},{4,2},{5,3},{6,4},{7,5},{8,14},{9,15},{10,... | collective-permute-start | bytes 720008 | tf_op jit(solution)/shard_map/ppermute | solution.py:299
  41.4 8.5 %collective-permute-start.10 = (bf16[2,96,625]{2,1,0:T(8,128)(2,1)S(1)}, bf16[2,96,625]{2,1,0:T(8,128)(2,1)S(1)}, u32[]{:S(2)}, u32[]{:S(2)}) collective-permute-start(bf16[2,96,625]{2,1,0:T(8,128)(2,1)S(1)} %collective-permute-done.7.refs_0_), channel_id=1, source_target_pairs={{0,16},{1,9},{2,18},{3,11},{4,20},{5,13},{6,22},{7,15},{8,24},{9,1... | collective-permute-start | bytes 720008 | tf_op jit(solution)/shard_map/ppermute | solution.py:310
  42.9 6.9 %collective-permute-start.9 = (bf16[2,96,625]{2,1,0:T(8,128)(2,1)S(1)}, bf16[2,96,625]{2,1,0:T(8,128)(2,1)S(1)}, u32[]{:S(2)}, u32[]{:S(2)}) collective-permute-start(bf16[2,96,625]{2,1,0:T(8,128)(2,1)S(1)} %collective-permute-done.7.refs_0_), channel_id=1, source_target_pairs={{0,8},{1,17},{2,10},{3,19},{4,12},{5,21},{6,14},{7,23},{8,0},{9,25... | collective-permute-start | bytes 720008 | tf_op jit(solution)/shard_map/ppermute | solution.py:309
  46.1 15.9 %copy-start.1 = (bf16[2,1600,384]{2,1,0:T(8,128)(2,1)}, bf16[2,1600,384]{2,1,0:T(8,128)(2,1)S(1)}, u32[]{:S(2)}) copy-start(bf16[2,1600,384]{2,1,0:T(8,128)(2,1)S(1)} %shard_map.74.refs_2_) | copy-start | bytes 7372804
  49.8 6.2 %collective-permute-start.13 = (bf16[2,96,625]{2,1,0:T(8,128)(2,1)S(1)}, bf16[2,96,625]{2,1,0:T(8,128)(2,1)S(1)}, u32[]{:S(2)}, u32[]{:S(2)}) collective-permute-start(bf16[2,96,625]{2,1,0:T(8,128)(2,1)S(1)} %collective-permute-done.9.refs_1_), channel_id=1, source_target_pairs={{0,16},{1,9},{2,18},{3,11},{4,20},{5,13},{6,22},{7,15},{8,24},{9,1... | collective-permute-start | bytes 720008 | tf_op jit(solution)/shard_map/ppermute | solution.py:310
  56.0 11.8 %collective-permute-start.17 = (bf16[2,1600,384]{2,1,0:T(8,128)(2,1)S(1)}, bf16[2,1600,384]{2,1,0:T(8,128)(2,1)}, u32[]{:S(2)}, u32[]{:S(2)}) collective-permute-start(bf16[2,1600,384]{2,1,0:T(8,128)(2,1)S(1)} %shard_map.74.refs_2_), channel_id=1, source_target_pairs={{0,1},{1,0},{2,3},{3,2},{4,5},{5,4},{6,7},{7,6},{8,9},{9,8},{10,11... | collective-permute-start | bytes 7372808 | tf_op jit(solution)/shard_map/ppermute | solution.py:296
  56.1 11.8 %collective-permute-start.16 = (bf16[625,256]{1,0:T(8,128)(2,1)S(1)}, bf16[625,256]{1,0:T(8,128)(2,1)S(1)}, u32[]{:S(2)}, u32[]{:S(2)}) collective-permute-start(bf16[625,256]{1,0:T(8,128)(2,1)S(1)} %collective-permute-done.3.refs_1_), channel_id=1, source_target_pairs={{0,2},{1,3},{2,4},{3,5},{4,6},{5,7},{6,0},{7,1},{8,10},{9,11},{10,... | collective-permute-start | bytes 960008 | tf_op jit(solution)/shard_map/ppermute | solution.py:299
  56.1 8.8 %collective-permute-start.15 = (bf16[2,96,625]{2,1,0:T(8,128)(2,1)S(1)}, bf16[2,96,625]{2,1,0:T(8,128)(2,1)S(1)}, u32[]{:S(2)}, u32[]{:S(2)}) collective-permute-start(bf16[2,96,625]{2,1,0:T(8,128)(2,1)S(1)} %collective-permute-done.11.refs_0_), channel_id=1, source_target_pairs={{0,16},{1,9},{2,18},{3,11},{4,20},{5,13},{6,22},{7,15},{8,24},{9,1... | collective-permute-start | bytes 720008 | tf_op jit(solution)/shard_map/ppermute | solution.py:310
  57.5 7.4 %collective-permute-start.14 = (bf16[2,96,625]{2,1,0:T(8,128)(2,1)S(1)}, bf16[2,96,625]{2,1,0:T(8,128)(2,1)S(1)}, u32[]{:S(2)}, u32[]{:S(2)}) collective-permute-start(bf16[2,96,625]{2,1,0:T(8,128)(2,1)S(1)} %collective-permute-done.11.refs_0_), channel_id=1, source_target_pairs={{0,8},{1,17},{2,10},{3,19},{4,12},{5,21},{6,14},{7,23},{8,0},{9,25... | collective-permute-start | bytes 720008 | tf_op jit(solution)/shard_map/ppermute | solution.py:309
  62.0 17.5 %copy-start.2 = (bf16[800,625]{1,0:T(8,128)(2,1)S(1)}, bf16[800,625]{1,0:T(8,128)(2,1)}, u32[]{:S(2)}) copy-start(bf16[800,625]{1,0:T(8,128)(2,1)} %constant.60.clone.matrix_ref) | copy-start | bytes 3000004
  67.9 6.2 %collective-permute-start.18 = (bf16[2,96,625]{2,1,0:T(8,128)(2,1)S(1)}, bf16[2,96,625]{2,1,0:T(8,128)(2,1)S(1)}, u32[]{:S(2)}, u32[]{:S(2)}) collective-permute-start(bf16[2,96,625]{2,1,0:T(8,128)(2,1)S(1)} %collective-permute-done.14.refs_1_), channel_id=1, source_target_pairs={{0,16},{1,9},{2,18},{3,11},{4,20},{5,13},{6,22},{7,15},{8,24},{9,1... | collective-permute-start | bytes 720008 | tf_op jit(solution)/shard_map/ppermute | solution.py:310
  69.3 10.1 %collective-permute-start.20 = (bf16[625,256]{1,0:T(8,128)(2,1)S(1)}, bf16[625,256]{1,0:T(8,128)(2,1)S(1)}, u32[]{:S(2)}, u32[]{:S(2)}) collective-permute-start(bf16[625,256]{1,0:T(8,128)(2,1)S(1)} %collective-permute-done.16.refs_2_), channel_id=1, source_target_pairs={{0,2},{1,3},{2,4},{3,5},{4,6},{5,7},{6,0},{7,1},{8,10},{9,11},{10,... | collective-permute-start | bytes 960008 | tf_op jit(solution)/shard_map/ppermute | solution.py:299
  74.1 12.4 %collective-permute-start.19 = (bf16[2,1600,384]{2,1,0:T(8,128)(2,1)}, bf16[2,1600,384]{2,1,0:T(8,128)(2,1)}, u32[]{:S(2)}, u32[]{:S(2)}) collective-permute-start(bf16[2,1600,384]{2,1,0:T(8,128)(2,1)} %shard_map.75.refs_4_), channel_id=1, source_target_pairs={{0,1},{1,0},{2,3},{3,2},{4,5},{5,4},{6,7},{7,6},{8,9},{9,8},{10,11... | collective-permute-start | bytes 7372808 | tf_op jit(solution)/shard_map/ppermute | solution.py:296
  77.5 3.9 %copy-start.6 = (s32[32,3]{0,1:T(4,128)S(1)}, s32[32,3]{0,1:T(4,128)}, u32[]{:S(2)}) copy-start(s32[32,3]{0,1:T(4,128)} %param.10) | copy-start | bytes 1156
  77.5 4.0 %copy-start.7 = (s32[32,4]{0,1:T(4,128)S(1)}, s32[32,4]{0,1:T(4,128)}, u32[]{:S(2)}) copy-start(s32[32,4]{0,1:T(4,128)} %param.11) | copy-start | bytes 1540
  79.4 7.0 %collective-permute-start.21 = (bf16[2,1600,384]{2,1,0:T(8,128)(2,1)}, bf16[2,1600,384]{2,1,0:T(8,128)(2,1)}, u32[]{:S(2)}, u32[]{:S(2)}) collective-permute-start(bf16[2,1600,384]{2,1,0:T(8,128)(2,1)} %shard_map.76.refs_6_), channel_id=1, source_target_pairs={{0,1},{1,0},{2,3},{3,2},{4,5},{5,4},{6,7},{7,6},{8,9},{9,8},{10,11... | collective-permute-start | bytes 7372808 | tf_op jit(solution)/shard_map/ppermute | solution.py:296
  80.9 5.6 %collective-permute-start.22 = (bf16[8,800,128]{2,1,0:T(8,128)(2,1)S(1)}, bf16[8,800,128]{2,1,0:T(8,128)(2,1)S(1)}, u32[]{:S(2)}, u32[]{:S(2)}) collective-permute-start(bf16[8,800,128]{2,1,0:T(8,128)(2,1)S(1)} %shard_map.77.refs_8_), channel_id=1, source_target_pairs={{0,1},{1,0},{2,3},{3,2},{4,5},{5,4},{6,7},{7,6},{8,9},{9,8},{10,11... | collective-permute-start | bytes 4915208 | tf_op jit(solution)/shard_map/ppermute | solution.py:296
  95.7 30.3 %collective-permute-start.24 = (bf16[2,625,128]{2,1,0:T(8,128)(2,1)S(1)}, bf16[2,625,128]{2,1,0:T(8,128)(2,1)S(1)}, u32[]{:S(2)}, u32[]{:S(2)}) collective-permute-start(bf16[2,625,128]{2,1,0:T(8,128)(2,1)S(1)} %bitcast.26), channel_id=1, source_target_pairs={{0,4},{1,5},{2,6},{3,7},{4,0},{5,1},{6,2},{7,3},{8,12},{9,13},{10,... | collective-permute-start | bytes 960008 | tf_op jit(solution)/shard_map/ppermute | solution.py:299
  105.1 20.9 %collective-permute-start.23 = (bf16[2,625,128]{2,1,0:T(8,128)(2,1)S(1)}, bf16[2,625,128]{2,1,0:T(8,128)(2,1)S(1)}, u32[]{:S(2)}, u32[]{:S(2)}) collective-permute-start(bf16[2,625,128]{2,1,0:T(8,128)(2,1)S(1)} %bitcast.27), channel_id=1, source_target_pairs={{0,6},{1,7},{2,0},{3,1},{4,2},{5,3},{6,4},{7,5},{8,14},{9,15},{10,... | collective-permute-start | bytes 960008 | tf_op jit(solution)/shard_map/ppermute | solution.py:299
  115.5 11.0 %copy-start.5 = (f32[2,128,625]{1,0,2:T(2,128)S(1)}, f32[2,128,625]{1,0,2:T(2,128)}, u32[]{:S(2)}) copy-start(f32[2,128,625]{1,0,2:T(2,128)} %param.9) | copy-start | bytes 1920004
  115.5 11.0 %collective-permute-start.25 = (bf16[2,625,128]{2,1,0:T(8,128)(2,1)S(1)}, bf16[2,625,128]{2,1,0:T(8,128)(2,1)S(1)}, u32[]{:S(2)}, u32[]{:S(2)}) collective-permute-start(bf16[2,625,128]{2,1,0:T(8,128)(2,1)S(1)} %bitcast.28), channel_id=1, source_target_pairs={{0,2},{1,3},{2,4},{3,5},{4,6},{5,7},{6,0},{7,1},{8,10},{9,11},{10,... | collective-permute-start | bytes 960008 | tf_op jit(solution)/shard_map/ppermute | solution.py:299
